TPU v7x, 32 devices: a whole 2x2x4 slice. The times are simulated.
32 devices in a mesh: shard: 8 (over z, y), tensor: 4 (over x, core).
Axes of the slice: x: 2, y: 2, z: 4, core: 2. Of those that a mesh axis runs over, the one named last changes fastest.
Arguments:
- grads: float32 [16, 384, 384], P('tensor', 'shard'), may hold values from -0.3 to 0.3
- moment_one: float32 [32, 73728], P(('tensor', 'shard')), may hold values from -0.3 to 0.3
- moment_two: float32 [32, 73728], P(('tensor', 'shard')), may hold values from 0.0005 to 0.01
- left_stat: float32 [32, 73728], P(('tensor', 'shard')), may hold values from -1 to 9, as said below
- right_stat: float32 [32, 73728], P(('tensor', 'shard')), may hold values from -1 to 9, as said below
- left_basis: float32 [32, 73728], P(('tensor', 'shard')), may hold values from -1 to 2
- right_basis: float32 [32, 73728], P(('tensor', 'shard')), may hold values from -1 to 2
Outputs:
- update: float32 [16, 384, 384], P('tensor', 'shard')
- new_moment_one: float32 [32, 73728], P(('tensor', 'shard'))
- new_moment_two: float32 [32, 73728], P(('tensor', 'shard'))
- new_left_stat: float32 [32, 73728], P(('tensor', 'shard'))
- new_right_stat: float32 [32, 73728], P(('tensor', 'shard'))
- new_left_basis: float32 [32, 73728], P(('tensor', 'shard'))
- new_right_basis: float32 [32, 73728], P(('tensor', 'shard'))
Inputs may be any that keep to these rules, and one draw needn't show every extreme that they name: `left_stat`: each tile of the statistics is symmetric. `right_stat`: each tile of the statistics is symmetric.
All inputs are finite; a program needn't handle non-finite values.
Results may differ from a plain program's by a relative error of at most 0.00024.
Values sent between devices are 32-bit elements; how exact they have to be, the bound alone decides.
No kernel may reach another device: no remote copies, remote signals or barrier semaphores. Data moves between devices by JAX's collectives and lax.ppermute only.
A program may use at most 64 MiB of HBM per device.

v0:
```python
import jax
import jax.numpy as jnp
from jax import lax
from jax.experimental import pallas as pl
from jax.experimental.pallas import tpu as pltpu
from jax.sharding import PartitionSpec as P

NS_ITERS = 5
BETA_ONE = 0.9
BETA_TWO = 0.95
ADAM_EPS = 1e-08
NORM_EPS = 1e-06
LINEAR_COEFF = 3.4445
CUBIC_COEFF = -4.775
QUINTIC_COEFF = 2.0315
LANES = 128
F32 = jnp.float32


def split(x):
    high = x.astype(jnp.bfloat16)
    return high, (x - high.astype(F32)).astype(jnp.bfloat16)


def dot(a, b, dims=((1,), (0,))):
    return dot_parts(split(a), split(b), dims)


def dot_parts(a, b, dims=((1,), (0,))):
    (ka,), (kb,) = dims
    left = jnp.concatenate([a[0], a[0], a[1]], axis=ka)
    right = jnp.concatenate([b[0], b[1], b[0]], axis=kb)
    return lax.dot_general(left, right, (dims, ((), ())), preferred_element_type=F32)


def swap(x):
    return pltpu.roll(x, LANES // 2, 1)


def low_lanes(shape):
    return lax.broadcasted_iota(jnp.int32, shape, 1) < LANES // 2


def pick(flag, x, y):
    return [jnp.where(flag, u, v) for u, v in zip(x, y)]


def thirds(ref, start=0, rows=None):
    rows = ref.shape[0] if rows is None else rows
    return [ref[pl.ds(start + k, rows // 3, stride=3), :] for k in range(3)]


def put_thirds(ref, parts):
    for k in range(3):
        ref[pl.ds(k, parts[k].shape[0], stride=3), :] = parts[k]


def interleave(scratch, index, even, odd):
    scratch[index, pl.ds(0, even.shape[0], stride=2), :] = even
    scratch[index, pl.ds(1, odd.shape[0], stride=2), :] = odd


def whole_of(scratch, first, second):
    a, b, c = first
    d, e, f = second
    low = low_lanes(a.shape)
    sb, sc, sd, se = swap(b), swap(c), swap(d), swap(e)
    interleave(scratch, 0, a, jnp.where(low, sb, sc))
    interleave(scratch, 1, jnp.where(low, b, sd), jnp.where(low, sc, e))
    interleave(scratch, 2, jnp.where(low, sd, se), f)
    return jnp.concatenate([scratch[0], scratch[1], scratch[2]], axis=1)


def half_of(scratch, flat):
    a, b, c = flat
    low = low_lanes(a.shape)
    sb, sc = swap(b), swap(c)
    interleave(scratch, 0, a, jnp.where(low, sb, sc))
    interleave(scratch, 1, jnp.where(low, b, 0.0), jnp.where(low, sc, 0.0))
    return jnp.concatenate([scratch[0], scratch[1]], axis=1)


def flat_of(scratch, half):
    scratch[0] = half[:, :LANES]
    scratch[1] = half[:, LANES:]
    pairs = half.shape[0] // 2
    even0 = scratch[0, pl.ds(0, pairs, stride=2), :]
    odd0 = swap(scratch[0, pl.ds(1, pairs, stride=2), :])
    even1 = scratch[1, pl.ds(0, pairs, stride=2), :]
    odd1 = swap(scratch[1, pl.ds(1, pairs, stride=2), :])
    low = low_lanes(even0.shape)
    return [even0, jnp.where(low, even1, odd0), jnp.where(low, odd0, odd1)]


def take_half(whole, first):
    one, two, three = whole[:, :LANES], whole[:, LANES : 2 * LANES], whole[:, 2 * LANES :]
    low = low_lanes(one.shape)
    s2, s3 = swap(two), swap(three)
    head = jnp.where(first, one, jnp.where(low, s2, s3))
    tail = jnp.where(low, jnp.where(first, two, s3), 0.0)
    return jnp.concatenate([head, tail], axis=1)


def is_left():
    return lax.rem(lax.axis_index("shard"), 2) == 0


def stats_kernel(grad_ref, left_ref, right_ref, got_ref, new_left_ref, new_right_ref, stat_ref, scratch):
    left = is_left()
    flat_rows = left_ref.shape[0]
    l_flat, r_flat = thirds(left_ref), thirds(right_ref)
    own, other = pick(left, l_flat, r_flat), pick(left, r_flat, l_flat)
    corner = thirds(got_ref, flat_rows, flat_rows // 2)
    placed = [jnp.concatenate([jnp.where(left, 0.0, c), jnp.where(left, c, 0.0)], axis=0) for c in corner]
    known = whole_of(scratch, pick(left, own, placed), pick(left, placed, own))
    full = known.shape[0]
    row = lax.broadcasted_iota(jnp.int32, known.shape, 0)
    column = lax.broadcasted_iota(jnp.int32, known.shape, 1)
    missing = (jnp.where(left, row, column) < full // 2) & (jnp.where(left, column, row) >= full // 2)
    stat = jnp.where(missing, known.T, known)
    grad = grad_ref[...]
    turned = grad.T
    a = jnp.where(left, grad, turned)
    b = jnp.where(left, turned, grad)
    product = dot(a, b)
    stat_ref[...] = 0.5 * stat + 0.5 * product
    new_own = [0.5 * u + 0.5 * v for u, v in zip(own, flat_of(scratch, take_half(product, left)))]
    other_product = dot(b, take_half(a, left))
    new_other = [0.5 * u + 0.5 * v for u, v in zip(other, flat_of(scratch, other_product))]
    put_thirds(new_left_ref, pick(left, new_own, new_other))
    put_thirds(new_right_ref, pick(left, new_other, new_own))


def refresh_kernel(stat_ref, left_ref, right_ref, got_ref, keep_ref, send_ref, scratch, x_ref):
    left = is_left()
    own = pick(left, thirds(left_ref), thirds(right_ref))
    got = thirds(got_ref, 0, left_ref.shape[0])
    basis = whole_of(scratch, pick(left, own, got), pick(left, got, own))
    power = dot(stat_ref[...], basis)
    x_ref[...] = power * (1.0 / jnp.sqrt(jnp.sum(power * power) + NORM_EPS))

    @pl.loop(0, NS_ITERS)
    def _(step):
        x = x_ref[...]
        parts = split(x)
        gram = dot_parts(parts, parts, ((1,), (1,)))
        gram_parts = split(gram)
        poly = CUBIC_COEFF * gram + QUINTIC_COEFF * dot_parts(gram_parts, gram_parts)
        x_ref[...] = LINEAR_COEFF * x + dot_parts(split(poly), parts)

    x = x_ref[...]
    put_thirds(send_ref, flat_of(scratch, take_half(x, jnp.logical_not(left))))
    put_thirds(keep_ref, flat_of(scratch, take_half(x, left)))


def update_kernel(
    grad_ref, left_ref, right_ref, got_ref, first_left_ref, one_ref, two_ref, new_one_ref, new_two_ref, update_ref, scratch
):
    left = is_left()
    own = thirds(left_ref)
    got = thirds(got_ref, 0, left_ref.shape[0])
    basis_left = whole_of(scratch, pick(left, own, thirds(first_left_ref)), pick(left, got, own))
    left_parts = split(basis_left)
    basis_right = split(half_of(scratch, thirds(right_ref)))
    inner = dot_parts(split(grad_ref[...]), basis_right)
    rotated = flat_of(scratch, dot(basis_left.T, inner))
    ones = thirds(one_ref)
    twos = thirds(two_ref)
    new_one = [BETA_ONE * m + (1.0 - BETA_ONE) * r for m, r in zip(ones, rotated)]
    new_two = [BETA_TWO * v + (1.0 - BETA_TWO) * r * r for v, r in zip(twos, rotated)]
    put_thirds(new_one_ref, new_one)
    put_thirds(new_two_ref, new_two)
    direction = [m / (jnp.sqrt(v) + ADAM_EPS) for m, v in zip(new_one, new_two)]
    outer = dot_parts(left_parts, split(half_of(scratch, direction)))
    update_ref[...] = dot_parts(split(outer), basis_right, ((1,), (1,)))


def call(kernel, outs, scratch, flops, nbytes):
    return pl.pallas_call(
        kernel,
        out_shape=[jax.ShapeDtypeStruct(s, F32) for s in outs],
        scratch_shapes=[pltpu.VMEM(s, F32) for s in scratch],
        compiler_params=pltpu.CompilerParams(vmem_limit_bytes=40 * 1024 * 1024),
        cost_estimate=pl.CostEstimate(flops=flops, bytes_accessed=nbytes, transcendentals=0),
    )


def local(grads, moment_one, moment_two, left_stat, right_stat, left_basis, right_basis):
    tiles_here, rows_here, full = grads.shape
    half = full // 2
    size = lax.axis_size("shard")
    flat_rows = full * half // LANES
    flat_shape = (flat_rows, LANES)
    parity = lax.axis_index("shard") % 2

    def flat(x):
        return x.reshape(flat_shape)

    one, two, l_stat, r_stat, l_basis, r_basis = map(
        flat, (moment_one, moment_two, left_stat, right_stat, left_basis, right_basis)
    )
    pieces = jnp.broadcast_to(grads[:, None], (tiles_here, 2, rows_here, full)).reshape(size, rows_here, full)
    grad = lax.all_to_all(pieces, "shard", split_axis=0, concat_axis=0, tiled=True).reshape(full, full)
    outgoing = jnp.where(
        parity == 0,
        jnp.concatenate([r_basis, r_stat[: flat_rows // 2]], axis=0),
        jnp.concatenate([l_basis, l_stat[flat_rows // 2 :]], axis=0),
    )
    got = lax.ppermute(outgoing, "shard", [(i, i ^ 1) for i in range(size)])
    first_left = lax.ppermute(l_basis, "shard", [(i, i + 1) for i in range(0, size, 2)])

    cube = 2 * full**3 * 3
    new_left, new_right, stat = call(
        stats_kernel, [flat_shape, flat_shape, (full, full)], [(3, full, LANES)], 2 * cube, 8 * full * full * 4
    )(grad, l_stat, r_stat, got)
    new_one, new_two, partial = call(
        update_kernel, [flat_shape, flat_shape, (full, full)], [(3, full, LANES)], 2 * cube, 8 * full * full * 4
    )(grad, l_basis, r_basis, got, first_left, one, two)
    returned = lax.all_to_all(
        partial.reshape(size, rows_here, full), "shard", split_axis=0, concat_axis=0, tiled=True
    )
    keep, send = call(
        refresh_kernel, [flat_shape, flat_shape], [(3, full, LANES), (full, full)], 16 * cube, 4 * full * full * 4
    )(stat, l_basis, r_basis, got)
    back = lax.ppermute(send, "shard", [(i, i ^ 1) for i in range(size)])
    new_l_basis = jnp.where(parity == 0, keep, back)
    new_r_basis = jnp.where(parity == 0, back, keep)
    update = returned.reshape(tiles_here, 2, rows_here, full).sum(axis=1)

    def unflat(x):
        return x.reshape(1, full * half)

    return (update, *map(unflat, (new_one, new_two, new_left, new_right, new_l_basis, new_r_basis)))


def solution(mesh):
    halves = P(("tensor", "shard"), None)
    rows = P("tensor", "shard", None)
    return jax.shard_map(
        local, mesh=mesh, in_specs=(rows,) + (halves,) * 6, out_specs=(rows,) + (halves,) * 6, check_vma=False
    )
```

profile of v0, /device:TPU:0, one launch (start us, length us, event | category | flops | bytes accessed | tf_op | source)
XLA Modules:
  0.0 65.8 jit_solution(17537740812611577456)
XLA Ops:
  0.6 1.8 %broadcast_in_dim.2 = f32[4,2,48,384]{3,2,1,0:T(8,128)} broadcast(f32[4,48,384]{2,1,0:T(8,128)} %param.7), dimensions={0,2,3} | broadcast | bytes 884736 | tf_op jit(solution)/shard_map/broadcast_in_dim | solution.py:202
  2.5 0.0 slice-start
  2.5 0.0 slice-start.1
  2.5 7.4 %all-to-all-start = ((f32[8,48,384]{2,1,0:T(8,128)}), f32[8,48,384]{2,1,0:T(8,128)S(1)}, u32[]{:S(2)}, u32[]{:S(2)}) async-start(f32[8,48,384]{2,1,0:T(8,128)} %bitcast), calls=%async_computation | async-start | bytes 1179648 | tf_op jit(solution)/shard_map/all_to_all | solution.py:203
  9.9 0.0 copy-start
  9.9 0.0 copy-start.1
  9.9 0.0 slice-done
  9.9 0.0 slice-done.1
  9.9 0.9 %copy-done = f32[1,73728]{1,0:T(1,128)S(1)} copy-done((f32[1,73728]{1,0:T(1,128)S(1)}, f32[1,73728]{1,0:T(1,128)}, u32[]{:S(2)}) %copy-start) | copy-done | bytes 294936
  10.8 0.1 copy-done.1
  10.9 0.0 copy-start.4
  10.9 0.0 copy-start.5
  11.0 2.1 %collective-permute-start = (f32[864,128]{1,0:T(8,128)S(1)}, f32[864,128]{1,0:T(8,128)S(1)}, u32[]{:S(2)}, u32[]{:S(2)}) collective-permute-start(f32[864,128]{1,0:T(8,128)S(1)} %maximum_select_fusion), channel_id=1, source_target_pairs={{0,4},{4,0},{8,12},{12,8},{16,20},{20,16},{24,28},{28,24},{1,5},{5... | collective-permute-start | bytes 1327112 | tf_op jit(solution)/shard_map/ppermute | solution.py:209
  13.1 2.1 %collective-permute-start.1 = (f32[576,128]{1,0:T(8,128)S(1)}, f32[576,128]{1,0:T(8,128)S(1)}, u32[]{:S(2)}, u32[]{:S(2)}) collective-permute-start(f32[576,128]{1,0:T(8,128)S(1)} %bitcast.22), channel_id=1, source_target_pairs={{0,4},{8,12},{16,20},{24,28},{1,5},{9,13},{17,21},{25,29},{2,6},{1... | collective-permute-start | bytes 884744 | tf_op jit(solution)/shard_map/ppermute | solution.py:210
  15.1 17.4 %collective-permute-done.1.first_left_ref = f32[576,128]{1,0:T(8,128)S(1)} collective-permute-done((f32[576,128]{1,0:T(8,128)S(1)}, f32[576,128]{1,0:T(8,128)S(1)}, u32[]{:S(2)}, u32[]{:S(2)}) %collective-permute-start.1) | collective-permute-done | bytes 294944 | tf_op jit(solution)/shard_map/ppermute | solution.py:210
  32.5 0.0 collective-permute-done.got_ref
  32.5 0.0 all-to-all-done
  32.5 0.0 copy-done.4
  32.5 0.0 copy-done.5
  32.5 3.8 %shard_map.126 = (f32[576,128]{1,0:T(8,128)}, f32[576,128]{1,0:T(8,128)}, f32[384,384]{1,0:T(8,128)}) custom-call(f32[384,384]{1,0:T(8,128)S(1)} %bitcast.19, f32[576,128]{1,0:T(8,128)S(1)} %bitcast.23, f32[576,128]{1,0:T(8,128)S(1)} %bitcast.26, f32[864,128]{1,0:T(8,128)S(1)} %collective-permute-done.got_ref, ...), custom_call_target="tpu_custom_call" | custom-call | flops 679477248 | bytes 4718592 | tf_op jit(solution)/shard_map/pallas_call | solution.py:216
  36.3 0.0 copy-start.2
  36.3 0.0 copy-start.3
  36.3 6.2 %all-to-all-start.1 = ((f32[8,48,384]{2,1,0:T(8,128)}), f32[8,48,384]{2,1,0:T(8,128)S(1)}, u32[]{:S(2)}, u32[]{:S(2)}) async-start(f32[8,48,384]{2,1,0:T(8,128)} %bitcast.8), calls=%async_computation.1 | async-start | bytes 1179648 | tf_op jit(solution)/shard_map/all_to_all | solution.py:219
  42.5 0.0 copy-done.2
  42.5 0.0 copy-done.3
  42.5 2.2 %shard_map.127 = (f32[576,128]{1,0:T(8,128)}, f32[576,128]{1,0:T(8,128)}, f32[384,384]{1,0:T(8,128)S(1)}) custom-call(f32[384,384]{1,0:T(8,128)S(1)} %bitcast.20, f32[576,128]{1,0:T(8,128)S(1)} %bitcast.30, f32[576,128]{1,0:T(8,128)S(1)} %bitcast.28, f32[864,128]{1,0:T(8,128)S(1)} %collective-permute-done.got_ref), custom_call_target="tpu_custom_call" | custom-call | flops 679477248 | bytes 4718592 | tf_op jit(solution)/shard_map/pallas_call | solution.py:213
  44.7 10.8 %shard_map.128 = (f32[576,128]{1,0:T(8,128)S(1)}, f32[576,128]{1,0:T(8,128)S(1)}) custom-call(f32[384,384]{1,0:T(8,128)S(1)} %get-tuple-element.20.stat_ref, f32[576,128]{1,0:T(8,128)S(1)} %bitcast.24, f32[576,128]{1,0:T(8,128)S(1)} %bitcast.27, f32[864,128]{1,0:T(8,128)S(1)} %collective-permute-done.got_ref), custom_call_target="tpu_custom_call" | custom-call | flops 5435817984 | bytes 2359296 | tf_op jit(solution)/shard_map/pallas_call | solution.py:222
  55.5 2.1 %collective-permute-start.2 = (f32[576,128]{1,0:T(8,128)S(1)}, f32[576,128]{1,0:T(8,128)S(1)}, u32[]{:S(2)}, u32[]{:S(2)}) collective-permute-start(f32[576,128]{1,0:T(8,128)S(1)} %get-tuple-element.22), channel_id=1, source_target_pairs={{0,4},{4,0},{8,12},{12,8},{16,20},{20,16},{24,28},{28,24},{1,5},{5... | collective-permute-start | bytes 884744 | tf_op jit(solution)/shard_map/ppermute | solution.py:225
  57.6 6.6 %collective-permute-done.2 = f32[576,128]{1,0:T(8,128)S(1)} collective-permute-done((f32[576,128]{1,0:T(8,128)S(1)}, f32[576,128]{1,0:T(8,128)S(1)}, u32[]{:S(2)}, u32[]{:S(2)}) %collective-permute-start.2) | collective-permute-done | bytes 294944 | tf_op jit(solution)/shard_map/ppermute | solution.py:225
  64.2 0.9 %broadcast_select_fusion = (f32[576,128]{1,0:T(8,128)}, f32[576,128]{1,0:T(8,128)}) fusion(f32[576,128]{1,0:T(8,128)S(1)} %collective-permute-done.2, f32[576,128]{1,0:T(8,128)S(1)} %get-tuple-element.21, pred[]{:T(512)S(6)} %eq.4), kind=kLoop, calls=%fused_computation.2 | loop fusion | flops 147456 | bytes 1179649 | tf_op jit(solution)/shard_map/jit(_where)/select_n | solution.py:227
  65.1 0.0 all-to-all-done.1
  65.1 0.7 %bitcast_reduce_fusion = f32[4,48,384]{2,1,0:T(8,128)} fusion(f32[8,48,384]{2,1,0:T(8,128)S(1)} %all-to-all-done.1), kind=kLoop, calls=%fused_computation | loop fusion | flops 73728 | bytes 884736 | tf_op jit(solution)/shard_map/reduce_sum | solution.py:228
  (1 shorter events, 0.0 us)
Async XLA Ops:
  2.5 7.4 %slice-start = ((f32[1,73728]{1,0:T(1,128)}), f32[1,36864]{1,0:T(1,128)S(1)}, s32[]{:S(2)}) async-start(f32[1,73728]{1,0:T(1,128)} %param.11), calls=%async_computation.2 | async-start | bytes 294912 | tf_op jit(solution)/shard_map/slice | solution.py:206
  2.5 7.4 %slice-start.1 = ((f32[1,73728]{1,0:T(1,128)}), f32[1,36864]{1,0:T(1,128)S(1)}, s32[]{:S(2)}) async-start(f32[1,73728]{1,0:T(1,128)} %param.10), calls=%async_computation.3 | async-start | bytes 294912 | tf_op jit(solution)/shard_map/slice | solution.py:207
  2.5 30.0 %all-to-all-start = ((f32[8,48,384]{2,1,0:T(8,128)}), f32[8,48,384]{2,1,0:T(8,128)S(1)}, u32[]{:S(2)}, u32[]{:S(2)}) async-start(f32[8,48,384]{2,1,0:T(8,128)} %bitcast), calls=%async_computation | async-start | bytes 1179648 | tf_op jit(solution)/shard_map/all_to_all | solution.py:203
  9.9 1.0 %copy-start = (f32[1,73728]{1,0:T(1,128)S(1)}, f32[1,73728]{1,0:T(1,128)}, u32[]{:S(2)}) copy-start(f32[1,73728]{1,0:T(1,128)} %param.12) | copy-start | bytes 884740
  9.9 1.0 %copy-start.1 = (f32[1,73728]{1,0:T(1,128)S(1)}, f32[1,73728]{1,0:T(1,128)}, u32[]{:S(2)}) copy-start(f32[1,73728]{1,0:T(1,128)} %param.13) | copy-start | bytes 884740
  10.9 21.6 %copy-start.4 = (f32[1,73728]{1,0:T(1,128)S(1)}, f32[1,73728]{1,0:T(1,128)}, u32[]{:S(2)}) copy-start(f32[1,73728]{1,0:T(1,128)} %param.8) | copy-start | bytes 884740
  10.9 21.6 %copy-start.5 = (f32[1,73728]{1,0:T(1,128)S(1)}, f32[1,73728]{1,0:T(1,128)}, u32[]{:S(2)}) copy-start(f32[1,73728]{1,0:T(1,128)} %param.9) | copy-start | bytes 884740
  11.0 21.5 %collective-permute-start = (f32[864,128]{1,0:T(8,128)S(1)}, f32[864,128]{1,0:T(8,128)S(1)}, u32[]{:S(2)}, u32[]{:S(2)}) collective-permute-start(f32[864,128]{1,0:T(8,128)S(1)} %maximum_select_fusion), channel_id=1, source_target_pairs={{0,4},{4,0},{8,12},{12,8},{16,20},{20,16},{24,28},{28,24},{1,5},{5... | collective-permute-start | bytes 1327112 | tf_op jit(solution)/shard_map/ppermute | solution.py:209
  13.1 19.4 %collective-permute-start.1 = (f32[576,128]{1,0:T(8,128)S(1)}, f32[576,128]{1,0:T(8,128)S(1)}, u32[]{:S(2)}, u32[]{:S(2)}) collective-permute-start(f32[576,128]{1,0:T(8,128)S(1)} %bitcast.22), channel_id=1, source_target_pairs={{0,4},{8,12},{16,20},{24,28},{1,5},{9,13},{17,21},{25,29},{2,6},{1... | collective-permute-start | bytes 884744 | tf_op jit(solution)/shard_map/ppermute | solution.py:210
  36.3 6.2 %copy-start.2 = (f32[1,73728]{1,0:T(1,128)S(1)}, f32[1,73728]{1,0:T(1,128)}, u32[]{:S(2)}) copy-start(f32[1,73728]{1,0:T(1,128)} %param.11) | copy-start | bytes 884740
  36.3 6.2 %copy-start.3 = (f32[1,73728]{1,0:T(1,128)S(1)}, f32[1,73728]{1,0:T(1,128)}, u32[]{:S(2)}) copy-start(f32[1,73728]{1,0:T(1,128)} %param.10) | copy-start | bytes 884740
  36.3 28.8 %all-to-all-start.1 = ((f32[8,48,384]{2,1,0:T(8,128)}), f32[8,48,384]{2,1,0:T(8,128)S(1)}, u32[]{:S(2)}, u32[]{:S(2)}) async-start(f32[8,48,384]{2,1,0:T(8,128)} %bitcast.8), calls=%async_computation.1 | async-start | bytes 1179648 | tf_op jit(solution)/shard_map/all_to_all | solution.py:219
  55.5 8.7 %collective-permute-start.2 = (f32[576,128]{1,0:T(8,128)S(1)}, f32[576,128]{1,0:T(8,128)S(1)}, u32[]{:S(2)}, u32[]{:S(2)}) collective-permute-start(f32[576,128]{1,0:T(8,128)S(1)} %get-tuple-element.22), channel_id=1, source_target_pairs={{0,4},{4,0},{8,12},{12,8},{16,20},{20,16},{24,28},{28,24},{1,5},{5... | collective-permute-start | bytes 884744 | tf_op jit(solution)/shard_map/ppermute | solution.py:225
where the time goes:
time: 66.2 us; the launch traced here: 65.8 us
  waiting for transfers between devices  24 us (36%)
  starting transfers between devices  19.9 us (30%)
  Pallas kernels  16.7 us (25%)
  local copies, waits for them, and re-layouts  2.87 us (4%)
  other arithmetic  1.64 us (2%)
  between operations  0.71 us (1%)
    ppermute x1, waiting for transfers between devices, local(): lax.ppermute(l_basis, 'shard', [(i, i + 1) for i in range(0, size, 2)])  17.4 us
    pallas_call x1, Pallas kernels, local(): call(refresh_kernel, [flat_shape, flat_shape], [(3, full, LANES), (full,...  10.8 us
    all_to_all x1, starting transfers between devices, local(): lax.all_to_all(pieces, 'shard', split_axis=0, concat_axis=0, tiled=True)  7.41 us
    ppermute x1, waiting for transfers between devices, local(): back = lax.ppermute(send, 'shard', [(i, i ^ 1) for i in range(size)])  6.64 us
    all_to_all x1, starting transfers between devices, local(): lax.all_to_all(partial.reshape(size, rows_here, full), 'shard', split_axi...  6.24 us
    pallas_call x1, Pallas kernels, local(): call(update_kernel, [flat_shape, flat_shape, (full, full)], [(3, full, LA...  3.77 us
    pallas_call x1, Pallas kernels, local(): call(stats_kernel, [flat_shape, flat_shape, (full, full)], [(3, full, LAN...  2.16 us
    ppermute x1, starting transfers between devices, local(): got = lax.ppermute(outgoing, 'shard', [(i, i ^ 1) for i in range(size)])  2.09 us
  transfers between devices with their start and end apart: 5, of which 2 were waited for; matrix products, arithmetic and copies ran while one was open for 1% of the time, Pallas kernels for 20%

commit v1 on v0

v1 whole, which is shorter than its diff:
```python
import functools

import jax
import jax.numpy as jnp
from jax import lax
from jax.experimental import pallas as pl
from jax.experimental.pallas import tpu as pltpu
from jax.sharding import PartitionSpec as P

NS_ITERS = 5
BETA_ONE = 0.9
BETA_TWO = 0.95
ADAM_EPS = 1e-08
NORM_EPS = 1e-06
LINEAR_COEFF = 3.4445
CUBIC_COEFF = -4.775
QUINTIC_COEFF = 2.0315
LANES = 128
F32 = jnp.float32


def split(x):
    high = x.astype(jnp.bfloat16)
    return high, (x - high.astype(F32)).astype(jnp.bfloat16)


def dot(a, b, dims=((1,), (0,))):
    return dot_parts(split(a), split(b), dims)


def dot_parts(a, b, dims=((1,), (0,))):
    (ka,), (kb,) = dims
    left = jnp.concatenate([a[0], a[0], a[1]], axis=ka)
    right = jnp.concatenate([b[0], b[1], b[0]], axis=kb)
    return lax.dot_general(left, right, (dims, ((), ())), preferred_element_type=F32)


def swap(x):
    return pltpu.roll(x, LANES // 2, 1)


def low_lanes(shape):
    return lax.broadcasted_iota(jnp.int32, shape, 1) < LANES // 2


def pick(flag, x, y):
    return [jnp.where(flag, u, v) for u, v in zip(x, y)]


def thirds(ref, start=0, rows=None):
    rows = ref.shape[0] if rows is None else rows
    return [ref[pl.ds(start + k, rows // 3, stride=3), :] for k in range(3)]


def put_thirds(ref, parts):
    for k in range(3):
        ref[pl.ds(k, parts[k].shape[0], stride=3), :] = parts[k]


def interleave(scratch, index, even, odd):
    scratch[index, pl.ds(0, even.shape[0], stride=2), :] = even
    scratch[index, pl.ds(1, odd.shape[0], stride=2), :] = odd


def whole_of(scratch, first, second):
    a, b, c = first
    d, e, f = second
    low = low_lanes(a.shape)
    sb, sc, sd, se = swap(b), swap(c), swap(d), swap(e)
    interleave(scratch, 0, a, jnp.where(low, sb, sc))
    interleave(scratch, 1, jnp.where(low, b, sd), jnp.where(low, sc, e))
    interleave(scratch, 2, jnp.where(low, sd, se), f)
    return jnp.concatenate([scratch[0], scratch[1], scratch[2]], axis=1)


def half_of(scratch, flat):
    a, b, c = flat
    low = low_lanes(a.shape)
    sb, sc = swap(b), swap(c)
    interleave(scratch, 0, a, jnp.where(low, sb, sc))
    interleave(scratch, 1, jnp.where(low, b, 0.0), jnp.where(low, sc, 0.0))
    return jnp.concatenate([scratch[0], scratch[1]], axis=1)


def flat_of(scratch, half):
    scratch[0] = half[:, :LANES]
    scratch[1] = half[:, LANES:]
    pairs = half.shape[0] // 2
    even0 = scratch[0, pl.ds(0, pairs, stride=2), :]
    odd0 = swap(scratch[0, pl.ds(1, pairs, stride=2), :])
    even1 = scratch[1, pl.ds(0, pairs, stride=2), :]
    odd1 = swap(scratch[1, pl.ds(1, pairs, stride=2), :])
    low = low_lanes(even0.shape)
    return [even0, jnp.where(low, even1, odd0), jnp.where(low, odd0, odd1)]


def take_half(whole, first):
    one, two, three = whole[:, :LANES], whole[:, LANES : 2 * LANES], whole[:, 2 * LANES :]
    low = low_lanes(one.shape)
    s2, s3 = swap(two), swap(three)
    head = jnp.where(first, one, jnp.where(low, s2, s3))
    tail = jnp.where(low, jnp.where(first, two, s3), 0.0)
    return jnp.concatenate([head, tail], axis=1)


def is_left():
    return lax.rem(lax.axis_index("shard"), 2) == 0


def gather_rows(left, mine_ref, theirs_ref):
    blocks = []
    for k in range(mine_ref.shape[0]):
        mine, theirs = mine_ref[k], theirs_ref[k]
        blocks += [jnp.where(left, mine, theirs), jnp.where(left, theirs, mine)]
    return jnp.concatenate(blocks, axis=0)


def prepare_kernel(l_stat_ref, r_stat_ref, l_basis_ref, r_basis_ref, got_ref, stat_ref, basis_ref, scratch):
    left = is_left()
    flat_rows = l_stat_ref.shape[0]
    own = pick(left, thirds(l_basis_ref), thirds(r_basis_ref))
    got = thirds(got_ref, 0, flat_rows)
    basis_ref[...] = whole_of(scratch, pick(left, own, got), pick(left, got, own))
    own = pick(left, thirds(l_stat_ref), thirds(r_stat_ref))
    corner = thirds(got_ref, flat_rows, flat_rows // 2)
    placed = [jnp.concatenate([jnp.where(left, 0.0, c), jnp.where(left, c, 0.0)], axis=0) for c in corner]
    known = whole_of(scratch, pick(left, own, placed), pick(left, placed, own))
    half = known.shape[0] // 2
    row = lax.broadcasted_iota(jnp.int32, known.shape, 0)
    column = lax.broadcasted_iota(jnp.int32, known.shape, 1)
    missing = (jnp.where(left, row, column) < half) & (jnp.where(left, column, row) >= half)
    stat_ref[...] = 0.5 * jnp.where(missing, known.T, known)


def iterate(x_ref, steps):
    @pl.loop(0, steps)
    def _(step):
        x = x_ref[...]
        parts = split(x)
        gram = dot_parts(parts, parts, ((1,), (1,)))
        gram_parts = split(gram)
        poly = CUBIC_COEFF * gram + QUINTIC_COEFF * dot_parts(gram_parts, gram_parts)
        x_ref[...] = LINEAR_COEFF * x + dot_parts(split(poly), parts)


def begin_kernel(steps, mine_ref, theirs_ref, stat_ref, basis_ref, grad_ref, new_stat_ref, x_ref):
    left = is_left()
    grad = gather_rows(left, mine_ref, theirs_ref)
    grad_ref[...] = grad
    turned = grad.T
    new_stat = stat_ref[...] + 0.5 * dot(jnp.where(left, grad, turned), jnp.where(left, turned, grad))
    new_stat_ref[...] = new_stat
    power = dot(new_stat, basis_ref[...])
    x_ref[...] = power * (1.0 / jnp.sqrt(jnp.sum(power * power) + NORM_EPS))
    iterate(x_ref, steps)


def end_kernel(steps, start_ref, keep_ref, send_ref, scratch, x_ref):
    left = is_left()
    x_ref[...] = start_ref[...]
    iterate(x_ref, steps)
    x = x_ref[...]
    put_thirds(send_ref, flat_of(scratch, take_half(x, jnp.logical_not(left))))
    put_thirds(keep_ref, flat_of(scratch, take_half(x, left)))


def update_kernel(
    grad_ref, basis_ref, left_ref, right_ref, first_left_ref, one_ref, two_ref, new_one_ref, new_two_ref, mine_ref, theirs_ref, scratch
):
    left = is_left()
    basis_left = jnp.where(left, basis_ref[...], whole_of(scratch, thirds(first_left_ref), thirds(left_ref)))
    left_parts = split(basis_left)
    basis_right = split(half_of(scratch, thirds(right_ref)))
    inner = dot_parts(split(grad_ref[...]), basis_right)
    rotated = flat_of(scratch, dot(basis_left.T, inner))
    ones = thirds(one_ref)
    twos = thirds(two_ref)
    new_one = [BETA_ONE * m + (1.0 - BETA_ONE) * r for m, r in zip(ones, rotated)]
    new_two = [BETA_TWO * v + (1.0 - BETA_TWO) * r * r for v, r in zip(twos, rotated)]
    put_thirds(new_one_ref, new_one)
    put_thirds(new_two_ref, new_two)
    direction = [m / (jnp.sqrt(v) + ADAM_EPS) for m, v in zip(new_one, new_two)]
    outer = dot_parts(left_parts, split(half_of(scratch, direction)))
    partial = dot_parts(split(outer), basis_right, ((1,), (1,)))
    rows = mine_ref.shape[1]
    for k in range(mine_ref.shape[0]):
        even = partial[2 * k * rows : (2 * k + 1) * rows]
        odd = partial[(2 * k + 1) * rows : (2 * k + 2) * rows]
        mine_ref[k] = jnp.where(left, even, odd)
        theirs_ref[k] = jnp.where(left, odd, even)


def stats_kernel(grad_ref, new_stat_ref, left_ref, right_ref, new_left_ref, new_right_ref, scratch):
    left = is_left()
    other = pick(left, thirds(right_ref), thirds(left_ref))
    grad = grad_ref[...]
    turned = grad.T
    a = jnp.where(left, grad, turned)
    b = jnp.where(left, turned, grad)
    new_own = flat_of(scratch, take_half(new_stat_ref[...], left))
    product = flat_of(scratch, dot(b, take_half(a, left)))
    new_other = [0.5 * u + 0.5 * v for u, v in zip(other, product)]
    put_thirds(new_left_ref, pick(left, new_own, new_other))
    put_thirds(new_right_ref, pick(left, new_other, new_own))


def call(kernel, outs, scratch, products, full, name):
    size = full * full
    return pl.pallas_call(
        kernel,
        out_shape=[jax.ShapeDtypeStruct(s, F32) for s in outs],
        scratch_shapes=[pltpu.VMEM(s, F32) for s in scratch],
        compiler_params=pltpu.CompilerParams(vmem_limit_bytes=40 * 1024 * 1024),
        cost_estimate=pl.CostEstimate(flops=int(products * 6 * full * size), bytes_accessed=16 * size, transcendentals=0),
        name=name,
    )


def after(x, *others):
    return lax.optimization_barrier((x, *others))[0]


def local(grads, moment_one, moment_two, left_stat, right_stat, left_basis, right_basis):
    tiles_here, rows_here, full = grads.shape
    size = lax.axis_size("shard")
    flat_rows = full * (full // 2) // LANES
    flat = (flat_rows, LANES)
    square = (full, full)
    blocks = (tiles_here, rows_here, full)
    parity = lax.axis_index("shard") % 2
    pairs = [(i, i ^ 1) for i in range(size)]
    sides = [list(range(k, size, 2)) for k in range(2)]
    aligned = rows_here % 8 == 0
    strips = blocks if aligned else (1, full // 2, full)

    def exchange(x):
        return lax.all_to_all(x, "shard", split_axis=0, concat_axis=0, axis_index_groups=sides, tiled=True)

    one, two, l_stat, r_stat, l_basis, r_basis = (
        x.reshape(flat) for x in (moment_one, moment_two, left_stat, right_stat, left_basis, right_basis)
    )
    outgoing = jnp.where(
        parity == 0,
        jnp.concatenate([r_basis, r_stat[: flat_rows // 2]], axis=0),
        jnp.concatenate([l_basis, l_stat[flat_rows // 2 :]], axis=0),
    )
    got = lax.ppermute(outgoing, "shard", pairs)
    mine = exchange(after(grads, outgoing))
    theirs = lax.ppermute(mine, "shard", pairs)
    first_left = lax.ppermute(after(l_basis, theirs), "shard", [(i, i + 1) for i in range(0, size, 2)])
    stat, basis = call(prepare_kernel, [square, square], [(3, full, LANES)], 0.1, full, "prepare")(
        l_stat, r_stat, l_basis, r_basis, got
    )
    if not aligned:
        mine, theirs = jnp.where(parity == 0, mine, theirs), jnp.where(parity == 0, theirs, mine)
        merged = jnp.stack([mine, theirs], axis=1).reshape(2, full // 2, full)
        mine = lax.dynamic_slice_in_dim(merged, parity, 1, 0)
        theirs = lax.dynamic_slice_in_dim(merged, 1 - parity, 1, 0)
    grad, new_stat, x = call(functools.partial(begin_kernel, 2), [square] * 3, [], 8, full, "begin")(
        mine, theirs, stat, basis
    )
    new_one, new_two, own_rows, other_rows = call(
        update_kernel, [flat, flat, strips, strips], [(3, full, LANES)], 2, full, "update"
    )(after(grad, x), basis, l_basis, r_basis, first_left, one, two)
    if not aligned:
        top = jnp.where(parity == 0, own_rows, other_rows)
        bottom = jnp.where(parity == 0, other_rows, own_rows)
        merged = jnp.concatenate([top, bottom], axis=1).reshape(tiles_here, 2, rows_here, full)
        own_rows = lax.dynamic_index_in_dim(merged, parity, 1, keepdims=False)
        other_rows = lax.dynamic_index_in_dim(merged, 1 - parity, 1, keepdims=False)
    got_rows = lax.ppermute(other_rows, "shard", pairs)
    keep, send = call(
        functools.partial(end_kernel, NS_ITERS - 2), [flat, flat], [(3, full, LANES), square], 9, full, "end"
    )(after(x, other_rows))
    back = lax.ppermute(send, "shard", pairs)
    update = exchange(after(own_rows, send) + after(got_rows, send))
    new_left, new_right = call(stats_kernel, [flat, flat], [(3, full, LANES)], 1, full, "stats")(
        after(grad, send), new_stat, l_stat, r_stat
    )
    new_l_basis = jnp.where(parity == 0, keep, back)
    new_r_basis = jnp.where(parity == 0, back, keep)
    halves = (new_one, new_two, new_left, new_right, new_l_basis, new_r_basis)
    return (update, *(x.reshape(1, flat_rows * LANES) for x in halves))


def solution(mesh):
    halves = P(("tensor", "shard"), None)
    rows = P("tensor", "shard", None)
    return jax.shard_map(
        local, mesh=mesh, in_specs=(rows,) + (halves,) * 6, out_specs=(rows,) + (halves,) * 6, check_vma=False
    )
```

time: 66.2 us -> 61.3 us (0.926)
  waiting for transfers between devices: 24 us -> 19.4 us
    ppermute x3 -> x5, waiting for transfers between devices: 24 us -> 6.82 us  [the longest x1 6.81 us: local(): theirs = lax.ppermute(mine, 'shard', pairs)]
    all_to_all x2, waiting for transfers between devices: 0.01 us -> 12.6 us  [exchange(): lax.all_to_all(x, 'shard', split_axis=0, concat_axis=0, axis_index_groups...]
    ppermute x3 -> x5, starting transfers between devices: 6.22 us -> 8.62 us  [the longest x1 3.43 us: local(): lax.ppermute(after(l_basis, theirs), 'shard', [(i, i + 1) for i in range(...]
    all_to_all x2, starting transfers between devices: 13.7 us -> 11.3 us  [exchange(): lax.all_to_all(x, 'shard', split_axis=0, concat_axis=0, axis_index_groups...]
    broadcast_in_dim x1 -> x0, local copies, waits for them, and re-layouts: 1.83 us -> none  [local(): jnp.broadcast_to(grads[:, None], (tiles_here, 2, rows_here, full))]
    slice x2 -> x1, local copies, waits for them, and re-layouts: 0.01 us -> 0.98 us  [local(): l_stat[flat_rows // 2:]]
    slice x2 -> x1, local copies, waits for them, and re-layouts: 0.01 us -> 0.92 us  [local(): r_stat[:flat_rows // 2]]
    add x0 -> x1, other arithmetic: none -> 0.74 us  [local(): update = exchange(after(own_rows, send) + after(got_rows, send))]
  transfers between devices with their start and end apart: 5 -> 7, of which waited for: 2 -> 3; matrix products, arithmetic and copies ran while one was open for 1% -> 3% of each run, Pallas kernels for 20% -> 22%
where the time goes in v1:
time: 61.3 us; the launch traced here: 60.9 us
  starting transfers between devices  19.9 us (32%)
  waiting for transfers between devices  19.4 us (32%)
  Pallas kernels  16.5 us (27%)
  local copies, waits for them, and re-layouts  2.65 us (4%)
  other arithmetic  1.65 us (3%)
  between operations  0.82 us (1%)
    all_to_all x2, waiting for transfers between devices, exchange(): lax.all_to_all(x, 'shard', split_axis=0, concat_axis=0, axis_index_groups...  12.6 us
    all_to_all x2, starting transfers between devices, exchange(): lax.all_to_all(x, 'shard', split_axis=0, concat_axis=0, axis_index_groups...  11.3 us
    ppermute x1, waiting for transfers between devices, local(): theirs = lax.ppermute(mine, 'shard', pairs)  6.81 us
    pallas_call x1, Pallas kernels, local(): call(functools.partial(end_kernel, NS_ITERS - 2), [flat, flat], [(3, full...  5.98 us
    pallas_call x1, Pallas kernels, local(): call(functools.partial(begin_kernel, 2), [square] * 3, [], 8, full, 'begin')  5.36 us
    ppermute x1, starting transfers between devices, local(): lax.ppermute(after(l_basis, theirs), 'shard', [(i, i + 1) for i in range(...  3.43 us
    pallas_call x1, Pallas kernels, local(): call(update_kernel, [flat, flat, strips, strips], [(3, full, LANES)], 2,...  2.93 us
    pallas_call x1, Pallas kernels, local(): call(stats_kernel, [flat, flat], [(3, full, LANES)], 1, full, 'stats')  1.69 us
  transfers between devices with their start and end apart: 7, of which 3 were waited for; matrix products, arithmetic and copies ran while one was open for 3% of the time, Pallas kernels for 22%

profile of v1, /device:TPU:0, one launch (start us, length us, event | category | flops | bytes accessed | tf_op | source)
XLA Modules:
  0.0 60.9 jit_solution(2832993984522622670)
XLA Ops:
  0.6 0.0 copy-start
  0.7 0.0 copy-start.1
  0.7 1.0 %slice.14 = f32[1,36864]{1,0:T(1,128)S(1)} slice(f32[1,73728]{1,0:T(1,128)} %param.10), slice={[0:1], [36864:73728]} | slice | bytes 294912 | tf_op jit(solution)/shard_map/slice | solution.py:245
  1.6 0.9 %slice.12 = f32[1,36864]{1,0:T(1,128)S(1)} slice(f32[1,73728]{1,0:T(1,128)} %param.11), slice={[0:1], [0:36864]} | slice | bytes 294912 | tf_op jit(solution)/shard_map/slice | solution.py:244
  2.6 0.0 copy-done
  2.6 0.0 copy-done.1
  2.7 0.0 copy-start.2
  2.7 0.0 copy-start.3
  2.7 6.5 %all-to-all-start = ((f32[4,48,384]{2,1,0:T(8,128)}), f32[4,48,384]{2,1,0:T(8,128)S(1)}, u32[]{:S(2)}, u32[]{:S(2)}) async-start(f32[4,48,384]{2,1,0:T(8,128)} %param.7), calls=%async_computation | async-start | bytes 589824 | tf_op jit(solution)/shard_map/all_to_all | solution.py:237
  9.1 1.5 %collective-permute-start.1 = (f32[864,128]{1,0:T(8,128)S(1)}, f32[864,128]{1,0:T(8,128)S(1)}, u32[]{:S(2)}, u32[]{:S(2)}) collective-permute-start(f32[864,128]{1,0:T(8,128)S(1)} %maximum_select_fusion), channel_id=1, source_target_pairs={{0,4},{4,0},{8,12},{12,8},{16,20},{20,16},{24,28},{28,24},{1,5},{5... | collective-permute-start | bytes 1327112 | tf_op jit(solution)/shard_map/ppermute | solution.py:247
  10.7 8.1 %all-to-all-done.mine_ref = f32[4,48,384]{2,1,0:T(8,128)S(1)} async-done(((f32[4,48,384]{2,1,0:T(8,128)}), f32[4,48,384]{2,1,0:T(8,128)S(1)}, u32[]{:S(2)}, u32[]{:S(2)}) %all-to-all-start) | async-done | bytes 294944 | tf_op jit(solution)/shard_map/all_to_all | solution.py:237
  18.8 1.5 %collective-permute-start = (f32[4,48,384]{2,1,0:T(8,128)S(1)}, f32[4,48,384]{2,1,0:T(8,128)S(1)}, u32[]{:S(2)}, u32[]{:S(2)}) collective-permute-start(f32[4,48,384]{2,1,0:T(8,128)S(1)} %all-to-all-done.mine_ref), channel_id=1, source_target_pairs={{0,4},{4,0},{8,12},{12,8},{16,20},{20,16},{24,28},{28,24},{1,5},{5... | collective-permute-start | bytes 884744 | tf_op jit(solution)/shard_map/ppermute | solution.py:249
  20.3 6.8 %collective-permute-done.theirs_ref = f32[4,48,384]{2,1,0:T(8,128)S(1)} collective-permute-done((f32[4,48,384]{2,1,0:T(8,128)S(1)}, f32[4,48,384]{2,1,0:T(8,128)S(1)}, u32[]{:S(2)}, u32[]{:S(2)}) %collective-permute-start) | collective-permute-done | bytes 294944 | tf_op jit(solution)/shard_map/ppermute | solution.py:249
  27.1 3.4 %collective-permute-start.2 = (f32[576,128]{1,0:T(8,128)S(1)}, f32[576,128]{1,0:T(8,128)S(1)}, u32[]{:S(2)}, u32[]{:S(2)}) collective-permute-start(f32[576,128]{1,0:T(8,128)S(1)} %bitcast.15), channel_id=1, source_target_pairs={{0,4},{8,12},{16,20},{24,28},{1,5},{9,13},{17,21},{25,29},{2,6},{1... | collective-permute-start | bytes 884744 | tf_op jit(solution)/shard_map/ppermute | solution.py:250
  30.5 0.0 collective-permute-done.1.got_ref
  30.5 0.0 copy-done.2
  30.5 0.0 copy-done.3
  30.6 0.5 prepare.1
  31.1 0.0 copy-start.4
  31.1 0.0 copy-start.5
  31.1 5.4 %begin.1 = (f32[384,384]{1,0:T(8,128)S(1)}, f32[384,384]{1,0:T(8,128)S(1)}, f32[384,384]{1,0:T(8,128)S(1)}) custom-call(f32[4,48,384]{2,1,0:T(8,128)S(1)} %all-to-all-done.mine_ref, f32[4,48,384]{2,1,0:T(8,128)S(1)} %collective-permute-done.theirs_ref, f32[384,384]{1,0:T(8,128)S(1)} %get-tuple-element.28.stat_ref, f32[384,384]{1,0:T(8,128)S(1)} %get-tuple-element.29.basis_ref), custom_call_target="tpu_custom_call" | custom-call | flops 2717908992 | bytes 2359296 | tf_op jit(solution)/shard_map/begin/pallas_call | solution.py:259
  36.5 0.0 collective-permute-done.2.first_left_ref
  36.5 0.0 copy-done.4
  36.5 0.0 copy-done.5
  36.5 2.9 %update.1 = (f32[576,128]{1,0:T(8,128)}, f32[576,128]{1,0:T(8,128)}, f32[4,48,384]{2,1,0:T(8,128)S(1)}, f32[4,48,384]{2,1,0:T(8,128)S(1)}) custom-call(f32[384,384]{1,0:T(8,128)S(1)} %get-tuple-element.42.grad_ref, f32[384,384]{1,0:T(8,128)S(1)} %get-tuple-element.29.basis_ref, f32[576,128]{1,0:T(8,128)S(1)} %bitcast.17, f32[576,128]{1,0:T(8,128)S(1)} %bitcast.20, ...), custom_call_target="tpu_custom_call" | custom-call | flops 679477248 | bytes 2359296 | tf_op jit(solution)/shard_map/update/pallas_call | solution.py:262
  39.5 1.4 %collective-permute-start.3 = (f32[4,48,384]{2,1,0:T(8,128)S(1)}, f32[4,48,384]{2,1,0:T(8,128)S(1)}, u32[]{:S(2)}, u32[]{:S(2)}) collective-permute-start(f32[4,48,384]{2,1,0:T(8,128)S(1)} %get-tuple-element.35), channel_id=1, source_target_pairs={{0,4},{4,0},{8,12},{12,8},{16,20},{20,16},{24,28},{28,24},{1,5},{5... | collective-permute-start | bytes 884744 | tf_op jit(solution)/shard_map/ppermute | solution.py:271
  40.9 6.0 %end.1 = (f32[576,128]{1,0:T(8,128)S(1)}, f32[576,128]{1,0:T(8,128)S(1)}) custom-call(f32[384,384]{1,0:T(8,128)S(1)} %get-tuple-element.36.start_ref), custom_call_target="tpu_custom_call" | custom-call | flops 3057647616 | bytes 2359296 | tf_op jit(solution)/shard_map/end/pallas_call | solution.py:272
  46.9 0.7 %collective-permute-start.4 = (f32[576,128]{1,0:T(8,128)S(1)}, f32[576,128]{1,0:T(8,128)S(1)}, u32[]{:S(2)}, u32[]{:S(2)}) collective-permute-start(f32[576,128]{1,0:T(8,128)S(1)} %get-tuple-element.37), channel_id=1, source_target_pairs={{0,4},{4,0},{8,12},{12,8},{16,20},{20,16},{24,28},{28,24},{1,5},{5... | collective-permute-start | bytes 884744 | tf_op jit(solution)/shard_map/ppermute | solution.py:275
  47.6 0.0 collective-permute-done.3
  47.6 0.7 %add.8 = f32[4,48,384]{2,1,0:T(8,128)} add(f32[4,48,384]{2,1,0:T(8,128)S(1)} %get-tuple-element.38, f32[4,48,384]{2,1,0:T(8,128)S(1)} %collective-permute-done.3) | non-fusion elementwise | flops 73728 | bytes 884736 | tf_op jit(solution)/shard_map/add | solution.py:276
  48.4 4.8 %all-to-all-start.1 = ((f32[4,48,384]{2,1,0:T(8,128)}), f32[4,48,384]{2,1,0:T(8,128)S(1)}, u32[]{:S(2)}, u32[]{:S(2)}) async-start(f32[4,48,384]{2,1,0:T(8,128)} %add.8), calls=%async_computation.1 | async-start | bytes 589824 | tf_op jit(solution)/shard_map/all_to_all | solution.py:237
  53.2 1.7 %stats.1 = (f32[576,128]{1,0:T(8,128)}, f32[576,128]{1,0:T(8,128)}) custom-call(f32[384,384]{1,0:T(8,128)S(1)} %get-tuple-element.42.grad_ref, f32[384,384]{1,0:T(8,128)S(1)} %get-tuple-element.43.new_stat_ref, f32[576,128]{1,0:T(8,128)S(1)} %bitcast.22, f32[576,128]{1,0:T(8,128)S(1)} %bitcast.24), custom_call_target="tpu_custom_call" | custom-call | flops 339738624 | bytes 2359296 | tf_op jit(solution)/shard_map/stats/pallas_call | solution.py:277
  54.8 0.0 collective-permute-done.4
  54.9 0.9 %broadcast_select_fusion = (f32[576,128]{1,0:T(8,128)}, f32[576,128]{1,0:T(8,128)}) fusion(f32[576,128]{1,0:T(8,128)S(1)} %collective-permute-done.4, f32[576,128]{1,0:T(8,128)S(1)} %get-tuple-element.46, pred[]{:T(512)S(6)} %eq.4), kind=kLoop, calls=%fused_computation.1 | loop fusion | flops 147456 | bytes 1179649 | tf_op jit(solution)/shard_map/jit(_where)/select_n | solution.py:281
  55.7 4.5 %all-to-all-done.1 = f32[4,48,384]{2,1,0:T(8,128)S(1)} async-done(((f32[4,48,384]{2,1,0:T(8,128)}), f32[4,48,384]{2,1,0:T(8,128)S(1)}, u32[]{:S(2)}, u32[]{:S(2)}) %all-to-all-start.1) | async-done | bytes 294944 | tf_op jit(solution)/shard_map/all_to_all | solution.py:237
  60.2 0.7 %copy.15 = f32[4,48,384]{2,1,0:T(8,128)} copy(f32[4,48,384]{2,1,0:T(8,128)S(1)} %all-to-all-done.1) | data formatting | bytes 589824
  (1 shorter events, 0.0 us)
Async XLA Ops:
  0.6 1.9 %copy-start = (f32[1,73728]{1,0:T(1,128)S(1)}, f32[1,73728]{1,0:T(1,128)}, u32[]{:S(2)}) copy-start(f32[1,73728]{1,0:T(1,128)} %param.12) | copy-start | bytes 884740
  0.7 1.9 %copy-start.1 = (f32[1,73728]{1,0:T(1,128)S(1)}, f32[1,73728]{1,0:T(1,128)}, u32[]{:S(2)}) copy-start(f32[1,73728]{1,0:T(1,128)} %param.13) | copy-start | bytes 884740
  2.7 27.9 %copy-start.2 = (f32[1,73728]{1,0:T(1,128)S(1)}, f32[1,73728]{1,0:T(1,128)}, u32[]{:S(2)}) copy-start(f32[1,73728]{1,0:T(1,128)} %param.10) | copy-start | bytes 884740
  2.7 27.9 %copy-start.3 = (f32[1,73728]{1,0:T(1,128)S(1)}, f32[1,73728]{1,0:T(1,128)}, u32[]{:S(2)}) copy-start(f32[1,73728]{1,0:T(1,128)} %param.11) | copy-start | bytes 884740
  2.7 16.1 %all-to-all-start = ((f32[4,48,384]{2,1,0:T(8,128)}), f32[4,48,384]{2,1,0:T(8,128)S(1)}, u32[]{:S(2)}, u32[]{:S(2)}) async-start(f32[4,48,384]{2,1,0:T(8,128)} %param.7), calls=%async_computation | async-start | bytes 589824 | tf_op jit(solution)/shard_map/all_to_all | solution.py:237
  9.1 21.4 %collective-permute-start.1 = (f32[864,128]{1,0:T(8,128)S(1)}, f32[864,128]{1,0:T(8,128)S(1)}, u32[]{:S(2)}, u32[]{:S(2)}) collective-permute-start(f32[864,128]{1,0:T(8,128)S(1)} %maximum_select_fusion), channel_id=1, source_target_pairs={{0,4},{4,0},{8,12},{12,8},{16,20},{20,16},{24,28},{28,24},{1,5},{5... | collective-permute-start | bytes 1327112 | tf_op jit(solution)/shard_map/ppermute | solution.py:247
  18.8 8.3 %collective-permute-start = (f32[4,48,384]{2,1,0:T(8,128)S(1)}, f32[4,48,384]{2,1,0:T(8,128)S(1)}, u32[]{:S(2)}, u32[]{:S(2)}) collective-permute-start(f32[4,48,384]{2,1,0:T(8,128)S(1)} %all-to-all-done.mine_ref), channel_id=1, source_target_pairs={{0,4},{4,0},{8,12},{12,8},{16,20},{20,16},{24,28},{28,24},{1,5},{5... | collective-permute-start | bytes 884744 | tf_op jit(solution)/shard_map/ppermute | solution.py:249
  27.1 9.4 %collective-permute-start.2 = (f32[576,128]{1,0:T(8,128)S(1)}, f32[576,128]{1,0:T(8,128)S(1)}, u32[]{:S(2)}, u32[]{:S(2)}) collective-permute-start(f32[576,128]{1,0:T(8,128)S(1)} %bitcast.15), channel_id=1, source_target_pairs={{0,4},{8,12},{16,20},{24,28},{1,5},{9,13},{17,21},{25,29},{2,6},{1... | collective-permute-start | bytes 884744 | tf_op jit(solution)/shard_map/ppermute | solution.py:250
  31.1 5.4 %copy-start.4 = (f32[1,73728]{1,0:T(1,128)S(1)}, f32[1,73728]{1,0:T(1,128)}, u32[]{:S(2)}) copy-start(f32[1,73728]{1,0:T(1,128)} %param.8) | copy-start | bytes 884740
  31.1 5.4 %copy-start.5 = (f32[1,73728]{1,0:T(1,128)S(1)}, f32[1,73728]{1,0:T(1,128)}, u32[]{:S(2)}) copy-start(f32[1,73728]{1,0:T(1,128)} %param.9) | copy-start | bytes 884740
  39.5 8.1 %collective-permute-start.3 = (f32[4,48,384]{2,1,0:T(8,128)S(1)}, f32[4,48,384]{2,1,0:T(8,128)S(1)}, u32[]{:S(2)}, u32[]{:S(2)}) collective-permute-start(f32[4,48,384]{2,1,0:T(8,128)S(1)} %get-tuple-element.35), channel_id=1, source_target_pairs={{0,4},{4,0},{8,12},{12,8},{16,20},{20,16},{24,28},{28,24},{1,5},{5... | collective-permute-start | bytes 884744 | tf_op jit(solution)/shard_map/ppermute | solution.py:271
  46.9 8.0 %collective-permute-start.4 = (f32[576,128]{1,0:T(8,128)S(1)}, f32[576,128]{1,0:T(8,128)S(1)}, u32[]{:S(2)}, u32[]{:S(2)}) collective-permute-start(f32[576,128]{1,0:T(8,128)S(1)} %get-tuple-element.37), channel_id=1, source_target_pairs={{0,4},{4,0},{8,12},{12,8},{16,20},{20,16},{24,28},{28,24},{1,5},{5... | collective-permute-start | bytes 884744 | tf_op jit(solution)/shard_map/ppermute | solution.py:275
  48.4 11.8 %all-to-all-start.1 = ((f32[4,48,384]{2,1,0:T(8,128)}), f32[4,48,384]{2,1,0:T(8,128)S(1)}, u32[]{:S(2)}, u32[]{:S(2)}) async-start(f32[4,48,384]{2,1,0:T(8,128)} %add.8), calls=%async_computation.1 | async-start | bytes 589824 | tf_op jit(solution)/shard_map/all_to_all | solution.py:237

commit v2 on v1

--- a/solution.py
+++ b/solution.py
@@ -107,12 +107,75 @@
     return lax.rem(lax.axis_index("shard"), 2) == 0
 
 
-def gather_rows(left, mine_ref, theirs_ref):
-    blocks = []
-    for k in range(mine_ref.shape[0]):
-        mine, theirs = mine_ref[k], theirs_ref[k]
-        blocks += [jnp.where(left, mine, theirs), jnp.where(left, theirs, mine)]
-    return jnp.concatenate(blocks, axis=0)
+def pack_kernel(hops, l_stat_ref, r_stat_ref, l_basis_ref, r_basis_ref, grads_ref, *refs):
+    out_ref, piece_refs, (corner, small, sems) = refs[0], refs[1 : 1 + len(hops)], refs[1 + len(hops) :]
+    left = is_left()
+    flat_rows = l_basis_ref.shape[0]
+    half_rows = flat_rows // 2
+    rows = grads_ref.shape[1]
+    here = lax.axis_index("shard") // 2
+
+    def copies(basis_ref, stat_ref, start):
+        return [
+            pltpu.make_async_copy(stat_ref.at[pl.ds(start, half_rows)], corner, sems.at[0]),
+            pltpu.make_async_copy(basis_ref, out_ref.at[pl.ds(0, flat_rows)], sems.at[1]),
+        ]
+
+    @pl.when(left)
+    def _():
+        for copy in copies(r_basis_ref, r_stat_ref, 0):
+            copy.start()
+
+    @pl.when(jnp.logical_not(left))
+    def _():
+        for copy in copies(l_basis_ref, l_stat_ref, half_rows):
+            copy.start()
+
+    more = []
+    for number, (hop, piece_ref) in enumerate(zip(hops, piece_refs)):
+        more.append(pltpu.make_async_copy(grads_ref.at[here ^ hop], piece_ref, sems.at[2 + number]))
+    if hops:
+        start = flat_rows + corner_rows(flat_rows)
+        for k in range(grads_ref.shape[2] // LANES):
+            source = grads_ref.at[here, :, pl.ds(k * LANES, LANES)]
+            more.append(
+                pltpu.make_async_copy(source, out_ref.at[pl.ds(start + k * rows, rows)], sems.at[2 + len(hops) + k])
+            )
+    for copy in more:
+        copy.start()
+    first, second = copies(l_basis_ref, l_stat_ref, half_rows)
+    first.wait()
+    third = half_rows // 9
+    a, b, c = thirds(corner)
+    low = low_lanes((third, LANES))
+    middle = slice(third, 2 * third)
+    small[pl.ds(0, third)] = jnp.where(low, a[:third], b[:third])
+    small[pl.ds(third, third)] = a[middle]
+    small[pl.ds(2 * third, third)] = jnp.where(low, swap(b[middle]), swap(c[middle]))
+    small[pl.ds(3 * third, 3 * third)] = corner[pl.ds(6 * third, 3 * third)]
+    last = pltpu.make_async_copy(small, out_ref.at[pl.ds(flat_rows, corner_rows(flat_rows))], sems.at[0])
+    last.start()
+    for copy in [second, *more, last]:
+        copy.wait()
+
+
+def corner_rows(flat_rows):
+    return flat_rows // 3
+
+
+def unpack_corner(got_ref, start, count):
+    third = count // 6
+    small = got_ref[pl.ds(start, third), :]
+    even = got_ref[pl.ds(start + third, third), :]
+    odd = swap(got_ref[pl.ds(start + 2 * third, third), :])
+    a, b, c = thirds(got_ref, start + 3 * third, 3 * third)
+    low = low_lanes(small.shape)
+    zero = jnp.zeros_like(small)
+    return [
+        jnp.concatenate([jnp.where(low, small, zero), even, a], axis=0),
+        jnp.concatenate([jnp.where(low, zero, small), jnp.where(low, zero, odd), b], axis=0),
+        jnp.concatenate([zero, jnp.where(low, odd, zero), c], axis=0),
+    ]
 
 
 def prepare_kernel(l_stat_ref, r_stat_ref, l_basis_ref, r_basis_ref, got_ref, stat_ref, basis_ref, scratch):
@@ -122,14 +185,23 @@
     got = thirds(got_ref, 0, flat_rows)
     basis_ref[...] = whole_of(scratch, pick(left, own, got), pick(left, got, own))
     own = pick(left, thirds(l_stat_ref), thirds(r_stat_ref))
-    corner = thirds(got_ref, flat_rows, flat_rows // 2)
+    corner = unpack_corner(got_ref, flat_rows, corner_rows(flat_rows))
     placed = [jnp.concatenate([jnp.where(left, 0.0, c), jnp.where(left, c, 0.0)], axis=0) for c in corner]
     known = whole_of(scratch, pick(left, own, placed), pick(left, placed, own))
     half = known.shape[0] // 2
+    part = half // 3
     row = lax.broadcasted_iota(jnp.int32, known.shape, 0)
     column = lax.broadcasted_iota(jnp.int32, known.shape, 1)
     missing = (jnp.where(left, row, column) < half) & (jnp.where(left, column, row) >= half)
+    offset = jnp.where(left, half, 0)
+    row, column = row - offset, column - offset
+    limit = jnp.where(row < part, part, 2 * part)
+    missing |= (row >= 0) & (row < 2 * part) & (column < half) & (column >= limit)
     stat_ref[...] = 0.5 * jnp.where(missing, known.T, known)
+
+
+def place_rows(grad_ref, block, rows, value):
+    grad_ref[pl.ds(pl.multiple_of(block * rows, 8), rows), :] = value
 
 
 def iterate(x_ref, steps):
@@ -143,10 +215,26 @@
         x_ref[...] = LINEAR_COEFF * x + dot_parts(split(poly), parts)
 
 
-def begin_kernel(steps, mine_ref, theirs_ref, stat_ref, basis_ref, grad_ref, new_stat_ref, x_ref):
-    left = is_left()
-    grad = gather_rows(left, mine_ref, theirs_ref)
-    grad_ref[...] = grad
+def begin_kernel(steps, hops, *refs):
+    left = is_left()
+    if hops:
+        grads_ref, got_ref, *rest = refs
+        mine_refs, theirs_refs = rest[: len(hops)], rest[len(hops) : 2 * len(hops)]
+        stat_ref, basis_ref, grad_ref, new_stat_ref, x_ref = rest[2 * len(hops) :]
+        rows = grads_ref.shape[1]
+        here = lax.axis_index("shard") // 2
+        parity = lax.axis_index("shard") % 2
+        start = got_ref.shape[0] - grad_ref.shape[1] // LANES * rows
+        received = [got_ref[pl.ds(start + k * rows, rows), :] for k in range(grad_ref.shape[1] // LANES)]
+        place_rows(grad_ref, 2 * here + parity, rows, grads_ref[here])
+        place_rows(grad_ref, 2 * here + 1 - parity, rows, jnp.concatenate(received, axis=1))
+        for hop, mine, theirs in zip(hops, mine_refs, theirs_refs):
+            place_rows(grad_ref, 2 * (here ^ hop) + parity, rows, mine[...])
+            place_rows(grad_ref, 2 * (here ^ hop) + 1 - parity, rows, theirs[...])
+    else:
+        whole_ref, stat_ref, basis_ref, grad_ref, new_stat_ref, x_ref = refs
+        grad_ref[...] = whole_ref[...]
+    grad = grad_ref[...]
     turned = grad.T
     new_stat = stat_ref[...] + 0.5 * dot(jnp.where(left, grad, turned), jnp.where(left, turned, grad))
     new_stat_ref[...] = new_stat
@@ -165,7 +253,20 @@
 
 
 def update_kernel(
-    grad_ref, basis_ref, left_ref, right_ref, first_left_ref, one_ref, two_ref, new_one_ref, new_two_ref, mine_ref, theirs_ref, scratch
+    hops,
+    grad_ref,
+    basis_ref,
+    left_ref,
+    right_ref,
+    first_left_ref,
+    one_ref,
+    two_ref,
+    new_one_ref,
+    new_two_ref,
+    mine_ref,
+    theirs_ref,
+    scratch,
+    partial_ref,
 ):
     left = is_left()
     basis_left = jnp.where(left, basis_ref[...], whole_of(scratch, thirds(first_left_ref), thirds(left_ref)))
@@ -181,13 +282,52 @@
     put_thirds(new_two_ref, new_two)
     direction = [m / (jnp.sqrt(v) + ADAM_EPS) for m, v in zip(new_one, new_two)]
     outer = dot_parts(left_parts, split(half_of(scratch, direction)))
-    partial = dot_parts(split(outer), basis_right, ((1,), (1,)))
+    partial_ref[...] = dot_parts(split(outer), basis_right, ((1,), (1,)))
     rows = mine_ref.shape[1]
-    for k in range(mine_ref.shape[0]):
-        even = partial[2 * k * rows : (2 * k + 1) * rows]
-        odd = partial[(2 * k + 1) * rows : (2 * k + 2) * rows]
-        mine_ref[k] = jnp.where(left, even, odd)
-        theirs_ref[k] = jnp.where(left, odd, even)
+    here = lax.axis_index("shard") // 2
+    parity = lax.axis_index("shard") % 2
+    for k, hop in enumerate((0, *hops)):
+        block = 2 * (here ^ hop) if hops else 0
+        mine_ref[k] = partial_ref[pl.ds(pl.multiple_of((block + parity) * rows, 8), rows), :]
+        theirs_ref[k] = partial_ref[pl.ds(pl.multiple_of((block + 1 - parity) * rows, 8), rows), :]
+
+
+def add_kernel(mine_ref, theirs_ref, *out_refs):
+    for k, out_ref in enumerate(out_refs):
+        out_ref[...] = mine_ref[k] + theirs_ref[k]
+
+
+def finish_kernel(hops, keep_ref, back_ref, *refs):
+    count = 1 + len(hops)
+    rows_refs = refs[:count]
+    update_ref, new_left_ref, new_right_ref, sems = refs[count:]
+    left = is_left()
+    here = lax.axis_index("shard") // 2
+
+    def copies(own_ref, other_ref):
+        return [
+            pltpu.make_async_copy(keep_ref, own_ref, sems.at[0]),
+            pltpu.make_async_copy(back_ref, other_ref, sems.at[1]),
+        ]
+
+    @pl.when(left)
+    def _():
+        for copy in copies(new_left_ref, new_right_ref):
+            copy.start()
+
+    @pl.when(jnp.logical_not(left))
+    def _():
+        for copy in copies(new_right_ref, new_left_ref):
+            copy.start()
+
+    rows = [
+        pltpu.make_async_copy(rows_refs[k], update_ref.at[here ^ hop], sems.at[2 + k])
+        for k, hop in enumerate((0, *hops))
+    ]
+    for copy in rows:
+        copy.start()
+    for copy in rows + copies(new_left_ref, new_right_ref):
+        copy.wait()
 
 
 def stats_kernel(grad_ref, new_stat_ref, left_ref, right_ref, new_left_ref, new_right_ref, scratch):
@@ -204,16 +344,24 @@
     put_thirds(new_right_ref, pick(left, new_other, new_own))
 
 
-def call(kernel, outs, scratch, products, full, name):
+def call(kernel, outs, scratch, products, full, name, copies=0, **specs):
     size = full * full
+    scratch = [pltpu.VMEM(s, F32) for s in scratch]
+    if copies:
+        scratch.append(pltpu.SemaphoreType.DMA((copies,)))
     return pl.pallas_call(
         kernel,
         out_shape=[jax.ShapeDtypeStruct(s, F32) for s in outs],
-        scratch_shapes=[pltpu.VMEM(s, F32) for s in scratch],
+        scratch_shapes=scratch,
         compiler_params=pltpu.CompilerParams(vmem_limit_bytes=40 * 1024 * 1024),
         cost_estimate=pl.CostEstimate(flops=int(products * 6 * full * size), bytes_accessed=16 * size, transcendentals=0),
         name=name,
-    )
+        **specs,
+    )
+
+
+def anywhere(count):
+    return [pl.BlockSpec(memory_space=pl.ANY)] * count
 
 
 def after(x, *others):
@@ -226,59 +374,94 @@
     flat_rows = full * (full // 2) // LANES
     flat = (flat_rows, LANES)
     square = (full, full)
-    blocks = (tiles_here, rows_here, full)
+    block = (rows_here, full)
     parity = lax.axis_index("shard") % 2
     pairs = [(i, i ^ 1) for i in range(size)]
     sides = [list(range(k, size, 2)) for k in range(2)]
-    aligned = rows_here % 8 == 0
-    strips = blocks if aligned else (1, full // 2, full)
+    near = size in (4, 8) and rows_here % 8 == 0
+    hops = {4: (1,), 8: (2, 3, 1)}[size] if near else ()
+    strips = (tiles_here, *block) if near else (1, full // 2, full)
 
     def exchange(x):
         return lax.all_to_all(x, "shard", split_axis=0, concat_axis=0, axis_index_groups=sides, tiled=True)
 
+    def hop_by(x, hop):
+        return lax.ppermute(x, "shard", [(i, i ^ (2 * hop)) for i in range(size)])
+
+    def partner(x):
+        return lax.ppermute(x, "shard", pairs)
+
     one, two, l_stat, r_stat, l_basis, r_basis = (
         x.reshape(flat) for x in (moment_one, moment_two, left_stat, right_stat, left_basis, right_basis)
     )
-    outgoing = jnp.where(
-        parity == 0,
-        jnp.concatenate([r_basis, r_stat[: flat_rows // 2]], axis=0),
-        jnp.concatenate([l_basis, l_stat[flat_rows // 2 :]], axis=0),
-    )
-    got = lax.ppermute(outgoing, "shard", pairs)
-    mine = exchange(after(grads, outgoing))
-    theirs = lax.ppermute(mine, "shard", pairs)
-    first_left = lax.ppermute(after(l_basis, theirs), "shard", [(i, i + 1) for i in range(0, size, 2)])
+    count = corner_rows(flat_rows)
+    outgoing_rows = flat_rows + count + (rows_here * (full // LANES) if near else 0)
+    outgoing, *pieces = call(
+        functools.partial(pack_kernel, hops),
+        [(outgoing_rows, LANES)] + [block] * len(hops),
+        [(flat_rows // 2, LANES), (count, LANES)],
+        0.1,
+        full,
+        "pack",
+        copies=2 + len(hops) + full // LANES,
+        in_specs=anywhere(5),
+        out_specs=anywhere(1 + len(hops)),
+    )(l_stat, r_stat, l_basis, r_basis, grads)
+    got = partner(outgoing)
+    if near:
+        mine = [hop_by(piece, hop) for hop, piece in zip(hops, pieces)]
+        theirs = [partner(x) for x in mine]
+        rows = (grads, got, *mine, *theirs)
+        last = theirs
+    else:
+        mine = exchange(grads)
+        theirs = partner(mine)
+        mine, last = jnp.where(parity == 0, mine, theirs), [theirs]
+        rows = (jnp.stack([mine, jnp.where(parity == 0, theirs, mine)], axis=1).reshape(square),)
+    first_left = partner(after(l_basis, *last))
     stat, basis = call(prepare_kernel, [square, square], [(3, full, LANES)], 0.1, full, "prepare")(
         l_stat, r_stat, l_basis, r_basis, got
     )
-    if not aligned:
-        mine, theirs = jnp.where(parity == 0, mine, theirs), jnp.where(parity == 0, theirs, mine)
-        merged = jnp.stack([mine, theirs], axis=1).reshape(2, full // 2, full)
-        mine = lax.dynamic_slice_in_dim(merged, parity, 1, 0)
-        theirs = lax.dynamic_slice_in_dim(merged, 1 - parity, 1, 0)
-    grad, new_stat, x = call(functools.partial(begin_kernel, 2), [square] * 3, [], 8, full, "begin")(
-        mine, theirs, stat, basis
+    grad, new_stat, x = call(functools.partial(begin_kernel, 2, hops), [square] * 3, [], 8, full, "begin")(
+        *rows, stat, basis
     )
     new_one, new_two, own_rows, other_rows = call(
-        update_kernel, [flat, flat, strips, strips], [(3, full, LANES)], 2, full, "update"
+        functools.partial(update_kernel, hops), [flat, flat, strips, strips], [(3, full, LANES), square], 2, full, "update"
     )(after(grad, x), basis, l_basis, r_basis, first_left, one, two)
-    if not aligned:
+    if not near:
         top = jnp.where(parity == 0, own_rows, other_rows)
         bottom = jnp.where(parity == 0, other_rows, own_rows)
         merged = jnp.concatenate([top, bottom], axis=1).reshape(tiles_here, 2, rows_here, full)
         own_rows = lax.dynamic_index_in_dim(merged, parity, 1, keepdims=False)
         other_rows = lax.dynamic_index_in_dim(merged, 1 - parity, 1, keepdims=False)
-    got_rows = lax.ppermute(other_rows, "shard", pairs)
+    got_rows = partner(other_rows)
     keep, send = call(
         functools.partial(end_kernel, NS_ITERS - 2), [flat, flat], [(3, full, LANES), square], 9, full, "end"
     )(after(x, other_rows))
-    back = lax.ppermute(send, "shard", pairs)
-    update = exchange(after(own_rows, send) + after(got_rows, send))
+    back = partner(send)
+    if near:
+        kept, *sums = call(add_kernel, [block] * (1 + len(hops)), [], 0.1, full, "add")(
+            after(own_rows, send), after(got_rows, send)
+        )
+        returned = [hop_by(x, hop) for hop, x in zip(hops, sums)]
+        update, new_l_basis, new_r_basis = call(
+            functools.partial(finish_kernel, hops),
+            [grads.shape, flat, flat],
+            [],
+            0.1,
+            full,
+            "finish",
+            copies=3 + len(hops),
+            in_specs=anywhere(3 + len(hops)),
+            out_specs=anywhere(3),
+        )(keep, back, kept, *returned)
+    else:
+        update = exchange(after(own_rows, send) + after(got_rows, send))
+        new_l_basis = jnp.where(parity == 0, keep, back)
+        new_r_basis = jnp.where(parity == 0, back, keep)
     new_left, new_right = call(stats_kernel, [flat, flat], [(3, full, LANES)], 1, full, "stats")(
         after(grad, send), new_stat, l_stat, r_stat
     )
-    new_l_basis = jnp.where(parity == 0, keep, back)
-    new_r_basis = jnp.where(parity == 0, back, keep)
     halves = (new_one, new_two, new_left, new_right, new_l_basis, new_r_basis)
     return (update, *(x.reshape(1, flat_rows * LANES) for x in halves))
 

time: 61.3 us -> 55.8 us (0.910)
  waiting for transfers between devices: 19.4 us -> 11.8 us
  Pallas kernels: 16.5 us -> 20.6 us
  other arithmetic: 1.65 us -> 0 us
  starting transfers between devices: 19.9 us -> 18.4 us
  local copies, waits for them, and re-layouts: 2.65 us -> 3.87 us
    all_to_all x2 -> x0, waiting for transfers between devices: 12.6 us -> none  [exchange(): lax.all_to_all(x, 'shard', split_axis=0, concat_axis=0, axis_index_groups...]
    all_to_all x2 -> x0, starting transfers between devices: 11.3 us -> none  [exchange(): lax.all_to_all(x, 'shard', split_axis=0, concat_axis=0, axis_index_groups...]
    ppermute x5 -> x13, starting transfers between devices: 8.62 us -> 18.4 us  [the longest x7 9.95 us: partner(): return lax.ppermute(x, 'shard', pairs)]
    ppermute x5 -> x13, waiting for transfers between devices: 6.82 us -> 11.8 us  [the longest x6 7.33 us: hop_by(): return lax.ppermute(x, 'shard', [(i, i ^ 2 * hop) for i in range(size)])]
    unnamed x13 -> x20, local copies, waits for them, and re-layouts: 0.75 us -> 3.87 us
    pallas_call x2 -> x5, Pallas kernels: 8.29 us -> 11.1 us  [the longest x1 5.41 us: local(): call(functools.partial(begin_kernel, 2, hops), [square] * 3, [], 8, full,...]
    slice x2 -> x0, local copies, waits for them, and re-layouts: 1.9 us -> none  [the longest x1 0.98 us: local(): l_stat[flat_rows // 2:]]
    pallas_call x1, Pallas kernels: 0.54 us -> 1.78 us  [local(): call(prepare_kernel, [square, square], [(3, full, LANES)], 0.1, full, 'pr...]
  transfers between devices with their start and end apart: 7 -> 13, of which waited for: 3 -> 8; matrix products, arithmetic and copies ran while one was open for 3% -> 0% of each run, Pallas kernels for 22% -> 27%
where the time goes in v2:
time: 55.8 us; the launch traced here: 55.4 us
  Pallas kernels  20.6 us (37%)
  starting transfers between devices  18.4 us (33%)
  waiting for transfers between devices  11.8 us (21%)
  local copies, waits for them, and re-layouts  3.87 us (7%)
  between operations  0.76 us (1%)
    ppermute x7, starting transfers between devices, partner(): return lax.ppermute(x, 'shard', pairs)  9.95 us
    ppermute x6, starting transfers between devices, hop_by(): return lax.ppermute(x, 'shard', [(i, i ^ 2 * hop) for i in range(size)])  8.41 us
    ppermute x6, waiting for transfers between devices, hop_by(): return lax.ppermute(x, 'shard', [(i, i ^ 2 * hop) for i in range(size)])  7.33 us
    pallas_call x1, Pallas kernels, local(): call(functools.partial(end_kernel, NS_ITERS - 2), [flat, flat], [(3, full...  5.97 us
    pallas_call x1, Pallas kernels, local(): call(functools.partial(begin_kernel, 2, hops), [square] * 3, [], 8, full,...  5.41 us
    ppermute x7, waiting for transfers between devices, partner(): return lax.ppermute(x, 'shard', pairs)  4.51 us
    pallas_call x1, Pallas kernels, local(): call(functools.partial(update_kernel, hops), [flat, flat, strips, strips]...  3.97 us
    unnamed x20, local copies, waits for them, and re-layouts  3.87 us
  transfers between devices with their start and end apart: 13, of which 8 were waited for; matrix products, arithmetic and copies ran while one was open for 0% of the time, Pallas kernels for 27%

profile of v2, /device:TPU:0, one launch (start us, length us, event | category | flops | bytes accessed | tf_op | source)
XLA Modules:
  0.0 55.4 jit_solution(5855477360323853982)
XLA Ops:
  0.6 0.0 copy-start
  0.6 1.0 %copy-done = f32[1,73728]{1,0:T(1,128)S(1)} copy-done((f32[1,73728]{1,0:T(1,128)S(1)}, f32[1,73728]{1,0:T(1,128)}, u32[]{:S(2)}) %copy-start) | copy-done | bytes 294936
  1.6 0.0 copy-start.2
  1.6 1.0 %copy-done.2 = f32[1,73728]{1,0:T(1,128)S(1)} copy-done((f32[1,73728]{1,0:T(1,128)S(1)}, f32[1,73728]{1,0:T(1,128)}, u32[]{:S(2)}) %copy-start.2) | copy-done | bytes 294936
  2.6 1.0 %copy-done.4 = f32[1,73728]{1,0:T(1,128)S(1)} copy-done((f32[1,73728]{1,0:T(1,128)S(1)}, f32[1,73728]{1,0:T(1,128)}, u32[]{:S(2)}) %copy-start.4) | copy-done | bytes 294936
  3.5 1.0 %copy-done.6 = f32[4,48,384]{2,1,0:T(8,128)S(1)} copy-done((f32[4,48,384]{2,1,0:T(8,128)S(1)}, f32[4,48,384]{2,1,0:T(8,128)}, u32[]{:S(2)}) %copy-start.6) | copy-done | bytes 294936
  4.5 0.8 %pack.1 = (f32[912,128]{1,0:T(8,128)S(1)}, f32[48,384]{1,0:T(8,128)S(1)}, f32[48,384]{1,0:T(8,128)S(1)}, f32[48,384]{1,0:T(8,128)S(1)}) custom-call(f32[576,128]{1,0:T(8,128)S(1)} %bitcast.12, f32[576,128]{1,0:T(8,128)S(1)} %bitcast.15, f32[576,128]{1,0:T(8,128)} %bitcast.2.l_basis_ref.left_ref, f32[576,128]{1,0:T(8,128)S(1)} %bitcast.18, ...), custom_call_target="tpu_custom_call" | custom-call | flops 33973864 | bytes 2359296 | tf_op jit(solution)/shard_map/pack/pallas_call | solution.py:399
  5.3 3.4 %collective-permute-start = (f32[912,128]{1,0:T(8,128)S(1)}, f32[912,128]{1,0:T(8,128)S(1)}, u32[]{:S(2)}, u32[]{:S(2)}) collective-permute-start(f32[912,128]{1,0:T(8,128)S(1)} %get-tuple-element.37), channel_id=1, source_target_pairs={{0,4},{4,0},{8,12},{12,8},{16,20},{20,16},{24,28},{28,24},{1,5},{5... | collective-permute-start | bytes 1400840 | tf_op jit(solution)/shard_map/ppermute | solution.py:392
  8.7 2.6 %collective-permute-start.1 = (f32[48,384]{1,0:T(8,128)S(1)}, f32[48,384]{1,0:T(8,128)S(1)}, u32[]{:S(2)}, u32[]{:S(2)}) collective-permute-start(f32[48,384]{1,0:T(8,128)S(1)} %get-tuple-element.38), channel_id=1, source_target_pairs={{0,16},{4,20},{8,24},{12,28},{16,0},{20,4},{24,8},{28,12},{1,17},{... | collective-permute-start | bytes 221192 | tf_op jit(solution)/shard_map/ppermute | solution.py:389
  11.3 1.3 %collective-permute-start.2 = (f32[48,384]{1,0:T(8,128)S(1)}, f32[48,384]{1,0:T(8,128)S(1)}, u32[]{:S(2)}, u32[]{:S(2)}) collective-permute-start(f32[48,384]{1,0:T(8,128)S(1)} %get-tuple-element.39), channel_id=1, source_target_pairs={{0,24},{4,28},{8,16},{12,20},{16,8},{20,12},{24,0},{28,4},{1,25},{... | collective-permute-start | bytes 221192 | tf_op jit(solution)/shard_map/ppermute | solution.py:389
  12.7 0.2 collective-permute-start.3
  12.9 3.2 %collective-permute-done.1.refs_2_ = f32[48,384]{1,0:T(8,128)S(1)} collective-permute-done((f32[48,384]{1,0:T(8,128)S(1)}, f32[48,384]{1,0:T(8,128)S(1)}, u32[]{:S(2)}, u32[]{:S(2)}) %collective-permute-start.1) | collective-permute-done | bytes 73760 | tf_op jit(solution)/shard_map/ppermute | solution.py:389
  16.1 0.6 %collective-permute-start.4 = (f32[48,384]{1,0:T(8,128)S(1)}, f32[48,384]{1,0:T(8,128)S(1)}, u32[]{:S(2)}, u32[]{:S(2)}) collective-permute-start(f32[48,384]{1,0:T(8,128)S(1)} %collective-permute-done.1.refs_2_), channel_id=1, source_target_pairs={{0,4},{4,0},{8,12},{12,8},{16,20},{20,16},{24,28},{28,24},{1,5},{5... | collective-permute-start | bytes 221192 | tf_op jit(solution)/shard_map/ppermute | solution.py:392
  16.7 0.9 %collective-permute-done.2.refs_3_ = f32[48,384]{1,0:T(8,128)S(1)} collective-permute-done((f32[48,384]{1,0:T(8,128)S(1)}, f32[48,384]{1,0:T(8,128)S(1)}, u32[]{:S(2)}, u32[]{:S(2)}) %collective-permute-start.2) | collective-permute-done | bytes 73760 | tf_op jit(solution)/shard_map/ppermute | solution.py:389
  17.6 0.5 collective-permute-start.5
  18.1 0.0 collective-permute-done.3.refs_4_
  18.1 1.5 %collective-permute-start.6 = (f32[48,384]{1,0:T(8,128)S(1)}, f32[48,384]{1,0:T(8,128)S(1)}, u32[]{:S(2)}, u32[]{:S(2)}) collective-permute-start(f32[48,384]{1,0:T(8,128)S(1)} %collective-permute-done.3.refs_4_), channel_id=1, source_target_pairs={{0,4},{4,0},{8,12},{12,8},{16,20},{20,16},{24,28},{28,24},{1,5},{5... | collective-permute-start | bytes 221192 | tf_op jit(solution)/shard_map/ppermute | solution.py:392
  19.7 2.2 %collective-permute-done.4.refs_5_ = f32[48,384]{1,0:T(8,128)S(1)} collective-permute-done((f32[48,384]{1,0:T(8,128)S(1)}, f32[48,384]{1,0:T(8,128)S(1)}, u32[]{:S(2)}, u32[]{:S(2)}) %collective-permute-start.4) | collective-permute-done | bytes 73760 | tf_op jit(solution)/shard_map/ppermute | solution.py:392
  21.8 1.5 %collective-permute-done.5.refs_6_ = f32[48,384]{1,0:T(8,128)S(1)} collective-permute-done((f32[48,384]{1,0:T(8,128)S(1)}, f32[48,384]{1,0:T(8,128)S(1)}, u32[]{:S(2)}, u32[]{:S(2)}) %collective-permute-start.5) | collective-permute-done | bytes 73760 | tf_op jit(solution)/shard_map/ppermute | solution.py:392
  23.4 0.8 %collective-permute-done.6.refs_7_ = f32[48,384]{1,0:T(8,128)S(1)} collective-permute-done((f32[48,384]{1,0:T(8,128)S(1)}, f32[48,384]{1,0:T(8,128)S(1)}, u32[]{:S(2)}, u32[]{:S(2)}) %collective-permute-start.6) | collective-permute-done | bytes 73760 | tf_op jit(solution)/shard_map/ppermute | solution.py:392
  24.2 1.7 %collective-permute-start.7 = (f32[576,128]{1,0:T(8,128)}, f32[576,128]{1,0:T(8,128)S(1)}, u32[]{:S(2)}, u32[]{:S(2)}) collective-permute-start(f32[576,128]{1,0:T(8,128)} %bitcast.2.l_basis_ref.left_ref), channel_id=1, source_target_pairs={{0,4},{4,0},{8,12},{12,8},{16,20},{20,16},{24,28},{28,24},{1,5},{5... | collective-permute-start | bytes 884744 | tf_op jit(solution)/shard_map/ppermute | solution.py:392
  25.9 0.0 collective-permute-done.got_ref.refs_1_
  25.9 1.8 %prepare.1 = (f32[384,384]{1,0:T(8,128)S(1)}, f32[384,384]{1,0:T(8,128)S(1)}) custom-call(f32[576,128]{1,0:T(8,128)S(1)} %bitcast.13, f32[576,128]{1,0:T(8,128)S(1)} %bitcast.16, f32[576,128]{1,0:T(8,128)} %bitcast.2.l_basis_ref.left_ref, f32[576,128]{1,0:T(8,128)S(1)} %bitcast.19, f32[912,128]{1,0:T(8,128)S(1)} %collective-permute-done.got_ref.refs_1_), custom_call_target="tpu_custom_call" | custom-call | flops 33973864 | bytes 2359296 | tf_op jit(solution)/shard_map/prepare/pallas_call | solution.py:422
  27.7 0.0 copy-done.7
  27.7 0.0 copy-start.5
  27.7 0.0 copy-start.8
  27.7 0.0 copy-start.9
  27.7 5.4 %begin.1 = (f32[384,384]{1,0:T(8,128)S(1)}, f32[384,384]{1,0:T(8,128)S(1)}, f32[384,384]{1,0:T(8,128)S(1)}) custom-call(f32[4,48,384]{2,1,0:T(8,128)S(1)} %copy-done.7, f32[912,128]{1,0:T(8,128)S(1)} %collective-permute-done.got_ref.refs_1_, f32[48,384]{1,0:T(8,128)S(1)} %collective-permute-done.1.refs_2_, f32[48,384]{1,0:T(8,128)S(1)} %collective-permute-done.2.refs_3_, ...), custom_call_target="tpu_custom_call" | custom-call | flops 2717908992 | bytes 2359296 | tf_op jit(solution)/shard_map/begin/pallas_call | solution.py:425
  33.1 0.0 collective-permute-done.7.first_left_ref
  33.2 0.0 copy-done.5
  33.2 0.0 copy-done.8
  33.2 0.0 copy-done.9
  33.2 4.0 %update.1 = (f32[576,128]{1,0:T(8,128)}, f32[576,128]{1,0:T(8,128)}, f32[4,48,384]{2,1,0:T(8,128)S(1)}, f32[4,48,384]{2,1,0:T(8,128)S(1)}) custom-call(f32[384,384]{1,0:T(8,128)S(1)} %get-tuple-element.61.grad_ref, f32[384,384]{1,0:T(8,128)S(1)} %get-tuple-element.42.refs_9_.basis_ref, f32[576,128]{1,0:T(8,128)} %bitcast.2.l_basis_ref.left_ref, ...), custom_call_target="tpu_custom_call" | custom-call | flops 679477248 | bytes 2359296 | tf_op jit(solution)/shard_map/update/pallas_call | solution.py:428
  37.2 0.9 %collective-permute-start.9 = (f32[4,48,384]{2,1,0:T(8,128)S(1)}, f32[4,48,384]{2,1,0:T(8,128)S(1)}, u32[]{:S(2)}, u32[]{:S(2)}) collective-permute-start(f32[4,48,384]{2,1,0:T(8,128)S(1)} %get-tuple-element.47), channel_id=1, source_target_pairs={{0,4},{4,0},{8,12},{12,8},{16,20},{20,16},{24,28},{28,24},{1,5},{5... | collective-permute-start | bytes 884744 | tf_op jit(solution)/shard_map/ppermute | solution.py:392
  38.0 6.0 %end.1 = (f32[576,128]{1,0:T(8,128)S(1)}, f32[576,128]{1,0:T(8,128)S(1)}) custom-call(f32[384,384]{1,0:T(8,128)S(1)} %get-tuple-element.48.start_ref), custom_call_target="tpu_custom_call" | custom-call | flops 3057647616 | bytes 2359296 | tf_op jit(solution)/shard_map/end/pallas_call | solution.py:438
  44.0 1.3 %collective-permute-start.8 = (f32[576,128]{1,0:T(8,128)S(1)}, f32[576,128]{1,0:T(8,128)S(1)}, u32[]{:S(2)}, u32[]{:S(2)}) collective-permute-start(f32[576,128]{1,0:T(8,128)S(1)} %get-tuple-element.50), channel_id=1, source_target_pairs={{0,4},{4,0},{8,12},{12,8},{16,20},{20,16},{24,28},{28,24},{1,5},{5... | collective-permute-start | bytes 884744 | tf_op jit(solution)/shard_map/ppermute | solution.py:392
  45.3 0.0 collective-permute-done.9.theirs_ref
  45.3 2.7 %collective-permute-start.10 = (f32[48,384]{1,0:T(8,128)S(1)}, f32[48,384]{1,0:T(8,128)S(1)}, u32[]{:S(2)}, u32[]{:S(2)}) collective-permute-start(f32[48,384]{1,0:T(8,128)S(1)} %get-tuple-element.55), channel_id=1, source_target_pairs={{0,16},{4,20},{8,24},{12,28},{16,0},{20,4},{24,8},{28,12},{1,17},{... | collective-permute-start | bytes 221192 | tf_op jit(solution)/shard_map/ppermute | solution.py:389
  48.0 1.4 %collective-permute-start.11 = (f32[48,384]{1,0:T(8,128)S(1)}, f32[48,384]{1,0:T(8,128)S(1)}, u32[]{:S(2)}, u32[]{:S(2)}) collective-permute-start(f32[48,384]{1,0:T(8,128)S(1)} %get-tuple-element.56), channel_id=1, source_target_pairs={{0,24},{4,28},{8,16},{12,20},{16,8},{20,12},{24,0},{28,4},{1,25},{... | collective-permute-start | bytes 221192 | tf_op jit(solution)/shard_map/ppermute | solution.py:389
  49.3 0.2 collective-permute-start.12
  49.6 0.0 copy-done.1
  49.6 0.0 copy-done.3
  49.6 1.7 %stats.1 = (f32[576,128]{1,0:T(8,128)}, f32[576,128]{1,0:T(8,128)}) custom-call(f32[384,384]{1,0:T(8,128)S(1)} %get-tuple-element.61.grad_ref, f32[384,384]{1,0:T(8,128)S(1)} %get-tuple-element.62.new_stat_ref, f32[576,128]{1,0:T(8,128)S(1)} %bitcast.14, f32[576,128]{1,0:T(8,128)S(1)} %bitcast.17), custom_call_target="tpu_custom_call" | custom-call | flops 339738624 | bytes 2359296 | tf_op jit(solution)/shard_map/stats/pallas_call | solution.py:462
  51.3 0.0 collective-permute-done.8.back_ref
  51.3 1.3 %collective-permute-done.10.refs_1_ = f32[48,384]{1,0:T(8,128)S(1)} collective-permute-done((f32[48,384]{1,0:T(8,128)S(1)}, f32[48,384]{1,0:T(8,128)S(1)}, u32[]{:S(2)}, u32[]{:S(2)}) %collective-permute-start.10) | collective-permute-done | bytes 73760 | tf_op jit(solution)/shard_map/ppermute | solution.py:389
  52.6 1.6 %collective-permute-done.11.refs_2_ = f32[48,384]{1,0:T(8,128)S(1)} collective-permute-done((f32[48,384]{1,0:T(8,128)S(1)}, f32[48,384]{1,0:T(8,128)S(1)}, u32[]{:S(2)}, u32[]{:S(2)}) %collective-permute-start.11) | collective-permute-done | bytes 73760 | tf_op jit(solution)/shard_map/ppermute | solution.py:389
  54.3 0.2 collective-permute-done.12.refs_3_
  54.5 1.0 %finish.1 = (f32[4,48,384]{2,1,0:T(8,128)}, f32[576,128]{1,0:T(8,128)}, f32[576,128]{1,0:T(8,128)}) custom-call(f32[576,128]{1,0:T(8,128)S(1)} %get-tuple-element.49.keep_ref, f32[576,128]{1,0:T(8,128)S(1)} %collective-permute-done.8.back_ref, f32[48,384]{1,0:T(8,128)S(1)} %get-tuple-element.54.refs_0_, f32[48,384]{1,0:T(8,128)S(1)} %collective-permute-done.10.refs_1_, ...), custom_call_target="tpu_custom_call" | custom-call | flops 33973864 | bytes 2359296 | tf_op jit(solution)/shard_map/finish/pallas_call | solution.py:447
  (6 shorter events, 0.0 us)
Async XLA Ops:
  0.6 1.0 %copy-start = (f32[1,73728]{1,0:T(1,128)S(1)}, f32[1,73728]{1,0:T(1,128)}, u32[]{:S(2)}) copy-start(f32[1,73728]{1,0:T(1,128)} %param.10) | copy-start | bytes 884740
  1.6 1.0 %copy-start.2 = (f32[1,73728]{1,0:T(1,128)S(1)}, f32[1,73728]{1,0:T(1,128)}, u32[]{:S(2)}) copy-start(f32[1,73728]{1,0:T(1,128)} %param.11) | copy-start | bytes 884740
  2.6 1.0 %copy-start.4 = (f32[1,73728]{1,0:T(1,128)S(1)}, f32[1,73728]{1,0:T(1,128)}, u32[]{:S(2)}) copy-start(f32[1,73728]{1,0:T(1,128)} %param.13) | copy-start | bytes 884740
  3.5 1.0 %copy-start.6 = (f32[4,48,384]{2,1,0:T(8,128)S(1)}, f32[4,48,384]{2,1,0:T(8,128)}, u32[]{:S(2)}) copy-start(f32[4,48,384]{2,1,0:T(8,128)} %refs_0_.1) | copy-start | bytes 884740
  5.3 20.6 %collective-permute-start = (f32[912,128]{1,0:T(8,128)S(1)}, f32[912,128]{1,0:T(8,128)S(1)}, u32[]{:S(2)}, u32[]{:S(2)}) collective-permute-start(f32[912,128]{1,0:T(8,128)S(1)} %get-tuple-element.37), channel_id=1, source_target_pairs={{0,4},{4,0},{8,12},{12,8},{16,20},{20,16},{24,28},{28,24},{1,5},{5... | collective-permute-start | bytes 1400840 | tf_op jit(solution)/shard_map/ppermute | solution.py:392
  8.7 7.4 %collective-permute-start.1 = (f32[48,384]{1,0:T(8,128)S(1)}, f32[48,384]{1,0:T(8,128)S(1)}, u32[]{:S(2)}, u32[]{:S(2)}) collective-permute-start(f32[48,384]{1,0:T(8,128)S(1)} %get-tuple-element.38), channel_id=1, source_target_pairs={{0,16},{4,20},{8,24},{12,28},{16,0},{20,4},{24,8},{28,12},{1,17},{... | collective-permute-start | bytes 221192 | tf_op jit(solution)/shard_map/ppermute | solution.py:389
  11.3 6.3 %collective-permute-start.2 = (f32[48,384]{1,0:T(8,128)S(1)}, f32[48,384]{1,0:T(8,128)S(1)}, u32[]{:S(2)}, u32[]{:S(2)}) collective-permute-start(f32[48,384]{1,0:T(8,128)S(1)} %get-tuple-element.39), channel_id=1, source_target_pairs={{0,24},{4,28},{8,16},{12,20},{16,8},{20,12},{24,0},{28,4},{1,25},{... | collective-permute-start | bytes 221192 | tf_op jit(solution)/shard_map/ppermute | solution.py:389
  12.7 15.0 %copy-start.7 = (f32[4,48,384]{2,1,0:T(8,128)S(1)}, f32[4,48,384]{2,1,0:T(8,128)}, u32[]{:S(2)}) copy-start(f32[4,48,384]{2,1,0:T(8,128)} %refs_0_.1) | copy-start | bytes 884740
  12.7 5.5 %collective-permute-start.3 = (f32[48,384]{1,0:T(8,128)S(1)}, f32[48,384]{1,0:T(8,128)S(1)}, u32[]{:S(2)}, u32[]{:S(2)}) collective-permute-start(f32[48,384]{1,0:T(8,128)S(1)} %get-tuple-element.40), channel_id=1, source_target_pairs={{0,8},{4,12},{8,0},{12,4},{16,24},{20,28},{24,16},{28,20},{1,9},{5... | collective-permute-start | bytes 221192 | tf_op jit(solution)/shard_map/ppermute | solution.py:389
  16.1 5.7 %collective-permute-start.4 = (f32[48,384]{1,0:T(8,128)S(1)}, f32[48,384]{1,0:T(8,128)S(1)}, u32[]{:S(2)}, u32[]{:S(2)}) collective-permute-start(f32[48,384]{1,0:T(8,128)S(1)} %collective-permute-done.1.refs_2_), channel_id=1, source_target_pairs={{0,4},{4,0},{8,12},{12,8},{16,20},{20,16},{24,28},{28,24},{1,5},{5... | collective-permute-start | bytes 221192 | tf_op jit(solution)/shard_map/ppermute | solution.py:392
  17.6 5.7 %collective-permute-start.5 = (f32[48,384]{1,0:T(8,128)S(1)}, f32[48,384]{1,0:T(8,128)S(1)}, u32[]{:S(2)}, u32[]{:S(2)}) collective-permute-start(f32[48,384]{1,0:T(8,128)S(1)} %collective-permute-done.2.refs_3_), channel_id=1, source_target_pairs={{0,4},{4,0},{8,12},{12,8},{16,20},{20,16},{24,28},{28,24},{1,5},{5... | collective-permute-start | bytes 221192 | tf_op jit(solution)/shard_map/ppermute | solution.py:392
  18.1 6.0 %collective-permute-start.6 = (f32[48,384]{1,0:T(8,128)S(1)}, f32[48,384]{1,0:T(8,128)S(1)}, u32[]{:S(2)}, u32[]{:S(2)}) collective-permute-start(f32[48,384]{1,0:T(8,128)S(1)} %collective-permute-done.3.refs_4_), channel_id=1, source_target_pairs={{0,4},{4,0},{8,12},{12,8},{16,20},{20,16},{24,28},{28,24},{1,5},{5... | collective-permute-start | bytes 221192 | tf_op jit(solution)/shard_map/ppermute | solution.py:392
  24.2 9.0 %collective-permute-start.7 = (f32[576,128]{1,0:T(8,128)}, f32[576,128]{1,0:T(8,128)S(1)}, u32[]{:S(2)}, u32[]{:S(2)}) collective-permute-start(f32[576,128]{1,0:T(8,128)} %bitcast.2.l_basis_ref.left_ref), channel_id=1, source_target_pairs={{0,4},{4,0},{8,12},{12,8},{16,20},{20,16},{24,28},{28,24},{1,5},{5... | collective-permute-start | bytes 884744 | tf_op jit(solution)/shard_map/ppermute | solution.py:392
  27.7 5.5 %copy-start.5 = (f32[1,73728]{1,0:T(1,128)S(1)}, f32[1,73728]{1,0:T(1,128)}, u32[]{:S(2)}) copy-start(f32[1,73728]{1,0:T(1,128)} %param.13) | copy-start | bytes 884740
  27.7 5.5 %copy-start.8 = (f32[1,73728]{1,0:T(1,128)S(1)}, f32[1,73728]{1,0:T(1,128)}, u32[]{:S(2)}) copy-start(f32[1,73728]{1,0:T(1,128)} %param.8) | copy-start | bytes 884740
  27.7 5.5 %copy-start.9 = (f32[1,73728]{1,0:T(1,128)S(1)}, f32[1,73728]{1,0:T(1,128)}, u32[]{:S(2)}) copy-start(f32[1,73728]{1,0:T(1,128)} %param.9) | copy-start | bytes 884740
  37.2 8.1 %collective-permute-start.9 = (f32[4,48,384]{2,1,0:T(8,128)S(1)}, f32[4,48,384]{2,1,0:T(8,128)S(1)}, u32[]{:S(2)}, u32[]{:S(2)}) collective-permute-start(f32[4,48,384]{2,1,0:T(8,128)S(1)} %get-tuple-element.47), channel_id=1, source_target_pairs={{0,4},{4,0},{8,12},{12,8},{16,20},{20,16},{24,28},{28,24},{1,5},{5... | collective-permute-start | bytes 884744 | tf_op jit(solution)/shard_map/ppermute | solution.py:392
  44.0 7.3 %collective-permute-start.8 = (f32[576,128]{1,0:T(8,128)S(1)}, f32[576,128]{1,0:T(8,128)S(1)}, u32[]{:S(2)}, u32[]{:S(2)}) collective-permute-start(f32[576,128]{1,0:T(8,128)S(1)} %get-tuple-element.50), channel_id=1, source_target_pairs={{0,4},{4,0},{8,12},{12,8},{16,20},{20,16},{24,28},{28,24},{1,5},{5... | collective-permute-start | bytes 884744 | tf_op jit(solution)/shard_map/ppermute | solution.py:392
  45.3 4.3 %copy-start.1 = (f32[1,73728]{1,0:T(1,128)S(1)}, f32[1,73728]{1,0:T(1,128)}, u32[]{:S(2)}) copy-start(f32[1,73728]{1,0:T(1,128)} %param.10) | copy-start | bytes 884740
  45.3 4.3 %copy-start.3 = (f32[1,73728]{1,0:T(1,128)S(1)}, f32[1,73728]{1,0:T(1,128)}, u32[]{:S(2)}) copy-start(f32[1,73728]{1,0:T(1,128)} %param.11) | copy-start | bytes 884740
  45.3 7.3 %collective-permute-start.10 = (f32[48,384]{1,0:T(8,128)S(1)}, f32[48,384]{1,0:T(8,128)S(1)}, u32[]{:S(2)}, u32[]{:S(2)}) collective-permute-start(f32[48,384]{1,0:T(8,128)S(1)} %get-tuple-element.55), channel_id=1, source_target_pairs={{0,16},{4,20},{8,24},{12,28},{16,0},{20,4},{24,8},{28,12},{1,17},{... | collective-permute-start | bytes 221192 | tf_op jit(solution)/shard_map/ppermute | solution.py:389
  48.0 6.3 %collective-permute-start.11 = (f32[48,384]{1,0:T(8,128)S(1)}, f32[48,384]{1,0:T(8,128)S(1)}, u32[]{:S(2)}, u32[]{:S(2)}) collective-permute-start(f32[48,384]{1,0:T(8,128)S(1)} %get-tuple-element.56), channel_id=1, source_target_pairs={{0,24},{4,28},{8,16},{12,20},{16,8},{20,12},{24,0},{28,4},{1,25},{... | collective-permute-start | bytes 221192 | tf_op jit(solution)/shard_map/ppermute | solution.py:389
  49.3 5.1 %collective-permute-start.12 = (f32[48,384]{1,0:T(8,128)S(1)}, f32[48,384]{1,0:T(8,128)S(1)}, u32[]{:S(2)}, u32[]{:S(2)}) collective-permute-start(f32[48,384]{1,0:T(8,128)S(1)} %get-tuple-element.57), channel_id=1, source_target_pairs={{0,8},{4,12},{8,0},{12,4},{16,24},{20,28},{24,16},{28,20},{1,9},{5... | collective-permute-start | bytes 221192 | tf_op jit(solution)/shard_map/ppermute | solution.py:389

commit v3 on v2

--- a/solution.py
+++ b/solution.py
@@ -108,7 +108,8 @@
 
 
 def pack_kernel(hops, l_stat_ref, r_stat_ref, l_basis_ref, r_basis_ref, grads_ref, *refs):
-    out_ref, piece_refs, (corner, small, sems) = refs[0], refs[1 : 1 + len(hops)], refs[1 + len(hops) :]
+    out_ref, small_ref, *refs = refs
+    piece_refs, (corner, sems) = refs[: len(hops)], refs[len(hops) :]
     left = is_left()
     flat_rows = l_basis_ref.shape[0]
     half_rows = flat_rows // 2
@@ -135,12 +136,10 @@
     for number, (hop, piece_ref) in enumerate(zip(hops, piece_refs)):
         more.append(pltpu.make_async_copy(grads_ref.at[here ^ hop], piece_ref, sems.at[2 + number]))
     if hops:
-        start = flat_rows + corner_rows(flat_rows)
         for k in range(grads_ref.shape[2] // LANES):
             source = grads_ref.at[here, :, pl.ds(k * LANES, LANES)]
-            more.append(
-                pltpu.make_async_copy(source, out_ref.at[pl.ds(start + k * rows, rows)], sems.at[2 + len(hops) + k])
-            )
+            target = out_ref.at[pl.ds(flat_rows + k * rows, rows)]
+            more.append(pltpu.make_async_copy(source, target, sems.at[2 + len(hops) + k]))
     for copy in more:
         copy.start()
     first, second = copies(l_basis_ref, l_stat_ref, half_rows)
@@ -149,13 +148,11 @@
     a, b, c = thirds(corner)
     low = low_lanes((third, LANES))
     middle = slice(third, 2 * third)
-    small[pl.ds(0, third)] = jnp.where(low, a[:third], b[:third])
-    small[pl.ds(third, third)] = a[middle]
-    small[pl.ds(2 * third, third)] = jnp.where(low, swap(b[middle]), swap(c[middle]))
-    small[pl.ds(3 * third, 3 * third)] = corner[pl.ds(6 * third, 3 * third)]
-    last = pltpu.make_async_copy(small, out_ref.at[pl.ds(flat_rows, corner_rows(flat_rows))], sems.at[0])
-    last.start()
-    for copy in [second, *more, last]:
+    small_ref[pl.ds(0, third)] = jnp.where(low, a[:third], b[:third])
+    small_ref[pl.ds(third, third)] = a[middle]
+    small_ref[pl.ds(2 * third, third)] = jnp.where(low, swap(b[middle]), swap(c[middle]))
+    small_ref[pl.ds(3 * third, 3 * third)] = corner[pl.ds(6 * third, 3 * third)]
+    for copy in [second, *more]:
         copy.wait()
 
 
@@ -163,12 +160,12 @@
     return flat_rows // 3
 
 
-def unpack_corner(got_ref, start, count):
-    third = count // 6
-    small = got_ref[pl.ds(start, third), :]
-    even = got_ref[pl.ds(start + third, third), :]
-    odd = swap(got_ref[pl.ds(start + 2 * third, third), :])
-    a, b, c = thirds(got_ref, start + 3 * third, 3 * third)
+def unpack_corner(got_ref):
+    third = got_ref.shape[0] // 6
+    small = got_ref[pl.ds(0, third), :]
+    even = got_ref[pl.ds(third, third), :]
+    odd = swap(got_ref[pl.ds(2 * third, third), :])
+    a, b, c = thirds(got_ref, 3 * third, 3 * third)
     low = low_lanes(small.shape)
     zero = jnp.zeros_like(small)
     return [
@@ -178,14 +175,8 @@
     ]
 
 
-def prepare_kernel(l_stat_ref, r_stat_ref, l_basis_ref, r_basis_ref, got_ref, stat_ref, basis_ref, scratch):
-    left = is_left()
-    flat_rows = l_stat_ref.shape[0]
-    own = pick(left, thirds(l_basis_ref), thirds(r_basis_ref))
-    got = thirds(got_ref, 0, flat_rows)
-    basis_ref[...] = whole_of(scratch, pick(left, own, got), pick(left, got, own))
-    own = pick(left, thirds(l_stat_ref), thirds(r_stat_ref))
-    corner = unpack_corner(got_ref, flat_rows, corner_rows(flat_rows))
+def statistic(left, own, got_ref, scratch):
+    corner = unpack_corner(got_ref)
     placed = [jnp.concatenate([jnp.where(left, 0.0, c), jnp.where(left, c, 0.0)], axis=0) for c in corner]
     known = whole_of(scratch, pick(left, own, placed), pick(left, placed, own))
     half = known.shape[0] // 2
@@ -197,7 +188,7 @@
     row, column = row - offset, column - offset
     limit = jnp.where(row < part, part, 2 * part)
     missing |= (row >= 0) & (row < 2 * part) & (column < half) & (column >= limit)
-    stat_ref[...] = 0.5 * jnp.where(missing, known.T, known)
+    return jnp.where(missing, known.T, known)
 
 
 def place_rows(grad_ref, block, rows, value):
@@ -215,16 +206,16 @@
         x_ref[...] = LINEAR_COEFF * x + dot_parts(split(poly), parts)
 
 
-def begin_kernel(steps, hops, *refs):
-    left = is_left()
+def products_kernel(hops, l_stat_ref, r_stat_ref, l_basis_ref, r_basis_ref, got_ref, *refs):
+    left = is_left()
+    outs = refs[-9:]
+    grad_ref, product_ref, basis_ref, right_ref, inner_ref, own_ref, other_ref, copy_ref, scratch = outs
     if hops:
-        grads_ref, got_ref, *rest = refs
-        mine_refs, theirs_refs = rest[: len(hops)], rest[len(hops) : 2 * len(hops)]
-        stat_ref, basis_ref, grad_ref, new_stat_ref, x_ref = rest[2 * len(hops) :]
+        grads_ref, mine_refs, theirs_refs = refs[0], refs[1 : 1 + len(hops)], refs[1 + len(hops) : 1 + 2 * len(hops)]
         rows = grads_ref.shape[1]
         here = lax.axis_index("shard") // 2
         parity = lax.axis_index("shard") % 2
-        start = got_ref.shape[0] - grad_ref.shape[1] // LANES * rows
+        start = l_basis_ref.shape[0]
         received = [got_ref[pl.ds(start + k * rows, rows), :] for k in range(grad_ref.shape[1] // LANES)]
         place_rows(grad_ref, 2 * here + parity, rows, grads_ref[here])
         place_rows(grad_ref, 2 * here + 1 - parity, rows, jnp.concatenate(received, axis=1))
@@ -232,11 +223,23 @@
             place_rows(grad_ref, 2 * (here ^ hop) + parity, rows, mine[...])
             place_rows(grad_ref, 2 * (here ^ hop) + 1 - parity, rows, theirs[...])
     else:
-        whole_ref, stat_ref, basis_ref, grad_ref, new_stat_ref, x_ref = refs
-        grad_ref[...] = whole_ref[...]
+        grad_ref[...] = refs[0][...]
+    own = pick(left, thirds(l_basis_ref), thirds(r_basis_ref))
+    got = thirds(got_ref, 0, l_basis_ref.shape[0])
+    basis_ref[...] = whole_of(scratch, pick(left, own, got), pick(left, got, own))
+    own_ref[...] = jnp.where(left, l_stat_ref[...], r_stat_ref[...])
+    other_ref[...] = jnp.where(left, r_stat_ref[...], l_stat_ref[...])
+    copy_ref[...] = l_basis_ref[...]
+    right = half_of(scratch, thirds(r_basis_ref))
+    right_ref[...] = right
     grad = grad_ref[...]
     turned = grad.T
-    new_stat = stat_ref[...] + 0.5 * dot(jnp.where(left, grad, turned), jnp.where(left, turned, grad))
+    product_ref[...] = dot(jnp.where(left, grad, turned), jnp.where(left, turned, grad))
+    inner_ref[...] = dot(grad, right)
+
+
+def begin_kernel(steps, own_ref, corner_ref, product_ref, basis_ref, new_stat_ref, x_ref, scratch):
+    new_stat = 0.5 * statistic(is_left(), thirds(own_ref), corner_ref, scratch) + 0.5 * product_ref[...]
     new_stat_ref[...] = new_stat
     power = dot(new_stat, basis_ref[...])
     x_ref[...] = power * (1.0 / jnp.sqrt(jnp.sum(power * power) + NORM_EPS))
@@ -254,7 +257,7 @@
 
 def update_kernel(
     hops,
-    grad_ref,
+    inner_ref,
     basis_ref,
     left_ref,
     right_ref,
@@ -271,9 +274,8 @@
     left = is_left()
     basis_left = jnp.where(left, basis_ref[...], whole_of(scratch, thirds(first_left_ref), thirds(left_ref)))
     left_parts = split(basis_left)
-    basis_right = split(half_of(scratch, thirds(right_ref)))
-    inner = dot_parts(split(grad_ref[...]), basis_right)
-    rotated = flat_of(scratch, dot(basis_left.T, inner))
+    basis_right = split(right_ref[...])
+    rotated = flat_of(scratch, dot(basis_left.T, inner_ref[...]))
     ones = thirds(one_ref)
     twos = thirds(two_ref)
     new_one = [BETA_ONE * m + (1.0 - BETA_ONE) * r for m, r in zip(ones, rotated)]
@@ -330,21 +332,20 @@
         copy.wait()
 
 
-def stats_kernel(grad_ref, new_stat_ref, left_ref, right_ref, new_left_ref, new_right_ref, scratch):
-    left = is_left()
-    other = pick(left, thirds(right_ref), thirds(left_ref))
+def stats_kernel(grad_ref, new_stat_ref, other_ref, new_left_ref, new_right_ref, scratch):
+    left = is_left()
     grad = grad_ref[...]
     turned = grad.T
     a = jnp.where(left, grad, turned)
     b = jnp.where(left, turned, grad)
     new_own = flat_of(scratch, take_half(new_stat_ref[...], left))
     product = flat_of(scratch, dot(b, take_half(a, left)))
-    new_other = [0.5 * u + 0.5 * v for u, v in zip(other, product)]
+    new_other = [0.5 * u + 0.5 * v for u, v in zip(thirds(other_ref), product)]
     put_thirds(new_left_ref, pick(left, new_own, new_other))
     put_thirds(new_right_ref, pick(left, new_other, new_own))
 
 
-def call(kernel, outs, scratch, products, full, name, copies=0, **specs):
+def call(kernel, outs, scratch, products, full, name, copies=0, limit=40, **specs):
     size = full * full
     scratch = [pltpu.VMEM(s, F32) for s in scratch]
     if copies:
@@ -353,7 +354,7 @@
         kernel,
         out_shape=[jax.ShapeDtypeStruct(s, F32) for s in outs],
         scratch_shapes=scratch,
-        compiler_params=pltpu.CompilerParams(vmem_limit_bytes=40 * 1024 * 1024),
+        compiler_params=pltpu.CompilerParams(vmem_limit_bytes=limit * 1024 * 1024),
         cost_estimate=pl.CostEstimate(flops=int(products * 6 * full * size), bytes_accessed=16 * size, transcendentals=0),
         name=name,
         **specs,
@@ -395,39 +396,46 @@
         x.reshape(flat) for x in (moment_one, moment_two, left_stat, right_stat, left_basis, right_basis)
     )
     count = corner_rows(flat_rows)
-    outgoing_rows = flat_rows + count + (rows_here * (full // LANES) if near else 0)
-    outgoing, *pieces = call(
+    outgoing_rows = flat_rows + (rows_here * (full // LANES) if near else 0)
+    outgoing, corner, *pieces = call(
         functools.partial(pack_kernel, hops),
-        [(outgoing_rows, LANES)] + [block] * len(hops),
-        [(flat_rows // 2, LANES), (count, LANES)],
+        [(outgoing_rows, LANES), (count, LANES)] + [block] * len(hops),
+        [(flat_rows // 2, LANES)],
         0.1,
         full,
         "pack",
         copies=2 + len(hops) + full // LANES,
-        in_specs=anywhere(5),
-        out_specs=anywhere(1 + len(hops)),
+        limit=63,
+        in_specs=[pl.BlockSpec(memory_space=pltpu.HBM)] * 5,
+        out_specs=anywhere(1) + [pl.BlockSpec(memory_space=pltpu.VMEM)] + anywhere(len(hops)),
     )(l_stat, r_stat, l_basis, r_basis, grads)
     got = partner(outgoing)
     if near:
         mine = [hop_by(piece, hop) for hop, piece in zip(hops, pieces)]
         theirs = [partner(x) for x in mine]
-        rows = (grads, got, *mine, *theirs)
-        last = theirs
+        rows = (grads, *mine, *theirs)
     else:
         mine = exchange(grads)
         theirs = partner(mine)
-        mine, last = jnp.where(parity == 0, mine, theirs), [theirs]
-        rows = (jnp.stack([mine, jnp.where(parity == 0, theirs, mine)], axis=1).reshape(square),)
-    first_left = partner(after(l_basis, *last))
-    stat, basis = call(prepare_kernel, [square, square], [(3, full, LANES)], 0.1, full, "prepare")(
-        l_stat, r_stat, l_basis, r_basis, got
-    )
-    grad, new_stat, x = call(functools.partial(begin_kernel, 2, hops), [square] * 3, [], 8, full, "begin")(
-        *rows, stat, basis
+        even, odd = jnp.where(parity == 0, mine, theirs), jnp.where(parity == 0, theirs, mine)
+        rows = (jnp.stack([even, odd], axis=1).reshape(square),)
+        mine = [mine]
+    got_corner = partner(after(corner, *mine))
+    grad, product, basis, right, inner, own, other, left = call(
+        functools.partial(products_kernel, hops),
+        [square, square, square, (full, 2 * LANES), (full, 2 * LANES), flat, flat, flat],
+        [(3, full, LANES)],
+        2,
+        full,
+        "products",
+    )(l_stat, r_stat, l_basis, r_basis, got, *rows)
+    first_left = partner(after(l_basis, product))
+    new_stat, x = call(functools.partial(begin_kernel, 2), [square] * 2, [(3, full, LANES)], 7, full, "begin")(
+        own, got_corner, product, basis
     )
     new_one, new_two, own_rows, other_rows = call(
         functools.partial(update_kernel, hops), [flat, flat, strips, strips], [(3, full, LANES), square], 2, full, "update"
-    )(after(grad, x), basis, l_basis, r_basis, first_left, one, two)
+    )(after(inner, x), basis, left, right, first_left, one, two)
     if not near:
         top = jnp.where(parity == 0, own_rows, other_rows)
         bottom = jnp.where(parity == 0, other_rows, own_rows)
@@ -460,7 +468,7 @@
         new_l_basis = jnp.where(parity == 0, keep, back)
         new_r_basis = jnp.where(parity == 0, back, keep)
     new_left, new_right = call(stats_kernel, [flat, flat], [(3, full, LANES)], 1, full, "stats")(
-        after(grad, send), new_stat, l_stat, r_stat
+        after(grad, send), new_stat, other
     )
     halves = (new_one, new_two, new_left, new_right, new_l_basis, new_r_basis)
     return (update, *(x.reshape(1, flat_rows * LANES) for x in halves))

time: 55.8 us -> 71.1 us (1.27)
  Pallas kernels: 20.6 us -> 38.3 us
  local copies, waits for them, and re-layouts: 3.87 us -> 0.98 us
  starting transfers between devices: 18.4 us -> 19.6 us
    pallas_call x3, Pallas kernels: 7.97 us -> 27.1 us  [the longest x1 19.7 us: local(): call(functools.partial(pack_kernel, hops), [(outgoing_rows, LANES), (coun...]
    unnamed x20 -> x12, local copies, waits for them, and re-layouts: 3.87 us -> 0.98 us
    ppermute x6, starting transfers between devices: 8.41 us -> 9.88 us  [hop_by(): return lax.ppermute(x, 'shard', [(i, i ^ 2 * hop) for i in range(size)])]
    pallas_call x1, Pallas kernels: 3.97 us -> 2.5 us  [local(): call(functools.partial(update_kernel, hops), [flat, flat, strips, strips]...]
    ppermute x7 -> x8, waiting for transfers between devices: 4.51 us -> 3.34 us  [partner(): return lax.ppermute(x, 'shard', pairs)]
    ppermute x7 -> x8, starting transfers between devices: 9.95 us -> 9.75 us  [partner(): return lax.ppermute(x, 'shard', pairs)]
  transfers between devices with their start and end apart: 13 -> 14, of which waited for: 8 -> 8; matrix products, arithmetic and copies ran while one was open for 0% -> 0% of each run, Pallas kernels for 27% -> 21%
where the time goes in v3:
time: 71.1 us; the launch traced here: 70.9 us
  Pallas kernels  38.3 us (54%)
  starting transfers between devices  19.6 us (28%)
  waiting for transfers between devices  11.3 us (16%)
  local copies, waits for them, and re-layouts  0.98 us (1%)
  between operations  0.72 us (1%)
    pallas_call x1, Pallas kernels, local(): call(functools.partial(pack_kernel, hops), [(outgoing_rows, LANES), (coun...  19.7 us
    ppermute x6, starting transfers between devices, hop_by(): return lax.ppermute(x, 'shard', [(i, i ^ 2 * hop) for i in range(size)])  9.88 us
    ppermute x8, starting transfers between devices, partner(): return lax.ppermute(x, 'shard', pairs)  9.75 us
    ppermute x6, waiting for transfers between devices, hop_by(): return lax.ppermute(x, 'shard', [(i, i ^ 2 * hop) for i in range(size)])  7.93 us
    pallas_call x1, Pallas kernels, local(): call(functools.partial(end_kernel, NS_ITERS - 2), [flat, flat], [(3, full...  5.97 us
    pallas_call x1, Pallas kernels, local(): call(functools.partial(begin_kernel, 2), [square] * 2, [(3, full, LANES)]...  5.17 us
    ppermute x8, waiting for transfers between devices, partner(): return lax.ppermute(x, 'shard', pairs)  3.34 us
    pallas_call x1, Pallas kernels, local(): call(functools.partial(update_kernel, hops), [flat, flat, strips, strips]...  2.5 us
  transfers between devices with their start and end apart: 14, of which 8 were waited for; matrix products, arithmetic and copies ran while one was open for 0% of the time, Pallas kernels for 21%

profile of v3, /device:TPU:0, one launch (start us, length us, event | category | flops | bytes accessed | tf_op | source)
XLA Modules:
  0.0 70.9 jit_solution(9366953303245068498)
XLA Ops:
  0.6 0.0 copy-start.2
  0.6 0.0 copy-start.3
  0.7 0.0 copy-start.4
  0.7 19.7 %pack.1 = (f32[720,128]{1,0:T(8,128)}, f32[192,128]{1,0:T(8,128)}, f32[48,384]{1,0:T(8,128)}, f32[48,384]{1,0:T(8,128)}, f32[48,384]{1,0:T(8,128)}) custom-call(f32[576,128]{1,0:T(8,128)} %bitcast.14, f32[576,128]{1,0:T(8,128)} %bitcast.16, f32[576,128]{1,0:T(8,128)} %bitcast.2.l_basis_ref, f32[576,128]{1,0:T(8,128)} %bitcast.18, f32[4,48,384]{2,1,0:T(8,128)} %refs_0_.1), custom_call_target="tpu_custom_call" | custom-call | flops 33973864 | bytes 2359296 | tf_op jit(solution)/shard_map/pack/pallas_call | solution.py:400
  20.4 3.0 %collective-permute-start = (f32[720,128]{1,0:T(8,128)}, f32[720,128]{1,0:T(8,128)S(1)}, u32[]{:S(2)}, u32[]{:S(2)}) collective-permute-start(f32[720,128]{1,0:T(8,128)} %get-tuple-element.44), channel_id=1, source_target_pairs={{0,4},{4,0},{8,12},{12,8},{16,20},{20,16},{24,28},{28,24},{1,5},{5... | collective-permute-start | bytes 1105928 | tf_op jit(solution)/shard_map/ppermute | solution.py:393
  23.4 2.6 %collective-permute-start.1 = (f32[48,384]{1,0:T(8,128)}, f32[48,384]{1,0:T(8,128)S(1)}, u32[]{:S(2)}, u32[]{:S(2)}) collective-permute-start(f32[48,384]{1,0:T(8,128)} %get-tuple-element.45), channel_id=1, source_target_pairs={{0,16},{4,20},{8,24},{12,28},{16,0},{20,4},{24,8},{28,12},{1,17},{... | collective-permute-start | bytes 221192 | tf_op jit(solution)/shard_map/ppermute | solution.py:390
  26.0 1.3 %collective-permute-start.2 = (f32[48,384]{1,0:T(8,128)}, f32[48,384]{1,0:T(8,128)S(1)}, u32[]{:S(2)}, u32[]{:S(2)}) collective-permute-start(f32[48,384]{1,0:T(8,128)} %get-tuple-element.46), channel_id=1, source_target_pairs={{0,24},{4,28},{8,16},{12,20},{16,8},{20,12},{24,0},{28,4},{1,25},{... | collective-permute-start | bytes 221192 | tf_op jit(solution)/shard_map/ppermute | solution.py:390
  27.3 0.2 collective-permute-start.3
  27.6 3.4 %collective-permute-done.1.refs_1_ = f32[48,384]{1,0:T(8,128)S(1)} collective-permute-done((f32[48,384]{1,0:T(8,128)}, f32[48,384]{1,0:T(8,128)S(1)}, u32[]{:S(2)}, u32[]{:S(2)}) %collective-permute-start.1) | collective-permute-done | bytes 73760 | tf_op jit(solution)/shard_map/ppermute | solution.py:390
  31.0 0.5 collective-permute-start.4
  31.5 1.1 %collective-permute-done.2.refs_2_ = f32[48,384]{1,0:T(8,128)S(1)} collective-permute-done((f32[48,384]{1,0:T(8,128)}, f32[48,384]{1,0:T(8,128)S(1)}, u32[]{:S(2)}, u32[]{:S(2)}) %collective-permute-start.2) | collective-permute-done | bytes 73760 | tf_op jit(solution)/shard_map/ppermute | solution.py:390
  32.5 0.5 collective-permute-start.5
  33.0 0.0 collective-permute-done.3.refs_3_
  33.0 1.5 %collective-permute-start.6 = (f32[48,384]{1,0:T(8,128)S(1)}, f32[48,384]{1,0:T(8,128)S(1)}, u32[]{:S(2)}, u32[]{:S(2)}) collective-permute-start(f32[48,384]{1,0:T(8,128)S(1)} %collective-permute-done.3.refs_3_), channel_id=1, source_target_pairs={{0,4},{4,0},{8,12},{12,8},{16,20},{20,16},{24,28},{28,24},{1,5},{5... | collective-permute-start | bytes 221192 | tf_op jit(solution)/shard_map/ppermute | solution.py:393
  34.5 0.5 collective-permute-start.7
  35.1 1.1 %collective-permute-done.4.refs_4_ = f32[48,384]{1,0:T(8,128)S(1)} collective-permute-done((f32[48,384]{1,0:T(8,128)S(1)}, f32[48,384]{1,0:T(8,128)S(1)}, u32[]{:S(2)}, u32[]{:S(2)}) %collective-permute-start.4) | collective-permute-done | bytes 73760 | tf_op jit(solution)/shard_map/ppermute | solution.py:393
  36.2 1.2 %collective-permute-done.5.refs_5_ = f32[48,384]{1,0:T(8,128)S(1)} collective-permute-done((f32[48,384]{1,0:T(8,128)S(1)}, f32[48,384]{1,0:T(8,128)S(1)}, u32[]{:S(2)}, u32[]{:S(2)}) %collective-permute-start.5) | collective-permute-done | bytes 73760 | tf_op jit(solution)/shard_map/ppermute | solution.py:393
  37.4 0.8 %collective-permute-done.6.refs_6_ = f32[48,384]{1,0:T(8,128)S(1)} collective-permute-done((f32[48,384]{1,0:T(8,128)S(1)}, f32[48,384]{1,0:T(8,128)S(1)}, u32[]{:S(2)}, u32[]{:S(2)}) %collective-permute-start.6) | collective-permute-done | bytes 73760 | tf_op jit(solution)/shard_map/ppermute | solution.py:393
  38.2 0.0 collective-permute-done.got_ref
  38.2 0.0 copy-done.2
  38.2 0.0 copy-done.3
  38.2 0.0 copy-done.4
  38.2 0.0 copy-start.5
  38.2 1.0 %copy-done.5 = f32[4,48,384]{2,1,0:T(8,128)S(1)} copy-done((f32[4,48,384]{2,1,0:T(8,128)S(1)}, f32[4,48,384]{2,1,0:T(8,128)}, u32[]{:S(2)}) %copy-start.5) | copy-done | bytes 294936
  39.2 2.3 %products.1 = (f32[384,384]{1,0:T(8,128)S(1)}, f32[384,384]{1,0:T(8,128)S(1)}, f32[384,384]{1,0:T(8,128)S(1)}, f32[384,256]{1,0:T(8,128)S(1)}, f32[384,256]{1,0:...) custom-call(f32[576,128]{1,0:T(8,128)S(1)} %bitcast.15, ...), custom_call_target="tpu_custom_call" | custom-call | flops 679477248 | bytes 2359296 | tf_op jit(solution)/shard_map/products/pallas_call | solution.py:424
  41.4 1.6 %collective-permute-start.8 = (f32[576,128]{1,0:T(8,128)}, f32[576,128]{1,0:T(8,128)S(1)}, u32[]{:S(2)}, u32[]{:S(2)}) collective-permute-start(f32[576,128]{1,0:T(8,128)} %bitcast.2.l_basis_ref), channel_id=1, source_target_pairs={{0,4},{4,0},{8,12},{12,8},{16,20},{20,16},{24,28},{28,24},{1,5},{5... | collective-permute-start | bytes 884744 | tf_op jit(solution)/shard_map/ppermute | solution.py:393
  43.0 0.0 collective-permute-done.7.corner_ref
  43.0 0.0 copy-start
  43.1 0.0 copy-start.1
  43.1 5.2 %begin.1 = (f32[384,384]{1,0:T(8,128)S(1)}, f32[384,384]{1,0:T(8,128)S(1)}) custom-call(f32[576,128]{1,0:T(8,128)S(1)} %get-tuple-element.48.own_ref, f32[192,128]{1,0:T(8,128)S(1)} %collective-permute-done.7.corner_ref, f32[384,384]{1,0:T(8,128)S(1)} %get-tuple-element.51.product_ref, f32[384,384]{1,0:T(8,128)S(1)} %get-tuple-element.52.basis_ref), custom_call_target="tpu_custom_call" | custom-call | flops 2378170368 | bytes 2359296 | tf_op jit(solution)/shard_map/begin/pallas_call | solution.py:433
  48.2 0.2 collective-permute-done.8.first_left_ref
  48.4 0.0 copy-done
  48.4 0.0 copy-done.1
  48.4 2.5 %update.1 = (f32[576,128]{1,0:T(8,128)}, f32[576,128]{1,0:T(8,128)}, f32[4,48,384]{2,1,0:T(8,128)S(1)}, f32[4,48,384]{2,1,0:T(8,128)S(1)}) custom-call(f32[384,256]{1,0:T(8,128)S(1)} %get-tuple-element.55.inner_ref, f32[384,384]{1,0:T(8,128)S(1)} %get-tuple-element.52.basis_ref, f32[576,128]{1,0:T(8,128)S(1)} %get-tuple-element.56.left_ref, ...), custom_call_target="tpu_custom_call" | custom-call | flops 679477248 | bytes 2359296 | tf_op jit(solution)/shard_map/update/pallas_call | solution.py:436
  50.9 1.7 %collective-permute-start.10 = (f32[4,48,384]{2,1,0:T(8,128)S(1)}, f32[4,48,384]{2,1,0:T(8,128)S(1)}, u32[]{:S(2)}, u32[]{:S(2)}) collective-permute-start(f32[4,48,384]{2,1,0:T(8,128)S(1)} %get-tuple-element.59), channel_id=1, source_target_pairs={{0,4},{4,0},{8,12},{12,8},{16,20},{20,16},{24,28},{28,24},{1,5},{5... | collective-permute-start | bytes 884744 | tf_op jit(solution)/shard_map/ppermute | solution.py:393
  52.6 6.0 %end.1 = (f32[576,128]{1,0:T(8,128)S(1)}, f32[576,128]{1,0:T(8,128)S(1)}) custom-call(f32[384,384]{1,0:T(8,128)S(1)} %get-tuple-element.60.start_ref), custom_call_target="tpu_custom_call" | custom-call | flops 3057647616 | bytes 2359296 | tf_op jit(solution)/shard_map/end/pallas_call | solution.py:446
  58.6 0.4 collective-permute-start.9
  59.0 0.0 collective-permute-done.10.theirs_ref
  59.1 4.2 %collective-permute-start.11 = (f32[48,384]{1,0:T(8,128)S(1)}, f32[48,384]{1,0:T(8,128)S(1)}, u32[]{:S(2)}, u32[]{:S(2)}) collective-permute-start(f32[48,384]{1,0:T(8,128)S(1)} %get-tuple-element.67), channel_id=1, source_target_pairs={{0,16},{4,20},{8,24},{12,28},{16,0},{20,4},{24,8},{28,12},{1,17},{... | collective-permute-start | bytes 221192 | tf_op jit(solution)/shard_map/ppermute | solution.py:390
  63.2 1.5 %collective-permute-start.12 = (f32[48,384]{1,0:T(8,128)S(1)}, f32[48,384]{1,0:T(8,128)S(1)}, u32[]{:S(2)}, u32[]{:S(2)}) collective-permute-start(f32[48,384]{1,0:T(8,128)S(1)} %get-tuple-element.68), channel_id=1, source_target_pairs={{0,24},{4,28},{8,16},{12,20},{16,8},{20,12},{24,0},{28,4},{1,25},{... | collective-permute-start | bytes 221192 | tf_op jit(solution)/shard_map/ppermute | solution.py:390
  64.8 0.0 collective-permute-start.13
  64.8 1.7 %stats.1 = (f32[576,128]{1,0:T(8,128)}, f32[576,128]{1,0:T(8,128)}) custom-call(f32[384,384]{1,0:T(8,128)S(1)} %get-tuple-element.74.grad_ref, f32[384,384]{1,0:T(8,128)S(1)} %get-tuple-element.75.new_stat_ref, f32[576,128]{1,0:T(8,128)S(1)} %get-tuple-element.76.other_ref), custom_call_target="tpu_custom_call" | custom-call | flops 339738624 | bytes 2359296 | tf_op jit(solution)/shard_map/stats/pallas_call | solution.py:470
  66.5 0.0 collective-permute-done.9.back_ref
  66.5 0.0 collective-permute-done.11.refs_1_
  66.5 3.0 %collective-permute-done.12.refs_2_ = f32[48,384]{1,0:T(8,128)S(1)} collective-permute-done((f32[48,384]{1,0:T(8,128)S(1)}, f32[48,384]{1,0:T(8,128)S(1)}, u32[]{:S(2)}, u32[]{:S(2)}) %collective-permute-start.12) | collective-permute-done | bytes 73760 | tf_op jit(solution)/shard_map/ppermute | solution.py:390
  69.5 0.4 collective-permute-done.13.refs_3_
  69.9 1.0 %finish.1 = (f32[4,48,384]{2,1,0:T(8,128)}, f32[576,128]{1,0:T(8,128)}, f32[576,128]{1,0:T(8,128)}) custom-call(f32[576,128]{1,0:T(8,128)S(1)} %get-tuple-element.61.keep_ref, f32[576,128]{1,0:T(8,128)S(1)} %collective-permute-done.9.back_ref, f32[48,384]{1,0:T(8,128)S(1)} %get-tuple-element.66.refs_0_, f32[48,384]{1,0:T(8,128)S(1)} %collective-permute-done.11.refs_1_, ...), custom_call_target="tpu_custom_call" | custom-call | flops 33973864 | bytes 2359296 | tf_op jit(solution)/shard_map/finish/pallas_call | solution.py:455
  (1 shorter events, 0.0 us)
Async XLA Ops:
  0.6 37.6 %copy-start.2 = (f32[1,73728]{1,0:T(1,128)S(1)}, f32[1,73728]{1,0:T(1,128)}, u32[]{:S(2)}) copy-start(f32[1,73728]{1,0:T(1,128)} %param.10) | copy-start | bytes 884740
  0.6 37.5 %copy-start.3 = (f32[1,73728]{1,0:T(1,128)S(1)}, f32[1,73728]{1,0:T(1,128)}, u32[]{:S(2)}) copy-start(f32[1,73728]{1,0:T(1,128)} %param.11) | copy-start | bytes 884740
  0.7 37.5 %copy-start.4 = (f32[1,73728]{1,0:T(1,128)S(1)}, f32[1,73728]{1,0:T(1,128)}, u32[]{:S(2)}) copy-start(f32[1,73728]{1,0:T(1,128)} %param.13) | copy-start | bytes 884740
  20.4 17.8 %collective-permute-start = (f32[720,128]{1,0:T(8,128)}, f32[720,128]{1,0:T(8,128)S(1)}, u32[]{:S(2)}, u32[]{:S(2)}) collective-permute-start(f32[720,128]{1,0:T(8,128)} %get-tuple-element.44), channel_id=1, source_target_pairs={{0,4},{4,0},{8,12},{12,8},{16,20},{20,16},{24,28},{28,24},{1,5},{5... | collective-permute-start | bytes 1105928 | tf_op jit(solution)/shard_map/ppermute | solution.py:393
  23.4 7.6 %collective-permute-start.1 = (f32[48,384]{1,0:T(8,128)}, f32[48,384]{1,0:T(8,128)S(1)}, u32[]{:S(2)}, u32[]{:S(2)}) collective-permute-start(f32[48,384]{1,0:T(8,128)} %get-tuple-element.45), channel_id=1, source_target_pairs={{0,16},{4,20},{8,24},{12,28},{16,0},{20,4},{24,8},{28,12},{1,17},{... | collective-permute-start | bytes 221192 | tf_op jit(solution)/shard_map/ppermute | solution.py:390
  26.0 6.5 %collective-permute-start.2 = (f32[48,384]{1,0:T(8,128)}, f32[48,384]{1,0:T(8,128)S(1)}, u32[]{:S(2)}, u32[]{:S(2)}) collective-permute-start(f32[48,384]{1,0:T(8,128)} %get-tuple-element.46), channel_id=1, source_target_pairs={{0,24},{4,28},{8,16},{12,20},{16,8},{20,12},{24,0},{28,4},{1,25},{... | collective-permute-start | bytes 221192 | tf_op jit(solution)/shard_map/ppermute | solution.py:390
  27.3 5.7 %collective-permute-start.3 = (f32[48,384]{1,0:T(8,128)}, f32[48,384]{1,0:T(8,128)S(1)}, u32[]{:S(2)}, u32[]{:S(2)}) collective-permute-start(f32[48,384]{1,0:T(8,128)} %get-tuple-element.47), channel_id=1, source_target_pairs={{0,8},{4,12},{8,0},{12,4},{16,24},{20,28},{24,16},{28,20},{1,9},{5... | collective-permute-start | bytes 221192 | tf_op jit(solution)/shard_map/ppermute | solution.py:390
  31.0 5.2 %collective-permute-start.4 = (f32[48,384]{1,0:T(8,128)S(1)}, f32[48,384]{1,0:T(8,128)S(1)}, u32[]{:S(2)}, u32[]{:S(2)}) collective-permute-start(f32[48,384]{1,0:T(8,128)S(1)} %collective-permute-done.1.refs_1_), channel_id=1, source_target_pairs={{0,4},{4,0},{8,12},{12,8},{16,20},{20,16},{24,28},{28,24},{1,5},{5... | collective-permute-start | bytes 221192 | tf_op jit(solution)/shard_map/ppermute | solution.py:393
  32.5 4.9 %collective-permute-start.5 = (f32[48,384]{1,0:T(8,128)S(1)}, f32[48,384]{1,0:T(8,128)S(1)}, u32[]{:S(2)}, u32[]{:S(2)}) collective-permute-start(f32[48,384]{1,0:T(8,128)S(1)} %collective-permute-done.2.refs_2_), channel_id=1, source_target_pairs={{0,4},{4,0},{8,12},{12,8},{16,20},{20,16},{24,28},{28,24},{1,5},{5... | collective-permute-start | bytes 221192 | tf_op jit(solution)/shard_map/ppermute | solution.py:393
  33.0 5.2 %collective-permute-start.6 = (f32[48,384]{1,0:T(8,128)S(1)}, f32[48,384]{1,0:T(8,128)S(1)}, u32[]{:S(2)}, u32[]{:S(2)}) collective-permute-start(f32[48,384]{1,0:T(8,128)S(1)} %collective-permute-done.3.refs_3_), channel_id=1, source_target_pairs={{0,4},{4,0},{8,12},{12,8},{16,20},{20,16},{24,28},{28,24},{1,5},{5... | collective-permute-start | bytes 221192 | tf_op jit(solution)/shard_map/ppermute | solution.py:393
  34.5 8.5 %collective-permute-start.7 = (f32[192,128]{1,0:T(8,128)}, f32[192,128]{1,0:T(8,128)S(1)}, u32[]{:S(2)}, u32[]{:S(2)}) collective-permute-start(f32[192,128]{1,0:T(8,128)} %get-tuple-element.50), channel_id=1, source_target_pairs={{0,4},{4,0},{8,12},{12,8},{16,20},{20,16},{24,28},{28,24},{1,5},{5... | collective-permute-start | bytes 294920 | tf_op jit(solution)/shard_map/ppermute | solution.py:393
  38.2 1.0 %copy-start.5 = (f32[4,48,384]{2,1,0:T(8,128)S(1)}, f32[4,48,384]{2,1,0:T(8,128)}, u32[]{:S(2)}) copy-start(f32[4,48,384]{2,1,0:T(8,128)} %refs_0_.1) | copy-start | bytes 884740
  41.4 7.0 %collective-permute-start.8 = (f32[576,128]{1,0:T(8,128)}, f32[576,128]{1,0:T(8,128)S(1)}, u32[]{:S(2)}, u32[]{:S(2)}) collective-permute-start(f32[576,128]{1,0:T(8,128)} %bitcast.2.l_basis_ref), channel_id=1, source_target_pairs={{0,4},{4,0},{8,12},{12,8},{16,20},{20,16},{24,28},{28,24},{1,5},{5... | collective-permute-start | bytes 884744 | tf_op jit(solution)/shard_map/ppermute | solution.py:393
  43.0 5.4 %copy-start = (f32[1,73728]{1,0:T(1,128)S(1)}, f32[1,73728]{1,0:T(1,128)}, u32[]{:S(2)}) copy-start(f32[1,73728]{1,0:T(1,128)} %param.8) | copy-start | bytes 884740
  43.1 5.4 %copy-start.1 = (f32[1,73728]{1,0:T(1,128)S(1)}, f32[1,73728]{1,0:T(1,128)}, u32[]{:S(2)}) copy-start(f32[1,73728]{1,0:T(1,128)} %param.9) | copy-start | bytes 884740
  50.9 8.1 %collective-permute-start.10 = (f32[4,48,384]{2,1,0:T(8,128)S(1)}, f32[4,48,384]{2,1,0:T(8,128)S(1)}, u32[]{:S(2)}, u32[]{:S(2)}) collective-permute-start(f32[4,48,384]{2,1,0:T(8,128)S(1)} %get-tuple-element.59), channel_id=1, source_target_pairs={{0,4},{4,0},{8,12},{12,8},{16,20},{20,16},{24,28},{28,24},{1,5},{5... | collective-permute-start | bytes 884744 | tf_op jit(solution)/shard_map/ppermute | solution.py:393
  58.6 7.9 %collective-permute-start.9 = (f32[576,128]{1,0:T(8,128)S(1)}, f32[576,128]{1,0:T(8,128)S(1)}, u32[]{:S(2)}, u32[]{:S(2)}) collective-permute-start(f32[576,128]{1,0:T(8,128)S(1)} %get-tuple-element.62), channel_id=1, source_target_pairs={{0,4},{4,0},{8,12},{12,8},{16,20},{20,16},{24,28},{28,24},{1,5},{5... | collective-permute-start | bytes 884744 | tf_op jit(solution)/shard_map/ppermute | solution.py:393
  59.1 7.4 %collective-permute-start.11 = (f32[48,384]{1,0:T(8,128)S(1)}, f32[48,384]{1,0:T(8,128)S(1)}, u32[]{:S(2)}, u32[]{:S(2)}) collective-permute-start(f32[48,384]{1,0:T(8,128)S(1)} %get-tuple-element.67), channel_id=1, source_target_pairs={{0,16},{4,20},{8,24},{12,28},{16,0},{20,4},{24,8},{28,12},{1,17},{... | collective-permute-start | bytes 221192 | tf_op jit(solution)/shard_map/ppermute | solution.py:390
  63.2 6.3 %collective-permute-start.12 = (f32[48,384]{1,0:T(8,128)S(1)}, f32[48,384]{1,0:T(8,128)S(1)}, u32[]{:S(2)}, u32[]{:S(2)}) collective-permute-start(f32[48,384]{1,0:T(8,128)S(1)} %get-tuple-element.68), channel_id=1, source_target_pairs={{0,24},{4,28},{8,16},{12,20},{16,8},{20,12},{24,0},{28,4},{1,25},{... | collective-permute-start | bytes 221192 | tf_op jit(solution)/shard_map/ppermute | solution.py:390
  64.8 5.1 %collective-permute-start.13 = (f32[48,384]{1,0:T(8,128)S(1)}, f32[48,384]{1,0:T(8,128)S(1)}, u32[]{:S(2)}, u32[]{:S(2)}) collective-permute-start(f32[48,384]{1,0:T(8,128)S(1)} %get-tuple-element.69), channel_id=1, source_target_pairs={{0,8},{4,12},{8,0},{12,4},{16,24},{20,28},{24,16},{28,20},{1,9},{5... | collective-permute-start | bytes 221192 | tf_op jit(solution)/shard_map/ppermute | solution.py:390

commit v4 on v3

--- a/solution.py
+++ b/solution.py
@@ -345,16 +345,16 @@
     put_thirds(new_right_ref, pick(left, new_other, new_own))
 
 
-def call(kernel, outs, scratch, products, full, name, copies=0, limit=40, **specs):
+def call(kernel, outs, scratch, products, full, name, copies=0, kind=jax.ShapeDtypeStruct, **specs):
     size = full * full
     scratch = [pltpu.VMEM(s, F32) for s in scratch]
     if copies:
         scratch.append(pltpu.SemaphoreType.DMA((copies,)))
     return pl.pallas_call(
         kernel,
-        out_shape=[jax.ShapeDtypeStruct(s, F32) for s in outs],
+        out_shape=[kind(s, F32) for s in outs],
         scratch_shapes=scratch,
-        compiler_params=pltpu.CompilerParams(vmem_limit_bytes=limit * 1024 * 1024),
+        compiler_params=pltpu.CompilerParams(vmem_limit_bytes=40 * 1024 * 1024),
         cost_estimate=pl.CostEstimate(flops=int(products * 6 * full * size), bytes_accessed=16 * size, transcendentals=0),
         name=name,
         **specs,
@@ -405,10 +405,10 @@
         full,
         "pack",
         copies=2 + len(hops) + full // LANES,
-        limit=63,
-        in_specs=[pl.BlockSpec(memory_space=pltpu.HBM)] * 5,
+        kind=pltpu.VMEM,
+        in_specs=anywhere(5),
         out_specs=anywhere(1) + [pl.BlockSpec(memory_space=pltpu.VMEM)] + anywhere(len(hops)),
-    )(l_stat, r_stat, l_basis, r_basis, grads)
+    )(*(pltpu.with_memory_space_constraint(x, pltpu.HBM) for x in (l_stat, r_stat, l_basis, r_basis, grads)))
     got = partner(outgoing)
     if near:
         mine = [hop_by(piece, hop) for hop, piece in zip(hops, pieces)]

time: 71.1 us -> 50.2 us (0.71)
  Pallas kernels: 38.3 us -> 19 us
  local copies, waits for them, and re-layouts: 0.98 us -> 0.03 us
    pallas_call x1, Pallas kernels: 19.7 us -> 1.31 us  [local(): call(functools.partial(pack_kernel, hops), [(outgoing_rows, LANES), (coun...]
    unnamed x12 -> x14, local copies, waits for them, and re-layouts: 0.98 us -> 0.03 us
    pallas_call x1, Pallas kernels: 2.26 us -> 1.33 us  [local(): call(functools.partial(products_kernel, hops), [square, square, square, (...]
  transfers between devices with their start and end apart: 14 -> 14, of which waited for: 8 -> 7; matrix products, arithmetic and copies ran while one was open for 0% -> 0% of each run, Pallas kernels for 21% -> 29%
where the time goes in v4:
time: 50.2 us; the launch traced here: 50 us
  starting transfers between devices  19.4 us (39%)
  Pallas kernels  19 us (38%)
  waiting for transfers between devices  10.8 us (22%)
  between operations  0.77 us (2%)
    ppermute x8, starting transfers between devices, partner(): return lax.ppermute(x, 'shard', pairs)  9.74 us
    ppermute x6, starting transfers between devices, hop_by(): return lax.ppermute(x, 'shard', [(i, i ^ 2 * hop) for i in range(size)])  9.67 us
    ppermute x6, waiting for transfers between devices, hop_by(): return lax.ppermute(x, 'shard', [(i, i ^ 2 * hop) for i in range(size)])  7.63 us
    pallas_call x1, Pallas kernels, local(): call(functools.partial(end_kernel, NS_ITERS - 2), [flat, flat], [(3, full...  5.98 us
    pallas_call x1, Pallas kernels, local(): call(functools.partial(begin_kernel, 2), [square] * 2, [(3, full, LANES)]...  5.19 us
    ppermute x8, waiting for transfers between devices, partner(): return lax.ppermute(x, 'shard', pairs)  3.14 us
    pallas_call x1, Pallas kernels, local(): call(functools.partial(update_kernel, hops), [flat, flat, strips, strips]...  2.51 us
    pallas_call x1, Pallas kernels, local(): call(stats_kernel, [flat, flat], [(3, full, LANES)], 1, full, 'stats')  1.71 us
  transfers between devices with their start and end apart: 14, of which 7 were waited for; matrix products, arithmetic and copies ran while one was open for 0% of the time, Pallas kernels for 29%

profile of v4, /device:TPU:0, one launch (start us, length us, event | category | flops | bytes accessed | tf_op | source)
XLA Modules:
  0.0 50.0 jit_solution(4617436812856868372)
XLA Ops:
  0.6 0.0 copy-start.2
  0.6 0.0 copy-start.3
  0.7 0.0 copy-start.4
  0.7 0.0 copy-start.5
  0.7 0.0 copy-start.6
  0.7 1.3 %pack.1 = (f32[720,128]{1,0:T(8,128)S(1)}, f32[192,128]{1,0:T(8,128)S(1)}, f32[48,384]{1,0:T(8,128)S(1)}, f32[48,384]{1,0:T(8,128)S(1)}, f32[48,384]{1,0:T(8,128)S(1)}) custom-call(f32[576,128]{1,0:T(8,128)} %bitcast.14, f32[576,128]{1,0:T(8,128)} %bitcast.16, f32[576,128]{1,0:T(8,128)} %bitcast.20, f32[576,128]{1,0:T(8,128)} %bitcast.18, f32[4,48,384]{2,1,0:T(8,128)} %refs_0_.1), custom_call_target="tpu_custom_call" | custom-call | flops 33973864 | bytes 2359296 | tf_op jit(solution)/shard_map/pack/pallas_call | solution.py:400
  2.0 3.0 %collective-permute-start = (f32[720,128]{1,0:T(8,128)S(1)}, f32[720,128]{1,0:T(8,128)S(1)}, u32[]{:S(2)}, u32[]{:S(2)}) collective-permute-start(f32[720,128]{1,0:T(8,128)S(1)} %get-tuple-element.44), channel_id=1, source_target_pairs={{0,4},{4,0},{8,12},{12,8},{16,20},{20,16},{24,28},{28,24},{1,5},{5... | collective-permute-start | bytes 1105928 | tf_op jit(solution)/shard_map/ppermute | solution.py:393
  5.0 2.6 %collective-permute-start.1 = (f32[48,384]{1,0:T(8,128)S(1)}, f32[48,384]{1,0:T(8,128)S(1)}, u32[]{:S(2)}, u32[]{:S(2)}) collective-permute-start(f32[48,384]{1,0:T(8,128)S(1)} %get-tuple-element.45), channel_id=1, source_target_pairs={{0,16},{4,20},{8,24},{12,28},{16,0},{20,4},{24,8},{28,12},{1,17},{... | collective-permute-start | bytes 221192 | tf_op jit(solution)/shard_map/ppermute | solution.py:390
  7.6 1.3 %collective-permute-start.2 = (f32[48,384]{1,0:T(8,128)S(1)}, f32[48,384]{1,0:T(8,128)S(1)}, u32[]{:S(2)}, u32[]{:S(2)}) collective-permute-start(f32[48,384]{1,0:T(8,128)S(1)} %get-tuple-element.46), channel_id=1, source_target_pairs={{0,24},{4,28},{8,16},{12,20},{16,8},{20,12},{24,0},{28,4},{1,25},{... | collective-permute-start | bytes 221192 | tf_op jit(solution)/shard_map/ppermute | solution.py:390
  9.0 0.2 collective-permute-start.3
  9.2 3.2 %collective-permute-done.1.refs_1_ = f32[48,384]{1,0:T(8,128)S(1)} collective-permute-done((f32[48,384]{1,0:T(8,128)S(1)}, f32[48,384]{1,0:T(8,128)S(1)}, u32[]{:S(2)}, u32[]{:S(2)}) %collective-permute-start.1) | collective-permute-done | bytes 73760 | tf_op jit(solution)/shard_map/ppermute | solution.py:390
  12.4 0.5 collective-permute-start.4
  12.9 1.1 %collective-permute-done.2.refs_2_ = f32[48,384]{1,0:T(8,128)S(1)} collective-permute-done((f32[48,384]{1,0:T(8,128)S(1)}, f32[48,384]{1,0:T(8,128)S(1)}, u32[]{:S(2)}, u32[]{:S(2)}) %collective-permute-start.2) | collective-permute-done | bytes 73760 | tf_op jit(solution)/shard_map/ppermute | solution.py:390
  13.9 0.5 %collective-permute-start.5 = (f32[48,384]{1,0:T(8,128)S(1)}, f32[48,384]{1,0:T(8,128)S(1)}, u32[]{:S(2)}, u32[]{:S(2)}) collective-permute-start(f32[48,384]{1,0:T(8,128)S(1)} %collective-permute-done.2.refs_2_), channel_id=1, source_target_pairs={{0,4},{4,0},{8,12},{12,8},{16,20},{20,16},{24,28},{28,24},{1,5},{5... | collective-permute-start | bytes 221192 | tf_op jit(solution)/shard_map/ppermute | solution.py:393
  14.4 0.0 collective-permute-done.3.refs_3_
  14.4 1.5 %collective-permute-start.6 = (f32[48,384]{1,0:T(8,128)S(1)}, f32[48,384]{1,0:T(8,128)S(1)}, u32[]{:S(2)}, u32[]{:S(2)}) collective-permute-start(f32[48,384]{1,0:T(8,128)S(1)} %collective-permute-done.3.refs_3_), channel_id=1, source_target_pairs={{0,4},{4,0},{8,12},{12,8},{16,20},{20,16},{24,28},{28,24},{1,5},{5... | collective-permute-start | bytes 221192 | tf_op jit(solution)/shard_map/ppermute | solution.py:393
  16.0 0.5 %collective-permute-start.7 = (f32[192,128]{1,0:T(8,128)S(1)}, f32[192,128]{1,0:T(8,128)S(1)}, u32[]{:S(2)}, u32[]{:S(2)}) collective-permute-start(f32[192,128]{1,0:T(8,128)S(1)} %get-tuple-element.50), channel_id=1, source_target_pairs={{0,4},{4,0},{8,12},{12,8},{16,20},{20,16},{24,28},{28,24},{1,5},{5... | collective-permute-start | bytes 294920 | tf_op jit(solution)/shard_map/ppermute | solution.py:393
  16.5 1.1 %collective-permute-done.4.refs_4_ = f32[48,384]{1,0:T(8,128)S(1)} collective-permute-done((f32[48,384]{1,0:T(8,128)S(1)}, f32[48,384]{1,0:T(8,128)S(1)}, u32[]{:S(2)}, u32[]{:S(2)}) %collective-permute-start.4) | collective-permute-done | bytes 73760 | tf_op jit(solution)/shard_map/ppermute | solution.py:393
  17.6 1.2 %collective-permute-done.5.refs_5_ = f32[48,384]{1,0:T(8,128)S(1)} collective-permute-done((f32[48,384]{1,0:T(8,128)S(1)}, f32[48,384]{1,0:T(8,128)S(1)}, u32[]{:S(2)}, u32[]{:S(2)}) %collective-permute-start.5) | collective-permute-done | bytes 73760 | tf_op jit(solution)/shard_map/ppermute | solution.py:393
  18.8 0.8 %collective-permute-done.6.refs_6_ = f32[48,384]{1,0:T(8,128)S(1)} collective-permute-done((f32[48,384]{1,0:T(8,128)S(1)}, f32[48,384]{1,0:T(8,128)S(1)}, u32[]{:S(2)}, u32[]{:S(2)}) %collective-permute-start.6) | collective-permute-done | bytes 73760 | tf_op jit(solution)/shard_map/ppermute | solution.py:393
  19.6 0.0 collective-permute-done.got_ref
  19.6 0.0 copy-done.2
  19.6 0.0 copy-done.3
  19.6 0.0 copy-done.4
  19.6 0.0 copy-done.5
  19.6 0.0 copy-done.6
  19.6 1.3 %products.1 = (f32[384,384]{1,0:T(8,128)S(1)}, f32[384,384]{1,0:T(8,128)S(1)}, f32[384,384]{1,0:T(8,128)S(1)}, f32[384,256]{1,0:T(8,128)S(1)}, f32[384,256]{1,0:...) custom-call(f32[576,128]{1,0:T(8,128)S(1)} %bitcast.15, ...), custom_call_target="tpu_custom_call" | custom-call | flops 679477248 | bytes 2359296 | tf_op jit(solution)/shard_map/products/pallas_call | solution.py:424
  21.0 1.6 %collective-permute-start.8 = (f32[576,128]{1,0:T(8,128)S(1)}, f32[576,128]{1,0:T(8,128)S(1)}, u32[]{:S(2)}, u32[]{:S(2)}) collective-permute-start(f32[576,128]{1,0:T(8,128)S(1)} %bitcast.22), channel_id=1, source_target_pairs={{0,4},{4,0},{8,12},{12,8},{16,20},{20,16},{24,28},{28,24},{1,5},{5... | collective-permute-start | bytes 884744 | tf_op jit(solution)/shard_map/ppermute | solution.py:393
  22.6 0.0 collective-permute-done.7.corner_ref
  22.6 0.0 copy-start
  22.6 5.2 %begin.1 = (f32[384,384]{1,0:T(8,128)S(1)}, f32[384,384]{1,0:T(8,128)S(1)}) custom-call(f32[576,128]{1,0:T(8,128)S(1)} %get-tuple-element.48.own_ref, f32[192,128]{1,0:T(8,128)S(1)} %collective-permute-done.7.corner_ref, f32[384,384]{1,0:T(8,128)S(1)} %get-tuple-element.51.product_ref, f32[384,384]{1,0:T(8,128)S(1)} %get-tuple-element.52.basis_ref), custom_call_target="tpu_custom_call" | custom-call | flops 2378170368 | bytes 2359296 | tf_op jit(solution)/shard_map/begin/pallas_call | solution.py:433
  27.8 0.0 collective-permute-done.8.first_left_ref
  27.8 0.0 copy-done
  27.8 0.0 copy-done.1
  27.8 2.5 %update.1 = (f32[576,128]{1,0:T(8,128)}, f32[576,128]{1,0:T(8,128)}, f32[4,48,384]{2,1,0:T(8,128)S(1)}, f32[4,48,384]{2,1,0:T(8,128)S(1)}) custom-call(f32[384,256]{1,0:T(8,128)S(1)} %get-tuple-element.55.inner_ref, f32[384,384]{1,0:T(8,128)S(1)} %get-tuple-element.52.basis_ref, f32[576,128]{1,0:T(8,128)S(1)} %get-tuple-element.56.left_ref, ...), custom_call_target="tpu_custom_call" | custom-call | flops 679477248 | bytes 2359296 | tf_op jit(solution)/shard_map/update/pallas_call | solution.py:436
  30.3 1.6 %collective-permute-start.10 = (f32[4,48,384]{2,1,0:T(8,128)S(1)}, f32[4,48,384]{2,1,0:T(8,128)S(1)}, u32[]{:S(2)}, u32[]{:S(2)}) collective-permute-start(f32[4,48,384]{2,1,0:T(8,128)S(1)} %get-tuple-element.59), channel_id=1, source_target_pairs={{0,4},{4,0},{8,12},{12,8},{16,20},{20,16},{24,28},{28,24},{1,5},{5... | collective-permute-start | bytes 884744 | tf_op jit(solution)/shard_map/ppermute | solution.py:393
  31.9 6.0 %end.1 = (f32[576,128]{1,0:T(8,128)S(1)}, f32[576,128]{1,0:T(8,128)S(1)}) custom-call(f32[384,384]{1,0:T(8,128)S(1)} %get-tuple-element.60.start_ref), custom_call_target="tpu_custom_call" | custom-call | flops 3057647616 | bytes 2359296 | tf_op jit(solution)/shard_map/end/pallas_call | solution.py:446
  37.9 0.5 collective-permute-start.9
  38.4 0.0 collective-permute-done.10.theirs_ref
  38.5 4.1 %collective-permute-start.11 = (f32[48,384]{1,0:T(8,128)S(1)}, f32[48,384]{1,0:T(8,128)S(1)}, u32[]{:S(2)}, u32[]{:S(2)}) collective-permute-start(f32[48,384]{1,0:T(8,128)S(1)} %get-tuple-element.67), channel_id=1, source_target_pairs={{0,16},{4,20},{8,24},{12,28},{16,0},{20,4},{24,8},{28,12},{1,17},{... | collective-permute-start | bytes 221192 | tf_op jit(solution)/shard_map/ppermute | solution.py:390
  42.6 1.3 %collective-permute-start.12 = (f32[48,384]{1,0:T(8,128)S(1)}, f32[48,384]{1,0:T(8,128)S(1)}, u32[]{:S(2)}, u32[]{:S(2)}) collective-permute-start(f32[48,384]{1,0:T(8,128)S(1)} %get-tuple-element.68), channel_id=1, source_target_pairs={{0,24},{4,28},{8,16},{12,20},{16,8},{20,12},{24,0},{28,4},{1,25},{... | collective-permute-start | bytes 221192 | tf_op jit(solution)/shard_map/ppermute | solution.py:390
  43.9 0.1 collective-permute-start.13
  44.0 1.7 %stats.1 = (f32[576,128]{1,0:T(8,128)}, f32[576,128]{1,0:T(8,128)}) custom-call(f32[384,384]{1,0:T(8,128)S(1)} %get-tuple-element.74.grad_ref, f32[384,384]{1,0:T(8,128)S(1)} %get-tuple-element.75.new_stat_ref, f32[576,128]{1,0:T(8,128)S(1)} %get-tuple-element.76.other_ref), custom_call_target="tpu_custom_call" | custom-call | flops 339738624 | bytes 2359296 | tf_op jit(solution)/shard_map/stats/pallas_call | solution.py:470
  45.7 0.0 collective-permute-done.9.back_ref
  45.7 0.0 collective-permute-done.11.refs_1_
  45.7 3.2 %collective-permute-done.12.refs_2_ = f32[48,384]{1,0:T(8,128)S(1)} collective-permute-done((f32[48,384]{1,0:T(8,128)S(1)}, f32[48,384]{1,0:T(8,128)S(1)}, u32[]{:S(2)}, u32[]{:S(2)}) %collective-permute-start.12) | collective-permute-done | bytes 73760 | tf_op jit(solution)/shard_map/ppermute | solution.py:390
  48.9 0.2 collective-permute-done.13.refs_3_
  49.0 1.0 %finish.1 = (f32[4,48,384]{2,1,0:T(8,128)}, f32[576,128]{1,0:T(8,128)}, f32[576,128]{1,0:T(8,128)}) custom-call(f32[576,128]{1,0:T(8,128)S(1)} %get-tuple-element.61.keep_ref, f32[576,128]{1,0:T(8,128)S(1)} %collective-permute-done.9.back_ref, f32[48,384]{1,0:T(8,128)S(1)} %get-tuple-element.66.refs_0_, f32[48,384]{1,0:T(8,128)S(1)} %collective-permute-done.11.refs_1_, ...), custom_call_target="tpu_custom_call" | custom-call | flops 33973864 | bytes 2359296 | tf_op jit(solution)/shard_map/finish/pallas_call | solution.py:455
  (2 shorter events, 0.0 us)
Async XLA Ops:
  0.6 19.0 %copy-start.2 = (f32[1,73728]{1,0:T(1,128)S(1)}, f32[1,73728]{1,0:T(1,128)}, u32[]{:S(2)}) copy-start(f32[1,73728]{1,0:T(1,128)} %param.10) | copy-start | bytes 884740
  0.6 19.0 %copy-start.3 = (f32[1,73728]{1,0:T(1,128)S(1)}, f32[1,73728]{1,0:T(1,128)}, u32[]{:S(2)}) copy-start(f32[1,73728]{1,0:T(1,128)} %param.11) | copy-start | bytes 884740
  0.7 19.0 %copy-start.4 = (f32[1,73728]{1,0:T(1,128)S(1)}, f32[1,73728]{1,0:T(1,128)}, u32[]{:S(2)}) copy-start(f32[1,73728]{1,0:T(1,128)} %param.13) | copy-start | bytes 884740
  0.7 19.0 %copy-start.5 = (f32[4,48,384]{2,1,0:T(8,128)S(1)}, f32[4,48,384]{2,1,0:T(8,128)}, u32[]{:S(2)}) copy-start(f32[4,48,384]{2,1,0:T(8,128)} %refs_0_.1) | copy-start | bytes 884740
  0.7 19.0 %copy-start.6 = (f32[1,73728]{1,0:T(1,128)S(1)}, f32[1,73728]{1,0:T(1,128)}, u32[]{:S(2)}) copy-start(f32[1,73728]{1,0:T(1,128)} %param.12) | copy-start | bytes 884740
  2.0 17.6 %collective-permute-start = (f32[720,128]{1,0:T(8,128)S(1)}, f32[720,128]{1,0:T(8,128)S(1)}, u32[]{:S(2)}, u32[]{:S(2)}) collective-permute-start(f32[720,128]{1,0:T(8,128)S(1)} %get-tuple-element.44), channel_id=1, source_target_pairs={{0,4},{4,0},{8,12},{12,8},{16,20},{20,16},{24,28},{28,24},{1,5},{5... | collective-permute-start | bytes 1105928 | tf_op jit(solution)/shard_map/ppermute | solution.py:393
  5.0 7.4 %collective-permute-start.1 = (f32[48,384]{1,0:T(8,128)S(1)}, f32[48,384]{1,0:T(8,128)S(1)}, u32[]{:S(2)}, u32[]{:S(2)}) collective-permute-start(f32[48,384]{1,0:T(8,128)S(1)} %get-tuple-element.45), channel_id=1, source_target_pairs={{0,16},{4,20},{8,24},{12,28},{16,0},{20,4},{24,8},{28,12},{1,17},{... | collective-permute-start | bytes 221192 | tf_op jit(solution)/shard_map/ppermute | solution.py:390
  7.6 6.3 %collective-permute-start.2 = (f32[48,384]{1,0:T(8,128)S(1)}, f32[48,384]{1,0:T(8,128)S(1)}, u32[]{:S(2)}, u32[]{:S(2)}) collective-permute-start(f32[48,384]{1,0:T(8,128)S(1)} %get-tuple-element.46), channel_id=1, source_target_pairs={{0,24},{4,28},{8,16},{12,20},{16,8},{20,12},{24,0},{28,4},{1,25},{... | collective-permute-start | bytes 221192 | tf_op jit(solution)/shard_map/ppermute | solution.py:390
  9.0 5.5 %collective-permute-start.3 = (f32[48,384]{1,0:T(8,128)S(1)}, f32[48,384]{1,0:T(8,128)S(1)}, u32[]{:S(2)}, u32[]{:S(2)}) collective-permute-start(f32[48,384]{1,0:T(8,128)S(1)} %get-tuple-element.47), channel_id=1, source_target_pairs={{0,8},{4,12},{8,0},{12,4},{16,24},{20,28},{24,16},{28,20},{1,9},{5... | collective-permute-start | bytes 221192 | tf_op jit(solution)/shard_map/ppermute | solution.py:390
  12.4 5.2 %collective-permute-start.4 = (f32[48,384]{1,0:T(8,128)S(1)}, f32[48,384]{1,0:T(8,128)S(1)}, u32[]{:S(2)}, u32[]{:S(2)}) collective-permute-start(f32[48,384]{1,0:T(8,128)S(1)} %collective-permute-done.1.refs_1_), channel_id=1, source_target_pairs={{0,4},{4,0},{8,12},{12,8},{16,20},{20,16},{24,28},{28,24},{1,5},{5... | collective-permute-start | bytes 221192 | tf_op jit(solution)/shard_map/ppermute | solution.py:393
  13.9 4.9 %collective-permute-start.5 = (f32[48,384]{1,0:T(8,128)S(1)}, f32[48,384]{1,0:T(8,128)S(1)}, u32[]{:S(2)}, u32[]{:S(2)}) collective-permute-start(f32[48,384]{1,0:T(8,128)S(1)} %collective-permute-done.2.refs_2_), channel_id=1, source_target_pairs={{0,4},{4,0},{8,12},{12,8},{16,20},{20,16},{24,28},{28,24},{1,5},{5... | collective-permute-start | bytes 221192 | tf_op jit(solution)/shard_map/ppermute | solution.py:393
  14.4 5.2 %collective-permute-start.6 = (f32[48,384]{1,0:T(8,128)S(1)}, f32[48,384]{1,0:T(8,128)S(1)}, u32[]{:S(2)}, u32[]{:S(2)}) collective-permute-start(f32[48,384]{1,0:T(8,128)S(1)} %collective-permute-done.3.refs_3_), channel_id=1, source_target_pairs={{0,4},{4,0},{8,12},{12,8},{16,20},{20,16},{24,28},{28,24},{1,5},{5... | collective-permute-start | bytes 221192 | tf_op jit(solution)/shard_map/ppermute | solution.py:393
  16.0 6.6 %collective-permute-start.7 = (f32[192,128]{1,0:T(8,128)S(1)}, f32[192,128]{1,0:T(8,128)S(1)}, u32[]{:S(2)}, u32[]{:S(2)}) collective-permute-start(f32[192,128]{1,0:T(8,128)S(1)} %get-tuple-element.50), channel_id=1, source_target_pairs={{0,4},{4,0},{8,12},{12,8},{16,20},{20,16},{24,28},{28,24},{1,5},{5... | collective-permute-start | bytes 294920 | tf_op jit(solution)/shard_map/ppermute | solution.py:393
  21.0 6.8 %collective-permute-start.8 = (f32[576,128]{1,0:T(8,128)S(1)}, f32[576,128]{1,0:T(8,128)S(1)}, u32[]{:S(2)}, u32[]{:S(2)}) collective-permute-start(f32[576,128]{1,0:T(8,128)S(1)} %bitcast.22), channel_id=1, source_target_pairs={{0,4},{4,0},{8,12},{12,8},{16,20},{20,16},{24,28},{28,24},{1,5},{5... | collective-permute-start | bytes 884744 | tf_op jit(solution)/shard_map/ppermute | solution.py:393
  22.6 5.2 %copy-start = (f32[1,73728]{1,0:T(1,128)S(1)}, f32[1,73728]{1,0:T(1,128)}, u32[]{:S(2)}) copy-start(f32[1,73728]{1,0:T(1,128)} %param.8) | copy-start | bytes 884740
  22.6 5.2 %copy-start.1 = (f32[1,73728]{1,0:T(1,128)S(1)}, f32[1,73728]{1,0:T(1,128)}, u32[]{:S(2)}) copy-start(f32[1,73728]{1,0:T(1,128)} %param.9) | copy-start | bytes 884740
  30.3 8.1 %collective-permute-start.10 = (f32[4,48,384]{2,1,0:T(8,128)S(1)}, f32[4,48,384]{2,1,0:T(8,128)S(1)}, u32[]{:S(2)}, u32[]{:S(2)}) collective-permute-start(f32[4,48,384]{2,1,0:T(8,128)S(1)} %get-tuple-element.59), channel_id=1, source_target_pairs={{0,4},{4,0},{8,12},{12,8},{16,20},{20,16},{24,28},{28,24},{1,5},{5... | collective-permute-start | bytes 884744 | tf_op jit(solution)/shard_map/ppermute | solution.py:393
  37.9 7.8 %collective-permute-start.9 = (f32[576,128]{1,0:T(8,128)S(1)}, f32[576,128]{1,0:T(8,128)S(1)}, u32[]{:S(2)}, u32[]{:S(2)}) collective-permute-start(f32[576,128]{1,0:T(8,128)S(1)} %get-tuple-element.62), channel_id=1, source_target_pairs={{0,4},{4,0},{8,12},{12,8},{16,20},{20,16},{24,28},{28,24},{1,5},{5... | collective-permute-start | bytes 884744 | tf_op jit(solution)/shard_map/ppermute | solution.py:393
  38.5 7.2 %collective-permute-start.11 = (f32[48,384]{1,0:T(8,128)S(1)}, f32[48,384]{1,0:T(8,128)S(1)}, u32[]{:S(2)}, u32[]{:S(2)}) collective-permute-start(f32[48,384]{1,0:T(8,128)S(1)} %get-tuple-element.67), channel_id=1, source_target_pairs={{0,16},{4,20},{8,24},{12,28},{16,0},{20,4},{24,8},{28,12},{1,17},{... | collective-permute-start | bytes 221192 | tf_op jit(solution)/shard_map/ppermute | solution.py:390
  42.6 6.3 %collective-permute-start.12 = (f32[48,384]{1,0:T(8,128)S(1)}, f32[48,384]{1,0:T(8,128)S(1)}, u32[]{:S(2)}, u32[]{:S(2)}) collective-permute-start(f32[48,384]{1,0:T(8,128)S(1)} %get-tuple-element.68), channel_id=1, source_target_pairs={{0,24},{4,28},{8,16},{12,20},{16,8},{20,12},{24,0},{28,4},{1,25},{... | collective-permute-start | bytes 221192 | tf_op jit(solution)/shard_map/ppermute | solution.py:390
  43.9 5.1 %collective-permute-start.13 = (f32[48,384]{1,0:T(8,128)S(1)}, f32[48,384]{1,0:T(8,128)S(1)}, u32[]{:S(2)}, u32[]{:S(2)}) collective-permute-start(f32[48,384]{1,0:T(8,128)S(1)} %get-tuple-element.69), channel_id=1, source_target_pairs={{0,8},{4,12},{8,0},{12,4},{16,24},{20,28},{24,16},{28,20},{1,9},{5... | collective-permute-start | bytes 221192 | tf_op jit(solution)/shard_map/ppermute | solution.py:390

commit v5 on v4

--- a/solution.py
+++ b/solution.py
@@ -33,6 +33,17 @@
     left = jnp.concatenate([a[0], a[0], a[1]], axis=ka)
     right = jnp.concatenate([b[0], b[1], b[0]], axis=kb)
     return lax.dot_general(left, right, (dims, ((), ())), preferred_element_type=F32)
+
+
+def symmetric_dot(a, b, dims=((1,), (0,))):
+    (ka,), (kb,) = dims
+    cut = a[0].shape[0] - LANES
+    head = lambda x, axis: lax.slice_in_dim(x, 0, cut, axis=axis)
+    tail = lambda x, axis: lax.slice_in_dim(x, cut, cut + LANES, axis=axis)
+    left = dot_parts(a, [head(x, 1 - kb) for x in b], dims)
+    corner = dot_parts([tail(x, 1 - ka) for x in a], [tail(x, 1 - kb) for x in b], dims)
+    right = jnp.concatenate([left[cut:].T, corner], axis=0)
+    return jnp.concatenate([left, right], axis=1)
 
 
 def swap(x):
@@ -195,15 +206,18 @@
     grad_ref[pl.ds(pl.multiple_of(block * rows, 8), rows), :] = value
 
 
+def polynomial(parts):
+    gram = symmetric_dot(parts, parts, ((1,), (1,)))
+    gram_parts = split(gram)
+    return CUBIC_COEFF * gram + QUINTIC_COEFF * symmetric_dot(gram_parts, gram_parts)
+
+
 def iterate(x_ref, steps):
     @pl.loop(0, steps)
     def _(step):
         x = x_ref[...]
         parts = split(x)
-        gram = dot_parts(parts, parts, ((1,), (1,)))
-        gram_parts = split(gram)
-        poly = CUBIC_COEFF * gram + QUINTIC_COEFF * dot_parts(gram_parts, gram_parts)
-        x_ref[...] = LINEAR_COEFF * x + dot_parts(split(poly), parts)
+        x_ref[...] = LINEAR_COEFF * x + dot_parts(split(polynomial(parts)), parts)
 
 
 def products_kernel(hops, l_stat_ref, r_stat_ref, l_basis_ref, r_basis_ref, got_ref, *refs):
@@ -233,8 +247,8 @@
     right = half_of(scratch, thirds(r_basis_ref))
     right_ref[...] = right
     grad = grad_ref[...]
-    turned = grad.T
-    product_ref[...] = dot(jnp.where(left, grad, turned), jnp.where(left, turned, grad))
+    parts = split(jnp.where(left, grad, grad.T))
+    product_ref[...] = symmetric_dot(parts, parts, ((1,), (1,)))
     inner_ref[...] = dot(grad, right)
 
 
@@ -246,13 +260,14 @@
     iterate(x_ref, steps)
 
 
-def end_kernel(steps, start_ref, keep_ref, send_ref, scratch, x_ref):
-    left = is_left()
+def end_kernel(steps, start_ref, x_ref, poly_ref, send_ref, scratch):
     x_ref[...] = start_ref[...]
-    iterate(x_ref, steps)
+    iterate(x_ref, steps - 1)
     x = x_ref[...]
-    put_thirds(send_ref, flat_of(scratch, take_half(x, jnp.logical_not(left))))
-    put_thirds(keep_ref, flat_of(scratch, take_half(x, left)))
+    poly = polynomial(split(x))
+    poly_ref[...] = poly
+    half = take_half(x, jnp.logical_not(is_left()))
+    put_thirds(send_ref, flat_of(scratch, LINEAR_COEFF * half + dot(poly, half)))
 
 
 def update_kernel(
@@ -332,8 +347,10 @@
         copy.wait()
 
 
-def stats_kernel(grad_ref, new_stat_ref, other_ref, new_left_ref, new_right_ref, scratch):
+def rest_kernel(x_ref, poly_ref, grad_ref, new_stat_ref, other_ref, keep_ref, new_left_ref, new_right_ref, scratch):
     left = is_left()
+    half = take_half(x_ref[...], left)
+    put_thirds(keep_ref, flat_of(scratch, LINEAR_COEFF * half + dot(poly_ref[...], half)))
     grad = grad_ref[...]
     turned = grad.T
     a = jnp.where(left, grad, turned)
@@ -443,10 +460,13 @@
         own_rows = lax.dynamic_index_in_dim(merged, parity, 1, keepdims=False)
         other_rows = lax.dynamic_index_in_dim(merged, 1 - parity, 1, keepdims=False)
     got_rows = partner(other_rows)
-    keep, send = call(
-        functools.partial(end_kernel, NS_ITERS - 2), [flat, flat], [(3, full, LANES), square], 9, full, "end"
+    x, poly, send = call(
+        functools.partial(end_kernel, NS_ITERS - 2), [square, square, flat], [(3, full, LANES)], 9, full, "end"
     )(after(x, other_rows))
     back = partner(send)
+    keep, new_left, new_right = call(rest_kernel, [flat, flat, flat], [(3, full, LANES)], 1.5, full, "rest")(
+        x, poly, grad, new_stat, other
+    )
     if near:
         kept, *sums = call(add_kernel, [block] * (1 + len(hops)), [], 0.1, full, "add")(
             after(own_rows, send), after(got_rows, send)
@@ -467,9 +487,6 @@
         update = exchange(after(own_rows, send) + after(got_rows, send))
         new_l_basis = jnp.where(parity == 0, keep, back)
         new_r_basis = jnp.where(parity == 0, back, keep)
-    new_left, new_right = call(stats_kernel, [flat, flat], [(3, full, LANES)], 1, full, "stats")(
-        after(grad, send), new_stat, other
-    )
     halves = (new_one, new_two, new_left, new_right, new_l_basis, new_r_basis)
     return (update, *(x.reshape(1, flat_rows * LANES) for x in halves))
 

time: 50.2 us -> 49.6 us (0.988)
  no operation moved by 1% of the time
where the time goes in v5:
time: 49.6 us; the launch traced here: 49.5 us
  starting transfers between devices  19.3 us (39%)
  Pallas kernels  19 us (38%)
  waiting for transfers between devices  10.4 us (21%)
  between operations  0.76 us (2%)
    ppermute x8, starting transfers between devices, partner(): return lax.ppermute(x, 'shard', pairs)  9.74 us
    ppermute x6, starting transfers between devices, hop_by(): return lax.ppermute(x, 'shard', [(i, i ^ 2 * hop) for i in range(size)])  9.57 us
    ppermute x6, waiting for transfers between devices, hop_by(): return lax.ppermute(x, 'shard', [(i, i ^ 2 * hop) for i in range(size)])  7.28 us
    pallas_call x1, Pallas kernels, local(): call(functools.partial(end_kernel, NS_ITERS - 2), [square, square, flat],...  5.69 us
    pallas_call x1, Pallas kernels, local(): call(functools.partial(begin_kernel, 2), [square] * 2, [(3, full, LANES)]...  5.29 us
    ppermute x8, waiting for transfers between devices, partner(): return lax.ppermute(x, 'shard', pairs)  3.14 us
    pallas_call x1, Pallas kernels, local(): call(functools.partial(update_kernel, hops), [flat, flat, strips, strips]...  2.51 us
    pallas_call x1, Pallas kernels, local(): call(rest_kernel, [flat, flat, flat], [(3, full, LANES)], 1.5, full, 'rest')  2.06 us
  transfers between devices with their start and end apart: 14, of which 7 were waited for; matrix products, arithmetic and copies ran while one was open for 0% of the time, Pallas kernels for 29%

profile of v5, /device:TPU:0, one launch (start us, length us, event | category | flops | bytes accessed | tf_op | source)
XLA Modules:
  0.0 49.5 jit_solution(2330501118082043239)
XLA Ops:
  0.6 0.0 copy-start.2
  0.6 0.0 copy-start.3
  0.7 0.0 copy-start.4
  0.7 0.0 copy-start.5
  0.7 0.0 copy-start.6
  0.7 1.3 %pack.1 = (f32[720,128]{1,0:T(8,128)S(1)}, f32[192,128]{1,0:T(8,128)S(1)}, f32[48,384]{1,0:T(8,128)S(1)}, f32[48,384]{1,0:T(8,128)S(1)}, f32[48,384]{1,0:T(8,128)S(1)}) custom-call(f32[576,128]{1,0:T(8,128)} %bitcast.14, f32[576,128]{1,0:T(8,128)} %bitcast.16, f32[576,128]{1,0:T(8,128)} %bitcast.20, f32[576,128]{1,0:T(8,128)} %bitcast.18, f32[4,48,384]{2,1,0:T(8,128)} %refs_0_.1), custom_call_target="tpu_custom_call" | custom-call | flops 33973864 | bytes 2359296 | tf_op jit(solution)/shard_map/pack/pallas_call | solution.py:417
  2.0 3.0 %collective-permute-start = (f32[720,128]{1,0:T(8,128)S(1)}, f32[720,128]{1,0:T(8,128)S(1)}, u32[]{:S(2)}, u32[]{:S(2)}) collective-permute-start(f32[720,128]{1,0:T(8,128)S(1)} %get-tuple-element.45), channel_id=1, source_target_pairs={{0,4},{4,0},{8,12},{12,8},{16,20},{20,16},{24,28},{28,24},{1,5},{5... | collective-permute-start | bytes 1105928 | tf_op jit(solution)/shard_map/ppermute | solution.py:410
  5.0 2.6 %collective-permute-start.1 = (f32[48,384]{1,0:T(8,128)S(1)}, f32[48,384]{1,0:T(8,128)S(1)}, u32[]{:S(2)}, u32[]{:S(2)}) collective-permute-start(f32[48,384]{1,0:T(8,128)S(1)} %get-tuple-element.46), channel_id=1, source_target_pairs={{0,16},{4,20},{8,24},{12,28},{16,0},{20,4},{24,8},{28,12},{1,17},{... | collective-permute-start | bytes 221192 | tf_op jit(solution)/shard_map/ppermute | solution.py:407
  7.6 1.3 %collective-permute-start.2 = (f32[48,384]{1,0:T(8,128)S(1)}, f32[48,384]{1,0:T(8,128)S(1)}, u32[]{:S(2)}, u32[]{:S(2)}) collective-permute-start(f32[48,384]{1,0:T(8,128)S(1)} %get-tuple-element.47), channel_id=1, source_target_pairs={{0,24},{4,28},{8,16},{12,20},{16,8},{20,12},{24,0},{28,4},{1,25},{... | collective-permute-start | bytes 221192 | tf_op jit(solution)/shard_map/ppermute | solution.py:407
  9.0 0.2 collective-permute-start.3
  9.2 3.2 %collective-permute-done.1.refs_1_ = f32[48,384]{1,0:T(8,128)S(1)} collective-permute-done((f32[48,384]{1,0:T(8,128)S(1)}, f32[48,384]{1,0:T(8,128)S(1)}, u32[]{:S(2)}, u32[]{:S(2)}) %collective-permute-start.1) | collective-permute-done | bytes 73760 | tf_op jit(solution)/shard_map/ppermute | solution.py:407
  12.4 0.5 collective-permute-start.4
  12.9 1.1 %collective-permute-done.2.refs_2_ = f32[48,384]{1,0:T(8,128)S(1)} collective-permute-done((f32[48,384]{1,0:T(8,128)S(1)}, f32[48,384]{1,0:T(8,128)S(1)}, u32[]{:S(2)}, u32[]{:S(2)}) %collective-permute-start.2) | collective-permute-done | bytes 73760 | tf_op jit(solution)/shard_map/ppermute | solution.py:407
  13.9 0.5 %collective-permute-start.5 = (f32[48,384]{1,0:T(8,128)S(1)}, f32[48,384]{1,0:T(8,128)S(1)}, u32[]{:S(2)}, u32[]{:S(2)}) collective-permute-start(f32[48,384]{1,0:T(8,128)S(1)} %collective-permute-done.2.refs_2_), channel_id=1, source_target_pairs={{0,4},{4,0},{8,12},{12,8},{16,20},{20,16},{24,28},{28,24},{1,5},{5... | collective-permute-start | bytes 221192 | tf_op jit(solution)/shard_map/ppermute | solution.py:410
  14.4 0.0 collective-permute-done.3.refs_3_
  14.4 1.5 %collective-permute-start.6 = (f32[48,384]{1,0:T(8,128)S(1)}, f32[48,384]{1,0:T(8,128)S(1)}, u32[]{:S(2)}, u32[]{:S(2)}) collective-permute-start(f32[48,384]{1,0:T(8,128)S(1)} %collective-permute-done.3.refs_3_), channel_id=1, source_target_pairs={{0,4},{4,0},{8,12},{12,8},{16,20},{20,16},{24,28},{28,24},{1,5},{5... | collective-permute-start | bytes 221192 | tf_op jit(solution)/shard_map/ppermute | solution.py:410
  16.0 0.5 %collective-permute-start.7 = (f32[192,128]{1,0:T(8,128)S(1)}, f32[192,128]{1,0:T(8,128)S(1)}, u32[]{:S(2)}, u32[]{:S(2)}) collective-permute-start(f32[192,128]{1,0:T(8,128)S(1)} %get-tuple-element.51), channel_id=1, source_target_pairs={{0,4},{4,0},{8,12},{12,8},{16,20},{20,16},{24,28},{28,24},{1,5},{5... | collective-permute-start | bytes 294920 | tf_op jit(solution)/shard_map/ppermute | solution.py:410
  16.5 1.1 %collective-permute-done.4.refs_4_ = f32[48,384]{1,0:T(8,128)S(1)} collective-permute-done((f32[48,384]{1,0:T(8,128)S(1)}, f32[48,384]{1,0:T(8,128)S(1)}, u32[]{:S(2)}, u32[]{:S(2)}) %collective-permute-start.4) | collective-permute-done | bytes 73760 | tf_op jit(solution)/shard_map/ppermute | solution.py:410
  17.6 1.2 %collective-permute-done.5.refs_5_ = f32[48,384]{1,0:T(8,128)S(1)} collective-permute-done((f32[48,384]{1,0:T(8,128)S(1)}, f32[48,384]{1,0:T(8,128)S(1)}, u32[]{:S(2)}, u32[]{:S(2)}) %collective-permute-start.5) | collective-permute-done | bytes 73760 | tf_op jit(solution)/shard_map/ppermute | solution.py:410
  18.8 0.8 %collective-permute-done.6.refs_6_ = f32[48,384]{1,0:T(8,128)S(1)} collective-permute-done((f32[48,384]{1,0:T(8,128)S(1)}, f32[48,384]{1,0:T(8,128)S(1)}, u32[]{:S(2)}, u32[]{:S(2)}) %collective-permute-start.6) | collective-permute-done | bytes 73760 | tf_op jit(solution)/shard_map/ppermute | solution.py:410
  19.6 0.0 collective-permute-done.got_ref
  19.6 0.0 copy-done.2
  19.6 0.0 copy-done.3
  19.6 0.0 copy-done.4
  19.6 0.0 copy-done.5
  19.6 0.0 copy-done.6
  19.6 1.1 %products.1 = (f32[384,384]{1,0:T(8,128)S(1)}, f32[384,384]{1,0:T(8,128)S(1)}, f32[384,384]{1,0:T(8,128)S(1)}, f32[384,256]{1,0:T(8,128)S(1)}, f32[384,256]{1,0:...) custom-call(f32[576,128]{1,0:T(8,128)S(1)} %bitcast.15, ...), custom_call_target="tpu_custom_call" | custom-call | flops 679477248 | bytes 2359296 | tf_op jit(solution)/shard_map/products/pallas_call | solution.py:441
  20.8 1.6 %collective-permute-start.8 = (f32[576,128]{1,0:T(8,128)S(1)}, f32[576,128]{1,0:T(8,128)S(1)}, u32[]{:S(2)}, u32[]{:S(2)}) collective-permute-start(f32[576,128]{1,0:T(8,128)S(1)} %bitcast.22), channel_id=1, source_target_pairs={{0,4},{4,0},{8,12},{12,8},{16,20},{20,16},{24,28},{28,24},{1,5},{5... | collective-permute-start | bytes 884744 | tf_op jit(solution)/shard_map/ppermute | solution.py:410
  22.4 0.0 collective-permute-done.7.corner_ref
  22.4 0.0 copy-start
  22.4 5.3 %begin.1 = (f32[384,384]{1,0:T(8,128)S(1)}, f32[384,384]{1,0:T(8,128)S(1)}) custom-call(f32[576,128]{1,0:T(8,128)S(1)} %get-tuple-element.49.own_ref, f32[192,128]{1,0:T(8,128)S(1)} %collective-permute-done.7.corner_ref, f32[384,384]{1,0:T(8,128)S(1)} %get-tuple-element.52.product_ref, f32[384,384]{1,0:T(8,128)S(1)} %get-tuple-element.53.basis_ref), custom_call_target="tpu_custom_call" | custom-call | flops 2378170368 | bytes 2359296 | tf_op jit(solution)/shard_map/begin/pallas_call | solution.py:450
  27.7 0.0 collective-permute-done.8.first_left_ref
  27.7 0.0 copy-done
  27.7 0.0 copy-done.1
  27.7 2.5 %update.1 = (f32[576,128]{1,0:T(8,128)}, f32[576,128]{1,0:T(8,128)}, f32[4,48,384]{2,1,0:T(8,128)S(1)}, f32[4,48,384]{2,1,0:T(8,128)S(1)}) custom-call(f32[384,256]{1,0:T(8,128)S(1)} %get-tuple-element.56.inner_ref, f32[384,384]{1,0:T(8,128)S(1)} %get-tuple-element.53.basis_ref, f32[576,128]{1,0:T(8,128)S(1)} %get-tuple-element.57.left_ref, ...), custom_call_target="tpu_custom_call" | custom-call | flops 679477248 | bytes 2359296 | tf_op jit(solution)/shard_map/update/pallas_call | solution.py:453
  30.2 1.5 %collective-permute-start.10 = (f32[4,48,384]{2,1,0:T(8,128)S(1)}, f32[4,48,384]{2,1,0:T(8,128)S(1)}, u32[]{:S(2)}, u32[]{:S(2)}) collective-permute-start(f32[4,48,384]{2,1,0:T(8,128)S(1)} %get-tuple-element.60), channel_id=1, source_target_pairs={{0,4},{4,0},{8,12},{12,8},{16,20},{20,16},{24,28},{28,24},{1,5},{5... | collective-permute-start | bytes 884744 | tf_op jit(solution)/shard_map/ppermute | solution.py:410
  31.7 5.7 %end.1 = (f32[384,384]{1,0:T(8,128)S(1)}, f32[384,384]{1,0:T(8,128)S(1)}, f32[576,128]{1,0:T(8,128)S(1)}) custom-call(f32[384,384]{1,0:T(8,128)S(1)} %get-tuple-element.61.start_ref), custom_call_target="tpu_custom_call" | custom-call | flops 3057647616 | bytes 2359296 | tf_op jit(solution)/shard_map/end/pallas_call | solution.py:463
  37.4 0.6 %collective-permute-start.9 = (f32[576,128]{1,0:T(8,128)S(1)}, f32[576,128]{1,0:T(8,128)S(1)}, u32[]{:S(2)}, u32[]{:S(2)}) collective-permute-start(f32[576,128]{1,0:T(8,128)S(1)} %get-tuple-element.68), channel_id=1, source_target_pairs={{0,4},{4,0},{8,12},{12,8},{16,20},{20,16},{24,28},{28,24},{1,5},{5... | collective-permute-start | bytes 884744 | tf_op jit(solution)/shard_map/ppermute | solution.py:410
  38.0 0.0 collective-permute-done.10.theirs_ref
  38.1 4.0 %collective-permute-start.11 = (f32[48,384]{1,0:T(8,128)S(1)}, f32[48,384]{1,0:T(8,128)S(1)}, u32[]{:S(2)}, u32[]{:S(2)}) collective-permute-start(f32[48,384]{1,0:T(8,128)S(1)} %get-tuple-element.73), channel_id=1, source_target_pairs={{0,16},{4,20},{8,24},{12,28},{16,0},{20,4},{24,8},{28,12},{1,17},{... | collective-permute-start | bytes 221192 | tf_op jit(solution)/shard_map/ppermute | solution.py:407
  42.1 1.3 %collective-permute-start.12 = (f32[48,384]{1,0:T(8,128)S(1)}, f32[48,384]{1,0:T(8,128)S(1)}, u32[]{:S(2)}, u32[]{:S(2)}) collective-permute-start(f32[48,384]{1,0:T(8,128)S(1)} %get-tuple-element.74), channel_id=1, source_target_pairs={{0,24},{4,28},{8,16},{12,20},{16,8},{20,12},{24,0},{28,4},{1,25},{... | collective-permute-start | bytes 221192 | tf_op jit(solution)/shard_map/ppermute | solution.py:407
  43.4 0.1 collective-permute-start.13
  43.5 2.1 %rest.1 = (f32[576,128]{1,0:T(8,128)S(1)}, f32[576,128]{1,0:T(8,128)}, f32[576,128]{1,0:T(8,128)}) custom-call(f32[384,384]{1,0:T(8,128)S(1)} %get-tuple-element.62.x_ref, f32[384,384]{1,0:T(8,128)S(1)} %get-tuple-element.63.poly_ref, f32[384,384]{1,0:T(8,128)S(1)} %get-tuple-element.64.grad_ref, f32[384,384]{1,0:T(8,128)S(1)} %get-tuple-element.65.new_stat_ref, ...), custom_call_target="tpu_custom_call" | custom-call | flops 509607936 | bytes 2359296 | tf_op jit(solution)/shard_map/rest/pallas_call | solution.py:467
  45.5 0.0 collective-permute-done.9.back_ref
  45.5 0.0 collective-permute-done.11.refs_1_
  45.5 2.8 %collective-permute-done.12.refs_2_ = f32[48,384]{1,0:T(8,128)S(1)} collective-permute-done((f32[48,384]{1,0:T(8,128)S(1)}, f32[48,384]{1,0:T(8,128)S(1)}, u32[]{:S(2)}, u32[]{:S(2)}) %collective-permute-start.12) | collective-permute-done | bytes 73760 | tf_op jit(solution)/shard_map/ppermute | solution.py:407
  48.3 0.2 collective-permute-done.13.refs_3_
  48.5 1.0 %finish.1 = (f32[4,48,384]{2,1,0:T(8,128)}, f32[576,128]{1,0:T(8,128)}, f32[576,128]{1,0:T(8,128)}) custom-call(f32[576,128]{1,0:T(8,128)S(1)} %get-tuple-element.67.keep_ref, f32[576,128]{1,0:T(8,128)S(1)} %collective-permute-done.9.back_ref, f32[48,384]{1,0:T(8,128)S(1)} %get-tuple-element.72.refs_0_, f32[48,384]{1,0:T(8,128)S(1)} %collective-permute-done.11.refs_1_, ...), custom_call_target="tpu_custom_call" | custom-call | flops 33973864 | bytes 2359296 | tf_op jit(solution)/shard_map/finish/pallas_call | solution.py:475
  (2 shorter events, 0.0 us)
Async XLA Ops:
  0.6 19.0 %copy-start.2 = (f32[1,73728]{1,0:T(1,128)S(1)}, f32[1,73728]{1,0:T(1,128)}, u32[]{:S(2)}) copy-start(f32[1,73728]{1,0:T(1,128)} %param.10) | copy-start | bytes 884740
  0.6 19.0 %copy-start.3 = (f32[1,73728]{1,0:T(1,128)S(1)}, f32[1,73728]{1,0:T(1,128)}, u32[]{:S(2)}) copy-start(f32[1,73728]{1,0:T(1,128)} %param.11) | copy-start | bytes 884740
  0.7 19.0 %copy-start.4 = (f32[1,73728]{1,0:T(1,128)S(1)}, f32[1,73728]{1,0:T(1,128)}, u32[]{:S(2)}) copy-start(f32[1,73728]{1,0:T(1,128)} %param.13) | copy-start | bytes 884740
  0.7 19.0 %copy-start.5 = (f32[4,48,384]{2,1,0:T(8,128)S(1)}, f32[4,48,384]{2,1,0:T(8,128)}, u32[]{:S(2)}) copy-start(f32[4,48,384]{2,1,0:T(8,128)} %refs_0_.1) | copy-start | bytes 884740
  0.7 19.0 %copy-start.6 = (f32[1,73728]{1,0:T(1,128)S(1)}, f32[1,73728]{1,0:T(1,128)}, u32[]{:S(2)}) copy-start(f32[1,73728]{1,0:T(1,128)} %param.12) | copy-start | bytes 884740
  2.0 17.6 %collective-permute-start = (f32[720,128]{1,0:T(8,128)S(1)}, f32[720,128]{1,0:T(8,128)S(1)}, u32[]{:S(2)}, u32[]{:S(2)}) collective-permute-start(f32[720,128]{1,0:T(8,128)S(1)} %get-tuple-element.45), channel_id=1, source_target_pairs={{0,4},{4,0},{8,12},{12,8},{16,20},{20,16},{24,28},{28,24},{1,5},{5... | collective-permute-start | bytes 1105928 | tf_op jit(solution)/shard_map/ppermute | solution.py:410
  5.0 7.4 %collective-permute-start.1 = (f32[48,384]{1,0:T(8,128)S(1)}, f32[48,384]{1,0:T(8,128)S(1)}, u32[]{:S(2)}, u32[]{:S(2)}) collective-permute-start(f32[48,384]{1,0:T(8,128)S(1)} %get-tuple-element.46), channel_id=1, source_target_pairs={{0,16},{4,20},{8,24},{12,28},{16,0},{20,4},{24,8},{28,12},{1,17},{... | collective-permute-start | bytes 221192 | tf_op jit(solution)/shard_map/ppermute | solution.py:407
  7.6 6.3 %collective-permute-start.2 = (f32[48,384]{1,0:T(8,128)S(1)}, f32[48,384]{1,0:T(8,128)S(1)}, u32[]{:S(2)}, u32[]{:S(2)}) collective-permute-start(f32[48,384]{1,0:T(8,128)S(1)} %get-tuple-element.47), channel_id=1, source_target_pairs={{0,24},{4,28},{8,16},{12,20},{16,8},{20,12},{24,0},{28,4},{1,25},{... | collective-permute-start | bytes 221192 | tf_op jit(solution)/shard_map/ppermute | solution.py:407
  9.0 5.5 %collective-permute-start.3 = (f32[48,384]{1,0:T(8,128)S(1)}, f32[48,384]{1,0:T(8,128)S(1)}, u32[]{:S(2)}, u32[]{:S(2)}) collective-permute-start(f32[48,384]{1,0:T(8,128)S(1)} %get-tuple-element.48), channel_id=1, source_target_pairs={{0,8},{4,12},{8,0},{12,4},{16,24},{20,28},{24,16},{28,20},{1,9},{5... | collective-permute-start | bytes 221192 | tf_op jit(solution)/shard_map/ppermute | solution.py:407
  12.4 5.2 %collective-permute-start.4 = (f32[48,384]{1,0:T(8,128)S(1)}, f32[48,384]{1,0:T(8,128)S(1)}, u32[]{:S(2)}, u32[]{:S(2)}) collective-permute-start(f32[48,384]{1,0:T(8,128)S(1)} %collective-permute-done.1.refs_1_), channel_id=1, source_target_pairs={{0,4},{4,0},{8,12},{12,8},{16,20},{20,16},{24,28},{28,24},{1,5},{5... | collective-permute-start | bytes 221192 | tf_op jit(solution)/shard_map/ppermute | solution.py:410
  13.9 4.9 %collective-permute-start.5 = (f32[48,384]{1,0:T(8,128)S(1)}, f32[48,384]{1,0:T(8,128)S(1)}, u32[]{:S(2)}, u32[]{:S(2)}) collective-permute-start(f32[48,384]{1,0:T(8,128)S(1)} %collective-permute-done.2.refs_2_), channel_id=1, source_target_pairs={{0,4},{4,0},{8,12},{12,8},{16,20},{20,16},{24,28},{28,24},{1,5},{5... | collective-permute-start | bytes 221192 | tf_op jit(solution)/shard_map/ppermute | solution.py:410
  14.4 5.2 %collective-permute-start.6 = (f32[48,384]{1,0:T(8,128)S(1)}, f32[48,384]{1,0:T(8,128)S(1)}, u32[]{:S(2)}, u32[]{:S(2)}) collective-permute-start(f32[48,384]{1,0:T(8,128)S(1)} %collective-permute-done.3.refs_3_), channel_id=1, source_target_pairs={{0,4},{4,0},{8,12},{12,8},{16,20},{20,16},{24,28},{28,24},{1,5},{5... | collective-permute-start | bytes 221192 | tf_op jit(solution)/shard_map/ppermute | solution.py:410
  16.0 6.4 %collective-permute-start.7 = (f32[192,128]{1,0:T(8,128)S(1)}, f32[192,128]{1,0:T(8,128)S(1)}, u32[]{:S(2)}, u32[]{:S(2)}) collective-permute-start(f32[192,128]{1,0:T(8,128)S(1)} %get-tuple-element.51), channel_id=1, source_target_pairs={{0,4},{4,0},{8,12},{12,8},{16,20},{20,16},{24,28},{28,24},{1,5},{5... | collective-permute-start | bytes 294920 | tf_op jit(solution)/shard_map/ppermute | solution.py:410
  20.8 6.9 %collective-permute-start.8 = (f32[576,128]{1,0:T(8,128)S(1)}, f32[576,128]{1,0:T(8,128)S(1)}, u32[]{:S(2)}, u32[]{:S(2)}) collective-permute-start(f32[576,128]{1,0:T(8,128)S(1)} %bitcast.22), channel_id=1, source_target_pairs={{0,4},{4,0},{8,12},{12,8},{16,20},{20,16},{24,28},{28,24},{1,5},{5... | collective-permute-start | bytes 884744 | tf_op jit(solution)/shard_map/ppermute | solution.py:410
  22.4 5.3 %copy-start = (f32[1,73728]{1,0:T(1,128)S(1)}, f32[1,73728]{1,0:T(1,128)}, u32[]{:S(2)}) copy-start(f32[1,73728]{1,0:T(1,128)} %param.8) | copy-start | bytes 884740
  22.4 5.3 %copy-start.1 = (f32[1,73728]{1,0:T(1,128)S(1)}, f32[1,73728]{1,0:T(1,128)}, u32[]{:S(2)}) copy-start(f32[1,73728]{1,0:T(1,128)} %param.9) | copy-start | bytes 884740
  30.2 7.8 %collective-permute-start.10 = (f32[4,48,384]{2,1,0:T(8,128)S(1)}, f32[4,48,384]{2,1,0:T(8,128)S(1)}, u32[]{:S(2)}, u32[]{:S(2)}) collective-permute-start(f32[4,48,384]{2,1,0:T(8,128)S(1)} %get-tuple-element.60), channel_id=1, source_target_pairs={{0,4},{4,0},{8,12},{12,8},{16,20},{20,16},{24,28},{28,24},{1,5},{5... | collective-permute-start | bytes 884744 | tf_op jit(solution)/shard_map/ppermute | solution.py:410
  37.4 8.1 %collective-permute-start.9 = (f32[576,128]{1,0:T(8,128)S(1)}, f32[576,128]{1,0:T(8,128)S(1)}, u32[]{:S(2)}, u32[]{:S(2)}) collective-permute-start(f32[576,128]{1,0:T(8,128)S(1)} %get-tuple-element.68), channel_id=1, source_target_pairs={{0,4},{4,0},{8,12},{12,8},{16,20},{20,16},{24,28},{28,24},{1,5},{5... | collective-permute-start | bytes 884744 | tf_op jit(solution)/shard_map/ppermute | solution.py:410
  38.1 7.5 %collective-permute-start.11 = (f32[48,384]{1,0:T(8,128)S(1)}, f32[48,384]{1,0:T(8,128)S(1)}, u32[]{:S(2)}, u32[]{:S(2)}) collective-permute-start(f32[48,384]{1,0:T(8,128)S(1)} %get-tuple-element.73), channel_id=1, source_target_pairs={{0,16},{4,20},{8,24},{12,28},{16,0},{20,4},{24,8},{28,12},{1,17},{... | collective-permute-start | bytes 221192 | tf_op jit(solution)/shard_map/ppermute | solution.py:407
  42.1 6.3 %collective-permute-start.12 = (f32[48,384]{1,0:T(8,128)S(1)}, f32[48,384]{1,0:T(8,128)S(1)}, u32[]{:S(2)}, u32[]{:S(2)}) collective-permute-start(f32[48,384]{1,0:T(8,128)S(1)} %get-tuple-element.74), channel_id=1, source_target_pairs={{0,24},{4,28},{8,16},{12,20},{16,8},{20,12},{24,0},{28,4},{1,25},{... | collective-permute-start | bytes 221192 | tf_op jit(solution)/shard_map/ppermute | solution.py:407
  43.4 5.1 %collective-permute-start.13 = (f32[48,384]{1,0:T(8,128)S(1)}, f32[48,384]{1,0:T(8,128)S(1)}, u32[]{:S(2)}, u32[]{:S(2)}) collective-permute-start(f32[48,384]{1,0:T(8,128)S(1)} %get-tuple-element.75), channel_id=1, source_target_pairs={{0,8},{4,12},{8,0},{12,4},{16,24},{20,28},{24,16},{28,20},{1,9},{5... | collective-permute-start | bytes 221192 | tf_op jit(solution)/shard_map/ppermute | solution.py:407

commit v6 on v5

--- a/solution.py
+++ b/solution.py
@@ -207,17 +207,16 @@
 
 
 def polynomial(parts):
-    gram = symmetric_dot(parts, parts, ((1,), (1,)))
+    gram = dot_parts(parts, parts, ((1,), (1,)))
     gram_parts = split(gram)
-    return CUBIC_COEFF * gram + QUINTIC_COEFF * symmetric_dot(gram_parts, gram_parts)
-
-
-def iterate(x_ref, steps):
-    @pl.loop(0, steps)
-    def _(step):
-        x = x_ref[...]
+    return CUBIC_COEFF * gram + QUINTIC_COEFF * dot_parts(gram_parts, gram_parts)
+
+
+def iterate(x, steps):
+    for _ in range(steps):
         parts = split(x)
-        x_ref[...] = LINEAR_COEFF * x + dot_parts(split(polynomial(parts)), parts)
+        x = LINEAR_COEFF * x + dot_parts(split(polynomial(parts)), parts)
+    return x
 
 
 def products_kernel(hops, l_stat_ref, r_stat_ref, l_basis_ref, r_basis_ref, got_ref, *refs):
@@ -256,14 +255,12 @@
     new_stat = 0.5 * statistic(is_left(), thirds(own_ref), corner_ref, scratch) + 0.5 * product_ref[...]
     new_stat_ref[...] = new_stat
     power = dot(new_stat, basis_ref[...])
-    x_ref[...] = power * (1.0 / jnp.sqrt(jnp.sum(power * power) + NORM_EPS))
-    iterate(x_ref, steps)
+    x_ref[...] = iterate(power * (1.0 / jnp.sqrt(jnp.sum(power * power) + NORM_EPS)), steps)
 
 
 def end_kernel(steps, start_ref, x_ref, poly_ref, send_ref, scratch):
-    x_ref[...] = start_ref[...]
-    iterate(x_ref, steps - 1)
-    x = x_ref[...]
+    x = iterate(start_ref[...], steps - 1)
+    x_ref[...] = x
     poly = polynomial(split(x))
     poly_ref[...] = poly
     half = take_half(x, jnp.logical_not(is_left()))
@@ -314,12 +311,8 @@
         out_ref[...] = mine_ref[k] + theirs_ref[k]
 
 
-def finish_kernel(hops, keep_ref, back_ref, *refs):
-    count = 1 + len(hops)
-    rows_refs = refs[:count]
-    update_ref, new_left_ref, new_right_ref, sems = refs[count:]
+def bases_kernel(keep_ref, back_ref, new_left_ref, new_right_ref, sems):
     left = is_left()
-    here = lax.axis_index("shard") // 2
 
     def copies(own_ref, other_ref):
         return [
@@ -337,13 +330,19 @@
         for copy in copies(new_right_ref, new_left_ref):
             copy.start()
 
-    rows = [
-        pltpu.make_async_copy(rows_refs[k], update_ref.at[here ^ hop], sems.at[2 + k])
-        for k, hop in enumerate((0, *hops))
+    for copy in copies(new_left_ref, new_right_ref):
+        copy.wait()
+
+
+def rows_kernel(hops, *refs):
+    rows_refs, (update_ref, sems) = refs[:-2], refs[-2:]
+    here = lax.axis_index("shard") // 2
+    copies = [
+        pltpu.make_async_copy(rows_refs[k], update_ref.at[here ^ hop], sems.at[k]) for k, hop in enumerate((0, *hops))
     ]
-    for copy in rows:
+    for copy in copies:
         copy.start()
-    for copy in rows + copies(new_left_ref, new_right_ref):
+    for copy in copies:
         copy.wait()
 
 
@@ -437,7 +436,7 @@
         even, odd = jnp.where(parity == 0, mine, theirs), jnp.where(parity == 0, theirs, mine)
         rows = (jnp.stack([even, odd], axis=1).reshape(square),)
         mine = [mine]
-    got_corner = partner(after(corner, *mine))
+    got_corner = partner(after(corner, theirs[0] if near else mine[0]))
     grad, product, basis, right, inner, own, other, left = call(
         functools.partial(products_kernel, hops),
         [square, square, square, (full, 2 * LANES), (full, 2 * LANES), flat, flat, flat],
@@ -472,21 +471,22 @@
             after(own_rows, send), after(got_rows, send)
         )
         returned = [hop_by(x, hop) for hop, x in zip(hops, sums)]
-        update, new_l_basis, new_r_basis = call(
-            functools.partial(finish_kernel, hops),
-            [grads.shape, flat, flat],
+        update = call(
+            functools.partial(rows_kernel, hops),
+            [grads.shape],
             [],
             0.1,
             full,
-            "finish",
-            copies=3 + len(hops),
-            in_specs=anywhere(3 + len(hops)),
-            out_specs=anywhere(3),
-        )(keep, back, kept, *returned)
+            "rows",
+            copies=1 + len(hops),
+            in_specs=anywhere(1 + len(hops)),
+            out_specs=anywhere(1),
+        )(kept, *returned)[0]
     else:
         update = exchange(after(own_rows, send) + after(got_rows, send))
-        new_l_basis = jnp.where(parity == 0, keep, back)
-        new_r_basis = jnp.where(parity == 0, back, keep)
+    new_l_basis, new_r_basis = call(
+        bases_kernel, [flat, flat], [], 0.1, full, "bases", copies=2, in_specs=anywhere(2), out_specs=anywhere(2)
+    )(keep, back)
     halves = (new_one, new_two, new_left, new_right, new_l_basis, new_r_basis)
     return (update, *(x.reshape(1, flat_rows * LANES) for x in halves))
 

time: 49.6 us -> 49.4 us (level)
  waiting for transfers between devices: 10.4 us -> 9.3 us
  starting transfers between devices: 19.3 us -> 19.8 us
    ppermute x6, waiting for transfers between devices: 7.28 us -> 6.21 us  [hop_by(): return lax.ppermute(x, 'shard', [(i, i ^ 2 * hop) for i in range(size)])]
    pallas_call x1 -> x2, Pallas kernels: 0.95 us -> 1.57 us  [the longest x1 0.83 us: local(): call(bases_kernel, [flat, flat], [], 0.1, full, 'bases', copies=2, in_spe...]
  transfers between devices with their start and end apart: 14 -> 14, of which waited for: 7 -> 8; matrix products, arithmetic and copies ran while one was open for 0% -> 0% of each run, Pallas kernels for 29% -> 30%
where the time goes in v6:
time: 49.4 us; the launch traced here: 49.2 us
  starting transfers between devices  19.8 us (40%)
  Pallas kernels  19.3 us (39%)
  waiting for transfers between devices  9.3 us (19%)
  between operations  0.76 us (2%)
    ppermute x8, starting transfers between devices, partner(): return lax.ppermute(x, 'shard', pairs)  10.2 us
    ppermute x6, starting transfers between devices, hop_by(): return lax.ppermute(x, 'shard', [(i, i ^ 2 * hop) for i in range(size)])  9.6 us
    ppermute x6, waiting for transfers between devices, hop_by(): return lax.ppermute(x, 'shard', [(i, i ^ 2 * hop) for i in range(size)])  6.21 us
    pallas_call x1, Pallas kernels, local(): call(functools.partial(end_kernel, NS_ITERS - 2), [square, square, flat],...  5.67 us
    pallas_call x1, Pallas kernels, local(): call(functools.partial(begin_kernel, 2), [square] * 2, [(3, full, LANES)]...  5.06 us
    ppermute x8, waiting for transfers between devices, partner(): return lax.ppermute(x, 'shard', pairs)  3.08 us
    pallas_call x1, Pallas kernels, local(): call(functools.partial(update_kernel, hops), [flat, flat, strips, strips]...  2.51 us
    pallas_call x1, Pallas kernels, local(): call(rest_kernel, [flat, flat, flat], [(3, full, LANES)], 1.5, full, 'rest')  2.06 us
  transfers between devices with their start and end apart: 14, of which 8 were waited for; matrix products, arithmetic and copies ran while one was open for 0% of the time, Pallas kernels for 30%

profile of v6, /device:TPU:0, one launch (start us, length us, event | category | flops | bytes accessed | tf_op | source)
XLA Modules:
  0.0 49.2 jit_solution(15341618950198464467)
XLA Ops:
  0.6 0.0 copy-start.2
  0.6 0.0 copy-start.3
  0.7 0.0 copy-start.4
  0.7 0.0 copy-start.5
  0.7 0.0 copy-start.6
  0.7 1.3 %pack.1 = (f32[720,128]{1,0:T(8,128)S(1)}, f32[192,128]{1,0:T(8,128)S(1)}, f32[48,384]{1,0:T(8,128)S(1)}, f32[48,384]{1,0:T(8,128)S(1)}, f32[48,384]{1,0:T(8,128)S(1)}) custom-call(f32[576,128]{1,0:T(8,128)} %bitcast.14, f32[576,128]{1,0:T(8,128)} %bitcast.16, f32[576,128]{1,0:T(8,128)} %bitcast.20, f32[576,128]{1,0:T(8,128)} %bitcast.18, f32[4,48,384]{2,1,0:T(8,128)} %refs_0_.1), custom_call_target="tpu_custom_call" | custom-call | flops 33973864 | bytes 2359296 | tf_op jit(solution)/shard_map/pack/pallas_call | solution.py:416
  2.0 3.0 %collective-permute-start = (f32[720,128]{1,0:T(8,128)S(1)}, f32[720,128]{1,0:T(8,128)S(1)}, u32[]{:S(2)}, u32[]{:S(2)}) collective-permute-start(f32[720,128]{1,0:T(8,128)S(1)} %get-tuple-element.44), channel_id=1, source_target_pairs={{0,4},{4,0},{8,12},{12,8},{16,20},{20,16},{24,28},{28,24},{1,5},{5... | collective-permute-start | bytes 1105928 | tf_op jit(solution)/shard_map/ppermute | solution.py:409
  5.0 2.6 %collective-permute-start.1 = (f32[48,384]{1,0:T(8,128)S(1)}, f32[48,384]{1,0:T(8,128)S(1)}, u32[]{:S(2)}, u32[]{:S(2)}) collective-permute-start(f32[48,384]{1,0:T(8,128)S(1)} %get-tuple-element.45), channel_id=1, source_target_pairs={{0,16},{4,20},{8,24},{12,28},{16,0},{20,4},{24,8},{28,12},{1,17},{... | collective-permute-start | bytes 221192 | tf_op jit(solution)/shard_map/ppermute | solution.py:406
  7.6 1.3 %collective-permute-start.2 = (f32[48,384]{1,0:T(8,128)S(1)}, f32[48,384]{1,0:T(8,128)S(1)}, u32[]{:S(2)}, u32[]{:S(2)}) collective-permute-start(f32[48,384]{1,0:T(8,128)S(1)} %get-tuple-element.46), channel_id=1, source_target_pairs={{0,24},{4,28},{8,16},{12,20},{16,8},{20,12},{24,0},{28,4},{1,25},{... | collective-permute-start | bytes 221192 | tf_op jit(solution)/shard_map/ppermute | solution.py:406
  9.0 0.2 collective-permute-start.3
  9.2 3.2 %collective-permute-done.1.refs_1_ = f32[48,384]{1,0:T(8,128)S(1)} collective-permute-done((f32[48,384]{1,0:T(8,128)S(1)}, f32[48,384]{1,0:T(8,128)S(1)}, u32[]{:S(2)}, u32[]{:S(2)}) %collective-permute-start.1) | collective-permute-done | bytes 73760 | tf_op jit(solution)/shard_map/ppermute | solution.py:406
  12.4 0.5 collective-permute-start.4
  12.9 1.1 %collective-permute-done.2.refs_2_ = f32[48,384]{1,0:T(8,128)S(1)} collective-permute-done((f32[48,384]{1,0:T(8,128)S(1)}, f32[48,384]{1,0:T(8,128)S(1)}, u32[]{:S(2)}, u32[]{:S(2)}) %collective-permute-start.2) | collective-permute-done | bytes 73760 | tf_op jit(solution)/shard_map/ppermute | solution.py:406
  13.9 0.5 %collective-permute-start.5 = (f32[48,384]{1,0:T(8,128)S(1)}, f32[48,384]{1,0:T(8,128)S(1)}, u32[]{:S(2)}, u32[]{:S(2)}) collective-permute-start(f32[48,384]{1,0:T(8,128)S(1)} %collective-permute-done.2.refs_2_), channel_id=1, source_target_pairs={{0,4},{4,0},{8,12},{12,8},{16,20},{20,16},{24,28},{28,24},{1,5},{5... | collective-permute-start | bytes 221192 | tf_op jit(solution)/shard_map/ppermute | solution.py:409
  14.4 0.0 collective-permute-done.3.refs_3_
  14.4 1.5 %collective-permute-start.6 = (f32[48,384]{1,0:T(8,128)S(1)}, f32[48,384]{1,0:T(8,128)S(1)}, u32[]{:S(2)}, u32[]{:S(2)}) collective-permute-start(f32[48,384]{1,0:T(8,128)S(1)} %collective-permute-done.3.refs_3_), channel_id=1, source_target_pairs={{0,4},{4,0},{8,12},{12,8},{16,20},{20,16},{24,28},{28,24},{1,5},{5... | collective-permute-start | bytes 221192 | tf_op jit(solution)/shard_map/ppermute | solution.py:409
  16.0 1.0 %collective-permute-done.4.refs_4_ = f32[48,384]{1,0:T(8,128)S(1)} collective-permute-done((f32[48,384]{1,0:T(8,128)S(1)}, f32[48,384]{1,0:T(8,128)S(1)}, u32[]{:S(2)}, u32[]{:S(2)}) %collective-permute-start.4) | collective-permute-done | bytes 73760 | tf_op jit(solution)/shard_map/ppermute | solution.py:409
  17.0 1.1 %collective-permute-start.7 = (f32[192,128]{1,0:T(8,128)S(1)}, f32[192,128]{1,0:T(8,128)S(1)}, u32[]{:S(2)}, u32[]{:S(2)}) collective-permute-start(f32[192,128]{1,0:T(8,128)S(1)} %get-tuple-element.51), channel_id=1, source_target_pairs={{0,4},{4,0},{8,12},{12,8},{16,20},{20,16},{24,28},{28,24},{1,5},{5... | collective-permute-start | bytes 294920 | tf_op jit(solution)/shard_map/ppermute | solution.py:409
  18.1 0.8 %collective-permute-done.5.refs_5_ = f32[48,384]{1,0:T(8,128)S(1)} collective-permute-done((f32[48,384]{1,0:T(8,128)S(1)}, f32[48,384]{1,0:T(8,128)S(1)}, u32[]{:S(2)}, u32[]{:S(2)}) %collective-permute-start.5) | collective-permute-done | bytes 73760 | tf_op jit(solution)/shard_map/ppermute | solution.py:409
  18.9 0.8 %collective-permute-done.6.refs_6_ = f32[48,384]{1,0:T(8,128)S(1)} collective-permute-done((f32[48,384]{1,0:T(8,128)S(1)}, f32[48,384]{1,0:T(8,128)S(1)}, u32[]{:S(2)}, u32[]{:S(2)}) %collective-permute-start.6) | collective-permute-done | bytes 73760 | tf_op jit(solution)/shard_map/ppermute | solution.py:409
  19.7 0.0 collective-permute-done.got_ref
  19.7 0.0 copy-done.2
  19.7 0.0 copy-done.3
  19.7 0.0 copy-done.4
  19.7 0.0 copy-done.5
  19.7 0.0 copy-done.6
  19.7 1.1 %products.1 = (f32[384,384]{1,0:T(8,128)S(1)}, f32[384,384]{1,0:T(8,128)S(1)}, f32[384,384]{1,0:T(8,128)S(1)}, f32[384,256]{1,0:T(8,128)S(1)}, f32[384,256]{1,0:...) custom-call(f32[576,128]{1,0:T(8,128)S(1)} %bitcast.15, ...), custom_call_target="tpu_custom_call" | custom-call | flops 679477248 | bytes 2359296 | tf_op jit(solution)/shard_map/products/pallas_call | solution.py:440
  20.9 1.5 %collective-permute-start.8 = (f32[576,128]{1,0:T(8,128)S(1)}, f32[576,128]{1,0:T(8,128)S(1)}, u32[]{:S(2)}, u32[]{:S(2)}) collective-permute-start(f32[576,128]{1,0:T(8,128)S(1)} %bitcast.22), channel_id=1, source_target_pairs={{0,4},{4,0},{8,12},{12,8},{16,20},{20,16},{24,28},{28,24},{1,5},{5... | collective-permute-start | bytes 884744 | tf_op jit(solution)/shard_map/ppermute | solution.py:409
  22.4 0.0 collective-permute-done.7.corner_ref
  22.4 5.1 %begin.1 = (f32[384,384]{1,0:T(8,128)S(1)}, f32[384,384]{1,0:T(8,128)S(1)}) custom-call(f32[576,128]{1,0:T(8,128)S(1)} %get-tuple-element.49.own_ref, f32[192,128]{1,0:T(8,128)S(1)} %collective-permute-done.7.corner_ref, f32[384,384]{1,0:T(8,128)S(1)} %get-tuple-element.52.product_ref, f32[384,384]{1,0:T(8,128)S(1)} %get-tuple-element.53.basis_ref), custom_call_target="tpu_custom_call" | custom-call | flops 2378170368 | bytes 2359296 | tf_op jit(solution)/shard_map/begin/pallas_call | solution.py:449
  27.5 0.4 collective-permute-done.8.first_left_ref
  27.9 0.0 copy-done
  27.9 0.0 copy-done.1
  27.9 2.5 %update.1 = (f32[576,128]{1,0:T(8,128)}, f32[576,128]{1,0:T(8,128)}, f32[4,48,384]{2,1,0:T(8,128)S(1)}, f32[4,48,384]{2,1,0:T(8,128)S(1)}) custom-call(f32[384,256]{1,0:T(8,128)S(1)} %get-tuple-element.55.inner_ref, f32[384,384]{1,0:T(8,128)S(1)} %get-tuple-element.53.basis_ref, f32[576,128]{1,0:T(8,128)S(1)} %get-tuple-element.56.left_ref, ...), custom_call_target="tpu_custom_call" | custom-call | flops 679477248 | bytes 2359296 | tf_op jit(solution)/shard_map/update/pallas_call | solution.py:452
  30.4 1.3 %collective-permute-start.9 = (f32[4,48,384]{2,1,0:T(8,128)S(1)}, f32[4,48,384]{2,1,0:T(8,128)S(1)}, u32[]{:S(2)}, u32[]{:S(2)}) collective-permute-start(f32[4,48,384]{2,1,0:T(8,128)S(1)} %get-tuple-element.60), channel_id=1, source_target_pairs={{0,4},{4,0},{8,12},{12,8},{16,20},{20,16},{24,28},{28,24},{1,5},{5... | collective-permute-start | bytes 884744 | tf_op jit(solution)/shard_map/ppermute | solution.py:409
  31.7 5.7 %end.1 = (f32[384,384]{1,0:T(8,128)S(1)}, f32[384,384]{1,0:T(8,128)S(1)}, f32[576,128]{1,0:T(8,128)S(1)}) custom-call(f32[384,384]{1,0:T(8,128)S(1)} %get-tuple-element.61.start_ref), custom_call_target="tpu_custom_call" | custom-call | flops 3057647616 | bytes 2359296 | tf_op jit(solution)/shard_map/end/pallas_call | solution.py:462
  37.4 0.8 %collective-permute-start.13 = (f32[576,128]{1,0:T(8,128)S(1)}, f32[576,128]{1,0:T(8,128)S(1)}, u32[]{:S(2)}, u32[]{:S(2)}) collective-permute-start(f32[576,128]{1,0:T(8,128)S(1)} %get-tuple-element.62), channel_id=1, source_target_pairs={{0,4},{4,0},{8,12},{12,8},{16,20},{20,16},{24,28},{28,24},{1,5},{5... | collective-permute-start | bytes 884744 | tf_op jit(solution)/shard_map/ppermute | solution.py:409
  38.2 0.0 collective-permute-done.9.theirs_ref
  38.2 3.9 %collective-permute-start.10 = (f32[48,384]{1,0:T(8,128)S(1)}, f32[48,384]{1,0:T(8,128)S(1)}, u32[]{:S(2)}, u32[]{:S(2)}) collective-permute-start(f32[48,384]{1,0:T(8,128)S(1)} %get-tuple-element.66), channel_id=1, source_target_pairs={{0,16},{4,20},{8,24},{12,28},{16,0},{20,4},{24,8},{28,12},{1,17},{... | collective-permute-start | bytes 221192 | tf_op jit(solution)/shard_map/ppermute | solution.py:406
  42.1 1.3 %collective-permute-start.11 = (f32[48,384]{1,0:T(8,128)S(1)}, f32[48,384]{1,0:T(8,128)S(1)}, u32[]{:S(2)}, u32[]{:S(2)}) collective-permute-start(f32[48,384]{1,0:T(8,128)S(1)} %get-tuple-element.67), channel_id=1, source_target_pairs={{0,24},{4,28},{8,16},{12,20},{16,8},{20,12},{24,0},{28,4},{1,25},{... | collective-permute-start | bytes 221192 | tf_op jit(solution)/shard_map/ppermute | solution.py:406
  43.4 0.3 collective-permute-start.12
  43.7 2.1 %rest.1 = (f32[576,128]{1,0:T(8,128)S(1)}, f32[576,128]{1,0:T(8,128)}, f32[576,128]{1,0:T(8,128)}) custom-call(f32[384,384]{1,0:T(8,128)S(1)} %get-tuple-element.71.x_ref, f32[384,384]{1,0:T(8,128)S(1)} %get-tuple-element.72.poly_ref, f32[384,384]{1,0:T(8,128)S(1)} %get-tuple-element.73.grad_ref, f32[384,384]{1,0:T(8,128)S(1)} %get-tuple-element.74.new_stat_ref, ...), custom_call_target="tpu_custom_call" | custom-call | flops 509607936 | bytes 2359296 | tf_op jit(solution)/shard_map/rest/pallas_call | solution.py:466
  45.7 0.0 collective-permute-done.13.back_ref
  45.7 0.8 %bases.1 = (f32[576,128]{1,0:T(8,128)}, f32[576,128]{1,0:T(8,128)}) custom-call(f32[576,128]{1,0:T(8,128)S(1)} %get-tuple-element.78.keep_ref, f32[576,128]{1,0:T(8,128)S(1)} %collective-permute-done.13.back_ref), custom_call_target="tpu_custom_call" | custom-call | flops 33973864 | bytes 2359296 | tf_op jit(solution)/shard_map/bases/pallas_call | solution.py:487
  46.6 0.0 collective-permute-done.10.refs_1_
  46.6 1.8 %collective-permute-done.11.refs_2_ = f32[48,384]{1,0:T(8,128)S(1)} collective-permute-done((f32[48,384]{1,0:T(8,128)S(1)}, f32[48,384]{1,0:T(8,128)S(1)}, u32[]{:S(2)}, u32[]{:S(2)}) %collective-permute-start.11) | collective-permute-done | bytes 73760 | tf_op jit(solution)/shard_map/ppermute | solution.py:406
  48.3 0.2 collective-permute-done.12.refs_3_
  48.5 0.7 %rows.1 = f32[4,48,384]{2,1,0:T(8,128)} custom-call(f32[48,384]{1,0:T(8,128)S(1)} %get-tuple-element.65.refs_0_, f32[48,384]{1,0:T(8,128)S(1)} %collective-permute-done.10.refs_1_, f32[48,384]{1,0:T(8,128)S(1)} %collective-permute-done.11.refs_2_, f32[48,384]{1,0:T(8,128)S(1)} %collective-permute-done.12.refs_3_), custom_call_target="tpu_custom_call" | custom-call | flops 33973864 | bytes 2359296 | tf_op jit(solution)/shard_map/rows/pallas_call | solution.py:474
  (3 shorter events, 0.0 us)
Async XLA Ops:
  0.6 19.1 %copy-start.2 = (f32[1,73728]{1,0:T(1,128)S(1)}, f32[1,73728]{1,0:T(1,128)}, u32[]{:S(2)}) copy-start(f32[1,73728]{1,0:T(1,128)} %param.10) | copy-start | bytes 884740
  0.6 19.1 %copy-start.3 = (f32[1,73728]{1,0:T(1,128)S(1)}, f32[1,73728]{1,0:T(1,128)}, u32[]{:S(2)}) copy-start(f32[1,73728]{1,0:T(1,128)} %param.11) | copy-start | bytes 884740
  0.7 19.1 %copy-start.4 = (f32[1,73728]{1,0:T(1,128)S(1)}, f32[1,73728]{1,0:T(1,128)}, u32[]{:S(2)}) copy-start(f32[1,73728]{1,0:T(1,128)} %param.13) | copy-start | bytes 884740
  0.7 19.1 %copy-start.5 = (f32[4,48,384]{2,1,0:T(8,128)S(1)}, f32[4,48,384]{2,1,0:T(8,128)}, u32[]{:S(2)}) copy-start(f32[4,48,384]{2,1,0:T(8,128)} %refs_0_.1) | copy-start | bytes 884740
  0.7 19.1 %copy-start.6 = (f32[1,73728]{1,0:T(1,128)S(1)}, f32[1,73728]{1,0:T(1,128)}, u32[]{:S(2)}) copy-start(f32[1,73728]{1,0:T(1,128)} %param.12) | copy-start | bytes 884740
  2.0 17.7 %collective-permute-start = (f32[720,128]{1,0:T(8,128)S(1)}, f32[720,128]{1,0:T(8,128)S(1)}, u32[]{:S(2)}, u32[]{:S(2)}) collective-permute-start(f32[720,128]{1,0:T(8,128)S(1)} %get-tuple-element.44), channel_id=1, source_target_pairs={{0,4},{4,0},{8,12},{12,8},{16,20},{20,16},{24,28},{28,24},{1,5},{5... | collective-permute-start | bytes 1105928 | tf_op jit(solution)/shard_map/ppermute | solution.py:409
  5.0 7.4 %collective-permute-start.1 = (f32[48,384]{1,0:T(8,128)S(1)}, f32[48,384]{1,0:T(8,128)S(1)}, u32[]{:S(2)}, u32[]{:S(2)}) collective-permute-start(f32[48,384]{1,0:T(8,128)S(1)} %get-tuple-element.45), channel_id=1, source_target_pairs={{0,16},{4,20},{8,24},{12,28},{16,0},{20,4},{24,8},{28,12},{1,17},{... | collective-permute-start | bytes 221192 | tf_op jit(solution)/shard_map/ppermute | solution.py:406
  7.6 6.3 %collective-permute-start.2 = (f32[48,384]{1,0:T(8,128)S(1)}, f32[48,384]{1,0:T(8,128)S(1)}, u32[]{:S(2)}, u32[]{:S(2)}) collective-permute-start(f32[48,384]{1,0:T(8,128)S(1)} %get-tuple-element.46), channel_id=1, source_target_pairs={{0,24},{4,28},{8,16},{12,20},{16,8},{20,12},{24,0},{28,4},{1,25},{... | collective-permute-start | bytes 221192 | tf_op jit(solution)/shard_map/ppermute | solution.py:406
  9.0 5.5 %collective-permute-start.3 = (f32[48,384]{1,0:T(8,128)S(1)}, f32[48,384]{1,0:T(8,128)S(1)}, u32[]{:S(2)}, u32[]{:S(2)}) collective-permute-start(f32[48,384]{1,0:T(8,128)S(1)} %get-tuple-element.47), channel_id=1, source_target_pairs={{0,8},{4,12},{8,0},{12,4},{16,24},{20,28},{24,16},{28,20},{1,9},{5... | collective-permute-start | bytes 221192 | tf_op jit(solution)/shard_map/ppermute | solution.py:406
  12.4 4.6 %collective-permute-start.4 = (f32[48,384]{1,0:T(8,128)S(1)}, f32[48,384]{1,0:T(8,128)S(1)}, u32[]{:S(2)}, u32[]{:S(2)}) collective-permute-start(f32[48,384]{1,0:T(8,128)S(1)} %collective-permute-done.1.refs_1_), channel_id=1, source_target_pairs={{0,4},{4,0},{8,12},{12,8},{16,20},{20,16},{24,28},{28,24},{1,5},{5... | collective-permute-start | bytes 221192 | tf_op jit(solution)/shard_map/ppermute | solution.py:409
  13.9 5.0 %collective-permute-start.5 = (f32[48,384]{1,0:T(8,128)S(1)}, f32[48,384]{1,0:T(8,128)S(1)}, u32[]{:S(2)}, u32[]{:S(2)}) collective-permute-start(f32[48,384]{1,0:T(8,128)S(1)} %collective-permute-done.2.refs_2_), channel_id=1, source_target_pairs={{0,4},{4,0},{8,12},{12,8},{16,20},{20,16},{24,28},{28,24},{1,5},{5... | collective-permute-start | bytes 221192 | tf_op jit(solution)/shard_map/ppermute | solution.py:409
  14.4 5.3 %collective-permute-start.6 = (f32[48,384]{1,0:T(8,128)S(1)}, f32[48,384]{1,0:T(8,128)S(1)}, u32[]{:S(2)}, u32[]{:S(2)}) collective-permute-start(f32[48,384]{1,0:T(8,128)S(1)} %collective-permute-done.3.refs_3_), channel_id=1, source_target_pairs={{0,4},{4,0},{8,12},{12,8},{16,20},{20,16},{24,28},{28,24},{1,5},{5... | collective-permute-start | bytes 221192 | tf_op jit(solution)/shard_map/ppermute | solution.py:409
  17.0 5.4 %collective-permute-start.7 = (f32[192,128]{1,0:T(8,128)S(1)}, f32[192,128]{1,0:T(8,128)S(1)}, u32[]{:S(2)}, u32[]{:S(2)}) collective-permute-start(f32[192,128]{1,0:T(8,128)S(1)} %get-tuple-element.51), channel_id=1, source_target_pairs={{0,4},{4,0},{8,12},{12,8},{16,20},{20,16},{24,28},{28,24},{1,5},{5... | collective-permute-start | bytes 294920 | tf_op jit(solution)/shard_map/ppermute | solution.py:409
  20.9 7.0 %collective-permute-start.8 = (f32[576,128]{1,0:T(8,128)S(1)}, f32[576,128]{1,0:T(8,128)S(1)}, u32[]{:S(2)}, u32[]{:S(2)}) collective-permute-start(f32[576,128]{1,0:T(8,128)S(1)} %bitcast.22), channel_id=1, source_target_pairs={{0,4},{4,0},{8,12},{12,8},{16,20},{20,16},{24,28},{28,24},{1,5},{5... | collective-permute-start | bytes 884744 | tf_op jit(solution)/shard_map/ppermute | solution.py:409
  22.4 5.5 %copy-start = (f32[1,73728]{1,0:T(1,128)S(1)}, f32[1,73728]{1,0:T(1,128)}, u32[]{:S(2)}) copy-start(f32[1,73728]{1,0:T(1,128)} %param.8) | copy-start | bytes 884740
  22.4 5.5 %copy-start.1 = (f32[1,73728]{1,0:T(1,128)S(1)}, f32[1,73728]{1,0:T(1,128)}, u32[]{:S(2)}) copy-start(f32[1,73728]{1,0:T(1,128)} %param.9) | copy-start | bytes 884740
  30.4 7.8 %collective-permute-start.9 = (f32[4,48,384]{2,1,0:T(8,128)S(1)}, f32[4,48,384]{2,1,0:T(8,128)S(1)}, u32[]{:S(2)}, u32[]{:S(2)}) collective-permute-start(f32[4,48,384]{2,1,0:T(8,128)S(1)} %get-tuple-element.60), channel_id=1, source_target_pairs={{0,4},{4,0},{8,12},{12,8},{16,20},{20,16},{24,28},{28,24},{1,5},{5... | collective-permute-start | bytes 884744 | tf_op jit(solution)/shard_map/ppermute | solution.py:409
  37.4 8.3 %collective-permute-start.13 = (f32[576,128]{1,0:T(8,128)S(1)}, f32[576,128]{1,0:T(8,128)S(1)}, u32[]{:S(2)}, u32[]{:S(2)}) collective-permute-start(f32[576,128]{1,0:T(8,128)S(1)} %get-tuple-element.62), channel_id=1, source_target_pairs={{0,4},{4,0},{8,12},{12,8},{16,20},{20,16},{24,28},{28,24},{1,5},{5... | collective-permute-start | bytes 884744 | tf_op jit(solution)/shard_map/ppermute | solution.py:409
  38.2 8.3 %collective-permute-start.10 = (f32[48,384]{1,0:T(8,128)S(1)}, f32[48,384]{1,0:T(8,128)S(1)}, u32[]{:S(2)}, u32[]{:S(2)}) collective-permute-start(f32[48,384]{1,0:T(8,128)S(1)} %get-tuple-element.66), channel_id=1, source_target_pairs={{0,16},{4,20},{8,24},{12,28},{16,0},{20,4},{24,8},{28,12},{1,17},{... | collective-permute-start | bytes 221192 | tf_op jit(solution)/shard_map/ppermute | solution.py:406
  42.1 6.3 %collective-permute-start.11 = (f32[48,384]{1,0:T(8,128)S(1)}, f32[48,384]{1,0:T(8,128)S(1)}, u32[]{:S(2)}, u32[]{:S(2)}) collective-permute-start(f32[48,384]{1,0:T(8,128)S(1)} %get-tuple-element.67), channel_id=1, source_target_pairs={{0,24},{4,28},{8,16},{12,20},{16,8},{20,12},{24,0},{28,4},{1,25},{... | collective-permute-start | bytes 221192 | tf_op jit(solution)/shard_map/ppermute | solution.py:406
  43.4 5.1 %collective-permute-start.12 = (f32[48,384]{1,0:T(8,128)S(1)}, f32[48,384]{1,0:T(8,128)S(1)}, u32[]{:S(2)}, u32[]{:S(2)}) collective-permute-start(f32[48,384]{1,0:T(8,128)S(1)} %get-tuple-element.68), channel_id=1, source_target_pairs={{0,8},{4,12},{8,0},{12,4},{16,24},{20,28},{24,16},{28,20},{1,9},{5... | collective-permute-start | bytes 221192 | tf_op jit(solution)/shard_map/ppermute | solution.py:406

commit v7 on v6

--- a/solution.py
+++ b/solution.py
@@ -8,6 +8,7 @@
 from jax.sharding import PartitionSpec as P
 
 NS_ITERS = 5
+EARLY_ITERS = 1
 BETA_ONE = 0.9
 BETA_TWO = 0.95
 ADAM_EPS = 1e-08
@@ -114,8 +115,12 @@
     return jnp.concatenate([head, tail], axis=1)
 
 
+def is_first():
+    return lax.rem(lax.axis_index("shard"), 2) == 0
+
+
 def is_left():
-    return lax.rem(lax.axis_index("shard"), 2) == 0
+    return lax.rem(lax.axis_index("shard") + lax.axis_index("tensor"), 2) == 0
 
 
 def pack_kernel(hops, l_stat_ref, r_stat_ref, l_basis_ref, r_basis_ref, grads_ref, *refs):
@@ -127,7 +132,9 @@
     rows = grads_ref.shape[1]
     here = lax.axis_index("shard") // 2
 
-    def copies(basis_ref, stat_ref, start):
+    start = pl.multiple_of(jnp.where(is_first(), 0, half_rows), 8)
+
+    def copies(basis_ref, stat_ref):
         return [
             pltpu.make_async_copy(stat_ref.at[pl.ds(start, half_rows)], corner, sems.at[0]),
             pltpu.make_async_copy(basis_ref, out_ref.at[pl.ds(0, flat_rows)], sems.at[1]),
@@ -135,12 +142,12 @@
 
     @pl.when(left)
     def _():
-        for copy in copies(r_basis_ref, r_stat_ref, 0):
+        for copy in copies(r_basis_ref, r_stat_ref):
             copy.start()
 
     @pl.when(jnp.logical_not(left))
     def _():
-        for copy in copies(l_basis_ref, l_stat_ref, half_rows):
+        for copy in copies(l_basis_ref, l_stat_ref):
             copy.start()
 
     more = []
@@ -153,7 +160,7 @@
             more.append(pltpu.make_async_copy(source, target, sems.at[2 + len(hops) + k]))
     for copy in more:
         copy.start()
-    first, second = copies(l_basis_ref, l_stat_ref, half_rows)
+    first, second = copies(l_basis_ref, l_stat_ref)
     first.wait()
     third = half_rows // 9
     a, b, c = thirds(corner)
@@ -186,16 +193,16 @@
     ]
 
 
-def statistic(left, own, got_ref, scratch):
+def statistic(first, own, got_ref, scratch):
     corner = unpack_corner(got_ref)
-    placed = [jnp.concatenate([jnp.where(left, 0.0, c), jnp.where(left, c, 0.0)], axis=0) for c in corner]
-    known = whole_of(scratch, pick(left, own, placed), pick(left, placed, own))
+    placed = [jnp.concatenate([jnp.where(first, 0.0, c), jnp.where(first, c, 0.0)], axis=0) for c in corner]
+    known = whole_of(scratch, pick(first, own, placed), pick(first, placed, own))
     half = known.shape[0] // 2
     part = half // 3
     row = lax.broadcasted_iota(jnp.int32, known.shape, 0)
     column = lax.broadcasted_iota(jnp.int32, known.shape, 1)
-    missing = (jnp.where(left, row, column) < half) & (jnp.where(left, column, row) >= half)
-    offset = jnp.where(left, half, 0)
+    missing = (jnp.where(first, row, column) < half) & (jnp.where(first, column, row) >= half)
+    offset = jnp.where(first, half, 0)
     row, column = row - offset, column - offset
     limit = jnp.where(row < part, part, 2 * part)
     missing |= (row >= 0) & (row < 2 * part) & (column < half) & (column >= limit)
@@ -239,7 +246,8 @@
         grad_ref[...] = refs[0][...]
     own = pick(left, thirds(l_basis_ref), thirds(r_basis_ref))
     got = thirds(got_ref, 0, l_basis_ref.shape[0])
-    basis_ref[...] = whole_of(scratch, pick(left, own, got), pick(left, got, own))
+    first = is_first()
+    basis_ref[...] = whole_of(scratch, pick(first, own, got), pick(first, got, own))
     own_ref[...] = jnp.where(left, l_stat_ref[...], r_stat_ref[...])
     other_ref[...] = jnp.where(left, r_stat_ref[...], l_stat_ref[...])
     copy_ref[...] = l_basis_ref[...]
@@ -252,7 +260,7 @@
 
 
 def begin_kernel(steps, own_ref, corner_ref, product_ref, basis_ref, new_stat_ref, x_ref, scratch):
-    new_stat = 0.5 * statistic(is_left(), thirds(own_ref), corner_ref, scratch) + 0.5 * product_ref[...]
+    new_stat = 0.5 * statistic(is_first(), thirds(own_ref), corner_ref, scratch) + 0.5 * product_ref[...]
     new_stat_ref[...] = new_stat
     power = dot(new_stat, basis_ref[...])
     x_ref[...] = iterate(power * (1.0 / jnp.sqrt(jnp.sum(power * power) + NORM_EPS)), steps)
@@ -263,7 +271,7 @@
     x_ref[...] = x
     poly = polynomial(split(x))
     poly_ref[...] = poly
-    half = take_half(x, jnp.logical_not(is_left()))
+    half = take_half(x, jnp.logical_not(is_first()))
     put_thirds(send_ref, flat_of(scratch, LINEAR_COEFF * half + dot(poly, half)))
 
 
@@ -273,7 +281,7 @@
     basis_ref,
     left_ref,
     right_ref,
-    first_left_ref,
+    other_left_ref,
     one_ref,
     two_ref,
     new_one_ref,
@@ -284,7 +292,9 @@
     partial_ref,
 ):
     left = is_left()
-    basis_left = jnp.where(left, basis_ref[...], whole_of(scratch, thirds(first_left_ref), thirds(left_ref)))
+    first = is_first()
+    own, got = thirds(left_ref), thirds(other_left_ref)
+    basis_left = jnp.where(left, basis_ref[...], whole_of(scratch, pick(first, own, got), pick(first, got, own)))
     left_parts = split(basis_left)
     basis_right = split(right_ref[...])
     rotated = flat_of(scratch, dot(basis_left.T, inner_ref[...]))
@@ -348,14 +358,15 @@
 
 def rest_kernel(x_ref, poly_ref, grad_ref, new_stat_ref, other_ref, keep_ref, new_left_ref, new_right_ref, scratch):
     left = is_left()
-    half = take_half(x_ref[...], left)
+    first = is_first()
+    half = take_half(x_ref[...], first)
     put_thirds(keep_ref, flat_of(scratch, LINEAR_COEFF * half + dot(poly_ref[...], half)))
     grad = grad_ref[...]
     turned = grad.T
     a = jnp.where(left, grad, turned)
     b = jnp.where(left, turned, grad)
-    new_own = flat_of(scratch, take_half(new_stat_ref[...], left))
-    product = flat_of(scratch, dot(b, take_half(a, left)))
+    new_own = flat_of(scratch, take_half(new_stat_ref[...], first))
+    product = flat_of(scratch, dot(b, take_half(a, first)))
     new_other = [0.5 * u + 0.5 * v for u, v in zip(thirds(other_ref), product)]
     put_thirds(new_left_ref, pick(left, new_own, new_other))
     put_thirds(new_right_ref, pick(left, new_other, new_own))
@@ -445,13 +456,21 @@
         full,
         "products",
     )(l_stat, r_stat, l_basis, r_basis, got, *rows)
-    first_left = partner(after(l_basis, product))
-    new_stat, x = call(functools.partial(begin_kernel, 2), [square] * 2, [(3, full, LANES)], 7, full, "begin")(
+    tensors = lax.axis_size("tensor")
+    place = lambda t, i: i * tensors + t
+    cycle = []
+    for t in range(0, tensors - tensors % 2, 2):
+        for i in range(0, size, 2):
+            cycle += [(place(t, i), place(t, i + 1)), (place(t, i + 1), place(t + 1, i + 1))]
+            cycle += [(place(t + 1, i + 1), place(t + 1, i)), (place(t + 1, i), place(t, i))]
+    cycle += [(place(t, i), place(t, i ^ 1)) for t in range(tensors - tensors % 2, tensors) for i in range(size)]
+    other_left = lax.ppermute(after(l_basis, *(theirs[:2] if near else mine)), ("shard", "tensor"), cycle)
+    new_stat, x = call(functools.partial(begin_kernel, EARLY_ITERS), [square] * 2, [(3, full, LANES)], 7, full, "begin")(
         own, got_corner, product, basis
     )
     new_one, new_two, own_rows, other_rows = call(
         functools.partial(update_kernel, hops), [flat, flat, strips, strips], [(3, full, LANES), square], 2, full, "update"
-    )(after(inner, x), basis, left, right, first_left, one, two)
+    )(after(inner, x), basis, left, right, other_left, one, two)
     if not near:
         top = jnp.where(parity == 0, own_rows, other_rows)
         bottom = jnp.where(parity == 0, other_rows, own_rows)
@@ -460,7 +479,7 @@
         other_rows = lax.dynamic_index_in_dim(merged, 1 - parity, 1, keepdims=False)
     got_rows = partner(other_rows)
     x, poly, send = call(
-        functools.partial(end_kernel, NS_ITERS - 2), [square, square, flat], [(3, full, LANES)], 9, full, "end"
+        functools.partial(end_kernel, NS_ITERS - EARLY_ITERS), [square, square, flat], [(3, full, LANES)], 9, full, "end"
     )(after(x, other_rows))
     back = partner(send)
     keep, new_left, new_right = call(rest_kernel, [flat, flat, flat], [(3, full, LANES)], 1.5, full, "rest")(

time: 49.4 us -> 49.1 us (level)
  starting transfers between devices: 19.8 us -> 19 us
    ppermute x8 -> x7, starting transfers between devices: 10.2 us -> 8.73 us  [partner(): return lax.ppermute(x, 'shard', pairs)]
    ppermute x0 -> x1, starting transfers between devices: none -> 0.68 us  [local(): lax.ppermute(after(l_basis, *(theirs[:2] if near else mine)), ('shard', '...]
    ppermute x8 -> x7, waiting for transfers between devices: 3.08 us -> 3.75 us  [partner(): return lax.ppermute(x, 'shard', pairs)]
where the time goes in v7:
time: 49.1 us; the launch traced here: 49 us
  Pallas kernels  19.4 us (40%)
  starting transfers between devices  19 us (39%)
  waiting for transfers between devices  9.77 us (20%)
  between operations  0.77 us (2%)
    ppermute x6, starting transfers between devices, hop_by(): return lax.ppermute(x, 'shard', [(i, i ^ 2 * hop) for i in range(size)])  9.63 us
    ppermute x7, starting transfers between devices, partner(): return lax.ppermute(x, 'shard', pairs)  8.73 us
    pallas_call x1, Pallas kernels, local(): call(functools.partial(end_kernel, NS_ITERS - EARLY_ITERS), [square, squa...  7.37 us
    ppermute x6, waiting for transfers between devices, hop_by(): return lax.ppermute(x, 'shard', [(i, i ^ 2 * hop) for i in range(size)])  6.01 us
    ppermute x7, waiting for transfers between devices, partner(): return lax.ppermute(x, 'shard', pairs)  3.75 us
    pallas_call x1, Pallas kernels, local(): call(functools.partial(begin_kernel, EARLY_ITERS), [square] * 2, [(3, ful...  3.35 us
    pallas_call x1, Pallas kernels, local(): call(functools.partial(update_kernel, hops), [flat, flat, strips, strips]...  2.53 us
    pallas_call x1, Pallas kernels, local(): call(rest_kernel, [flat, flat, flat], [(3, full, LANES)], 1.5, full, 'rest')  2.06 us
  transfers between devices with their start and end apart: 14, of which 8 were waited for; matrix products, arithmetic and copies ran while one was open for 0% of the time, Pallas kernels for 30%

profile of v7, /device:TPU:0, one launch (start us, length us, event | category | flops | bytes accessed | tf_op | source)
XLA Modules:
  0.0 49.0 jit_solution(1797658190694731539)
XLA Ops:
  0.6 0.0 copy-start.6
  0.6 0.0 copy-start.2
  0.7 0.0 copy-start.3
  0.7 0.0 copy-start.4
  0.7 0.0 copy-start.5
  0.7 1.3 %pack.1 = (f32[720,128]{1,0:T(8,128)S(1)}, f32[192,128]{1,0:T(8,128)S(1)}, f32[48,384]{1,0:T(8,128)S(1)}, f32[48,384]{1,0:T(8,128)S(1)}, f32[48,384]{1,0:T(8,128)S(1)}) custom-call(f32[576,128]{1,0:T(8,128)} %bitcast.14, f32[576,128]{1,0:T(8,128)} %bitcast.16, f32[576,128]{1,0:T(8,128)} %bitcast.20, f32[576,128]{1,0:T(8,128)} %bitcast.18, f32[4,48,384]{2,1,0:T(8,128)} %refs_0_.1), custom_call_target="tpu_custom_call" | custom-call | flops 33973864 | bytes 2359296 | tf_op jit(solution)/shard_map/pack/pallas_call | solution.py:427
  2.0 3.0 %collective-permute-start = (f32[720,128]{1,0:T(8,128)S(1)}, f32[720,128]{1,0:T(8,128)S(1)}, u32[]{:S(2)}, u32[]{:S(2)}) collective-permute-start(f32[720,128]{1,0:T(8,128)S(1)} %get-tuple-element.44), channel_id=1, source_target_pairs={{0,4},{4,0},{8,12},{12,8},{16,20},{20,16},{24,28},{28,24},{1,5},{5... | collective-permute-start | bytes 1105928 | tf_op jit(solution)/shard_map/ppermute | solution.py:420
  5.0 2.6 %collective-permute-start.1 = (f32[48,384]{1,0:T(8,128)S(1)}, f32[48,384]{1,0:T(8,128)S(1)}, u32[]{:S(2)}, u32[]{:S(2)}) collective-permute-start(f32[48,384]{1,0:T(8,128)S(1)} %get-tuple-element.45), channel_id=1, source_target_pairs={{0,16},{4,20},{8,24},{12,28},{16,0},{20,4},{24,8},{28,12},{1,17},{... | collective-permute-start | bytes 221192 | tf_op jit(solution)/shard_map/ppermute | solution.py:417
  7.6 1.3 %collective-permute-start.2 = (f32[48,384]{1,0:T(8,128)S(1)}, f32[48,384]{1,0:T(8,128)S(1)}, u32[]{:S(2)}, u32[]{:S(2)}) collective-permute-start(f32[48,384]{1,0:T(8,128)S(1)} %get-tuple-element.46), channel_id=1, source_target_pairs={{0,24},{4,28},{8,16},{12,20},{16,8},{20,12},{24,0},{28,4},{1,25},{... | collective-permute-start | bytes 221192 | tf_op jit(solution)/shard_map/ppermute | solution.py:417
  9.0 0.2 collective-permute-start.3
  9.2 3.2 %collective-permute-done.1.refs_1_ = f32[48,384]{1,0:T(8,128)S(1)} collective-permute-done((f32[48,384]{1,0:T(8,128)S(1)}, f32[48,384]{1,0:T(8,128)S(1)}, u32[]{:S(2)}, u32[]{:S(2)}) %collective-permute-start.1) | collective-permute-done | bytes 73760 | tf_op jit(solution)/shard_map/ppermute | solution.py:417
  12.4 0.5 collective-permute-start.4
  12.9 1.1 %collective-permute-done.2.refs_2_ = f32[48,384]{1,0:T(8,128)S(1)} collective-permute-done((f32[48,384]{1,0:T(8,128)S(1)}, f32[48,384]{1,0:T(8,128)S(1)}, u32[]{:S(2)}, u32[]{:S(2)}) %collective-permute-start.2) | collective-permute-done | bytes 73760 | tf_op jit(solution)/shard_map/ppermute | solution.py:417
  13.9 0.5 %collective-permute-start.5 = (f32[48,384]{1,0:T(8,128)S(1)}, f32[48,384]{1,0:T(8,128)S(1)}, u32[]{:S(2)}, u32[]{:S(2)}) collective-permute-start(f32[48,384]{1,0:T(8,128)S(1)} %collective-permute-done.2.refs_2_), channel_id=1, source_target_pairs={{0,4},{4,0},{8,12},{12,8},{16,20},{20,16},{24,28},{28,24},{1,5},{5... | collective-permute-start | bytes 221192 | tf_op jit(solution)/shard_map/ppermute | solution.py:420
  14.4 0.0 collective-permute-done.3.refs_3_
  14.5 1.5 %collective-permute-start.6 = (f32[48,384]{1,0:T(8,128)S(1)}, f32[48,384]{1,0:T(8,128)S(1)}, u32[]{:S(2)}, u32[]{:S(2)}) collective-permute-start(f32[48,384]{1,0:T(8,128)S(1)} %collective-permute-done.3.refs_3_), channel_id=1, source_target_pairs={{0,4},{4,0},{8,12},{12,8},{16,20},{20,16},{24,28},{28,24},{1,5},{5... | collective-permute-start | bytes 221192 | tf_op jit(solution)/shard_map/ppermute | solution.py:420
  16.0 1.0 %collective-permute-done.4.refs_4_ = f32[48,384]{1,0:T(8,128)S(1)} collective-permute-done((f32[48,384]{1,0:T(8,128)S(1)}, f32[48,384]{1,0:T(8,128)S(1)}, u32[]{:S(2)}, u32[]{:S(2)}) %collective-permute-start.4) | collective-permute-done | bytes 73760 | tf_op jit(solution)/shard_map/ppermute | solution.py:420
  17.0 1.1 %collective-permute-start.7 = (f32[192,128]{1,0:T(8,128)S(1)}, f32[192,128]{1,0:T(8,128)S(1)}, u32[]{:S(2)}, u32[]{:S(2)}) collective-permute-start(f32[192,128]{1,0:T(8,128)S(1)} %get-tuple-element.51), channel_id=1, source_target_pairs={{0,4},{4,0},{8,12},{12,8},{16,20},{20,16},{24,28},{28,24},{1,5},{5... | collective-permute-start | bytes 294920 | tf_op jit(solution)/shard_map/ppermute | solution.py:420
  18.1 0.9 %collective-permute-done.5.refs_5_ = f32[48,384]{1,0:T(8,128)S(1)} collective-permute-done((f32[48,384]{1,0:T(8,128)S(1)}, f32[48,384]{1,0:T(8,128)S(1)}, u32[]{:S(2)}, u32[]{:S(2)}) %collective-permute-start.5) | collective-permute-done | bytes 73760 | tf_op jit(solution)/shard_map/ppermute | solution.py:420
  19.0 0.0 copy-done.6
  19.0 0.7 %collective-permute-start.8 = (f32[576,128]{1,0:T(8,128)S(1)}, f32[576,128]{1,0:T(8,128)S(1)}, u32[]{:S(2)}, u32[]{:S(2)}) collective-permute-start(f32[576,128]{1,0:T(8,128)S(1)} %bitcast.21), channel_id=1, source_target_pairs={{0,4},{4,5},{5,1},{1,0},{8,12},{12,13},{13,9},{9,8},{16,20},{20,21... | collective-permute-start | bytes 884744 | tf_op jit(solution)/shard_map/ppermute | solution.py:467
  19.7 0.9 %collective-permute-done.6.refs_6_ = f32[48,384]{1,0:T(8,128)S(1)} collective-permute-done((f32[48,384]{1,0:T(8,128)S(1)}, f32[48,384]{1,0:T(8,128)S(1)}, u32[]{:S(2)}, u32[]{:S(2)}) %collective-permute-start.6) | collective-permute-done | bytes 73760 | tf_op jit(solution)/shard_map/ppermute | solution.py:420
  20.6 0.0 collective-permute-done.got_ref
  20.6 0.0 copy-done.2
  20.6 0.0 copy-done.3
  20.6 0.0 copy-done.4
  20.6 0.0 copy-done.5
  20.6 1.1 %products.1 = (f32[384,384]{1,0:T(8,128)S(1)}, f32[384,384]{1,0:T(8,128)S(1)}, f32[384,384]{1,0:T(8,128)S(1)}, f32[384,256]{1,0:T(8,128)S(1)}, f32[384,256]{1,0:...) custom-call(f32[576,128]{1,0:T(8,128)S(1)} %bitcast.15, ...), custom_call_target="tpu_custom_call" | custom-call | flops 679477248 | bytes 2359296 | tf_op jit(solution)/shard_map/products/pallas_call | solution.py:451
  21.8 0.9 %collective-permute-done.7.corner_ref = f32[192,128]{1,0:T(8,128)S(1)} collective-permute-done((f32[192,128]{1,0:T(8,128)S(1)}, f32[192,128]{1,0:T(8,128)S(1)}, u32[]{:S(2)}, u32[]{:S(2)}) %collective-permute-start.7) | collective-permute-done | bytes 98336 | tf_op jit(solution)/shard_map/ppermute | solution.py:420
  22.7 3.4 %begin.1 = (f32[384,384]{1,0:T(8,128)S(1)}, f32[384,384]{1,0:T(8,128)S(1)}) custom-call(f32[576,128]{1,0:T(8,128)S(1)} %get-tuple-element.49.own_ref, f32[192,128]{1,0:T(8,128)S(1)} %collective-permute-done.7.corner_ref, f32[384,384]{1,0:T(8,128)S(1)} %get-tuple-element.52.product_ref, f32[384,384]{1,0:T(8,128)S(1)} %get-tuple-element.53.basis_ref), custom_call_target="tpu_custom_call" | custom-call | flops 2378170368 | bytes 2359296 | tf_op jit(solution)/shard_map/begin/pallas_call | solution.py:468
  26.0 0.0 collective-permute-done.8.other_left_ref
  26.1 0.0 copy-done
  26.1 0.0 copy-done.1
  26.1 2.5 %update.1 = (f32[576,128]{1,0:T(8,128)}, f32[576,128]{1,0:T(8,128)}, f32[4,48,384]{2,1,0:T(8,128)S(1)}, f32[4,48,384]{2,1,0:T(8,128)S(1)}) custom-call(f32[384,256]{1,0:T(8,128)S(1)} %get-tuple-element.55.inner_ref, f32[384,384]{1,0:T(8,128)S(1)} %get-tuple-element.53.basis_ref, f32[576,128]{1,0:T(8,128)S(1)} %get-tuple-element.56.left_ref, ...), custom_call_target="tpu_custom_call" | custom-call | flops 679477248 | bytes 2359296 | tf_op jit(solution)/shard_map/update/pallas_call | solution.py:471
  28.6 0.3 collective-permute-start.9
  28.9 7.4 %end.1 = (f32[384,384]{1,0:T(8,128)S(1)}, f32[384,384]{1,0:T(8,128)S(1)}, f32[576,128]{1,0:T(8,128)S(1)}) custom-call(f32[384,384]{1,0:T(8,128)S(1)} %get-tuple-element.61.start_ref), custom_call_target="tpu_custom_call" | custom-call | flops 3057647616 | bytes 2359296 | tf_op jit(solution)/shard_map/end/pallas_call | solution.py:481
  36.3 1.8 %collective-permute-start.13 = (f32[576,128]{1,0:T(8,128)S(1)}, f32[576,128]{1,0:T(8,128)S(1)}, u32[]{:S(2)}, u32[]{:S(2)}) collective-permute-start(f32[576,128]{1,0:T(8,128)S(1)} %get-tuple-element.62), channel_id=1, source_target_pairs={{0,4},{4,0},{8,12},{12,8},{16,20},{20,16},{24,28},{28,24},{1,5},{5... | collective-permute-start | bytes 884744 | tf_op jit(solution)/shard_map/ppermute | solution.py:420
  38.1 0.0 collective-permute-done.9.theirs_ref
  38.1 3.2 %collective-permute-start.10 = (f32[48,384]{1,0:T(8,128)S(1)}, f32[48,384]{1,0:T(8,128)S(1)}, u32[]{:S(2)}, u32[]{:S(2)}) collective-permute-start(f32[48,384]{1,0:T(8,128)S(1)} %get-tuple-element.66), channel_id=1, source_target_pairs={{0,16},{4,20},{8,24},{12,28},{16,0},{20,4},{24,8},{28,12},{1,17},{... | collective-permute-start | bytes 221192 | tf_op jit(solution)/shard_map/ppermute | solution.py:417
  41.3 1.8 %collective-permute-start.11 = (f32[48,384]{1,0:T(8,128)S(1)}, f32[48,384]{1,0:T(8,128)S(1)}, u32[]{:S(2)}, u32[]{:S(2)}) collective-permute-start(f32[48,384]{1,0:T(8,128)S(1)} %get-tuple-element.67), channel_id=1, source_target_pairs={{0,24},{4,28},{8,16},{12,20},{16,8},{20,12},{24,0},{28,4},{1,25},{... | collective-permute-start | bytes 221192 | tf_op jit(solution)/shard_map/ppermute | solution.py:417
  43.1 0.5 collective-permute-start.12
  43.6 2.1 %rest.1 = (f32[576,128]{1,0:T(8,128)S(1)}, f32[576,128]{1,0:T(8,128)}, f32[576,128]{1,0:T(8,128)}) custom-call(f32[384,384]{1,0:T(8,128)S(1)} %get-tuple-element.71.x_ref, f32[384,384]{1,0:T(8,128)S(1)} %get-tuple-element.72.poly_ref, f32[384,384]{1,0:T(8,128)S(1)} %get-tuple-element.73.grad_ref, f32[384,384]{1,0:T(8,128)S(1)} %get-tuple-element.74.new_stat_ref, ...), custom_call_target="tpu_custom_call" | custom-call | flops 509607936 | bytes 2359296 | tf_op jit(solution)/shard_map/rest/pallas_call | solution.py:485
  45.6 0.0 collective-permute-done.13.back_ref
  45.6 0.8 %bases.1 = (f32[576,128]{1,0:T(8,128)}, f32[576,128]{1,0:T(8,128)}) custom-call(f32[576,128]{1,0:T(8,128)S(1)} %get-tuple-element.78.keep_ref, f32[576,128]{1,0:T(8,128)S(1)} %collective-permute-done.13.back_ref), custom_call_target="tpu_custom_call" | custom-call | flops 33973864 | bytes 2359296 | tf_op jit(solution)/shard_map/bases/pallas_call | solution.py:506
  46.5 0.0 collective-permute-done.10.refs_1_
  46.5 1.1 %collective-permute-done.11.refs_2_ = f32[48,384]{1,0:T(8,128)S(1)} collective-permute-done((f32[48,384]{1,0:T(8,128)S(1)}, f32[48,384]{1,0:T(8,128)S(1)}, u32[]{:S(2)}, u32[]{:S(2)}) %collective-permute-start.11) | collective-permute-done | bytes 73760 | tf_op jit(solution)/shard_map/ppermute | solution.py:417
  47.6 0.6 %collective-permute-done.12.refs_3_ = f32[48,384]{1,0:T(8,128)S(1)} collective-permute-done((f32[48,384]{1,0:T(8,128)S(1)}, f32[48,384]{1,0:T(8,128)S(1)}, u32[]{:S(2)}, u32[]{:S(2)}) %collective-permute-start.12) | collective-permute-done | bytes 73760 | tf_op jit(solution)/shard_map/ppermute | solution.py:417
  48.2 0.7 %rows.1 = f32[4,48,384]{2,1,0:T(8,128)} custom-call(f32[48,384]{1,0:T(8,128)S(1)} %get-tuple-element.65.refs_0_, f32[48,384]{1,0:T(8,128)S(1)} %collective-permute-done.10.refs_1_, f32[48,384]{1,0:T(8,128)S(1)} %collective-permute-done.11.refs_2_, f32[48,384]{1,0:T(8,128)S(1)} %collective-permute-done.12.refs_3_), custom_call_target="tpu_custom_call" | custom-call | flops 33973864 | bytes 2359296 | tf_op jit(solution)/shard_map/rows/pallas_call | solution.py:493
  (3 shorter events, 0.0 us)
Async XLA Ops:
  0.6 18.4 %copy-start.6 = (f32[1,73728]{1,0:T(1,128)S(1)}, f32[1,73728]{1,0:T(1,128)}, u32[]{:S(2)}) copy-start(f32[1,73728]{1,0:T(1,128)} %param.12) | copy-start | bytes 884740
  0.6 19.9 %copy-start.2 = (f32[1,73728]{1,0:T(1,128)S(1)}, f32[1,73728]{1,0:T(1,128)}, u32[]{:S(2)}) copy-start(f32[1,73728]{1,0:T(1,128)} %param.10) | copy-start | bytes 884740
  0.7 19.9 %copy-start.3 = (f32[1,73728]{1,0:T(1,128)S(1)}, f32[1,73728]{1,0:T(1,128)}, u32[]{:S(2)}) copy-start(f32[1,73728]{1,0:T(1,128)} %param.11) | copy-start | bytes 884740
  0.7 19.9 %copy-start.4 = (f32[1,73728]{1,0:T(1,128)S(1)}, f32[1,73728]{1,0:T(1,128)}, u32[]{:S(2)}) copy-start(f32[1,73728]{1,0:T(1,128)} %param.13) | copy-start | bytes 884740
  0.7 19.9 %copy-start.5 = (f32[4,48,384]{2,1,0:T(8,128)S(1)}, f32[4,48,384]{2,1,0:T(8,128)}, u32[]{:S(2)}) copy-start(f32[4,48,384]{2,1,0:T(8,128)} %refs_0_.1) | copy-start | bytes 884740
  2.0 18.6 %collective-permute-start = (f32[720,128]{1,0:T(8,128)S(1)}, f32[720,128]{1,0:T(8,128)S(1)}, u32[]{:S(2)}, u32[]{:S(2)}) collective-permute-start(f32[720,128]{1,0:T(8,128)S(1)} %get-tuple-element.44), channel_id=1, source_target_pairs={{0,4},{4,0},{8,12},{12,8},{16,20},{20,16},{24,28},{28,24},{1,5},{5... | collective-permute-start | bytes 1105928 | tf_op jit(solution)/shard_map/ppermute | solution.py:420
  5.0 7.4 %collective-permute-start.1 = (f32[48,384]{1,0:T(8,128)S(1)}, f32[48,384]{1,0:T(8,128)S(1)}, u32[]{:S(2)}, u32[]{:S(2)}) collective-permute-start(f32[48,384]{1,0:T(8,128)S(1)} %get-tuple-element.45), channel_id=1, source_target_pairs={{0,16},{4,20},{8,24},{12,28},{16,0},{20,4},{24,8},{28,12},{1,17},{... | collective-permute-start | bytes 221192 | tf_op jit(solution)/shard_map/ppermute | solution.py:417
  7.6 6.3 %collective-permute-start.2 = (f32[48,384]{1,0:T(8,128)S(1)}, f32[48,384]{1,0:T(8,128)S(1)}, u32[]{:S(2)}, u32[]{:S(2)}) collective-permute-start(f32[48,384]{1,0:T(8,128)S(1)} %get-tuple-element.46), channel_id=1, source_target_pairs={{0,24},{4,28},{8,16},{12,20},{16,8},{20,12},{24,0},{28,4},{1,25},{... | collective-permute-start | bytes 221192 | tf_op jit(solution)/shard_map/ppermute | solution.py:417
  9.0 5.5 %collective-permute-start.3 = (f32[48,384]{1,0:T(8,128)S(1)}, f32[48,384]{1,0:T(8,128)S(1)}, u32[]{:S(2)}, u32[]{:S(2)}) collective-permute-start(f32[48,384]{1,0:T(8,128)S(1)} %get-tuple-element.47), channel_id=1, source_target_pairs={{0,8},{4,12},{8,0},{12,4},{16,24},{20,28},{24,16},{28,20},{1,9},{5... | collective-permute-start | bytes 221192 | tf_op jit(solution)/shard_map/ppermute | solution.py:417
  12.4 4.6 %collective-permute-start.4 = (f32[48,384]{1,0:T(8,128)S(1)}, f32[48,384]{1,0:T(8,128)S(1)}, u32[]{:S(2)}, u32[]{:S(2)}) collective-permute-start(f32[48,384]{1,0:T(8,128)S(1)} %collective-permute-done.1.refs_1_), channel_id=1, source_target_pairs={{0,4},{4,0},{8,12},{12,8},{16,20},{20,16},{24,28},{28,24},{1,5},{5... | collective-permute-start | bytes 221192 | tf_op jit(solution)/shard_map/ppermute | solution.py:420
  13.9 5.1 %collective-permute-start.5 = (f32[48,384]{1,0:T(8,128)S(1)}, f32[48,384]{1,0:T(8,128)S(1)}, u32[]{:S(2)}, u32[]{:S(2)}) collective-permute-start(f32[48,384]{1,0:T(8,128)S(1)} %collective-permute-done.2.refs_2_), channel_id=1, source_target_pairs={{0,4},{4,0},{8,12},{12,8},{16,20},{20,16},{24,28},{28,24},{1,5},{5... | collective-permute-start | bytes 221192 | tf_op jit(solution)/shard_map/ppermute | solution.py:420
  14.5 6.1 %collective-permute-start.6 = (f32[48,384]{1,0:T(8,128)S(1)}, f32[48,384]{1,0:T(8,128)S(1)}, u32[]{:S(2)}, u32[]{:S(2)}) collective-permute-start(f32[48,384]{1,0:T(8,128)S(1)} %collective-permute-done.3.refs_3_), channel_id=1, source_target_pairs={{0,4},{4,0},{8,12},{12,8},{16,20},{20,16},{24,28},{28,24},{1,5},{5... | collective-permute-start | bytes 221192 | tf_op jit(solution)/shard_map/ppermute | solution.py:420
  17.0 5.7 %collective-permute-start.7 = (f32[192,128]{1,0:T(8,128)S(1)}, f32[192,128]{1,0:T(8,128)S(1)}, u32[]{:S(2)}, u32[]{:S(2)}) collective-permute-start(f32[192,128]{1,0:T(8,128)S(1)} %get-tuple-element.51), channel_id=1, source_target_pairs={{0,4},{4,0},{8,12},{12,8},{16,20},{20,16},{24,28},{28,24},{1,5},{5... | collective-permute-start | bytes 294920 | tf_op jit(solution)/shard_map/ppermute | solution.py:420
  19.0 7.0 %collective-permute-start.8 = (f32[576,128]{1,0:T(8,128)S(1)}, f32[576,128]{1,0:T(8,128)S(1)}, u32[]{:S(2)}, u32[]{:S(2)}) collective-permute-start(f32[576,128]{1,0:T(8,128)S(1)} %bitcast.21), channel_id=1, source_target_pairs={{0,4},{4,5},{5,1},{1,0},{8,12},{12,13},{13,9},{9,8},{16,20},{20,21... | collective-permute-start | bytes 884744 | tf_op jit(solution)/shard_map/ppermute | solution.py:467
  22.7 3.4 %copy-start = (f32[1,73728]{1,0:T(1,128)S(1)}, f32[1,73728]{1,0:T(1,128)}, u32[]{:S(2)}) copy-start(f32[1,73728]{1,0:T(1,128)} %param.8) | copy-start | bytes 884740
  22.7 3.4 %copy-start.1 = (f32[1,73728]{1,0:T(1,128)S(1)}, f32[1,73728]{1,0:T(1,128)}, u32[]{:S(2)}) copy-start(f32[1,73728]{1,0:T(1,128)} %param.9) | copy-start | bytes 884740
  28.6 9.5 %collective-permute-start.9 = (f32[4,48,384]{2,1,0:T(8,128)S(1)}, f32[4,48,384]{2,1,0:T(8,128)S(1)}, u32[]{:S(2)}, u32[]{:S(2)}) collective-permute-start(f32[4,48,384]{2,1,0:T(8,128)S(1)} %get-tuple-element.60), channel_id=1, source_target_pairs={{0,4},{4,0},{8,12},{12,8},{16,20},{20,16},{24,28},{28,24},{1,5},{5... | collective-permute-start | bytes 884744 | tf_op jit(solution)/shard_map/ppermute | solution.py:420
  36.3 9.3 %collective-permute-start.13 = (f32[576,128]{1,0:T(8,128)S(1)}, f32[576,128]{1,0:T(8,128)S(1)}, u32[]{:S(2)}, u32[]{:S(2)}) collective-permute-start(f32[576,128]{1,0:T(8,128)S(1)} %get-tuple-element.62), channel_id=1, source_target_pairs={{0,4},{4,0},{8,12},{12,8},{16,20},{20,16},{24,28},{28,24},{1,5},{5... | collective-permute-start | bytes 884744 | tf_op jit(solution)/shard_map/ppermute | solution.py:420
  38.1 8.4 %collective-permute-start.10 = (f32[48,384]{1,0:T(8,128)S(1)}, f32[48,384]{1,0:T(8,128)S(1)}, u32[]{:S(2)}, u32[]{:S(2)}) collective-permute-start(f32[48,384]{1,0:T(8,128)S(1)} %get-tuple-element.66), channel_id=1, source_target_pairs={{0,16},{4,20},{8,24},{12,28},{16,0},{20,4},{24,8},{28,12},{1,17},{... | collective-permute-start | bytes 221192 | tf_op jit(solution)/shard_map/ppermute | solution.py:417
  41.3 6.3 %collective-permute-start.11 = (f32[48,384]{1,0:T(8,128)S(1)}, f32[48,384]{1,0:T(8,128)S(1)}, u32[]{:S(2)}, u32[]{:S(2)}) collective-permute-start(f32[48,384]{1,0:T(8,128)S(1)} %get-tuple-element.67), channel_id=1, source_target_pairs={{0,24},{4,28},{8,16},{12,20},{16,8},{20,12},{24,0},{28,4},{1,25},{... | collective-permute-start | bytes 221192 | tf_op jit(solution)/shard_map/ppermute | solution.py:417
  43.1 5.1 %collective-permute-start.12 = (f32[48,384]{1,0:T(8,128)S(1)}, f32[48,384]{1,0:T(8,128)S(1)}, u32[]{:S(2)}, u32[]{:S(2)}) collective-permute-start(f32[48,384]{1,0:T(8,128)S(1)} %get-tuple-element.68), channel_id=1, source_target_pairs={{0,8},{4,12},{8,0},{12,4},{16,24},{20,28},{24,16},{28,20},{1,9},{5... | collective-permute-start | bytes 221192 | tf_op jit(solution)/shard_map/ppermute | solution.py:417

commit v8 on v7

--- a/solution.py
+++ b/solution.py
@@ -123,45 +123,56 @@
     return lax.rem(lax.axis_index("shard") + lax.axis_index("tensor"), 2) == 0
 
 
-def pack_kernel(hops, l_stat_ref, r_stat_ref, l_basis_ref, r_basis_ref, grads_ref, *refs):
-    out_ref, small_ref, *refs = refs
+def first_pack_kernel(blocks, l_basis_ref, r_basis_ref, grads_ref, out_ref, sems):
+    left = is_left()
+    flat_rows = l_basis_ref.shape[0]
+    rows = grads_ref.shape[1]
+    here = lax.axis_index("shard") // 2
+    basis_copy = lambda ref: pltpu.make_async_copy(ref, out_ref.at[pl.ds(0, flat_rows)], sems.at[0])
+
+    @pl.when(left)
+    def _():
+        basis_copy(r_basis_ref).start()
+
+    @pl.when(jnp.logical_not(left))
+    def _():
+        basis_copy(l_basis_ref).start()
+
+    copies = []
+    for k in range(blocks):
+        source = grads_ref.at[here, :, pl.ds(k * LANES, LANES)]
+        target = out_ref.at[pl.ds(flat_rows + k * rows, rows)]
+        copies.append(pltpu.make_async_copy(source, target, sems.at[1 + k]))
+    for copy in copies:
+        copy.start()
+    basis_copy(l_basis_ref).wait()
+    for copy in copies:
+        copy.wait()
+
+
+def pack_kernel(hops, l_stat_ref, r_stat_ref, grads_ref, small_ref, *refs):
     piece_refs, (corner, sems) = refs[: len(hops)], refs[len(hops) :]
     left = is_left()
-    flat_rows = l_basis_ref.shape[0]
-    half_rows = flat_rows // 2
-    rows = grads_ref.shape[1]
+    half_rows = l_stat_ref.shape[0] // 2
     here = lax.axis_index("shard") // 2
-
     start = pl.multiple_of(jnp.where(is_first(), 0, half_rows), 8)
-
-    def copies(basis_ref, stat_ref):
-        return [
-            pltpu.make_async_copy(stat_ref.at[pl.ds(start, half_rows)], corner, sems.at[0]),
-            pltpu.make_async_copy(basis_ref, out_ref.at[pl.ds(0, flat_rows)], sems.at[1]),
-        ]
+    stat_copy = lambda ref: pltpu.make_async_copy(ref.at[pl.ds(start, half_rows)], corner, sems.at[0])
 
     @pl.when(left)
     def _():
-        for copy in copies(r_basis_ref, r_stat_ref):
-            copy.start()
+        stat_copy(r_stat_ref).start()
 
     @pl.when(jnp.logical_not(left))
     def _():
-        for copy in copies(l_basis_ref, l_stat_ref):
-            copy.start()
-
-    more = []
-    for number, (hop, piece_ref) in enumerate(zip(hops, piece_refs)):
-        more.append(pltpu.make_async_copy(grads_ref.at[here ^ hop], piece_ref, sems.at[2 + number]))
-    if hops:
-        for k in range(grads_ref.shape[2] // LANES):
-            source = grads_ref.at[here, :, pl.ds(k * LANES, LANES)]
-            target = out_ref.at[pl.ds(flat_rows + k * rows, rows)]
-            more.append(pltpu.make_async_copy(source, target, sems.at[2 + len(hops) + k]))
-    for copy in more:
+        stat_copy(l_stat_ref).start()
+
+    copies = [
+        pltpu.make_async_copy(grads_ref.at[here ^ hop], piece_ref, sems.at[1 + number])
+        for number, (hop, piece_ref) in enumerate(zip(hops, piece_refs))
+    ]
+    for copy in copies:
         copy.start()
-    first, second = copies(l_basis_ref, l_stat_ref)
-    first.wait()
+    stat_copy(l_stat_ref).wait()
     third = half_rows // 9
     a, b, c = thirds(corner)
     low = low_lanes((third, LANES))
@@ -170,7 +181,7 @@
     small_ref[pl.ds(third, third)] = a[middle]
     small_ref[pl.ds(2 * third, third)] = jnp.where(low, swap(b[middle]), swap(c[middle]))
     small_ref[pl.ds(3 * third, 3 * third)] = corner[pl.ds(6 * third, 3 * third)]
-    for copy in [second, *more]:
+    for copy in copies:
         copy.wait()
 
 
@@ -266,13 +277,14 @@
     x_ref[...] = iterate(power * (1.0 / jnp.sqrt(jnp.sum(power * power) + NORM_EPS)), steps)
 
 
-def end_kernel(steps, start_ref, x_ref, poly_ref, send_ref, scratch):
-    x = iterate(start_ref[...], steps - 1)
-    x_ref[...] = x
-    poly = polynomial(split(x))
-    poly_ref[...] = poly
-    half = take_half(x, jnp.logical_not(is_first()))
-    put_thirds(send_ref, flat_of(scratch, LINEAR_COEFF * half + dot(poly, half)))
+def rows_for(hops, outer_ref, right_parts, out_ref, offset):
+    rows = out_ref.shape[1]
+    here = lax.axis_index("shard") // 2
+    starts = [pl.multiple_of((2 * (here ^ hop) + offset) * rows, 8) if hops else 0 for hop in (0, *hops)]
+    outer = [outer_ref[pl.ds(start, rows), :] for start in starts]
+    partial = dot_parts(split(jnp.concatenate(outer, axis=0)), right_parts, ((1,), (1,)))
+    for k in range(len(starts)):
+        out_ref[k] = partial[k * rows : (k + 1) * rows]
 
 
 def update_kernel(
@@ -284,20 +296,21 @@
     other_left_ref,
     one_ref,
     two_ref,
+    start_ref,
     new_one_ref,
     new_two_ref,
-    mine_ref,
     theirs_ref,
+    outer_ref,
+    x_ref,
     scratch,
-    partial_ref,
 ):
-    left = is_left()
-    first = is_first()
+    left, first = is_left(), is_first()
     own, got = thirds(left_ref), thirds(other_left_ref)
     basis_left = jnp.where(left, basis_ref[...], whole_of(scratch, pick(first, own, got), pick(first, got, own)))
     left_parts = split(basis_left)
-    basis_right = split(right_ref[...])
+    right_parts = split(right_ref[...])
     rotated = flat_of(scratch, dot(basis_left.T, inner_ref[...]))
+    x_ref[...] = iterate(start_ref[...], 1)
     ones = thirds(one_ref)
     twos = thirds(two_ref)
     new_one = [BETA_ONE * m + (1.0 - BETA_ONE) * r for m, r in zip(ones, rotated)]
@@ -305,15 +318,18 @@
     put_thirds(new_one_ref, new_one)
     put_thirds(new_two_ref, new_two)
     direction = [m / (jnp.sqrt(v) + ADAM_EPS) for m, v in zip(new_one, new_two)]
-    outer = dot_parts(left_parts, split(half_of(scratch, direction)))
-    partial_ref[...] = dot_parts(split(outer), basis_right, ((1,), (1,)))
-    rows = mine_ref.shape[1]
-    here = lax.axis_index("shard") // 2
-    parity = lax.axis_index("shard") % 2
-    for k, hop in enumerate((0, *hops)):
-        block = 2 * (here ^ hop) if hops else 0
-        mine_ref[k] = partial_ref[pl.ds(pl.multiple_of((block + parity) * rows, 8), rows), :]
-        theirs_ref[k] = partial_ref[pl.ds(pl.multiple_of((block + 1 - parity) * rows, 8), rows), :]
+    outer_ref[...] = dot_parts(left_parts, split(half_of(scratch, direction)))
+    rows_for(hops, outer_ref, right_parts, theirs_ref, 1 - lax.axis_index("shard") % 2)
+
+
+def end_kernel(hops, steps, start_ref, outer_ref, right_ref, x_ref, poly_ref, send_ref, mine_ref, scratch):
+    x = iterate(start_ref[...], steps - 1)
+    x_ref[...] = x
+    rows_for(hops, outer_ref, split(right_ref[...]), mine_ref, lax.axis_index("shard") % 2)
+    poly = polynomial(split(x))
+    poly_ref[...] = poly
+    half = take_half(x, jnp.logical_not(is_first()))
+    put_thirds(send_ref, flat_of(scratch, LINEAR_COEFF * half + dot(poly, half)))
 
 
 def add_kernel(mine_ref, theirs_ref, *out_refs):
@@ -408,7 +424,7 @@
     sides = [list(range(k, size, 2)) for k in range(2)]
     near = size in (4, 8) and rows_here % 8 == 0
     hops = {4: (1,), 8: (2, 3, 1)}[size] if near else ()
-    strips = (tiles_here, *block) if near else (1, full // 2, full)
+    strips = (tiles_here, *block) if near else (1, full, full)
 
     def exchange(x):
         return lax.all_to_all(x, "shard", split_axis=0, concat_axis=0, axis_index_groups=sides, tiled=True)
@@ -424,18 +440,32 @@
     )
     count = corner_rows(flat_rows)
     outgoing_rows = flat_rows + (rows_here * (full // LANES) if near else 0)
-    outgoing, corner, *pieces = call(
+    in_hbm = lambda *xs: [pltpu.with_memory_space_constraint(x, pltpu.HBM) for x in xs]
+    blocks = full // LANES if near else 0
+    (outgoing,) = call(
+        functools.partial(first_pack_kernel, blocks),
+        [(outgoing_rows, LANES)],
+        [],
+        0.1,
+        full,
+        "first_pack",
+        copies=1 + blocks,
+        kind=pltpu.VMEM,
+        in_specs=anywhere(3),
+        out_specs=anywhere(1),
+    )(*in_hbm(l_basis, r_basis, grads))
+    corner, *pieces = call(
         functools.partial(pack_kernel, hops),
-        [(outgoing_rows, LANES), (count, LANES)] + [block] * len(hops),
+        [(count, LANES)] + [block] * len(hops),
         [(flat_rows // 2, LANES)],
         0.1,
         full,
         "pack",
-        copies=2 + len(hops) + full // LANES,
+        copies=1 + len(hops),
         kind=pltpu.VMEM,
-        in_specs=anywhere(5),
-        out_specs=anywhere(1) + [pl.BlockSpec(memory_space=pltpu.VMEM)] + anywhere(len(hops)),
-    )(*(pltpu.with_memory_space_constraint(x, pltpu.HBM) for x in (l_stat, r_stat, l_basis, r_basis, grads)))
+        in_specs=anywhere(3),
+        out_specs=[pl.BlockSpec(memory_space=pltpu.VMEM)] + anywhere(len(hops)),
+    )(*in_hbm(l_stat, r_stat, grads))
     got = partner(outgoing)
     if near:
         mine = [hop_by(piece, hop) for hop, piece in zip(hops, pieces)]
@@ -468,19 +498,22 @@
     new_stat, x = call(functools.partial(begin_kernel, EARLY_ITERS), [square] * 2, [(3, full, LANES)], 7, full, "begin")(
         own, got_corner, product, basis
     )
-    new_one, new_two, own_rows, other_rows = call(
-        functools.partial(update_kernel, hops), [flat, flat, strips, strips], [(3, full, LANES), square], 2, full, "update"
-    )(after(inner, x), basis, left, right, other_left, one, two)
+    wide = (full, 2 * LANES)
+    new_one, new_two, other_rows, outer, x = call(
+        functools.partial(update_kernel, hops), [flat, flat, strips, wide, square], [(3, full, LANES)], 5, full, "update"
+    )(inner, basis, left, right, other_left, one, two, x)
     if not near:
-        top = jnp.where(parity == 0, own_rows, other_rows)
-        bottom = jnp.where(parity == 0, other_rows, own_rows)
-        merged = jnp.concatenate([top, bottom], axis=1).reshape(tiles_here, 2, rows_here, full)
-        own_rows = lax.dynamic_index_in_dim(merged, parity, 1, keepdims=False)
-        other_rows = lax.dynamic_index_in_dim(merged, 1 - parity, 1, keepdims=False)
+        partial = other_rows.reshape(tiles_here, 2, rows_here, full)
+        other_rows = lax.dynamic_index_in_dim(partial, 1 - parity, 1, keepdims=False)
     got_rows = partner(other_rows)
-    x, poly, send = call(
-        functools.partial(end_kernel, NS_ITERS - EARLY_ITERS), [square, square, flat], [(3, full, LANES)], 9, full, "end"
-    )(after(x, other_rows))
+    x, poly, send, own_rows = call(
+        functools.partial(end_kernel, hops, NS_ITERS - EARLY_ITERS - 1),
+        [square, square, flat, strips],
+        [(3, full, LANES)],
+        9,
+        full,
+        "end",
+    )(after(x, other_rows), outer, right)
     back = partner(send)
     keep, new_left, new_right = call(rest_kernel, [flat, flat, flat], [(3, full, LANES)], 1.5, full, "rest")(
         x, poly, grad, new_stat, other
@@ -502,6 +535,7 @@
             out_specs=anywhere(1),
         )(kept, *returned)[0]
     else:
+        own_rows = lax.dynamic_index_in_dim(partial, parity, 1, keepdims=False)
         update = exchange(after(own_rows, send) + after(got_rows, send))
     new_l_basis, new_r_basis = call(
         bases_kernel, [flat, flat], [], 0.1, full, "bases", copies=2, in_specs=anywhere(2), out_specs=anywhere(2)

time: 49.1 us -> 49.6 us (1.010)
  waiting for transfers between devices: 9.77 us -> 11.4 us
  starting transfers between devices: 19 us -> 17.5 us
    ppermute x7, waiting for transfers between devices: 3.75 us -> 5.35 us  [partner(): return lax.ppermute(x, 'shard', pairs)]
    ppermute x7, starting transfers between devices: 8.73 us -> 8.03 us  [partner(): return lax.ppermute(x, 'shard', pairs)]
    ppermute x6, starting transfers between devices: 9.63 us -> 9.06 us  [hop_by(): return lax.ppermute(x, 'shard', [(i, i ^ 2 * hop) for i in range(size)])]
    pallas_call x3 -> x4, Pallas kernels: 11.2 us -> 11.6 us  [the longest x1 5.78 us: local(): call(functools.partial(end_kernel, hops, NS_ITERS - EARLY_ITERS - 1), [sq...]
  transfers between devices with their start and end apart: 14 -> 14, of which waited for: 8 -> 8; matrix products, arithmetic and copies ran while one was open for 0% -> 0% of each run, Pallas kernels for 30% -> 29%
where the time goes in v8:
time: 49.6 us; the launch traced here: 49.5 us
  Pallas kernels  19.8 us (40%)
  starting transfers between devices  17.5 us (35%)
  waiting for transfers between devices  11.4 us (23%)
  between operations  0.76 us (2%)
    ppermute x6, starting transfers between devices, hop_by(): return lax.ppermute(x, 'shard', [(i, i ^ 2 * hop) for i in range(size)])  9.06 us
    ppermute x7, starting transfers between devices, partner(): return lax.ppermute(x, 'shard', pairs)  8.03 us
    ppermute x6, waiting for transfers between devices, hop_by(): return lax.ppermute(x, 'shard', [(i, i ^ 2 * hop) for i in range(size)])  6.04 us
    pallas_call x1, Pallas kernels, local(): call(functools.partial(end_kernel, hops, NS_ITERS - EARLY_ITERS - 1), [sq...  5.78 us
    ppermute x7, waiting for transfers between devices, partner(): return lax.ppermute(x, 'shard', pairs)  5.35 us
    pallas_call x1, Pallas kernels, local(): call(functools.partial(update_kernel, hops), [flat, flat, strips, wide, s...  3.66 us
    pallas_call x1, Pallas kernels, local(): call(functools.partial(begin_kernel, EARLY_ITERS), [square] * 2, [(3, ful...  3.34 us
    pallas_call x1, Pallas kernels, local(): call(rest_kernel, [flat, flat, flat], [(3, full, LANES)], 1.5, full, 'rest')  2.04 us
  transfers between devices with their start and end apart: 14, of which 8 were waited for; matrix products, arithmetic and copies ran while one was open for 0% of the time, Pallas kernels for 29%

profile of v8, /device:TPU:0, one launch (start us, length us, event | category | flops | bytes accessed | tf_op | source)
XLA Modules:
  0.0 49.5 jit_solution(17344706183695229555)
XLA Ops:
  0.6 0.0 copy-start.4
  0.6 0.0 copy-start.3
  0.7 1.1 %first_pack.1 = f32[720,128]{1,0:T(8,128)S(1)} custom-call(f32[576,128]{1,0:T(8,128)} %bitcast.18, f32[576,128]{1,0:T(8,128)} %bitcast.16, f32[4,48,384]{2,1,0:T(8,128)} %refs_0_.1), custom_call_target="tpu_custom_call" | custom-call | flops 33973864 | bytes 2359296 | tf_op jit(solution)/shard_map/first_pack/pallas_call | solution.py:445
  1.7 3.0 %collective-permute-start = (f32[720,128]{1,0:T(8,128)S(1)}, f32[720,128]{1,0:T(8,128)S(1)}, u32[]{:S(2)}, u32[]{:S(2)}) collective-permute-start(f32[720,128]{1,0:T(8,128)S(1)} %first_pack.1), channel_id=1, source_target_pairs={{0,4},{4,0},{8,12},{12,8},{16,20},{20,16},{24,28},{28,24},{1,5},{5... | collective-permute-start | bytes 1105928 | tf_op jit(solution)/shard_map/ppermute | solution.py:436
  4.8 0.0 copy-start
  4.8 0.0 copy-start.1
  4.8 1.1 %pack.1 = (f32[192,128]{1,0:T(8,128)S(1)}, f32[48,384]{1,0:T(8,128)S(1)}, f32[48,384]{1,0:T(8,128)S(1)}, f32[48,384]{1,0:T(8,128)S(1)}) custom-call(f32[576,128]{1,0:T(8,128)} %bitcast.12, f32[576,128]{1,0:T(8,128)} %bitcast.14, f32[4,48,384]{2,1,0:T(8,128)} %refs_0_.1), custom_call_target="tpu_custom_call" | custom-call | flops 33973864 | bytes 2359296 | tf_op jit(solution)/shard_map/pack/pallas_call | solution.py:457
  5.9 2.7 %collective-permute-start.1 = (f32[48,384]{1,0:T(8,128)S(1)}, f32[48,384]{1,0:T(8,128)S(1)}, u32[]{:S(2)}, u32[]{:S(2)}) collective-permute-start(f32[48,384]{1,0:T(8,128)S(1)} %get-tuple-element.44), channel_id=1, source_target_pairs={{0,16},{4,20},{8,24},{12,28},{16,0},{20,4},{24,8},{28,12},{1,17},{... | collective-permute-start | bytes 221192 | tf_op jit(solution)/shard_map/ppermute | solution.py:433
  8.6 1.3 %collective-permute-start.2 = (f32[48,384]{1,0:T(8,128)S(1)}, f32[48,384]{1,0:T(8,128)S(1)}, u32[]{:S(2)}, u32[]{:S(2)}) collective-permute-start(f32[48,384]{1,0:T(8,128)S(1)} %get-tuple-element.45), channel_id=1, source_target_pairs={{0,24},{4,28},{8,16},{12,20},{16,8},{20,12},{24,0},{28,4},{1,25},{... | collective-permute-start | bytes 221192 | tf_op jit(solution)/shard_map/ppermute | solution.py:433
  9.9 0.2 collective-permute-start.3
  10.2 3.2 %collective-permute-done.1.refs_1_ = f32[48,384]{1,0:T(8,128)S(1)} collective-permute-done((f32[48,384]{1,0:T(8,128)S(1)}, f32[48,384]{1,0:T(8,128)S(1)}, u32[]{:S(2)}, u32[]{:S(2)}) %collective-permute-start.1) | collective-permute-done | bytes 73760 | tf_op jit(solution)/shard_map/ppermute | solution.py:433
  13.4 0.5 collective-permute-start.4
  13.8 1.1 %collective-permute-done.2.refs_2_ = f32[48,384]{1,0:T(8,128)S(1)} collective-permute-done((f32[48,384]{1,0:T(8,128)S(1)}, f32[48,384]{1,0:T(8,128)S(1)}, u32[]{:S(2)}, u32[]{:S(2)}) %collective-permute-start.2) | collective-permute-done | bytes 73760 | tf_op jit(solution)/shard_map/ppermute | solution.py:433
  14.9 0.5 %collective-permute-start.5 = (f32[48,384]{1,0:T(8,128)S(1)}, f32[48,384]{1,0:T(8,128)S(1)}, u32[]{:S(2)}, u32[]{:S(2)}) collective-permute-start(f32[48,384]{1,0:T(8,128)S(1)} %collective-permute-done.2.refs_2_), channel_id=1, source_target_pairs={{0,4},{4,0},{8,12},{12,8},{16,20},{20,16},{24,28},{28,24},{1,5},{5... | collective-permute-start | bytes 221192 | tf_op jit(solution)/shard_map/ppermute | solution.py:436
  15.4 0.0 collective-permute-done.3.refs_3_
  15.4 1.5 %collective-permute-start.6 = (f32[48,384]{1,0:T(8,128)S(1)}, f32[48,384]{1,0:T(8,128)S(1)}, u32[]{:S(2)}, u32[]{:S(2)}) collective-permute-start(f32[48,384]{1,0:T(8,128)S(1)} %collective-permute-done.3.refs_3_), channel_id=1, source_target_pairs={{0,4},{4,0},{8,12},{12,8},{16,20},{20,16},{24,28},{28,24},{1,5},{5... | collective-permute-start | bytes 221192 | tf_op jit(solution)/shard_map/ppermute | solution.py:436
  16.9 1.6 %collective-permute-done.4.refs_4_ = f32[48,384]{1,0:T(8,128)S(1)} collective-permute-done((f32[48,384]{1,0:T(8,128)S(1)}, f32[48,384]{1,0:T(8,128)S(1)}, u32[]{:S(2)}, u32[]{:S(2)}) %collective-permute-start.4) | collective-permute-done | bytes 73760 | tf_op jit(solution)/shard_map/ppermute | solution.py:436
  18.6 0.4 collective-permute-start.8
  19.0 1.2 %collective-permute-done.5.refs_5_ = f32[48,384]{1,0:T(8,128)S(1)} collective-permute-done((f32[48,384]{1,0:T(8,128)S(1)}, f32[48,384]{1,0:T(8,128)S(1)}, u32[]{:S(2)}, u32[]{:S(2)}) %collective-permute-start.5) | collective-permute-done | bytes 73760 | tf_op jit(solution)/shard_map/ppermute | solution.py:436
  20.1 0.0 copy-done.4
  20.1 0.5 collective-permute-start.7
  20.6 1.1 %collective-permute-done.6.refs_6_ = f32[48,384]{1,0:T(8,128)S(1)} collective-permute-done((f32[48,384]{1,0:T(8,128)S(1)}, f32[48,384]{1,0:T(8,128)S(1)}, u32[]{:S(2)}, u32[]{:S(2)}) %collective-permute-start.6) | collective-permute-done | bytes 73760 | tf_op jit(solution)/shard_map/ppermute | solution.py:436
  21.7 0.0 collective-permute-done.got_ref
  21.7 0.0 copy-done.3
  21.7 0.0 copy-done
  21.7 0.0 copy-done.1
  21.7 0.0 copy-done.2
  21.7 1.1 %products.1 = (f32[384,384]{1,0:T(8,128)S(1)}, f32[384,384]{1,0:T(8,128)S(1)}, f32[384,384]{1,0:T(8,128)S(1)}, f32[384,256]{1,0:T(8,128)S(1)}, f32[384,256]{1,0:...) custom-call(f32[576,128]{1,0:T(8,128)S(1)} %bitcast.13, ...), custom_call_target="tpu_custom_call" | custom-call | flops 679477248 | bytes 2359296 | tf_op jit(solution)/shard_map/products/pallas_call | solution.py:481
  22.9 1.4 %collective-permute-done.8.corner_ref = f32[192,128]{1,0:T(8,128)S(1)} collective-permute-done((f32[192,128]{1,0:T(8,128)S(1)}, f32[192,128]{1,0:T(8,128)S(1)}, u32[]{:S(2)}, u32[]{:S(2)}) %collective-permute-start.8) | collective-permute-done | bytes 98336 | tf_op jit(solution)/shard_map/ppermute | solution.py:436
  24.3 3.3 %begin.1 = (f32[384,384]{1,0:T(8,128)S(1)}, f32[384,384]{1,0:T(8,128)S(1)}) custom-call(f32[576,128]{1,0:T(8,128)S(1)} %get-tuple-element.52.own_ref, f32[192,128]{1,0:T(8,128)S(1)} %collective-permute-done.8.corner_ref, f32[384,384]{1,0:T(8,128)S(1)} %get-tuple-element.55.product_ref, f32[384,384]{1,0:T(8,128)S(1)} %get-tuple-element.48.basis_ref), custom_call_target="tpu_custom_call" | custom-call | flops 2378170368 | bytes 2359296 | tf_op jit(solution)/shard_map/begin/pallas_call | solution.py:498
  27.6 0.0 collective-permute-done.7.other_left_ref
  27.6 0.0 copy-done.5
  27.7 0.0 copy-done.6
  27.7 3.7 %update.1 = (f32[576,128]{1,0:T(8,128)}, f32[576,128]{1,0:T(8,128)}, f32[4,48,384]{2,1,0:T(8,128)S(1)}, f32[384,256]{1,0:T(8,128)S(1)}, f32[384,384]{1,0:T(8,128)S(1)}) custom-call(f32[384,256]{1,0:T(8,128)S(1)} %get-tuple-element.47.inner_ref, f32[384,384]{1,0:T(8,128)S(1)} %get-tuple-element.48.basis_ref, f32[576,128]{1,0:T(8,128)S(1)} %get-tuple-element.49.left_ref, ...), custom_call_target="tpu_custom_call" | custom-call | flops 1698693120 | bytes 2359296 | tf_op jit(solution)/shard_map/update/pallas_call | solution.py:502
  31.3 0.0 collective-permute-start.9
  31.3 5.8 %end.1 = (f32[384,384]{1,0:T(8,128)S(1)}, f32[384,384]{1,0:T(8,128)S(1)}, f32[576,128]{1,0:T(8,128)S(1)}, f32[4,48,384]{2,1,0:T(8,128)S(1)}) custom-call(f32[384,384]{1,0:T(8,128)S(1)} %get-tuple-element.59.start_ref, f32[384,256]{1,0:T(8,128)S(1)} %get-tuple-element.60.outer_ref, f32[384,256]{1,0:T(8,128)S(1)} %get-tuple-element.50.right_ref), custom_call_target="tpu_custom_call" | custom-call | flops 3057647616 | bytes 2359296 | tf_op jit(solution)/shard_map/end/pallas_call | solution.py:509
  37.1 2.1 %collective-permute-start.13 = (f32[576,128]{1,0:T(8,128)S(1)}, f32[576,128]{1,0:T(8,128)S(1)}, u32[]{:S(2)}, u32[]{:S(2)}) collective-permute-start(f32[576,128]{1,0:T(8,128)S(1)} %get-tuple-element.62), channel_id=1, source_target_pairs={{0,4},{4,0},{8,12},{12,8},{16,20},{20,16},{24,28},{28,24},{1,5},{5... | collective-permute-start | bytes 884744 | tf_op jit(solution)/shard_map/ppermute | solution.py:436
  39.2 0.0 collective-permute-done.9.theirs_ref
  39.2 2.6 %collective-permute-start.10 = (f32[48,384]{1,0:T(8,128)S(1)}, f32[48,384]{1,0:T(8,128)S(1)}, u32[]{:S(2)}, u32[]{:S(2)}) collective-permute-start(f32[48,384]{1,0:T(8,128)S(1)} %get-tuple-element.66), channel_id=1, source_target_pairs={{0,16},{4,20},{8,24},{12,28},{16,0},{20,4},{24,8},{28,12},{1,17},{... | collective-permute-start | bytes 221192 | tf_op jit(solution)/shard_map/ppermute | solution.py:433
  41.8 1.8 %collective-permute-start.11 = (f32[48,384]{1,0:T(8,128)S(1)}, f32[48,384]{1,0:T(8,128)S(1)}, u32[]{:S(2)}, u32[]{:S(2)}) collective-permute-start(f32[48,384]{1,0:T(8,128)S(1)} %get-tuple-element.67), channel_id=1, source_target_pairs={{0,24},{4,28},{8,16},{12,20},{16,8},{20,12},{24,0},{28,4},{1,25},{... | collective-permute-start | bytes 221192 | tf_op jit(solution)/shard_map/ppermute | solution.py:433
  43.6 0.5 collective-permute-start.12
  44.1 2.0 %rest.1 = (f32[576,128]{1,0:T(8,128)S(1)}, f32[576,128]{1,0:T(8,128)}, f32[576,128]{1,0:T(8,128)}) custom-call(f32[384,384]{1,0:T(8,128)S(1)} %get-tuple-element.71.x_ref, f32[384,384]{1,0:T(8,128)S(1)} %get-tuple-element.72.poly_ref, f32[384,384]{1,0:T(8,128)S(1)} %get-tuple-element.73.grad_ref, f32[384,384]{1,0:T(8,128)S(1)} %get-tuple-element.74.new_stat_ref, ...), custom_call_target="tpu_custom_call" | custom-call | flops 509607936 | bytes 2359296 | tf_op jit(solution)/shard_map/rest/pallas_call | solution.py:518
  46.1 0.0 collective-permute-done.13.back_ref
  46.1 0.8 %bases.1 = (f32[576,128]{1,0:T(8,128)}, f32[576,128]{1,0:T(8,128)}) custom-call(f32[576,128]{1,0:T(8,128)S(1)} %get-tuple-element.78.keep_ref, f32[576,128]{1,0:T(8,128)S(1)} %collective-permute-done.13.back_ref), custom_call_target="tpu_custom_call" | custom-call | flops 33973864 | bytes 2359296 | tf_op jit(solution)/shard_map/bases/pallas_call | solution.py:540
  46.9 0.0 collective-permute-done.10.refs_1_
  46.9 1.2 %collective-permute-done.11.refs_2_ = f32[48,384]{1,0:T(8,128)S(1)} collective-permute-done((f32[48,384]{1,0:T(8,128)S(1)}, f32[48,384]{1,0:T(8,128)S(1)}, u32[]{:S(2)}, u32[]{:S(2)}) %collective-permute-start.11) | collective-permute-done | bytes 73760 | tf_op jit(solution)/shard_map/ppermute | solution.py:433
  48.1 0.6 %collective-permute-done.12.refs_3_ = f32[48,384]{1,0:T(8,128)S(1)} collective-permute-done((f32[48,384]{1,0:T(8,128)S(1)}, f32[48,384]{1,0:T(8,128)S(1)}, u32[]{:S(2)}, u32[]{:S(2)}) %collective-permute-start.12) | collective-permute-done | bytes 73760 | tf_op jit(solution)/shard_map/ppermute | solution.py:433
  48.7 0.7 %rows.1 = f32[4,48,384]{2,1,0:T(8,128)} custom-call(f32[48,384]{1,0:T(8,128)S(1)} %get-tuple-element.65.refs_0_, f32[48,384]{1,0:T(8,128)S(1)} %collective-permute-done.10.refs_1_, f32[48,384]{1,0:T(8,128)S(1)} %collective-permute-done.11.refs_2_, f32[48,384]{1,0:T(8,128)S(1)} %collective-permute-done.12.refs_3_), custom_call_target="tpu_custom_call" | custom-call | flops 33973864 | bytes 2359296 | tf_op jit(solution)/shard_map/rows/pallas_call | solution.py:526
  (4 shorter events, 0.0 us)
Async XLA Ops:
  0.6 19.5 %copy-start.4 = (f32[1,73728]{1,0:T(1,128)S(1)}, f32[1,73728]{1,0:T(1,128)}, u32[]{:S(2)}) copy-start(f32[1,73728]{1,0:T(1,128)} %param.12) | copy-start | bytes 884740
  0.6 21.1 %copy-start.3 = (f32[1,73728]{1,0:T(1,128)S(1)}, f32[1,73728]{1,0:T(1,128)}, u32[]{:S(2)}) copy-start(f32[1,73728]{1,0:T(1,128)} %param.13) | copy-start | bytes 884740
  1.7 20.0 %collective-permute-start = (f32[720,128]{1,0:T(8,128)S(1)}, f32[720,128]{1,0:T(8,128)S(1)}, u32[]{:S(2)}, u32[]{:S(2)}) collective-permute-start(f32[720,128]{1,0:T(8,128)S(1)} %first_pack.1), channel_id=1, source_target_pairs={{0,4},{4,0},{8,12},{12,8},{16,20},{20,16},{24,28},{28,24},{1,5},{5... | collective-permute-start | bytes 1105928 | tf_op jit(solution)/shard_map/ppermute | solution.py:436
  4.8 17.0 %copy-start = (f32[4,48,384]{2,1,0:T(8,128)S(1)}, f32[4,48,384]{2,1,0:T(8,128)}, u32[]{:S(2)}) copy-start(f32[4,48,384]{2,1,0:T(8,128)} %refs_0_.1) | copy-start | bytes 884740
  4.8 17.0 %copy-start.1 = (f32[1,73728]{1,0:T(1,128)S(1)}, f32[1,73728]{1,0:T(1,128)}, u32[]{:S(2)}) copy-start(f32[1,73728]{1,0:T(1,128)} %param.10) | copy-start | bytes 884740
  4.8 17.0 %copy-start.2 = (f32[1,73728]{1,0:T(1,128)S(1)}, f32[1,73728]{1,0:T(1,128)}, u32[]{:S(2)}) copy-start(f32[1,73728]{1,0:T(1,128)} %param.11) | copy-start | bytes 884740
  5.9 7.4 %collective-permute-start.1 = (f32[48,384]{1,0:T(8,128)S(1)}, f32[48,384]{1,0:T(8,128)S(1)}, u32[]{:S(2)}, u32[]{:S(2)}) collective-permute-start(f32[48,384]{1,0:T(8,128)S(1)} %get-tuple-element.44), channel_id=1, source_target_pairs={{0,16},{4,20},{8,24},{12,28},{16,0},{20,4},{24,8},{28,12},{1,17},{... | collective-permute-start | bytes 221192 | tf_op jit(solution)/shard_map/ppermute | solution.py:433
  8.6 6.3 %collective-permute-start.2 = (f32[48,384]{1,0:T(8,128)S(1)}, f32[48,384]{1,0:T(8,128)S(1)}, u32[]{:S(2)}, u32[]{:S(2)}) collective-permute-start(f32[48,384]{1,0:T(8,128)S(1)} %get-tuple-element.45), channel_id=1, source_target_pairs={{0,24},{4,28},{8,16},{12,20},{16,8},{20,12},{24,0},{28,4},{1,25},{... | collective-permute-start | bytes 221192 | tf_op jit(solution)/shard_map/ppermute | solution.py:433
  9.9 5.5 %collective-permute-start.3 = (f32[48,384]{1,0:T(8,128)S(1)}, f32[48,384]{1,0:T(8,128)S(1)}, u32[]{:S(2)}, u32[]{:S(2)}) collective-permute-start(f32[48,384]{1,0:T(8,128)S(1)} %get-tuple-element.46), channel_id=1, source_target_pairs={{0,8},{4,12},{8,0},{12,4},{16,24},{20,28},{24,16},{28,20},{1,9},{5... | collective-permute-start | bytes 221192 | tf_op jit(solution)/shard_map/ppermute | solution.py:433
  13.4 5.2 %collective-permute-start.4 = (f32[48,384]{1,0:T(8,128)S(1)}, f32[48,384]{1,0:T(8,128)S(1)}, u32[]{:S(2)}, u32[]{:S(2)}) collective-permute-start(f32[48,384]{1,0:T(8,128)S(1)} %collective-permute-done.1.refs_1_), channel_id=1, source_target_pairs={{0,4},{4,0},{8,12},{12,8},{16,20},{20,16},{24,28},{28,24},{1,5},{5... | collective-permute-start | bytes 221192 | tf_op jit(solution)/shard_map/ppermute | solution.py:436
  14.9 5.3 %collective-permute-start.5 = (f32[48,384]{1,0:T(8,128)S(1)}, f32[48,384]{1,0:T(8,128)S(1)}, u32[]{:S(2)}, u32[]{:S(2)}) collective-permute-start(f32[48,384]{1,0:T(8,128)S(1)} %collective-permute-done.2.refs_2_), channel_id=1, source_target_pairs={{0,4},{4,0},{8,12},{12,8},{16,20},{20,16},{24,28},{28,24},{1,5},{5... | collective-permute-start | bytes 221192 | tf_op jit(solution)/shard_map/ppermute | solution.py:436
  15.4 6.3 %collective-permute-start.6 = (f32[48,384]{1,0:T(8,128)S(1)}, f32[48,384]{1,0:T(8,128)S(1)}, u32[]{:S(2)}, u32[]{:S(2)}) collective-permute-start(f32[48,384]{1,0:T(8,128)S(1)} %collective-permute-done.3.refs_3_), channel_id=1, source_target_pairs={{0,4},{4,0},{8,12},{12,8},{16,20},{20,16},{24,28},{28,24},{1,5},{5... | collective-permute-start | bytes 221192 | tf_op jit(solution)/shard_map/ppermute | solution.py:436
  18.6 5.7 %collective-permute-start.8 = (f32[192,128]{1,0:T(8,128)S(1)}, f32[192,128]{1,0:T(8,128)S(1)}, u32[]{:S(2)}, u32[]{:S(2)}) collective-permute-start(f32[192,128]{1,0:T(8,128)S(1)} %get-tuple-element.54), channel_id=1, source_target_pairs={{0,4},{4,0},{8,12},{12,8},{16,20},{20,16},{24,28},{28,24},{1,5},{5... | collective-permute-start | bytes 294920 | tf_op jit(solution)/shard_map/ppermute | solution.py:436
  20.1 7.5 %collective-permute-start.7 = (f32[576,128]{1,0:T(8,128)S(1)}, f32[576,128]{1,0:T(8,128)S(1)}, u32[]{:S(2)}, u32[]{:S(2)}) collective-permute-start(f32[576,128]{1,0:T(8,128)S(1)} %bitcast.19), channel_id=1, source_target_pairs={{0,4},{4,5},{5,1},{1,0},{8,12},{12,13},{13,9},{9,8},{16,20},{20,21... | collective-permute-start | bytes 884744 | tf_op jit(solution)/shard_map/ppermute | solution.py:497
  24.3 3.4 %copy-start.5 = (f32[1,73728]{1,0:T(1,128)S(1)}, f32[1,73728]{1,0:T(1,128)}, u32[]{:S(2)}) copy-start(f32[1,73728]{1,0:T(1,128)} %param.8) | copy-start | bytes 884740
  24.3 3.4 %copy-start.6 = (f32[1,73728]{1,0:T(1,128)S(1)}, f32[1,73728]{1,0:T(1,128)}, u32[]{:S(2)}) copy-start(f32[1,73728]{1,0:T(1,128)} %param.9) | copy-start | bytes 884740
  31.3 7.9 %collective-permute-start.9 = (f32[4,48,384]{2,1,0:T(8,128)S(1)}, f32[4,48,384]{2,1,0:T(8,128)S(1)}, u32[]{:S(2)}, u32[]{:S(2)}) collective-permute-start(f32[4,48,384]{2,1,0:T(8,128)S(1)} %get-tuple-element.58), channel_id=1, source_target_pairs={{0,4},{4,0},{8,12},{12,8},{16,20},{20,16},{24,28},{28,24},{1,5},{5... | collective-permute-start | bytes 884744 | tf_op jit(solution)/shard_map/ppermute | solution.py:436
  37.1 9.0 %collective-permute-start.13 = (f32[576,128]{1,0:T(8,128)S(1)}, f32[576,128]{1,0:T(8,128)S(1)}, u32[]{:S(2)}, u32[]{:S(2)}) collective-permute-start(f32[576,128]{1,0:T(8,128)S(1)} %get-tuple-element.62), channel_id=1, source_target_pairs={{0,4},{4,0},{8,12},{12,8},{16,20},{20,16},{24,28},{28,24},{1,5},{5... | collective-permute-start | bytes 884744 | tf_op jit(solution)/shard_map/ppermute | solution.py:436
  39.2 7.7 %collective-permute-start.10 = (f32[48,384]{1,0:T(8,128)S(1)}, f32[48,384]{1,0:T(8,128)S(1)}, u32[]{:S(2)}, u32[]{:S(2)}) collective-permute-start(f32[48,384]{1,0:T(8,128)S(1)} %get-tuple-element.66), channel_id=1, source_target_pairs={{0,16},{4,20},{8,24},{12,28},{16,0},{20,4},{24,8},{28,12},{1,17},{... | collective-permute-start | bytes 221192 | tf_op jit(solution)/shard_map/ppermute | solution.py:433
  41.8 6.3 %collective-permute-start.11 = (f32[48,384]{1,0:T(8,128)S(1)}, f32[48,384]{1,0:T(8,128)S(1)}, u32[]{:S(2)}, u32[]{:S(2)}) collective-permute-start(f32[48,384]{1,0:T(8,128)S(1)} %get-tuple-element.67), channel_id=1, source_target_pairs={{0,24},{4,28},{8,16},{12,20},{16,8},{20,12},{24,0},{28,4},{1,25},{... | collective-permute-start | bytes 221192 | tf_op jit(solution)/shard_map/ppermute | solution.py:433
  43.6 5.1 %collective-permute-start.12 = (f32[48,384]{1,0:T(8,128)S(1)}, f32[48,384]{1,0:T(8,128)S(1)}, u32[]{:S(2)}, u32[]{:S(2)}) collective-permute-start(f32[48,384]{1,0:T(8,128)S(1)} %get-tuple-element.68), channel_id=1, source_target_pairs={{0,8},{4,12},{8,0},{12,4},{16,24},{20,28},{24,16},{28,20},{1,9},{5... | collective-permute-start | bytes 221192 | tf_op jit(solution)/shard_map/ppermute | solution.py:433

commit v9 on v7

--- a/solution.py
+++ b/solution.py
@@ -217,6 +217,19 @@
     gram = dot_parts(parts, parts, ((1,), (1,)))
     gram_parts = split(gram)
     return CUBIC_COEFF * gram + QUINTIC_COEFF * dot_parts(gram_parts, gram_parts)
+
+
+def blocked_step(x):
+    parts = split(x)
+    gram = dot_parts(parts, parts, ((1,), (1,)))
+    gram_parts = split(gram)
+    rows = x.shape[0] // 2
+    blocks = []
+    for k in range(2):
+        block = slice(k * rows, (k + 1) * rows)
+        poly = CUBIC_COEFF * gram[block] + QUINTIC_COEFF * dot_parts([part[block] for part in gram_parts], gram_parts)
+        blocks.append(LINEAR_COEFF * x[block] + dot_parts(split(poly), parts))
+    return jnp.concatenate(blocks, axis=0)
 
 
 def iterate(x, steps):
@@ -266,13 +279,14 @@
     x_ref[...] = iterate(power * (1.0 / jnp.sqrt(jnp.sum(power * power) + NORM_EPS)), steps)
 
 
-def end_kernel(steps, start_ref, x_ref, poly_ref, send_ref, scratch):
-    x = iterate(start_ref[...], steps - 1)
-    x_ref[...] = x
-    poly = polynomial(split(x))
-    poly_ref[...] = poly
-    half = take_half(x, jnp.logical_not(is_first()))
-    put_thirds(send_ref, flat_of(scratch, LINEAR_COEFF * half + dot(poly, half)))
+def rows_for(hops, outer_ref, right_parts, out_ref, offset):
+    rows = out_ref.shape[1]
+    here = lax.axis_index("shard") // 2
+    starts = [pl.multiple_of((2 * (here ^ hop) + offset) * rows, 8) if hops else 0 for hop in (0, *hops)]
+    outer = [outer_ref[pl.ds(start, rows), :] for start in starts]
+    partial = dot_parts(split(jnp.concatenate(outer, axis=0)), right_parts, ((1,), (1,)))
+    for k in range(len(starts)):
+        out_ref[k] = partial[k * rows : (k + 1) * rows]
 
 
 def update_kernel(
@@ -284,20 +298,24 @@
     other_left_ref,
     one_ref,
     two_ref,
+    start_ref,
     new_one_ref,
     new_two_ref,
-    mine_ref,
     theirs_ref,
+    outer_ref,
+    x_ref,
     scratch,
-    partial_ref,
 ):
-    left = is_left()
-    first = is_first()
+    left, first = is_left(), is_first()
+    x = start_ref[...]
+    parts = split(x)
+    gram = dot_parts(parts, parts, ((1,), (1,)))
     own, got = thirds(left_ref), thirds(other_left_ref)
     basis_left = jnp.where(left, basis_ref[...], whole_of(scratch, pick(first, own, got), pick(first, got, own)))
-    left_parts = split(basis_left)
-    basis_right = split(right_ref[...])
-    rotated = flat_of(scratch, dot(basis_left.T, inner_ref[...]))
+    rotated = dot(basis_left.T, inner_ref[...])
+    gram_parts = split(gram)
+    square = dot_parts(gram_parts, gram_parts)
+    rotated = flat_of(scratch, rotated)
     ones = thirds(one_ref)
     twos = thirds(two_ref)
     new_one = [BETA_ONE * m + (1.0 - BETA_ONE) * r for m, r in zip(ones, rotated)]
@@ -305,15 +323,23 @@
     put_thirds(new_one_ref, new_one)
     put_thirds(new_two_ref, new_two)
     direction = [m / (jnp.sqrt(v) + ADAM_EPS) for m, v in zip(new_one, new_two)]
-    outer = dot_parts(left_parts, split(half_of(scratch, direction)))
-    partial_ref[...] = dot_parts(split(outer), basis_right, ((1,), (1,)))
-    rows = mine_ref.shape[1]
-    here = lax.axis_index("shard") // 2
-    parity = lax.axis_index("shard") % 2
-    for k, hop in enumerate((0, *hops)):
-        block = 2 * (here ^ hop) if hops else 0
-        mine_ref[k] = partial_ref[pl.ds(pl.multiple_of((block + parity) * rows, 8), rows), :]
-        theirs_ref[k] = partial_ref[pl.ds(pl.multiple_of((block + 1 - parity) * rows, 8), rows), :]
+    outer_ref[...] = dot_parts(split(basis_left), split(half_of(scratch, direction)))
+    poly_parts = split(CUBIC_COEFF * gram + QUINTIC_COEFF * square)
+    moved = dot_parts(poly_parts, parts)
+    rows_for(hops, outer_ref, split(right_ref[...]), theirs_ref, 1 - lax.axis_index("shard") % 2)
+    x_ref[...] = LINEAR_COEFF * x + moved
+
+
+def end_kernel(hops, steps, start_ref, outer_ref, right_ref, x_ref, poly_ref, send_ref, mine_ref, scratch):
+    x = start_ref[...]
+    for _ in range(steps - 1):
+        x = blocked_step(x)
+    x_ref[...] = x
+    rows_for(hops, outer_ref, split(right_ref[...]), mine_ref, lax.axis_index("shard") % 2)
+    poly = polynomial(split(x))
+    poly_ref[...] = poly
+    half = take_half(x, jnp.logical_not(is_first()))
+    put_thirds(send_ref, flat_of(scratch, LINEAR_COEFF * half + dot(poly, half)))
 
 
 def add_kernel(mine_ref, theirs_ref, *out_refs):
@@ -408,7 +434,7 @@
     sides = [list(range(k, size, 2)) for k in range(2)]
     near = size in (4, 8) and rows_here % 8 == 0
     hops = {4: (1,), 8: (2, 3, 1)}[size] if near else ()
-    strips = (tiles_here, *block) if near else (1, full // 2, full)
+    strips = (tiles_here, *block) if near else (1, full, full)
 
     def exchange(x):
         return lax.all_to_all(x, "shard", split_axis=0, concat_axis=0, axis_index_groups=sides, tiled=True)
@@ -468,19 +494,22 @@
     new_stat, x = call(functools.partial(begin_kernel, EARLY_ITERS), [square] * 2, [(3, full, LANES)], 7, full, "begin")(
         own, got_corner, product, basis
     )
-    new_one, new_two, own_rows, other_rows = call(
-        functools.partial(update_kernel, hops), [flat, flat, strips, strips], [(3, full, LANES), square], 2, full, "update"
-    )(after(inner, x), basis, left, right, other_left, one, two)
+    wide = (full, 2 * LANES)
+    new_one, new_two, other_rows, outer, x = call(
+        functools.partial(update_kernel, hops), [flat, flat, strips, wide, square], [(3, full, LANES)], 5, full, "update"
+    )(inner, basis, left, right, other_left, one, two, x)
     if not near:
-        top = jnp.where(parity == 0, own_rows, other_rows)
-        bottom = jnp.where(parity == 0, other_rows, own_rows)
-        merged = jnp.concatenate([top, bottom], axis=1).reshape(tiles_here, 2, rows_here, full)
-        own_rows = lax.dynamic_index_in_dim(merged, parity, 1, keepdims=False)
-        other_rows = lax.dynamic_index_in_dim(merged, 1 - parity, 1, keepdims=False)
+        partial = other_rows.reshape(tiles_here, 2, rows_here, full)
+        other_rows = lax.dynamic_index_in_dim(partial, 1 - parity, 1, keepdims=False)
     got_rows = partner(other_rows)
-    x, poly, send = call(
-        functools.partial(end_kernel, NS_ITERS - EARLY_ITERS), [square, square, flat], [(3, full, LANES)], 9, full, "end"
-    )(after(x, other_rows))
+    x, poly, send, own_rows = call(
+        functools.partial(end_kernel, hops, NS_ITERS - EARLY_ITERS - 1),
+        [square, square, flat, strips],
+        [(3, full, LANES)],
+        9,
+        full,
+        "end",
+    )(after(x, other_rows), outer, right)
     back = partner(send)
     keep, new_left, new_right = call(rest_kernel, [flat, flat, flat], [(3, full, LANES)], 1.5, full, "rest")(
         x, poly, grad, new_stat, other
@@ -502,6 +531,7 @@
             out_specs=anywhere(1),
         )(kept, *returned)[0]
     else:
+        own_rows = lax.dynamic_index_in_dim(partial, parity, 1, keepdims=False)
         update = exchange(after(own_rows, send) + after(got_rows, send))
     new_l_basis, new_r_basis = call(
         bases_kernel, [flat, flat], [], 0.1, full, "bases", copies=2, in_specs=anywhere(2), out_specs=anywhere(2)

time: 49.1 us -> 48.5 us (0.988)
  Pallas kernels: 19.4 us -> 18.7 us
    pallas_call x2, Pallas kernels: 9.89 us -> 9.27 us  [the longest x1 6.03 us: local(): call(functools.partial(end_kernel, hops, NS_ITERS - EARLY_ITERS - 1), [sq...]
  transfers between devices with their start and end apart: 14 -> 14, of which waited for: 8 -> 8; matrix products, arithmetic and copies ran while one was open for 0% -> 0% of each run, Pallas kernels for 30% -> 28%
where the time goes in v9:
time: 48.5 us; the launch traced here: 48.3 us
  starting transfers between devices  19 us (39%)
  Pallas kernels  18.7 us (39%)
  waiting for transfers between devices  9.8 us (20%)
  between operations  0.77 us (2%)
    ppermute x6, starting transfers between devices, hop_by(): return lax.ppermute(x, 'shard', [(i, i ^ 2 * hop) for i in range(size)])  9.63 us
    ppermute x7, starting transfers between devices, partner(): return lax.ppermute(x, 'shard', pairs)  8.73 us
    ppermute x6, waiting for transfers between devices, hop_by(): return lax.ppermute(x, 'shard', [(i, i ^ 2 * hop) for i in range(size)])  6.04 us
    pallas_call x1, Pallas kernels, local(): call(functools.partial(end_kernel, hops, NS_ITERS - EARLY_ITERS - 1), [sq...  6.03 us
    ppermute x7, waiting for transfers between devices, partner(): return lax.ppermute(x, 'shard', pairs)  3.75 us
    pallas_call x1, Pallas kernels, local(): call(functools.partial(begin_kernel, EARLY_ITERS), [square] * 2, [(3, ful...  3.35 us
    pallas_call x1, Pallas kernels, local(): call(functools.partial(update_kernel, hops), [flat, flat, strips, wide, s...  3.25 us
    pallas_call x1, Pallas kernels, local(): call(rest_kernel, [flat, flat, flat], [(3, full, LANES)], 1.5, full, 'rest')  2.04 us
  transfers between devices with their start and end apart: 14, of which 8 were waited for; matrix products, arithmetic and copies ran while one was open for 0% of the time, Pallas kernels for 28%

profile of v9, /device:TPU:0, one launch (start us, length us, event | category | flops | bytes accessed | tf_op | source)
XLA Modules:
  0.0 48.3 jit_solution(2271777150464156086)
XLA Ops:
  0.6 0.0 copy-start.4
  0.6 0.0 copy-start
  0.7 0.0 copy-start.1
  0.7 0.0 copy-start.2
  0.7 0.0 copy-start.3
  0.7 1.3 %pack.1 = (f32[720,128]{1,0:T(8,128)S(1)}, f32[192,128]{1,0:T(8,128)S(1)}, f32[48,384]{1,0:T(8,128)S(1)}, f32[48,384]{1,0:T(8,128)S(1)}, f32[48,384]{1,0:T(8,128)S(1)}) custom-call(f32[576,128]{1,0:T(8,128)} %bitcast.12, f32[576,128]{1,0:T(8,128)} %bitcast.14, f32[576,128]{1,0:T(8,128)} %bitcast.18, f32[576,128]{1,0:T(8,128)} %bitcast.16, f32[4,48,384]{2,1,0:T(8,128)} %refs_0_.1), custom_call_target="tpu_custom_call" | custom-call | flops 33973864 | bytes 2359296 | tf_op jit(solution)/shard_map/pack/pallas_call | solution.py:453
  2.0 3.0 %collective-permute-start = (f32[720,128]{1,0:T(8,128)S(1)}, f32[720,128]{1,0:T(8,128)S(1)}, u32[]{:S(2)}, u32[]{:S(2)}) collective-permute-start(f32[720,128]{1,0:T(8,128)S(1)} %get-tuple-element.45), channel_id=1, source_target_pairs={{0,4},{4,0},{8,12},{12,8},{16,20},{20,16},{24,28},{28,24},{1,5},{5... | collective-permute-start | bytes 1105928 | tf_op jit(solution)/shard_map/ppermute | solution.py:446
  5.0 2.6 %collective-permute-start.1 = (f32[48,384]{1,0:T(8,128)S(1)}, f32[48,384]{1,0:T(8,128)S(1)}, u32[]{:S(2)}, u32[]{:S(2)}) collective-permute-start(f32[48,384]{1,0:T(8,128)S(1)} %get-tuple-element.46), channel_id=1, source_target_pairs={{0,16},{4,20},{8,24},{12,28},{16,0},{20,4},{24,8},{28,12},{1,17},{... | collective-permute-start | bytes 221192 | tf_op jit(solution)/shard_map/ppermute | solution.py:443
  7.6 1.3 %collective-permute-start.2 = (f32[48,384]{1,0:T(8,128)S(1)}, f32[48,384]{1,0:T(8,128)S(1)}, u32[]{:S(2)}, u32[]{:S(2)}) collective-permute-start(f32[48,384]{1,0:T(8,128)S(1)} %get-tuple-element.47), channel_id=1, source_target_pairs={{0,24},{4,28},{8,16},{12,20},{16,8},{20,12},{24,0},{28,4},{1,25},{... | collective-permute-start | bytes 221192 | tf_op jit(solution)/shard_map/ppermute | solution.py:443
  9.0 0.2 collective-permute-start.3
  9.2 3.2 %collective-permute-done.1.refs_1_ = f32[48,384]{1,0:T(8,128)S(1)} collective-permute-done((f32[48,384]{1,0:T(8,128)S(1)}, f32[48,384]{1,0:T(8,128)S(1)}, u32[]{:S(2)}, u32[]{:S(2)}) %collective-permute-start.1) | collective-permute-done | bytes 73760 | tf_op jit(solution)/shard_map/ppermute | solution.py:443
  12.4 0.5 collective-permute-start.4
  12.9 1.1 %collective-permute-done.2.refs_2_ = f32[48,384]{1,0:T(8,128)S(1)} collective-permute-done((f32[48,384]{1,0:T(8,128)S(1)}, f32[48,384]{1,0:T(8,128)S(1)}, u32[]{:S(2)}, u32[]{:S(2)}) %collective-permute-start.2) | collective-permute-done | bytes 73760 | tf_op jit(solution)/shard_map/ppermute | solution.py:443
  13.9 0.5 %collective-permute-start.5 = (f32[48,384]{1,0:T(8,128)S(1)}, f32[48,384]{1,0:T(8,128)S(1)}, u32[]{:S(2)}, u32[]{:S(2)}) collective-permute-start(f32[48,384]{1,0:T(8,128)S(1)} %collective-permute-done.2.refs_2_), channel_id=1, source_target_pairs={{0,4},{4,0},{8,12},{12,8},{16,20},{20,16},{24,28},{28,24},{1,5},{5... | collective-permute-start | bytes 221192 | tf_op jit(solution)/shard_map/ppermute | solution.py:446
  14.4 0.0 collective-permute-done.3.refs_3_
  14.5 1.5 %collective-permute-start.6 = (f32[48,384]{1,0:T(8,128)S(1)}, f32[48,384]{1,0:T(8,128)S(1)}, u32[]{:S(2)}, u32[]{:S(2)}) collective-permute-start(f32[48,384]{1,0:T(8,128)S(1)} %collective-permute-done.3.refs_3_), channel_id=1, source_target_pairs={{0,4},{4,0},{8,12},{12,8},{16,20},{20,16},{24,28},{28,24},{1,5},{5... | collective-permute-start | bytes 221192 | tf_op jit(solution)/shard_map/ppermute | solution.py:446
  16.0 1.0 %collective-permute-done.4.refs_4_ = f32[48,384]{1,0:T(8,128)S(1)} collective-permute-done((f32[48,384]{1,0:T(8,128)S(1)}, f32[48,384]{1,0:T(8,128)S(1)}, u32[]{:S(2)}, u32[]{:S(2)}) %collective-permute-start.4) | collective-permute-done | bytes 73760 | tf_op jit(solution)/shard_map/ppermute | solution.py:446
  17.0 1.1 %collective-permute-start.8 = (f32[192,128]{1,0:T(8,128)S(1)}, f32[192,128]{1,0:T(8,128)S(1)}, u32[]{:S(2)}, u32[]{:S(2)}) collective-permute-start(f32[192,128]{1,0:T(8,128)S(1)} %get-tuple-element.56), channel_id=1, source_target_pairs={{0,4},{4,0},{8,12},{12,8},{16,20},{20,16},{24,28},{28,24},{1,5},{5... | collective-permute-start | bytes 294920 | tf_op jit(solution)/shard_map/ppermute | solution.py:446
  18.1 0.9 %collective-permute-done.5.refs_5_ = f32[48,384]{1,0:T(8,128)S(1)} collective-permute-done((f32[48,384]{1,0:T(8,128)S(1)}, f32[48,384]{1,0:T(8,128)S(1)}, u32[]{:S(2)}, u32[]{:S(2)}) %collective-permute-start.5) | collective-permute-done | bytes 73760 | tf_op jit(solution)/shard_map/ppermute | solution.py:446
  19.0 0.0 copy-done.4
  19.0 0.7 %collective-permute-start.7 = (f32[576,128]{1,0:T(8,128)S(1)}, f32[576,128]{1,0:T(8,128)S(1)}, u32[]{:S(2)}, u32[]{:S(2)}) collective-permute-start(f32[576,128]{1,0:T(8,128)S(1)} %bitcast.19), channel_id=1, source_target_pairs={{0,4},{4,5},{5,1},{1,0},{8,12},{12,13},{13,9},{9,8},{16,20},{20,21... | collective-permute-start | bytes 884744 | tf_op jit(solution)/shard_map/ppermute | solution.py:493
  19.7 0.9 %collective-permute-done.6.refs_6_ = f32[48,384]{1,0:T(8,128)S(1)} collective-permute-done((f32[48,384]{1,0:T(8,128)S(1)}, f32[48,384]{1,0:T(8,128)S(1)}, u32[]{:S(2)}, u32[]{:S(2)}) %collective-permute-start.6) | collective-permute-done | bytes 73760 | tf_op jit(solution)/shard_map/ppermute | solution.py:446
  20.6 0.0 collective-permute-done.got_ref
  20.6 0.0 copy-done
  20.6 0.0 copy-done.1
  20.6 0.0 copy-done.2
  20.6 0.0 copy-done.3
  20.6 1.1 %products.1 = (f32[384,384]{1,0:T(8,128)S(1)}, f32[384,384]{1,0:T(8,128)S(1)}, f32[384,384]{1,0:T(8,128)S(1)}, f32[384,256]{1,0:T(8,128)S(1)}, f32[384,256]{1,0:...) custom-call(f32[576,128]{1,0:T(8,128)S(1)} %bitcast.13, ...), custom_call_target="tpu_custom_call" | custom-call | flops 679477248 | bytes 2359296 | tf_op jit(solution)/shard_map/products/pallas_call | solution.py:477
  21.7 0.9 %collective-permute-done.8.corner_ref = f32[192,128]{1,0:T(8,128)S(1)} collective-permute-done((f32[192,128]{1,0:T(8,128)S(1)}, f32[192,128]{1,0:T(8,128)S(1)}, u32[]{:S(2)}, u32[]{:S(2)}) %collective-permute-start.8) | collective-permute-done | bytes 98336 | tf_op jit(solution)/shard_map/ppermute | solution.py:446
  22.7 3.4 %begin.1 = (f32[384,384]{1,0:T(8,128)S(1)}, f32[384,384]{1,0:T(8,128)S(1)}) custom-call(f32[576,128]{1,0:T(8,128)S(1)} %get-tuple-element.54.own_ref, f32[192,128]{1,0:T(8,128)S(1)} %collective-permute-done.8.corner_ref, f32[384,384]{1,0:T(8,128)S(1)} %get-tuple-element.57.product_ref, f32[384,384]{1,0:T(8,128)S(1)} %get-tuple-element.50.basis_ref), custom_call_target="tpu_custom_call" | custom-call | flops 2378170368 | bytes 2359296 | tf_op jit(solution)/shard_map/begin/pallas_call | solution.py:494
  26.0 0.0 collective-permute-done.7.other_left_ref
  26.1 0.0 copy-done.5
  26.1 0.0 copy-done.6
  26.1 3.2 %update.1 = (f32[576,128]{1,0:T(8,128)}, f32[576,128]{1,0:T(8,128)}, f32[4,48,384]{2,1,0:T(8,128)S(1)}, f32[384,256]{1,0:T(8,128)S(1)}, f32[384,384]{1,0:T(8,128)S(1)}) custom-call(f32[384,256]{1,0:T(8,128)S(1)} %get-tuple-element.49.inner_ref, f32[384,384]{1,0:T(8,128)S(1)} %get-tuple-element.50.basis_ref, f32[576,128]{1,0:T(8,128)S(1)} %get-tuple-element.51.left_ref, ...), custom_call_target="tpu_custom_call" | custom-call | flops 1698693120 | bytes 2359296 | tf_op jit(solution)/shard_map/update/pallas_call | solution.py:498
  29.3 0.3 collective-permute-start.9
  29.7 6.0 %end.1 = (f32[384,384]{1,0:T(8,128)S(1)}, f32[384,384]{1,0:T(8,128)S(1)}, f32[576,128]{1,0:T(8,128)S(1)}, f32[4,48,384]{2,1,0:T(8,128)S(1)}) custom-call(f32[384,384]{1,0:T(8,128)S(1)} %get-tuple-element.61.start_ref, f32[384,256]{1,0:T(8,128)S(1)} %get-tuple-element.62.outer_ref, f32[384,256]{1,0:T(8,128)S(1)} %get-tuple-element.52.right_ref), custom_call_target="tpu_custom_call" | custom-call | flops 3057647616 | bytes 2359296 | tf_op jit(solution)/shard_map/end/pallas_call | solution.py:505
  35.7 1.8 %collective-permute-start.13 = (f32[576,128]{1,0:T(8,128)S(1)}, f32[576,128]{1,0:T(8,128)S(1)}, u32[]{:S(2)}, u32[]{:S(2)}) collective-permute-start(f32[576,128]{1,0:T(8,128)S(1)} %get-tuple-element.64), channel_id=1, source_target_pairs={{0,4},{4,0},{8,12},{12,8},{16,20},{20,16},{24,28},{28,24},{1,5},{5... | collective-permute-start | bytes 884744 | tf_op jit(solution)/shard_map/ppermute | solution.py:446
  37.4 0.0 collective-permute-done.9.theirs_ref
  37.5 3.2 %collective-permute-start.10 = (f32[48,384]{1,0:T(8,128)S(1)}, f32[48,384]{1,0:T(8,128)S(1)}, u32[]{:S(2)}, u32[]{:S(2)}) collective-permute-start(f32[48,384]{1,0:T(8,128)S(1)} %get-tuple-element.68), channel_id=1, source_target_pairs={{0,16},{4,20},{8,24},{12,28},{16,0},{20,4},{24,8},{28,12},{1,17},{... | collective-permute-start | bytes 221192 | tf_op jit(solution)/shard_map/ppermute | solution.py:443
  40.7 1.8 %collective-permute-start.11 = (f32[48,384]{1,0:T(8,128)S(1)}, f32[48,384]{1,0:T(8,128)S(1)}, u32[]{:S(2)}, u32[]{:S(2)}) collective-permute-start(f32[48,384]{1,0:T(8,128)S(1)} %get-tuple-element.69), channel_id=1, source_target_pairs={{0,24},{4,28},{8,16},{12,20},{16,8},{20,12},{24,0},{28,4},{1,25},{... | collective-permute-start | bytes 221192 | tf_op jit(solution)/shard_map/ppermute | solution.py:443
  42.5 0.5 %collective-permute-start.12 = (f32[48,384]{1,0:T(8,128)S(1)}, f32[48,384]{1,0:T(8,128)S(1)}, u32[]{:S(2)}, u32[]{:S(2)}) collective-permute-start(f32[48,384]{1,0:T(8,128)S(1)} %get-tuple-element.70), channel_id=1, source_target_pairs={{0,8},{4,12},{8,0},{12,4},{16,24},{20,28},{24,16},{28,20},{1,9},{5... | collective-permute-start | bytes 221192 | tf_op jit(solution)/shard_map/ppermute | solution.py:443
  42.9 2.0 %rest.1 = (f32[576,128]{1,0:T(8,128)S(1)}, f32[576,128]{1,0:T(8,128)}, f32[576,128]{1,0:T(8,128)}) custom-call(f32[384,384]{1,0:T(8,128)S(1)} %get-tuple-element.73.x_ref, f32[384,384]{1,0:T(8,128)S(1)} %get-tuple-element.74.poly_ref, f32[384,384]{1,0:T(8,128)S(1)} %get-tuple-element.75.grad_ref, f32[384,384]{1,0:T(8,128)S(1)} %get-tuple-element.76.new_stat_ref, ...), custom_call_target="tpu_custom_call" | custom-call | flops 509607936 | bytes 2359296 | tf_op jit(solution)/shard_map/rest/pallas_call | solution.py:514
  45.0 0.0 collective-permute-done.13.back_ref
  45.0 0.8 %bases.1 = (f32[576,128]{1,0:T(8,128)}, f32[576,128]{1,0:T(8,128)}) custom-call(f32[576,128]{1,0:T(8,128)S(1)} %get-tuple-element.80.keep_ref, f32[576,128]{1,0:T(8,128)S(1)} %collective-permute-done.13.back_ref), custom_call_target="tpu_custom_call" | custom-call | flops 33973864 | bytes 2359296 | tf_op jit(solution)/shard_map/bases/pallas_call | solution.py:536
  45.8 0.0 collective-permute-done.10.refs_1_
  45.8 1.2 %collective-permute-done.11.refs_2_ = f32[48,384]{1,0:T(8,128)S(1)} collective-permute-done((f32[48,384]{1,0:T(8,128)S(1)}, f32[48,384]{1,0:T(8,128)S(1)}, u32[]{:S(2)}, u32[]{:S(2)}) %collective-permute-start.11) | collective-permute-done | bytes 73760 | tf_op jit(solution)/shard_map/ppermute | solution.py:443
  47.0 0.6 %collective-permute-done.12.refs_3_ = f32[48,384]{1,0:T(8,128)S(1)} collective-permute-done((f32[48,384]{1,0:T(8,128)S(1)}, f32[48,384]{1,0:T(8,128)S(1)}, u32[]{:S(2)}, u32[]{:S(2)}) %collective-permute-start.12) | collective-permute-done | bytes 73760 | tf_op jit(solution)/shard_map/ppermute | solution.py:443
  47.6 0.7 %rows.1 = f32[4,48,384]{2,1,0:T(8,128)} custom-call(f32[48,384]{1,0:T(8,128)S(1)} %get-tuple-element.67.refs_0_, f32[48,384]{1,0:T(8,128)S(1)} %collective-permute-done.10.refs_1_, f32[48,384]{1,0:T(8,128)S(1)} %collective-permute-done.11.refs_2_, f32[48,384]{1,0:T(8,128)S(1)} %collective-permute-done.12.refs_3_), custom_call_target="tpu_custom_call" | custom-call | flops 33973864 | bytes 2359296 | tf_op jit(solution)/shard_map/rows/pallas_call | solution.py:522
  (3 shorter events, 0.0 us)
Async XLA Ops:
  0.6 18.4 %copy-start.4 = (f32[1,73728]{1,0:T(1,128)S(1)}, f32[1,73728]{1,0:T(1,128)}, u32[]{:S(2)}) copy-start(f32[1,73728]{1,0:T(1,128)} %param.12) | copy-start | bytes 884740
  0.6 19.9 %copy-start = (f32[1,73728]{1,0:T(1,128)S(1)}, f32[1,73728]{1,0:T(1,128)}, u32[]{:S(2)}) copy-start(f32[1,73728]{1,0:T(1,128)} %param.10) | copy-start | bytes 884740
  0.7 19.9 %copy-start.1 = (f32[1,73728]{1,0:T(1,128)S(1)}, f32[1,73728]{1,0:T(1,128)}, u32[]{:S(2)}) copy-start(f32[1,73728]{1,0:T(1,128)} %param.11) | copy-start | bytes 884740
  0.7 19.9 %copy-start.2 = (f32[1,73728]{1,0:T(1,128)S(1)}, f32[1,73728]{1,0:T(1,128)}, u32[]{:S(2)}) copy-start(f32[1,73728]{1,0:T(1,128)} %param.13) | copy-start | bytes 884740
  0.7 19.9 %copy-start.3 = (f32[4,48,384]{2,1,0:T(8,128)S(1)}, f32[4,48,384]{2,1,0:T(8,128)}, u32[]{:S(2)}) copy-start(f32[4,48,384]{2,1,0:T(8,128)} %refs_0_.1) | copy-start | bytes 884740
  2.0 18.6 %collective-permute-start = (f32[720,128]{1,0:T(8,128)S(1)}, f32[720,128]{1,0:T(8,128)S(1)}, u32[]{:S(2)}, u32[]{:S(2)}) collective-permute-start(f32[720,128]{1,0:T(8,128)S(1)} %get-tuple-element.45), channel_id=1, source_target_pairs={{0,4},{4,0},{8,12},{12,8},{16,20},{20,16},{24,28},{28,24},{1,5},{5... | collective-permute-start | bytes 1105928 | tf_op jit(solution)/shard_map/ppermute | solution.py:446
  5.0 7.4 %collective-permute-start.1 = (f32[48,384]{1,0:T(8,128)S(1)}, f32[48,384]{1,0:T(8,128)S(1)}, u32[]{:S(2)}, u32[]{:S(2)}) collective-permute-start(f32[48,384]{1,0:T(8,128)S(1)} %get-tuple-element.46), channel_id=1, source_target_pairs={{0,16},{4,20},{8,24},{12,28},{16,0},{20,4},{24,8},{28,12},{1,17},{... | collective-permute-start | bytes 221192 | tf_op jit(solution)/shard_map/ppermute | solution.py:443
  7.6 6.3 %collective-permute-start.2 = (f32[48,384]{1,0:T(8,128)S(1)}, f32[48,384]{1,0:T(8,128)S(1)}, u32[]{:S(2)}, u32[]{:S(2)}) collective-permute-start(f32[48,384]{1,0:T(8,128)S(1)} %get-tuple-element.47), channel_id=1, source_target_pairs={{0,24},{4,28},{8,16},{12,20},{16,8},{20,12},{24,0},{28,4},{1,25},{... | collective-permute-start | bytes 221192 | tf_op jit(solution)/shard_map/ppermute | solution.py:443
  9.0 5.5 %collective-permute-start.3 = (f32[48,384]{1,0:T(8,128)S(1)}, f32[48,384]{1,0:T(8,128)S(1)}, u32[]{:S(2)}, u32[]{:S(2)}) collective-permute-start(f32[48,384]{1,0:T(8,128)S(1)} %get-tuple-element.48), channel_id=1, source_target_pairs={{0,8},{4,12},{8,0},{12,4},{16,24},{20,28},{24,16},{28,20},{1,9},{5... | collective-permute-start | bytes 221192 | tf_op jit(solution)/shard_map/ppermute | solution.py:443
  12.4 4.6 %collective-permute-start.4 = (f32[48,384]{1,0:T(8,128)S(1)}, f32[48,384]{1,0:T(8,128)S(1)}, u32[]{:S(2)}, u32[]{:S(2)}) collective-permute-start(f32[48,384]{1,0:T(8,128)S(1)} %collective-permute-done.1.refs_1_), channel_id=1, source_target_pairs={{0,4},{4,0},{8,12},{12,8},{16,20},{20,16},{24,28},{28,24},{1,5},{5... | collective-permute-start | bytes 221192 | tf_op jit(solution)/shard_map/ppermute | solution.py:446
  13.9 5.1 %collective-permute-start.5 = (f32[48,384]{1,0:T(8,128)S(1)}, f32[48,384]{1,0:T(8,128)S(1)}, u32[]{:S(2)}, u32[]{:S(2)}) collective-permute-start(f32[48,384]{1,0:T(8,128)S(1)} %collective-permute-done.2.refs_2_), channel_id=1, source_target_pairs={{0,4},{4,0},{8,12},{12,8},{16,20},{20,16},{24,28},{28,24},{1,5},{5... | collective-permute-start | bytes 221192 | tf_op jit(solution)/shard_map/ppermute | solution.py:446
  14.5 6.1 %collective-permute-start.6 = (f32[48,384]{1,0:T(8,128)S(1)}, f32[48,384]{1,0:T(8,128)S(1)}, u32[]{:S(2)}, u32[]{:S(2)}) collective-permute-start(f32[48,384]{1,0:T(8,128)S(1)} %collective-permute-done.3.refs_3_), channel_id=1, source_target_pairs={{0,4},{4,0},{8,12},{12,8},{16,20},{20,16},{24,28},{28,24},{1,5},{5... | collective-permute-start | bytes 221192 | tf_op jit(solution)/shard_map/ppermute | solution.py:446
  17.0 5.7 %collective-permute-start.8 = (f32[192,128]{1,0:T(8,128)S(1)}, f32[192,128]{1,0:T(8,128)S(1)}, u32[]{:S(2)}, u32[]{:S(2)}) collective-permute-start(f32[192,128]{1,0:T(8,128)S(1)} %get-tuple-element.56), channel_id=1, source_target_pairs={{0,4},{4,0},{8,12},{12,8},{16,20},{20,16},{24,28},{28,24},{1,5},{5... | collective-permute-start | bytes 294920 | tf_op jit(solution)/shard_map/ppermute | solution.py:446
  19.0 7.0 %collective-permute-start.7 = (f32[576,128]{1,0:T(8,128)S(1)}, f32[576,128]{1,0:T(8,128)S(1)}, u32[]{:S(2)}, u32[]{:S(2)}) collective-permute-start(f32[576,128]{1,0:T(8,128)S(1)} %bitcast.19), channel_id=1, source_target_pairs={{0,4},{4,5},{5,1},{1,0},{8,12},{12,13},{13,9},{9,8},{16,20},{20,21... | collective-permute-start | bytes 884744 | tf_op jit(solution)/shard_map/ppermute | solution.py:493
  22.7 3.4 %copy-start.5 = (f32[1,73728]{1,0:T(1,128)S(1)}, f32[1,73728]{1,0:T(1,128)}, u32[]{:S(2)}) copy-start(f32[1,73728]{1,0:T(1,128)} %param.8) | copy-start | bytes 884740
  22.7 3.4 %copy-start.6 = (f32[1,73728]{1,0:T(1,128)S(1)}, f32[1,73728]{1,0:T(1,128)}, u32[]{:S(2)}) copy-start(f32[1,73728]{1,0:T(1,128)} %param.9) | copy-start | bytes 884740
  29.3 8.1 %collective-permute-start.9 = (f32[4,48,384]{2,1,0:T(8,128)S(1)}, f32[4,48,384]{2,1,0:T(8,128)S(1)}, u32[]{:S(2)}, u32[]{:S(2)}) collective-permute-start(f32[4,48,384]{2,1,0:T(8,128)S(1)} %get-tuple-element.60), channel_id=1, source_target_pairs={{0,4},{4,0},{8,12},{12,8},{16,20},{20,16},{24,28},{28,24},{1,5},{5... | collective-permute-start | bytes 884744 | tf_op jit(solution)/shard_map/ppermute | solution.py:446
  35.7 9.3 %collective-permute-start.13 = (f32[576,128]{1,0:T(8,128)S(1)}, f32[576,128]{1,0:T(8,128)S(1)}, u32[]{:S(2)}, u32[]{:S(2)}) collective-permute-start(f32[576,128]{1,0:T(8,128)S(1)} %get-tuple-element.64), channel_id=1, source_target_pairs={{0,4},{4,0},{8,12},{12,8},{16,20},{20,16},{24,28},{28,24},{1,5},{5... | collective-permute-start | bytes 884744 | tf_op jit(solution)/shard_map/ppermute | solution.py:446
  37.5 8.3 %collective-permute-start.10 = (f32[48,384]{1,0:T(8,128)S(1)}, f32[48,384]{1,0:T(8,128)S(1)}, u32[]{:S(2)}, u32[]{:S(2)}) collective-permute-start(f32[48,384]{1,0:T(8,128)S(1)} %get-tuple-element.68), channel_id=1, source_target_pairs={{0,16},{4,20},{8,24},{12,28},{16,0},{20,4},{24,8},{28,12},{1,17},{... | collective-permute-start | bytes 221192 | tf_op jit(solution)/shard_map/ppermute | solution.py:443
  40.7 6.3 %collective-permute-start.11 = (f32[48,384]{1,0:T(8,128)S(1)}, f32[48,384]{1,0:T(8,128)S(1)}, u32[]{:S(2)}, u32[]{:S(2)}) collective-permute-start(f32[48,384]{1,0:T(8,128)S(1)} %get-tuple-element.69), channel_id=1, source_target_pairs={{0,24},{4,28},{8,16},{12,20},{16,8},{20,12},{24,0},{28,4},{1,25},{... | collective-permute-start | bytes 221192 | tf_op jit(solution)/shard_map/ppermute | solution.py:443
  42.5 5.1 %collective-permute-start.12 = (f32[48,384]{1,0:T(8,128)S(1)}, f32[48,384]{1,0:T(8,128)S(1)}, u32[]{:S(2)}, u32[]{:S(2)}) collective-permute-start(f32[48,384]{1,0:T(8,128)S(1)} %get-tuple-element.70), channel_id=1, source_target_pairs={{0,8},{4,12},{8,0},{12,4},{16,24},{20,28},{24,16},{28,20},{1,9},{5... | collective-permute-start | bytes 221192 | tf_op jit(solution)/shard_map/ppermute | solution.py:443

commit v10 on v9

--- a/solution.py
+++ b/solution.py
@@ -123,15 +123,12 @@
     return lax.rem(lax.axis_index("shard") + lax.axis_index("tensor"), 2) == 0
 
 
-def pack_kernel(hops, l_stat_ref, r_stat_ref, l_basis_ref, r_basis_ref, grads_ref, *refs):
-    out_ref, small_ref, *refs = refs
+def pack_kernel(hops, l_stat_ref, r_stat_ref, l_basis_ref, r_basis_ref, grads_ref, out_ref, *refs):
     piece_refs, (corner, sems) = refs[: len(hops)], refs[len(hops) :]
     left = is_left()
     flat_rows = l_basis_ref.shape[0]
     half_rows = flat_rows // 2
-    rows = grads_ref.shape[1]
     here = lax.axis_index("shard") // 2
-
     start = pl.multiple_of(jnp.where(is_first(), 0, half_rows), 8)
 
     def copies(basis_ref, stat_ref):
@@ -150,14 +147,10 @@
         for copy in copies(l_basis_ref, l_stat_ref):
             copy.start()
 
-    more = []
-    for number, (hop, piece_ref) in enumerate(zip(hops, piece_refs)):
-        more.append(pltpu.make_async_copy(grads_ref.at[here ^ hop], piece_ref, sems.at[2 + number]))
-    if hops:
-        for k in range(grads_ref.shape[2] // LANES):
-            source = grads_ref.at[here, :, pl.ds(k * LANES, LANES)]
-            target = out_ref.at[pl.ds(flat_rows + k * rows, rows)]
-            more.append(pltpu.make_async_copy(source, target, sems.at[2 + len(hops) + k]))
+    more = [
+        pltpu.make_async_copy(grads_ref.at[here ^ hop], piece_ref, sems.at[2 + number])
+        for number, (hop, piece_ref) in enumerate(zip(hops, piece_refs))
+    ]
     for copy in more:
         copy.start()
     first, second = copies(l_basis_ref, l_stat_ref)
@@ -166,24 +159,30 @@
     a, b, c = thirds(corner)
     low = low_lanes((third, LANES))
     middle = slice(third, 2 * third)
-    small_ref[pl.ds(0, third)] = jnp.where(low, a[:third], b[:third])
-    small_ref[pl.ds(third, third)] = a[middle]
-    small_ref[pl.ds(2 * third, third)] = jnp.where(low, swap(b[middle]), swap(c[middle]))
-    small_ref[pl.ds(3 * third, 3 * third)] = corner[pl.ds(6 * third, 3 * third)]
+    out_ref[pl.ds(flat_rows, third)] = jnp.where(low, a[:third], b[:third])
+    out_ref[pl.ds(flat_rows + third, third)] = a[middle]
+    out_ref[pl.ds(flat_rows + 2 * third, third)] = jnp.where(low, swap(b[middle]), swap(c[middle]))
+    out_ref[pl.ds(flat_rows + 3 * third, 3 * third)] = corner[pl.ds(6 * third, 3 * third)]
     for copy in [second, *more]:
         copy.wait()
 
 
+def slices_kernel(hops, grads_ref, *piece_refs):
+    here = lax.axis_index("shard") // 2
+    for hop, piece_ref in zip(hops, piece_refs):
+        piece_ref[...] = grads_ref[here ^ hop]
+
+
 def corner_rows(flat_rows):
     return flat_rows // 3
 
 
-def unpack_corner(got_ref):
-    third = got_ref.shape[0] // 6
-    small = got_ref[pl.ds(0, third), :]
-    even = got_ref[pl.ds(third, third), :]
-    odd = swap(got_ref[pl.ds(2 * third, third), :])
-    a, b, c = thirds(got_ref, 3 * third, 3 * third)
+def unpack_corner(got_ref, start, count):
+    third = count // 6
+    small = got_ref[pl.ds(start, third), :]
+    even = got_ref[pl.ds(start + third, third), :]
+    odd = swap(got_ref[pl.ds(start + 2 * third, third), :])
+    a, b, c = thirds(got_ref, start + 3 * third, 3 * third)
     low = low_lanes(small.shape)
     zero = jnp.zeros_like(small)
     return [
@@ -194,7 +193,8 @@
 
 
 def statistic(first, own, got_ref, scratch):
-    corner = unpack_corner(got_ref)
+    flat_rows = got_ref.shape[0] * 3 // 4
+    corner = unpack_corner(got_ref, flat_rows, corner_rows(flat_rows))
     placed = [jnp.concatenate([jnp.where(first, 0.0, c), jnp.where(first, c, 0.0)], axis=0) for c in corner]
     known = whole_of(scratch, pick(first, own, placed), pick(first, placed, own))
     half = known.shape[0] // 2
@@ -219,19 +219,6 @@
     return CUBIC_COEFF * gram + QUINTIC_COEFF * dot_parts(gram_parts, gram_parts)
 
 
-def blocked_step(x):
-    parts = split(x)
-    gram = dot_parts(parts, parts, ((1,), (1,)))
-    gram_parts = split(gram)
-    rows = x.shape[0] // 2
-    blocks = []
-    for k in range(2):
-        block = slice(k * rows, (k + 1) * rows)
-        poly = CUBIC_COEFF * gram[block] + QUINTIC_COEFF * dot_parts([part[block] for part in gram_parts], gram_parts)
-        blocks.append(LINEAR_COEFF * x[block] + dot_parts(split(poly), parts))
-    return jnp.concatenate(blocks, axis=0)
-
-
 def iterate(x, steps):
     for _ in range(steps):
         parts = split(x)
@@ -239,31 +226,22 @@
     return x
 
 
-def products_kernel(hops, l_stat_ref, r_stat_ref, l_basis_ref, r_basis_ref, got_ref, *refs):
+def products_kernel(hops, r_basis_ref, *refs):
     left = is_left()
-    outs = refs[-9:]
-    grad_ref, product_ref, basis_ref, right_ref, inner_ref, own_ref, other_ref, copy_ref, scratch = outs
+    grad_ref, product_ref, right_ref, inner_ref, scratch = refs[-5:]
     if hops:
-        grads_ref, mine_refs, theirs_refs = refs[0], refs[1 : 1 + len(hops)], refs[1 + len(hops) : 1 + 2 * len(hops)]
+        grads_ref, swapped_ref = refs[:2]
+        mine_refs, theirs_refs = refs[2 : 2 + len(hops)], refs[2 + len(hops) : 2 + 2 * len(hops)]
         rows = grads_ref.shape[1]
         here = lax.axis_index("shard") // 2
         parity = lax.axis_index("shard") % 2
-        start = l_basis_ref.shape[0]
-        received = [got_ref[pl.ds(start + k * rows, rows), :] for k in range(grad_ref.shape[1] // LANES)]
         place_rows(grad_ref, 2 * here + parity, rows, grads_ref[here])
-        place_rows(grad_ref, 2 * here + 1 - parity, rows, jnp.concatenate(received, axis=1))
+        place_rows(grad_ref, 2 * here + 1 - parity, rows, swapped_ref[here])
         for hop, mine, theirs in zip(hops, mine_refs, theirs_refs):
             place_rows(grad_ref, 2 * (here ^ hop) + parity, rows, mine[...])
             place_rows(grad_ref, 2 * (here ^ hop) + 1 - parity, rows, theirs[...])
     else:
         grad_ref[...] = refs[0][...]
-    own = pick(left, thirds(l_basis_ref), thirds(r_basis_ref))
-    got = thirds(got_ref, 0, l_basis_ref.shape[0])
-    first = is_first()
-    basis_ref[...] = whole_of(scratch, pick(first, own, got), pick(first, got, own))
-    own_ref[...] = jnp.where(left, l_stat_ref[...], r_stat_ref[...])
-    other_ref[...] = jnp.where(left, r_stat_ref[...], l_stat_ref[...])
-    copy_ref[...] = l_basis_ref[...]
     right = half_of(scratch, thirds(r_basis_ref))
     right_ref[...] = right
     grad = grad_ref[...]
@@ -272,8 +250,19 @@
     inner_ref[...] = dot(grad, right)
 
 
-def begin_kernel(steps, own_ref, corner_ref, product_ref, basis_ref, new_stat_ref, x_ref, scratch):
-    new_stat = 0.5 * statistic(is_first(), thirds(own_ref), corner_ref, scratch) + 0.5 * product_ref[...]
+def prepare_kernel(l_stat_ref, r_stat_ref, l_basis_ref, r_basis_ref, got_ref, stat_ref, basis_ref, other_ref, copy_ref, scratch):
+    left, first = is_left(), is_first()
+    own = pick(left, thirds(l_basis_ref), thirds(r_basis_ref))
+    got = thirds(got_ref, 0, l_basis_ref.shape[0])
+    basis_ref[...] = whole_of(scratch, pick(first, own, got), pick(first, got, own))
+    other_ref[...] = jnp.where(left, r_stat_ref[...], l_stat_ref[...])
+    copy_ref[...] = l_basis_ref[...]
+    own = pick(left, thirds(l_stat_ref), thirds(r_stat_ref))
+    stat_ref[...] = 0.5 * statistic(first, own, got_ref, scratch)
+
+
+def begin_kernel(steps, stat_ref, product_ref, basis_ref, new_stat_ref, x_ref):
+    new_stat = stat_ref[...] + 0.5 * product_ref[...]
     new_stat_ref[...] = new_stat
     power = dot(new_stat, basis_ref[...])
     x_ref[...] = iterate(power * (1.0 / jnp.sqrt(jnp.sum(power * power) + NORM_EPS)), steps)
@@ -331,9 +320,7 @@
 
 
 def end_kernel(hops, steps, start_ref, outer_ref, right_ref, x_ref, poly_ref, send_ref, mine_ref, scratch):
-    x = start_ref[...]
-    for _ in range(steps - 1):
-        x = blocked_step(x)
+    x = iterate(start_ref[...], steps - 1)
     x_ref[...] = x
     rows_for(hops, outer_ref, split(right_ref[...]), mine_ref, lax.axis_index("shard") % 2)
     poly = polynomial(split(x))
@@ -448,40 +435,39 @@
     one, two, l_stat, r_stat, l_basis, r_basis = (
         x.reshape(flat) for x in (moment_one, moment_two, left_stat, right_stat, left_basis, right_basis)
     )
-    count = corner_rows(flat_rows)
-    outgoing_rows = flat_rows + (rows_here * (full // LANES) if near else 0)
-    outgoing, corner, *pieces = call(
+    outgoing, *pieces = call(
         functools.partial(pack_kernel, hops),
-        [(outgoing_rows, LANES), (count, LANES)] + [block] * len(hops),
+        [(flat_rows + corner_rows(flat_rows), LANES)] + [block] * len(hops),
         [(flat_rows // 2, LANES)],
         0.1,
         full,
         "pack",
-        copies=2 + len(hops) + full // LANES,
+        copies=2 + len(hops),
         kind=pltpu.VMEM,
         in_specs=anywhere(5),
-        out_specs=anywhere(1) + [pl.BlockSpec(memory_space=pltpu.VMEM)] + anywhere(len(hops)),
+        out_specs=[pl.BlockSpec(memory_space=pltpu.VMEM)] + anywhere(len(hops)),
     )(*(pltpu.with_memory_space_constraint(x, pltpu.HBM) for x in (l_stat, r_stat, l_basis, r_basis, grads)))
-    got = partner(outgoing)
     if near:
+        swapped = partner(grads)
         mine = [hop_by(piece, hop) for hop, piece in zip(hops, pieces)]
-        theirs = [partner(x) for x in mine]
-        rows = (grads, *mine, *theirs)
+        got = partner(outgoing)
+        pieces = call(functools.partial(slices_kernel, hops), [block] * len(hops), [], 0.1, full, "slices")(swapped)
+        theirs = [hop_by(after(piece, x), hop) for hop, piece, x in zip(hops, pieces, mine)]
+        rows = (grads, swapped, *mine, *theirs)
     else:
+        got = partner(outgoing)
         mine = exchange(grads)
         theirs = partner(mine)
         even, odd = jnp.where(parity == 0, mine, theirs), jnp.where(parity == 0, theirs, mine)
         rows = (jnp.stack([even, odd], axis=1).reshape(square),)
-        mine = [mine]
-    got_corner = partner(after(corner, theirs[0] if near else mine[0]))
-    grad, product, basis, right, inner, own, other, left = call(
-        functools.partial(products_kernel, hops),
-        [square, square, square, (full, 2 * LANES), (full, 2 * LANES), flat, flat, flat],
-        [(3, full, LANES)],
-        2,
-        full,
-        "products",
-    )(l_stat, r_stat, l_basis, r_basis, got, *rows)
+        theirs = [theirs]
+    wide = (full, 2 * LANES)
+    grad, product, right, inner = call(
+        functools.partial(products_kernel, hops), [square, square, wide, wide], [(3, full, LANES)], 2, full, "products"
+    )(r_basis, *rows)
+    stat, basis, other, left = call(
+        prepare_kernel, [square, square, flat, flat], [(3, full, LANES)], 0.1, full, "prepare"
+    )(l_stat, r_stat, l_basis, r_basis, got)
     tensors = lax.axis_size("tensor")
     place = lambda t, i: i * tensors + t
     cycle = []
@@ -490,11 +476,10 @@
             cycle += [(place(t, i), place(t, i + 1)), (place(t, i + 1), place(t + 1, i + 1))]
             cycle += [(place(t + 1, i + 1), place(t + 1, i)), (place(t + 1, i), place(t, i))]
     cycle += [(place(t, i), place(t, i ^ 1)) for t in range(tensors - tensors % 2, tensors) for i in range(size)]
-    other_left = lax.ppermute(after(l_basis, *(theirs[:2] if near else mine)), ("shard", "tensor"), cycle)
-    new_stat, x = call(functools.partial(begin_kernel, EARLY_ITERS), [square] * 2, [(3, full, LANES)], 7, full, "begin")(
-        own, got_corner, product, basis
+    other_left = lax.ppermute(after(l_basis, theirs[0]), ("shard", "tensor"), cycle)
+    new_stat, x = call(functools.partial(begin_kernel, EARLY_ITERS), [square] * 2, [], 7, full, "begin")(
+        stat, product, basis
     )
-    wide = (full, 2 * LANES)
     new_one, new_two, other_rows, outer, x = call(
         functools.partial(update_kernel, hops), [flat, flat, strips, wide, square], [(3, full, LANES)], 5, full, "update"
     )(inner, basis, left, right, other_left, one, two, x)

time: 48.5 us -> 48.5 us (level)
  starting transfers between devices: 19 us -> 23.9 us
  waiting for transfers between devices: 9.8 us -> 5.13 us
    ppermute x6 -> x9, starting transfers between devices: 9.63 us -> 16.5 us  [hop_by(): return lax.ppermute(x, 'shard', [(i, i ^ 2 * hop) for i in range(size)])]
    ppermute x7 -> x4, starting transfers between devices: 8.73 us -> 5.23 us  [partner(): return lax.ppermute(x, 'shard', pairs)]
    ppermute x6 -> x9, waiting for transfers between devices: 6.04 us -> 3.06 us  [hop_by(): return lax.ppermute(x, 'shard', [(i, i ^ 2 * hop) for i in range(size)])]
    ppermute x7 -> x4, waiting for transfers between devices: 3.75 us -> 2.07 us  [partner(): return lax.ppermute(x, 'shard', pairs)]
    ppermute x1, starting transfers between devices: 0.68 us -> 2.12 us  [local(): lax.ppermute(after(l_basis, theirs[0]), ('shard', 'tensor'), cycle)]
    pallas_call x3 -> x5, Pallas kernels: 5.8 us -> 5.91 us  [the longest x1 2.82 us: local(): call(functools.partial(begin_kernel, EARLY_ITERS), [square] * 2, [], 7, f...]
  transfers between devices with their start and end apart: 14 -> 14, of which waited for: 8 -> 5; matrix products, arithmetic and copies ran while one was open for 0% -> 0% of each run, Pallas kernels for 28% -> 30%
where the time goes in v10:
time: 48.5 us; the launch traced here: 48.3 us
  starting transfers between devices  23.9 us (49%)
  Pallas kernels  18.5 us (38%)
  waiting for transfers between devices  5.13 us (11%)
  between operations  0.78 us (2%)
    ppermute x9, starting transfers between devices, hop_by(): return lax.ppermute(x, 'shard', [(i, i ^ 2 * hop) for i in range(size)])  16.5 us
    pallas_call x1, Pallas kernels, local(): call(functools.partial(end_kernel, hops, NS_ITERS - EARLY_ITERS - 1), [sq...  5.77 us
    ppermute x4, starting transfers between devices, partner(): return lax.ppermute(x, 'shard', pairs)  5.23 us
    pallas_call x1, Pallas kernels, local(): call(functools.partial(update_kernel, hops), [flat, flat, strips, wide, s...  3.21 us
    ppermute x9, waiting for transfers between devices, hop_by(): return lax.ppermute(x, 'shard', [(i, i ^ 2 * hop) for i in range(size)])  3.06 us
    pallas_call x1, Pallas kernels, local(): call(functools.partial(begin_kernel, EARLY_ITERS), [square] * 2, [], 7, f...  2.82 us
    ppermute x1, starting transfers between devices, local(): lax.ppermute(after(l_basis, theirs[0]), ('shard', 'tensor'), cycle)  2.12 us
    ppermute x4, waiting for transfers between devices, partner(): return lax.ppermute(x, 'shard', pairs)  2.07 us
  transfers between devices with their start and end apart: 14, of which 5 were waited for; matrix products, arithmetic and copies ran while one was open for 0% of the time, Pallas kernels for 30%

profile of v10, /device:TPU:0, one launch (start us, length us, event | category | flops | bytes accessed | tf_op | source)
XLA Modules:
  0.0 48.3 jit_solution(12503887105570885610)
XLA Ops:
  0.6 3.0 %collective-permute-start = (f32[4,48,384]{2,1,0:T(8,128)}, f32[4,48,384]{2,1,0:T(8,128)S(1)}, u32[]{:S(2)}, u32[]{:S(2)}) collective-permute-start(f32[4,48,384]{2,1,0:T(8,128)} %refs_0_.1), channel_id=1, source_target_pairs={{0,4},{4,0},{8,12},{12,8},{16,20},{20,16},{24,28},{28,24},{1,5},{5... | collective-permute-start | bytes 884744 | tf_op jit(solution)/shard_map/ppermute | solution.py:433
  3.7 0.0 copy-start.3
  3.7 1.2 %pack.1 = (f32[768,128]{1,0:T(8,128)S(1)}, f32[48,384]{1,0:T(8,128)S(1)}, f32[48,384]{1,0:T(8,128)S(1)}, f32[48,384]{1,0:T(8,128)S(1)}) custom-call(f32[576,128]{1,0:T(8,128)} %bitcast.15, f32[576,128]{1,0:T(8,128)} %bitcast.17, f32[576,128]{1,0:T(8,128)} %bitcast.19, f32[576,128]{1,0:T(8,128)} %bitcast.12, f32[4,48,384]{2,1,0:T(8,128)} %refs_0_.1), custom_call_target="tpu_custom_call" | custom-call | flops 33973864 | bytes 2359296 | tf_op jit(solution)/shard_map/pack/pallas_call | solution.py:438
  4.9 0.0 copy-start
  4.9 0.1 collective-permute-start.7
  5.0 3.1 %collective-permute-start.1 = (f32[48,384]{1,0:T(8,128)S(1)}, f32[48,384]{1,0:T(8,128)S(1)}, u32[]{:S(2)}, u32[]{:S(2)}) collective-permute-start(f32[48,384]{1,0:T(8,128)S(1)} %get-tuple-element.49), channel_id=1, source_target_pairs={{0,16},{4,20},{8,24},{12,28},{16,0},{20,4},{24,8},{28,12},{1,17},{... | collective-permute-start | bytes 221192 | tf_op jit(solution)/shard_map/ppermute | solution.py:430
  8.1 1.3 %collective-permute-start.2 = (f32[48,384]{1,0:T(8,128)S(1)}, f32[48,384]{1,0:T(8,128)S(1)}, u32[]{:S(2)}, u32[]{:S(2)}) collective-permute-start(f32[48,384]{1,0:T(8,128)S(1)} %get-tuple-element.50), channel_id=1, source_target_pairs={{0,24},{4,28},{8,16},{12,20},{16,8},{20,12},{24,0},{28,4},{1,25},{... | collective-permute-start | bytes 221192 | tf_op jit(solution)/shard_map/ppermute | solution.py:430
  9.4 0.2 collective-permute-start.3
  9.6 2.1 %collective-permute-done.grads_ref.refs_1_ = f32[4,48,384]{2,1,0:T(8,128)S(1)} collective-permute-done((f32[4,48,384]{2,1,0:T(8,128)}, f32[4,48,384]{2,1,0:T(8,128)S(1)}, u32[]{:S(2)}, u32[]{:S(2)}) %collective-permute-start) | collective-permute-done | bytes 294944 | tf_op jit(solution)/shard_map/ppermute | solution.py:433
  11.7 0.0 collective-permute-done.1.refs_2_
  11.7 3.2 %collective-permute-start.4 = (f32[48,384]{1,0:T(8,128)S(1)}, f32[48,384]{1,0:T(8,128)S(1)}, u32[]{:S(2)}, u32[]{:S(2)}) collective-permute-start(f32[48,384]{1,0:T(8,128)S(1)} %get-tuple-element.53), channel_id=1, source_target_pairs={{0,16},{4,20},{8,24},{12,28},{16,0},{20,4},{24,8},{28,12},{1,17},{... | collective-permute-start | bytes 221192 | tf_op jit(solution)/shard_map/ppermute | solution.py:430
  14.9 0.0 collective-permute-done.2.refs_3_
  14.9 1.8 %collective-permute-start.5 = (f32[48,384]{1,0:T(8,128)S(1)}, f32[48,384]{1,0:T(8,128)S(1)}, u32[]{:S(2)}, u32[]{:S(2)}) collective-permute-start(f32[48,384]{1,0:T(8,128)S(1)} %get-tuple-element.55), channel_id=1, source_target_pairs={{0,24},{4,28},{8,16},{12,20},{16,8},{20,12},{24,0},{28,4},{1,25},{... | collective-permute-start | bytes 221192 | tf_op jit(solution)/shard_map/ppermute | solution.py:430
  16.8 0.0 collective-permute-done.3.refs_4_
  16.8 1.8 %collective-permute-start.6 = (f32[48,384]{1,0:T(8,128)S(1)}, f32[48,384]{1,0:T(8,128)S(1)}, u32[]{:S(2)}, u32[]{:S(2)}) collective-permute-start(f32[48,384]{1,0:T(8,128)S(1)} %get-tuple-element.57), channel_id=1, source_target_pairs={{0,8},{4,12},{8,0},{12,4},{16,24},{20,28},{24,16},{28,20},{1,9},{5... | collective-permute-start | bytes 221192 | tf_op jit(solution)/shard_map/ppermute | solution.py:430
  18.5 1.1 %collective-permute-done.4.refs_5_ = f32[48,384]{1,0:T(8,128)S(1)} collective-permute-done((f32[48,384]{1,0:T(8,128)S(1)}, f32[48,384]{1,0:T(8,128)S(1)}, u32[]{:S(2)}, u32[]{:S(2)}) %collective-permute-start.4) | collective-permute-done | bytes 73760 | tf_op jit(solution)/shard_map/ppermute | solution.py:430
  19.6 0.0 copy-done.3
  19.6 2.1 %collective-permute-start.8 = (f32[576,128]{1,0:T(8,128)S(1)}, f32[576,128]{1,0:T(8,128)S(1)}, u32[]{:S(2)}, u32[]{:S(2)}) collective-permute-start(f32[576,128]{1,0:T(8,128)S(1)} %bitcast.20), channel_id=1, source_target_pairs={{0,4},{4,5},{5,1},{1,0},{8,12},{12,13},{13,9},{9,8},{16,20},{20,21... | collective-permute-start | bytes 884744 | tf_op jit(solution)/shard_map/ppermute | solution.py:479
  21.8 0.0 collective-permute-done.5.refs_6_
  21.8 0.1 collective-permute-done.6.refs_7_
  21.9 0.0 copy-done.4
  21.9 0.0 copy-done
  21.9 1.0 %products.1 = (f32[384,384]{1,0:T(8,128)S(1)}, f32[384,384]{1,0:T(8,128)S(1)}, f32[384,256]{1,0:T(8,128)S(1)}, f32[384,256]{1,0:T(8,128)S(1)}) custom-call(f32[576,128]{1,0:T(8,128)S(1)} %bitcast.13, f32[4,48,384]{2,1,0:T(8,128)S(1)} %copy-done.4, f32[4,48,384]{2,1,0:T(8,128)S(1)} %collective-permute-done.grads_ref.refs_1_, ...), custom_call_target="tpu_custom_call" | custom-call | flops 679477248 | bytes 2359296 | tf_op jit(solution)/shard_map/products/pallas_call | solution.py:465
  22.9 0.0 collective-permute-done.7.got_ref
  22.9 0.0 copy-done.1
  22.9 0.0 copy-done.2
  22.9 0.8 %prepare.1 = (f32[384,384]{1,0:T(8,128)S(1)}, f32[384,384]{1,0:T(8,128)S(1)}, f32[576,128]{1,0:T(8,128)S(1)}, f32[576,128]{1,0:T(8,128)S(1)}) custom-call(f32[576,128]{1,0:T(8,128)S(1)} %bitcast.16, f32[576,128]{1,0:T(8,128)S(1)} %bitcast.18, f32[576,128]{1,0:T(8,128)S(1)} %bitcast.21, f32[576,128]{1,0:T(8,128)S(1)} %bitcast.14, ...), custom_call_target="tpu_custom_call" | custom-call | flops 33973864 | bytes 2359296 | tf_op jit(solution)/shard_map/prepare/pallas_call | solution.py:468
  23.8 0.0 copy-start.5
  23.8 0.0 copy-start.6
  23.8 2.8 %begin.1 = (f32[384,384]{1,0:T(8,128)S(1)}, f32[384,384]{1,0:T(8,128)S(1)}) custom-call(f32[384,384]{1,0:T(8,128)S(1)} %get-tuple-element.64.stat_ref, f32[384,384]{1,0:T(8,128)S(1)} %get-tuple-element.65.product_ref, f32[384,384]{1,0:T(8,128)S(1)} %get-tuple-element.60.basis_ref), custom_call_target="tpu_custom_call" | custom-call | flops 2378170368 | bytes 2359296 | tf_op jit(solution)/shard_map/begin/pallas_call | solution.py:480
  26.6 0.0 collective-permute-done.8.other_left_ref
  26.7 0.0 copy-done.5
  26.7 0.0 copy-done.6
  26.7 3.2 %update.1 = (f32[576,128]{1,0:T(8,128)}, f32[576,128]{1,0:T(8,128)}, f32[4,48,384]{2,1,0:T(8,128)S(1)}, f32[384,256]{1,0:T(8,128)S(1)}, f32[384,384]{1,0:T(8,128)S(1)}) custom-call(f32[384,256]{1,0:T(8,128)S(1)} %get-tuple-element.58.inner_ref, f32[384,384]{1,0:T(8,128)S(1)} %get-tuple-element.60.basis_ref, f32[576,128]{1,0:T(8,128)S(1)} %get-tuple-element.61.left_ref, ...), custom_call_target="tpu_custom_call" | custom-call | flops 1698693120 | bytes 2359296 | tf_op jit(solution)/shard_map/update/pallas_call | solution.py:483
  29.9 1.8 %collective-permute-start.9 = (f32[4,48,384]{2,1,0:T(8,128)S(1)}, f32[4,48,384]{2,1,0:T(8,128)S(1)}, u32[]{:S(2)}, u32[]{:S(2)}) collective-permute-start(f32[4,48,384]{2,1,0:T(8,128)S(1)} %get-tuple-element.68), channel_id=1, source_target_pairs={{0,4},{4,0},{8,12},{12,8},{16,20},{20,16},{24,28},{28,24},{1,5},{5... | collective-permute-start | bytes 884744 | tf_op jit(solution)/shard_map/ppermute | solution.py:433
  31.7 5.8 %end.1 = (f32[384,384]{1,0:T(8,128)S(1)}, f32[384,384]{1,0:T(8,128)S(1)}, f32[576,128]{1,0:T(8,128)S(1)}, f32[4,48,384]{2,1,0:T(8,128)S(1)}) custom-call(f32[384,384]{1,0:T(8,128)S(1)} %get-tuple-element.69.start_ref, f32[384,256]{1,0:T(8,128)S(1)} %get-tuple-element.70.outer_ref, f32[384,256]{1,0:T(8,128)S(1)} %get-tuple-element.62.right_ref), custom_call_target="tpu_custom_call" | custom-call | flops 3057647616 | bytes 2359296 | tf_op jit(solution)/shard_map/end/pallas_call | solution.py:490
  37.5 0.3 collective-permute-start.13
  37.8 0.0 collective-permute-done.9.theirs_ref
  37.8 3.1 %collective-permute-start.10 = (f32[48,384]{1,0:T(8,128)S(1)}, f32[48,384]{1,0:T(8,128)S(1)}, u32[]{:S(2)}, u32[]{:S(2)}) collective-permute-start(f32[48,384]{1,0:T(8,128)S(1)} %get-tuple-element.76), channel_id=1, source_target_pairs={{0,16},{4,20},{8,24},{12,28},{16,0},{20,4},{24,8},{28,12},{1,17},{... | collective-permute-start | bytes 221192 | tf_op jit(solution)/shard_map/ppermute | solution.py:430
  40.9 1.5 %collective-permute-start.11 = (f32[48,384]{1,0:T(8,128)S(1)}, f32[48,384]{1,0:T(8,128)S(1)}, u32[]{:S(2)}, u32[]{:S(2)}) collective-permute-start(f32[48,384]{1,0:T(8,128)S(1)} %get-tuple-element.77), channel_id=1, source_target_pairs={{0,24},{4,28},{8,16},{12,20},{16,8},{20,12},{24,0},{28,4},{1,25},{... | collective-permute-start | bytes 221192 | tf_op jit(solution)/shard_map/ppermute | solution.py:430
  42.4 0.5 %collective-permute-start.12 = (f32[48,384]{1,0:T(8,128)S(1)}, f32[48,384]{1,0:T(8,128)S(1)}, u32[]{:S(2)}, u32[]{:S(2)}) collective-permute-start(f32[48,384]{1,0:T(8,128)S(1)} %get-tuple-element.78), channel_id=1, source_target_pairs={{0,8},{4,12},{8,0},{12,4},{16,24},{20,28},{24,16},{28,20},{1,9},{5... | collective-permute-start | bytes 221192 | tf_op jit(solution)/shard_map/ppermute | solution.py:430
  42.9 2.0 %rest.1 = (f32[576,128]{1,0:T(8,128)S(1)}, f32[576,128]{1,0:T(8,128)}, f32[576,128]{1,0:T(8,128)}) custom-call(f32[384,384]{1,0:T(8,128)S(1)} %get-tuple-element.81.x_ref, f32[384,384]{1,0:T(8,128)S(1)} %get-tuple-element.82.poly_ref, f32[384,384]{1,0:T(8,128)S(1)} %get-tuple-element.83.grad_ref, f32[384,384]{1,0:T(8,128)S(1)} %get-tuple-element.84.new_stat_ref, ...), custom_call_target="tpu_custom_call" | custom-call | flops 509607936 | bytes 2359296 | tf_op jit(solution)/shard_map/rest/pallas_call | solution.py:499
  44.9 0.0 collective-permute-done.13.back_ref
  44.9 0.8 %bases.1 = (f32[576,128]{1,0:T(8,128)}, f32[576,128]{1,0:T(8,128)}) custom-call(f32[576,128]{1,0:T(8,128)S(1)} %get-tuple-element.88.keep_ref, f32[576,128]{1,0:T(8,128)S(1)} %collective-permute-done.13.back_ref), custom_call_target="tpu_custom_call" | custom-call | flops 33973864 | bytes 2359296 | tf_op jit(solution)/shard_map/bases/pallas_call | solution.py:521
  45.8 0.0 collective-permute-done.10.refs_1_
  45.8 1.5 %collective-permute-done.11.refs_2_ = f32[48,384]{1,0:T(8,128)S(1)} collective-permute-done((f32[48,384]{1,0:T(8,128)S(1)}, f32[48,384]{1,0:T(8,128)S(1)}, u32[]{:S(2)}, u32[]{:S(2)}) %collective-permute-start.11) | collective-permute-done | bytes 73760 | tf_op jit(solution)/shard_map/ppermute | solution.py:430
  47.2 0.3 collective-permute-done.12.refs_3_
  47.6 0.7 %rows.1 = f32[4,48,384]{2,1,0:T(8,128)} custom-call(f32[48,384]{1,0:T(8,128)S(1)} %get-tuple-element.75.refs_0_, f32[48,384]{1,0:T(8,128)S(1)} %collective-permute-done.10.refs_1_, f32[48,384]{1,0:T(8,128)S(1)} %collective-permute-done.11.refs_2_, f32[48,384]{1,0:T(8,128)S(1)} %collective-permute-done.12.refs_3_), custom_call_target="tpu_custom_call" | custom-call | flops 33973864 | bytes 2359296 | tf_op jit(solution)/shard_map/rows/pallas_call | solution.py:507
  (5 shorter events, 0.1 us)
Async XLA Ops:
  0.6 11.1 %collective-permute-start = (f32[4,48,384]{2,1,0:T(8,128)}, f32[4,48,384]{2,1,0:T(8,128)S(1)}, u32[]{:S(2)}, u32[]{:S(2)}) collective-permute-start(f32[4,48,384]{2,1,0:T(8,128)} %refs_0_.1), channel_id=1, source_target_pairs={{0,4},{4,0},{8,12},{12,8},{16,20},{20,16},{24,28},{28,24},{1,5},{5... | collective-permute-start | bytes 884744 | tf_op jit(solution)/shard_map/ppermute | solution.py:433
  3.7 16.0 %copy-start.3 = (f32[1,73728]{1,0:T(1,128)S(1)}, f32[1,73728]{1,0:T(1,128)}, u32[]{:S(2)}) copy-start(f32[1,73728]{1,0:T(1,128)} %param.12) | copy-start | bytes 884740
  3.7 18.2 %copy-start.4 = (f32[4,48,384]{2,1,0:T(8,128)S(1)}, f32[4,48,384]{2,1,0:T(8,128)}, u32[]{:S(2)}) copy-start(f32[4,48,384]{2,1,0:T(8,128)} %refs_0_.1) | copy-start | bytes 884740
  4.9 17.0 %copy-start = (f32[1,73728]{1,0:T(1,128)S(1)}, f32[1,73728]{1,0:T(1,128)}, u32[]{:S(2)}) copy-start(f32[1,73728]{1,0:T(1,128)} %param.13) | copy-start | bytes 884740
  4.9 18.0 %collective-permute-start.7 = (f32[768,128]{1,0:T(8,128)S(1)}, f32[768,128]{1,0:T(8,128)S(1)}, u32[]{:S(2)}, u32[]{:S(2)}) collective-permute-start(f32[768,128]{1,0:T(8,128)S(1)} %get-tuple-element.59), channel_id=1, source_target_pairs={{0,4},{4,0},{8,12},{12,8},{16,20},{20,16},{24,28},{28,24},{1,5},{5... | collective-permute-start | bytes 1179656 | tf_op jit(solution)/shard_map/ppermute | solution.py:433
  5.0 6.7 %collective-permute-start.1 = (f32[48,384]{1,0:T(8,128)S(1)}, f32[48,384]{1,0:T(8,128)S(1)}, u32[]{:S(2)}, u32[]{:S(2)}) collective-permute-start(f32[48,384]{1,0:T(8,128)S(1)} %get-tuple-element.49), channel_id=1, source_target_pairs={{0,16},{4,20},{8,24},{12,28},{16,0},{20,4},{24,8},{28,12},{1,17},{... | collective-permute-start | bytes 221192 | tf_op jit(solution)/shard_map/ppermute | solution.py:430
  8.1 6.9 %collective-permute-start.2 = (f32[48,384]{1,0:T(8,128)S(1)}, f32[48,384]{1,0:T(8,128)S(1)}, u32[]{:S(2)}, u32[]{:S(2)}) collective-permute-start(f32[48,384]{1,0:T(8,128)S(1)} %get-tuple-element.50), channel_id=1, source_target_pairs={{0,24},{4,28},{8,16},{12,20},{16,8},{20,12},{24,0},{28,4},{1,25},{... | collective-permute-start | bytes 221192 | tf_op jit(solution)/shard_map/ppermute | solution.py:430
  9.4 7.3 %collective-permute-start.3 = (f32[48,384]{1,0:T(8,128)S(1)}, f32[48,384]{1,0:T(8,128)S(1)}, u32[]{:S(2)}, u32[]{:S(2)}) collective-permute-start(f32[48,384]{1,0:T(8,128)S(1)} %get-tuple-element.51), channel_id=1, source_target_pairs={{0,8},{4,12},{8,0},{12,4},{16,24},{20,28},{24,16},{28,20},{1,9},{5... | collective-permute-start | bytes 221192 | tf_op jit(solution)/shard_map/ppermute | solution.py:430
  11.7 7.9 %collective-permute-start.4 = (f32[48,384]{1,0:T(8,128)S(1)}, f32[48,384]{1,0:T(8,128)S(1)}, u32[]{:S(2)}, u32[]{:S(2)}) collective-permute-start(f32[48,384]{1,0:T(8,128)S(1)} %get-tuple-element.53), channel_id=1, source_target_pairs={{0,16},{4,20},{8,24},{12,28},{16,0},{20,4},{24,8},{28,12},{1,17},{... | collective-permute-start | bytes 221192 | tf_op jit(solution)/shard_map/ppermute | solution.py:430
  14.9 6.8 %collective-permute-start.5 = (f32[48,384]{1,0:T(8,128)S(1)}, f32[48,384]{1,0:T(8,128)S(1)}, u32[]{:S(2)}, u32[]{:S(2)}) collective-permute-start(f32[48,384]{1,0:T(8,128)S(1)} %get-tuple-element.55), channel_id=1, source_target_pairs={{0,24},{4,28},{8,16},{12,20},{16,8},{20,12},{24,0},{28,4},{1,25},{... | collective-permute-start | bytes 221192 | tf_op jit(solution)/shard_map/ppermute | solution.py:430
  16.8 6.2 %copy-start.1 = (f32[1,73728]{1,0:T(1,128)S(1)}, f32[1,73728]{1,0:T(1,128)}, u32[]{:S(2)}) copy-start(f32[1,73728]{1,0:T(1,128)} %param.10) | copy-start | bytes 884740
  16.8 6.2 %copy-start.2 = (f32[1,73728]{1,0:T(1,128)S(1)}, f32[1,73728]{1,0:T(1,128)}, u32[]{:S(2)}) copy-start(f32[1,73728]{1,0:T(1,128)} %param.11) | copy-start | bytes 884740
  16.8 5.1 %collective-permute-start.6 = (f32[48,384]{1,0:T(8,128)S(1)}, f32[48,384]{1,0:T(8,128)S(1)}, u32[]{:S(2)}, u32[]{:S(2)}) collective-permute-start(f32[48,384]{1,0:T(8,128)S(1)} %get-tuple-element.57), channel_id=1, source_target_pairs={{0,8},{4,12},{8,0},{12,4},{16,24},{20,28},{24,16},{28,20},{1,9},{5... | collective-permute-start | bytes 221192 | tf_op jit(solution)/shard_map/ppermute | solution.py:430
  19.6 7.0 %collective-permute-start.8 = (f32[576,128]{1,0:T(8,128)S(1)}, f32[576,128]{1,0:T(8,128)S(1)}, u32[]{:S(2)}, u32[]{:S(2)}) collective-permute-start(f32[576,128]{1,0:T(8,128)S(1)} %bitcast.20), channel_id=1, source_target_pairs={{0,4},{4,5},{5,1},{1,0},{8,12},{12,13},{13,9},{9,8},{16,20},{20,21... | collective-permute-start | bytes 884744 | tf_op jit(solution)/shard_map/ppermute | solution.py:479
  23.8 2.9 %copy-start.5 = (f32[1,73728]{1,0:T(1,128)S(1)}, f32[1,73728]{1,0:T(1,128)}, u32[]{:S(2)}) copy-start(f32[1,73728]{1,0:T(1,128)} %param.8) | copy-start | bytes 884740
  23.8 2.9 %copy-start.6 = (f32[1,73728]{1,0:T(1,128)S(1)}, f32[1,73728]{1,0:T(1,128)}, u32[]{:S(2)}) copy-start(f32[1,73728]{1,0:T(1,128)} %param.9) | copy-start | bytes 884740
  29.9 7.9 %collective-permute-start.9 = (f32[4,48,384]{2,1,0:T(8,128)S(1)}, f32[4,48,384]{2,1,0:T(8,128)S(1)}, u32[]{:S(2)}, u32[]{:S(2)}) collective-permute-start(f32[4,48,384]{2,1,0:T(8,128)S(1)} %get-tuple-element.68), channel_id=1, source_target_pairs={{0,4},{4,0},{8,12},{12,8},{16,20},{20,16},{24,28},{28,24},{1,5},{5... | collective-permute-start | bytes 884744 | tf_op jit(solution)/shard_map/ppermute | solution.py:433
  37.5 7.5 %collective-permute-start.13 = (f32[576,128]{1,0:T(8,128)S(1)}, f32[576,128]{1,0:T(8,128)S(1)}, u32[]{:S(2)}, u32[]{:S(2)}) collective-permute-start(f32[576,128]{1,0:T(8,128)S(1)} %get-tuple-element.72), channel_id=1, source_target_pairs={{0,4},{4,0},{8,12},{12,8},{16,20},{20,16},{24,28},{28,24},{1,5},{5... | collective-permute-start | bytes 884744 | tf_op jit(solution)/shard_map/ppermute | solution.py:433
  37.8 8.0 %collective-permute-start.10 = (f32[48,384]{1,0:T(8,128)S(1)}, f32[48,384]{1,0:T(8,128)S(1)}, u32[]{:S(2)}, u32[]{:S(2)}) collective-permute-start(f32[48,384]{1,0:T(8,128)S(1)} %get-tuple-element.76), channel_id=1, source_target_pairs={{0,16},{4,20},{8,24},{12,28},{16,0},{20,4},{24,8},{28,12},{1,17},{... | collective-permute-start | bytes 221192 | tf_op jit(solution)/shard_map/ppermute | solution.py:430
  40.9 6.3 %collective-permute-start.11 = (f32[48,384]{1,0:T(8,128)S(1)}, f32[48,384]{1,0:T(8,128)S(1)}, u32[]{:S(2)}, u32[]{:S(2)}) collective-permute-start(f32[48,384]{1,0:T(8,128)S(1)} %get-tuple-element.77), channel_id=1, source_target_pairs={{0,24},{4,28},{8,16},{12,20},{16,8},{20,12},{24,0},{28,4},{1,25},{... | collective-permute-start | bytes 221192 | tf_op jit(solution)/shard_map/ppermute | solution.py:430
  42.4 5.1 %collective-permute-start.12 = (f32[48,384]{1,0:T(8,128)S(1)}, f32[48,384]{1,0:T(8,128)S(1)}, u32[]{:S(2)}, u32[]{:S(2)}) collective-permute-start(f32[48,384]{1,0:T(8,128)S(1)} %get-tuple-element.78), channel_id=1, source_target_pairs={{0,8},{4,12},{8,0},{12,4},{16,24},{20,28},{24,16},{28,20},{1,9},{5... | collective-permute-start | bytes 221192 | tf_op jit(solution)/shard_map/ppermute | solution.py:430

commit v11 on v8

--- a/solution.py
+++ b/solution.py
@@ -8,7 +8,6 @@
 from jax.sharding import PartitionSpec as P
 
 NS_ITERS = 5
-EARLY_ITERS = 1
 BETA_ONE = 0.9
 BETA_TWO = 0.95
 ADAM_EPS = 1e-08
@@ -123,40 +122,19 @@
     return lax.rem(lax.axis_index("shard") + lax.axis_index("tensor"), 2) == 0
 
 
-def first_pack_kernel(blocks, l_basis_ref, r_basis_ref, grads_ref, out_ref, sems):
-    left = is_left()
-    flat_rows = l_basis_ref.shape[0]
-    rows = grads_ref.shape[1]
-    here = lax.axis_index("shard") // 2
-    basis_copy = lambda ref: pltpu.make_async_copy(ref, out_ref.at[pl.ds(0, flat_rows)], sems.at[0])
-
-    @pl.when(left)
-    def _():
-        basis_copy(r_basis_ref).start()
-
-    @pl.when(jnp.logical_not(left))
-    def _():
-        basis_copy(l_basis_ref).start()
-
-    copies = []
-    for k in range(blocks):
-        source = grads_ref.at[here, :, pl.ds(k * LANES, LANES)]
-        target = out_ref.at[pl.ds(flat_rows + k * rows, rows)]
-        copies.append(pltpu.make_async_copy(source, target, sems.at[1 + k]))
-    for copy in copies:
-        copy.start()
-    basis_copy(l_basis_ref).wait()
-    for copy in copies:
-        copy.wait()
-
-
 def pack_kernel(hops, l_stat_ref, r_stat_ref, grads_ref, small_ref, *refs):
-    piece_refs, (corner, sems) = refs[: len(hops)], refs[len(hops) :]
+    piece_refs, (corner, sems) = refs[:-2], refs[-2:]
     left = is_left()
     half_rows = l_stat_ref.shape[0] // 2
     here = lax.axis_index("shard") // 2
     start = pl.multiple_of(jnp.where(is_first(), 0, half_rows), 8)
     stat_copy = lambda ref: pltpu.make_async_copy(ref.at[pl.ds(start, half_rows)], corner, sems.at[0])
+    copies = [
+        pltpu.make_async_copy(grads_ref.at[here ^ hop], piece_ref, sems.at[1 + number])
+        for number, (hop, piece_ref) in enumerate(zip((*hops, 0), piece_refs))
+    ]
+    for copy in copies:
+        copy.start()
 
     @pl.when(left)
     def _():
@@ -166,12 +144,6 @@
     def _():
         stat_copy(l_stat_ref).start()
 
-    copies = [
-        pltpu.make_async_copy(grads_ref.at[here ^ hop], piece_ref, sems.at[1 + number])
-        for number, (hop, piece_ref) in enumerate(zip(hops, piece_refs))
-    ]
-    for copy in copies:
-        copy.start()
     stat_copy(l_stat_ref).wait()
     third = half_rows // 9
     a, b, c = thirds(corner)
@@ -237,44 +209,33 @@
     return x
 
 
-def products_kernel(hops, l_stat_ref, r_stat_ref, l_basis_ref, r_basis_ref, got_ref, *refs):
+def products_kernel(hops, l_stat_ref, r_stat_ref, l_basis_ref, r_basis_ref, *refs):
     left = is_left()
     outs = refs[-9:]
-    grad_ref, product_ref, basis_ref, right_ref, inner_ref, own_ref, other_ref, copy_ref, scratch = outs
+    grad_ref, product_ref, right_ref, inner_ref, own_ref, other_ref, left_copy_ref, right_copy_ref, scratch = outs
     if hops:
-        grads_ref, mine_refs, theirs_refs = refs[0], refs[1 : 1 + len(hops)], refs[1 + len(hops) : 1 + 2 * len(hops)]
+        grads_ref, swapped_ref = refs[:2]
+        mine_refs, theirs_refs = refs[2 : 2 + len(hops)], refs[2 + len(hops) : 2 + 2 * len(hops)]
         rows = grads_ref.shape[1]
         here = lax.axis_index("shard") // 2
         parity = lax.axis_index("shard") % 2
-        start = l_basis_ref.shape[0]
-        received = [got_ref[pl.ds(start + k * rows, rows), :] for k in range(grad_ref.shape[1] // LANES)]
         place_rows(grad_ref, 2 * here + parity, rows, grads_ref[here])
-        place_rows(grad_ref, 2 * here + 1 - parity, rows, jnp.concatenate(received, axis=1))
+        place_rows(grad_ref, 2 * here + 1 - parity, rows, swapped_ref[...])
         for hop, mine, theirs in zip(hops, mine_refs, theirs_refs):
             place_rows(grad_ref, 2 * (here ^ hop) + parity, rows, mine[...])
             place_rows(grad_ref, 2 * (here ^ hop) + 1 - parity, rows, theirs[...])
     else:
         grad_ref[...] = refs[0][...]
-    own = pick(left, thirds(l_basis_ref), thirds(r_basis_ref))
-    got = thirds(got_ref, 0, l_basis_ref.shape[0])
-    first = is_first()
-    basis_ref[...] = whole_of(scratch, pick(first, own, got), pick(first, got, own))
     own_ref[...] = jnp.where(left, l_stat_ref[...], r_stat_ref[...])
     other_ref[...] = jnp.where(left, r_stat_ref[...], l_stat_ref[...])
-    copy_ref[...] = l_basis_ref[...]
+    left_copy_ref[...] = l_basis_ref[...]
+    right_copy_ref[...] = r_basis_ref[...]
     right = half_of(scratch, thirds(r_basis_ref))
     right_ref[...] = right
     grad = grad_ref[...]
     parts = split(jnp.where(left, grad, grad.T))
     product_ref[...] = symmetric_dot(parts, parts, ((1,), (1,)))
     inner_ref[...] = dot(grad, right)
-
-
-def begin_kernel(steps, own_ref, corner_ref, product_ref, basis_ref, new_stat_ref, x_ref, scratch):
-    new_stat = 0.5 * statistic(is_first(), thirds(own_ref), corner_ref, scratch) + 0.5 * product_ref[...]
-    new_stat_ref[...] = new_stat
-    power = dot(new_stat, basis_ref[...])
-    x_ref[...] = iterate(power * (1.0 / jnp.sqrt(jnp.sum(power * power) + NORM_EPS)), steps)
 
 
 def rows_for(hops, outer_ref, right_parts, out_ref, offset):
@@ -287,30 +248,30 @@
         out_ref[k] = partial[k * rows : (k + 1) * rows]
 
 
+def whole_basis(scratch, own_ref, got_ref):
+    first = is_first()
+    own, got = thirds(own_ref), thirds(got_ref)
+    return whole_of(scratch, pick(first, own, got), pick(first, got, own))
+
+
 def update_kernel(
     hops,
     inner_ref,
-    basis_ref,
     left_ref,
+    got_left_ref,
     right_ref,
-    other_left_ref,
     one_ref,
     two_ref,
-    start_ref,
     new_one_ref,
     new_two_ref,
     theirs_ref,
     outer_ref,
-    x_ref,
+    basis_left_ref,
     scratch,
 ):
-    left, first = is_left(), is_first()
-    own, got = thirds(left_ref), thirds(other_left_ref)
-    basis_left = jnp.where(left, basis_ref[...], whole_of(scratch, pick(first, own, got), pick(first, got, own)))
-    left_parts = split(basis_left)
-    right_parts = split(right_ref[...])
+    basis_left = whole_basis(scratch, left_ref, got_left_ref)
+    basis_left_ref[...] = basis_left
     rotated = flat_of(scratch, dot(basis_left.T, inner_ref[...]))
-    x_ref[...] = iterate(start_ref[...], 1)
     ones = thirds(one_ref)
     twos = thirds(two_ref)
     new_one = [BETA_ONE * m + (1.0 - BETA_ONE) * r for m, r in zip(ones, rotated)]
@@ -318,17 +279,38 @@
     put_thirds(new_one_ref, new_one)
     put_thirds(new_two_ref, new_two)
     direction = [m / (jnp.sqrt(v) + ADAM_EPS) for m, v in zip(new_one, new_two)]
-    outer_ref[...] = dot_parts(left_parts, split(half_of(scratch, direction)))
-    rows_for(hops, outer_ref, right_parts, theirs_ref, 1 - lax.axis_index("shard") % 2)
-
-
-def end_kernel(hops, steps, start_ref, outer_ref, right_ref, x_ref, poly_ref, send_ref, mine_ref, scratch):
-    x = iterate(start_ref[...], steps - 1)
+    outer_ref[...] = dot_parts(split(basis_left), split(half_of(scratch, direction)))
+    rows_for(hops, outer_ref, split(right_ref[...]), theirs_ref, 1 - lax.axis_index("shard") % 2)
+
+
+def refresh_kernel(
+    hops,
+    own_ref,
+    corner_ref,
+    product_ref,
+    basis_left_ref,
+    right_flat_ref,
+    got_right_ref,
+    outer_ref,
+    right_ref,
+    new_stat_ref,
+    x_ref,
+    poly_ref,
+    send_ref,
+    mine_ref,
+    scratch,
+):
+    left, first = is_left(), is_first()
+    new_stat = 0.5 * statistic(first, thirds(own_ref), corner_ref, scratch) + 0.5 * product_ref[...]
+    new_stat_ref[...] = new_stat
+    basis = jnp.where(left, basis_left_ref[...], whole_basis(scratch, right_flat_ref, got_right_ref))
+    power = dot(new_stat, basis)
+    x = iterate(power * (1.0 / jnp.sqrt(jnp.sum(power * power) + NORM_EPS)), NS_ITERS - 1)
     x_ref[...] = x
     rows_for(hops, outer_ref, split(right_ref[...]), mine_ref, lax.axis_index("shard") % 2)
     poly = polynomial(split(x))
     poly_ref[...] = poly
-    half = take_half(x, jnp.logical_not(is_first()))
+    half = take_half(x, jnp.logical_not(first))
     put_thirds(send_ref, flat_of(scratch, LINEAR_COEFF * half + dot(poly, half)))
 
 
@@ -438,54 +420,6 @@
     one, two, l_stat, r_stat, l_basis, r_basis = (
         x.reshape(flat) for x in (moment_one, moment_two, left_stat, right_stat, left_basis, right_basis)
     )
-    count = corner_rows(flat_rows)
-    outgoing_rows = flat_rows + (rows_here * (full // LANES) if near else 0)
-    in_hbm = lambda *xs: [pltpu.with_memory_space_constraint(x, pltpu.HBM) for x in xs]
-    blocks = full // LANES if near else 0
-    (outgoing,) = call(
-        functools.partial(first_pack_kernel, blocks),
-        [(outgoing_rows, LANES)],
-        [],
-        0.1,
-        full,
-        "first_pack",
-        copies=1 + blocks,
-        kind=pltpu.VMEM,
-        in_specs=anywhere(3),
-        out_specs=anywhere(1),
-    )(*in_hbm(l_basis, r_basis, grads))
-    corner, *pieces = call(
-        functools.partial(pack_kernel, hops),
-        [(count, LANES)] + [block] * len(hops),
-        [(flat_rows // 2, LANES)],
-        0.1,
-        full,
-        "pack",
-        copies=1 + len(hops),
-        kind=pltpu.VMEM,
-        in_specs=anywhere(3),
-        out_specs=[pl.BlockSpec(memory_space=pltpu.VMEM)] + anywhere(len(hops)),
-    )(*in_hbm(l_stat, r_stat, grads))
-    got = partner(outgoing)
-    if near:
-        mine = [hop_by(piece, hop) for hop, piece in zip(hops, pieces)]
-        theirs = [partner(x) for x in mine]
-        rows = (grads, *mine, *theirs)
-    else:
-        mine = exchange(grads)
-        theirs = partner(mine)
-        even, odd = jnp.where(parity == 0, mine, theirs), jnp.where(parity == 0, theirs, mine)
-        rows = (jnp.stack([even, odd], axis=1).reshape(square),)
-        mine = [mine]
-    got_corner = partner(after(corner, theirs[0] if near else mine[0]))
-    grad, product, basis, right, inner, own, other, left = call(
-        functools.partial(products_kernel, hops),
-        [square, square, square, (full, 2 * LANES), (full, 2 * LANES), flat, flat, flat],
-        [(3, full, LANES)],
-        2,
-        full,
-        "products",
-    )(l_stat, r_stat, l_basis, r_basis, got, *rows)
     tensors = lax.axis_size("tensor")
     place = lambda t, i: i * tensors + t
     cycle = []
@@ -494,26 +428,58 @@
             cycle += [(place(t, i), place(t, i + 1)), (place(t, i + 1), place(t + 1, i + 1))]
             cycle += [(place(t + 1, i + 1), place(t + 1, i)), (place(t + 1, i), place(t, i))]
     cycle += [(place(t, i), place(t, i ^ 1)) for t in range(tensors - tensors % 2, tensors) for i in range(size)]
-    other_left = lax.ppermute(after(l_basis, *(theirs[:2] if near else mine)), ("shard", "tensor"), cycle)
-    new_stat, x = call(functools.partial(begin_kernel, EARLY_ITERS), [square] * 2, [(3, full, LANES)], 7, full, "begin")(
-        own, got_corner, product, basis
-    )
+
+    got_left = partner(l_basis)
+    count = len(hops) + 1 if near else 0
+    corner, *pieces = call(
+        functools.partial(pack_kernel, hops),
+        [(corner_rows(flat_rows), LANES)] + [block] * count,
+        [(flat_rows // 2, LANES)],
+        0.1,
+        full,
+        "pack",
+        copies=1 + count,
+        kind=pltpu.VMEM,
+        in_specs=anywhere(3),
+        out_specs=[pl.BlockSpec(memory_space=pltpu.VMEM)] + anywhere(count),
+    )(*(pltpu.with_memory_space_constraint(x, pltpu.HBM) for x in (l_stat, r_stat, grads)))
+    if near:
+        mine = [hop_by(piece, hop) for hop, piece in zip(hops, pieces)]
+        swapped = partner(pieces[-1])
+        theirs = [partner(x) for x in mine]
+        rows = (grads, swapped, *mine, *theirs)
+    else:
+        mine = exchange(grads)
+        theirs = partner(mine)
+        even, odd = jnp.where(parity == 0, mine, theirs), jnp.where(parity == 0, theirs, mine)
+        rows = (jnp.stack([even, odd], axis=1).reshape(square),)
+        mine, theirs = [mine], [theirs]
+    got_right = lax.ppermute(after(r_basis, got_left, *([swapped] if near else []), *theirs), ("shard", "tensor"), cycle)
+    got_corner = partner(after(corner, got_left, theirs[0]))
     wide = (full, 2 * LANES)
-    new_one, new_two, other_rows, outer, x = call(
-        functools.partial(update_kernel, hops), [flat, flat, strips, wide, square], [(3, full, LANES)], 5, full, "update"
-    )(inner, basis, left, right, other_left, one, two, x)
+    grad, product, right, inner, own, other, left, right_flat = call(
+        functools.partial(products_kernel, hops),
+        [square, square, wide, wide, flat, flat, flat, flat],
+        [(3, full, LANES)],
+        2,
+        full,
+        "products",
+    )(l_stat, r_stat, l_basis, r_basis, *rows)
+    new_one, new_two, other_rows, outer, basis_left = call(
+        functools.partial(update_kernel, hops), [flat, flat, strips, wide, square], [(3, full, LANES)], 3, full, "update"
+    )(inner, left, got_left, right, one, two)
     if not near:
         partial = other_rows.reshape(tiles_here, 2, rows_here, full)
         other_rows = lax.dynamic_index_in_dim(partial, 1 - parity, 1, keepdims=False)
     got_rows = partner(other_rows)
-    x, poly, send, own_rows = call(
-        functools.partial(end_kernel, hops, NS_ITERS - EARLY_ITERS - 1),
-        [square, square, flat, strips],
+    new_stat, x, poly, send, own_rows = call(
+        functools.partial(refresh_kernel, hops),
+        [square, square, square, flat, strips],
         [(3, full, LANES)],
-        9,
+        16,
         full,
-        "end",
-    )(after(x, other_rows), outer, right)
+        "refresh",
+    )(after(own, other_rows), got_corner, product, basis_left, right_flat, got_right, outer, right)
     back = partner(send)
     keep, new_left, new_right = call(rest_kernel, [flat, flat, flat], [(3, full, LANES)], 1.5, full, "rest")(
         x, poly, grad, new_stat, other

time: 49.6 us -> 50.6 us (1.020)
  local copies, waits for them, and re-layouts: 0.03 us -> 1.94 us
  waiting for transfers between devices: 11.4 us -> 9.58 us
  starting transfers between devices: 17.5 us -> 18.6 us
    ppermute x7 -> x8, waiting for transfers between devices: 5.35 us -> 3.12 us  [partner(): return lax.ppermute(x, 'shard', pairs)]
    unnamed x14, local copies, waits for them, and re-layouts: 0.03 us -> 1.94 us
    pallas_call x1, Pallas kernels: 3.66 us -> 2.65 us  [local(): call(functools.partial(update_kernel, hops), [flat, flat, strips, wide, s...]
    ppermute x1, starting transfers between devices: 0.45 us -> 1.24 us  [local(): lax.ppermute(after(r_basis, got_left, *([swapped] if near else []), *thei...]
    pallas_call x5 -> x3, Pallas kernels: 12.5 us -> 13.2 us  [the longest x1 10.9 us: local(): call(functools.partial(refresh_kernel, hops), [square, square, square, fl...]
    ppermute x7 -> x8, starting transfers between devices: 8.03 us -> 8.41 us  [partner(): return lax.ppermute(x, 'shard', pairs)]
  transfers between devices with their start and end apart: 14 -> 15, of which waited for: 8 -> 7; matrix products, arithmetic and copies ran while one was open for 0% -> 0% of each run, Pallas kernels for 29% -> 37%
where the time goes in v11:
time: 50.6 us; the launch traced here: 50.4 us
  Pallas kernels  19.5 us (39%)
  starting transfers between devices  18.6 us (37%)
  waiting for transfers between devices  9.58 us (19%)
  local copies, waits for them, and re-layouts  1.94 us (4%)
  between operations  0.71 us (1%)
    pallas_call x1, Pallas kernels, local(): call(functools.partial(refresh_kernel, hops), [square, square, square, fl...  10.9 us
    ppermute x6, starting transfers between devices, hop_by(): return lax.ppermute(x, 'shard', [(i, i ^ 2 * hop) for i in range(size)])  8.97 us
    ppermute x8, starting transfers between devices, partner(): return lax.ppermute(x, 'shard', pairs)  8.41 us
    ppermute x6, waiting for transfers between devices, hop_by(): return lax.ppermute(x, 'shard', [(i, i ^ 2 * hop) for i in range(size)])  6.45 us
    ppermute x8, waiting for transfers between devices, partner(): return lax.ppermute(x, 'shard', pairs)  3.12 us
    pallas_call x1, Pallas kernels, local(): call(functools.partial(update_kernel, hops), [flat, flat, strips, wide, s...  2.65 us
    pallas_call x1, Pallas kernels, local(): call(rest_kernel, [flat, flat, flat], [(3, full, LANES)], 1.5, full, 'rest')  2.01 us
    unnamed x14, local copies, waits for them, and re-layouts  1.94 us
  transfers between devices with their start and end apart: 15, of which 7 were waited for; matrix products, arithmetic and copies ran while one was open for 0% of the time, Pallas kernels for 37%

profile of v11, /device:TPU:0, one launch (start us, length us, event | category | flops | bytes accessed | tf_op | source)
XLA Modules:
  0.0 50.4 jit_solution(1744498489994497548)
XLA Ops:
  0.6 3.0 %collective-permute-start.7 = (f32[576,128]{1,0:T(8,128)}, f32[576,128]{1,0:T(8,128)S(1)}, u32[]{:S(2)}, u32[]{:S(2)}) collective-permute-start(f32[576,128]{1,0:T(8,128)} %bitcast.16), channel_id=1, source_target_pairs={{0,4},{4,0},{8,12},{12,8},{16,20},{20,16},{24,28},{28,24},{1,5},{5... | collective-permute-start | bytes 884744 | tf_op jit(solution)/shard_map/ppermute | solution.py:418
  3.7 0.0 copy-start
  3.7 0.0 copy-start.1
  3.7 0.0 copy-start.2
  3.7 1.3 %pack.1 = (f32[192,128]{1,0:T(8,128)S(1)}, f32[48,384]{1,0:T(8,128)S(1)}, f32[48,384]{1,0:T(8,128)S(1)}, f32[48,384]{1,0:T(8,128)S(1)}, f32[48,384]{1,0:T(8,128)S(1)}) custom-call(f32[576,128]{1,0:T(8,128)} %bitcast.12, f32[576,128]{1,0:T(8,128)} %bitcast.14, f32[4,48,384]{2,1,0:T(8,128)} %refs_0_.1), custom_call_target="tpu_custom_call" | custom-call | flops 33973864 | bytes 2359296 | tf_op jit(solution)/shard_map/pack/pallas_call | solution.py:434
  4.9 2.7 %collective-permute-start.1 = (f32[48,384]{1,0:T(8,128)S(1)}, f32[48,384]{1,0:T(8,128)S(1)}, u32[]{:S(2)}, u32[]{:S(2)}) collective-permute-start(f32[48,384]{1,0:T(8,128)S(1)} %get-tuple-element.45), channel_id=1, source_target_pairs={{0,16},{4,20},{8,24},{12,28},{16,0},{20,4},{24,8},{28,12},{1,17},{... | collective-permute-start | bytes 221192 | tf_op jit(solution)/shard_map/ppermute | solution.py:415
  7.6 1.3 %collective-permute-start.2 = (f32[48,384]{1,0:T(8,128)S(1)}, f32[48,384]{1,0:T(8,128)S(1)}, u32[]{:S(2)}, u32[]{:S(2)}) collective-permute-start(f32[48,384]{1,0:T(8,128)S(1)} %get-tuple-element.46), channel_id=1, source_target_pairs={{0,24},{4,28},{8,16},{12,20},{16,8},{20,12},{24,0},{28,4},{1,25},{... | collective-permute-start | bytes 221192 | tf_op jit(solution)/shard_map/ppermute | solution.py:415
  8.9 0.2 collective-permute-start.3
  9.2 0.5 %collective-permute-start = (f32[48,384]{1,0:T(8,128)S(1)}, f32[48,384]{1,0:T(8,128)S(1)}, u32[]{:S(2)}, u32[]{:S(2)}) collective-permute-start(f32[48,384]{1,0:T(8,128)S(1)} %get-tuple-element.44), channel_id=1, source_target_pairs={{0,4},{4,0},{8,12},{12,8},{16,20},{20,16},{24,28},{28,24},{1,5},{5... | collective-permute-start | bytes 221192 | tf_op jit(solution)/shard_map/ppermute | solution.py:418
  9.7 2.7 %collective-permute-done.1.refs_2_ = f32[48,384]{1,0:T(8,128)S(1)} collective-permute-done((f32[48,384]{1,0:T(8,128)S(1)}, f32[48,384]{1,0:T(8,128)S(1)}, u32[]{:S(2)}, u32[]{:S(2)}) %collective-permute-start.1) | collective-permute-done | bytes 73760 | tf_op jit(solution)/shard_map/ppermute | solution.py:415
  12.4 0.5 collective-permute-start.4
  12.9 1.1 %collective-permute-done.2.refs_3_ = f32[48,384]{1,0:T(8,128)S(1)} collective-permute-done((f32[48,384]{1,0:T(8,128)S(1)}, f32[48,384]{1,0:T(8,128)S(1)}, u32[]{:S(2)}, u32[]{:S(2)}) %collective-permute-start.2) | collective-permute-done | bytes 73760 | tf_op jit(solution)/shard_map/ppermute | solution.py:415
  13.9 0.5 %collective-permute-start.5 = (f32[48,384]{1,0:T(8,128)S(1)}, f32[48,384]{1,0:T(8,128)S(1)}, u32[]{:S(2)}, u32[]{:S(2)}) collective-permute-start(f32[48,384]{1,0:T(8,128)S(1)} %collective-permute-done.2.refs_3_), channel_id=1, source_target_pairs={{0,4},{4,0},{8,12},{12,8},{16,20},{20,16},{24,28},{28,24},{1,5},{5... | collective-permute-start | bytes 221192 | tf_op jit(solution)/shard_map/ppermute | solution.py:418
  14.4 0.0 collective-permute-done.3.refs_4_
  14.4 1.5 %collective-permute-start.6 = (f32[48,384]{1,0:T(8,128)S(1)}, f32[48,384]{1,0:T(8,128)S(1)}, u32[]{:S(2)}, u32[]{:S(2)}) collective-permute-start(f32[48,384]{1,0:T(8,128)S(1)} %collective-permute-done.3.refs_4_), channel_id=1, source_target_pairs={{0,4},{4,0},{8,12},{12,8},{16,20},{20,16},{24,28},{28,24},{1,5},{5... | collective-permute-start | bytes 221192 | tf_op jit(solution)/shard_map/ppermute | solution.py:418
  15.9 0.0 collective-permute-done.refs_1_
  15.9 1.0 %collective-permute-done.4.refs_5_ = f32[48,384]{1,0:T(8,128)S(1)} collective-permute-done((f32[48,384]{1,0:T(8,128)S(1)}, f32[48,384]{1,0:T(8,128)S(1)}, u32[]{:S(2)}, u32[]{:S(2)}) %collective-permute-start.4) | collective-permute-done | bytes 73760 | tf_op jit(solution)/shard_map/ppermute | solution.py:418
  16.9 1.3 %collective-permute-done.5.refs_6_ = f32[48,384]{1,0:T(8,128)S(1)} collective-permute-done((f32[48,384]{1,0:T(8,128)S(1)}, f32[48,384]{1,0:T(8,128)S(1)}, u32[]{:S(2)}, u32[]{:S(2)}) %collective-permute-start.5) | collective-permute-done | bytes 73760 | tf_op jit(solution)/shard_map/ppermute | solution.py:418
  18.3 0.8 %collective-permute-done.6.refs_7_ = f32[48,384]{1,0:T(8,128)S(1)} collective-permute-done((f32[48,384]{1,0:T(8,128)S(1)}, f32[48,384]{1,0:T(8,128)S(1)}, u32[]{:S(2)}, u32[]{:S(2)}) %collective-permute-start.6) | collective-permute-done | bytes 73760 | tf_op jit(solution)/shard_map/ppermute | solution.py:418
  19.0 0.0 collective-permute-done.7.got_left_ref
  19.1 1.2 %collective-permute-start.9 = (f32[576,128]{1,0:T(8,128)}, f32[576,128]{1,0:T(8,128)S(1)}, u32[]{:S(2)}, u32[]{:S(2)}) collective-permute-start(f32[576,128]{1,0:T(8,128)} %bitcast.20), channel_id=1, source_target_pairs={{0,4},{4,5},{5,1},{1,0},{8,12},{12,13},{13,9},{9,8},{16,20},{20,21... | collective-permute-start | bytes 884744 | tf_op jit(solution)/shard_map/ppermute | solution.py:457
  20.3 0.0 collective-permute-start.8
  20.3 0.0 copy-done
  20.3 0.0 copy-done.1
  20.3 0.0 copy-done.2
  20.3 0.0 copy-start.3
  20.3 1.0 %copy-done.3 = f32[1,73728]{1,0:T(1,128)S(1)} copy-done((f32[1,73728]{1,0:T(1,128)S(1)}, f32[1,73728]{1,0:T(1,128)}, u32[]{:S(2)}) %copy-start.3) | copy-done | bytes 294936
  21.3 1.0 %copy-done.6 = f32[1,73728]{1,0:T(1,128)S(1)} copy-done((f32[1,73728]{1,0:T(1,128)S(1)}, f32[1,73728]{1,0:T(1,128)}, u32[]{:S(2)}) %copy-start.6) | copy-done | bytes 294936
  22.3 1.0 %products.1 = (f32[384,384]{1,0:T(8,128)S(1)}, f32[384,384]{1,0:T(8,128)S(1)}, f32[384,256]{1,0:T(8,128)S(1)}, f32[384,256]{1,0:T(8,128)S(1)}, f32[576,128]{1,0:...) custom-call(f32[576,128]{1,0:T(8,128)S(1)} %bitcast.13, ...), custom_call_target="tpu_custom_call" | custom-call | flops 679477248 | bytes 2359296 | tf_op jit(solution)/shard_map/products/pallas_call | solution.py:460
  23.3 0.0 copy-done.4
  23.3 0.0 copy-done.5
  23.3 2.6 %update.1 = (f32[576,128]{1,0:T(8,128)}, f32[576,128]{1,0:T(8,128)}, f32[4,48,384]{2,1,0:T(8,128)S(1)}, f32[384,256]{1,0:T(8,128)S(1)}, f32[384,384]{1,0:T(8,128)S(1)}) custom-call(f32[384,256]{1,0:T(8,128)S(1)} %get-tuple-element.49.inner_ref, f32[576,128]{1,0:T(8,128)S(1)} %get-tuple-element.50.left_ref, ...), custom_call_target="tpu_custom_call" | custom-call | flops 1019215872 | bytes 2359296 | tf_op jit(solution)/shard_map/update/pallas_call | solution.py:468
  26.0 2.0 %collective-permute-start.10 = (f32[4,48,384]{2,1,0:T(8,128)S(1)}, f32[4,48,384]{2,1,0:T(8,128)S(1)}, u32[]{:S(2)}, u32[]{:S(2)}) collective-permute-start(f32[4,48,384]{2,1,0:T(8,128)S(1)} %get-tuple-element.52), channel_id=1, source_target_pairs={{0,4},{4,0},{8,12},{12,8},{16,20},{20,16},{24,28},{28,24},{1,5},{5... | collective-permute-start | bytes 884744 | tf_op jit(solution)/shard_map/ppermute | solution.py:418
  28.0 0.0 collective-permute-done.8.corner_ref
  28.0 0.0 collective-permute-done.9.got_right_ref
  28.0 10.9 %refresh.1 = (f32[384,384]{1,0:T(8,128)S(1)}, f32[384,384]{1,0:T(8,128)S(1)}, f32[384,384]{1,0:T(8,128)S(1)}, f32[576,128]{1,0:T(8,128)S(1)}, f32[4,48,384]{2,1,0:T(8,128)S(1)}) custom-call(f32[576,128]{1,0:T(8,128)S(1)} %get-tuple-element.53.own_ref, f32[192,128]{1,0:T(8,128)S(1)} %collective-permute-done.8.corner_ref, ...), custom_call_target="tpu_custom_call" | custom-call | flops 5435817984 | bytes 2359296 | tf_op jit(solution)/shard_map/refresh/pallas_call | solution.py:475
  38.9 0.4 collective-permute-start.14
  39.3 0.0 collective-permute-done.10.theirs_ref
  39.3 3.2 %collective-permute-start.11 = (f32[48,384]{1,0:T(8,128)S(1)}, f32[48,384]{1,0:T(8,128)S(1)}, u32[]{:S(2)}, u32[]{:S(2)}) collective-permute-start(f32[48,384]{1,0:T(8,128)S(1)} %get-tuple-element.66), channel_id=1, source_target_pairs={{0,16},{4,20},{8,24},{12,28},{16,0},{20,4},{24,8},{28,12},{1,17},{... | collective-permute-start | bytes 221192 | tf_op jit(solution)/shard_map/ppermute | solution.py:415
  42.5 1.1 %collective-permute-start.12 = (f32[48,384]{1,0:T(8,128)S(1)}, f32[48,384]{1,0:T(8,128)S(1)}, u32[]{:S(2)}, u32[]{:S(2)}) collective-permute-start(f32[48,384]{1,0:T(8,128)S(1)} %get-tuple-element.67), channel_id=1, source_target_pairs={{0,24},{4,28},{8,16},{12,20},{16,8},{20,12},{24,0},{28,4},{1,25},{... | collective-permute-start | bytes 221192 | tf_op jit(solution)/shard_map/ppermute | solution.py:415
  43.6 0.5 collective-permute-start.13
  44.0 2.0 %rest.1 = (f32[576,128]{1,0:T(8,128)S(1)}, f32[576,128]{1,0:T(8,128)}, f32[576,128]{1,0:T(8,128)}) custom-call(f32[384,384]{1,0:T(8,128)S(1)} %get-tuple-element.71.x_ref, f32[384,384]{1,0:T(8,128)S(1)} %get-tuple-element.72.poly_ref, f32[384,384]{1,0:T(8,128)S(1)} %get-tuple-element.73.grad_ref, f32[384,384]{1,0:T(8,128)S(1)} %get-tuple-element.74.new_stat_ref, ...), custom_call_target="tpu_custom_call" | custom-call | flops 509607936 | bytes 2359296 | tf_op jit(solution)/shard_map/rest/pallas_call | solution.py:484
  46.1 0.7 %collective-permute-done.11.refs_1_ = f32[48,384]{1,0:T(8,128)S(1)} collective-permute-done((f32[48,384]{1,0:T(8,128)S(1)}, f32[48,384]{1,0:T(8,128)S(1)}, u32[]{:S(2)}, u32[]{:S(2)}) %collective-permute-start.11) | collective-permute-done | bytes 73760 | tf_op jit(solution)/shard_map/ppermute | solution.py:415
  46.8 2.0 %collective-permute-done.12.refs_2_ = f32[48,384]{1,0:T(8,128)S(1)} collective-permute-done((f32[48,384]{1,0:T(8,128)S(1)}, f32[48,384]{1,0:T(8,128)S(1)}, u32[]{:S(2)}, u32[]{:S(2)}) %collective-permute-start.12) | collective-permute-done | bytes 73760 | tf_op jit(solution)/shard_map/ppermute | solution.py:415
  48.7 0.0 collective-permute-done.13.refs_3_
  48.8 0.7 %rows.1 = f32[4,48,384]{2,1,0:T(8,128)} custom-call(f32[48,384]{1,0:T(8,128)S(1)} %get-tuple-element.65.refs_0_, f32[48,384]{1,0:T(8,128)S(1)} %collective-permute-done.11.refs_1_, f32[48,384]{1,0:T(8,128)S(1)} %collective-permute-done.12.refs_2_, f32[48,384]{1,0:T(8,128)S(1)} %collective-permute-done.13.refs_3_), custom_call_target="tpu_custom_call" | custom-call | flops 33973864 | bytes 2359296 | tf_op jit(solution)/shard_map/rows/pallas_call | solution.py:492
  49.5 0.0 collective-permute-done.14.back_ref
  49.5 0.8 %bases.1 = (f32[576,128]{1,0:T(8,128)}, f32[576,128]{1,0:T(8,128)}) custom-call(f32[576,128]{1,0:T(8,128)S(1)} %get-tuple-element.78.keep_ref, f32[576,128]{1,0:T(8,128)S(1)} %collective-permute-done.14.back_ref), custom_call_target="tpu_custom_call" | custom-call | flops 33973864 | bytes 2359296 | tf_op jit(solution)/shard_map/bases/pallas_call | solution.py:506
  (4 shorter events, 0.0 us)
Async XLA Ops:
  0.6 18.4 %collective-permute-start.7 = (f32[576,128]{1,0:T(8,128)}, f32[576,128]{1,0:T(8,128)S(1)}, u32[]{:S(2)}, u32[]{:S(2)}) collective-permute-start(f32[576,128]{1,0:T(8,128)} %bitcast.16), channel_id=1, source_target_pairs={{0,4},{4,0},{8,12},{12,8},{16,20},{20,16},{24,28},{28,24},{1,5},{5... | collective-permute-start | bytes 884744 | tf_op jit(solution)/shard_map/ppermute | solution.py:418
  3.7 16.7 %copy-start = (f32[1,73728]{1,0:T(1,128)S(1)}, f32[1,73728]{1,0:T(1,128)}, u32[]{:S(2)}) copy-start(f32[1,73728]{1,0:T(1,128)} %param.10) | copy-start | bytes 884740
  3.7 16.7 %copy-start.1 = (f32[1,73728]{1,0:T(1,128)S(1)}, f32[1,73728]{1,0:T(1,128)}, u32[]{:S(2)}) copy-start(f32[1,73728]{1,0:T(1,128)} %param.11) | copy-start | bytes 884740
  3.7 16.7 %copy-start.2 = (f32[4,48,384]{2,1,0:T(8,128)S(1)}, f32[4,48,384]{2,1,0:T(8,128)}, u32[]{:S(2)}) copy-start(f32[4,48,384]{2,1,0:T(8,128)} %refs_0_.1) | copy-start | bytes 884740
  4.9 7.4 %collective-permute-start.1 = (f32[48,384]{1,0:T(8,128)S(1)}, f32[48,384]{1,0:T(8,128)S(1)}, u32[]{:S(2)}, u32[]{:S(2)}) collective-permute-start(f32[48,384]{1,0:T(8,128)S(1)} %get-tuple-element.45), channel_id=1, source_target_pairs={{0,16},{4,20},{8,24},{12,28},{16,0},{20,4},{24,8},{28,12},{1,17},{... | collective-permute-start | bytes 221192 | tf_op jit(solution)/shard_map/ppermute | solution.py:415
  7.6 6.3 %collective-permute-start.2 = (f32[48,384]{1,0:T(8,128)S(1)}, f32[48,384]{1,0:T(8,128)S(1)}, u32[]{:S(2)}, u32[]{:S(2)}) collective-permute-start(f32[48,384]{1,0:T(8,128)S(1)} %get-tuple-element.46), channel_id=1, source_target_pairs={{0,24},{4,28},{8,16},{12,20},{16,8},{20,12},{24,0},{28,4},{1,25},{... | collective-permute-start | bytes 221192 | tf_op jit(solution)/shard_map/ppermute | solution.py:415
  8.9 5.5 %collective-permute-start.3 = (f32[48,384]{1,0:T(8,128)S(1)}, f32[48,384]{1,0:T(8,128)S(1)}, u32[]{:S(2)}, u32[]{:S(2)}) collective-permute-start(f32[48,384]{1,0:T(8,128)S(1)} %get-tuple-element.47), channel_id=1, source_target_pairs={{0,8},{4,12},{8,0},{12,4},{16,24},{20,28},{24,16},{28,20},{1,9},{5... | collective-permute-start | bytes 221192 | tf_op jit(solution)/shard_map/ppermute | solution.py:415
  9.2 6.8 %collective-permute-start = (f32[48,384]{1,0:T(8,128)S(1)}, f32[48,384]{1,0:T(8,128)S(1)}, u32[]{:S(2)}, u32[]{:S(2)}) collective-permute-start(f32[48,384]{1,0:T(8,128)S(1)} %get-tuple-element.44), channel_id=1, source_target_pairs={{0,4},{4,0},{8,12},{12,8},{16,20},{20,16},{24,28},{28,24},{1,5},{5... | collective-permute-start | bytes 221192 | tf_op jit(solution)/shard_map/ppermute | solution.py:418
  12.4 4.6 %collective-permute-start.4 = (f32[48,384]{1,0:T(8,128)S(1)}, f32[48,384]{1,0:T(8,128)S(1)}, u32[]{:S(2)}, u32[]{:S(2)}) collective-permute-start(f32[48,384]{1,0:T(8,128)S(1)} %collective-permute-done.1.refs_2_), channel_id=1, source_target_pairs={{0,4},{4,0},{8,12},{12,8},{16,20},{20,16},{24,28},{28,24},{1,5},{5... | collective-permute-start | bytes 221192 | tf_op jit(solution)/shard_map/ppermute | solution.py:418
  13.9 4.4 %collective-permute-start.5 = (f32[48,384]{1,0:T(8,128)S(1)}, f32[48,384]{1,0:T(8,128)S(1)}, u32[]{:S(2)}, u32[]{:S(2)}) collective-permute-start(f32[48,384]{1,0:T(8,128)S(1)} %collective-permute-done.2.refs_3_), channel_id=1, source_target_pairs={{0,4},{4,0},{8,12},{12,8},{16,20},{20,16},{24,28},{28,24},{1,5},{5... | collective-permute-start | bytes 221192 | tf_op jit(solution)/shard_map/ppermute | solution.py:418
  14.4 4.6 %collective-permute-start.6 = (f32[48,384]{1,0:T(8,128)S(1)}, f32[48,384]{1,0:T(8,128)S(1)}, u32[]{:S(2)}, u32[]{:S(2)}) collective-permute-start(f32[48,384]{1,0:T(8,128)S(1)} %collective-permute-done.3.refs_4_), channel_id=1, source_target_pairs={{0,4},{4,0},{8,12},{12,8},{16,20},{20,16},{24,28},{28,24},{1,5},{5... | collective-permute-start | bytes 221192 | tf_op jit(solution)/shard_map/ppermute | solution.py:418
  19.1 8.9 %collective-permute-start.9 = (f32[576,128]{1,0:T(8,128)}, f32[576,128]{1,0:T(8,128)S(1)}, u32[]{:S(2)}, u32[]{:S(2)}) collective-permute-start(f32[576,128]{1,0:T(8,128)} %bitcast.20), channel_id=1, source_target_pairs={{0,4},{4,5},{5,1},{1,0},{8,12},{12,13},{13,9},{9,8},{16,20},{20,21... | collective-permute-start | bytes 884744 | tf_op jit(solution)/shard_map/ppermute | solution.py:457
  20.3 7.7 %collective-permute-start.8 = (f32[192,128]{1,0:T(8,128)S(1)}, f32[192,128]{1,0:T(8,128)S(1)}, u32[]{:S(2)}, u32[]{:S(2)}) collective-permute-start(f32[192,128]{1,0:T(8,128)S(1)} %get-tuple-element.55), channel_id=1, source_target_pairs={{0,4},{4,0},{8,12},{12,8},{16,20},{20,16},{24,28},{28,24},{1,5},{5... | collective-permute-start | bytes 294920 | tf_op jit(solution)/shard_map/ppermute | solution.py:418
  20.3 1.0 %copy-start.3 = (f32[1,73728]{1,0:T(1,128)S(1)}, f32[1,73728]{1,0:T(1,128)}, u32[]{:S(2)}) copy-start(f32[1,73728]{1,0:T(1,128)} %param.12) | copy-start | bytes 884740
  21.3 1.0 %copy-start.6 = (f32[1,73728]{1,0:T(1,128)S(1)}, f32[1,73728]{1,0:T(1,128)}, u32[]{:S(2)}) copy-start(f32[1,73728]{1,0:T(1,128)} %param.13) | copy-start | bytes 884740
  22.3 1.1 %copy-start.4 = (f32[1,73728]{1,0:T(1,128)S(1)}, f32[1,73728]{1,0:T(1,128)}, u32[]{:S(2)}) copy-start(f32[1,73728]{1,0:T(1,128)} %param.8) | copy-start | bytes 884740
  22.3 1.1 %copy-start.5 = (f32[1,73728]{1,0:T(1,128)S(1)}, f32[1,73728]{1,0:T(1,128)}, u32[]{:S(2)}) copy-start(f32[1,73728]{1,0:T(1,128)} %param.9) | copy-start | bytes 884740
  26.0 13.3 %collective-permute-start.10 = (f32[4,48,384]{2,1,0:T(8,128)S(1)}, f32[4,48,384]{2,1,0:T(8,128)S(1)}, u32[]{:S(2)}, u32[]{:S(2)}) collective-permute-start(f32[4,48,384]{2,1,0:T(8,128)S(1)} %get-tuple-element.52), channel_id=1, source_target_pairs={{0,4},{4,0},{8,12},{12,8},{16,20},{20,16},{24,28},{28,24},{1,5},{5... | collective-permute-start | bytes 884744 | tf_op jit(solution)/shard_map/ppermute | solution.py:418
  38.9 10.6 %collective-permute-start.14 = (f32[576,128]{1,0:T(8,128)S(1)}, f32[576,128]{1,0:T(8,128)S(1)}, u32[]{:S(2)}, u32[]{:S(2)}) collective-permute-start(f32[576,128]{1,0:T(8,128)S(1)} %get-tuple-element.62), channel_id=1, source_target_pairs={{0,4},{4,0},{8,12},{12,8},{16,20},{20,16},{24,28},{28,24},{1,5},{5... | collective-permute-start | bytes 884744 | tf_op jit(solution)/shard_map/ppermute | solution.py:418
  39.3 7.5 %collective-permute-start.11 = (f32[48,384]{1,0:T(8,128)S(1)}, f32[48,384]{1,0:T(8,128)S(1)}, u32[]{:S(2)}, u32[]{:S(2)}) collective-permute-start(f32[48,384]{1,0:T(8,128)S(1)} %get-tuple-element.66), channel_id=1, source_target_pairs={{0,16},{4,20},{8,24},{12,28},{16,0},{20,4},{24,8},{28,12},{1,17},{... | collective-permute-start | bytes 221192 | tf_op jit(solution)/shard_map/ppermute | solution.py:415
  42.5 6.3 %collective-permute-start.12 = (f32[48,384]{1,0:T(8,128)S(1)}, f32[48,384]{1,0:T(8,128)S(1)}, u32[]{:S(2)}, u32[]{:S(2)}) collective-permute-start(f32[48,384]{1,0:T(8,128)S(1)} %get-tuple-element.67), channel_id=1, source_target_pairs={{0,24},{4,28},{8,16},{12,20},{16,8},{20,12},{24,0},{28,4},{1,25},{... | collective-permute-start | bytes 221192 | tf_op jit(solution)/shard_map/ppermute | solution.py:415
  43.6 5.2 %collective-permute-start.13 = (f32[48,384]{1,0:T(8,128)S(1)}, f32[48,384]{1,0:T(8,128)S(1)}, u32[]{:S(2)}, u32[]{:S(2)}) collective-permute-start(f32[48,384]{1,0:T(8,128)S(1)} %get-tuple-element.68), channel_id=1, source_target_pairs={{0,8},{4,12},{8,0},{12,4},{16,24},{20,28},{24,16},{28,20},{1,9},{5... | collective-permute-start | bytes 221192 | tf_op jit(solution)/shard_map/ppermute | solution.py:415

commit v12 on v9

--- a/solution.py
+++ b/solution.py
@@ -217,19 +217,6 @@
     gram = dot_parts(parts, parts, ((1,), (1,)))
     gram_parts = split(gram)
     return CUBIC_COEFF * gram + QUINTIC_COEFF * dot_parts(gram_parts, gram_parts)
-
-
-def blocked_step(x):
-    parts = split(x)
-    gram = dot_parts(parts, parts, ((1,), (1,)))
-    gram_parts = split(gram)
-    rows = x.shape[0] // 2
-    blocks = []
-    for k in range(2):
-        block = slice(k * rows, (k + 1) * rows)
-        poly = CUBIC_COEFF * gram[block] + QUINTIC_COEFF * dot_parts([part[block] for part in gram_parts], gram_parts)
-        blocks.append(LINEAR_COEFF * x[block] + dot_parts(split(poly), parts))
-    return jnp.concatenate(blocks, axis=0)
 
 
 def iterate(x, steps):
@@ -331,9 +318,7 @@
 
 
 def end_kernel(hops, steps, start_ref, outer_ref, right_ref, x_ref, poly_ref, send_ref, mine_ref, scratch):
-    x = start_ref[...]
-    for _ in range(steps - 1):
-        x = blocked_step(x)
+    x = iterate(start_ref[...], steps - 1)
     x_ref[...] = x
     rows_for(hops, outer_ref, split(right_ref[...]), mine_ref, lax.axis_index("shard") % 2)
     poly = polynomial(split(x))
@@ -490,7 +475,7 @@
             cycle += [(place(t, i), place(t, i + 1)), (place(t, i + 1), place(t + 1, i + 1))]
             cycle += [(place(t + 1, i + 1), place(t + 1, i)), (place(t + 1, i), place(t, i))]
     cycle += [(place(t, i), place(t, i ^ 1)) for t in range(tensors - tensors % 2, tensors) for i in range(size)]
-    other_left = lax.ppermute(after(l_basis, *(theirs[:2] if near else mine)), ("shard", "tensor"), cycle)
+    other_left = lax.ppermute(after(l_basis, product), ("shard", "tensor"), cycle)
     new_stat, x = call(functools.partial(begin_kernel, EARLY_ITERS), [square] * 2, [(3, full, LANES)], 7, full, "begin")(
         own, got_corner, product, basis
     )

time: 48.5 us -> 48.7 us (level)
  starting transfers between devices: 19 us -> 19.7 us
    ppermute x7, waiting for transfers between devices: 3.75 us -> 2.63 us  [partner(): return lax.ppermute(x, 'shard', pairs)]
    ppermute x1, waiting for transfers between devices: 0.01 us -> 0.87 us  [local(): lax.ppermute(after(l_basis, product), ('shard', 'tensor'), cycle)]
    ppermute x1, starting transfers between devices: 0.68 us -> 1.47 us  [local(): lax.ppermute(after(l_basis, product), ('shard', 'tensor'), cycle)]
    ppermute x6, starting transfers between devices: 9.63 us -> 9.04 us  [hop_by(): return lax.ppermute(x, 'shard', [(i, i ^ 2 * hop) for i in range(size)])]
  transfers between devices with their start and end apart: 14 -> 14, of which waited for: 8 -> 8; matrix products, arithmetic and copies ran while one was open for 0% -> 0% of each run, Pallas kernels for 28% -> 27%
where the time goes in v12:
time: 48.7 us; the launch traced here: 48.5 us
  starting transfers between devices  19.7 us (40%)
  Pallas kernels  18.5 us (38%)
  waiting for transfers between devices  9.54 us (20%)
  between operations  0.77 us (2%)
    ppermute x7, starting transfers between devices, partner(): return lax.ppermute(x, 'shard', pairs)  9.19 us
    ppermute x6, starting transfers between devices, hop_by(): return lax.ppermute(x, 'shard', [(i, i ^ 2 * hop) for i in range(size)])  9.04 us
    ppermute x6, waiting for transfers between devices, hop_by(): return lax.ppermute(x, 'shard', [(i, i ^ 2 * hop) for i in range(size)])  6.04 us
    pallas_call x1, Pallas kernels, local(): call(functools.partial(end_kernel, hops, NS_ITERS - EARLY_ITERS - 1), [sq...  5.78 us
    pallas_call x1, Pallas kernels, local(): call(functools.partial(begin_kernel, EARLY_ITERS), [square] * 2, [(3, ful...  3.35 us
    pallas_call x1, Pallas kernels, local(): call(functools.partial(update_kernel, hops), [flat, flat, strips, wide, s...  3.24 us
    ppermute x7, waiting for transfers between devices, partner(): return lax.ppermute(x, 'shard', pairs)  2.63 us
    pallas_call x1, Pallas kernels, local(): call(rest_kernel, [flat, flat, flat], [(3, full, LANES)], 1.5, full, 'rest')  2.04 us
  transfers between devices with their start and end apart: 14, of which 8 were waited for; matrix products, arithmetic and copies ran while one was open for 0% of the time, Pallas kernels for 27%

profile of v12, /device:TPU:0, one launch (start us, length us, event | category | flops | bytes accessed | tf_op | source)
XLA Modules:
  0.0 48.5 jit_solution(8743421757054672683)
XLA Ops:
  0.6 0.0 copy-start
  0.6 0.0 copy-start.1
  0.7 0.0 copy-start.2
  0.7 0.0 copy-start.3
  0.7 0.0 copy-start.4
  0.7 1.3 %pack.1 = (f32[720,128]{1,0:T(8,128)S(1)}, f32[192,128]{1,0:T(8,128)S(1)}, f32[48,384]{1,0:T(8,128)S(1)}, f32[48,384]{1,0:T(8,128)S(1)}, f32[48,384]{1,0:T(8,128)S(1)}) custom-call(f32[576,128]{1,0:T(8,128)} %bitcast.12, f32[576,128]{1,0:T(8,128)} %bitcast.14, f32[576,128]{1,0:T(8,128)} %bitcast.18, f32[576,128]{1,0:T(8,128)} %bitcast.16, f32[4,48,384]{2,1,0:T(8,128)} %refs_0_.1), custom_call_target="tpu_custom_call" | custom-call | flops 33973864 | bytes 2359296 | tf_op jit(solution)/shard_map/pack/pallas_call | solution.py:438
  2.0 3.0 %collective-permute-start = (f32[720,128]{1,0:T(8,128)S(1)}, f32[720,128]{1,0:T(8,128)S(1)}, u32[]{:S(2)}, u32[]{:S(2)}) collective-permute-start(f32[720,128]{1,0:T(8,128)S(1)} %get-tuple-element.45), channel_id=1, source_target_pairs={{0,4},{4,0},{8,12},{12,8},{16,20},{20,16},{24,28},{28,24},{1,5},{5... | collective-permute-start | bytes 1105928 | tf_op jit(solution)/shard_map/ppermute | solution.py:431
  5.0 2.6 %collective-permute-start.1 = (f32[48,384]{1,0:T(8,128)S(1)}, f32[48,384]{1,0:T(8,128)S(1)}, u32[]{:S(2)}, u32[]{:S(2)}) collective-permute-start(f32[48,384]{1,0:T(8,128)S(1)} %get-tuple-element.46), channel_id=1, source_target_pairs={{0,16},{4,20},{8,24},{12,28},{16,0},{20,4},{24,8},{28,12},{1,17},{... | collective-permute-start | bytes 221192 | tf_op jit(solution)/shard_map/ppermute | solution.py:428
  7.6 1.3 %collective-permute-start.2 = (f32[48,384]{1,0:T(8,128)S(1)}, f32[48,384]{1,0:T(8,128)S(1)}, u32[]{:S(2)}, u32[]{:S(2)}) collective-permute-start(f32[48,384]{1,0:T(8,128)S(1)} %get-tuple-element.47), channel_id=1, source_target_pairs={{0,24},{4,28},{8,16},{12,20},{16,8},{20,12},{24,0},{28,4},{1,25},{... | collective-permute-start | bytes 221192 | tf_op jit(solution)/shard_map/ppermute | solution.py:428
  9.0 0.2 collective-permute-start.3
  9.2 3.2 %collective-permute-done.1.refs_1_ = f32[48,384]{1,0:T(8,128)S(1)} collective-permute-done((f32[48,384]{1,0:T(8,128)S(1)}, f32[48,384]{1,0:T(8,128)S(1)}, u32[]{:S(2)}, u32[]{:S(2)}) %collective-permute-start.1) | collective-permute-done | bytes 73760 | tf_op jit(solution)/shard_map/ppermute | solution.py:428
  12.4 0.5 collective-permute-start.4
  12.9 1.1 %collective-permute-done.2.refs_2_ = f32[48,384]{1,0:T(8,128)S(1)} collective-permute-done((f32[48,384]{1,0:T(8,128)S(1)}, f32[48,384]{1,0:T(8,128)S(1)}, u32[]{:S(2)}, u32[]{:S(2)}) %collective-permute-start.2) | collective-permute-done | bytes 73760 | tf_op jit(solution)/shard_map/ppermute | solution.py:428
  13.9 0.5 %collective-permute-start.5 = (f32[48,384]{1,0:T(8,128)S(1)}, f32[48,384]{1,0:T(8,128)S(1)}, u32[]{:S(2)}, u32[]{:S(2)}) collective-permute-start(f32[48,384]{1,0:T(8,128)S(1)} %collective-permute-done.2.refs_2_), channel_id=1, source_target_pairs={{0,4},{4,0},{8,12},{12,8},{16,20},{20,16},{24,28},{28,24},{1,5},{5... | collective-permute-start | bytes 221192 | tf_op jit(solution)/shard_map/ppermute | solution.py:431
  14.4 0.0 collective-permute-done.3.refs_3_
  14.5 1.5 %collective-permute-start.6 = (f32[48,384]{1,0:T(8,128)S(1)}, f32[48,384]{1,0:T(8,128)S(1)}, u32[]{:S(2)}, u32[]{:S(2)}) collective-permute-start(f32[48,384]{1,0:T(8,128)S(1)} %collective-permute-done.3.refs_3_), channel_id=1, source_target_pairs={{0,4},{4,0},{8,12},{12,8},{16,20},{20,16},{24,28},{28,24},{1,5},{5... | collective-permute-start | bytes 221192 | tf_op jit(solution)/shard_map/ppermute | solution.py:431
  16.0 1.0 %collective-permute-done.4.refs_4_ = f32[48,384]{1,0:T(8,128)S(1)} collective-permute-done((f32[48,384]{1,0:T(8,128)S(1)}, f32[48,384]{1,0:T(8,128)S(1)}, u32[]{:S(2)}, u32[]{:S(2)}) %collective-permute-start.4) | collective-permute-done | bytes 73760 | tf_op jit(solution)/shard_map/ppermute | solution.py:431
  17.0 1.1 %collective-permute-start.8 = (f32[192,128]{1,0:T(8,128)S(1)}, f32[192,128]{1,0:T(8,128)S(1)}, u32[]{:S(2)}, u32[]{:S(2)}) collective-permute-start(f32[192,128]{1,0:T(8,128)S(1)} %get-tuple-element.57), channel_id=1, source_target_pairs={{0,4},{4,0},{8,12},{12,8},{16,20},{20,16},{24,28},{28,24},{1,5},{5... | collective-permute-start | bytes 294920 | tf_op jit(solution)/shard_map/ppermute | solution.py:431
  18.1 0.8 %collective-permute-done.5.refs_5_ = f32[48,384]{1,0:T(8,128)S(1)} collective-permute-done((f32[48,384]{1,0:T(8,128)S(1)}, f32[48,384]{1,0:T(8,128)S(1)}, u32[]{:S(2)}, u32[]{:S(2)}) %collective-permute-start.5) | collective-permute-done | bytes 73760 | tf_op jit(solution)/shard_map/ppermute | solution.py:431
  18.9 0.8 %collective-permute-done.6.refs_6_ = f32[48,384]{1,0:T(8,128)S(1)} collective-permute-done((f32[48,384]{1,0:T(8,128)S(1)}, f32[48,384]{1,0:T(8,128)S(1)}, u32[]{:S(2)}, u32[]{:S(2)}) %collective-permute-start.6) | collective-permute-done | bytes 73760 | tf_op jit(solution)/shard_map/ppermute | solution.py:431
  19.7 0.0 collective-permute-done.got_ref
  19.7 0.0 copy-done
  19.7 0.0 copy-done.1
  19.7 0.0 copy-done.2
  19.7 0.0 copy-done.3
  19.7 0.0 copy-done.4
  19.7 1.1 %products.1 = (f32[384,384]{1,0:T(8,128)S(1)}, f32[384,384]{1,0:T(8,128)S(1)}, f32[384,384]{1,0:T(8,128)S(1)}, f32[384,256]{1,0:T(8,128)S(1)}, f32[384,256]{1,0:...) custom-call(f32[576,128]{1,0:T(8,128)S(1)} %bitcast.13, ...), custom_call_target="tpu_custom_call" | custom-call | flops 679477248 | bytes 2359296 | tf_op jit(solution)/shard_map/products/pallas_call | solution.py:462
  20.9 1.5 %collective-permute-start.7 = (f32[576,128]{1,0:T(8,128)S(1)}, f32[576,128]{1,0:T(8,128)S(1)}, u32[]{:S(2)}, u32[]{:S(2)}) collective-permute-start(f32[576,128]{1,0:T(8,128)S(1)} %bitcast.20), channel_id=1, source_target_pairs={{0,4},{4,5},{5,1},{1,0},{8,12},{12,13},{13,9},{9,8},{16,20},{20,21... | collective-permute-start | bytes 884744 | tf_op jit(solution)/shard_map/ppermute | solution.py:478
  22.4 0.0 collective-permute-done.8.corner_ref
  22.4 3.4 %begin.1 = (f32[384,384]{1,0:T(8,128)S(1)}, f32[384,384]{1,0:T(8,128)S(1)}) custom-call(f32[576,128]{1,0:T(8,128)S(1)} %get-tuple-element.55.own_ref, f32[192,128]{1,0:T(8,128)S(1)} %collective-permute-done.8.corner_ref, f32[384,384]{1,0:T(8,128)S(1)} %get-tuple-element.53.product_ref, f32[384,384]{1,0:T(8,128)S(1)} %get-tuple-element.50.basis_ref), custom_call_target="tpu_custom_call" | custom-call | flops 2378170368 | bytes 2359296 | tf_op jit(solution)/shard_map/begin/pallas_call | solution.py:479
  25.7 0.9 %collective-permute-done.7.other_left_ref = f32[576,128]{1,0:T(8,128)S(1)} collective-permute-done((f32[576,128]{1,0:T(8,128)S(1)}, f32[576,128]{1,0:T(8,128)S(1)}, u32[]{:S(2)}, u32[]{:S(2)}) %collective-permute-start.7) | collective-permute-done | bytes 294944 | tf_op jit(solution)/shard_map/ppermute | solution.py:478
  26.6 0.0 copy-done.5
  26.6 0.0 copy-done.6
  26.6 3.2 %update.1 = (f32[576,128]{1,0:T(8,128)}, f32[576,128]{1,0:T(8,128)}, f32[4,48,384]{2,1,0:T(8,128)S(1)}, f32[384,256]{1,0:T(8,128)S(1)}, f32[384,384]{1,0:T(8,128)S(1)}) custom-call(f32[384,256]{1,0:T(8,128)S(1)} %get-tuple-element.49.inner_ref, f32[384,384]{1,0:T(8,128)S(1)} %get-tuple-element.50.basis_ref, f32[576,128]{1,0:T(8,128)S(1)} %get-tuple-element.51.left_ref, ...), custom_call_target="tpu_custom_call" | custom-call | flops 1698693120 | bytes 2359296 | tf_op jit(solution)/shard_map/update/pallas_call | solution.py:483
  29.8 2.5 %collective-permute-start.9 = (f32[4,48,384]{2,1,0:T(8,128)S(1)}, f32[4,48,384]{2,1,0:T(8,128)S(1)}, u32[]{:S(2)}, u32[]{:S(2)}) collective-permute-start(f32[4,48,384]{2,1,0:T(8,128)S(1)} %get-tuple-element.60), channel_id=1, source_target_pairs={{0,4},{4,0},{8,12},{12,8},{16,20},{20,16},{24,28},{28,24},{1,5},{5... | collective-permute-start | bytes 884744 | tf_op jit(solution)/shard_map/ppermute | solution.py:431
  32.3 5.8 %end.1 = (f32[384,384]{1,0:T(8,128)S(1)}, f32[384,384]{1,0:T(8,128)S(1)}, f32[576,128]{1,0:T(8,128)S(1)}, f32[4,48,384]{2,1,0:T(8,128)S(1)}) custom-call(f32[384,384]{1,0:T(8,128)S(1)} %get-tuple-element.61.start_ref, f32[384,256]{1,0:T(8,128)S(1)} %get-tuple-element.62.outer_ref, f32[384,256]{1,0:T(8,128)S(1)} %get-tuple-element.52.right_ref), custom_call_target="tpu_custom_call" | custom-call | flops 3057647616 | bytes 2359296 | tf_op jit(solution)/shard_map/end/pallas_call | solution.py:490
  38.1 0.1 collective-permute-start.13
  38.2 0.0 collective-permute-done.9.theirs_ref
  38.2 3.2 %collective-permute-start.10 = (f32[48,384]{1,0:T(8,128)S(1)}, f32[48,384]{1,0:T(8,128)S(1)}, u32[]{:S(2)}, u32[]{:S(2)}) collective-permute-start(f32[48,384]{1,0:T(8,128)S(1)} %get-tuple-element.68), channel_id=1, source_target_pairs={{0,16},{4,20},{8,24},{12,28},{16,0},{20,4},{24,8},{28,12},{1,17},{... | collective-permute-start | bytes 221192 | tf_op jit(solution)/shard_map/ppermute | solution.py:428
  41.4 1.2 %collective-permute-start.11 = (f32[48,384]{1,0:T(8,128)S(1)}, f32[48,384]{1,0:T(8,128)S(1)}, u32[]{:S(2)}, u32[]{:S(2)}) collective-permute-start(f32[48,384]{1,0:T(8,128)S(1)} %get-tuple-element.69), channel_id=1, source_target_pairs={{0,24},{4,28},{8,16},{12,20},{16,8},{20,12},{24,0},{28,4},{1,25},{... | collective-permute-start | bytes 221192 | tf_op jit(solution)/shard_map/ppermute | solution.py:428
  42.6 0.5 %collective-permute-start.12 = (f32[48,384]{1,0:T(8,128)S(1)}, f32[48,384]{1,0:T(8,128)S(1)}, u32[]{:S(2)}, u32[]{:S(2)}) collective-permute-start(f32[48,384]{1,0:T(8,128)S(1)} %get-tuple-element.70), channel_id=1, source_target_pairs={{0,8},{4,12},{8,0},{12,4},{16,24},{20,28},{24,16},{28,20},{1,9},{5... | collective-permute-start | bytes 221192 | tf_op jit(solution)/shard_map/ppermute | solution.py:428
  43.1 2.0 %rest.1 = (f32[576,128]{1,0:T(8,128)S(1)}, f32[576,128]{1,0:T(8,128)}, f32[576,128]{1,0:T(8,128)}) custom-call(f32[384,384]{1,0:T(8,128)S(1)} %get-tuple-element.73.x_ref, f32[384,384]{1,0:T(8,128)S(1)} %get-tuple-element.74.poly_ref, f32[384,384]{1,0:T(8,128)S(1)} %get-tuple-element.75.grad_ref, f32[384,384]{1,0:T(8,128)S(1)} %get-tuple-element.76.new_stat_ref, ...), custom_call_target="tpu_custom_call" | custom-call | flops 509607936 | bytes 2359296 | tf_op jit(solution)/shard_map/rest/pallas_call | solution.py:499
  45.2 0.0 collective-permute-done.13.back_ref
  45.2 0.8 %bases.1 = (f32[576,128]{1,0:T(8,128)}, f32[576,128]{1,0:T(8,128)}) custom-call(f32[576,128]{1,0:T(8,128)S(1)} %get-tuple-element.80.keep_ref, f32[576,128]{1,0:T(8,128)S(1)} %collective-permute-done.13.back_ref), custom_call_target="tpu_custom_call" | custom-call | flops 33973864 | bytes 2359296 | tf_op jit(solution)/shard_map/bases/pallas_call | solution.py:521
  46.0 0.0 collective-permute-done.10.refs_1_
  46.0 1.7 %collective-permute-done.11.refs_2_ = f32[48,384]{1,0:T(8,128)S(1)} collective-permute-done((f32[48,384]{1,0:T(8,128)S(1)}, f32[48,384]{1,0:T(8,128)S(1)}, u32[]{:S(2)}, u32[]{:S(2)}) %collective-permute-start.11) | collective-permute-done | bytes 73760 | tf_op jit(solution)/shard_map/ppermute | solution.py:428
  47.7 0.1 collective-permute-done.12.refs_3_
  47.8 0.7 %rows.1 = f32[4,48,384]{2,1,0:T(8,128)} custom-call(f32[48,384]{1,0:T(8,128)S(1)} %get-tuple-element.67.refs_0_, f32[48,384]{1,0:T(8,128)S(1)} %collective-permute-done.10.refs_1_, f32[48,384]{1,0:T(8,128)S(1)} %collective-permute-done.11.refs_2_, f32[48,384]{1,0:T(8,128)S(1)} %collective-permute-done.12.refs_3_), custom_call_target="tpu_custom_call" | custom-call | flops 33973864 | bytes 2359296 | tf_op jit(solution)/shard_map/rows/pallas_call | solution.py:507
  (3 shorter events, 0.0 us)
Async XLA Ops:
  0.6 19.1 %copy-start = (f32[1,73728]{1,0:T(1,128)S(1)}, f32[1,73728]{1,0:T(1,128)}, u32[]{:S(2)}) copy-start(f32[1,73728]{1,0:T(1,128)} %param.10) | copy-start | bytes 884740
  0.6 19.1 %copy-start.1 = (f32[1,73728]{1,0:T(1,128)S(1)}, f32[1,73728]{1,0:T(1,128)}, u32[]{:S(2)}) copy-start(f32[1,73728]{1,0:T(1,128)} %param.11) | copy-start | bytes 884740
  0.7 19.1 %copy-start.2 = (f32[1,73728]{1,0:T(1,128)S(1)}, f32[1,73728]{1,0:T(1,128)}, u32[]{:S(2)}) copy-start(f32[1,73728]{1,0:T(1,128)} %param.13) | copy-start | bytes 884740
  0.7 19.1 %copy-start.3 = (f32[4,48,384]{2,1,0:T(8,128)S(1)}, f32[4,48,384]{2,1,0:T(8,128)}, u32[]{:S(2)}) copy-start(f32[4,48,384]{2,1,0:T(8,128)} %refs_0_.1) | copy-start | bytes 884740
  0.7 19.1 %copy-start.4 = (f32[1,73728]{1,0:T(1,128)S(1)}, f32[1,73728]{1,0:T(1,128)}, u32[]{:S(2)}) copy-start(f32[1,73728]{1,0:T(1,128)} %param.12) | copy-start | bytes 884740
  2.0 17.7 %collective-permute-start = (f32[720,128]{1,0:T(8,128)S(1)}, f32[720,128]{1,0:T(8,128)S(1)}, u32[]{:S(2)}, u32[]{:S(2)}) collective-permute-start(f32[720,128]{1,0:T(8,128)S(1)} %get-tuple-element.45), channel_id=1, source_target_pairs={{0,4},{4,0},{8,12},{12,8},{16,20},{20,16},{24,28},{28,24},{1,5},{5... | collective-permute-start | bytes 1105928 | tf_op jit(solution)/shard_map/ppermute | solution.py:431
  5.0 7.4 %collective-permute-start.1 = (f32[48,384]{1,0:T(8,128)S(1)}, f32[48,384]{1,0:T(8,128)S(1)}, u32[]{:S(2)}, u32[]{:S(2)}) collective-permute-start(f32[48,384]{1,0:T(8,128)S(1)} %get-tuple-element.46), channel_id=1, source_target_pairs={{0,16},{4,20},{8,24},{12,28},{16,0},{20,4},{24,8},{28,12},{1,17},{... | collective-permute-start | bytes 221192 | tf_op jit(solution)/shard_map/ppermute | solution.py:428
  7.6 6.3 %collective-permute-start.2 = (f32[48,384]{1,0:T(8,128)S(1)}, f32[48,384]{1,0:T(8,128)S(1)}, u32[]{:S(2)}, u32[]{:S(2)}) collective-permute-start(f32[48,384]{1,0:T(8,128)S(1)} %get-tuple-element.47), channel_id=1, source_target_pairs={{0,24},{4,28},{8,16},{12,20},{16,8},{20,12},{24,0},{28,4},{1,25},{... | collective-permute-start | bytes 221192 | tf_op jit(solution)/shard_map/ppermute | solution.py:428
  9.0 5.5 %collective-permute-start.3 = (f32[48,384]{1,0:T(8,128)S(1)}, f32[48,384]{1,0:T(8,128)S(1)}, u32[]{:S(2)}, u32[]{:S(2)}) collective-permute-start(f32[48,384]{1,0:T(8,128)S(1)} %get-tuple-element.48), channel_id=1, source_target_pairs={{0,8},{4,12},{8,0},{12,4},{16,24},{20,28},{24,16},{28,20},{1,9},{5... | collective-permute-start | bytes 221192 | tf_op jit(solution)/shard_map/ppermute | solution.py:428
  12.4 4.6 %collective-permute-start.4 = (f32[48,384]{1,0:T(8,128)S(1)}, f32[48,384]{1,0:T(8,128)S(1)}, u32[]{:S(2)}, u32[]{:S(2)}) collective-permute-start(f32[48,384]{1,0:T(8,128)S(1)} %collective-permute-done.1.refs_1_), channel_id=1, source_target_pairs={{0,4},{4,0},{8,12},{12,8},{16,20},{20,16},{24,28},{28,24},{1,5},{5... | collective-permute-start | bytes 221192 | tf_op jit(solution)/shard_map/ppermute | solution.py:431
  13.9 5.0 %collective-permute-start.5 = (f32[48,384]{1,0:T(8,128)S(1)}, f32[48,384]{1,0:T(8,128)S(1)}, u32[]{:S(2)}, u32[]{:S(2)}) collective-permute-start(f32[48,384]{1,0:T(8,128)S(1)} %collective-permute-done.2.refs_2_), channel_id=1, source_target_pairs={{0,4},{4,0},{8,12},{12,8},{16,20},{20,16},{24,28},{28,24},{1,5},{5... | collective-permute-start | bytes 221192 | tf_op jit(solution)/shard_map/ppermute | solution.py:431
  14.5 5.3 %collective-permute-start.6 = (f32[48,384]{1,0:T(8,128)S(1)}, f32[48,384]{1,0:T(8,128)S(1)}, u32[]{:S(2)}, u32[]{:S(2)}) collective-permute-start(f32[48,384]{1,0:T(8,128)S(1)} %collective-permute-done.3.refs_3_), channel_id=1, source_target_pairs={{0,4},{4,0},{8,12},{12,8},{16,20},{20,16},{24,28},{28,24},{1,5},{5... | collective-permute-start | bytes 221192 | tf_op jit(solution)/shard_map/ppermute | solution.py:431
  17.0 5.4 %collective-permute-start.8 = (f32[192,128]{1,0:T(8,128)S(1)}, f32[192,128]{1,0:T(8,128)S(1)}, u32[]{:S(2)}, u32[]{:S(2)}) collective-permute-start(f32[192,128]{1,0:T(8,128)S(1)} %get-tuple-element.57), channel_id=1, source_target_pairs={{0,4},{4,0},{8,12},{12,8},{16,20},{20,16},{24,28},{28,24},{1,5},{5... | collective-permute-start | bytes 294920 | tf_op jit(solution)/shard_map/ppermute | solution.py:431
  20.9 5.7 %collective-permute-start.7 = (f32[576,128]{1,0:T(8,128)S(1)}, f32[576,128]{1,0:T(8,128)S(1)}, u32[]{:S(2)}, u32[]{:S(2)}) collective-permute-start(f32[576,128]{1,0:T(8,128)S(1)} %bitcast.20), channel_id=1, source_target_pairs={{0,4},{4,5},{5,1},{1,0},{8,12},{12,13},{13,9},{9,8},{16,20},{20,21... | collective-permute-start | bytes 884744 | tf_op jit(solution)/shard_map/ppermute | solution.py:478
  22.4 4.2 %copy-start.5 = (f32[1,73728]{1,0:T(1,128)S(1)}, f32[1,73728]{1,0:T(1,128)}, u32[]{:S(2)}) copy-start(f32[1,73728]{1,0:T(1,128)} %param.8) | copy-start | bytes 884740
  22.4 4.2 %copy-start.6 = (f32[1,73728]{1,0:T(1,128)S(1)}, f32[1,73728]{1,0:T(1,128)}, u32[]{:S(2)}) copy-start(f32[1,73728]{1,0:T(1,128)} %param.9) | copy-start | bytes 884740
  29.8 8.3 %collective-permute-start.9 = (f32[4,48,384]{2,1,0:T(8,128)S(1)}, f32[4,48,384]{2,1,0:T(8,128)S(1)}, u32[]{:S(2)}, u32[]{:S(2)}) collective-permute-start(f32[4,48,384]{2,1,0:T(8,128)S(1)} %get-tuple-element.60), channel_id=1, source_target_pairs={{0,4},{4,0},{8,12},{12,8},{16,20},{20,16},{24,28},{28,24},{1,5},{5... | collective-permute-start | bytes 884744 | tf_op jit(solution)/shard_map/ppermute | solution.py:431
  38.1 7.0 %collective-permute-start.13 = (f32[576,128]{1,0:T(8,128)S(1)}, f32[576,128]{1,0:T(8,128)S(1)}, u32[]{:S(2)}, u32[]{:S(2)}) collective-permute-start(f32[576,128]{1,0:T(8,128)S(1)} %get-tuple-element.64), channel_id=1, source_target_pairs={{0,4},{4,0},{8,12},{12,8},{16,20},{20,16},{24,28},{28,24},{1,5},{5... | collective-permute-start | bytes 884744 | tf_op jit(solution)/shard_map/ppermute | solution.py:431
  38.2 7.8 %collective-permute-start.10 = (f32[48,384]{1,0:T(8,128)S(1)}, f32[48,384]{1,0:T(8,128)S(1)}, u32[]{:S(2)}, u32[]{:S(2)}) collective-permute-start(f32[48,384]{1,0:T(8,128)S(1)} %get-tuple-element.68), channel_id=1, source_target_pairs={{0,16},{4,20},{8,24},{12,28},{16,0},{20,4},{24,8},{28,12},{1,17},{... | collective-permute-start | bytes 221192 | tf_op jit(solution)/shard_map/ppermute | solution.py:428
  41.4 6.3 %collective-permute-start.11 = (f32[48,384]{1,0:T(8,128)S(1)}, f32[48,384]{1,0:T(8,128)S(1)}, u32[]{:S(2)}, u32[]{:S(2)}) collective-permute-start(f32[48,384]{1,0:T(8,128)S(1)} %get-tuple-element.69), channel_id=1, source_target_pairs={{0,24},{4,28},{8,16},{12,20},{16,8},{20,12},{24,0},{28,4},{1,25},{... | collective-permute-start | bytes 221192 | tf_op jit(solution)/shard_map/ppermute | solution.py:428
  42.6 5.1 %collective-permute-start.12 = (f32[48,384]{1,0:T(8,128)S(1)}, f32[48,384]{1,0:T(8,128)S(1)}, u32[]{:S(2)}, u32[]{:S(2)}) collective-permute-start(f32[48,384]{1,0:T(8,128)S(1)} %get-tuple-element.70), channel_id=1, source_target_pairs={{0,8},{4,12},{8,0},{12,4},{16,24},{20,28},{24,16},{28,20},{1,9},{5... | collective-permute-start | bytes 221192 | tf_op jit(solution)/shard_map/ppermute | solution.py:428

commit v13 on v12

--- a/solution.py
+++ b/solution.py
@@ -193,20 +193,25 @@
     ]
 
 
-def statistic(first, own, got_ref, scratch):
-    corner = unpack_corner(got_ref)
-    placed = [jnp.concatenate([jnp.where(first, 0.0, c), jnp.where(first, c, 0.0)], axis=0) for c in corner]
-    known = whole_of(scratch, pick(first, own, placed), pick(first, placed, own))
+def known_part(first, own, scratch):
+    zeros = [jnp.zeros_like(x) for x in own]
+    known = whole_of(scratch, pick(first, own, zeros), pick(first, zeros, own))
     half = known.shape[0] // 2
-    part = half // 3
     row = lax.broadcasted_iota(jnp.int32, known.shape, 0)
     column = lax.broadcasted_iota(jnp.int32, known.shape, 1)
     missing = (jnp.where(first, row, column) < half) & (jnp.where(first, column, row) >= half)
-    offset = jnp.where(first, half, 0)
-    row, column = row - offset, column - offset
-    limit = jnp.where(row < part, part, 2 * part)
-    missing |= (row >= 0) & (row < 2 * part) & (column < half) & (column >= limit)
     return jnp.where(missing, known.T, known)
+
+
+def corner_part(corner_ref, scratch):
+    corner = half_of(scratch, unpack_corner(corner_ref))
+    rows, wide = corner.shape
+    turned = jnp.concatenate([corner, jnp.zeros((wide - rows, wide), F32)], axis=0).T[:rows]
+    part = rows // 3
+    row = lax.broadcasted_iota(jnp.int32, corner.shape, 0)
+    column = lax.broadcasted_iota(jnp.int32, corner.shape, 1)
+    missing = (row < 2 * part) & (column >= jnp.where(row < part, part, 2 * part))
+    return jnp.where(missing, turned, corner)
 
 
 def place_rows(grad_ref, block, rows, value):
@@ -229,7 +234,7 @@
 def products_kernel(hops, l_stat_ref, r_stat_ref, l_basis_ref, r_basis_ref, got_ref, *refs):
     left = is_left()
     outs = refs[-9:]
-    grad_ref, product_ref, basis_ref, right_ref, inner_ref, own_ref, other_ref, copy_ref, scratch = outs
+    grad_ref, stat_ref, power_ref, basis_ref, right_ref, inner_ref, other_ref, copy_ref, scratch = outs
     if hops:
         grads_ref, mine_refs, theirs_refs = refs[0], refs[1 : 1 + len(hops)], refs[1 + len(hops) : 1 + 2 * len(hops)]
         rows = grads_ref.shape[1]
@@ -247,22 +252,29 @@
     own = pick(left, thirds(l_basis_ref), thirds(r_basis_ref))
     got = thirds(got_ref, 0, l_basis_ref.shape[0])
     first = is_first()
-    basis_ref[...] = whole_of(scratch, pick(first, own, got), pick(first, got, own))
-    own_ref[...] = jnp.where(left, l_stat_ref[...], r_stat_ref[...])
+    basis = whole_of(scratch, pick(first, own, got), pick(first, got, own))
+    basis_ref[...] = basis
+    known = known_part(first, pick(left, thirds(l_stat_ref), thirds(r_stat_ref)), scratch)
     other_ref[...] = jnp.where(left, r_stat_ref[...], l_stat_ref[...])
     copy_ref[...] = l_basis_ref[...]
     right = half_of(scratch, thirds(r_basis_ref))
     right_ref[...] = right
     grad = grad_ref[...]
     parts = split(jnp.where(left, grad, grad.T))
-    product_ref[...] = symmetric_dot(parts, parts, ((1,), (1,)))
+    stat = 0.5 * known + 0.5 * symmetric_dot(parts, parts, ((1,), (1,)))
+    stat_ref[...] = stat
+    power_ref[...] = dot(stat, basis)
     inner_ref[...] = dot(grad, right)
 
 
-def begin_kernel(steps, own_ref, corner_ref, product_ref, basis_ref, new_stat_ref, x_ref, scratch):
-    new_stat = 0.5 * statistic(is_first(), thirds(own_ref), corner_ref, scratch) + 0.5 * product_ref[...]
-    new_stat_ref[...] = new_stat
-    power = dot(new_stat, basis_ref[...])
+def begin_kernel(steps, corner_ref, power_ref, basis_ref, x_ref, scratch):
+    first = is_first()
+    corner = corner_part(corner_ref, scratch)
+    rows, wide = corner.shape
+    basis = jnp.where(first, basis_ref[pl.ds(rows, rows), :], basis_ref[pl.ds(0, rows), :])
+    basis = jnp.concatenate([basis, jnp.zeros((wide - rows, 2 * rows), F32)], axis=0)
+    term = 0.5 * dot(corner, basis)
+    power = power_ref[...] + jnp.concatenate([jnp.where(first, 0.0, term), jnp.where(first, term, 0.0)], axis=0)
     x_ref[...] = iterate(power * (1.0 / jnp.sqrt(jnp.sum(power * power) + NORM_EPS)), steps)
 
 
@@ -459,9 +471,9 @@
         rows = (jnp.stack([even, odd], axis=1).reshape(square),)
         mine = [mine]
     got_corner = partner(after(corner, theirs[0] if near else mine[0]))
-    grad, product, basis, right, inner, own, other, left = call(
+    grad, new_stat, power, basis, right, inner, other, left = call(
         functools.partial(products_kernel, hops),
-        [square, square, square, (full, 2 * LANES), (full, 2 * LANES), flat, flat, flat],
+        [square, square, square, square, (full, 2 * LANES), (full, 2 * LANES), flat, flat],
         [(3, full, LANES)],
         2,
         full,
@@ -475,10 +487,10 @@
             cycle += [(place(t, i), place(t, i + 1)), (place(t, i + 1), place(t + 1, i + 1))]
             cycle += [(place(t + 1, i + 1), place(t + 1, i)), (place(t + 1, i), place(t, i))]
     cycle += [(place(t, i), place(t, i ^ 1)) for t in range(tensors - tensors % 2, tensors) for i in range(size)]
-    other_left = lax.ppermute(after(l_basis, product), ("shard", "tensor"), cycle)
-    new_stat, x = call(functools.partial(begin_kernel, EARLY_ITERS), [square] * 2, [(3, full, LANES)], 7, full, "begin")(
-        own, got_corner, product, basis
-    )
+    other_left = lax.ppermute(after(l_basis, *(theirs[:2] if near else mine)), ("shard", "tensor"), cycle)
+    (x,) = call(
+        functools.partial(begin_kernel, EARLY_ITERS), [square], [(2, full // 2, LANES)], 7, full, "begin"
+    )(got_corner, power, basis)
     wide = (full, 2 * LANES)
     new_one, new_two, other_rows, outer, x = call(
         functools.partial(update_kernel, hops), [flat, flat, strips, wide, square], [(3, full, LANES)], 5, full, "update"

time: 48.7 us -> 47.6 us (0.977)
  starting transfers between devices: 19.7 us -> 18.6 us
    ppermute x1, waiting for transfers between devices: 0.87 us -> 0.01 us  [local(): lax.ppermute(after(l_basis, *(theirs[:2] if near else mine)), ('shard', '...]
    ppermute x1, starting transfers between devices: 1.47 us -> 0.68 us  [local(): lax.ppermute(after(l_basis, *(theirs[:2] if near else mine)), ('shard', '...]
    ppermute x7, waiting for transfers between devices: 2.63 us -> 3.2 us  [partner(): return lax.ppermute(x, 'shard', pairs)]
  transfers between devices with their start and end apart: 14 -> 14, of which waited for: 8 -> 8; matrix products, arithmetic and copies ran while one was open for 0% -> 0% of each run, Pallas kernels for 27% -> 29%
where the time goes in v13:
time: 47.6 us; the launch traced here: 47.5 us
  Pallas kernels  18.9 us (40%)
  starting transfers between devices  18.6 us (39%)
  waiting for transfers between devices  9.22 us (19%)
  between operations  0.79 us (2%)
    ppermute x6, starting transfers between devices, hop_by(): return lax.ppermute(x, 'shard', [(i, i ^ 2 * hop) for i in range(size)])  9.16 us
    ppermute x7, starting transfers between devices, partner(): return lax.ppermute(x, 'shard', pairs)  8.73 us
    ppermute x6, waiting for transfers between devices, hop_by(): return lax.ppermute(x, 'shard', [(i, i ^ 2 * hop) for i in range(size)])  6.02 us
    pallas_call x1, Pallas kernels, local(): call(functools.partial(end_kernel, hops, NS_ITERS - EARLY_ITERS - 1), [sq...  5.78 us
    pallas_call x1, Pallas kernels, local(): call(functools.partial(update_kernel, hops), [flat, flat, strips, wide, s...  3.25 us
    ppermute x7, waiting for transfers between devices, partner(): return lax.ppermute(x, 'shard', pairs)  3.2 us
    pallas_call x1, Pallas kernels, local(): call(functools.partial(begin_kernel, EARLY_ITERS), [square], [(2, full //...  2.66 us
    pallas_call x1, Pallas kernels, local(): call(functools.partial(products_kernel, hops), [square, square, square, s...  2.19 us
  transfers between devices with their start and end apart: 14, of which 8 were waited for; matrix products, arithmetic and copies ran while one was open for 0% of the time, Pallas kernels for 29%

profile of v13, /device:TPU:0, one launch (start us, length us, event | category | flops | bytes accessed | tf_op | source)
XLA Modules:
  0.0 47.5 jit_solution(13697566499596685247)
XLA Ops:
  0.6 0.0 copy-start.4
  0.6 0.0 copy-start
  0.7 0.0 copy-start.1
  0.7 0.0 copy-start.2
  0.7 0.0 copy-start.3
  0.7 1.3 %pack.1 = (f32[720,128]{1,0:T(8,128)S(1)}, f32[192,128]{1,0:T(8,128)S(1)}, f32[48,384]{1,0:T(8,128)S(1)}, f32[48,384]{1,0:T(8,128)S(1)}, f32[48,384]{1,0:T(8,128)S(1)}) custom-call(f32[576,128]{1,0:T(8,128)} %bitcast.12, f32[576,128]{1,0:T(8,128)} %bitcast.14, f32[576,128]{1,0:T(8,128)} %bitcast.18, f32[576,128]{1,0:T(8,128)} %bitcast.16, f32[4,48,384]{2,1,0:T(8,128)} %refs_0_.1), custom_call_target="tpu_custom_call" | custom-call | flops 33973864 | bytes 2359296 | tf_op jit(solution)/shard_map/pack/pallas_call | solution.py:450
  2.0 3.0 %collective-permute-start = (f32[720,128]{1,0:T(8,128)S(1)}, f32[720,128]{1,0:T(8,128)S(1)}, u32[]{:S(2)}, u32[]{:S(2)}) collective-permute-start(f32[720,128]{1,0:T(8,128)S(1)} %get-tuple-element.43), channel_id=1, source_target_pairs={{0,4},{4,0},{8,12},{12,8},{16,20},{20,16},{24,28},{28,24},{1,5},{5... | collective-permute-start | bytes 1105928 | tf_op jit(solution)/shard_map/ppermute | solution.py:443
  5.0 2.6 %collective-permute-start.1 = (f32[48,384]{1,0:T(8,128)S(1)}, f32[48,384]{1,0:T(8,128)S(1)}, u32[]{:S(2)}, u32[]{:S(2)}) collective-permute-start(f32[48,384]{1,0:T(8,128)S(1)} %get-tuple-element.44), channel_id=1, source_target_pairs={{0,16},{4,20},{8,24},{12,28},{16,0},{20,4},{24,8},{28,12},{1,17},{... | collective-permute-start | bytes 221192 | tf_op jit(solution)/shard_map/ppermute | solution.py:440
  7.6 1.3 %collective-permute-start.2 = (f32[48,384]{1,0:T(8,128)S(1)}, f32[48,384]{1,0:T(8,128)S(1)}, u32[]{:S(2)}, u32[]{:S(2)}) collective-permute-start(f32[48,384]{1,0:T(8,128)S(1)} %get-tuple-element.45), channel_id=1, source_target_pairs={{0,24},{4,28},{8,16},{12,20},{16,8},{20,12},{24,0},{28,4},{1,25},{... | collective-permute-start | bytes 221192 | tf_op jit(solution)/shard_map/ppermute | solution.py:440
  9.0 0.2 collective-permute-start.3
  9.2 3.2 %collective-permute-done.1.refs_1_ = f32[48,384]{1,0:T(8,128)S(1)} collective-permute-done((f32[48,384]{1,0:T(8,128)S(1)}, f32[48,384]{1,0:T(8,128)S(1)}, u32[]{:S(2)}, u32[]{:S(2)}) %collective-permute-start.1) | collective-permute-done | bytes 73760 | tf_op jit(solution)/shard_map/ppermute | solution.py:440
  12.4 0.5 collective-permute-start.4
  12.9 1.1 %collective-permute-done.2.refs_2_ = f32[48,384]{1,0:T(8,128)S(1)} collective-permute-done((f32[48,384]{1,0:T(8,128)S(1)}, f32[48,384]{1,0:T(8,128)S(1)}, u32[]{:S(2)}, u32[]{:S(2)}) %collective-permute-start.2) | collective-permute-done | bytes 73760 | tf_op jit(solution)/shard_map/ppermute | solution.py:440
  13.9 0.5 %collective-permute-start.5 = (f32[48,384]{1,0:T(8,128)S(1)}, f32[48,384]{1,0:T(8,128)S(1)}, u32[]{:S(2)}, u32[]{:S(2)}) collective-permute-start(f32[48,384]{1,0:T(8,128)S(1)} %collective-permute-done.2.refs_2_), channel_id=1, source_target_pairs={{0,4},{4,0},{8,12},{12,8},{16,20},{20,16},{24,28},{28,24},{1,5},{5... | collective-permute-start | bytes 221192 | tf_op jit(solution)/shard_map/ppermute | solution.py:443
  14.4 0.0 collective-permute-done.3.refs_3_
  14.5 1.5 %collective-permute-start.6 = (f32[48,384]{1,0:T(8,128)S(1)}, f32[48,384]{1,0:T(8,128)S(1)}, u32[]{:S(2)}, u32[]{:S(2)}) collective-permute-start(f32[48,384]{1,0:T(8,128)S(1)} %collective-permute-done.3.refs_3_), channel_id=1, source_target_pairs={{0,4},{4,0},{8,12},{12,8},{16,20},{20,16},{24,28},{28,24},{1,5},{5... | collective-permute-start | bytes 221192 | tf_op jit(solution)/shard_map/ppermute | solution.py:443
  16.0 1.0 %collective-permute-done.4.refs_4_ = f32[48,384]{1,0:T(8,128)S(1)} collective-permute-done((f32[48,384]{1,0:T(8,128)S(1)}, f32[48,384]{1,0:T(8,128)S(1)}, u32[]{:S(2)}, u32[]{:S(2)}) %collective-permute-start.4) | collective-permute-done | bytes 73760 | tf_op jit(solution)/shard_map/ppermute | solution.py:443
  17.0 1.1 %collective-permute-start.8 = (f32[192,128]{1,0:T(8,128)S(1)}, f32[192,128]{1,0:T(8,128)S(1)}, u32[]{:S(2)}, u32[]{:S(2)}) collective-permute-start(f32[192,128]{1,0:T(8,128)S(1)} %get-tuple-element.53), channel_id=1, source_target_pairs={{0,4},{4,0},{8,12},{12,8},{16,20},{20,16},{24,28},{28,24},{1,5},{5... | collective-permute-start | bytes 294920 | tf_op jit(solution)/shard_map/ppermute | solution.py:443
  18.1 0.9 %collective-permute-done.5.refs_5_ = f32[48,384]{1,0:T(8,128)S(1)} collective-permute-done((f32[48,384]{1,0:T(8,128)S(1)}, f32[48,384]{1,0:T(8,128)S(1)}, u32[]{:S(2)}, u32[]{:S(2)}) %collective-permute-start.5) | collective-permute-done | bytes 73760 | tf_op jit(solution)/shard_map/ppermute | solution.py:443
  19.0 0.0 copy-done.4
  19.0 0.7 %collective-permute-start.7 = (f32[576,128]{1,0:T(8,128)S(1)}, f32[576,128]{1,0:T(8,128)S(1)}, u32[]{:S(2)}, u32[]{:S(2)}) collective-permute-start(f32[576,128]{1,0:T(8,128)S(1)} %bitcast.19), channel_id=1, source_target_pairs={{0,4},{4,5},{5,1},{1,0},{8,12},{12,13},{13,9},{9,8},{16,20},{20,21... | collective-permute-start | bytes 884744 | tf_op jit(solution)/shard_map/ppermute | solution.py:490
  19.7 0.9 %collective-permute-done.6.refs_6_ = f32[48,384]{1,0:T(8,128)S(1)} collective-permute-done((f32[48,384]{1,0:T(8,128)S(1)}, f32[48,384]{1,0:T(8,128)S(1)}, u32[]{:S(2)}, u32[]{:S(2)}) %collective-permute-start.6) | collective-permute-done | bytes 73760 | tf_op jit(solution)/shard_map/ppermute | solution.py:443
  20.6 0.0 collective-permute-done.got_ref
  20.6 0.0 copy-done
  20.6 0.0 copy-done.1
  20.6 2.2 %products.1 = (f32[384,384]{1,0:T(8,128)S(1)}, f32[384,384]{1,0:T(8,128)S(1)}, f32[384,384]{1,0:T(8,128)S(1)}, f32[384,384]{1,0:T(8,128)S(1)}, f32[384,256]{1,0:...) custom-call(f32[576,128]{1,0:T(8,128)S(1)} %bitcast.13, ...), custom_call_target="tpu_custom_call" | custom-call | flops 679477248 | bytes 2359296 | tf_op jit(solution)/shard_map/products/pallas_call | solution.py:474
  22.8 0.0 collective-permute-done.8.corner_ref
  22.8 0.0 copy-start.5
  22.8 0.0 copy-start.6
  22.8 2.7 %begin.1.start_ref = f32[384,384]{1,0:T(8,128)S(1)} custom-call(f32[192,128]{1,0:T(8,128)S(1)} %collective-permute-done.8.corner_ref, f32[384,384]{1,0:T(8,128)S(1)} %get-tuple-element.54.power_ref, f32[384,384]{1,0:T(8,128)S(1)} %get-tuple-element.48.basis_ref), custom_call_target="tpu_custom_call" | custom-call | flops 2378170368 | bytes 2359296 | tf_op jit(solution)/shard_map/begin/pallas_call | solution.py:491
  25.5 0.0 collective-permute-done.7.other_left_ref
  25.5 0.0 copy-done.5
  25.5 0.0 copy-done.6
  25.5 3.3 %update.1 = (f32[576,128]{1,0:T(8,128)}, f32[576,128]{1,0:T(8,128)}, f32[4,48,384]{2,1,0:T(8,128)S(1)}, f32[384,256]{1,0:T(8,128)S(1)}, f32[384,384]{1,0:T(8,128)S(1)}) custom-call(f32[384,256]{1,0:T(8,128)S(1)} %get-tuple-element.47.inner_ref, f32[384,384]{1,0:T(8,128)S(1)} %get-tuple-element.48.basis_ref, f32[576,128]{1,0:T(8,128)S(1)} %get-tuple-element.49.left_ref, ...), custom_call_target="tpu_custom_call" | custom-call | flops 1698693120 | bytes 2359296 | tf_op jit(solution)/shard_map/update/pallas_call | solution.py:495
  28.8 0.9 %collective-permute-start.9 = (f32[4,48,384]{2,1,0:T(8,128)S(1)}, f32[4,48,384]{2,1,0:T(8,128)S(1)}, u32[]{:S(2)}, u32[]{:S(2)}) collective-permute-start(f32[4,48,384]{2,1,0:T(8,128)S(1)} %get-tuple-element.56), channel_id=1, source_target_pairs={{0,4},{4,0},{8,12},{12,8},{16,20},{20,16},{24,28},{28,24},{1,5},{5... | collective-permute-start | bytes 884744 | tf_op jit(solution)/shard_map/ppermute | solution.py:443
  29.7 5.8 %end.1 = (f32[384,384]{1,0:T(8,128)S(1)}, f32[384,384]{1,0:T(8,128)S(1)}, f32[576,128]{1,0:T(8,128)S(1)}, f32[4,48,384]{2,1,0:T(8,128)S(1)}) custom-call(f32[384,384]{1,0:T(8,128)S(1)} %get-tuple-element.57.start_ref, f32[384,256]{1,0:T(8,128)S(1)} %get-tuple-element.58.outer_ref, f32[384,256]{1,0:T(8,128)S(1)} %get-tuple-element.50.right_ref), custom_call_target="tpu_custom_call" | custom-call | flops 3057647616 | bytes 2359296 | tf_op jit(solution)/shard_map/end/pallas_call | solution.py:502
  35.4 1.2 %collective-permute-start.13 = (f32[576,128]{1,0:T(8,128)S(1)}, f32[576,128]{1,0:T(8,128)S(1)}, u32[]{:S(2)}, u32[]{:S(2)}) collective-permute-start(f32[576,128]{1,0:T(8,128)S(1)} %get-tuple-element.60), channel_id=1, source_target_pairs={{0,4},{4,0},{8,12},{12,8},{16,20},{20,16},{24,28},{28,24},{1,5},{5... | collective-permute-start | bytes 884744 | tf_op jit(solution)/shard_map/ppermute | solution.py:443
  36.7 0.4 collective-permute-done.9.theirs_ref
  37.1 3.3 %collective-permute-start.10 = (f32[48,384]{1,0:T(8,128)S(1)}, f32[48,384]{1,0:T(8,128)S(1)}, u32[]{:S(2)}, u32[]{:S(2)}) collective-permute-start(f32[48,384]{1,0:T(8,128)S(1)} %get-tuple-element.64), channel_id=1, source_target_pairs={{0,16},{4,20},{8,24},{12,28},{16,0},{20,4},{24,8},{28,12},{1,17},{... | collective-permute-start | bytes 221192 | tf_op jit(solution)/shard_map/ppermute | solution.py:440
  40.3 1.2 %collective-permute-start.11 = (f32[48,384]{1,0:T(8,128)S(1)}, f32[48,384]{1,0:T(8,128)S(1)}, u32[]{:S(2)}, u32[]{:S(2)}) collective-permute-start(f32[48,384]{1,0:T(8,128)S(1)} %get-tuple-element.65), channel_id=1, source_target_pairs={{0,24},{4,28},{8,16},{12,20},{16,8},{20,12},{24,0},{28,4},{1,25},{... | collective-permute-start | bytes 221192 | tf_op jit(solution)/shard_map/ppermute | solution.py:440
  41.6 0.5 %collective-permute-start.12 = (f32[48,384]{1,0:T(8,128)S(1)}, f32[48,384]{1,0:T(8,128)S(1)}, u32[]{:S(2)}, u32[]{:S(2)}) collective-permute-start(f32[48,384]{1,0:T(8,128)S(1)} %get-tuple-element.66), channel_id=1, source_target_pairs={{0,8},{4,12},{8,0},{12,4},{16,24},{20,28},{24,16},{28,20},{1,9},{5... | collective-permute-start | bytes 221192 | tf_op jit(solution)/shard_map/ppermute | solution.py:440
  42.1 2.1 %rest.1 = (f32[576,128]{1,0:T(8,128)S(1)}, f32[576,128]{1,0:T(8,128)}, f32[576,128]{1,0:T(8,128)}) custom-call(f32[384,384]{1,0:T(8,128)S(1)} %get-tuple-element.69.x_ref, f32[384,384]{1,0:T(8,128)S(1)} %get-tuple-element.70.poly_ref, f32[384,384]{1,0:T(8,128)S(1)} %get-tuple-element.71.grad_ref, f32[384,384]{1,0:T(8,128)S(1)} %get-tuple-element.72.new_stat_ref, ...), custom_call_target="tpu_custom_call" | custom-call | flops 509607936 | bytes 2359296 | tf_op jit(solution)/shard_map/rest/pallas_call | solution.py:511
  44.1 0.0 collective-permute-done.13.back_ref
  44.1 0.8 %bases.1 = (f32[576,128]{1,0:T(8,128)}, f32[576,128]{1,0:T(8,128)}) custom-call(f32[576,128]{1,0:T(8,128)S(1)} %get-tuple-element.76.keep_ref, f32[576,128]{1,0:T(8,128)S(1)} %collective-permute-done.13.back_ref), custom_call_target="tpu_custom_call" | custom-call | flops 33973864 | bytes 2359296 | tf_op jit(solution)/shard_map/bases/pallas_call | solution.py:533
  45.0 0.0 collective-permute-done.10.refs_1_
  45.0 1.7 %collective-permute-done.11.refs_2_ = f32[48,384]{1,0:T(8,128)S(1)} collective-permute-done((f32[48,384]{1,0:T(8,128)S(1)}, f32[48,384]{1,0:T(8,128)S(1)}, u32[]{:S(2)}, u32[]{:S(2)}) %collective-permute-start.11) | collective-permute-done | bytes 73760 | tf_op jit(solution)/shard_map/ppermute | solution.py:440
  46.6 0.1 collective-permute-done.12.refs_3_
  46.7 0.7 %rows.1 = f32[4,48,384]{2,1,0:T(8,128)} custom-call(f32[48,384]{1,0:T(8,128)S(1)} %get-tuple-element.63.refs_0_, f32[48,384]{1,0:T(8,128)S(1)} %collective-permute-done.10.refs_1_, f32[48,384]{1,0:T(8,128)S(1)} %collective-permute-done.11.refs_2_, f32[48,384]{1,0:T(8,128)S(1)} %collective-permute-done.12.refs_3_), custom_call_target="tpu_custom_call" | custom-call | flops 33973864 | bytes 2359296 | tf_op jit(solution)/shard_map/rows/pallas_call | solution.py:519
  (3 shorter events, 0.0 us)
Async XLA Ops:
  0.6 18.4 %copy-start.4 = (f32[1,73728]{1,0:T(1,128)S(1)}, f32[1,73728]{1,0:T(1,128)}, u32[]{:S(2)}) copy-start(f32[1,73728]{1,0:T(1,128)} %param.12) | copy-start | bytes 884740
  0.6 19.9 %copy-start = (f32[1,73728]{1,0:T(1,128)S(1)}, f32[1,73728]{1,0:T(1,128)}, u32[]{:S(2)}) copy-start(f32[1,73728]{1,0:T(1,128)} %param.10) | copy-start | bytes 884740
  0.7 19.9 %copy-start.1 = (f32[1,73728]{1,0:T(1,128)S(1)}, f32[1,73728]{1,0:T(1,128)}, u32[]{:S(2)}) copy-start(f32[1,73728]{1,0:T(1,128)} %param.11) | copy-start | bytes 884740
  0.7 19.9 %copy-start.2 = (f32[1,73728]{1,0:T(1,128)S(1)}, f32[1,73728]{1,0:T(1,128)}, u32[]{:S(2)}) copy-start(f32[1,73728]{1,0:T(1,128)} %param.13) | copy-start | bytes 884740
  0.7 19.9 %copy-start.3 = (f32[4,48,384]{2,1,0:T(8,128)S(1)}, f32[4,48,384]{2,1,0:T(8,128)}, u32[]{:S(2)}) copy-start(f32[4,48,384]{2,1,0:T(8,128)} %refs_0_.1) | copy-start | bytes 884740
  2.0 18.6 %collective-permute-start = (f32[720,128]{1,0:T(8,128)S(1)}, f32[720,128]{1,0:T(8,128)S(1)}, u32[]{:S(2)}, u32[]{:S(2)}) collective-permute-start(f32[720,128]{1,0:T(8,128)S(1)} %get-tuple-element.43), channel_id=1, source_target_pairs={{0,4},{4,0},{8,12},{12,8},{16,20},{20,16},{24,28},{28,24},{1,5},{5... | collective-permute-start | bytes 1105928 | tf_op jit(solution)/shard_map/ppermute | solution.py:443
  5.0 7.4 %collective-permute-start.1 = (f32[48,384]{1,0:T(8,128)S(1)}, f32[48,384]{1,0:T(8,128)S(1)}, u32[]{:S(2)}, u32[]{:S(2)}) collective-permute-start(f32[48,384]{1,0:T(8,128)S(1)} %get-tuple-element.44), channel_id=1, source_target_pairs={{0,16},{4,20},{8,24},{12,28},{16,0},{20,4},{24,8},{28,12},{1,17},{... | collective-permute-start | bytes 221192 | tf_op jit(solution)/shard_map/ppermute | solution.py:440
  7.6 6.3 %collective-permute-start.2 = (f32[48,384]{1,0:T(8,128)S(1)}, f32[48,384]{1,0:T(8,128)S(1)}, u32[]{:S(2)}, u32[]{:S(2)}) collective-permute-start(f32[48,384]{1,0:T(8,128)S(1)} %get-tuple-element.45), channel_id=1, source_target_pairs={{0,24},{4,28},{8,16},{12,20},{16,8},{20,12},{24,0},{28,4},{1,25},{... | collective-permute-start | bytes 221192 | tf_op jit(solution)/shard_map/ppermute | solution.py:440
  9.0 5.5 %collective-permute-start.3 = (f32[48,384]{1,0:T(8,128)S(1)}, f32[48,384]{1,0:T(8,128)S(1)}, u32[]{:S(2)}, u32[]{:S(2)}) collective-permute-start(f32[48,384]{1,0:T(8,128)S(1)} %get-tuple-element.46), channel_id=1, source_target_pairs={{0,8},{4,12},{8,0},{12,4},{16,24},{20,28},{24,16},{28,20},{1,9},{5... | collective-permute-start | bytes 221192 | tf_op jit(solution)/shard_map/ppermute | solution.py:440
  12.4 4.6 %collective-permute-start.4 = (f32[48,384]{1,0:T(8,128)S(1)}, f32[48,384]{1,0:T(8,128)S(1)}, u32[]{:S(2)}, u32[]{:S(2)}) collective-permute-start(f32[48,384]{1,0:T(8,128)S(1)} %collective-permute-done.1.refs_1_), channel_id=1, source_target_pairs={{0,4},{4,0},{8,12},{12,8},{16,20},{20,16},{24,28},{28,24},{1,5},{5... | collective-permute-start | bytes 221192 | tf_op jit(solution)/shard_map/ppermute | solution.py:443
  13.9 5.1 %collective-permute-start.5 = (f32[48,384]{1,0:T(8,128)S(1)}, f32[48,384]{1,0:T(8,128)S(1)}, u32[]{:S(2)}, u32[]{:S(2)}) collective-permute-start(f32[48,384]{1,0:T(8,128)S(1)} %collective-permute-done.2.refs_2_), channel_id=1, source_target_pairs={{0,4},{4,0},{8,12},{12,8},{16,20},{20,16},{24,28},{28,24},{1,5},{5... | collective-permute-start | bytes 221192 | tf_op jit(solution)/shard_map/ppermute | solution.py:443
  14.5 6.1 %collective-permute-start.6 = (f32[48,384]{1,0:T(8,128)S(1)}, f32[48,384]{1,0:T(8,128)S(1)}, u32[]{:S(2)}, u32[]{:S(2)}) collective-permute-start(f32[48,384]{1,0:T(8,128)S(1)} %collective-permute-done.3.refs_3_), channel_id=1, source_target_pairs={{0,4},{4,0},{8,12},{12,8},{16,20},{20,16},{24,28},{28,24},{1,5},{5... | collective-permute-start | bytes 221192 | tf_op jit(solution)/shard_map/ppermute | solution.py:443
  17.0 5.8 %collective-permute-start.8 = (f32[192,128]{1,0:T(8,128)S(1)}, f32[192,128]{1,0:T(8,128)S(1)}, u32[]{:S(2)}, u32[]{:S(2)}) collective-permute-start(f32[192,128]{1,0:T(8,128)S(1)} %get-tuple-element.53), channel_id=1, source_target_pairs={{0,4},{4,0},{8,12},{12,8},{16,20},{20,16},{24,28},{28,24},{1,5},{5... | collective-permute-start | bytes 294920 | tf_op jit(solution)/shard_map/ppermute | solution.py:443
  19.0 6.5 %collective-permute-start.7 = (f32[576,128]{1,0:T(8,128)S(1)}, f32[576,128]{1,0:T(8,128)S(1)}, u32[]{:S(2)}, u32[]{:S(2)}) collective-permute-start(f32[576,128]{1,0:T(8,128)S(1)} %bitcast.19), channel_id=1, source_target_pairs={{0,4},{4,5},{5,1},{1,0},{8,12},{12,13},{13,9},{9,8},{16,20},{20,21... | collective-permute-start | bytes 884744 | tf_op jit(solution)/shard_map/ppermute | solution.py:490
  22.8 2.7 %copy-start.5 = (f32[1,73728]{1,0:T(1,128)S(1)}, f32[1,73728]{1,0:T(1,128)}, u32[]{:S(2)}) copy-start(f32[1,73728]{1,0:T(1,128)} %param.8) | copy-start | bytes 884740
  22.8 2.7 %copy-start.6 = (f32[1,73728]{1,0:T(1,128)S(1)}, f32[1,73728]{1,0:T(1,128)}, u32[]{:S(2)}) copy-start(f32[1,73728]{1,0:T(1,128)} %param.9) | copy-start | bytes 884740
  28.8 8.3 %collective-permute-start.9 = (f32[4,48,384]{2,1,0:T(8,128)S(1)}, f32[4,48,384]{2,1,0:T(8,128)S(1)}, u32[]{:S(2)}, u32[]{:S(2)}) collective-permute-start(f32[4,48,384]{2,1,0:T(8,128)S(1)} %get-tuple-element.56), channel_id=1, source_target_pairs={{0,4},{4,0},{8,12},{12,8},{16,20},{20,16},{24,28},{28,24},{1,5},{5... | collective-permute-start | bytes 884744 | tf_op jit(solution)/shard_map/ppermute | solution.py:443
  35.4 8.7 %collective-permute-start.13 = (f32[576,128]{1,0:T(8,128)S(1)}, f32[576,128]{1,0:T(8,128)S(1)}, u32[]{:S(2)}, u32[]{:S(2)}) collective-permute-start(f32[576,128]{1,0:T(8,128)S(1)} %get-tuple-element.60), channel_id=1, source_target_pairs={{0,4},{4,0},{8,12},{12,8},{16,20},{20,16},{24,28},{28,24},{1,5},{5... | collective-permute-start | bytes 884744 | tf_op jit(solution)/shard_map/ppermute | solution.py:443
  37.1 7.9 %collective-permute-start.10 = (f32[48,384]{1,0:T(8,128)S(1)}, f32[48,384]{1,0:T(8,128)S(1)}, u32[]{:S(2)}, u32[]{:S(2)}) collective-permute-start(f32[48,384]{1,0:T(8,128)S(1)} %get-tuple-element.64), channel_id=1, source_target_pairs={{0,16},{4,20},{8,24},{12,28},{16,0},{20,4},{24,8},{28,12},{1,17},{... | collective-permute-start | bytes 221192 | tf_op jit(solution)/shard_map/ppermute | solution.py:440
  40.3 6.3 %collective-permute-start.11 = (f32[48,384]{1,0:T(8,128)S(1)}, f32[48,384]{1,0:T(8,128)S(1)}, u32[]{:S(2)}, u32[]{:S(2)}) collective-permute-start(f32[48,384]{1,0:T(8,128)S(1)} %get-tuple-element.65), channel_id=1, source_target_pairs={{0,24},{4,28},{8,16},{12,20},{16,8},{20,12},{24,0},{28,4},{1,25},{... | collective-permute-start | bytes 221192 | tf_op jit(solution)/shard_map/ppermute | solution.py:440
  41.6 5.1 %collective-permute-start.12 = (f32[48,384]{1,0:T(8,128)S(1)}, f32[48,384]{1,0:T(8,128)S(1)}, u32[]{:S(2)}, u32[]{:S(2)}) collective-permute-start(f32[48,384]{1,0:T(8,128)S(1)} %get-tuple-element.66), channel_id=1, source_target_pairs={{0,8},{4,12},{8,0},{12,4},{16,24},{20,28},{24,16},{28,20},{1,9},{5... | collective-permute-start | bytes 221192 | tf_op jit(solution)/shard_map/ppermute | solution.py:440

commit v14 on v13

--- a/solution.py
+++ b/solution.py
@@ -480,14 +480,8 @@
         "products",
     )(l_stat, r_stat, l_basis, r_basis, got, *rows)
     tensors = lax.axis_size("tensor")
-    place = lambda t, i: i * tensors + t
-    cycle = []
-    for t in range(0, tensors - tensors % 2, 2):
-        for i in range(0, size, 2):
-            cycle += [(place(t, i), place(t, i + 1)), (place(t, i + 1), place(t + 1, i + 1))]
-            cycle += [(place(t + 1, i + 1), place(t + 1, i)), (place(t + 1, i), place(t, i))]
-    cycle += [(place(t, i), place(t, i ^ 1)) for t in range(tensors - tensors % 2, tensors) for i in range(size)]
-    other_left = lax.ppermute(after(l_basis, *(theirs[:2] if near else mine)), ("shard", "tensor"), cycle)
+    one_way = [(i * tensors + t, (i ^ 1) * tensors + t) for i in range(size) for t in range(tensors) if (i + t) % 2 == 0]
+    other_left = lax.ppermute(after(l_basis, *(theirs[:2] if near else mine)), ("shard", "tensor"), one_way)
     (x,) = call(
         functools.partial(begin_kernel, EARLY_ITERS), [square], [(2, full // 2, LANES)], 7, full, "begin"
     )(got_corner, power, basis)

time: 47.6 us -> 48.1 us (1.011)
  starting transfers between devices: 18.6 us -> 20.3 us
  waiting for transfers between devices: 9.22 us -> 7.86 us
    ppermute x1, starting transfers between devices: 0.68 us -> 2.67 us  [local(): lax.ppermute(after(l_basis, *(theirs[:2] if near else mine)), ('shard', '...]
    ppermute x7, waiting for transfers between devices: 3.2 us -> 1.84 us  [partner(): return lax.ppermute(x, 'shard', pairs)]
  transfers between devices with their start and end apart: 14 -> 14, of which waited for: 8 -> 6; matrix products, arithmetic and copies ran while one was open for 0% -> 0% of each run, Pallas kernels for 29% -> 28%
where the time goes in v14:
time: 48.1 us; the launch traced here: 47.9 us
  starting transfers between devices  20.3 us (42%)
  Pallas kernels  18.9 us (39%)
  waiting for transfers between devices  7.86 us (16%)
  between operations  0.83 us (2%)
    ppermute x6, starting transfers between devices, hop_by(): return lax.ppermute(x, 'shard', [(i, i ^ 2 * hop) for i in range(size)])  8.93 us
    ppermute x7, starting transfers between devices, partner(): return lax.ppermute(x, 'shard', pairs)  8.73 us
    ppermute x6, waiting for transfers between devices, hop_by(): return lax.ppermute(x, 'shard', [(i, i ^ 2 * hop) for i in range(size)])  6.02 us
    pallas_call x1, Pallas kernels, local(): call(functools.partial(end_kernel, hops, NS_ITERS - EARLY_ITERS - 1), [sq...  5.78 us
    pallas_call x1, Pallas kernels, local(): call(functools.partial(update_kernel, hops), [flat, flat, strips, wide, s...  3.25 us
    ppermute x1, starting transfers between devices, local(): lax.ppermute(after(l_basis, *(theirs[:2] if near else mine)), ('shard', '...  2.67 us
    pallas_call x1, Pallas kernels, local(): call(functools.partial(begin_kernel, EARLY_ITERS), [square], [(2, full //...  2.66 us
    pallas_call x1, Pallas kernels, local(): call(functools.partial(products_kernel, hops), [square, square, square, s...  2.19 us
  transfers between devices with their start and end apart: 14, of which 6 were waited for; matrix products, arithmetic and copies ran while one was open for 0% of the time, Pallas kernels for 28%

profile of v14, /device:TPU:0, one launch (start us, length us, event | category | flops | bytes accessed | tf_op | source)
XLA Modules:
  0.0 47.9 jit_solution(11159496990993807607)
XLA Ops:
  0.6 0.0 copy-start.4
  0.6 0.0 copy-start
  0.7 0.0 copy-start.1
  0.7 0.0 copy-start.2
  0.7 0.0 copy-start.3
  0.7 1.3 %pack.1 = (f32[720,128]{1,0:T(8,128)S(1)}, f32[192,128]{1,0:T(8,128)S(1)}, f32[48,384]{1,0:T(8,128)S(1)}, f32[48,384]{1,0:T(8,128)S(1)}, f32[48,384]{1,0:T(8,128)S(1)}) custom-call(f32[576,128]{1,0:T(8,128)} %bitcast.12, f32[576,128]{1,0:T(8,128)} %bitcast.14, f32[576,128]{1,0:T(8,128)} %bitcast.18, f32[576,128]{1,0:T(8,128)} %bitcast.16, f32[4,48,384]{2,1,0:T(8,128)} %refs_0_.1), custom_call_target="tpu_custom_call" | custom-call | flops 33973864 | bytes 2359296 | tf_op jit(solution)/shard_map/pack/pallas_call | solution.py:450
  2.0 3.0 %collective-permute-start = (f32[720,128]{1,0:T(8,128)S(1)}, f32[720,128]{1,0:T(8,128)S(1)}, u32[]{:S(2)}, u32[]{:S(2)}) collective-permute-start(f32[720,128]{1,0:T(8,128)S(1)} %get-tuple-element.43), channel_id=1, source_target_pairs={{0,4},{4,0},{8,12},{12,8},{16,20},{20,16},{24,28},{28,24},{1,5},{5... | collective-permute-start | bytes 1105928 | tf_op jit(solution)/shard_map/ppermute | solution.py:443
  5.0 2.6 %collective-permute-start.1 = (f32[48,384]{1,0:T(8,128)S(1)}, f32[48,384]{1,0:T(8,128)S(1)}, u32[]{:S(2)}, u32[]{:S(2)}) collective-permute-start(f32[48,384]{1,0:T(8,128)S(1)} %get-tuple-element.44), channel_id=1, source_target_pairs={{0,16},{4,20},{8,24},{12,28},{16,0},{20,4},{24,8},{28,12},{1,17},{... | collective-permute-start | bytes 221192 | tf_op jit(solution)/shard_map/ppermute | solution.py:440
  7.6 1.3 %collective-permute-start.2 = (f32[48,384]{1,0:T(8,128)S(1)}, f32[48,384]{1,0:T(8,128)S(1)}, u32[]{:S(2)}, u32[]{:S(2)}) collective-permute-start(f32[48,384]{1,0:T(8,128)S(1)} %get-tuple-element.45), channel_id=1, source_target_pairs={{0,24},{4,28},{8,16},{12,20},{16,8},{20,12},{24,0},{28,4},{1,25},{... | collective-permute-start | bytes 221192 | tf_op jit(solution)/shard_map/ppermute | solution.py:440
  9.0 0.2 collective-permute-start.3
  9.2 3.2 %collective-permute-done.1.refs_1_ = f32[48,384]{1,0:T(8,128)S(1)} collective-permute-done((f32[48,384]{1,0:T(8,128)S(1)}, f32[48,384]{1,0:T(8,128)S(1)}, u32[]{:S(2)}, u32[]{:S(2)}) %collective-permute-start.1) | collective-permute-done | bytes 73760 | tf_op jit(solution)/shard_map/ppermute | solution.py:440
  12.4 0.5 collective-permute-start.4
  12.9 1.1 %collective-permute-done.2.refs_2_ = f32[48,384]{1,0:T(8,128)S(1)} collective-permute-done((f32[48,384]{1,0:T(8,128)S(1)}, f32[48,384]{1,0:T(8,128)S(1)}, u32[]{:S(2)}, u32[]{:S(2)}) %collective-permute-start.2) | collective-permute-done | bytes 73760 | tf_op jit(solution)/shard_map/ppermute | solution.py:440
  13.9 0.5 %collective-permute-start.5 = (f32[48,384]{1,0:T(8,128)S(1)}, f32[48,384]{1,0:T(8,128)S(1)}, u32[]{:S(2)}, u32[]{:S(2)}) collective-permute-start(f32[48,384]{1,0:T(8,128)S(1)} %collective-permute-done.2.refs_2_), channel_id=1, source_target_pairs={{0,4},{4,0},{8,12},{12,8},{16,20},{20,16},{24,28},{28,24},{1,5},{5... | collective-permute-start | bytes 221192 | tf_op jit(solution)/shard_map/ppermute | solution.py:443
  14.4 0.0 collective-permute-done.3.refs_3_
  14.5 1.5 %collective-permute-start.6 = (f32[48,384]{1,0:T(8,128)S(1)}, f32[48,384]{1,0:T(8,128)S(1)}, u32[]{:S(2)}, u32[]{:S(2)}) collective-permute-start(f32[48,384]{1,0:T(8,128)S(1)} %collective-permute-done.3.refs_3_), channel_id=1, source_target_pairs={{0,4},{4,0},{8,12},{12,8},{16,20},{20,16},{24,28},{28,24},{1,5},{5... | collective-permute-start | bytes 221192 | tf_op jit(solution)/shard_map/ppermute | solution.py:443
  16.0 1.0 %collective-permute-done.4.refs_4_ = f32[48,384]{1,0:T(8,128)S(1)} collective-permute-done((f32[48,384]{1,0:T(8,128)S(1)}, f32[48,384]{1,0:T(8,128)S(1)}, u32[]{:S(2)}, u32[]{:S(2)}) %collective-permute-start.4) | collective-permute-done | bytes 73760 | tf_op jit(solution)/shard_map/ppermute | solution.py:443
  17.0 1.1 %collective-permute-start.8 = (f32[192,128]{1,0:T(8,128)S(1)}, f32[192,128]{1,0:T(8,128)S(1)}, u32[]{:S(2)}, u32[]{:S(2)}) collective-permute-start(f32[192,128]{1,0:T(8,128)S(1)} %get-tuple-element.53), channel_id=1, source_target_pairs={{0,4},{4,0},{8,12},{12,8},{16,20},{20,16},{24,28},{28,24},{1,5},{5... | collective-permute-start | bytes 294920 | tf_op jit(solution)/shard_map/ppermute | solution.py:443
  18.1 0.8 %collective-permute-done.5.refs_5_ = f32[48,384]{1,0:T(8,128)S(1)} collective-permute-done((f32[48,384]{1,0:T(8,128)S(1)}, f32[48,384]{1,0:T(8,128)S(1)}, u32[]{:S(2)}, u32[]{:S(2)}) %collective-permute-start.5) | collective-permute-done | bytes 73760 | tf_op jit(solution)/shard_map/ppermute | solution.py:443
  18.9 0.0 copy-done.4
  18.9 2.7 %collective-permute-start.7 = (f32[576,128]{1,0:T(8,128)S(1)}, f32[576,128]{1,0:T(8,128)S(1)}, u32[]{:S(2)}, u32[]{:S(2)}) collective-permute-start(f32[576,128]{1,0:T(8,128)S(1)} %bitcast.19), channel_id=1, source_target_pairs={{0,4},{2,6},{5,1},{7,3},{8,12},{10,14},{13,9},{15,11},{16,20},{18,... | collective-permute-start | bytes 884744 | tf_op jit(solution)/shard_map/ppermute | solution.py:484
  21.6 0.0 collective-permute-done.6.refs_6_
  21.6 0.0 collective-permute-done.got_ref
  21.6 0.0 copy-done
  21.6 0.0 copy-done.1
  21.6 0.0 copy-done.2
  21.6 0.0 copy-done.3
  21.7 2.2 %products.1 = (f32[384,384]{1,0:T(8,128)S(1)}, f32[384,384]{1,0:T(8,128)S(1)}, f32[384,384]{1,0:T(8,128)S(1)}, f32[384,384]{1,0:T(8,128)S(1)}, f32[384,256]{1,0:...) custom-call(f32[576,128]{1,0:T(8,128)S(1)} %bitcast.13, ...), custom_call_target="tpu_custom_call" | custom-call | flops 679477248 | bytes 2359296 | tf_op jit(solution)/shard_map/products/pallas_call | solution.py:474
  23.9 0.0 collective-permute-done.8.corner_ref
  23.9 0.0 copy-start.5
  23.9 0.0 copy-start.6
  23.9 2.7 %begin.1.start_ref = f32[384,384]{1,0:T(8,128)S(1)} custom-call(f32[192,128]{1,0:T(8,128)S(1)} %collective-permute-done.8.corner_ref, f32[384,384]{1,0:T(8,128)S(1)} %get-tuple-element.54.power_ref, f32[384,384]{1,0:T(8,128)S(1)} %get-tuple-element.48.basis_ref), custom_call_target="tpu_custom_call" | custom-call | flops 2378170368 | bytes 2359296 | tf_op jit(solution)/shard_map/begin/pallas_call | solution.py:485
  26.6 0.0 collective-permute-done.7.other_left_ref
  26.6 3.3 %update.1 = (f32[576,128]{1,0:T(8,128)}, f32[576,128]{1,0:T(8,128)}, f32[4,48,384]{2,1,0:T(8,128)S(1)}, f32[384,256]{1,0:T(8,128)S(1)}, f32[384,384]{1,0:T(8,128)S(1)}) custom-call(f32[384,256]{1,0:T(8,128)S(1)} %get-tuple-element.47.inner_ref, f32[384,384]{1,0:T(8,128)S(1)} %get-tuple-element.48.basis_ref, f32[576,128]{1,0:T(8,128)S(1)} %get-tuple-element.49.left_ref, ...), custom_call_target="tpu_custom_call" | custom-call | flops 1698693120 | bytes 2359296 | tf_op jit(solution)/shard_map/update/pallas_call | solution.py:489
  29.8 1.7 %collective-permute-start.9 = (f32[4,48,384]{2,1,0:T(8,128)S(1)}, f32[4,48,384]{2,1,0:T(8,128)S(1)}, u32[]{:S(2)}, u32[]{:S(2)}) collective-permute-start(f32[4,48,384]{2,1,0:T(8,128)S(1)} %get-tuple-element.56), channel_id=1, source_target_pairs={{0,4},{4,0},{8,12},{12,8},{16,20},{20,16},{24,28},{28,24},{1,5},{5... | collective-permute-start | bytes 884744 | tf_op jit(solution)/shard_map/ppermute | solution.py:443
  31.5 5.8 %end.1 = (f32[384,384]{1,0:T(8,128)S(1)}, f32[384,384]{1,0:T(8,128)S(1)}, f32[576,128]{1,0:T(8,128)S(1)}, f32[4,48,384]{2,1,0:T(8,128)S(1)}) custom-call(f32[384,384]{1,0:T(8,128)S(1)} %get-tuple-element.57.start_ref, f32[384,256]{1,0:T(8,128)S(1)} %get-tuple-element.58.outer_ref, f32[384,256]{1,0:T(8,128)S(1)} %get-tuple-element.50.right_ref), custom_call_target="tpu_custom_call" | custom-call | flops 3057647616 | bytes 2359296 | tf_op jit(solution)/shard_map/end/pallas_call | solution.py:496
  37.3 0.4 collective-permute-start.13
  37.7 0.0 collective-permute-done.9.theirs_ref
  37.8 2.9 %collective-permute-start.10 = (f32[48,384]{1,0:T(8,128)S(1)}, f32[48,384]{1,0:T(8,128)S(1)}, u32[]{:S(2)}, u32[]{:S(2)}) collective-permute-start(f32[48,384]{1,0:T(8,128)S(1)} %get-tuple-element.64), channel_id=1, source_target_pairs={{0,16},{4,20},{8,24},{12,28},{16,0},{20,4},{24,8},{28,12},{1,17},{... | collective-permute-start | bytes 221192 | tf_op jit(solution)/shard_map/ppermute | solution.py:440
  40.7 1.4 %collective-permute-start.11 = (f32[48,384]{1,0:T(8,128)S(1)}, f32[48,384]{1,0:T(8,128)S(1)}, u32[]{:S(2)}, u32[]{:S(2)}) collective-permute-start(f32[48,384]{1,0:T(8,128)S(1)} %get-tuple-element.65), channel_id=1, source_target_pairs={{0,24},{4,28},{8,16},{12,20},{16,8},{20,12},{24,0},{28,4},{1,25},{... | collective-permute-start | bytes 221192 | tf_op jit(solution)/shard_map/ppermute | solution.py:440
  42.0 0.5 %collective-permute-start.12 = (f32[48,384]{1,0:T(8,128)S(1)}, f32[48,384]{1,0:T(8,128)S(1)}, u32[]{:S(2)}, u32[]{:S(2)}) collective-permute-start(f32[48,384]{1,0:T(8,128)S(1)} %get-tuple-element.66), channel_id=1, source_target_pairs={{0,8},{4,12},{8,0},{12,4},{16,24},{20,28},{24,16},{28,20},{1,9},{5... | collective-permute-start | bytes 221192 | tf_op jit(solution)/shard_map/ppermute | solution.py:440
  42.5 2.1 %rest.1 = (f32[576,128]{1,0:T(8,128)S(1)}, f32[576,128]{1,0:T(8,128)}, f32[576,128]{1,0:T(8,128)}) custom-call(f32[384,384]{1,0:T(8,128)S(1)} %get-tuple-element.69.x_ref, f32[384,384]{1,0:T(8,128)S(1)} %get-tuple-element.70.poly_ref, f32[384,384]{1,0:T(8,128)S(1)} %get-tuple-element.71.grad_ref, f32[384,384]{1,0:T(8,128)S(1)} %get-tuple-element.72.new_stat_ref, ...), custom_call_target="tpu_custom_call" | custom-call | flops 509607936 | bytes 2359296 | tf_op jit(solution)/shard_map/rest/pallas_call | solution.py:505
  44.6 0.0 collective-permute-done.13.back_ref
  44.6 0.8 %bases.1 = (f32[576,128]{1,0:T(8,128)}, f32[576,128]{1,0:T(8,128)}) custom-call(f32[576,128]{1,0:T(8,128)S(1)} %get-tuple-element.76.keep_ref, f32[576,128]{1,0:T(8,128)S(1)} %collective-permute-done.13.back_ref), custom_call_target="tpu_custom_call" | custom-call | flops 33973864 | bytes 2359296 | tf_op jit(solution)/shard_map/bases/pallas_call | solution.py:527
  45.4 0.0 collective-permute-done.10.refs_1_
  45.4 1.5 %collective-permute-done.11.refs_2_ = f32[48,384]{1,0:T(8,128)S(1)} collective-permute-done((f32[48,384]{1,0:T(8,128)S(1)}, f32[48,384]{1,0:T(8,128)S(1)}, u32[]{:S(2)}, u32[]{:S(2)}) %collective-permute-start.11) | collective-permute-done | bytes 73760 | tf_op jit(solution)/shard_map/ppermute | solution.py:440
  47.0 0.2 collective-permute-done.12.refs_3_
  47.2 0.7 %rows.1 = f32[4,48,384]{2,1,0:T(8,128)} custom-call(f32[48,384]{1,0:T(8,128)S(1)} %get-tuple-element.63.refs_0_, f32[48,384]{1,0:T(8,128)S(1)} %collective-permute-done.10.refs_1_, f32[48,384]{1,0:T(8,128)S(1)} %collective-permute-done.11.refs_2_, f32[48,384]{1,0:T(8,128)S(1)} %collective-permute-done.12.refs_3_), custom_call_target="tpu_custom_call" | custom-call | flops 33973864 | bytes 2359296 | tf_op jit(solution)/shard_map/rows/pallas_call | solution.py:513
  (3 shorter events, 0.0 us)
Async XLA Ops:
  0.6 18.3 %copy-start.4 = (f32[1,73728]{1,0:T(1,128)S(1)}, f32[1,73728]{1,0:T(1,128)}, u32[]{:S(2)}) copy-start(f32[1,73728]{1,0:T(1,128)} %param.12) | copy-start | bytes 884740
  0.6 21.0 %copy-start = (f32[1,73728]{1,0:T(1,128)S(1)}, f32[1,73728]{1,0:T(1,128)}, u32[]{:S(2)}) copy-start(f32[1,73728]{1,0:T(1,128)} %param.10) | copy-start | bytes 884740
  0.7 21.0 %copy-start.1 = (f32[1,73728]{1,0:T(1,128)S(1)}, f32[1,73728]{1,0:T(1,128)}, u32[]{:S(2)}) copy-start(f32[1,73728]{1,0:T(1,128)} %param.11) | copy-start | bytes 884740
  0.7 21.0 %copy-start.2 = (f32[1,73728]{1,0:T(1,128)S(1)}, f32[1,73728]{1,0:T(1,128)}, u32[]{:S(2)}) copy-start(f32[1,73728]{1,0:T(1,128)} %param.13) | copy-start | bytes 884740
  0.7 21.0 %copy-start.3 = (f32[4,48,384]{2,1,0:T(8,128)S(1)}, f32[4,48,384]{2,1,0:T(8,128)}, u32[]{:S(2)}) copy-start(f32[4,48,384]{2,1,0:T(8,128)} %refs_0_.1) | copy-start | bytes 884740
  2.0 19.6 %collective-permute-start = (f32[720,128]{1,0:T(8,128)S(1)}, f32[720,128]{1,0:T(8,128)S(1)}, u32[]{:S(2)}, u32[]{:S(2)}) collective-permute-start(f32[720,128]{1,0:T(8,128)S(1)} %get-tuple-element.43), channel_id=1, source_target_pairs={{0,4},{4,0},{8,12},{12,8},{16,20},{20,16},{24,28},{28,24},{1,5},{5... | collective-permute-start | bytes 1105928 | tf_op jit(solution)/shard_map/ppermute | solution.py:443
  5.0 7.4 %collective-permute-start.1 = (f32[48,384]{1,0:T(8,128)S(1)}, f32[48,384]{1,0:T(8,128)S(1)}, u32[]{:S(2)}, u32[]{:S(2)}) collective-permute-start(f32[48,384]{1,0:T(8,128)S(1)} %get-tuple-element.44), channel_id=1, source_target_pairs={{0,16},{4,20},{8,24},{12,28},{16,0},{20,4},{24,8},{28,12},{1,17},{... | collective-permute-start | bytes 221192 | tf_op jit(solution)/shard_map/ppermute | solution.py:440
  7.6 6.3 %collective-permute-start.2 = (f32[48,384]{1,0:T(8,128)S(1)}, f32[48,384]{1,0:T(8,128)S(1)}, u32[]{:S(2)}, u32[]{:S(2)}) collective-permute-start(f32[48,384]{1,0:T(8,128)S(1)} %get-tuple-element.45), channel_id=1, source_target_pairs={{0,24},{4,28},{8,16},{12,20},{16,8},{20,12},{24,0},{28,4},{1,25},{... | collective-permute-start | bytes 221192 | tf_op jit(solution)/shard_map/ppermute | solution.py:440
  9.0 5.5 %collective-permute-start.3 = (f32[48,384]{1,0:T(8,128)S(1)}, f32[48,384]{1,0:T(8,128)S(1)}, u32[]{:S(2)}, u32[]{:S(2)}) collective-permute-start(f32[48,384]{1,0:T(8,128)S(1)} %get-tuple-element.46), channel_id=1, source_target_pairs={{0,8},{4,12},{8,0},{12,4},{16,24},{20,28},{24,16},{28,20},{1,9},{5... | collective-permute-start | bytes 221192 | tf_op jit(solution)/shard_map/ppermute | solution.py:440
  12.4 4.6 %collective-permute-start.4 = (f32[48,384]{1,0:T(8,128)S(1)}, f32[48,384]{1,0:T(8,128)S(1)}, u32[]{:S(2)}, u32[]{:S(2)}) collective-permute-start(f32[48,384]{1,0:T(8,128)S(1)} %collective-permute-done.1.refs_1_), channel_id=1, source_target_pairs={{0,4},{4,0},{8,12},{12,8},{16,20},{20,16},{24,28},{28,24},{1,5},{5... | collective-permute-start | bytes 221192 | tf_op jit(solution)/shard_map/ppermute | solution.py:443
  13.9 5.0 %collective-permute-start.5 = (f32[48,384]{1,0:T(8,128)S(1)}, f32[48,384]{1,0:T(8,128)S(1)}, u32[]{:S(2)}, u32[]{:S(2)}) collective-permute-start(f32[48,384]{1,0:T(8,128)S(1)} %collective-permute-done.2.refs_2_), channel_id=1, source_target_pairs={{0,4},{4,0},{8,12},{12,8},{16,20},{20,16},{24,28},{28,24},{1,5},{5... | collective-permute-start | bytes 221192 | tf_op jit(solution)/shard_map/ppermute | solution.py:443
  14.5 7.1 %collective-permute-start.6 = (f32[48,384]{1,0:T(8,128)S(1)}, f32[48,384]{1,0:T(8,128)S(1)}, u32[]{:S(2)}, u32[]{:S(2)}) collective-permute-start(f32[48,384]{1,0:T(8,128)S(1)} %collective-permute-done.3.refs_3_), channel_id=1, source_target_pairs={{0,4},{4,0},{8,12},{12,8},{16,20},{20,16},{24,28},{28,24},{1,5},{5... | collective-permute-start | bytes 221192 | tf_op jit(solution)/shard_map/ppermute | solution.py:443
  17.0 6.9 %collective-permute-start.8 = (f32[192,128]{1,0:T(8,128)S(1)}, f32[192,128]{1,0:T(8,128)S(1)}, u32[]{:S(2)}, u32[]{:S(2)}) collective-permute-start(f32[192,128]{1,0:T(8,128)S(1)} %get-tuple-element.53), channel_id=1, source_target_pairs={{0,4},{4,0},{8,12},{12,8},{16,20},{20,16},{24,28},{28,24},{1,5},{5... | collective-permute-start | bytes 294920 | tf_op jit(solution)/shard_map/ppermute | solution.py:443
  18.9 7.6 %collective-permute-start.7 = (f32[576,128]{1,0:T(8,128)S(1)}, f32[576,128]{1,0:T(8,128)S(1)}, u32[]{:S(2)}, u32[]{:S(2)}) collective-permute-start(f32[576,128]{1,0:T(8,128)S(1)} %bitcast.19), channel_id=1, source_target_pairs={{0,4},{2,6},{5,1},{7,3},{8,12},{10,14},{13,9},{15,11},{16,20},{18,... | collective-permute-start | bytes 884744 | tf_op jit(solution)/shard_map/ppermute | solution.py:484
  23.9 2.7 %copy-start.5 = (f32[1,73728]{1,0:T(1,128)S(1)}, f32[1,73728]{1,0:T(1,128)}, u32[]{:S(2)}) copy-start(f32[1,73728]{1,0:T(1,128)} %param.8) | copy-start | bytes 884740
  23.9 2.7 %copy-start.6 = (f32[1,73728]{1,0:T(1,128)S(1)}, f32[1,73728]{1,0:T(1,128)}, u32[]{:S(2)}) copy-start(f32[1,73728]{1,0:T(1,128)} %param.9) | copy-start | bytes 884740
  29.8 7.9 %collective-permute-start.9 = (f32[4,48,384]{2,1,0:T(8,128)S(1)}, f32[4,48,384]{2,1,0:T(8,128)S(1)}, u32[]{:S(2)}, u32[]{:S(2)}) collective-permute-start(f32[4,48,384]{2,1,0:T(8,128)S(1)} %get-tuple-element.56), channel_id=1, source_target_pairs={{0,4},{4,0},{8,12},{12,8},{16,20},{20,16},{24,28},{28,24},{1,5},{5... | collective-permute-start | bytes 884744 | tf_op jit(solution)/shard_map/ppermute | solution.py:443
  37.3 7.3 %collective-permute-start.13 = (f32[576,128]{1,0:T(8,128)S(1)}, f32[576,128]{1,0:T(8,128)S(1)}, u32[]{:S(2)}, u32[]{:S(2)}) collective-permute-start(f32[576,128]{1,0:T(8,128)S(1)} %get-tuple-element.60), channel_id=1, source_target_pairs={{0,4},{4,0},{8,12},{12,8},{16,20},{20,16},{24,28},{28,24},{1,5},{5... | collective-permute-start | bytes 884744 | tf_op jit(solution)/shard_map/ppermute | solution.py:443
  37.8 7.7 %collective-permute-start.10 = (f32[48,384]{1,0:T(8,128)S(1)}, f32[48,384]{1,0:T(8,128)S(1)}, u32[]{:S(2)}, u32[]{:S(2)}) collective-permute-start(f32[48,384]{1,0:T(8,128)S(1)} %get-tuple-element.64), channel_id=1, source_target_pairs={{0,16},{4,20},{8,24},{12,28},{16,0},{20,4},{24,8},{28,12},{1,17},{... | collective-permute-start | bytes 221192 | tf_op jit(solution)/shard_map/ppermute | solution.py:440
  40.7 6.3 %collective-permute-start.11 = (f32[48,384]{1,0:T(8,128)S(1)}, f32[48,384]{1,0:T(8,128)S(1)}, u32[]{:S(2)}, u32[]{:S(2)}) collective-permute-start(f32[48,384]{1,0:T(8,128)S(1)} %get-tuple-element.65), channel_id=1, source_target_pairs={{0,24},{4,28},{8,16},{12,20},{16,8},{20,12},{24,0},{28,4},{1,25},{... | collective-permute-start | bytes 221192 | tf_op jit(solution)/shard_map/ppermute | solution.py:440
  42.0 5.1 %collective-permute-start.12 = (f32[48,384]{1,0:T(8,128)S(1)}, f32[48,384]{1,0:T(8,128)S(1)}, u32[]{:S(2)}, u32[]{:S(2)}) collective-permute-start(f32[48,384]{1,0:T(8,128)S(1)} %get-tuple-element.66), channel_id=1, source_target_pairs={{0,8},{4,12},{8,0},{12,4},{16,24},{20,28},{24,16},{28,20},{1,9},{5... | collective-permute-start | bytes 221192 | tf_op jit(solution)/shard_map/ppermute | solution.py:440

commit v15 on v13

--- a/solution.py
+++ b/solution.py
@@ -231,17 +231,30 @@
     return x
 
 
-def products_kernel(hops, l_stat_ref, r_stat_ref, l_basis_ref, r_basis_ref, got_ref, *refs):
+def prepare_kernel(
+    l_stat_ref, r_stat_ref, l_basis_ref, r_basis_ref, got_ref, basis_ref, known_ref, right_ref, other_ref, copy_ref, scratch
+):
+    left, first = is_left(), is_first()
+    own = pick(left, thirds(l_basis_ref), thirds(r_basis_ref))
+    got = thirds(got_ref, 0, l_basis_ref.shape[0])
+    basis_ref[...] = whole_of(scratch, pick(first, own, got), pick(first, got, own))
+    known_ref[...] = 0.5 * known_part(first, pick(left, thirds(l_stat_ref), thirds(r_stat_ref)), scratch)
+    right_ref[...] = half_of(scratch, thirds(r_basis_ref))
+    other_ref[...] = jnp.where(left, r_stat_ref[...], l_stat_ref[...])
+    copy_ref[...] = l_basis_ref[...]
+
+
+def products_kernel(hops, basis_ref, known_ref, right_ref, got_ref, *refs):
     left = is_left()
-    outs = refs[-9:]
-    grad_ref, stat_ref, power_ref, basis_ref, right_ref, inner_ref, other_ref, copy_ref, scratch = outs
+    grad_ref, stat_ref, power_ref, inner_ref = refs[-4:]
     if hops:
         grads_ref, mine_refs, theirs_refs = refs[0], refs[1 : 1 + len(hops)], refs[1 + len(hops) : 1 + 2 * len(hops)]
         rows = grads_ref.shape[1]
         here = lax.axis_index("shard") // 2
         parity = lax.axis_index("shard") % 2
-        start = l_basis_ref.shape[0]
-        received = [got_ref[pl.ds(start + k * rows, rows), :] for k in range(grad_ref.shape[1] // LANES)]
+        blocks = grad_ref.shape[1] // LANES
+        start = got_ref.shape[0] - blocks * rows
+        received = [got_ref[pl.ds(start + k * rows, rows), :] for k in range(blocks)]
         place_rows(grad_ref, 2 * here + parity, rows, grads_ref[here])
         place_rows(grad_ref, 2 * here + 1 - parity, rows, jnp.concatenate(received, axis=1))
         for hop, mine, theirs in zip(hops, mine_refs, theirs_refs):
@@ -249,22 +262,12 @@
             place_rows(grad_ref, 2 * (here ^ hop) + 1 - parity, rows, theirs[...])
     else:
         grad_ref[...] = refs[0][...]
-    own = pick(left, thirds(l_basis_ref), thirds(r_basis_ref))
-    got = thirds(got_ref, 0, l_basis_ref.shape[0])
-    first = is_first()
-    basis = whole_of(scratch, pick(first, own, got), pick(first, got, own))
-    basis_ref[...] = basis
-    known = known_part(first, pick(left, thirds(l_stat_ref), thirds(r_stat_ref)), scratch)
-    other_ref[...] = jnp.where(left, r_stat_ref[...], l_stat_ref[...])
-    copy_ref[...] = l_basis_ref[...]
-    right = half_of(scratch, thirds(r_basis_ref))
-    right_ref[...] = right
     grad = grad_ref[...]
     parts = split(jnp.where(left, grad, grad.T))
-    stat = 0.5 * known + 0.5 * symmetric_dot(parts, parts, ((1,), (1,)))
+    stat = known_ref[...] + 0.5 * symmetric_dot(parts, parts, ((1,), (1,)))
     stat_ref[...] = stat
-    power_ref[...] = dot(stat, basis)
-    inner_ref[...] = dot(grad, right)
+    power_ref[...] = dot(stat, basis_ref[...])
+    inner_ref[...] = dot(grad, right_ref[...])
 
 
 def begin_kernel(steps, corner_ref, power_ref, basis_ref, x_ref, scratch):
@@ -471,14 +474,13 @@
         rows = (jnp.stack([even, odd], axis=1).reshape(square),)
         mine = [mine]
     got_corner = partner(after(corner, theirs[0] if near else mine[0]))
-    grad, new_stat, power, basis, right, inner, other, left = call(
-        functools.partial(products_kernel, hops),
-        [square, square, square, square, (full, 2 * LANES), (full, 2 * LANES), flat, flat],
-        [(3, full, LANES)],
-        2,
-        full,
-        "products",
-    )(l_stat, r_stat, l_basis, r_basis, got, *rows)
+    wide = (full, 2 * LANES)
+    basis, known, right, other, left = call(
+        prepare_kernel, [square, square, wide, flat, flat], [(3, full, LANES)], 0.1, full, "prepare"
+    )(l_stat, r_stat, l_basis, r_basis, got)
+    grad, new_stat, power, inner = call(
+        functools.partial(products_kernel, hops), [square, square, square, wide], [], 3, full, "products"
+    )(basis, known, right, got, *rows)
     tensors = lax.axis_size("tensor")
     place = lambda t, i: i * tensors + t
     cycle = []
@@ -487,11 +489,10 @@
             cycle += [(place(t, i), place(t, i + 1)), (place(t, i + 1), place(t + 1, i + 1))]
             cycle += [(place(t + 1, i + 1), place(t + 1, i)), (place(t + 1, i), place(t, i))]
     cycle += [(place(t, i), place(t, i ^ 1)) for t in range(tensors - tensors % 2, tensors) for i in range(size)]
-    other_left = lax.ppermute(after(l_basis, *(theirs[:2] if near else mine)), ("shard", "tensor"), cycle)
+    other_left = lax.ppermute(after(l_basis, basis, *(theirs[:2] if near else mine)), ("shard", "tensor"), cycle)
     (x,) = call(
         functools.partial(begin_kernel, EARLY_ITERS), [square], [(2, full // 2, LANES)], 7, full, "begin"
     )(got_corner, power, basis)
-    wide = (full, 2 * LANES)
     new_one, new_two, other_rows, outer, x = call(
         functools.partial(update_kernel, hops), [flat, flat, strips, wide, square], [(3, full, LANES)], 5, full, "update"
     )(inner, basis, left, right, other_left, one, two, x)

time: 47.6 us -> 47.5 us (level)
  waiting for transfers between devices: 9.22 us -> 8.18 us
  starting transfers between devices: 18.6 us -> 19.1 us
    ppermute x7, waiting for transfers between devices: 3.2 us -> 2.15 us  [partner(): return lax.ppermute(x, 'shard', pairs)]
    pallas_call x1 -> x2, Pallas kernels: 2.19 us -> 2.67 us  [the longest x1 1.94 us: local(): call(functools.partial(products_kernel, hops), [square, square, square, w...]
  transfers between devices with their start and end apart: 14 -> 14, of which waited for: 8 -> 7; matrix products, arithmetic and copies ran while one was open for 0% -> 0% of each run, Pallas kernels for 29% -> 30%
where the time goes in v15:
time: 47.5 us; the launch traced here: 47.3 us
  Pallas kernels  19.3 us (41%)
  starting transfers between devices  19.1 us (40%)
  waiting for transfers between devices  8.18 us (17%)
  between operations  0.77 us (2%)
    ppermute x6, starting transfers between devices, hop_by(): return lax.ppermute(x, 'shard', [(i, i ^ 2 * hop) for i in range(size)])  9.47 us
    ppermute x7, starting transfers between devices, partner(): return lax.ppermute(x, 'shard', pairs)  8.74 us
    ppermute x6, waiting for transfers between devices, hop_by(): return lax.ppermute(x, 'shard', [(i, i ^ 2 * hop) for i in range(size)])  6.02 us
    pallas_call x1, Pallas kernels, local(): call(functools.partial(end_kernel, hops, NS_ITERS - EARLY_ITERS - 1), [sq...  5.77 us
    pallas_call x1, Pallas kernels, local(): call(functools.partial(update_kernel, hops), [flat, flat, strips, wide, s...  3.21 us
    pallas_call x1, Pallas kernels, local(): call(functools.partial(begin_kernel, EARLY_ITERS), [square], [(2, full //...  2.66 us
    ppermute x7, waiting for transfers between devices, partner(): return lax.ppermute(x, 'shard', pairs)  2.15 us
    pallas_call x1, Pallas kernels, local(): call(rest_kernel, [flat, flat, flat], [(3, full, LANES)], 1.5, full, 'rest')  2.06 us
  transfers between devices with their start and end apart: 14, of which 7 were waited for; matrix products, arithmetic and copies ran while one was open for 0% of the time, Pallas kernels for 30%

profile of v15, /device:TPU:0, one launch (start us, length us, event | category | flops | bytes accessed | tf_op | source)
XLA Modules:
  0.0 47.3 jit_solution(17852090453688399343)
XLA Ops:
  0.6 0.0 copy-start
  0.6 0.0 copy-start.1
  0.7 0.0 copy-start.2
  0.7 0.0 copy-start.3
  0.7 1.3 %pack.1 = (f32[720,128]{1,0:T(8,128)S(1)}, f32[192,128]{1,0:T(8,128)S(1)}, f32[48,384]{1,0:T(8,128)S(1)}, f32[48,384]{1,0:T(8,128)S(1)}, f32[48,384]{1,0:T(8,128)S(1)}) custom-call(f32[576,128]{1,0:T(8,128)} %bitcast.12, f32[576,128]{1,0:T(8,128)} %bitcast.14, f32[576,128]{1,0:T(8,128)} %bitcast.18, f32[576,128]{1,0:T(8,128)} %bitcast.16, f32[4,48,384]{2,1,0:T(8,128)} %refs_0_.1), custom_call_target="tpu_custom_call" | custom-call | flops 33973864 | bytes 2359296 | tf_op jit(solution)/shard_map/pack/pallas_call | solution.py:453
  2.0 3.0 %collective-permute-start = (f32[720,128]{1,0:T(8,128)S(1)}, f32[720,128]{1,0:T(8,128)S(1)}, u32[]{:S(2)}, u32[]{:S(2)}) collective-permute-start(f32[720,128]{1,0:T(8,128)S(1)} %get-tuple-element.44), channel_id=1, source_target_pairs={{0,4},{4,0},{8,12},{12,8},{16,20},{20,16},{24,28},{28,24},{1,5},{5... | collective-permute-start | bytes 1105928 | tf_op jit(solution)/shard_map/ppermute | solution.py:446
  5.0 2.6 %collective-permute-start.1 = (f32[48,384]{1,0:T(8,128)S(1)}, f32[48,384]{1,0:T(8,128)S(1)}, u32[]{:S(2)}, u32[]{:S(2)}) collective-permute-start(f32[48,384]{1,0:T(8,128)S(1)} %get-tuple-element.48), channel_id=1, source_target_pairs={{0,16},{4,20},{8,24},{12,28},{16,0},{20,4},{24,8},{28,12},{1,17},{... | collective-permute-start | bytes 221192 | tf_op jit(solution)/shard_map/ppermute | solution.py:443
  7.6 1.3 %collective-permute-start.2 = (f32[48,384]{1,0:T(8,128)S(1)}, f32[48,384]{1,0:T(8,128)S(1)}, u32[]{:S(2)}, u32[]{:S(2)}) collective-permute-start(f32[48,384]{1,0:T(8,128)S(1)} %get-tuple-element.49), channel_id=1, source_target_pairs={{0,24},{4,28},{8,16},{12,20},{16,8},{20,12},{24,0},{28,4},{1,25},{... | collective-permute-start | bytes 221192 | tf_op jit(solution)/shard_map/ppermute | solution.py:443
  8.9 0.2 collective-permute-start.3
  9.2 3.2 %collective-permute-done.1.refs_1_ = f32[48,384]{1,0:T(8,128)S(1)} collective-permute-done((f32[48,384]{1,0:T(8,128)S(1)}, f32[48,384]{1,0:T(8,128)S(1)}, u32[]{:S(2)}, u32[]{:S(2)}) %collective-permute-start.1) | collective-permute-done | bytes 73760 | tf_op jit(solution)/shard_map/ppermute | solution.py:443
  12.4 0.5 collective-permute-start.4
  12.9 1.1 %collective-permute-done.2.refs_2_ = f32[48,384]{1,0:T(8,128)S(1)} collective-permute-done((f32[48,384]{1,0:T(8,128)S(1)}, f32[48,384]{1,0:T(8,128)S(1)}, u32[]{:S(2)}, u32[]{:S(2)}) %collective-permute-start.2) | collective-permute-done | bytes 73760 | tf_op jit(solution)/shard_map/ppermute | solution.py:443
  13.9 0.5 %collective-permute-start.5 = (f32[48,384]{1,0:T(8,128)S(1)}, f32[48,384]{1,0:T(8,128)S(1)}, u32[]{:S(2)}, u32[]{:S(2)}) collective-permute-start(f32[48,384]{1,0:T(8,128)S(1)} %collective-permute-done.2.refs_2_), channel_id=1, source_target_pairs={{0,4},{4,0},{8,12},{12,8},{16,20},{20,16},{24,28},{28,24},{1,5},{5... | collective-permute-start | bytes 221192 | tf_op jit(solution)/shard_map/ppermute | solution.py:446
  14.4 0.0 collective-permute-done.3.refs_3_
  14.4 1.5 %collective-permute-start.6 = (f32[48,384]{1,0:T(8,128)S(1)}, f32[48,384]{1,0:T(8,128)S(1)}, u32[]{:S(2)}, u32[]{:S(2)}) collective-permute-start(f32[48,384]{1,0:T(8,128)S(1)} %collective-permute-done.3.refs_3_), channel_id=1, source_target_pairs={{0,4},{4,0},{8,12},{12,8},{16,20},{20,16},{24,28},{28,24},{1,5},{5... | collective-permute-start | bytes 221192 | tf_op jit(solution)/shard_map/ppermute | solution.py:446
  15.9 1.0 %collective-permute-done.4.refs_4_ = f32[48,384]{1,0:T(8,128)S(1)} collective-permute-done((f32[48,384]{1,0:T(8,128)S(1)}, f32[48,384]{1,0:T(8,128)S(1)}, u32[]{:S(2)}, u32[]{:S(2)}) %collective-permute-start.4) | collective-permute-done | bytes 73760 | tf_op jit(solution)/shard_map/ppermute | solution.py:446
  17.0 1.1 %collective-permute-start.8 = (f32[192,128]{1,0:T(8,128)S(1)}, f32[192,128]{1,0:T(8,128)S(1)}, u32[]{:S(2)}, u32[]{:S(2)}) collective-permute-start(f32[192,128]{1,0:T(8,128)S(1)} %get-tuple-element.55), channel_id=1, source_target_pairs={{0,4},{4,0},{8,12},{12,8},{16,20},{20,16},{24,28},{28,24},{1,5},{5... | collective-permute-start | bytes 294920 | tf_op jit(solution)/shard_map/ppermute | solution.py:446
  18.1 0.0 collective-permute-done.got_ref
  18.1 0.0 copy-done
  18.1 0.0 copy-done.1
  18.1 0.0 copy-done.2
  18.1 0.0 copy-done.3
  18.1 0.7 %prepare.1 = (f32[384,384]{1,0:T(8,128)S(1)}, f32[384,384]{1,0:T(8,128)S(1)}, f32[384,256]{1,0:T(8,128)S(1)}, f32[576,128]{1,0:T(8,128)S(1)}, f32[576,128]{1,0:T(8,128)S(1)}) custom-call(f32[576,128]{1,0:T(8,128)S(1)} %bitcast.13, f32[576,128]{1,0:T(8,128)S(1)} %bitcast.15, f32[576,128]{1,0:T(8,128)S(1)} %bitcast.19, f32[576,128]{1,0:T(8,128)S(1)} %bitcast.17, ...), custom_call_target="tpu_custom_call" | custom-call | flops 33973864 | bytes 2359296 | tf_op jit(solution)/shard_map/prepare/pallas_call | solution.py:478
  18.8 0.0 collective-permute-done.5.refs_5_
  18.9 0.9 %collective-permute-start.7 = (f32[576,128]{1,0:T(8,128)S(1)}, f32[576,128]{1,0:T(8,128)S(1)}, u32[]{:S(2)}, u32[]{:S(2)}) collective-permute-start(f32[576,128]{1,0:T(8,128)S(1)} %bitcast.20), channel_id=1, source_target_pairs={{0,4},{4,5},{5,1},{1,0},{8,12},{12,13},{13,9},{9,8},{16,20},{20,21... | collective-permute-start | bytes 884744 | tf_op jit(solution)/shard_map/ppermute | solution.py:492
  19.8 0.5 %collective-permute-done.6.refs_6_ = f32[48,384]{1,0:T(8,128)S(1)} collective-permute-done((f32[48,384]{1,0:T(8,128)S(1)}, f32[48,384]{1,0:T(8,128)S(1)}, u32[]{:S(2)}, u32[]{:S(2)}) %collective-permute-start.6) | collective-permute-done | bytes 73760 | tf_op jit(solution)/shard_map/ppermute | solution.py:446
  20.3 0.0 copy-done.4
  20.3 1.9 %products.1 = (f32[384,384]{1,0:T(8,128)S(1)}, f32[384,384]{1,0:T(8,128)S(1)}, f32[384,384]{1,0:T(8,128)S(1)}, f32[384,256]{1,0:T(8,128)S(1)}) custom-call(f32[384,384]{1,0:T(8,128)S(1)} %get-tuple-element.45.basis_ref, f32[384,384]{1,0:T(8,128)S(1)} %get-tuple-element.46.known_ref, f32[384,256]{1,0:T(8,128)S(1)} %get-tuple-element.47.right_ref, ...), custom_call_target="tpu_custom_call" | custom-call | flops 1019215872 | bytes 2359296 | tf_op jit(solution)/shard_map/products/pallas_call | solution.py:481
  22.2 0.4 collective-permute-done.8.corner_ref
  22.7 2.7 %begin.1.start_ref = f32[384,384]{1,0:T(8,128)S(1)} custom-call(f32[192,128]{1,0:T(8,128)S(1)} %collective-permute-done.8.corner_ref, f32[384,384]{1,0:T(8,128)S(1)} %get-tuple-element.56.power_ref, f32[384,384]{1,0:T(8,128)S(1)} %get-tuple-element.45.basis_ref), custom_call_target="tpu_custom_call" | custom-call | flops 2378170368 | bytes 2359296 | tf_op jit(solution)/shard_map/begin/pallas_call | solution.py:493
  25.4 0.0 collective-permute-done.7.other_left_ref
  25.4 0.0 copy-done.5
  25.4 0.0 copy-done.6
  25.4 3.2 %update.1 = (f32[576,128]{1,0:T(8,128)}, f32[576,128]{1,0:T(8,128)}, f32[4,48,384]{2,1,0:T(8,128)S(1)}, f32[384,256]{1,0:T(8,128)S(1)}, f32[384,384]{1,0:T(8,128)S(1)}) custom-call(f32[384,256]{1,0:T(8,128)S(1)} %get-tuple-element.51.inner_ref, f32[384,384]{1,0:T(8,128)S(1)} %get-tuple-element.45.basis_ref, f32[576,128]{1,0:T(8,128)S(1)} %get-tuple-element.52.left_ref, ...), custom_call_target="tpu_custom_call" | custom-call | flops 1698693120 | bytes 2359296 | tf_op jit(solution)/shard_map/update/pallas_call | solution.py:496
  28.6 1.1 %collective-permute-start.9 = (f32[4,48,384]{2,1,0:T(8,128)S(1)}, f32[4,48,384]{2,1,0:T(8,128)S(1)}, u32[]{:S(2)}, u32[]{:S(2)}) collective-permute-start(f32[4,48,384]{2,1,0:T(8,128)S(1)} %get-tuple-element.58), channel_id=1, source_target_pairs={{0,4},{4,0},{8,12},{12,8},{16,20},{20,16},{24,28},{28,24},{1,5},{5... | collective-permute-start | bytes 884744 | tf_op jit(solution)/shard_map/ppermute | solution.py:446
  29.7 5.8 %end.1 = (f32[384,384]{1,0:T(8,128)S(1)}, f32[384,384]{1,0:T(8,128)S(1)}, f32[576,128]{1,0:T(8,128)S(1)}, f32[4,48,384]{2,1,0:T(8,128)S(1)}) custom-call(f32[384,384]{1,0:T(8,128)S(1)} %get-tuple-element.59.start_ref, f32[384,256]{1,0:T(8,128)S(1)} %get-tuple-element.60.outer_ref, f32[384,256]{1,0:T(8,128)S(1)} %get-tuple-element.47.right_ref), custom_call_target="tpu_custom_call" | custom-call | flops 3057647616 | bytes 2359296 | tf_op jit(solution)/shard_map/end/pallas_call | solution.py:503
  35.5 1.0 %collective-permute-start.13 = (f32[576,128]{1,0:T(8,128)S(1)}, f32[576,128]{1,0:T(8,128)S(1)}, u32[]{:S(2)}, u32[]{:S(2)}) collective-permute-start(f32[576,128]{1,0:T(8,128)S(1)} %get-tuple-element.62), channel_id=1, source_target_pairs={{0,4},{4,0},{8,12},{12,8},{16,20},{20,16},{24,28},{28,24},{1,5},{5... | collective-permute-start | bytes 884744 | tf_op jit(solution)/shard_map/ppermute | solution.py:446
  36.5 0.1 collective-permute-done.9.theirs_ref
  36.6 3.6 %collective-permute-start.10 = (f32[48,384]{1,0:T(8,128)S(1)}, f32[48,384]{1,0:T(8,128)S(1)}, u32[]{:S(2)}, u32[]{:S(2)}) collective-permute-start(f32[48,384]{1,0:T(8,128)S(1)} %get-tuple-element.66), channel_id=1, source_target_pairs={{0,16},{4,20},{8,24},{12,28},{16,0},{20,4},{24,8},{28,12},{1,17},{... | collective-permute-start | bytes 221192 | tf_op jit(solution)/shard_map/ppermute | solution.py:443
  40.3 1.2 %collective-permute-start.11 = (f32[48,384]{1,0:T(8,128)S(1)}, f32[48,384]{1,0:T(8,128)S(1)}, u32[]{:S(2)}, u32[]{:S(2)}) collective-permute-start(f32[48,384]{1,0:T(8,128)S(1)} %get-tuple-element.67), channel_id=1, source_target_pairs={{0,24},{4,28},{8,16},{12,20},{16,8},{20,12},{24,0},{28,4},{1,25},{... | collective-permute-start | bytes 221192 | tf_op jit(solution)/shard_map/ppermute | solution.py:443
  41.5 0.5 %collective-permute-start.12 = (f32[48,384]{1,0:T(8,128)S(1)}, f32[48,384]{1,0:T(8,128)S(1)}, u32[]{:S(2)}, u32[]{:S(2)}) collective-permute-start(f32[48,384]{1,0:T(8,128)S(1)} %get-tuple-element.68), channel_id=1, source_target_pairs={{0,8},{4,12},{8,0},{12,4},{16,24},{20,28},{24,16},{28,20},{1,9},{5... | collective-permute-start | bytes 221192 | tf_op jit(solution)/shard_map/ppermute | solution.py:443
  41.9 2.1 %rest.1 = (f32[576,128]{1,0:T(8,128)S(1)}, f32[576,128]{1,0:T(8,128)}, f32[576,128]{1,0:T(8,128)}) custom-call(f32[384,384]{1,0:T(8,128)S(1)} %get-tuple-element.71.x_ref, f32[384,384]{1,0:T(8,128)S(1)} %get-tuple-element.72.poly_ref, f32[384,384]{1,0:T(8,128)S(1)} %get-tuple-element.73.grad_ref, f32[384,384]{1,0:T(8,128)S(1)} %get-tuple-element.74.new_stat_ref, ...), custom_call_target="tpu_custom_call" | custom-call | flops 509607936 | bytes 2359296 | tf_op jit(solution)/shard_map/rest/pallas_call | solution.py:512
  44.0 0.0 collective-permute-done.13.back_ref
  44.0 0.8 %bases.1 = (f32[576,128]{1,0:T(8,128)}, f32[576,128]{1,0:T(8,128)}) custom-call(f32[576,128]{1,0:T(8,128)S(1)} %get-tuple-element.78.keep_ref, f32[576,128]{1,0:T(8,128)S(1)} %collective-permute-done.13.back_ref), custom_call_target="tpu_custom_call" | custom-call | flops 33973864 | bytes 2359296 | tf_op jit(solution)/shard_map/bases/pallas_call | solution.py:534
  44.8 0.0 collective-permute-done.10.refs_1_
  44.8 1.7 %collective-permute-done.11.refs_2_ = f32[48,384]{1,0:T(8,128)S(1)} collective-permute-done((f32[48,384]{1,0:T(8,128)S(1)}, f32[48,384]{1,0:T(8,128)S(1)}, u32[]{:S(2)}, u32[]{:S(2)}) %collective-permute-start.11) | collective-permute-done | bytes 73760 | tf_op jit(solution)/shard_map/ppermute | solution.py:443
  46.6 0.0 collective-permute-done.12.refs_3_
  46.6 0.7 %rows.1 = f32[4,48,384]{2,1,0:T(8,128)} custom-call(f32[48,384]{1,0:T(8,128)S(1)} %get-tuple-element.65.refs_0_, f32[48,384]{1,0:T(8,128)S(1)} %collective-permute-done.10.refs_1_, f32[48,384]{1,0:T(8,128)S(1)} %collective-permute-done.11.refs_2_, f32[48,384]{1,0:T(8,128)S(1)} %collective-permute-done.12.refs_3_), custom_call_target="tpu_custom_call" | custom-call | flops 33973864 | bytes 2359296 | tf_op jit(solution)/shard_map/rows/pallas_call | solution.py:520
  (4 shorter events, 0.0 us)
Async XLA Ops:
  0.6 17.4 %copy-start = (f32[1,73728]{1,0:T(1,128)S(1)}, f32[1,73728]{1,0:T(1,128)}, u32[]{:S(2)}) copy-start(f32[1,73728]{1,0:T(1,128)} %param.10) | copy-start | bytes 884740
  0.6 17.4 %copy-start.1 = (f32[1,73728]{1,0:T(1,128)S(1)}, f32[1,73728]{1,0:T(1,128)}, u32[]{:S(2)}) copy-start(f32[1,73728]{1,0:T(1,128)} %param.11) | copy-start | bytes 884740
  0.7 17.4 %copy-start.2 = (f32[1,73728]{1,0:T(1,128)S(1)}, f32[1,73728]{1,0:T(1,128)}, u32[]{:S(2)}) copy-start(f32[1,73728]{1,0:T(1,128)} %param.13) | copy-start | bytes 884740
  0.7 17.4 %copy-start.3 = (f32[1,73728]{1,0:T(1,128)S(1)}, f32[1,73728]{1,0:T(1,128)}, u32[]{:S(2)}) copy-start(f32[1,73728]{1,0:T(1,128)} %param.12) | copy-start | bytes 884740
  2.0 16.1 %collective-permute-start = (f32[720,128]{1,0:T(8,128)S(1)}, f32[720,128]{1,0:T(8,128)S(1)}, u32[]{:S(2)}, u32[]{:S(2)}) collective-permute-start(f32[720,128]{1,0:T(8,128)S(1)} %get-tuple-element.44), channel_id=1, source_target_pairs={{0,4},{4,0},{8,12},{12,8},{16,20},{20,16},{24,28},{28,24},{1,5},{5... | collective-permute-start | bytes 1105928 | tf_op jit(solution)/shard_map/ppermute | solution.py:446
  5.0 7.4 %collective-permute-start.1 = (f32[48,384]{1,0:T(8,128)S(1)}, f32[48,384]{1,0:T(8,128)S(1)}, u32[]{:S(2)}, u32[]{:S(2)}) collective-permute-start(f32[48,384]{1,0:T(8,128)S(1)} %get-tuple-element.48), channel_id=1, source_target_pairs={{0,16},{4,20},{8,24},{12,28},{16,0},{20,4},{24,8},{28,12},{1,17},{... | collective-permute-start | bytes 221192 | tf_op jit(solution)/shard_map/ppermute | solution.py:443
  7.6 6.3 %collective-permute-start.2 = (f32[48,384]{1,0:T(8,128)S(1)}, f32[48,384]{1,0:T(8,128)S(1)}, u32[]{:S(2)}, u32[]{:S(2)}) collective-permute-start(f32[48,384]{1,0:T(8,128)S(1)} %get-tuple-element.49), channel_id=1, source_target_pairs={{0,24},{4,28},{8,16},{12,20},{16,8},{20,12},{24,0},{28,4},{1,25},{... | collective-permute-start | bytes 221192 | tf_op jit(solution)/shard_map/ppermute | solution.py:443
  8.9 5.5 %collective-permute-start.3 = (f32[48,384]{1,0:T(8,128)S(1)}, f32[48,384]{1,0:T(8,128)S(1)}, u32[]{:S(2)}, u32[]{:S(2)}) collective-permute-start(f32[48,384]{1,0:T(8,128)S(1)} %get-tuple-element.50), channel_id=1, source_target_pairs={{0,8},{4,12},{8,0},{12,4},{16,24},{20,28},{24,16},{28,20},{1,9},{5... | collective-permute-start | bytes 221192 | tf_op jit(solution)/shard_map/ppermute | solution.py:443
  12.4 4.6 %collective-permute-start.4 = (f32[48,384]{1,0:T(8,128)S(1)}, f32[48,384]{1,0:T(8,128)S(1)}, u32[]{:S(2)}, u32[]{:S(2)}) collective-permute-start(f32[48,384]{1,0:T(8,128)S(1)} %collective-permute-done.1.refs_1_), channel_id=1, source_target_pairs={{0,4},{4,0},{8,12},{12,8},{16,20},{20,16},{24,28},{28,24},{1,5},{5... | collective-permute-start | bytes 221192 | tf_op jit(solution)/shard_map/ppermute | solution.py:446
  13.9 5.0 %collective-permute-start.5 = (f32[48,384]{1,0:T(8,128)S(1)}, f32[48,384]{1,0:T(8,128)S(1)}, u32[]{:S(2)}, u32[]{:S(2)}) collective-permute-start(f32[48,384]{1,0:T(8,128)S(1)} %collective-permute-done.2.refs_2_), channel_id=1, source_target_pairs={{0,4},{4,0},{8,12},{12,8},{16,20},{20,16},{24,28},{28,24},{1,5},{5... | collective-permute-start | bytes 221192 | tf_op jit(solution)/shard_map/ppermute | solution.py:446
  14.4 5.9 %collective-permute-start.6 = (f32[48,384]{1,0:T(8,128)S(1)}, f32[48,384]{1,0:T(8,128)S(1)}, u32[]{:S(2)}, u32[]{:S(2)}) collective-permute-start(f32[48,384]{1,0:T(8,128)S(1)} %collective-permute-done.3.refs_3_), channel_id=1, source_target_pairs={{0,4},{4,0},{8,12},{12,8},{16,20},{20,16},{24,28},{28,24},{1,5},{5... | collective-permute-start | bytes 221192 | tf_op jit(solution)/shard_map/ppermute | solution.py:446
  17.0 3.4 %copy-start.4 = (f32[4,48,384]{2,1,0:T(8,128)S(1)}, f32[4,48,384]{2,1,0:T(8,128)}, u32[]{:S(2)}) copy-start(f32[4,48,384]{2,1,0:T(8,128)} %refs_0_.1) | copy-start | bytes 884740
  17.0 5.7 %collective-permute-start.8 = (f32[192,128]{1,0:T(8,128)S(1)}, f32[192,128]{1,0:T(8,128)S(1)}, u32[]{:S(2)}, u32[]{:S(2)}) collective-permute-start(f32[192,128]{1,0:T(8,128)S(1)} %get-tuple-element.55), channel_id=1, source_target_pairs={{0,4},{4,0},{8,12},{12,8},{16,20},{20,16},{24,28},{28,24},{1,5},{5... | collective-permute-start | bytes 294920 | tf_op jit(solution)/shard_map/ppermute | solution.py:446
  18.9 6.5 %collective-permute-start.7 = (f32[576,128]{1,0:T(8,128)S(1)}, f32[576,128]{1,0:T(8,128)S(1)}, u32[]{:S(2)}, u32[]{:S(2)}) collective-permute-start(f32[576,128]{1,0:T(8,128)S(1)} %bitcast.20), channel_id=1, source_target_pairs={{0,4},{4,5},{5,1},{1,0},{8,12},{12,13},{13,9},{9,8},{16,20},{20,21... | collective-permute-start | bytes 884744 | tf_op jit(solution)/shard_map/ppermute | solution.py:492
  22.7 2.7 %copy-start.5 = (f32[1,73728]{1,0:T(1,128)S(1)}, f32[1,73728]{1,0:T(1,128)}, u32[]{:S(2)}) copy-start(f32[1,73728]{1,0:T(1,128)} %param.8) | copy-start | bytes 884740
  22.7 2.7 %copy-start.6 = (f32[1,73728]{1,0:T(1,128)S(1)}, f32[1,73728]{1,0:T(1,128)}, u32[]{:S(2)}) copy-start(f32[1,73728]{1,0:T(1,128)} %param.9) | copy-start | bytes 884740
  28.6 8.0 %collective-permute-start.9 = (f32[4,48,384]{2,1,0:T(8,128)S(1)}, f32[4,48,384]{2,1,0:T(8,128)S(1)}, u32[]{:S(2)}, u32[]{:S(2)}) collective-permute-start(f32[4,48,384]{2,1,0:T(8,128)S(1)} %get-tuple-element.58), channel_id=1, source_target_pairs={{0,4},{4,0},{8,12},{12,8},{16,20},{20,16},{24,28},{28,24},{1,5},{5... | collective-permute-start | bytes 884744 | tf_op jit(solution)/shard_map/ppermute | solution.py:446
  35.5 8.5 %collective-permute-start.13 = (f32[576,128]{1,0:T(8,128)S(1)}, f32[576,128]{1,0:T(8,128)S(1)}, u32[]{:S(2)}, u32[]{:S(2)}) collective-permute-start(f32[576,128]{1,0:T(8,128)S(1)} %get-tuple-element.62), channel_id=1, source_target_pairs={{0,4},{4,0},{8,12},{12,8},{16,20},{20,16},{24,28},{28,24},{1,5},{5... | collective-permute-start | bytes 884744 | tf_op jit(solution)/shard_map/ppermute | solution.py:446
  36.6 8.2 %collective-permute-start.10 = (f32[48,384]{1,0:T(8,128)S(1)}, f32[48,384]{1,0:T(8,128)S(1)}, u32[]{:S(2)}, u32[]{:S(2)}) collective-permute-start(f32[48,384]{1,0:T(8,128)S(1)} %get-tuple-element.66), channel_id=1, source_target_pairs={{0,16},{4,20},{8,24},{12,28},{16,0},{20,4},{24,8},{28,12},{1,17},{... | collective-permute-start | bytes 221192 | tf_op jit(solution)/shard_map/ppermute | solution.py:443
  40.3 6.3 %collective-permute-start.11 = (f32[48,384]{1,0:T(8,128)S(1)}, f32[48,384]{1,0:T(8,128)S(1)}, u32[]{:S(2)}, u32[]{:S(2)}) collective-permute-start(f32[48,384]{1,0:T(8,128)S(1)} %get-tuple-element.67), channel_id=1, source_target_pairs={{0,24},{4,28},{8,16},{12,20},{16,8},{20,12},{24,0},{28,4},{1,25},{... | collective-permute-start | bytes 221192 | tf_op jit(solution)/shard_map/ppermute | solution.py:443
  41.5 5.1 %collective-permute-start.12 = (f32[48,384]{1,0:T(8,128)S(1)}, f32[48,384]{1,0:T(8,128)S(1)}, u32[]{:S(2)}, u32[]{:S(2)}) collective-permute-start(f32[48,384]{1,0:T(8,128)S(1)} %get-tuple-element.68), channel_id=1, source_target_pairs={{0,8},{4,12},{8,0},{12,4},{16,24},{20,28},{24,16},{28,20},{1,9},{5... | collective-permute-start | bytes 221192 | tf_op jit(solution)/shard_map/ppermute | solution.py:443

commit v16 on v15

--- a/solution.py
+++ b/solution.py
@@ -8,7 +8,6 @@
 from jax.sharding import PartitionSpec as P
 
 NS_ITERS = 5
-EARLY_ITERS = 1
 BETA_ONE = 0.9
 BETA_TWO = 0.95
 ADAM_EPS = 1e-08
@@ -244,9 +243,9 @@
     copy_ref[...] = l_basis_ref[...]
 
 
-def products_kernel(hops, basis_ref, known_ref, right_ref, got_ref, *refs):
+def products_kernel(hops, basis_ref, known_ref, got_ref, *refs):
     left = is_left()
-    grad_ref, stat_ref, power_ref, inner_ref = refs[-4:]
+    grad_ref, stat_ref, power_ref = refs[-3:]
     if hops:
         grads_ref, mine_refs, theirs_refs = refs[0], refs[1 : 1 + len(hops)], refs[1 + len(hops) : 1 + 2 * len(hops)]
         rows = grads_ref.shape[1]
@@ -267,10 +266,9 @@
     stat = known_ref[...] + 0.5 * symmetric_dot(parts, parts, ((1,), (1,)))
     stat_ref[...] = stat
     power_ref[...] = dot(stat, basis_ref[...])
-    inner_ref[...] = dot(grad, right_ref[...])
-
-
-def begin_kernel(steps, corner_ref, power_ref, basis_ref, x_ref, scratch):
+
+
+def begin_kernel(corner_ref, power_ref, basis_ref, grad_ref, right_ref, x_ref, inner_ref, scratch):
     first = is_first()
     corner = corner_part(corner_ref, scratch)
     rows, wide = corner.shape
@@ -278,7 +276,14 @@
     basis = jnp.concatenate([basis, jnp.zeros((wide - rows, 2 * rows), F32)], axis=0)
     term = 0.5 * dot(corner, basis)
     power = power_ref[...] + jnp.concatenate([jnp.where(first, 0.0, term), jnp.where(first, term, 0.0)], axis=0)
-    x_ref[...] = iterate(power * (1.0 / jnp.sqrt(jnp.sum(power * power) + NORM_EPS)), steps)
+    grad_parts, right_parts = split(grad_ref[...]), split(right_ref[...])
+    x = power * (1.0 / jnp.sqrt(jnp.sum(power * power) + NORM_EPS))
+    parts = split(x)
+    gram = dot_parts(parts, parts, ((1,), (1,)))
+    inner_ref[...] = dot_parts(grad_parts, right_parts)
+    gram_parts = split(gram)
+    poly = CUBIC_COEFF * gram + QUINTIC_COEFF * dot_parts(gram_parts, gram_parts)
+    x_ref[...] = LINEAR_COEFF * x + dot_parts(split(poly), parts)
 
 
 def rows_for(hops, outer_ref, right_parts, out_ref, offset):
@@ -332,14 +337,17 @@
     x_ref[...] = LINEAR_COEFF * x + moved
 
 
-def end_kernel(hops, steps, start_ref, outer_ref, right_ref, x_ref, poly_ref, send_ref, mine_ref, scratch):
+def end_kernel(steps, start_ref, x_ref, poly_ref, send_ref, scratch):
     x = iterate(start_ref[...], steps - 1)
     x_ref[...] = x
-    rows_for(hops, outer_ref, split(right_ref[...]), mine_ref, lax.axis_index("shard") % 2)
     poly = polynomial(split(x))
     poly_ref[...] = poly
     half = take_half(x, jnp.logical_not(is_first()))
     put_thirds(send_ref, flat_of(scratch, LINEAR_COEFF * half + dot(poly, half)))
+
+
+def own_rows_kernel(hops, outer_ref, right_ref, mine_ref):
+    rows_for(hops, outer_ref, split(right_ref[...]), mine_ref, lax.axis_index("shard") % 2)
 
 
 def add_kernel(mine_ref, theirs_ref, *out_refs):
@@ -478,9 +486,9 @@
     basis, known, right, other, left = call(
         prepare_kernel, [square, square, wide, flat, flat], [(3, full, LANES)], 0.1, full, "prepare"
     )(l_stat, r_stat, l_basis, r_basis, got)
-    grad, new_stat, power, inner = call(
-        functools.partial(products_kernel, hops), [square, square, square, wide], [], 3, full, "products"
-    )(basis, known, right, got, *rows)
+    grad, new_stat, power = call(
+        functools.partial(products_kernel, hops), [square, square, square], [], 3, full, "products"
+    )(basis, known, got, *rows)
     tensors = lax.axis_size("tensor")
     place = lambda t, i: i * tensors + t
     cycle = []
@@ -490,9 +498,9 @@
             cycle += [(place(t + 1, i + 1), place(t + 1, i)), (place(t + 1, i), place(t, i))]
     cycle += [(place(t, i), place(t, i ^ 1)) for t in range(tensors - tensors % 2, tensors) for i in range(size)]
     other_left = lax.ppermute(after(l_basis, basis, *(theirs[:2] if near else mine)), ("shard", "tensor"), cycle)
-    (x,) = call(
-        functools.partial(begin_kernel, EARLY_ITERS), [square], [(2, full // 2, LANES)], 7, full, "begin"
-    )(got_corner, power, basis)
+    x, inner = call(begin_kernel, [square, wide], [(2, full // 2, LANES)], 7, full, "begin")(
+        got_corner, power, basis, grad, right
+    )
     new_one, new_two, other_rows, outer, x = call(
         functools.partial(update_kernel, hops), [flat, flat, strips, wide, square], [(3, full, LANES)], 5, full, "update"
     )(inner, basis, left, right, other_left, one, two, x)
@@ -500,22 +508,18 @@
         partial = other_rows.reshape(tiles_here, 2, rows_here, full)
         other_rows = lax.dynamic_index_in_dim(partial, 1 - parity, 1, keepdims=False)
     got_rows = partner(other_rows)
-    x, poly, send, own_rows = call(
-        functools.partial(end_kernel, hops, NS_ITERS - EARLY_ITERS - 1),
-        [square, square, flat, strips],
-        [(3, full, LANES)],
-        9,
-        full,
-        "end",
-    )(after(x, other_rows), outer, right)
+    x, poly, send = call(
+        functools.partial(end_kernel, NS_ITERS - 2), [square, square, flat], [(3, full, LANES)], 9, full, "end"
+    )(after(x, other_rows))
     back = partner(send)
     keep, new_left, new_right = call(rest_kernel, [flat, flat, flat], [(3, full, LANES)], 1.5, full, "rest")(
         x, poly, grad, new_stat, other
     )
     if near:
-        kept, *sums = call(add_kernel, [block] * (1 + len(hops)), [], 0.1, full, "add")(
-            after(own_rows, send), after(got_rows, send)
+        (own_rows,) = call(functools.partial(own_rows_kernel, hops), [strips], [], 0.5, full, "own_rows")(
+            after(outer, send), right
         )
+        kept, *sums = call(add_kernel, [block] * (1 + len(hops)), [], 0.1, full, "add")(own_rows, after(got_rows, send))
         returned = [hop_by(x, hop) for hop, x in zip(hops, sums)]
         update = call(
             functools.partial(rows_kernel, hops),

time: 47.5 us -> 47.9 us (level)
    pallas_call x3 -> x4, Pallas kernels: 10.4 us -> 10.2 us  [the longest x1 5.67 us: local(): call(functools.partial(end_kernel, NS_ITERS - 2), [square, square, flat],...]
  transfers between devices with their start and end apart: 14 -> 14, of which waited for: 7 -> 7; matrix products, arithmetic and copies ran while one was open for 0% -> 0% of each run, Pallas kernels for 30% -> 29%
where the time goes in v16:
time: 47.9 us; the launch traced here: 47.8 us
  Pallas kernels  19.2 us (40%)
  starting transfers between devices  19.2 us (40%)
  waiting for transfers between devices  8.55 us (18%)
  between operations  0.8 us (2%)
    ppermute x6, starting transfers between devices, hop_by(): return lax.ppermute(x, 'shard', [(i, i ^ 2 * hop) for i in range(size)])  9.59 us
    ppermute x7, starting transfers between devices, partner(): return lax.ppermute(x, 'shard', pairs)  8.74 us
    ppermute x6, waiting for transfers between devices, hop_by(): return lax.ppermute(x, 'shard', [(i, i ^ 2 * hop) for i in range(size)])  6.02 us
    pallas_call x1, Pallas kernels, local(): call(functools.partial(end_kernel, NS_ITERS - 2), [square, square, flat],...  5.67 us
    pallas_call x1, Pallas kernels, local(): call(functools.partial(update_kernel, hops), [flat, flat, strips, wide, s...  3.24 us
    pallas_call x1, Pallas kernels, local(): call(begin_kernel, [square, wide], [(2, full // 2, LANES)], 7, full, 'beg...  2.76 us
    ppermute x7, waiting for transfers between devices, partner(): return lax.ppermute(x, 'shard', pairs)  2.54 us
    pallas_call x1, Pallas kernels, local(): call(rest_kernel, [flat, flat, flat], [(3, full, LANES)], 1.5, full, 'rest')  2.06 us
  transfers between devices with their start and end apart: 14, of which 7 were waited for; matrix products, arithmetic and copies ran while one was open for 0% of the time, Pallas kernels for 29%

profile of v16, /device:TPU:0, one launch (start us, length us, event | category | flops | bytes accessed | tf_op | source)
XLA Modules:
  0.0 47.8 jit_solution(11314588354551776448)
XLA Ops:
  0.6 0.0 copy-start
  0.6 0.0 copy-start.1
  0.7 0.0 copy-start.2
  0.7 0.0 copy-start.3
  0.7 1.3 %pack.1 = (f32[720,128]{1,0:T(8,128)S(1)}, f32[192,128]{1,0:T(8,128)S(1)}, f32[48,384]{1,0:T(8,128)S(1)}, f32[48,384]{1,0:T(8,128)S(1)}, f32[48,384]{1,0:T(8,128)S(1)}) custom-call(f32[576,128]{1,0:T(8,128)} %bitcast.12, f32[576,128]{1,0:T(8,128)} %bitcast.14, f32[576,128]{1,0:T(8,128)} %bitcast.18, f32[576,128]{1,0:T(8,128)} %bitcast.16, f32[4,48,384]{2,1,0:T(8,128)} %refs_0_.1), custom_call_target="tpu_custom_call" | custom-call | flops 33973864 | bytes 2359296 | tf_op jit(solution)/shard_map/pack/pallas_call | solution.py:461
  2.0 3.0 %collective-permute-start.3 = (f32[720,128]{1,0:T(8,128)S(1)}, f32[720,128]{1,0:T(8,128)S(1)}, u32[]{:S(2)}, u32[]{:S(2)}) collective-permute-start(f32[720,128]{1,0:T(8,128)S(1)} %get-tuple-element.47), channel_id=1, source_target_pairs={{0,4},{4,0},{8,12},{12,8},{16,20},{20,16},{24,28},{28,24},{1,5},{5... | collective-permute-start | bytes 1105928 | tf_op jit(solution)/shard_map/ppermute | solution.py:454
  5.0 2.6 %collective-permute-start = (f32[48,384]{1,0:T(8,128)S(1)}, f32[48,384]{1,0:T(8,128)S(1)}, u32[]{:S(2)}, u32[]{:S(2)}) collective-permute-start(f32[48,384]{1,0:T(8,128)S(1)} %get-tuple-element.45), channel_id=1, source_target_pairs={{0,16},{4,20},{8,24},{12,28},{16,0},{20,4},{24,8},{28,12},{1,17},{... | collective-permute-start | bytes 221192 | tf_op jit(solution)/shard_map/ppermute | solution.py:451
  7.6 1.3 %collective-permute-start.4 = (f32[48,384]{1,0:T(8,128)S(1)}, f32[48,384]{1,0:T(8,128)S(1)}, u32[]{:S(2)}, u32[]{:S(2)}) collective-permute-start(f32[48,384]{1,0:T(8,128)S(1)} %get-tuple-element.50), channel_id=1, source_target_pairs={{0,24},{4,28},{8,16},{12,20},{16,8},{20,12},{24,0},{28,4},{1,25},{... | collective-permute-start | bytes 221192 | tf_op jit(solution)/shard_map/ppermute | solution.py:451
  8.9 0.2 collective-permute-start.5
  9.2 3.2 %collective-permute-done.refs_1_ = f32[48,384]{1,0:T(8,128)S(1)} collective-permute-done((f32[48,384]{1,0:T(8,128)S(1)}, f32[48,384]{1,0:T(8,128)S(1)}, u32[]{:S(2)}, u32[]{:S(2)}) %collective-permute-start) | collective-permute-done | bytes 73760 | tf_op jit(solution)/shard_map/ppermute | solution.py:451
  12.4 0.5 collective-permute-start.1
  12.9 1.1 %collective-permute-done.4.refs_2_ = f32[48,384]{1,0:T(8,128)S(1)} collective-permute-done((f32[48,384]{1,0:T(8,128)S(1)}, f32[48,384]{1,0:T(8,128)S(1)}, u32[]{:S(2)}, u32[]{:S(2)}) %collective-permute-start.4) | collective-permute-done | bytes 73760 | tf_op jit(solution)/shard_map/ppermute | solution.py:451
  13.9 0.5 %collective-permute-start.6 = (f32[48,384]{1,0:T(8,128)S(1)}, f32[48,384]{1,0:T(8,128)S(1)}, u32[]{:S(2)}, u32[]{:S(2)}) collective-permute-start(f32[48,384]{1,0:T(8,128)S(1)} %collective-permute-done.4.refs_2_), channel_id=1, source_target_pairs={{0,4},{4,0},{8,12},{12,8},{16,20},{20,16},{24,28},{28,24},{1,5},{5... | collective-permute-start | bytes 221192 | tf_op jit(solution)/shard_map/ppermute | solution.py:454
  14.4 0.0 collective-permute-done.5.refs_3_
  14.4 1.5 %collective-permute-start.7 = (f32[48,384]{1,0:T(8,128)S(1)}, f32[48,384]{1,0:T(8,128)S(1)}, u32[]{:S(2)}, u32[]{:S(2)}) collective-permute-start(f32[48,384]{1,0:T(8,128)S(1)} %collective-permute-done.5.refs_3_), channel_id=1, source_target_pairs={{0,4},{4,0},{8,12},{12,8},{16,20},{20,16},{24,28},{28,24},{1,5},{5... | collective-permute-start | bytes 221192 | tf_op jit(solution)/shard_map/ppermute | solution.py:454
  15.9 1.0 %collective-permute-done.1.refs_4_ = f32[48,384]{1,0:T(8,128)S(1)} collective-permute-done((f32[48,384]{1,0:T(8,128)S(1)}, f32[48,384]{1,0:T(8,128)S(1)}, u32[]{:S(2)}, u32[]{:S(2)}) %collective-permute-start.1) | collective-permute-done | bytes 73760 | tf_op jit(solution)/shard_map/ppermute | solution.py:454
  17.0 1.1 %collective-permute-start.2 = (f32[192,128]{1,0:T(8,128)S(1)}, f32[192,128]{1,0:T(8,128)S(1)}, u32[]{:S(2)}, u32[]{:S(2)}) collective-permute-start(f32[192,128]{1,0:T(8,128)S(1)} %get-tuple-element.46), channel_id=1, source_target_pairs={{0,4},{4,0},{8,12},{12,8},{16,20},{20,16},{24,28},{28,24},{1,5},{5... | collective-permute-start | bytes 294920 | tf_op jit(solution)/shard_map/ppermute | solution.py:454
  18.1 0.0 collective-permute-done.3.got_ref
  18.1 0.0 copy-done
  18.1 0.0 copy-done.1
  18.1 0.0 copy-done.2
  18.1 0.0 copy-done.3
  18.1 0.7 %prepare.1 = (f32[384,384]{1,0:T(8,128)S(1)}, f32[384,384]{1,0:T(8,128)S(1)}, f32[384,256]{1,0:T(8,128)S(1)}, f32[576,128]{1,0:T(8,128)S(1)}, f32[576,128]{1,0:T(8,128)S(1)}) custom-call(f32[576,128]{1,0:T(8,128)S(1)} %bitcast.13, f32[576,128]{1,0:T(8,128)S(1)} %bitcast.15, f32[576,128]{1,0:T(8,128)S(1)} %bitcast.19, f32[576,128]{1,0:T(8,128)S(1)} %bitcast.17, ...), custom_call_target="tpu_custom_call" | custom-call | flops 33973864 | bytes 2359296 | tf_op jit(solution)/shard_map/prepare/pallas_call | solution.py:486
  18.8 0.0 collective-permute-done.6.refs_5_
  18.9 0.9 %collective-permute-start.8 = (f32[576,128]{1,0:T(8,128)S(1)}, f32[576,128]{1,0:T(8,128)S(1)}, u32[]{:S(2)}, u32[]{:S(2)}) collective-permute-start(f32[576,128]{1,0:T(8,128)S(1)} %bitcast.20), channel_id=1, source_target_pairs={{0,4},{4,5},{5,1},{1,0},{8,12},{12,13},{13,9},{9,8},{16,20},{20,21... | collective-permute-start | bytes 884744 | tf_op jit(solution)/shard_map/ppermute | solution.py:500
  19.8 0.5 %collective-permute-done.7.refs_6_ = f32[48,384]{1,0:T(8,128)S(1)} collective-permute-done((f32[48,384]{1,0:T(8,128)S(1)}, f32[48,384]{1,0:T(8,128)S(1)}, u32[]{:S(2)}, u32[]{:S(2)}) %collective-permute-start.7) | collective-permute-done | bytes 73760 | tf_op jit(solution)/shard_map/ppermute | solution.py:454
  20.3 0.0 copy-done.4
  20.3 1.4 %products.1 = (f32[384,384]{1,0:T(8,128)S(1)}, f32[384,384]{1,0:T(8,128)S(1)}, f32[384,384]{1,0:T(8,128)S(1)}) custom-call(f32[384,384]{1,0:T(8,128)S(1)} %get-tuple-element.48.basis_ref, f32[384,384]{1,0:T(8,128)S(1)} %get-tuple-element.49.known_ref, f32[720,128]{1,0:T(8,128)S(1)} %collective-permute-done.3.got_ref, f32[4,48,384]{2,1,0:T(8,128)S(1)} %copy-done.4, ...), custom_call_target="tpu_custom_call" | custom-call | flops 1019215872 | bytes 2359296 | tf_op jit(solution)/shard_map/products/pallas_call | solution.py:489
  21.7 1.0 %collective-permute-done.2.corner_ref = f32[192,128]{1,0:T(8,128)S(1)} collective-permute-done((f32[192,128]{1,0:T(8,128)S(1)}, f32[192,128]{1,0:T(8,128)S(1)}, u32[]{:S(2)}, u32[]{:S(2)}) %collective-permute-start.2) | collective-permute-done | bytes 98336 | tf_op jit(solution)/shard_map/ppermute | solution.py:454
  22.7 2.8 %begin.1 = (f32[384,384]{1,0:T(8,128)S(1)}, f32[384,256]{1,0:T(8,128)S(1)}) custom-call(f32[192,128]{1,0:T(8,128)S(1)} %collective-permute-done.2.corner_ref, f32[384,384]{1,0:T(8,128)S(1)} %get-tuple-element.52.power_ref, f32[384,384]{1,0:T(8,128)S(1)} %get-tuple-element.48.basis_ref, f32[384,384]{1,0:T(8,128)S(1)} %get-tuple-element.53.grad_ref, ...), custom_call_target="tpu_custom_call" | custom-call | flops 2378170368 | bytes 2359296 | tf_op jit(solution)/shard_map/begin/pallas_call | solution.py:501
  25.5 0.0 collective-permute-done.8.other_left_ref
  25.5 0.0 copy-done.5
  25.5 3.2 %update.1 = (f32[576,128]{1,0:T(8,128)}, f32[576,128]{1,0:T(8,128)}, f32[4,48,384]{2,1,0:T(8,128)S(1)}, f32[384,256]{1,0:T(8,128)S(1)}, f32[384,384]{1,0:T(8,128)S(1)}) custom-call(f32[384,256]{1,0:T(8,128)S(1)} %get-tuple-element.55.inner_ref, f32[384,384]{1,0:T(8,128)S(1)} %get-tuple-element.48.basis_ref, f32[576,128]{1,0:T(8,128)S(1)} %get-tuple-element.56.left_ref, ...), custom_call_target="tpu_custom_call" | custom-call | flops 1698693120 | bytes 2359296 | tf_op jit(solution)/shard_map/update/pallas_call | solution.py:504
  28.7 1.0 %collective-permute-start.9 = (f32[4,48,384]{2,1,0:T(8,128)S(1)}, f32[4,48,384]{2,1,0:T(8,128)S(1)}, u32[]{:S(2)}, u32[]{:S(2)}) collective-permute-start(f32[4,48,384]{2,1,0:T(8,128)S(1)} %get-tuple-element.61), channel_id=1, source_target_pairs={{0,4},{4,0},{8,12},{12,8},{16,20},{20,16},{24,28},{28,24},{1,5},{5... | collective-permute-start | bytes 884744 | tf_op jit(solution)/shard_map/ppermute | solution.py:454
  29.8 5.7 %end.1 = (f32[384,384]{1,0:T(8,128)S(1)}, f32[384,384]{1,0:T(8,128)S(1)}, f32[576,128]{1,0:T(8,128)S(1)}) custom-call(f32[384,384]{1,0:T(8,128)S(1)} %get-tuple-element.62.start_ref), custom_call_target="tpu_custom_call" | custom-call | flops 3057647616 | bytes 2359296 | tf_op jit(solution)/shard_map/end/pallas_call | solution.py:511
  35.4 1.1 %collective-permute-start.13 = (f32[576,128]{1,0:T(8,128)S(1)}, f32[576,128]{1,0:T(8,128)S(1)}, u32[]{:S(2)}, u32[]{:S(2)}) collective-permute-start(f32[576,128]{1,0:T(8,128)S(1)} %get-tuple-element.63), channel_id=1, source_target_pairs={{0,4},{4,0},{8,12},{12,8},{16,20},{20,16},{24,28},{28,24},{1,5},{5... | collective-permute-start | bytes 884744 | tf_op jit(solution)/shard_map/ppermute | solution.py:454
  36.5 0.4 own_rows.1.mine_ref
  36.9 0.0 collective-permute-done.9.theirs_ref
  37.0 3.5 %collective-permute-start.10 = (f32[48,384]{1,0:T(8,128)S(1)}, f32[48,384]{1,0:T(8,128)S(1)}, u32[]{:S(2)}, u32[]{:S(2)}) collective-permute-start(f32[48,384]{1,0:T(8,128)S(1)} %get-tuple-element.67), channel_id=1, source_target_pairs={{0,16},{4,20},{8,24},{12,28},{16,0},{20,4},{24,8},{28,12},{1,17},{... | collective-permute-start | bytes 221192 | tf_op jit(solution)/shard_map/ppermute | solution.py:451
  40.4 1.5 %collective-permute-start.11 = (f32[48,384]{1,0:T(8,128)S(1)}, f32[48,384]{1,0:T(8,128)S(1)}, u32[]{:S(2)}, u32[]{:S(2)}) collective-permute-start(f32[48,384]{1,0:T(8,128)S(1)} %get-tuple-element.68), channel_id=1, source_target_pairs={{0,24},{4,28},{8,16},{12,20},{16,8},{20,12},{24,0},{28,4},{1,25},{... | collective-permute-start | bytes 221192 | tf_op jit(solution)/shard_map/ppermute | solution.py:451
  41.9 0.5 %collective-permute-start.12 = (f32[48,384]{1,0:T(8,128)S(1)}, f32[48,384]{1,0:T(8,128)S(1)}, u32[]{:S(2)}, u32[]{:S(2)}) collective-permute-start(f32[48,384]{1,0:T(8,128)S(1)} %get-tuple-element.69), channel_id=1, source_target_pairs={{0,8},{4,12},{8,0},{12,4},{16,24},{20,28},{24,16},{28,20},{1,9},{5... | collective-permute-start | bytes 221192 | tf_op jit(solution)/shard_map/ppermute | solution.py:451
  42.4 2.1 %rest.1 = (f32[576,128]{1,0:T(8,128)S(1)}, f32[576,128]{1,0:T(8,128)}, f32[576,128]{1,0:T(8,128)}) custom-call(f32[384,384]{1,0:T(8,128)S(1)} %get-tuple-element.72.x_ref, f32[384,384]{1,0:T(8,128)S(1)} %get-tuple-element.73.poly_ref, f32[384,384]{1,0:T(8,128)S(1)} %get-tuple-element.53.grad_ref, f32[384,384]{1,0:T(8,128)S(1)} %get-tuple-element.74.new_stat_ref, ...), custom_call_target="tpu_custom_call" | custom-call | flops 509607936 | bytes 2359296 | tf_op jit(solution)/shard_map/rest/pallas_call | solution.py:515
  44.4 0.0 collective-permute-done.13.back_ref
  44.4 0.8 %bases.1 = (f32[576,128]{1,0:T(8,128)}, f32[576,128]{1,0:T(8,128)}) custom-call(f32[576,128]{1,0:T(8,128)S(1)} %get-tuple-element.78.keep_ref, f32[576,128]{1,0:T(8,128)S(1)} %collective-permute-done.13.back_ref), custom_call_target="tpu_custom_call" | custom-call | flops 33973864 | bytes 2359296 | tf_op jit(solution)/shard_map/bases/pallas_call | solution.py:538
  45.3 0.0 collective-permute-done.10.refs_1_
  45.3 1.4 %collective-permute-done.11.refs_2_ = f32[48,384]{1,0:T(8,128)S(1)} collective-permute-done((f32[48,384]{1,0:T(8,128)S(1)}, f32[48,384]{1,0:T(8,128)S(1)}, u32[]{:S(2)}, u32[]{:S(2)}) %collective-permute-start.11) | collective-permute-done | bytes 73760 | tf_op jit(solution)/shard_map/ppermute | solution.py:451
  46.7 0.3 collective-permute-done.12.refs_3_
  47.0 0.7 %rows.1 = f32[4,48,384]{2,1,0:T(8,128)} custom-call(f32[48,384]{1,0:T(8,128)S(1)} %get-tuple-element.66.refs_0_, f32[48,384]{1,0:T(8,128)S(1)} %collective-permute-done.10.refs_1_, f32[48,384]{1,0:T(8,128)S(1)} %collective-permute-done.11.refs_2_, f32[48,384]{1,0:T(8,128)S(1)} %collective-permute-done.12.refs_3_), custom_call_target="tpu_custom_call" | custom-call | flops 33973864 | bytes 2359296 | tf_op jit(solution)/shard_map/rows/pallas_call | solution.py:524
  (5 shorter events, 0.0 us)
Async XLA Ops:
  0.6 17.4 %copy-start = (f32[1,73728]{1,0:T(1,128)S(1)}, f32[1,73728]{1,0:T(1,128)}, u32[]{:S(2)}) copy-start(f32[1,73728]{1,0:T(1,128)} %param.10) | copy-start | bytes 884740
  0.6 17.4 %copy-start.1 = (f32[1,73728]{1,0:T(1,128)S(1)}, f32[1,73728]{1,0:T(1,128)}, u32[]{:S(2)}) copy-start(f32[1,73728]{1,0:T(1,128)} %param.11) | copy-start | bytes 884740
  0.7 17.4 %copy-start.2 = (f32[1,73728]{1,0:T(1,128)S(1)}, f32[1,73728]{1,0:T(1,128)}, u32[]{:S(2)}) copy-start(f32[1,73728]{1,0:T(1,128)} %param.13) | copy-start | bytes 884740
  0.7 17.4 %copy-start.3 = (f32[1,73728]{1,0:T(1,128)S(1)}, f32[1,73728]{1,0:T(1,128)}, u32[]{:S(2)}) copy-start(f32[1,73728]{1,0:T(1,128)} %param.12) | copy-start | bytes 884740
  2.0 16.1 %collective-permute-start.3 = (f32[720,128]{1,0:T(8,128)S(1)}, f32[720,128]{1,0:T(8,128)S(1)}, u32[]{:S(2)}, u32[]{:S(2)}) collective-permute-start(f32[720,128]{1,0:T(8,128)S(1)} %get-tuple-element.47), channel_id=1, source_target_pairs={{0,4},{4,0},{8,12},{12,8},{16,20},{20,16},{24,28},{28,24},{1,5},{5... | collective-permute-start | bytes 1105928 | tf_op jit(solution)/shard_map/ppermute | solution.py:454
  5.0 7.4 %collective-permute-start = (f32[48,384]{1,0:T(8,128)S(1)}, f32[48,384]{1,0:T(8,128)S(1)}, u32[]{:S(2)}, u32[]{:S(2)}) collective-permute-start(f32[48,384]{1,0:T(8,128)S(1)} %get-tuple-element.45), channel_id=1, source_target_pairs={{0,16},{4,20},{8,24},{12,28},{16,0},{20,4},{24,8},{28,12},{1,17},{... | collective-permute-start | bytes 221192 | tf_op jit(solution)/shard_map/ppermute | solution.py:451
  7.6 6.3 %collective-permute-start.4 = (f32[48,384]{1,0:T(8,128)S(1)}, f32[48,384]{1,0:T(8,128)S(1)}, u32[]{:S(2)}, u32[]{:S(2)}) collective-permute-start(f32[48,384]{1,0:T(8,128)S(1)} %get-tuple-element.50), channel_id=1, source_target_pairs={{0,24},{4,28},{8,16},{12,20},{16,8},{20,12},{24,0},{28,4},{1,25},{... | collective-permute-start | bytes 221192 | tf_op jit(solution)/shard_map/ppermute | solution.py:451
  8.9 5.5 %collective-permute-start.5 = (f32[48,384]{1,0:T(8,128)S(1)}, f32[48,384]{1,0:T(8,128)S(1)}, u32[]{:S(2)}, u32[]{:S(2)}) collective-permute-start(f32[48,384]{1,0:T(8,128)S(1)} %get-tuple-element.51), channel_id=1, source_target_pairs={{0,8},{4,12},{8,0},{12,4},{16,24},{20,28},{24,16},{28,20},{1,9},{5... | collective-permute-start | bytes 221192 | tf_op jit(solution)/shard_map/ppermute | solution.py:451
  12.4 4.6 %collective-permute-start.1 = (f32[48,384]{1,0:T(8,128)S(1)}, f32[48,384]{1,0:T(8,128)S(1)}, u32[]{:S(2)}, u32[]{:S(2)}) collective-permute-start(f32[48,384]{1,0:T(8,128)S(1)} %collective-permute-done.refs_1_), channel_id=1, source_target_pairs={{0,4},{4,0},{8,12},{12,8},{16,20},{20,16},{24,28},{28,24},{1,5},{5... | collective-permute-start | bytes 221192 | tf_op jit(solution)/shard_map/ppermute | solution.py:454
  13.9 5.0 %collective-permute-start.6 = (f32[48,384]{1,0:T(8,128)S(1)}, f32[48,384]{1,0:T(8,128)S(1)}, u32[]{:S(2)}, u32[]{:S(2)}) collective-permute-start(f32[48,384]{1,0:T(8,128)S(1)} %collective-permute-done.4.refs_2_), channel_id=1, source_target_pairs={{0,4},{4,0},{8,12},{12,8},{16,20},{20,16},{24,28},{28,24},{1,5},{5... | collective-permute-start | bytes 221192 | tf_op jit(solution)/shard_map/ppermute | solution.py:454
  14.4 5.9 %collective-permute-start.7 = (f32[48,384]{1,0:T(8,128)S(1)}, f32[48,384]{1,0:T(8,128)S(1)}, u32[]{:S(2)}, u32[]{:S(2)}) collective-permute-start(f32[48,384]{1,0:T(8,128)S(1)} %collective-permute-done.5.refs_3_), channel_id=1, source_target_pairs={{0,4},{4,0},{8,12},{12,8},{16,20},{20,16},{24,28},{28,24},{1,5},{5... | collective-permute-start | bytes 221192 | tf_op jit(solution)/shard_map/ppermute | solution.py:454
  17.0 3.4 %copy-start.4 = (f32[4,48,384]{2,1,0:T(8,128)S(1)}, f32[4,48,384]{2,1,0:T(8,128)}, u32[]{:S(2)}) copy-start(f32[4,48,384]{2,1,0:T(8,128)} %refs_0_.1) | copy-start | bytes 884740
  17.0 5.7 %collective-permute-start.2 = (f32[192,128]{1,0:T(8,128)S(1)}, f32[192,128]{1,0:T(8,128)S(1)}, u32[]{:S(2)}, u32[]{:S(2)}) collective-permute-start(f32[192,128]{1,0:T(8,128)S(1)} %get-tuple-element.46), channel_id=1, source_target_pairs={{0,4},{4,0},{8,12},{12,8},{16,20},{20,16},{24,28},{28,24},{1,5},{5... | collective-permute-start | bytes 294920 | tf_op jit(solution)/shard_map/ppermute | solution.py:454
  18.9 6.6 %collective-permute-start.8 = (f32[576,128]{1,0:T(8,128)S(1)}, f32[576,128]{1,0:T(8,128)S(1)}, u32[]{:S(2)}, u32[]{:S(2)}) collective-permute-start(f32[576,128]{1,0:T(8,128)S(1)} %bitcast.20), channel_id=1, source_target_pairs={{0,4},{4,5},{5,1},{1,0},{8,12},{12,13},{13,9},{9,8},{16,20},{20,21... | collective-permute-start | bytes 884744 | tf_op jit(solution)/shard_map/ppermute | solution.py:500
  22.7 2.8 %copy-start.5 = (f32[1,73728]{1,0:T(1,128)S(1)}, f32[1,73728]{1,0:T(1,128)}, u32[]{:S(2)}) copy-start(f32[1,73728]{1,0:T(1,128)} %param.8) | copy-start | bytes 884740
  22.7 2.8 %copy-start.6 = (f32[1,73728]{1,0:T(1,128)S(1)}, f32[1,73728]{1,0:T(1,128)}, u32[]{:S(2)}) copy-start(f32[1,73728]{1,0:T(1,128)} %param.9) | copy-start | bytes 884740
  28.7 8.2 %collective-permute-start.9 = (f32[4,48,384]{2,1,0:T(8,128)S(1)}, f32[4,48,384]{2,1,0:T(8,128)S(1)}, u32[]{:S(2)}, u32[]{:S(2)}) collective-permute-start(f32[4,48,384]{2,1,0:T(8,128)S(1)} %get-tuple-element.61), channel_id=1, source_target_pairs={{0,4},{4,0},{8,12},{12,8},{16,20},{20,16},{24,28},{28,24},{1,5},{5... | collective-permute-start | bytes 884744 | tf_op jit(solution)/shard_map/ppermute | solution.py:454
  35.4 9.0 %collective-permute-start.13 = (f32[576,128]{1,0:T(8,128)S(1)}, f32[576,128]{1,0:T(8,128)S(1)}, u32[]{:S(2)}, u32[]{:S(2)}) collective-permute-start(f32[576,128]{1,0:T(8,128)S(1)} %get-tuple-element.63), channel_id=1, source_target_pairs={{0,4},{4,0},{8,12},{12,8},{16,20},{20,16},{24,28},{28,24},{1,5},{5... | collective-permute-start | bytes 884744 | tf_op jit(solution)/shard_map/ppermute | solution.py:454
  37.0 8.3 %collective-permute-start.10 = (f32[48,384]{1,0:T(8,128)S(1)}, f32[48,384]{1,0:T(8,128)S(1)}, u32[]{:S(2)}, u32[]{:S(2)}) collective-permute-start(f32[48,384]{1,0:T(8,128)S(1)} %get-tuple-element.67), channel_id=1, source_target_pairs={{0,16},{4,20},{8,24},{12,28},{16,0},{20,4},{24,8},{28,12},{1,17},{... | collective-permute-start | bytes 221192 | tf_op jit(solution)/shard_map/ppermute | solution.py:451
  40.4 6.3 %collective-permute-start.11 = (f32[48,384]{1,0:T(8,128)S(1)}, f32[48,384]{1,0:T(8,128)S(1)}, u32[]{:S(2)}, u32[]{:S(2)}) collective-permute-start(f32[48,384]{1,0:T(8,128)S(1)} %get-tuple-element.68), channel_id=1, source_target_pairs={{0,24},{4,28},{8,16},{12,20},{16,8},{20,12},{24,0},{28,4},{1,25},{... | collective-permute-start | bytes 221192 | tf_op jit(solution)/shard_map/ppermute | solution.py:451
  41.9 5.1 %collective-permute-start.12 = (f32[48,384]{1,0:T(8,128)S(1)}, f32[48,384]{1,0:T(8,128)S(1)}, u32[]{:S(2)}, u32[]{:S(2)}) collective-permute-start(f32[48,384]{1,0:T(8,128)S(1)} %get-tuple-element.69), channel_id=1, source_target_pairs={{0,8},{4,12},{8,0},{12,4},{16,24},{20,28},{24,16},{28,20},{1,9},{5... | collective-permute-start | bytes 221192 | tf_op jit(solution)/shard_map/ppermute | solution.py:451

commit v17 on v16

--- a/solution.py
+++ b/solution.py
@@ -337,17 +337,14 @@
     x_ref[...] = LINEAR_COEFF * x + moved
 
 
-def end_kernel(steps, start_ref, x_ref, poly_ref, send_ref, scratch):
+def end_kernel(hops, steps, start_ref, outer_ref, right_ref, x_ref, poly_ref, send_ref, mine_ref, scratch):
     x = iterate(start_ref[...], steps - 1)
     x_ref[...] = x
+    rows_for(hops, outer_ref, split(right_ref[...]), mine_ref, lax.axis_index("shard") % 2)
     poly = polynomial(split(x))
     poly_ref[...] = poly
     half = take_half(x, jnp.logical_not(is_first()))
     put_thirds(send_ref, flat_of(scratch, LINEAR_COEFF * half + dot(poly, half)))
-
-
-def own_rows_kernel(hops, outer_ref, right_ref, mine_ref):
-    rows_for(hops, outer_ref, split(right_ref[...]), mine_ref, lax.axis_index("shard") % 2)
 
 
 def add_kernel(mine_ref, theirs_ref, *out_refs):
@@ -508,18 +505,22 @@
         partial = other_rows.reshape(tiles_here, 2, rows_here, full)
         other_rows = lax.dynamic_index_in_dim(partial, 1 - parity, 1, keepdims=False)
     got_rows = partner(other_rows)
-    x, poly, send = call(
-        functools.partial(end_kernel, NS_ITERS - 2), [square, square, flat], [(3, full, LANES)], 9, full, "end"
-    )(after(x, other_rows))
+    x, poly, send, own_rows = call(
+        functools.partial(end_kernel, hops, NS_ITERS - 2),
+        [square, square, flat, strips],
+        [(3, full, LANES)],
+        9,
+        full,
+        "end",
+    )(after(x, other_rows), outer, right)
     back = partner(send)
     keep, new_left, new_right = call(rest_kernel, [flat, flat, flat], [(3, full, LANES)], 1.5, full, "rest")(
         x, poly, grad, new_stat, other
     )
     if near:
-        (own_rows,) = call(functools.partial(own_rows_kernel, hops), [strips], [], 0.5, full, "own_rows")(
-            after(outer, send), right
+        kept, *sums = call(add_kernel, [block] * (1 + len(hops)), [], 0.1, full, "add")(
+            after(own_rows, send), after(got_rows, send)
         )
-        kept, *sums = call(add_kernel, [block] * (1 + len(hops)), [], 0.1, full, "add")(own_rows, after(got_rows, send))
         returned = [hop_by(x, hop) for hop, x in zip(hops, sums)]
         update = call(
             functools.partial(rows_kernel, hops),

time: 47.9 us -> 47.6 us (level)
    pallas_call x2 -> x1, Pallas kernels: 6.05 us -> 5.77 us  [local(): call(functools.partial(end_kernel, hops, NS_ITERS - 2), [square, square,...]
where the time goes in v17:
time: 47.6 us; the launch traced here: 47.5 us
  starting transfers between devices  19.2 us (40%)
  Pallas kernels  18.8 us (39%)
  waiting for transfers between devices  8.58 us (18%)
  between operations  0.78 us (2%)
    ppermute x6, starting transfers between devices, hop_by(): return lax.ppermute(x, 'shard', [(i, i ^ 2 * hop) for i in range(size)])  9.61 us
    ppermute x7, starting transfers between devices, partner(): return lax.ppermute(x, 'shard', pairs)  8.73 us
    ppermute x6, waiting for transfers between devices, hop_by(): return lax.ppermute(x, 'shard', [(i, i ^ 2 * hop) for i in range(size)])  6.02 us
    pallas_call x1, Pallas kernels, local(): call(functools.partial(end_kernel, hops, NS_ITERS - 2), [square, square,...  5.77 us
    pallas_call x1, Pallas kernels, local(): call(functools.partial(update_kernel, hops), [flat, flat, strips, wide, s...  3.21 us
    pallas_call x1, Pallas kernels, local(): call(begin_kernel, [square, wide], [(2, full // 2, LANES)], 7, full, 'beg...  2.77 us
    ppermute x7, waiting for transfers between devices, partner(): return lax.ppermute(x, 'shard', pairs)  2.56 us
    pallas_call x1, Pallas kernels, local(): call(rest_kernel, [flat, flat, flat], [(3, full, LANES)], 1.5, full, 'rest')  2.06 us
  transfers between devices with their start and end apart: 14, of which 7 were waited for; matrix products, arithmetic and copies ran while one was open for 0% of the time, Pallas kernels for 29%

profile of v17, /device:TPU:0, one launch (start us, length us, event | category | flops | bytes accessed | tf_op | source)
XLA Modules:
  0.0 47.5 jit_solution(11073000640125850135)
XLA Ops:
  0.6 0.0 copy-start
  0.6 0.0 copy-start.1
  0.7 0.0 copy-start.2
  0.7 0.0 copy-start.3
  0.7 1.3 %pack.1 = (f32[720,128]{1,0:T(8,128)S(1)}, f32[192,128]{1,0:T(8,128)S(1)}, f32[48,384]{1,0:T(8,128)S(1)}, f32[48,384]{1,0:T(8,128)S(1)}, f32[48,384]{1,0:T(8,128)S(1)}) custom-call(f32[576,128]{1,0:T(8,128)} %bitcast.12, f32[576,128]{1,0:T(8,128)} %bitcast.14, f32[576,128]{1,0:T(8,128)} %bitcast.18, f32[576,128]{1,0:T(8,128)} %bitcast.16, f32[4,48,384]{2,1,0:T(8,128)} %refs_0_.1), custom_call_target="tpu_custom_call" | custom-call | flops 33973864 | bytes 2359296 | tf_op jit(solution)/shard_map/pack/pallas_call | solution.py:458
  2.0 3.0 %collective-permute-start.3 = (f32[720,128]{1,0:T(8,128)S(1)}, f32[720,128]{1,0:T(8,128)S(1)}, u32[]{:S(2)}, u32[]{:S(2)}) collective-permute-start(f32[720,128]{1,0:T(8,128)S(1)} %get-tuple-element.48), channel_id=1, source_target_pairs={{0,4},{4,0},{8,12},{12,8},{16,20},{20,16},{24,28},{28,24},{1,5},{5... | collective-permute-start | bytes 1105928 | tf_op jit(solution)/shard_map/ppermute | solution.py:451
  5.0 2.6 %collective-permute-start = (f32[48,384]{1,0:T(8,128)S(1)}, f32[48,384]{1,0:T(8,128)S(1)}, u32[]{:S(2)}, u32[]{:S(2)}) collective-permute-start(f32[48,384]{1,0:T(8,128)S(1)} %get-tuple-element.46), channel_id=1, source_target_pairs={{0,16},{4,20},{8,24},{12,28},{16,0},{20,4},{24,8},{28,12},{1,17},{... | collective-permute-start | bytes 221192 | tf_op jit(solution)/shard_map/ppermute | solution.py:448
  7.6 1.3 %collective-permute-start.4 = (f32[48,384]{1,0:T(8,128)S(1)}, f32[48,384]{1,0:T(8,128)S(1)}, u32[]{:S(2)}, u32[]{:S(2)}) collective-permute-start(f32[48,384]{1,0:T(8,128)S(1)} %get-tuple-element.51), channel_id=1, source_target_pairs={{0,24},{4,28},{8,16},{12,20},{16,8},{20,12},{24,0},{28,4},{1,25},{... | collective-permute-start | bytes 221192 | tf_op jit(solution)/shard_map/ppermute | solution.py:448
  8.9 0.2 collective-permute-start.5
  9.2 3.2 %collective-permute-done.refs_1_ = f32[48,384]{1,0:T(8,128)S(1)} collective-permute-done((f32[48,384]{1,0:T(8,128)S(1)}, f32[48,384]{1,0:T(8,128)S(1)}, u32[]{:S(2)}, u32[]{:S(2)}) %collective-permute-start) | collective-permute-done | bytes 73760 | tf_op jit(solution)/shard_map/ppermute | solution.py:448
  12.4 0.5 collective-permute-start.1
  12.9 1.1 %collective-permute-done.4.refs_2_ = f32[48,384]{1,0:T(8,128)S(1)} collective-permute-done((f32[48,384]{1,0:T(8,128)S(1)}, f32[48,384]{1,0:T(8,128)S(1)}, u32[]{:S(2)}, u32[]{:S(2)}) %collective-permute-start.4) | collective-permute-done | bytes 73760 | tf_op jit(solution)/shard_map/ppermute | solution.py:448
  13.9 0.5 %collective-permute-start.6 = (f32[48,384]{1,0:T(8,128)S(1)}, f32[48,384]{1,0:T(8,128)S(1)}, u32[]{:S(2)}, u32[]{:S(2)}) collective-permute-start(f32[48,384]{1,0:T(8,128)S(1)} %collective-permute-done.4.refs_2_), channel_id=1, source_target_pairs={{0,4},{4,0},{8,12},{12,8},{16,20},{20,16},{24,28},{28,24},{1,5},{5... | collective-permute-start | bytes 221192 | tf_op jit(solution)/shard_map/ppermute | solution.py:451
  14.4 0.0 collective-permute-done.5.refs_3_
  14.4 1.5 %collective-permute-start.7 = (f32[48,384]{1,0:T(8,128)S(1)}, f32[48,384]{1,0:T(8,128)S(1)}, u32[]{:S(2)}, u32[]{:S(2)}) collective-permute-start(f32[48,384]{1,0:T(8,128)S(1)} %collective-permute-done.5.refs_3_), channel_id=1, source_target_pairs={{0,4},{4,0},{8,12},{12,8},{16,20},{20,16},{24,28},{28,24},{1,5},{5... | collective-permute-start | bytes 221192 | tf_op jit(solution)/shard_map/ppermute | solution.py:451
  15.9 1.0 %collective-permute-done.1.refs_4_ = f32[48,384]{1,0:T(8,128)S(1)} collective-permute-done((f32[48,384]{1,0:T(8,128)S(1)}, f32[48,384]{1,0:T(8,128)S(1)}, u32[]{:S(2)}, u32[]{:S(2)}) %collective-permute-start.1) | collective-permute-done | bytes 73760 | tf_op jit(solution)/shard_map/ppermute | solution.py:451
  17.0 1.1 %collective-permute-start.2 = (f32[192,128]{1,0:T(8,128)S(1)}, f32[192,128]{1,0:T(8,128)S(1)}, u32[]{:S(2)}, u32[]{:S(2)}) collective-permute-start(f32[192,128]{1,0:T(8,128)S(1)} %get-tuple-element.47), channel_id=1, source_target_pairs={{0,4},{4,0},{8,12},{12,8},{16,20},{20,16},{24,28},{28,24},{1,5},{5... | collective-permute-start | bytes 294920 | tf_op jit(solution)/shard_map/ppermute | solution.py:451
  18.1 0.0 collective-permute-done.3.got_ref
  18.1 0.0 copy-done
  18.1 0.0 copy-done.1
  18.1 0.0 copy-done.2
  18.1 0.0 copy-done.3
  18.1 0.7 %prepare.1 = (f32[384,384]{1,0:T(8,128)S(1)}, f32[384,384]{1,0:T(8,128)S(1)}, f32[384,256]{1,0:T(8,128)S(1)}, f32[576,128]{1,0:T(8,128)S(1)}, f32[576,128]{1,0:T(8,128)S(1)}) custom-call(f32[576,128]{1,0:T(8,128)S(1)} %bitcast.13, f32[576,128]{1,0:T(8,128)S(1)} %bitcast.15, f32[576,128]{1,0:T(8,128)S(1)} %bitcast.19, f32[576,128]{1,0:T(8,128)S(1)} %bitcast.17, ...), custom_call_target="tpu_custom_call" | custom-call | flops 33973864 | bytes 2359296 | tf_op jit(solution)/shard_map/prepare/pallas_call | solution.py:483
  18.8 0.0 collective-permute-done.6.refs_5_
  18.9 0.9 %collective-permute-start.8 = (f32[576,128]{1,0:T(8,128)S(1)}, f32[576,128]{1,0:T(8,128)S(1)}, u32[]{:S(2)}, u32[]{:S(2)}) collective-permute-start(f32[576,128]{1,0:T(8,128)S(1)} %bitcast.20), channel_id=1, source_target_pairs={{0,4},{4,5},{5,1},{1,0},{8,12},{12,13},{13,9},{9,8},{16,20},{20,21... | collective-permute-start | bytes 884744 | tf_op jit(solution)/shard_map/ppermute | solution.py:497
  19.8 0.5 %collective-permute-done.7.refs_6_ = f32[48,384]{1,0:T(8,128)S(1)} collective-permute-done((f32[48,384]{1,0:T(8,128)S(1)}, f32[48,384]{1,0:T(8,128)S(1)}, u32[]{:S(2)}, u32[]{:S(2)}) %collective-permute-start.7) | collective-permute-done | bytes 73760 | tf_op jit(solution)/shard_map/ppermute | solution.py:451
  20.3 0.0 copy-done.4
  20.3 1.4 %products.1 = (f32[384,384]{1,0:T(8,128)S(1)}, f32[384,384]{1,0:T(8,128)S(1)}, f32[384,384]{1,0:T(8,128)S(1)}) custom-call(f32[384,384]{1,0:T(8,128)S(1)} %get-tuple-element.49.basis_ref, f32[384,384]{1,0:T(8,128)S(1)} %get-tuple-element.50.known_ref, f32[720,128]{1,0:T(8,128)S(1)} %collective-permute-done.3.got_ref, f32[4,48,384]{2,1,0:T(8,128)S(1)} %copy-done.4, ...), custom_call_target="tpu_custom_call" | custom-call | flops 1019215872 | bytes 2359296 | tf_op jit(solution)/shard_map/products/pallas_call | solution.py:486
  21.7 1.0 %collective-permute-done.2.corner_ref = f32[192,128]{1,0:T(8,128)S(1)} collective-permute-done((f32[192,128]{1,0:T(8,128)S(1)}, f32[192,128]{1,0:T(8,128)S(1)}, u32[]{:S(2)}, u32[]{:S(2)}) %collective-permute-start.2) | collective-permute-done | bytes 98336 | tf_op jit(solution)/shard_map/ppermute | solution.py:451
  22.7 2.8 %begin.1 = (f32[384,384]{1,0:T(8,128)S(1)}, f32[384,256]{1,0:T(8,128)S(1)}) custom-call(f32[192,128]{1,0:T(8,128)S(1)} %collective-permute-done.2.corner_ref, f32[384,384]{1,0:T(8,128)S(1)} %get-tuple-element.53.power_ref, f32[384,384]{1,0:T(8,128)S(1)} %get-tuple-element.49.basis_ref, f32[384,384]{1,0:T(8,128)S(1)} %get-tuple-element.54.grad_ref, ...), custom_call_target="tpu_custom_call" | custom-call | flops 2378170368 | bytes 2359296 | tf_op jit(solution)/shard_map/begin/pallas_call | solution.py:498
  25.5 0.0 collective-permute-done.8.other_left_ref
  25.5 0.0 copy-done.5
  25.5 0.0 copy-done.6
  25.5 3.2 %update.1 = (f32[576,128]{1,0:T(8,128)}, f32[576,128]{1,0:T(8,128)}, f32[4,48,384]{2,1,0:T(8,128)S(1)}, f32[384,256]{1,0:T(8,128)S(1)}, f32[384,384]{1,0:T(8,128)S(1)}) custom-call(f32[384,256]{1,0:T(8,128)S(1)} %get-tuple-element.56.inner_ref, f32[384,384]{1,0:T(8,128)S(1)} %get-tuple-element.49.basis_ref, f32[576,128]{1,0:T(8,128)S(1)} %get-tuple-element.57.left_ref, ...), custom_call_target="tpu_custom_call" | custom-call | flops 1698693120 | bytes 2359296 | tf_op jit(solution)/shard_map/update/pallas_call | solution.py:501
  28.7 1.0 %collective-permute-start.9 = (f32[4,48,384]{2,1,0:T(8,128)S(1)}, f32[4,48,384]{2,1,0:T(8,128)S(1)}, u32[]{:S(2)}, u32[]{:S(2)}) collective-permute-start(f32[4,48,384]{2,1,0:T(8,128)S(1)} %get-tuple-element.61), channel_id=1, source_target_pairs={{0,4},{4,0},{8,12},{12,8},{16,20},{20,16},{24,28},{28,24},{1,5},{5... | collective-permute-start | bytes 884744 | tf_op jit(solution)/shard_map/ppermute | solution.py:451
  29.7 5.8 %end.1 = (f32[384,384]{1,0:T(8,128)S(1)}, f32[384,384]{1,0:T(8,128)S(1)}, f32[576,128]{1,0:T(8,128)S(1)}, f32[4,48,384]{2,1,0:T(8,128)S(1)}) custom-call(f32[384,384]{1,0:T(8,128)S(1)} %get-tuple-element.62.start_ref, f32[384,256]{1,0:T(8,128)S(1)} %get-tuple-element.63.outer_ref, f32[384,256]{1,0:T(8,128)S(1)} %get-tuple-element.55.right_ref), custom_call_target="tpu_custom_call" | custom-call | flops 3057647616 | bytes 2359296 | tf_op jit(solution)/shard_map/end/pallas_call | solution.py:508
  35.5 1.1 %collective-permute-start.13 = (f32[576,128]{1,0:T(8,128)S(1)}, f32[576,128]{1,0:T(8,128)S(1)}, u32[]{:S(2)}, u32[]{:S(2)}) collective-permute-start(f32[576,128]{1,0:T(8,128)S(1)} %get-tuple-element.65), channel_id=1, source_target_pairs={{0,4},{4,0},{8,12},{12,8},{16,20},{20,16},{24,28},{28,24},{1,5},{5... | collective-permute-start | bytes 884744 | tf_op jit(solution)/shard_map/ppermute | solution.py:451
  36.6 0.0 collective-permute-done.9.theirs_ref
  36.6 3.7 %collective-permute-start.10 = (f32[48,384]{1,0:T(8,128)S(1)}, f32[48,384]{1,0:T(8,128)S(1)}, u32[]{:S(2)}, u32[]{:S(2)}) collective-permute-start(f32[48,384]{1,0:T(8,128)S(1)} %get-tuple-element.69), channel_id=1, source_target_pairs={{0,16},{4,20},{8,24},{12,28},{16,0},{20,4},{24,8},{28,12},{1,17},{... | collective-permute-start | bytes 221192 | tf_op jit(solution)/shard_map/ppermute | solution.py:448
  40.3 1.3 %collective-permute-start.11 = (f32[48,384]{1,0:T(8,128)S(1)}, f32[48,384]{1,0:T(8,128)S(1)}, u32[]{:S(2)}, u32[]{:S(2)}) collective-permute-start(f32[48,384]{1,0:T(8,128)S(1)} %get-tuple-element.70), channel_id=1, source_target_pairs={{0,24},{4,28},{8,16},{12,20},{16,8},{20,12},{24,0},{28,4},{1,25},{... | collective-permute-start | bytes 221192 | tf_op jit(solution)/shard_map/ppermute | solution.py:448
  41.6 0.5 %collective-permute-start.12 = (f32[48,384]{1,0:T(8,128)S(1)}, f32[48,384]{1,0:T(8,128)S(1)}, u32[]{:S(2)}, u32[]{:S(2)}) collective-permute-start(f32[48,384]{1,0:T(8,128)S(1)} %get-tuple-element.71), channel_id=1, source_target_pairs={{0,8},{4,12},{8,0},{12,4},{16,24},{20,28},{24,16},{28,20},{1,9},{5... | collective-permute-start | bytes 221192 | tf_op jit(solution)/shard_map/ppermute | solution.py:448
  42.1 2.1 %rest.1 = (f32[576,128]{1,0:T(8,128)S(1)}, f32[576,128]{1,0:T(8,128)}, f32[576,128]{1,0:T(8,128)}) custom-call(f32[384,384]{1,0:T(8,128)S(1)} %get-tuple-element.74.x_ref, f32[384,384]{1,0:T(8,128)S(1)} %get-tuple-element.75.poly_ref, f32[384,384]{1,0:T(8,128)S(1)} %get-tuple-element.54.grad_ref, f32[384,384]{1,0:T(8,128)S(1)} %get-tuple-element.76.new_stat_ref, ...), custom_call_target="tpu_custom_call" | custom-call | flops 509607936 | bytes 2359296 | tf_op jit(solution)/shard_map/rest/pallas_call | solution.py:517
  44.1 0.0 collective-permute-done.13.back_ref
  44.1 0.8 %bases.1 = (f32[576,128]{1,0:T(8,128)}, f32[576,128]{1,0:T(8,128)}) custom-call(f32[576,128]{1,0:T(8,128)S(1)} %get-tuple-element.80.keep_ref, f32[576,128]{1,0:T(8,128)S(1)} %collective-permute-done.13.back_ref), custom_call_target="tpu_custom_call" | custom-call | flops 33973864 | bytes 2359296 | tf_op jit(solution)/shard_map/bases/pallas_call | solution.py:539
  45.0 0.0 collective-permute-done.10.refs_1_
  45.0 1.6 %collective-permute-done.11.refs_2_ = f32[48,384]{1,0:T(8,128)S(1)} collective-permute-done((f32[48,384]{1,0:T(8,128)S(1)}, f32[48,384]{1,0:T(8,128)S(1)}, u32[]{:S(2)}, u32[]{:S(2)}) %collective-permute-start.11) | collective-permute-done | bytes 73760 | tf_op jit(solution)/shard_map/ppermute | solution.py:448
  46.6 0.1 collective-permute-done.12.refs_3_
  46.7 0.7 %rows.1 = f32[4,48,384]{2,1,0:T(8,128)} custom-call(f32[48,384]{1,0:T(8,128)S(1)} %get-tuple-element.68.refs_0_, f32[48,384]{1,0:T(8,128)S(1)} %collective-permute-done.10.refs_1_, f32[48,384]{1,0:T(8,128)S(1)} %collective-permute-done.11.refs_2_, f32[48,384]{1,0:T(8,128)S(1)} %collective-permute-done.12.refs_3_), custom_call_target="tpu_custom_call" | custom-call | flops 33973864 | bytes 2359296 | tf_op jit(solution)/shard_map/rows/pallas_call | solution.py:525
  (4 shorter events, 0.0 us)
Async XLA Ops:
  0.6 17.4 %copy-start = (f32[1,73728]{1,0:T(1,128)S(1)}, f32[1,73728]{1,0:T(1,128)}, u32[]{:S(2)}) copy-start(f32[1,73728]{1,0:T(1,128)} %param.10) | copy-start | bytes 884740
  0.6 17.4 %copy-start.1 = (f32[1,73728]{1,0:T(1,128)S(1)}, f32[1,73728]{1,0:T(1,128)}, u32[]{:S(2)}) copy-start(f32[1,73728]{1,0:T(1,128)} %param.11) | copy-start | bytes 884740
  0.7 17.4 %copy-start.2 = (f32[1,73728]{1,0:T(1,128)S(1)}, f32[1,73728]{1,0:T(1,128)}, u32[]{:S(2)}) copy-start(f32[1,73728]{1,0:T(1,128)} %param.13) | copy-start | bytes 884740
  0.7 17.4 %copy-start.3 = (f32[1,73728]{1,0:T(1,128)S(1)}, f32[1,73728]{1,0:T(1,128)}, u32[]{:S(2)}) copy-start(f32[1,73728]{1,0:T(1,128)} %param.12) | copy-start | bytes 884740
  2.0 16.1 %collective-permute-start.3 = (f32[720,128]{1,0:T(8,128)S(1)}, f32[720,128]{1,0:T(8,128)S(1)}, u32[]{:S(2)}, u32[]{:S(2)}) collective-permute-start(f32[720,128]{1,0:T(8,128)S(1)} %get-tuple-element.48), channel_id=1, source_target_pairs={{0,4},{4,0},{8,12},{12,8},{16,20},{20,16},{24,28},{28,24},{1,5},{5... | collective-permute-start | bytes 1105928 | tf_op jit(solution)/shard_map/ppermute | solution.py:451
  5.0 7.4 %collective-permute-start = (f32[48,384]{1,0:T(8,128)S(1)}, f32[48,384]{1,0:T(8,128)S(1)}, u32[]{:S(2)}, u32[]{:S(2)}) collective-permute-start(f32[48,384]{1,0:T(8,128)S(1)} %get-tuple-element.46), channel_id=1, source_target_pairs={{0,16},{4,20},{8,24},{12,28},{16,0},{20,4},{24,8},{28,12},{1,17},{... | collective-permute-start | bytes 221192 | tf_op jit(solution)/shard_map/ppermute | solution.py:448
  7.6 6.3 %collective-permute-start.4 = (f32[48,384]{1,0:T(8,128)S(1)}, f32[48,384]{1,0:T(8,128)S(1)}, u32[]{:S(2)}, u32[]{:S(2)}) collective-permute-start(f32[48,384]{1,0:T(8,128)S(1)} %get-tuple-element.51), channel_id=1, source_target_pairs={{0,24},{4,28},{8,16},{12,20},{16,8},{20,12},{24,0},{28,4},{1,25},{... | collective-permute-start | bytes 221192 | tf_op jit(solution)/shard_map/ppermute | solution.py:448
  8.9 5.5 %collective-permute-start.5 = (f32[48,384]{1,0:T(8,128)S(1)}, f32[48,384]{1,0:T(8,128)S(1)}, u32[]{:S(2)}, u32[]{:S(2)}) collective-permute-start(f32[48,384]{1,0:T(8,128)S(1)} %get-tuple-element.52), channel_id=1, source_target_pairs={{0,8},{4,12},{8,0},{12,4},{16,24},{20,28},{24,16},{28,20},{1,9},{5... | collective-permute-start | bytes 221192 | tf_op jit(solution)/shard_map/ppermute | solution.py:448
  12.4 4.6 %collective-permute-start.1 = (f32[48,384]{1,0:T(8,128)S(1)}, f32[48,384]{1,0:T(8,128)S(1)}, u32[]{:S(2)}, u32[]{:S(2)}) collective-permute-start(f32[48,384]{1,0:T(8,128)S(1)} %collective-permute-done.refs_1_), channel_id=1, source_target_pairs={{0,4},{4,0},{8,12},{12,8},{16,20},{20,16},{24,28},{28,24},{1,5},{5... | collective-permute-start | bytes 221192 | tf_op jit(solution)/shard_map/ppermute | solution.py:451
  13.9 5.0 %collective-permute-start.6 = (f32[48,384]{1,0:T(8,128)S(1)}, f32[48,384]{1,0:T(8,128)S(1)}, u32[]{:S(2)}, u32[]{:S(2)}) collective-permute-start(f32[48,384]{1,0:T(8,128)S(1)} %collective-permute-done.4.refs_2_), channel_id=1, source_target_pairs={{0,4},{4,0},{8,12},{12,8},{16,20},{20,16},{24,28},{28,24},{1,5},{5... | collective-permute-start | bytes 221192 | tf_op jit(solution)/shard_map/ppermute | solution.py:451
  14.4 5.9 %collective-permute-start.7 = (f32[48,384]{1,0:T(8,128)S(1)}, f32[48,384]{1,0:T(8,128)S(1)}, u32[]{:S(2)}, u32[]{:S(2)}) collective-permute-start(f32[48,384]{1,0:T(8,128)S(1)} %collective-permute-done.5.refs_3_), channel_id=1, source_target_pairs={{0,4},{4,0},{8,12},{12,8},{16,20},{20,16},{24,28},{28,24},{1,5},{5... | collective-permute-start | bytes 221192 | tf_op jit(solution)/shard_map/ppermute | solution.py:451
  17.0 3.4 %copy-start.4 = (f32[4,48,384]{2,1,0:T(8,128)S(1)}, f32[4,48,384]{2,1,0:T(8,128)}, u32[]{:S(2)}) copy-start(f32[4,48,384]{2,1,0:T(8,128)} %refs_0_.1) | copy-start | bytes 884740
  17.0 5.7 %collective-permute-start.2 = (f32[192,128]{1,0:T(8,128)S(1)}, f32[192,128]{1,0:T(8,128)S(1)}, u32[]{:S(2)}, u32[]{:S(2)}) collective-permute-start(f32[192,128]{1,0:T(8,128)S(1)} %get-tuple-element.47), channel_id=1, source_target_pairs={{0,4},{4,0},{8,12},{12,8},{16,20},{20,16},{24,28},{28,24},{1,5},{5... | collective-permute-start | bytes 294920 | tf_op jit(solution)/shard_map/ppermute | solution.py:451
  18.9 6.6 %collective-permute-start.8 = (f32[576,128]{1,0:T(8,128)S(1)}, f32[576,128]{1,0:T(8,128)S(1)}, u32[]{:S(2)}, u32[]{:S(2)}) collective-permute-start(f32[576,128]{1,0:T(8,128)S(1)} %bitcast.20), channel_id=1, source_target_pairs={{0,4},{4,5},{5,1},{1,0},{8,12},{12,13},{13,9},{9,8},{16,20},{20,21... | collective-permute-start | bytes 884744 | tf_op jit(solution)/shard_map/ppermute | solution.py:497
  22.7 2.8 %copy-start.5 = (f32[1,73728]{1,0:T(1,128)S(1)}, f32[1,73728]{1,0:T(1,128)}, u32[]{:S(2)}) copy-start(f32[1,73728]{1,0:T(1,128)} %param.8) | copy-start | bytes 884740
  22.7 2.8 %copy-start.6 = (f32[1,73728]{1,0:T(1,128)S(1)}, f32[1,73728]{1,0:T(1,128)}, u32[]{:S(2)}) copy-start(f32[1,73728]{1,0:T(1,128)} %param.9) | copy-start | bytes 884740
  28.7 7.9 %collective-permute-start.9 = (f32[4,48,384]{2,1,0:T(8,128)S(1)}, f32[4,48,384]{2,1,0:T(8,128)S(1)}, u32[]{:S(2)}, u32[]{:S(2)}) collective-permute-start(f32[4,48,384]{2,1,0:T(8,128)S(1)} %get-tuple-element.61), channel_id=1, source_target_pairs={{0,4},{4,0},{8,12},{12,8},{16,20},{20,16},{24,28},{28,24},{1,5},{5... | collective-permute-start | bytes 884744 | tf_op jit(solution)/shard_map/ppermute | solution.py:451
  35.5 8.6 %collective-permute-start.13 = (f32[576,128]{1,0:T(8,128)S(1)}, f32[576,128]{1,0:T(8,128)S(1)}, u32[]{:S(2)}, u32[]{:S(2)}) collective-permute-start(f32[576,128]{1,0:T(8,128)S(1)} %get-tuple-element.65), channel_id=1, source_target_pairs={{0,4},{4,0},{8,12},{12,8},{16,20},{20,16},{24,28},{28,24},{1,5},{5... | collective-permute-start | bytes 884744 | tf_op jit(solution)/shard_map/ppermute | solution.py:451
  36.6 8.3 %collective-permute-start.10 = (f32[48,384]{1,0:T(8,128)S(1)}, f32[48,384]{1,0:T(8,128)S(1)}, u32[]{:S(2)}, u32[]{:S(2)}) collective-permute-start(f32[48,384]{1,0:T(8,128)S(1)} %get-tuple-element.69), channel_id=1, source_target_pairs={{0,16},{4,20},{8,24},{12,28},{16,0},{20,4},{24,8},{28,12},{1,17},{... | collective-permute-start | bytes 221192 | tf_op jit(solution)/shard_map/ppermute | solution.py:448
  40.3 6.3 %collective-permute-start.11 = (f32[48,384]{1,0:T(8,128)S(1)}, f32[48,384]{1,0:T(8,128)S(1)}, u32[]{:S(2)}, u32[]{:S(2)}) collective-permute-start(f32[48,384]{1,0:T(8,128)S(1)} %get-tuple-element.70), channel_id=1, source_target_pairs={{0,24},{4,28},{8,16},{12,20},{16,8},{20,12},{24,0},{28,4},{1,25},{... | collective-permute-start | bytes 221192 | tf_op jit(solution)/shard_map/ppermute | solution.py:448
  41.6 5.1 %collective-permute-start.12 = (f32[48,384]{1,0:T(8,128)S(1)}, f32[48,384]{1,0:T(8,128)S(1)}, u32[]{:S(2)}, u32[]{:S(2)}) collective-permute-start(f32[48,384]{1,0:T(8,128)S(1)} %get-tuple-element.71), channel_id=1, source_target_pairs={{0,8},{4,12},{8,0},{12,4},{16,24},{20,28},{24,16},{28,20},{1,9},{5... | collective-permute-start | bytes 221192 | tf_op jit(solution)/shard_map/ppermute | solution.py:448

commit v18 on v17

--- a/solution.py
+++ b/solution.py
@@ -231,14 +231,27 @@
 
 
 def prepare_kernel(
-    l_stat_ref, r_stat_ref, l_basis_ref, r_basis_ref, got_ref, basis_ref, known_ref, right_ref, other_ref, copy_ref, scratch
+    l_stat_ref,
+    r_stat_ref,
+    l_basis_ref,
+    r_basis_ref,
+    got_ref,
+    basis_ref,
+    known_ref,
+    right_ref,
+    turned_ref,
+    other_ref,
+    copy_ref,
+    scratch,
 ):
     left, first = is_left(), is_first()
     own = pick(left, thirds(l_basis_ref), thirds(r_basis_ref))
     got = thirds(got_ref, 0, l_basis_ref.shape[0])
     basis_ref[...] = whole_of(scratch, pick(first, own, got), pick(first, got, own))
     known_ref[...] = 0.5 * known_part(first, pick(left, thirds(l_stat_ref), thirds(r_stat_ref)), scratch)
-    right_ref[...] = half_of(scratch, thirds(r_basis_ref))
+    right = half_of(scratch, thirds(r_basis_ref))
+    right_ref[...] = right
+    turned_ref[...] = right.T
     other_ref[...] = jnp.where(left, r_stat_ref[...], l_stat_ref[...])
     copy_ref[...] = l_basis_ref[...]
 
@@ -268,7 +281,7 @@
     power_ref[...] = dot(stat, basis_ref[...])
 
 
-def begin_kernel(corner_ref, power_ref, basis_ref, grad_ref, right_ref, x_ref, inner_ref, scratch):
+def begin_kernel(corner_ref, power_ref, basis_ref, grad_ref, turned_ref, x_ref, inner_ref, scratch):
     first = is_first()
     corner = corner_part(corner_ref, scratch)
     rows, wide = corner.shape
@@ -276,11 +289,11 @@
     basis = jnp.concatenate([basis, jnp.zeros((wide - rows, 2 * rows), F32)], axis=0)
     term = 0.5 * dot(corner, basis)
     power = power_ref[...] + jnp.concatenate([jnp.where(first, 0.0, term), jnp.where(first, term, 0.0)], axis=0)
-    grad_parts, right_parts = split(grad_ref[...]), split(right_ref[...])
+    grad_parts, turned_parts = split(grad_ref[...]), split(turned_ref[...])
     x = power * (1.0 / jnp.sqrt(jnp.sum(power * power) + NORM_EPS))
     parts = split(x)
     gram = dot_parts(parts, parts, ((1,), (1,)))
-    inner_ref[...] = dot_parts(grad_parts, right_parts)
+    inner_ref[...] = dot_parts(turned_parts, grad_parts, ((1,), (1,)))
     gram_parts = split(gram)
     poly = CUBIC_COEFF * gram + QUINTIC_COEFF * dot_parts(gram_parts, gram_parts)
     x_ref[...] = LINEAR_COEFF * x + dot_parts(split(poly), parts)
@@ -319,7 +332,8 @@
     gram = dot_parts(parts, parts, ((1,), (1,)))
     own, got = thirds(left_ref), thirds(other_left_ref)
     basis_left = jnp.where(left, basis_ref[...], whole_of(scratch, pick(first, own, got), pick(first, got, own)))
-    rotated = dot(basis_left.T, inner_ref[...])
+    left_parts = split(basis_left)
+    rotated = dot_parts(split(inner_ref[...]), left_parts).T
     gram_parts = split(gram)
     square = dot_parts(gram_parts, gram_parts)
     rotated = flat_of(scratch, rotated)
@@ -330,7 +344,7 @@
     put_thirds(new_one_ref, new_one)
     put_thirds(new_two_ref, new_two)
     direction = [m / (jnp.sqrt(v) + ADAM_EPS) for m, v in zip(new_one, new_two)]
-    outer_ref[...] = dot_parts(split(basis_left), split(half_of(scratch, direction)))
+    outer_ref[...] = dot_parts(left_parts, split(half_of(scratch, direction)))
     poly_parts = split(CUBIC_COEFF * gram + QUINTIC_COEFF * square)
     moved = dot_parts(poly_parts, parts)
     rows_for(hops, outer_ref, split(right_ref[...]), theirs_ref, 1 - lax.axis_index("shard") % 2)
@@ -480,8 +494,9 @@
         mine = [mine]
     got_corner = partner(after(corner, theirs[0] if near else mine[0]))
     wide = (full, 2 * LANES)
-    basis, known, right, other, left = call(
-        prepare_kernel, [square, square, wide, flat, flat], [(3, full, LANES)], 0.1, full, "prepare"
+    tall = (2 * LANES, full)
+    basis, known, right, turned, other, left = call(
+        prepare_kernel, [square, square, wide, tall, flat, flat], [(3, full, LANES)], 0.1, full, "prepare"
     )(l_stat, r_stat, l_basis, r_basis, got)
     grad, new_stat, power = call(
         functools.partial(products_kernel, hops), [square, square, square], [], 3, full, "products"
@@ -495,8 +510,8 @@
             cycle += [(place(t + 1, i + 1), place(t + 1, i)), (place(t + 1, i), place(t, i))]
     cycle += [(place(t, i), place(t, i ^ 1)) for t in range(tensors - tensors % 2, tensors) for i in range(size)]
     other_left = lax.ppermute(after(l_basis, basis, *(theirs[:2] if near else mine)), ("shard", "tensor"), cycle)
-    x, inner = call(begin_kernel, [square, wide], [(2, full // 2, LANES)], 7, full, "begin")(
-        got_corner, power, basis, grad, right
+    x, inner = call(begin_kernel, [square, tall], [(2, full // 2, LANES)], 7, full, "begin")(
+        got_corner, power, basis, grad, turned
     )
     new_one, new_two, other_rows, outer, x = call(
         functools.partial(update_kernel, hops), [flat, flat, strips, wide, square], [(3, full, LANES)], 5, full, "update"

time: 47.6 us -> 47.3 us (level)
  no operation moved by 1% of the time
where the time goes in v18:
time: 47.3 us; the launch traced here: 47.2 us
  starting transfers between devices  19.2 us (41%)
  Pallas kernels  18.6 us (39%)
  waiting for transfers between devices  8.57 us (18%)
  between operations  0.77 us (2%)
    ppermute x6, starting transfers between devices, hop_by(): return lax.ppermute(x, 'shard', [(i, i ^ 2 * hop) for i in range(size)])  9.6 us
    ppermute x7, starting transfers between devices, partner(): return lax.ppermute(x, 'shard', pairs)  8.73 us
    ppermute x6, waiting for transfers between devices, hop_by(): return lax.ppermute(x, 'shard', [(i, i ^ 2 * hop) for i in range(size)])  6.02 us
    pallas_call x1, Pallas kernels, local(): call(functools.partial(end_kernel, hops, NS_ITERS - 2), [square, square,...  5.77 us
    pallas_call x1, Pallas kernels, local(): call(begin_kernel, [square, tall], [(2, full // 2, LANES)], 7, full, 'beg...  2.87 us
    pallas_call x1, Pallas kernels, local(): call(functools.partial(update_kernel, hops), [flat, flat, strips, wide, s...  2.84 us
    ppermute x7, waiting for transfers between devices, partner(): return lax.ppermute(x, 'shard', pairs)  2.55 us
    pallas_call x1, Pallas kernels, local(): call(rest_kernel, [flat, flat, flat], [(3, full, LANES)], 1.5, full, 'rest')  2.06 us
  transfers between devices with their start and end apart: 14, of which 7 were waited for; matrix products, arithmetic and copies ran while one was open for 0% of the time, Pallas kernels for 29%

profile of v18, /device:TPU:0, one launch (start us, length us, event | category | flops | bytes accessed | tf_op | source)
XLA Modules:
  0.0 47.2 jit_solution(7858908458368496292)
XLA Ops:
  0.6 0.0 copy-start
  0.6 0.0 copy-start.1
  0.7 0.0 copy-start.2
  0.7 0.0 copy-start.3
  0.7 1.3 %pack.1 = (f32[720,128]{1,0:T(8,128)S(1)}, f32[192,128]{1,0:T(8,128)S(1)}, f32[48,384]{1,0:T(8,128)S(1)}, f32[48,384]{1,0:T(8,128)S(1)}, f32[48,384]{1,0:T(8,128)S(1)}) custom-call(f32[576,128]{1,0:T(8,128)} %bitcast.12, f32[576,128]{1,0:T(8,128)} %bitcast.14, f32[576,128]{1,0:T(8,128)} %bitcast.18, f32[576,128]{1,0:T(8,128)} %bitcast.16, f32[4,48,384]{2,1,0:T(8,128)} %refs_0_.1), custom_call_target="tpu_custom_call" | custom-call | flops 33973864 | bytes 2359296 | tf_op jit(solution)/shard_map/pack/pallas_call | solution.py:472
  2.0 3.0 %collective-permute-start.3 = (f32[720,128]{1,0:T(8,128)S(1)}, f32[720,128]{1,0:T(8,128)S(1)}, u32[]{:S(2)}, u32[]{:S(2)}) collective-permute-start(f32[720,128]{1,0:T(8,128)S(1)} %get-tuple-element.49), channel_id=1, source_target_pairs={{0,4},{4,0},{8,12},{12,8},{16,20},{20,16},{24,28},{28,24},{1,5},{5... | collective-permute-start | bytes 1105928 | tf_op jit(solution)/shard_map/ppermute | solution.py:465
  5.0 2.6 %collective-permute-start = (f32[48,384]{1,0:T(8,128)S(1)}, f32[48,384]{1,0:T(8,128)S(1)}, u32[]{:S(2)}, u32[]{:S(2)}) collective-permute-start(f32[48,384]{1,0:T(8,128)S(1)} %get-tuple-element.47), channel_id=1, source_target_pairs={{0,16},{4,20},{8,24},{12,28},{16,0},{20,4},{24,8},{28,12},{1,17},{... | collective-permute-start | bytes 221192 | tf_op jit(solution)/shard_map/ppermute | solution.py:462
  7.6 1.3 %collective-permute-start.4 = (f32[48,384]{1,0:T(8,128)S(1)}, f32[48,384]{1,0:T(8,128)S(1)}, u32[]{:S(2)}, u32[]{:S(2)}) collective-permute-start(f32[48,384]{1,0:T(8,128)S(1)} %get-tuple-element.52), channel_id=1, source_target_pairs={{0,24},{4,28},{8,16},{12,20},{16,8},{20,12},{24,0},{28,4},{1,25},{... | collective-permute-start | bytes 221192 | tf_op jit(solution)/shard_map/ppermute | solution.py:462
  8.9 0.2 collective-permute-start.5
  9.2 3.2 %collective-permute-done.refs_1_ = f32[48,384]{1,0:T(8,128)S(1)} collective-permute-done((f32[48,384]{1,0:T(8,128)S(1)}, f32[48,384]{1,0:T(8,128)S(1)}, u32[]{:S(2)}, u32[]{:S(2)}) %collective-permute-start) | collective-permute-done | bytes 73760 | tf_op jit(solution)/shard_map/ppermute | solution.py:462
  12.4 0.5 collective-permute-start.1
  12.9 1.1 %collective-permute-done.4.refs_2_ = f32[48,384]{1,0:T(8,128)S(1)} collective-permute-done((f32[48,384]{1,0:T(8,128)S(1)}, f32[48,384]{1,0:T(8,128)S(1)}, u32[]{:S(2)}, u32[]{:S(2)}) %collective-permute-start.4) | collective-permute-done | bytes 73760 | tf_op jit(solution)/shard_map/ppermute | solution.py:462
  13.9 0.5 %collective-permute-start.6 = (f32[48,384]{1,0:T(8,128)S(1)}, f32[48,384]{1,0:T(8,128)S(1)}, u32[]{:S(2)}, u32[]{:S(2)}) collective-permute-start(f32[48,384]{1,0:T(8,128)S(1)} %collective-permute-done.4.refs_2_), channel_id=1, source_target_pairs={{0,4},{4,0},{8,12},{12,8},{16,20},{20,16},{24,28},{28,24},{1,5},{5... | collective-permute-start | bytes 221192 | tf_op jit(solution)/shard_map/ppermute | solution.py:465
  14.4 0.0 collective-permute-done.5.refs_3_
  14.4 1.5 %collective-permute-start.7 = (f32[48,384]{1,0:T(8,128)S(1)}, f32[48,384]{1,0:T(8,128)S(1)}, u32[]{:S(2)}, u32[]{:S(2)}) collective-permute-start(f32[48,384]{1,0:T(8,128)S(1)} %collective-permute-done.5.refs_3_), channel_id=1, source_target_pairs={{0,4},{4,0},{8,12},{12,8},{16,20},{20,16},{24,28},{28,24},{1,5},{5... | collective-permute-start | bytes 221192 | tf_op jit(solution)/shard_map/ppermute | solution.py:465
  15.9 1.0 %collective-permute-done.1.refs_4_ = f32[48,384]{1,0:T(8,128)S(1)} collective-permute-done((f32[48,384]{1,0:T(8,128)S(1)}, f32[48,384]{1,0:T(8,128)S(1)}, u32[]{:S(2)}, u32[]{:S(2)}) %collective-permute-start.1) | collective-permute-done | bytes 73760 | tf_op jit(solution)/shard_map/ppermute | solution.py:465
  17.0 1.1 %collective-permute-start.2 = (f32[192,128]{1,0:T(8,128)S(1)}, f32[192,128]{1,0:T(8,128)S(1)}, u32[]{:S(2)}, u32[]{:S(2)}) collective-permute-start(f32[192,128]{1,0:T(8,128)S(1)} %get-tuple-element.48), channel_id=1, source_target_pairs={{0,4},{4,0},{8,12},{12,8},{16,20},{20,16},{24,28},{28,24},{1,5},{5... | collective-permute-start | bytes 294920 | tf_op jit(solution)/shard_map/ppermute | solution.py:465
  18.1 0.0 collective-permute-done.3.got_ref
  18.1 0.0 copy-done
  18.1 0.0 copy-done.1
  18.1 0.0 copy-done.2
  18.1 0.0 copy-done.3
  18.1 0.7 %prepare.1 = (f32[384,384]{1,0:T(8,128)S(1)}, f32[384,384]{1,0:T(8,128)S(1)}, f32[384,256]{1,0:T(8,128)S(1)}, f32[256,384]{1,0:T(8,128)S(1)}, f32[576,128]{1,0:T(8,128)S(1)}, /*index=5*/f32[576,128]{1,0:T(8,128)S(1)}) custom-call(f32[576,128]{1,0:T(8,128)S(1)} %bitcast.13, f32[576,128]{1,0:T(8,128)S(1)} %bitcast.15, f32[576,128]{1,0:T(8,128)S(1)} %bitcast.19, ...), custom_call_target="tpu_custom_call" | custom-call | flops 33973864 | bytes 2359296 | tf_op jit(solution)/shard_map/prepare/pallas_call | solution.py:498
  18.9 0.0 collective-permute-done.6.refs_5_
  18.9 0.9 %collective-permute-start.8 = (f32[576,128]{1,0:T(8,128)S(1)}, f32[576,128]{1,0:T(8,128)S(1)}, u32[]{:S(2)}, u32[]{:S(2)}) collective-permute-start(f32[576,128]{1,0:T(8,128)S(1)} %bitcast.20), channel_id=1, source_target_pairs={{0,4},{4,5},{5,1},{1,0},{8,12},{12,13},{13,9},{9,8},{16,20},{20,21... | collective-permute-start | bytes 884744 | tf_op jit(solution)/shard_map/ppermute | solution.py:512
  19.8 0.5 %collective-permute-done.7.refs_6_ = f32[48,384]{1,0:T(8,128)S(1)} collective-permute-done((f32[48,384]{1,0:T(8,128)S(1)}, f32[48,384]{1,0:T(8,128)S(1)}, u32[]{:S(2)}, u32[]{:S(2)}) %collective-permute-start.7) | collective-permute-done | bytes 73760 | tf_op jit(solution)/shard_map/ppermute | solution.py:465
  20.3 0.0 copy-done.4
  20.3 1.4 %products.1 = (f32[384,384]{1,0:T(8,128)S(1)}, f32[384,384]{1,0:T(8,128)S(1)}, f32[384,384]{1,0:T(8,128)S(1)}) custom-call(f32[384,384]{1,0:T(8,128)S(1)} %get-tuple-element.50.basis_ref, f32[384,384]{1,0:T(8,128)S(1)} %get-tuple-element.51.known_ref, f32[720,128]{1,0:T(8,128)S(1)} %collective-permute-done.3.got_ref, f32[4,48,384]{2,1,0:T(8,128)S(1)} %copy-done.4, ...), custom_call_target="tpu_custom_call" | custom-call | flops 1019215872 | bytes 2359296 | tf_op jit(solution)/shard_map/products/pallas_call | solution.py:501
  21.7 1.0 %collective-permute-done.2.corner_ref = f32[192,128]{1,0:T(8,128)S(1)} collective-permute-done((f32[192,128]{1,0:T(8,128)S(1)}, f32[192,128]{1,0:T(8,128)S(1)}, u32[]{:S(2)}, u32[]{:S(2)}) %collective-permute-start.2) | collective-permute-done | bytes 98336 | tf_op jit(solution)/shard_map/ppermute | solution.py:465
  22.7 2.9 %begin.1 = (f32[384,384]{1,0:T(8,128)S(1)}, f32[256,384]{1,0:T(8,128)S(1)}) custom-call(f32[192,128]{1,0:T(8,128)S(1)} %collective-permute-done.2.corner_ref, f32[384,384]{1,0:T(8,128)S(1)} %get-tuple-element.54.power_ref, f32[384,384]{1,0:T(8,128)S(1)} %get-tuple-element.50.basis_ref, f32[384,384]{1,0:T(8,128)S(1)} %get-tuple-element.55.grad_ref, ...), custom_call_target="tpu_custom_call" | custom-call | flops 2378170368 | bytes 2359296 | tf_op jit(solution)/shard_map/begin/pallas_call | solution.py:513
  25.6 0.0 collective-permute-done.8.other_left_ref
  25.6 0.0 copy-done.5
  25.6 0.0 copy-done.6
  25.6 2.8 %update.1 = (f32[576,128]{1,0:T(8,128)}, f32[576,128]{1,0:T(8,128)}, f32[4,48,384]{2,1,0:T(8,128)S(1)}, f32[384,256]{1,0:T(8,128)S(1)}, f32[384,384]{1,0:T(8,128)S(1)}) custom-call(f32[256,384]{1,0:T(8,128)S(1)} %get-tuple-element.57.inner_ref, f32[384,384]{1,0:T(8,128)S(1)} %get-tuple-element.50.basis_ref, f32[576,128]{1,0:T(8,128)S(1)} %get-tuple-element.58.left_ref, ...), custom_call_target="tpu_custom_call" | custom-call | flops 1698693120 | bytes 2359296 | tf_op jit(solution)/shard_map/update/pallas_call | solution.py:516
  28.4 0.9 %collective-permute-start.9 = (f32[4,48,384]{2,1,0:T(8,128)S(1)}, f32[4,48,384]{2,1,0:T(8,128)S(1)}, u32[]{:S(2)}, u32[]{:S(2)}) collective-permute-start(f32[4,48,384]{2,1,0:T(8,128)S(1)} %get-tuple-element.63), channel_id=1, source_target_pairs={{0,4},{4,0},{8,12},{12,8},{16,20},{20,16},{24,28},{28,24},{1,5},{5... | collective-permute-start | bytes 884744 | tf_op jit(solution)/shard_map/ppermute | solution.py:465
  29.4 5.8 %end.1 = (f32[384,384]{1,0:T(8,128)S(1)}, f32[384,384]{1,0:T(8,128)S(1)}, f32[576,128]{1,0:T(8,128)S(1)}, f32[4,48,384]{2,1,0:T(8,128)S(1)}) custom-call(f32[384,384]{1,0:T(8,128)S(1)} %get-tuple-element.64.start_ref, f32[384,256]{1,0:T(8,128)S(1)} %get-tuple-element.65.outer_ref, f32[384,256]{1,0:T(8,128)S(1)} %get-tuple-element.59.right_ref), custom_call_target="tpu_custom_call" | custom-call | flops 3057647616 | bytes 2359296 | tf_op jit(solution)/shard_map/end/pallas_call | solution.py:523
  35.1 1.2 %collective-permute-start.13 = (f32[576,128]{1,0:T(8,128)S(1)}, f32[576,128]{1,0:T(8,128)S(1)}, u32[]{:S(2)}, u32[]{:S(2)}) collective-permute-start(f32[576,128]{1,0:T(8,128)S(1)} %get-tuple-element.67), channel_id=1, source_target_pairs={{0,4},{4,0},{8,12},{12,8},{16,20},{20,16},{24,28},{28,24},{1,5},{5... | collective-permute-start | bytes 884744 | tf_op jit(solution)/shard_map/ppermute | solution.py:465
  36.3 0.0 collective-permute-done.9.theirs_ref
  36.3 3.6 %collective-permute-start.10 = (f32[48,384]{1,0:T(8,128)S(1)}, f32[48,384]{1,0:T(8,128)S(1)}, u32[]{:S(2)}, u32[]{:S(2)}) collective-permute-start(f32[48,384]{1,0:T(8,128)S(1)} %get-tuple-element.71), channel_id=1, source_target_pairs={{0,16},{4,20},{8,24},{12,28},{16,0},{20,4},{24,8},{28,12},{1,17},{... | collective-permute-start | bytes 221192 | tf_op jit(solution)/shard_map/ppermute | solution.py:462
  39.9 1.4 %collective-permute-start.11 = (f32[48,384]{1,0:T(8,128)S(1)}, f32[48,384]{1,0:T(8,128)S(1)}, u32[]{:S(2)}, u32[]{:S(2)}) collective-permute-start(f32[48,384]{1,0:T(8,128)S(1)} %get-tuple-element.72), channel_id=1, source_target_pairs={{0,24},{4,28},{8,16},{12,20},{16,8},{20,12},{24,0},{28,4},{1,25},{... | collective-permute-start | bytes 221192 | tf_op jit(solution)/shard_map/ppermute | solution.py:462
  41.3 0.5 %collective-permute-start.12 = (f32[48,384]{1,0:T(8,128)S(1)}, f32[48,384]{1,0:T(8,128)S(1)}, u32[]{:S(2)}, u32[]{:S(2)}) collective-permute-start(f32[48,384]{1,0:T(8,128)S(1)} %get-tuple-element.73), channel_id=1, source_target_pairs={{0,8},{4,12},{8,0},{12,4},{16,24},{20,28},{24,16},{28,20},{1,9},{5... | collective-permute-start | bytes 221192 | tf_op jit(solution)/shard_map/ppermute | solution.py:462
  41.8 2.1 %rest.1 = (f32[576,128]{1,0:T(8,128)S(1)}, f32[576,128]{1,0:T(8,128)}, f32[576,128]{1,0:T(8,128)}) custom-call(f32[384,384]{1,0:T(8,128)S(1)} %get-tuple-element.76.x_ref, f32[384,384]{1,0:T(8,128)S(1)} %get-tuple-element.77.poly_ref, f32[384,384]{1,0:T(8,128)S(1)} %get-tuple-element.55.grad_ref, f32[384,384]{1,0:T(8,128)S(1)} %get-tuple-element.78.new_stat_ref, ...), custom_call_target="tpu_custom_call" | custom-call | flops 509607936 | bytes 2359296 | tf_op jit(solution)/shard_map/rest/pallas_call | solution.py:532
  43.8 0.0 collective-permute-done.13.back_ref
  43.8 0.8 %bases.1 = (f32[576,128]{1,0:T(8,128)}, f32[576,128]{1,0:T(8,128)}) custom-call(f32[576,128]{1,0:T(8,128)S(1)} %get-tuple-element.82.keep_ref, f32[576,128]{1,0:T(8,128)S(1)} %collective-permute-done.13.back_ref), custom_call_target="tpu_custom_call" | custom-call | flops 33973864 | bytes 2359296 | tf_op jit(solution)/shard_map/bases/pallas_call | solution.py:554
  44.7 0.0 collective-permute-done.10.refs_1_
  44.7 1.5 %collective-permute-done.11.refs_2_ = f32[48,384]{1,0:T(8,128)S(1)} collective-permute-done((f32[48,384]{1,0:T(8,128)S(1)}, f32[48,384]{1,0:T(8,128)S(1)}, u32[]{:S(2)}, u32[]{:S(2)}) %collective-permute-start.11) | collective-permute-done | bytes 73760 | tf_op jit(solution)/shard_map/ppermute | solution.py:462
  46.2 0.2 collective-permute-done.12.refs_3_
  46.4 0.7 %rows.1 = f32[4,48,384]{2,1,0:T(8,128)} custom-call(f32[48,384]{1,0:T(8,128)S(1)} %get-tuple-element.70.refs_0_, f32[48,384]{1,0:T(8,128)S(1)} %collective-permute-done.10.refs_1_, f32[48,384]{1,0:T(8,128)S(1)} %collective-permute-done.11.refs_2_, f32[48,384]{1,0:T(8,128)S(1)} %collective-permute-done.12.refs_3_), custom_call_target="tpu_custom_call" | custom-call | flops 33973864 | bytes 2359296 | tf_op jit(solution)/shard_map/rows/pallas_call | solution.py:540
  (4 shorter events, 0.0 us)
Async XLA Ops:
  0.6 17.4 %copy-start = (f32[1,73728]{1,0:T(1,128)S(1)}, f32[1,73728]{1,0:T(1,128)}, u32[]{:S(2)}) copy-start(f32[1,73728]{1,0:T(1,128)} %param.10) | copy-start | bytes 884740
  0.6 17.4 %copy-start.1 = (f32[1,73728]{1,0:T(1,128)S(1)}, f32[1,73728]{1,0:T(1,128)}, u32[]{:S(2)}) copy-start(f32[1,73728]{1,0:T(1,128)} %param.11) | copy-start | bytes 884740
  0.7 17.4 %copy-start.2 = (f32[1,73728]{1,0:T(1,128)S(1)}, f32[1,73728]{1,0:T(1,128)}, u32[]{:S(2)}) copy-start(f32[1,73728]{1,0:T(1,128)} %param.13) | copy-start | bytes 884740
  0.7 17.4 %copy-start.3 = (f32[1,73728]{1,0:T(1,128)S(1)}, f32[1,73728]{1,0:T(1,128)}, u32[]{:S(2)}) copy-start(f32[1,73728]{1,0:T(1,128)} %param.12) | copy-start | bytes 884740
  2.0 16.1 %collective-permute-start.3 = (f32[720,128]{1,0:T(8,128)S(1)}, f32[720,128]{1,0:T(8,128)S(1)}, u32[]{:S(2)}, u32[]{:S(2)}) collective-permute-start(f32[720,128]{1,0:T(8,128)S(1)} %get-tuple-element.49), channel_id=1, source_target_pairs={{0,4},{4,0},{8,12},{12,8},{16,20},{20,16},{24,28},{28,24},{1,5},{5... | collective-permute-start | bytes 1105928 | tf_op jit(solution)/shard_map/ppermute | solution.py:465
  5.0 7.4 %collective-permute-start = (f32[48,384]{1,0:T(8,128)S(1)}, f32[48,384]{1,0:T(8,128)S(1)}, u32[]{:S(2)}, u32[]{:S(2)}) collective-permute-start(f32[48,384]{1,0:T(8,128)S(1)} %get-tuple-element.47), channel_id=1, source_target_pairs={{0,16},{4,20},{8,24},{12,28},{16,0},{20,4},{24,8},{28,12},{1,17},{... | collective-permute-start | bytes 221192 | tf_op jit(solution)/shard_map/ppermute | solution.py:462
  7.6 6.3 %collective-permute-start.4 = (f32[48,384]{1,0:T(8,128)S(1)}, f32[48,384]{1,0:T(8,128)S(1)}, u32[]{:S(2)}, u32[]{:S(2)}) collective-permute-start(f32[48,384]{1,0:T(8,128)S(1)} %get-tuple-element.52), channel_id=1, source_target_pairs={{0,24},{4,28},{8,16},{12,20},{16,8},{20,12},{24,0},{28,4},{1,25},{... | collective-permute-start | bytes 221192 | tf_op jit(solution)/shard_map/ppermute | solution.py:462
  8.9 5.5 %collective-permute-start.5 = (f32[48,384]{1,0:T(8,128)S(1)}, f32[48,384]{1,0:T(8,128)S(1)}, u32[]{:S(2)}, u32[]{:S(2)}) collective-permute-start(f32[48,384]{1,0:T(8,128)S(1)} %get-tuple-element.53), channel_id=1, source_target_pairs={{0,8},{4,12},{8,0},{12,4},{16,24},{20,28},{24,16},{28,20},{1,9},{5... | collective-permute-start | bytes 221192 | tf_op jit(solution)/shard_map/ppermute | solution.py:462
  12.4 4.6 %collective-permute-start.1 = (f32[48,384]{1,0:T(8,128)S(1)}, f32[48,384]{1,0:T(8,128)S(1)}, u32[]{:S(2)}, u32[]{:S(2)}) collective-permute-start(f32[48,384]{1,0:T(8,128)S(1)} %collective-permute-done.refs_1_), channel_id=1, source_target_pairs={{0,4},{4,0},{8,12},{12,8},{16,20},{20,16},{24,28},{28,24},{1,5},{5... | collective-permute-start | bytes 221192 | tf_op jit(solution)/shard_map/ppermute | solution.py:465
  13.9 5.0 %collective-permute-start.6 = (f32[48,384]{1,0:T(8,128)S(1)}, f32[48,384]{1,0:T(8,128)S(1)}, u32[]{:S(2)}, u32[]{:S(2)}) collective-permute-start(f32[48,384]{1,0:T(8,128)S(1)} %collective-permute-done.4.refs_2_), channel_id=1, source_target_pairs={{0,4},{4,0},{8,12},{12,8},{16,20},{20,16},{24,28},{28,24},{1,5},{5... | collective-permute-start | bytes 221192 | tf_op jit(solution)/shard_map/ppermute | solution.py:465
  14.4 5.9 %collective-permute-start.7 = (f32[48,384]{1,0:T(8,128)S(1)}, f32[48,384]{1,0:T(8,128)S(1)}, u32[]{:S(2)}, u32[]{:S(2)}) collective-permute-start(f32[48,384]{1,0:T(8,128)S(1)} %collective-permute-done.5.refs_3_), channel_id=1, source_target_pairs={{0,4},{4,0},{8,12},{12,8},{16,20},{20,16},{24,28},{28,24},{1,5},{5... | collective-permute-start | bytes 221192 | tf_op jit(solution)/shard_map/ppermute | solution.py:465
  17.0 3.3 %copy-start.4 = (f32[4,48,384]{2,1,0:T(8,128)S(1)}, f32[4,48,384]{2,1,0:T(8,128)}, u32[]{:S(2)}) copy-start(f32[4,48,384]{2,1,0:T(8,128)} %refs_0_.1) | copy-start | bytes 884740
  17.0 5.7 %collective-permute-start.2 = (f32[192,128]{1,0:T(8,128)S(1)}, f32[192,128]{1,0:T(8,128)S(1)}, u32[]{:S(2)}, u32[]{:S(2)}) collective-permute-start(f32[192,128]{1,0:T(8,128)S(1)} %get-tuple-element.48), channel_id=1, source_target_pairs={{0,4},{4,0},{8,12},{12,8},{16,20},{20,16},{24,28},{28,24},{1,5},{5... | collective-permute-start | bytes 294920 | tf_op jit(solution)/shard_map/ppermute | solution.py:465
  18.9 6.7 %collective-permute-start.8 = (f32[576,128]{1,0:T(8,128)S(1)}, f32[576,128]{1,0:T(8,128)S(1)}, u32[]{:S(2)}, u32[]{:S(2)}) collective-permute-start(f32[576,128]{1,0:T(8,128)S(1)} %bitcast.20), channel_id=1, source_target_pairs={{0,4},{4,5},{5,1},{1,0},{8,12},{12,13},{13,9},{9,8},{16,20},{20,21... | collective-permute-start | bytes 884744 | tf_op jit(solution)/shard_map/ppermute | solution.py:512
  22.7 2.9 %copy-start.5 = (f32[1,73728]{1,0:T(1,128)S(1)}, f32[1,73728]{1,0:T(1,128)}, u32[]{:S(2)}) copy-start(f32[1,73728]{1,0:T(1,128)} %param.8) | copy-start | bytes 884740
  22.7 2.9 %copy-start.6 = (f32[1,73728]{1,0:T(1,128)S(1)}, f32[1,73728]{1,0:T(1,128)}, u32[]{:S(2)}) copy-start(f32[1,73728]{1,0:T(1,128)} %param.9) | copy-start | bytes 884740
  28.4 7.9 %collective-permute-start.9 = (f32[4,48,384]{2,1,0:T(8,128)S(1)}, f32[4,48,384]{2,1,0:T(8,128)S(1)}, u32[]{:S(2)}, u32[]{:S(2)}) collective-permute-start(f32[4,48,384]{2,1,0:T(8,128)S(1)} %get-tuple-element.63), channel_id=1, source_target_pairs={{0,4},{4,0},{8,12},{12,8},{16,20},{20,16},{24,28},{28,24},{1,5},{5... | collective-permute-start | bytes 884744 | tf_op jit(solution)/shard_map/ppermute | solution.py:465
  35.1 8.7 %collective-permute-start.13 = (f32[576,128]{1,0:T(8,128)S(1)}, f32[576,128]{1,0:T(8,128)S(1)}, u32[]{:S(2)}, u32[]{:S(2)}) collective-permute-start(f32[576,128]{1,0:T(8,128)S(1)} %get-tuple-element.67), channel_id=1, source_target_pairs={{0,4},{4,0},{8,12},{12,8},{16,20},{20,16},{24,28},{28,24},{1,5},{5... | collective-permute-start | bytes 884744 | tf_op jit(solution)/shard_map/ppermute | solution.py:465
  36.3 8.3 %collective-permute-start.10 = (f32[48,384]{1,0:T(8,128)S(1)}, f32[48,384]{1,0:T(8,128)S(1)}, u32[]{:S(2)}, u32[]{:S(2)}) collective-permute-start(f32[48,384]{1,0:T(8,128)S(1)} %get-tuple-element.71), channel_id=1, source_target_pairs={{0,16},{4,20},{8,24},{12,28},{16,0},{20,4},{24,8},{28,12},{1,17},{... | collective-permute-start | bytes 221192 | tf_op jit(solution)/shard_map/ppermute | solution.py:462
  39.9 6.3 %collective-permute-start.11 = (f32[48,384]{1,0:T(8,128)S(1)}, f32[48,384]{1,0:T(8,128)S(1)}, u32[]{:S(2)}, u32[]{:S(2)}) collective-permute-start(f32[48,384]{1,0:T(8,128)S(1)} %get-tuple-element.72), channel_id=1, source_target_pairs={{0,24},{4,28},{8,16},{12,20},{16,8},{20,12},{24,0},{28,4},{1,25},{... | collective-permute-start | bytes 221192 | tf_op jit(solution)/shard_map/ppermute | solution.py:462
  41.3 5.1 %collective-permute-start.12 = (f32[48,384]{1,0:T(8,128)S(1)}, f32[48,384]{1,0:T(8,128)S(1)}, u32[]{:S(2)}, u32[]{:S(2)}) collective-permute-start(f32[48,384]{1,0:T(8,128)S(1)} %get-tuple-element.73), channel_id=1, source_target_pairs={{0,8},{4,12},{8,0},{12,4},{16,24},{20,28},{24,16},{28,20},{1,9},{5... | collective-permute-start | bytes 221192 | tf_op jit(solution)/shard_map/ppermute | solution.py:462

commit v19 on v18

--- a/solution.py
+++ b/solution.py
@@ -256,9 +256,9 @@
     copy_ref[...] = l_basis_ref[...]
 
 
-def products_kernel(hops, basis_ref, known_ref, got_ref, *refs):
+def products_kernel(hops, basis_ref, known_ref, turned_ref, got_ref, *refs):
     left = is_left()
-    grad_ref, stat_ref, power_ref = refs[-3:]
+    grad_ref, stat_ref, power_ref, inner_ref = refs[-4:]
     if hops:
         grads_ref, mine_refs, theirs_refs = refs[0], refs[1 : 1 + len(hops)], refs[1 + len(hops) : 1 + 2 * len(hops)]
         rows = grads_ref.shape[1]
@@ -279,9 +279,10 @@
     stat = known_ref[...] + 0.5 * symmetric_dot(parts, parts, ((1,), (1,)))
     stat_ref[...] = stat
     power_ref[...] = dot(stat, basis_ref[...])
-
-
-def begin_kernel(corner_ref, power_ref, basis_ref, grad_ref, turned_ref, x_ref, inner_ref, scratch):
+    inner_ref[...] = dot(turned_ref[...], grad, ((1,), (1,)))
+
+
+def begin_kernel(corner_ref, power_ref, basis_ref, x_ref, scratch):
     first = is_first()
     corner = corner_part(corner_ref, scratch)
     rows, wide = corner.shape
@@ -289,14 +290,7 @@
     basis = jnp.concatenate([basis, jnp.zeros((wide - rows, 2 * rows), F32)], axis=0)
     term = 0.5 * dot(corner, basis)
     power = power_ref[...] + jnp.concatenate([jnp.where(first, 0.0, term), jnp.where(first, term, 0.0)], axis=0)
-    grad_parts, turned_parts = split(grad_ref[...]), split(turned_ref[...])
-    x = power * (1.0 / jnp.sqrt(jnp.sum(power * power) + NORM_EPS))
-    parts = split(x)
-    gram = dot_parts(parts, parts, ((1,), (1,)))
-    inner_ref[...] = dot_parts(turned_parts, grad_parts, ((1,), (1,)))
-    gram_parts = split(gram)
-    poly = CUBIC_COEFF * gram + QUINTIC_COEFF * dot_parts(gram_parts, gram_parts)
-    x_ref[...] = LINEAR_COEFF * x + dot_parts(split(poly), parts)
+    x_ref[...] = iterate(power * (1.0 / jnp.sqrt(jnp.sum(power * power) + NORM_EPS)), 1)
 
 
 def rows_for(hops, outer_ref, right_parts, out_ref, offset):
@@ -498,9 +492,9 @@
     basis, known, right, turned, other, left = call(
         prepare_kernel, [square, square, wide, tall, flat, flat], [(3, full, LANES)], 0.1, full, "prepare"
     )(l_stat, r_stat, l_basis, r_basis, got)
-    grad, new_stat, power = call(
-        functools.partial(products_kernel, hops), [square, square, square], [], 3, full, "products"
-    )(basis, known, got, *rows)
+    grad, new_stat, power, inner = call(
+        functools.partial(products_kernel, hops), [square, square, square, tall], [], 3, full, "products"
+    )(basis, known, turned, got, *rows)
     tensors = lax.axis_size("tensor")
     place = lambda t, i: i * tensors + t
     cycle = []
@@ -510,9 +504,7 @@
             cycle += [(place(t + 1, i + 1), place(t + 1, i)), (place(t + 1, i), place(t, i))]
     cycle += [(place(t, i), place(t, i ^ 1)) for t in range(tensors - tensors % 2, tensors) for i in range(size)]
     other_left = lax.ppermute(after(l_basis, basis, *(theirs[:2] if near else mine)), ("shard", "tensor"), cycle)
-    x, inner = call(begin_kernel, [square, tall], [(2, full // 2, LANES)], 7, full, "begin")(
-        got_corner, power, basis, grad, turned
-    )
+    (x,) = call(begin_kernel, [square], [(2, full // 2, LANES)], 7, full, "begin")(got_corner, power, basis)
     new_one, new_two, other_rows, outer, x = call(
         functools.partial(update_kernel, hops), [flat, flat, strips, wide, square], [(3, full, LANES)], 5, full, "update"
     )(inner, basis, left, right, other_left, one, two, x)

time: 47.3 us -> 47.1 us (level)
  transfers between devices with their start and end apart: 14 -> 14, of which waited for: 7 -> 7; matrix products, arithmetic and copies ran while one was open for 0% -> 0% of each run, Pallas kernels for 29% -> 30%
where the time goes in v19:
time: 47.1 us; the launch traced here: 47 us
  starting transfers between devices  19.2 us (41%)
  Pallas kernels  18.8 us (40%)
  waiting for transfers between devices  8.18 us (17%)
  between operations  0.77 us (2%)
    ppermute x6, starting transfers between devices, hop_by(): return lax.ppermute(x, 'shard', [(i, i ^ 2 * hop) for i in range(size)])  9.54 us
    ppermute x7, starting transfers between devices, partner(): return lax.ppermute(x, 'shard', pairs)  8.73 us
    ppermute x6, waiting for transfers between devices, hop_by(): return lax.ppermute(x, 'shard', [(i, i ^ 2 * hop) for i in range(size)])  6.02 us
    pallas_call x1, Pallas kernels, local(): call(functools.partial(end_kernel, hops, NS_ITERS - 2), [square, square,...  5.78 us
    pallas_call x1, Pallas kernels, local(): call(functools.partial(update_kernel, hops), [flat, flat, strips, wide, s...  2.84 us
    pallas_call x1, Pallas kernels, local(): call(begin_kernel, [square], [(2, full // 2, LANES)], 7, full, 'begin')  2.66 us
    ppermute x7, waiting for transfers between devices, partner(): return lax.ppermute(x, 'shard', pairs)  2.15 us
    pallas_call x1, Pallas kernels, local(): call(rest_kernel, [flat, flat, flat], [(3, full, LANES)], 1.5, full, 'rest')  2.06 us
  transfers between devices with their start and end apart: 14, of which 7 were waited for; matrix products, arithmetic and copies ran while one was open for 0% of the time, Pallas kernels for 30%

profile of v19, /device:TPU:0, one launch (start us, length us, event | category | flops | bytes accessed | tf_op | source)
XLA Modules:
  0.0 47.0 jit_solution(6127375741179939511)
XLA Ops:
  0.6 0.0 copy-start
  0.6 0.0 copy-start.1
  0.7 0.0 copy-start.2
  0.7 0.0 copy-start.3
  0.7 1.3 %pack.1 = (f32[720,128]{1,0:T(8,128)S(1)}, f32[192,128]{1,0:T(8,128)S(1)}, f32[48,384]{1,0:T(8,128)S(1)}, f32[48,384]{1,0:T(8,128)S(1)}, f32[48,384]{1,0:T(8,128)S(1)}) custom-call(f32[576,128]{1,0:T(8,128)} %bitcast.12, f32[576,128]{1,0:T(8,128)} %bitcast.14, f32[576,128]{1,0:T(8,128)} %bitcast.18, f32[576,128]{1,0:T(8,128)} %bitcast.16, f32[4,48,384]{2,1,0:T(8,128)} %refs_0_.1), custom_call_target="tpu_custom_call" | custom-call | flops 33973864 | bytes 2359296 | tf_op jit(solution)/shard_map/pack/pallas_call | solution.py:466
  2.0 3.0 %collective-permute-start = (f32[720,128]{1,0:T(8,128)S(1)}, f32[720,128]{1,0:T(8,128)S(1)}, u32[]{:S(2)}, u32[]{:S(2)}) collective-permute-start(f32[720,128]{1,0:T(8,128)S(1)} %get-tuple-element.45), channel_id=1, source_target_pairs={{0,4},{4,0},{8,12},{12,8},{16,20},{20,16},{24,28},{28,24},{1,5},{5... | collective-permute-start | bytes 1105928 | tf_op jit(solution)/shard_map/ppermute | solution.py:459
  5.0 2.6 %collective-permute-start.1 = (f32[48,384]{1,0:T(8,128)S(1)}, f32[48,384]{1,0:T(8,128)S(1)}, u32[]{:S(2)}, u32[]{:S(2)}) collective-permute-start(f32[48,384]{1,0:T(8,128)S(1)} %get-tuple-element.49), channel_id=1, source_target_pairs={{0,16},{4,20},{8,24},{12,28},{16,0},{20,4},{24,8},{28,12},{1,17},{... | collective-permute-start | bytes 221192 | tf_op jit(solution)/shard_map/ppermute | solution.py:456
  7.6 1.3 %collective-permute-start.2 = (f32[48,384]{1,0:T(8,128)S(1)}, f32[48,384]{1,0:T(8,128)S(1)}, u32[]{:S(2)}, u32[]{:S(2)}) collective-permute-start(f32[48,384]{1,0:T(8,128)S(1)} %get-tuple-element.50), channel_id=1, source_target_pairs={{0,24},{4,28},{8,16},{12,20},{16,8},{20,12},{24,0},{28,4},{1,25},{... | collective-permute-start | bytes 221192 | tf_op jit(solution)/shard_map/ppermute | solution.py:456
  8.9 0.2 collective-permute-start.3
  9.2 3.2 %collective-permute-done.1.refs_1_ = f32[48,384]{1,0:T(8,128)S(1)} collective-permute-done((f32[48,384]{1,0:T(8,128)S(1)}, f32[48,384]{1,0:T(8,128)S(1)}, u32[]{:S(2)}, u32[]{:S(2)}) %collective-permute-start.1) | collective-permute-done | bytes 73760 | tf_op jit(solution)/shard_map/ppermute | solution.py:456
  12.4 0.5 collective-permute-start.4
  12.9 1.1 %collective-permute-done.2.refs_2_ = f32[48,384]{1,0:T(8,128)S(1)} collective-permute-done((f32[48,384]{1,0:T(8,128)S(1)}, f32[48,384]{1,0:T(8,128)S(1)}, u32[]{:S(2)}, u32[]{:S(2)}) %collective-permute-start.2) | collective-permute-done | bytes 73760 | tf_op jit(solution)/shard_map/ppermute | solution.py:456
  13.9 0.5 %collective-permute-start.5 = (f32[48,384]{1,0:T(8,128)S(1)}, f32[48,384]{1,0:T(8,128)S(1)}, u32[]{:S(2)}, u32[]{:S(2)}) collective-permute-start(f32[48,384]{1,0:T(8,128)S(1)} %collective-permute-done.2.refs_2_), channel_id=1, source_target_pairs={{0,4},{4,0},{8,12},{12,8},{16,20},{20,16},{24,28},{28,24},{1,5},{5... | collective-permute-start | bytes 221192 | tf_op jit(solution)/shard_map/ppermute | solution.py:459
  14.4 0.0 collective-permute-done.3.refs_3_
  14.4 1.5 %collective-permute-start.6 = (f32[48,384]{1,0:T(8,128)S(1)}, f32[48,384]{1,0:T(8,128)S(1)}, u32[]{:S(2)}, u32[]{:S(2)}) collective-permute-start(f32[48,384]{1,0:T(8,128)S(1)} %collective-permute-done.3.refs_3_), channel_id=1, source_target_pairs={{0,4},{4,0},{8,12},{12,8},{16,20},{20,16},{24,28},{28,24},{1,5},{5... | collective-permute-start | bytes 221192 | tf_op jit(solution)/shard_map/ppermute | solution.py:459
  15.9 1.0 %collective-permute-done.4.refs_4_ = f32[48,384]{1,0:T(8,128)S(1)} collective-permute-done((f32[48,384]{1,0:T(8,128)S(1)}, f32[48,384]{1,0:T(8,128)S(1)}, u32[]{:S(2)}, u32[]{:S(2)}) %collective-permute-start.4) | collective-permute-done | bytes 73760 | tf_op jit(solution)/shard_map/ppermute | solution.py:459
  17.0 1.1 %collective-permute-start.8 = (f32[192,128]{1,0:T(8,128)S(1)}, f32[192,128]{1,0:T(8,128)S(1)}, u32[]{:S(2)}, u32[]{:S(2)}) collective-permute-start(f32[192,128]{1,0:T(8,128)S(1)} %get-tuple-element.57), channel_id=1, source_target_pairs={{0,4},{4,0},{8,12},{12,8},{16,20},{20,16},{24,28},{28,24},{1,5},{5... | collective-permute-start | bytes 294920 | tf_op jit(solution)/shard_map/ppermute | solution.py:459
  18.1 0.0 collective-permute-done.got_ref
  18.1 0.0 copy-done
  18.1 0.0 copy-done.1
  18.1 0.0 copy-done.2
  18.1 0.0 copy-done.3
  18.1 0.7 %prepare.1 = (f32[384,384]{1,0:T(8,128)S(1)}, f32[384,384]{1,0:T(8,128)S(1)}, f32[384,256]{1,0:T(8,128)S(1)}, f32[256,384]{1,0:T(8,128)S(1)}, f32[576,128]{1,0:T(8,128)S(1)}, /*index=5*/f32[576,128]{1,0:T(8,128)S(1)}) custom-call(f32[576,128]{1,0:T(8,128)S(1)} %bitcast.13, f32[576,128]{1,0:T(8,128)S(1)} %bitcast.15, f32[576,128]{1,0:T(8,128)S(1)} %bitcast.19, ...), custom_call_target="tpu_custom_call" | custom-call | flops 33973864 | bytes 2359296 | tf_op jit(solution)/shard_map/prepare/pallas_call | solution.py:492
  18.9 0.0 collective-permute-done.5.refs_5_
  18.9 0.9 %collective-permute-start.7 = (f32[576,128]{1,0:T(8,128)S(1)}, f32[576,128]{1,0:T(8,128)S(1)}, u32[]{:S(2)}, u32[]{:S(2)}) collective-permute-start(f32[576,128]{1,0:T(8,128)S(1)} %bitcast.20), channel_id=1, source_target_pairs={{0,4},{4,5},{5,1},{1,0},{8,12},{12,13},{13,9},{9,8},{16,20},{20,21... | collective-permute-start | bytes 884744 | tf_op jit(solution)/shard_map/ppermute | solution.py:506
  19.8 0.5 %collective-permute-done.6.refs_6_ = f32[48,384]{1,0:T(8,128)S(1)} collective-permute-done((f32[48,384]{1,0:T(8,128)S(1)}, f32[48,384]{1,0:T(8,128)S(1)}, u32[]{:S(2)}, u32[]{:S(2)}) %collective-permute-start.6) | collective-permute-done | bytes 73760 | tf_op jit(solution)/shard_map/ppermute | solution.py:459
  20.3 0.0 copy-done.4
  20.3 1.8 %products.1 = (f32[384,384]{1,0:T(8,128)S(1)}, f32[384,384]{1,0:T(8,128)S(1)}, f32[384,384]{1,0:T(8,128)S(1)}, f32[256,384]{1,0:T(8,128)S(1)}) custom-call(f32[384,384]{1,0:T(8,128)S(1)} %get-tuple-element.46.basis_ref, f32[384,384]{1,0:T(8,128)S(1)} %get-tuple-element.47.known_ref, f32[256,384]{1,0:T(8,128)S(1)} %get-tuple-element.48.turned_ref, ...), custom_call_target="tpu_custom_call" | custom-call | flops 1019215872 | bytes 2359296 | tf_op jit(solution)/shard_map/products/pallas_call | solution.py:495
  22.2 0.5 %collective-permute-done.8.corner_ref = f32[192,128]{1,0:T(8,128)S(1)} collective-permute-done((f32[192,128]{1,0:T(8,128)S(1)}, f32[192,128]{1,0:T(8,128)S(1)}, u32[]{:S(2)}, u32[]{:S(2)}) %collective-permute-start.8) | collective-permute-done | bytes 98336 | tf_op jit(solution)/shard_map/ppermute | solution.py:459
  22.7 2.7 %begin.1.start_ref = f32[384,384]{1,0:T(8,128)S(1)} custom-call(f32[192,128]{1,0:T(8,128)S(1)} %collective-permute-done.8.corner_ref, f32[384,384]{1,0:T(8,128)S(1)} %get-tuple-element.58.power_ref, f32[384,384]{1,0:T(8,128)S(1)} %get-tuple-element.46.basis_ref), custom_call_target="tpu_custom_call" | custom-call | flops 2378170368 | bytes 2359296 | tf_op jit(solution)/shard_map/begin/pallas_call | solution.py:507
  25.4 0.0 collective-permute-done.7.other_left_ref
  25.4 0.0 copy-done.5
  25.4 0.0 copy-done.6
  25.4 2.8 %update.1 = (f32[576,128]{1,0:T(8,128)}, f32[576,128]{1,0:T(8,128)}, f32[4,48,384]{2,1,0:T(8,128)S(1)}, f32[384,256]{1,0:T(8,128)S(1)}, f32[384,384]{1,0:T(8,128)S(1)}) custom-call(f32[256,384]{1,0:T(8,128)S(1)} %get-tuple-element.52.inner_ref, f32[384,384]{1,0:T(8,128)S(1)} %get-tuple-element.46.basis_ref, f32[576,128]{1,0:T(8,128)S(1)} %get-tuple-element.53.left_ref, ...), custom_call_target="tpu_custom_call" | custom-call | flops 1698693120 | bytes 2359296 | tf_op jit(solution)/shard_map/update/pallas_call | solution.py:508
  28.2 1.1 %collective-permute-start.9 = (f32[4,48,384]{2,1,0:T(8,128)S(1)}, f32[4,48,384]{2,1,0:T(8,128)S(1)}, u32[]{:S(2)}, u32[]{:S(2)}) collective-permute-start(f32[4,48,384]{2,1,0:T(8,128)S(1)} %get-tuple-element.60), channel_id=1, source_target_pairs={{0,4},{4,0},{8,12},{12,8},{16,20},{20,16},{24,28},{28,24},{1,5},{5... | collective-permute-start | bytes 884744 | tf_op jit(solution)/shard_map/ppermute | solution.py:459
  29.4 5.8 %end.1 = (f32[384,384]{1,0:T(8,128)S(1)}, f32[384,384]{1,0:T(8,128)S(1)}, f32[576,128]{1,0:T(8,128)S(1)}, f32[4,48,384]{2,1,0:T(8,128)S(1)}) custom-call(f32[384,384]{1,0:T(8,128)S(1)} %get-tuple-element.61.start_ref, f32[384,256]{1,0:T(8,128)S(1)} %get-tuple-element.62.outer_ref, f32[384,256]{1,0:T(8,128)S(1)} %get-tuple-element.54.right_ref), custom_call_target="tpu_custom_call" | custom-call | flops 3057647616 | bytes 2359296 | tf_op jit(solution)/shard_map/end/pallas_call | solution.py:515
  35.1 1.0 %collective-permute-start.13 = (f32[576,128]{1,0:T(8,128)S(1)}, f32[576,128]{1,0:T(8,128)S(1)}, u32[]{:S(2)}, u32[]{:S(2)}) collective-permute-start(f32[576,128]{1,0:T(8,128)S(1)} %get-tuple-element.64), channel_id=1, source_target_pairs={{0,4},{4,0},{8,12},{12,8},{16,20},{20,16},{24,28},{28,24},{1,5},{5... | collective-permute-start | bytes 884744 | tf_op jit(solution)/shard_map/ppermute | solution.py:459
  36.1 0.1 collective-permute-done.9.theirs_ref
  36.2 3.7 %collective-permute-start.10 = (f32[48,384]{1,0:T(8,128)S(1)}, f32[48,384]{1,0:T(8,128)S(1)}, u32[]{:S(2)}, u32[]{:S(2)}) collective-permute-start(f32[48,384]{1,0:T(8,128)S(1)} %get-tuple-element.68), channel_id=1, source_target_pairs={{0,16},{4,20},{8,24},{12,28},{16,0},{20,4},{24,8},{28,12},{1,17},{... | collective-permute-start | bytes 221192 | tf_op jit(solution)/shard_map/ppermute | solution.py:456
  39.9 1.2 %collective-permute-start.11 = (f32[48,384]{1,0:T(8,128)S(1)}, f32[48,384]{1,0:T(8,128)S(1)}, u32[]{:S(2)}, u32[]{:S(2)}) collective-permute-start(f32[48,384]{1,0:T(8,128)S(1)} %get-tuple-element.69), channel_id=1, source_target_pairs={{0,24},{4,28},{8,16},{12,20},{16,8},{20,12},{24,0},{28,4},{1,25},{... | collective-permute-start | bytes 221192 | tf_op jit(solution)/shard_map/ppermute | solution.py:456
  41.1 0.5 %collective-permute-start.12 = (f32[48,384]{1,0:T(8,128)S(1)}, f32[48,384]{1,0:T(8,128)S(1)}, u32[]{:S(2)}, u32[]{:S(2)}) collective-permute-start(f32[48,384]{1,0:T(8,128)S(1)} %get-tuple-element.70), channel_id=1, source_target_pairs={{0,8},{4,12},{8,0},{12,4},{16,24},{20,28},{24,16},{28,20},{1,9},{5... | collective-permute-start | bytes 221192 | tf_op jit(solution)/shard_map/ppermute | solution.py:456
  41.6 2.1 %rest.1 = (f32[576,128]{1,0:T(8,128)S(1)}, f32[576,128]{1,0:T(8,128)}, f32[576,128]{1,0:T(8,128)}) custom-call(f32[384,384]{1,0:T(8,128)S(1)} %get-tuple-element.73.x_ref, f32[384,384]{1,0:T(8,128)S(1)} %get-tuple-element.74.poly_ref, f32[384,384]{1,0:T(8,128)S(1)} %get-tuple-element.75.grad_ref, f32[384,384]{1,0:T(8,128)S(1)} %get-tuple-element.76.new_stat_ref, ...), custom_call_target="tpu_custom_call" | custom-call | flops 509607936 | bytes 2359296 | tf_op jit(solution)/shard_map/rest/pallas_call | solution.py:524
  43.6 0.0 collective-permute-done.13.back_ref
  43.6 0.8 %bases.1 = (f32[576,128]{1,0:T(8,128)}, f32[576,128]{1,0:T(8,128)}) custom-call(f32[576,128]{1,0:T(8,128)S(1)} %get-tuple-element.80.keep_ref, f32[576,128]{1,0:T(8,128)S(1)} %collective-permute-done.13.back_ref), custom_call_target="tpu_custom_call" | custom-call | flops 33973864 | bytes 2359296 | tf_op jit(solution)/shard_map/bases/pallas_call | solution.py:546
  44.5 0.0 collective-permute-done.10.refs_1_
  44.5 1.7 %collective-permute-done.11.refs_2_ = f32[48,384]{1,0:T(8,128)S(1)} collective-permute-done((f32[48,384]{1,0:T(8,128)S(1)}, f32[48,384]{1,0:T(8,128)S(1)}, u32[]{:S(2)}, u32[]{:S(2)}) %collective-permute-start.11) | collective-permute-done | bytes 73760 | tf_op jit(solution)/shard_map/ppermute | solution.py:456
  46.2 0.0 collective-permute-done.12.refs_3_
  46.2 0.7 %rows.1 = f32[4,48,384]{2,1,0:T(8,128)} custom-call(f32[48,384]{1,0:T(8,128)S(1)} %get-tuple-element.67.refs_0_, f32[48,384]{1,0:T(8,128)S(1)} %collective-permute-done.10.refs_1_, f32[48,384]{1,0:T(8,128)S(1)} %collective-permute-done.11.refs_2_, f32[48,384]{1,0:T(8,128)S(1)} %collective-permute-done.12.refs_3_), custom_call_target="tpu_custom_call" | custom-call | flops 33973864 | bytes 2359296 | tf_op jit(solution)/shard_map/rows/pallas_call | solution.py:532
  (4 shorter events, 0.0 us)
Async XLA Ops:
  0.6 17.4 %copy-start = (f32[1,73728]{1,0:T(1,128)S(1)}, f32[1,73728]{1,0:T(1,128)}, u32[]{:S(2)}) copy-start(f32[1,73728]{1,0:T(1,128)} %param.10) | copy-start | bytes 884740
  0.6 17.4 %copy-start.1 = (f32[1,73728]{1,0:T(1,128)S(1)}, f32[1,73728]{1,0:T(1,128)}, u32[]{:S(2)}) copy-start(f32[1,73728]{1,0:T(1,128)} %param.11) | copy-start | bytes 884740
  0.7 17.4 %copy-start.2 = (f32[1,73728]{1,0:T(1,128)S(1)}, f32[1,73728]{1,0:T(1,128)}, u32[]{:S(2)}) copy-start(f32[1,73728]{1,0:T(1,128)} %param.13) | copy-start | bytes 884740
  0.7 17.4 %copy-start.3 = (f32[1,73728]{1,0:T(1,128)S(1)}, f32[1,73728]{1,0:T(1,128)}, u32[]{:S(2)}) copy-start(f32[1,73728]{1,0:T(1,128)} %param.12) | copy-start | bytes 884740
  2.0 16.1 %collective-permute-start = (f32[720,128]{1,0:T(8,128)S(1)}, f32[720,128]{1,0:T(8,128)S(1)}, u32[]{:S(2)}, u32[]{:S(2)}) collective-permute-start(f32[720,128]{1,0:T(8,128)S(1)} %get-tuple-element.45), channel_id=1, source_target_pairs={{0,4},{4,0},{8,12},{12,8},{16,20},{20,16},{24,28},{28,24},{1,5},{5... | collective-permute-start | bytes 1105928 | tf_op jit(solution)/shard_map/ppermute | solution.py:459
  5.0 7.4 %collective-permute-start.1 = (f32[48,384]{1,0:T(8,128)S(1)}, f32[48,384]{1,0:T(8,128)S(1)}, u32[]{:S(2)}, u32[]{:S(2)}) collective-permute-start(f32[48,384]{1,0:T(8,128)S(1)} %get-tuple-element.49), channel_id=1, source_target_pairs={{0,16},{4,20},{8,24},{12,28},{16,0},{20,4},{24,8},{28,12},{1,17},{... | collective-permute-start | bytes 221192 | tf_op jit(solution)/shard_map/ppermute | solution.py:456
  7.6 6.3 %collective-permute-start.2 = (f32[48,384]{1,0:T(8,128)S(1)}, f32[48,384]{1,0:T(8,128)S(1)}, u32[]{:S(2)}, u32[]{:S(2)}) collective-permute-start(f32[48,384]{1,0:T(8,128)S(1)} %get-tuple-element.50), channel_id=1, source_target_pairs={{0,24},{4,28},{8,16},{12,20},{16,8},{20,12},{24,0},{28,4},{1,25},{... | collective-permute-start | bytes 221192 | tf_op jit(solution)/shard_map/ppermute | solution.py:456
  8.9 5.5 %collective-permute-start.3 = (f32[48,384]{1,0:T(8,128)S(1)}, f32[48,384]{1,0:T(8,128)S(1)}, u32[]{:S(2)}, u32[]{:S(2)}) collective-permute-start(f32[48,384]{1,0:T(8,128)S(1)} %get-tuple-element.51), channel_id=1, source_target_pairs={{0,8},{4,12},{8,0},{12,4},{16,24},{20,28},{24,16},{28,20},{1,9},{5... | collective-permute-start | bytes 221192 | tf_op jit(solution)/shard_map/ppermute | solution.py:456
  12.4 4.6 %collective-permute-start.4 = (f32[48,384]{1,0:T(8,128)S(1)}, f32[48,384]{1,0:T(8,128)S(1)}, u32[]{:S(2)}, u32[]{:S(2)}) collective-permute-start(f32[48,384]{1,0:T(8,128)S(1)} %collective-permute-done.1.refs_1_), channel_id=1, source_target_pairs={{0,4},{4,0},{8,12},{12,8},{16,20},{20,16},{24,28},{28,24},{1,5},{5... | collective-permute-start | bytes 221192 | tf_op jit(solution)/shard_map/ppermute | solution.py:459
  13.9 5.0 %collective-permute-start.5 = (f32[48,384]{1,0:T(8,128)S(1)}, f32[48,384]{1,0:T(8,128)S(1)}, u32[]{:S(2)}, u32[]{:S(2)}) collective-permute-start(f32[48,384]{1,0:T(8,128)S(1)} %collective-permute-done.2.refs_2_), channel_id=1, source_target_pairs={{0,4},{4,0},{8,12},{12,8},{16,20},{20,16},{24,28},{28,24},{1,5},{5... | collective-permute-start | bytes 221192 | tf_op jit(solution)/shard_map/ppermute | solution.py:459
  14.4 5.9 %collective-permute-start.6 = (f32[48,384]{1,0:T(8,128)S(1)}, f32[48,384]{1,0:T(8,128)S(1)}, u32[]{:S(2)}, u32[]{:S(2)}) collective-permute-start(f32[48,384]{1,0:T(8,128)S(1)} %collective-permute-done.3.refs_3_), channel_id=1, source_target_pairs={{0,4},{4,0},{8,12},{12,8},{16,20},{20,16},{24,28},{28,24},{1,5},{5... | collective-permute-start | bytes 221192 | tf_op jit(solution)/shard_map/ppermute | solution.py:459
  17.0 3.3 %copy-start.4 = (f32[4,48,384]{2,1,0:T(8,128)S(1)}, f32[4,48,384]{2,1,0:T(8,128)}, u32[]{:S(2)}) copy-start(f32[4,48,384]{2,1,0:T(8,128)} %refs_0_.1) | copy-start | bytes 884740
  17.0 5.7 %collective-permute-start.8 = (f32[192,128]{1,0:T(8,128)S(1)}, f32[192,128]{1,0:T(8,128)S(1)}, u32[]{:S(2)}, u32[]{:S(2)}) collective-permute-start(f32[192,128]{1,0:T(8,128)S(1)} %get-tuple-element.57), channel_id=1, source_target_pairs={{0,4},{4,0},{8,12},{12,8},{16,20},{20,16},{24,28},{28,24},{1,5},{5... | collective-permute-start | bytes 294920 | tf_op jit(solution)/shard_map/ppermute | solution.py:459
  18.9 6.5 %collective-permute-start.7 = (f32[576,128]{1,0:T(8,128)S(1)}, f32[576,128]{1,0:T(8,128)S(1)}, u32[]{:S(2)}, u32[]{:S(2)}) collective-permute-start(f32[576,128]{1,0:T(8,128)S(1)} %bitcast.20), channel_id=1, source_target_pairs={{0,4},{4,5},{5,1},{1,0},{8,12},{12,13},{13,9},{9,8},{16,20},{20,21... | collective-permute-start | bytes 884744 | tf_op jit(solution)/shard_map/ppermute | solution.py:506
  22.7 2.7 %copy-start.5 = (f32[1,73728]{1,0:T(1,128)S(1)}, f32[1,73728]{1,0:T(1,128)}, u32[]{:S(2)}) copy-start(f32[1,73728]{1,0:T(1,128)} %param.8) | copy-start | bytes 884740
  22.7 2.7 %copy-start.6 = (f32[1,73728]{1,0:T(1,128)S(1)}, f32[1,73728]{1,0:T(1,128)}, u32[]{:S(2)}) copy-start(f32[1,73728]{1,0:T(1,128)} %param.9) | copy-start | bytes 884740
  28.2 7.9 %collective-permute-start.9 = (f32[4,48,384]{2,1,0:T(8,128)S(1)}, f32[4,48,384]{2,1,0:T(8,128)S(1)}, u32[]{:S(2)}, u32[]{:S(2)}) collective-permute-start(f32[4,48,384]{2,1,0:T(8,128)S(1)} %get-tuple-element.60), channel_id=1, source_target_pairs={{0,4},{4,0},{8,12},{12,8},{16,20},{20,16},{24,28},{28,24},{1,5},{5... | collective-permute-start | bytes 884744 | tf_op jit(solution)/shard_map/ppermute | solution.py:459
  35.1 8.5 %collective-permute-start.13 = (f32[576,128]{1,0:T(8,128)S(1)}, f32[576,128]{1,0:T(8,128)S(1)}, u32[]{:S(2)}, u32[]{:S(2)}) collective-permute-start(f32[576,128]{1,0:T(8,128)S(1)} %get-tuple-element.64), channel_id=1, source_target_pairs={{0,4},{4,0},{8,12},{12,8},{16,20},{20,16},{24,28},{28,24},{1,5},{5... | collective-permute-start | bytes 884744 | tf_op jit(solution)/shard_map/ppermute | solution.py:459
  36.2 8.3 %collective-permute-start.10 = (f32[48,384]{1,0:T(8,128)S(1)}, f32[48,384]{1,0:T(8,128)S(1)}, u32[]{:S(2)}, u32[]{:S(2)}) collective-permute-start(f32[48,384]{1,0:T(8,128)S(1)} %get-tuple-element.68), channel_id=1, source_target_pairs={{0,16},{4,20},{8,24},{12,28},{16,0},{20,4},{24,8},{28,12},{1,17},{... | collective-permute-start | bytes 221192 | tf_op jit(solution)/shard_map/ppermute | solution.py:456
  39.9 6.3 %collective-permute-start.11 = (f32[48,384]{1,0:T(8,128)S(1)}, f32[48,384]{1,0:T(8,128)S(1)}, u32[]{:S(2)}, u32[]{:S(2)}) collective-permute-start(f32[48,384]{1,0:T(8,128)S(1)} %get-tuple-element.69), channel_id=1, source_target_pairs={{0,24},{4,28},{8,16},{12,20},{16,8},{20,12},{24,0},{28,4},{1,25},{... | collective-permute-start | bytes 221192 | tf_op jit(solution)/shard_map/ppermute | solution.py:456
  41.1 5.1 %collective-permute-start.12 = (f32[48,384]{1,0:T(8,128)S(1)}, f32[48,384]{1,0:T(8,128)S(1)}, u32[]{:S(2)}, u32[]{:S(2)}) collective-permute-start(f32[48,384]{1,0:T(8,128)S(1)} %get-tuple-element.70), channel_id=1, source_target_pairs={{0,8},{4,12},{8,0},{12,4},{16,24},{20,28},{24,16},{28,20},{1,9},{5... | collective-permute-start | bytes 221192 | tf_op jit(solution)/shard_map/ppermute | solution.py:456

commit v20 on v19

--- a/solution.py
+++ b/solution.py
@@ -503,7 +503,7 @@
             cycle += [(place(t, i), place(t, i + 1)), (place(t, i + 1), place(t + 1, i + 1))]
             cycle += [(place(t + 1, i + 1), place(t + 1, i)), (place(t + 1, i), place(t, i))]
     cycle += [(place(t, i), place(t, i ^ 1)) for t in range(tensors - tensors % 2, tensors) for i in range(size)]
-    other_left = lax.ppermute(after(l_basis, basis, *(theirs[:2] if near else mine)), ("shard", "tensor"), cycle)
+    other_left = lax.ppermute(after(l_basis, *(theirs[:2] if near else mine)), ("shard", "tensor"), cycle)
     (x,) = call(begin_kernel, [square], [(2, full // 2, LANES)], 7, full, "begin")(got_corner, power, basis)
     new_one, new_two, other_rows, outer, x = call(
         functools.partial(update_kernel, hops), [flat, flat, strips, wide, square], [(3, full, LANES)], 5, full, "update"

time: 47.1 us -> 47.6 us (1.011)
  waiting for transfers between devices: 8.18 us -> 9.28 us
  starting transfers between devices: 19.2 us -> 18.6 us
    ppermute x7, waiting for transfers between devices: 2.15 us -> 3.26 us  [partner(): return lax.ppermute(x, 'shard', pairs)]
  transfers between devices with their start and end apart: 14 -> 14, of which waited for: 7 -> 9; matrix products, arithmetic and copies ran while one was open for 0% -> 0% of each run, Pallas kernels for 30% -> 29%
where the time goes in v20:
time: 47.6 us; the launch traced here: 47.5 us
  Pallas kernels  18.8 us (39%)
  starting transfers between devices  18.6 us (39%)
  waiting for transfers between devices  9.28 us (19%)
  between operations  0.77 us (2%)
    ppermute x6, starting transfers between devices, hop_by(): return lax.ppermute(x, 'shard', [(i, i ^ 2 * hop) for i in range(size)])  9.16 us
    ppermute x7, starting transfers between devices, partner(): return lax.ppermute(x, 'shard', pairs)  8.73 us
    ppermute x6, waiting for transfers between devices, hop_by(): return lax.ppermute(x, 'shard', [(i, i ^ 2 * hop) for i in range(size)])  6.02 us
    pallas_call x1, Pallas kernels, local(): call(functools.partial(end_kernel, hops, NS_ITERS - 2), [square, square,...  5.78 us
    ppermute x7, waiting for transfers between devices, partner(): return lax.ppermute(x, 'shard', pairs)  3.26 us
    pallas_call x1, Pallas kernels, local(): call(functools.partial(update_kernel, hops), [flat, flat, strips, wide, s...  2.84 us
    pallas_call x1, Pallas kernels, local(): call(begin_kernel, [square], [(2, full // 2, LANES)], 7, full, 'begin')  2.65 us
    pallas_call x1, Pallas kernels, local(): call(rest_kernel, [flat, flat, flat], [(3, full, LANES)], 1.5, full, 'rest')  2.06 us
  transfers between devices with their start and end apart: 14, of which 9 were waited for; matrix products, arithmetic and copies ran while one was open for 0% of the time, Pallas kernels for 29%

profile of v20, /device:TPU:0, one launch (start us, length us, event | category | flops | bytes accessed | tf_op | source)
XLA Modules:
  0.0 47.5 jit_solution(16723447693418386745)
XLA Ops:
  0.6 0.0 copy-start.3
  0.6 0.0 copy-start
  0.7 0.0 copy-start.1
  0.7 0.0 copy-start.2
  0.7 1.3 %pack.1 = (f32[720,128]{1,0:T(8,128)S(1)}, f32[192,128]{1,0:T(8,128)S(1)}, f32[48,384]{1,0:T(8,128)S(1)}, f32[48,384]{1,0:T(8,128)S(1)}, f32[48,384]{1,0:T(8,128)S(1)}) custom-call(f32[576,128]{1,0:T(8,128)} %bitcast.12, f32[576,128]{1,0:T(8,128)} %bitcast.14, f32[576,128]{1,0:T(8,128)} %bitcast.18, f32[576,128]{1,0:T(8,128)} %bitcast.16, f32[4,48,384]{2,1,0:T(8,128)} %refs_0_.1), custom_call_target="tpu_custom_call" | custom-call | flops 33973864 | bytes 2359296 | tf_op jit(solution)/shard_map/pack/pallas_call | solution.py:466
  2.0 3.0 %collective-permute-start = (f32[720,128]{1,0:T(8,128)S(1)}, f32[720,128]{1,0:T(8,128)S(1)}, u32[]{:S(2)}, u32[]{:S(2)}) collective-permute-start(f32[720,128]{1,0:T(8,128)S(1)} %get-tuple-element.45), channel_id=1, source_target_pairs={{0,4},{4,0},{8,12},{12,8},{16,20},{20,16},{24,28},{28,24},{1,5},{5... | collective-permute-start | bytes 1105928 | tf_op jit(solution)/shard_map/ppermute | solution.py:459
  5.0 2.6 %collective-permute-start.1 = (f32[48,384]{1,0:T(8,128)S(1)}, f32[48,384]{1,0:T(8,128)S(1)}, u32[]{:S(2)}, u32[]{:S(2)}) collective-permute-start(f32[48,384]{1,0:T(8,128)S(1)} %get-tuple-element.49), channel_id=1, source_target_pairs={{0,16},{4,20},{8,24},{12,28},{16,0},{20,4},{24,8},{28,12},{1,17},{... | collective-permute-start | bytes 221192 | tf_op jit(solution)/shard_map/ppermute | solution.py:456
  7.6 1.3 %collective-permute-start.2 = (f32[48,384]{1,0:T(8,128)S(1)}, f32[48,384]{1,0:T(8,128)S(1)}, u32[]{:S(2)}, u32[]{:S(2)}) collective-permute-start(f32[48,384]{1,0:T(8,128)S(1)} %get-tuple-element.50), channel_id=1, source_target_pairs={{0,24},{4,28},{8,16},{12,20},{16,8},{20,12},{24,0},{28,4},{1,25},{... | collective-permute-start | bytes 221192 | tf_op jit(solution)/shard_map/ppermute | solution.py:456
  8.9 0.2 collective-permute-start.3
  9.2 3.2 %collective-permute-done.1.refs_1_ = f32[48,384]{1,0:T(8,128)S(1)} collective-permute-done((f32[48,384]{1,0:T(8,128)S(1)}, f32[48,384]{1,0:T(8,128)S(1)}, u32[]{:S(2)}, u32[]{:S(2)}) %collective-permute-start.1) | collective-permute-done | bytes 73760 | tf_op jit(solution)/shard_map/ppermute | solution.py:456
  12.4 0.5 collective-permute-start.4
  12.9 1.1 %collective-permute-done.2.refs_2_ = f32[48,384]{1,0:T(8,128)S(1)} collective-permute-done((f32[48,384]{1,0:T(8,128)S(1)}, f32[48,384]{1,0:T(8,128)S(1)}, u32[]{:S(2)}, u32[]{:S(2)}) %collective-permute-start.2) | collective-permute-done | bytes 73760 | tf_op jit(solution)/shard_map/ppermute | solution.py:456
  13.9 0.5 %collective-permute-start.5 = (f32[48,384]{1,0:T(8,128)S(1)}, f32[48,384]{1,0:T(8,128)S(1)}, u32[]{:S(2)}, u32[]{:S(2)}) collective-permute-start(f32[48,384]{1,0:T(8,128)S(1)} %collective-permute-done.2.refs_2_), channel_id=1, source_target_pairs={{0,4},{4,0},{8,12},{12,8},{16,20},{20,16},{24,28},{28,24},{1,5},{5... | collective-permute-start | bytes 221192 | tf_op jit(solution)/shard_map/ppermute | solution.py:459
  14.4 0.0 collective-permute-done.3.refs_3_
  14.4 1.5 %collective-permute-start.6 = (f32[48,384]{1,0:T(8,128)S(1)}, f32[48,384]{1,0:T(8,128)S(1)}, u32[]{:S(2)}, u32[]{:S(2)}) collective-permute-start(f32[48,384]{1,0:T(8,128)S(1)} %collective-permute-done.3.refs_3_), channel_id=1, source_target_pairs={{0,4},{4,0},{8,12},{12,8},{16,20},{20,16},{24,28},{28,24},{1,5},{5... | collective-permute-start | bytes 221192 | tf_op jit(solution)/shard_map/ppermute | solution.py:459
  15.9 1.0 %collective-permute-done.4.refs_4_ = f32[48,384]{1,0:T(8,128)S(1)} collective-permute-done((f32[48,384]{1,0:T(8,128)S(1)}, f32[48,384]{1,0:T(8,128)S(1)}, u32[]{:S(2)}, u32[]{:S(2)}) %collective-permute-start.4) | collective-permute-done | bytes 73760 | tf_op jit(solution)/shard_map/ppermute | solution.py:459
  17.0 1.1 %collective-permute-start.8 = (f32[192,128]{1,0:T(8,128)S(1)}, f32[192,128]{1,0:T(8,128)S(1)}, u32[]{:S(2)}, u32[]{:S(2)}) collective-permute-start(f32[192,128]{1,0:T(8,128)S(1)} %get-tuple-element.57), channel_id=1, source_target_pairs={{0,4},{4,0},{8,12},{12,8},{16,20},{20,16},{24,28},{28,24},{1,5},{5... | collective-permute-start | bytes 294920 | tf_op jit(solution)/shard_map/ppermute | solution.py:459
  18.1 0.9 %collective-permute-done.5.refs_5_ = f32[48,384]{1,0:T(8,128)S(1)} collective-permute-done((f32[48,384]{1,0:T(8,128)S(1)}, f32[48,384]{1,0:T(8,128)S(1)}, u32[]{:S(2)}, u32[]{:S(2)}) %collective-permute-start.5) | collective-permute-done | bytes 73760 | tf_op jit(solution)/shard_map/ppermute | solution.py:459
  19.0 0.0 copy-done.3
  19.0 0.7 %collective-permute-start.7 = (f32[576,128]{1,0:T(8,128)S(1)}, f32[576,128]{1,0:T(8,128)S(1)}, u32[]{:S(2)}, u32[]{:S(2)}) collective-permute-start(f32[576,128]{1,0:T(8,128)S(1)} %bitcast.19), channel_id=1, source_target_pairs={{0,4},{4,5},{5,1},{1,0},{8,12},{12,13},{13,9},{9,8},{16,20},{20,21... | collective-permute-start | bytes 884744 | tf_op jit(solution)/shard_map/ppermute | solution.py:506
  19.7 0.0 collective-permute-done.got_ref
  19.7 0.0 copy-done
  19.7 0.0 copy-done.1
  19.7 0.0 copy-done.2
  19.7 0.7 %prepare.1 = (f32[384,384]{1,0:T(8,128)S(1)}, f32[384,384]{1,0:T(8,128)S(1)}, f32[384,256]{1,0:T(8,128)S(1)}, f32[256,384]{1,0:T(8,128)S(1)}, f32[576,128]{1,0:T(8,128)S(1)}, /*index=5*/f32[576,128]{1,0:T(8,128)S(1)}) custom-call(f32[576,128]{1,0:T(8,128)S(1)} %bitcast.13, f32[576,128]{1,0:T(8,128)S(1)} %bitcast.15, f32[576,128]{1,0:T(8,128)S(1)} %bitcast.20, ...), custom_call_target="tpu_custom_call" | custom-call | flops 33973864 | bytes 2359296 | tf_op jit(solution)/shard_map/prepare/pallas_call | solution.py:492
  20.4 0.1 collective-permute-done.6.refs_6_
  20.5 0.0 copy-done.4
  20.6 1.8 %products.1 = (f32[384,384]{1,0:T(8,128)S(1)}, f32[384,384]{1,0:T(8,128)S(1)}, f32[384,384]{1,0:T(8,128)S(1)}, f32[256,384]{1,0:T(8,128)S(1)}) custom-call(f32[384,384]{1,0:T(8,128)S(1)} %get-tuple-element.46.basis_ref, f32[384,384]{1,0:T(8,128)S(1)} %get-tuple-element.47.known_ref, f32[256,384]{1,0:T(8,128)S(1)} %get-tuple-element.48.turned_ref, ...), custom_call_target="tpu_custom_call" | custom-call | flops 1019215872 | bytes 2359296 | tf_op jit(solution)/shard_map/products/pallas_call | solution.py:495
  22.4 0.2 collective-permute-done.8.corner_ref
  22.7 2.7 %begin.1.start_ref = f32[384,384]{1,0:T(8,128)S(1)} custom-call(f32[192,128]{1,0:T(8,128)S(1)} %collective-permute-done.8.corner_ref, f32[384,384]{1,0:T(8,128)S(1)} %get-tuple-element.58.power_ref, f32[384,384]{1,0:T(8,128)S(1)} %get-tuple-element.46.basis_ref), custom_call_target="tpu_custom_call" | custom-call | flops 2378170368 | bytes 2359296 | tf_op jit(solution)/shard_map/begin/pallas_call | solution.py:507
  25.3 0.0 collective-permute-done.7.other_left_ref
  25.3 0.0 copy-done.5
  25.3 0.0 copy-done.6
  25.4 2.8 %update.1 = (f32[576,128]{1,0:T(8,128)}, f32[576,128]{1,0:T(8,128)}, f32[4,48,384]{2,1,0:T(8,128)S(1)}, f32[384,256]{1,0:T(8,128)S(1)}, f32[384,384]{1,0:T(8,128)S(1)}) custom-call(f32[256,384]{1,0:T(8,128)S(1)} %get-tuple-element.52.inner_ref, f32[384,384]{1,0:T(8,128)S(1)} %get-tuple-element.46.basis_ref, f32[576,128]{1,0:T(8,128)S(1)} %get-tuple-element.53.left_ref, ...), custom_call_target="tpu_custom_call" | custom-call | flops 1698693120 | bytes 2359296 | tf_op jit(solution)/shard_map/update/pallas_call | solution.py:508
  28.2 1.0 %collective-permute-start.9 = (f32[4,48,384]{2,1,0:T(8,128)S(1)}, f32[4,48,384]{2,1,0:T(8,128)S(1)}, u32[]{:S(2)}, u32[]{:S(2)}) collective-permute-start(f32[4,48,384]{2,1,0:T(8,128)S(1)} %get-tuple-element.60), channel_id=1, source_target_pairs={{0,4},{4,0},{8,12},{12,8},{16,20},{20,16},{24,28},{28,24},{1,5},{5... | collective-permute-start | bytes 884744 | tf_op jit(solution)/shard_map/ppermute | solution.py:459
  29.2 5.8 %end.1 = (f32[384,384]{1,0:T(8,128)S(1)}, f32[384,384]{1,0:T(8,128)S(1)}, f32[576,128]{1,0:T(8,128)S(1)}, f32[4,48,384]{2,1,0:T(8,128)S(1)}) custom-call(f32[384,384]{1,0:T(8,128)S(1)} %get-tuple-element.61.start_ref, f32[384,256]{1,0:T(8,128)S(1)} %get-tuple-element.62.outer_ref, f32[384,256]{1,0:T(8,128)S(1)} %get-tuple-element.54.right_ref), custom_call_target="tpu_custom_call" | custom-call | flops 3057647616 | bytes 2359296 | tf_op jit(solution)/shard_map/end/pallas_call | solution.py:515
  35.0 1.1 %collective-permute-start.13 = (f32[576,128]{1,0:T(8,128)S(1)}, f32[576,128]{1,0:T(8,128)S(1)}, u32[]{:S(2)}, u32[]{:S(2)}) collective-permute-start(f32[576,128]{1,0:T(8,128)S(1)} %get-tuple-element.64), channel_id=1, source_target_pairs={{0,4},{4,0},{8,12},{12,8},{16,20},{20,16},{24,28},{28,24},{1,5},{5... | collective-permute-start | bytes 884744 | tf_op jit(solution)/shard_map/ppermute | solution.py:459
  36.1 1.0 %collective-permute-done.9.theirs_ref = f32[4,48,384]{2,1,0:T(8,128)S(1)} collective-permute-done((f32[4,48,384]{2,1,0:T(8,128)S(1)}, f32[4,48,384]{2,1,0:T(8,128)S(1)}, u32[]{:S(2)}, u32[]{:S(2)}) %collective-permute-start.9) | collective-permute-done | bytes 294944 | tf_op jit(solution)/shard_map/ppermute | solution.py:459
  37.1 3.2 %collective-permute-start.10 = (f32[48,384]{1,0:T(8,128)S(1)}, f32[48,384]{1,0:T(8,128)S(1)}, u32[]{:S(2)}, u32[]{:S(2)}) collective-permute-start(f32[48,384]{1,0:T(8,128)S(1)} %get-tuple-element.68), channel_id=1, source_target_pairs={{0,16},{4,20},{8,24},{12,28},{16,0},{20,4},{24,8},{28,12},{1,17},{... | collective-permute-start | bytes 221192 | tf_op jit(solution)/shard_map/ppermute | solution.py:456
  40.3 1.3 %collective-permute-start.11 = (f32[48,384]{1,0:T(8,128)S(1)}, f32[48,384]{1,0:T(8,128)S(1)}, u32[]{:S(2)}, u32[]{:S(2)}) collective-permute-start(f32[48,384]{1,0:T(8,128)S(1)} %get-tuple-element.69), channel_id=1, source_target_pairs={{0,24},{4,28},{8,16},{12,20},{16,8},{20,12},{24,0},{28,4},{1,25},{... | collective-permute-start | bytes 221192 | tf_op jit(solution)/shard_map/ppermute | solution.py:456
  41.6 0.5 %collective-permute-start.12 = (f32[48,384]{1,0:T(8,128)S(1)}, f32[48,384]{1,0:T(8,128)S(1)}, u32[]{:S(2)}, u32[]{:S(2)}) collective-permute-start(f32[48,384]{1,0:T(8,128)S(1)} %get-tuple-element.70), channel_id=1, source_target_pairs={{0,8},{4,12},{8,0},{12,4},{16,24},{20,28},{24,16},{28,20},{1,9},{5... | collective-permute-start | bytes 221192 | tf_op jit(solution)/shard_map/ppermute | solution.py:456
  42.1 2.1 %rest.1 = (f32[576,128]{1,0:T(8,128)S(1)}, f32[576,128]{1,0:T(8,128)}, f32[576,128]{1,0:T(8,128)}) custom-call(f32[384,384]{1,0:T(8,128)S(1)} %get-tuple-element.73.x_ref, f32[384,384]{1,0:T(8,128)S(1)} %get-tuple-element.74.poly_ref, f32[384,384]{1,0:T(8,128)S(1)} %get-tuple-element.75.grad_ref, f32[384,384]{1,0:T(8,128)S(1)} %get-tuple-element.76.new_stat_ref, ...), custom_call_target="tpu_custom_call" | custom-call | flops 509607936 | bytes 2359296 | tf_op jit(solution)/shard_map/rest/pallas_call | solution.py:524
  44.1 0.0 collective-permute-done.13.back_ref
  44.1 0.8 %bases.1 = (f32[576,128]{1,0:T(8,128)}, f32[576,128]{1,0:T(8,128)}) custom-call(f32[576,128]{1,0:T(8,128)S(1)} %get-tuple-element.80.keep_ref, f32[576,128]{1,0:T(8,128)S(1)} %collective-permute-done.13.back_ref), custom_call_target="tpu_custom_call" | custom-call | flops 33973864 | bytes 2359296 | tf_op jit(solution)/shard_map/bases/pallas_call | solution.py:546
  44.9 0.0 collective-permute-done.10.refs_1_
  45.0 1.6 %collective-permute-done.11.refs_2_ = f32[48,384]{1,0:T(8,128)S(1)} collective-permute-done((f32[48,384]{1,0:T(8,128)S(1)}, f32[48,384]{1,0:T(8,128)S(1)}, u32[]{:S(2)}, u32[]{:S(2)}) %collective-permute-start.11) | collective-permute-done | bytes 73760 | tf_op jit(solution)/shard_map/ppermute | solution.py:456
  46.6 0.1 collective-permute-done.12.refs_3_
  46.7 0.7 %rows.1 = f32[4,48,384]{2,1,0:T(8,128)} custom-call(f32[48,384]{1,0:T(8,128)S(1)} %get-tuple-element.67.refs_0_, f32[48,384]{1,0:T(8,128)S(1)} %collective-permute-done.10.refs_1_, f32[48,384]{1,0:T(8,128)S(1)} %collective-permute-done.11.refs_2_, f32[48,384]{1,0:T(8,128)S(1)} %collective-permute-done.12.refs_3_), custom_call_target="tpu_custom_call" | custom-call | flops 33973864 | bytes 2359296 | tf_op jit(solution)/shard_map/rows/pallas_call | solution.py:532
  (4 shorter events, 0.0 us)
Async XLA Ops:
  0.6 18.3 %copy-start.3 = (f32[1,73728]{1,0:T(1,128)S(1)}, f32[1,73728]{1,0:T(1,128)}, u32[]{:S(2)}) copy-start(f32[1,73728]{1,0:T(1,128)} %param.12) | copy-start | bytes 884740
  0.6 19.0 %copy-start = (f32[1,73728]{1,0:T(1,128)S(1)}, f32[1,73728]{1,0:T(1,128)}, u32[]{:S(2)}) copy-start(f32[1,73728]{1,0:T(1,128)} %param.10) | copy-start | bytes 884740
  0.7 19.0 %copy-start.1 = (f32[1,73728]{1,0:T(1,128)S(1)}, f32[1,73728]{1,0:T(1,128)}, u32[]{:S(2)}) copy-start(f32[1,73728]{1,0:T(1,128)} %param.11) | copy-start | bytes 884740
  0.7 19.0 %copy-start.2 = (f32[1,73728]{1,0:T(1,128)S(1)}, f32[1,73728]{1,0:T(1,128)}, u32[]{:S(2)}) copy-start(f32[1,73728]{1,0:T(1,128)} %param.13) | copy-start | bytes 884740
  2.0 17.7 %collective-permute-start = (f32[720,128]{1,0:T(8,128)S(1)}, f32[720,128]{1,0:T(8,128)S(1)}, u32[]{:S(2)}, u32[]{:S(2)}) collective-permute-start(f32[720,128]{1,0:T(8,128)S(1)} %get-tuple-element.45), channel_id=1, source_target_pairs={{0,4},{4,0},{8,12},{12,8},{16,20},{20,16},{24,28},{28,24},{1,5},{5... | collective-permute-start | bytes 1105928 | tf_op jit(solution)/shard_map/ppermute | solution.py:459
  5.0 7.4 %collective-permute-start.1 = (f32[48,384]{1,0:T(8,128)S(1)}, f32[48,384]{1,0:T(8,128)S(1)}, u32[]{:S(2)}, u32[]{:S(2)}) collective-permute-start(f32[48,384]{1,0:T(8,128)S(1)} %get-tuple-element.49), channel_id=1, source_target_pairs={{0,16},{4,20},{8,24},{12,28},{16,0},{20,4},{24,8},{28,12},{1,17},{... | collective-permute-start | bytes 221192 | tf_op jit(solution)/shard_map/ppermute | solution.py:456
  7.6 6.3 %collective-permute-start.2 = (f32[48,384]{1,0:T(8,128)S(1)}, f32[48,384]{1,0:T(8,128)S(1)}, u32[]{:S(2)}, u32[]{:S(2)}) collective-permute-start(f32[48,384]{1,0:T(8,128)S(1)} %get-tuple-element.50), channel_id=1, source_target_pairs={{0,24},{4,28},{8,16},{12,20},{16,8},{20,12},{24,0},{28,4},{1,25},{... | collective-permute-start | bytes 221192 | tf_op jit(solution)/shard_map/ppermute | solution.py:456
  8.9 5.5 %collective-permute-start.3 = (f32[48,384]{1,0:T(8,128)S(1)}, f32[48,384]{1,0:T(8,128)S(1)}, u32[]{:S(2)}, u32[]{:S(2)}) collective-permute-start(f32[48,384]{1,0:T(8,128)S(1)} %get-tuple-element.51), channel_id=1, source_target_pairs={{0,8},{4,12},{8,0},{12,4},{16,24},{20,28},{24,16},{28,20},{1,9},{5... | collective-permute-start | bytes 221192 | tf_op jit(solution)/shard_map/ppermute | solution.py:456
  12.4 4.6 %collective-permute-start.4 = (f32[48,384]{1,0:T(8,128)S(1)}, f32[48,384]{1,0:T(8,128)S(1)}, u32[]{:S(2)}, u32[]{:S(2)}) collective-permute-start(f32[48,384]{1,0:T(8,128)S(1)} %collective-permute-done.1.refs_1_), channel_id=1, source_target_pairs={{0,4},{4,0},{8,12},{12,8},{16,20},{20,16},{24,28},{28,24},{1,5},{5... | collective-permute-start | bytes 221192 | tf_op jit(solution)/shard_map/ppermute | solution.py:459
  13.9 5.1 %collective-permute-start.5 = (f32[48,384]{1,0:T(8,128)S(1)}, f32[48,384]{1,0:T(8,128)S(1)}, u32[]{:S(2)}, u32[]{:S(2)}) collective-permute-start(f32[48,384]{1,0:T(8,128)S(1)} %collective-permute-done.2.refs_2_), channel_id=1, source_target_pairs={{0,4},{4,0},{8,12},{12,8},{16,20},{20,16},{24,28},{28,24},{1,5},{5... | collective-permute-start | bytes 221192 | tf_op jit(solution)/shard_map/ppermute | solution.py:459
  14.4 6.1 %collective-permute-start.6 = (f32[48,384]{1,0:T(8,128)S(1)}, f32[48,384]{1,0:T(8,128)S(1)}, u32[]{:S(2)}, u32[]{:S(2)}) collective-permute-start(f32[48,384]{1,0:T(8,128)S(1)} %collective-permute-done.3.refs_3_), channel_id=1, source_target_pairs={{0,4},{4,0},{8,12},{12,8},{16,20},{20,16},{24,28},{28,24},{1,5},{5... | collective-permute-start | bytes 221192 | tf_op jit(solution)/shard_map/ppermute | solution.py:459
  17.0 3.6 %copy-start.4 = (f32[4,48,384]{2,1,0:T(8,128)S(1)}, f32[4,48,384]{2,1,0:T(8,128)}, u32[]{:S(2)}) copy-start(f32[4,48,384]{2,1,0:T(8,128)} %refs_0_.1) | copy-start | bytes 884740
  17.0 5.7 %collective-permute-start.8 = (f32[192,128]{1,0:T(8,128)S(1)}, f32[192,128]{1,0:T(8,128)S(1)}, u32[]{:S(2)}, u32[]{:S(2)}) collective-permute-start(f32[192,128]{1,0:T(8,128)S(1)} %get-tuple-element.57), channel_id=1, source_target_pairs={{0,4},{4,0},{8,12},{12,8},{16,20},{20,16},{24,28},{28,24},{1,5},{5... | collective-permute-start | bytes 294920 | tf_op jit(solution)/shard_map/ppermute | solution.py:459
  19.0 6.4 %collective-permute-start.7 = (f32[576,128]{1,0:T(8,128)S(1)}, f32[576,128]{1,0:T(8,128)S(1)}, u32[]{:S(2)}, u32[]{:S(2)}) collective-permute-start(f32[576,128]{1,0:T(8,128)S(1)} %bitcast.19), channel_id=1, source_target_pairs={{0,4},{4,5},{5,1},{1,0},{8,12},{12,13},{13,9},{9,8},{16,20},{20,21... | collective-permute-start | bytes 884744 | tf_op jit(solution)/shard_map/ppermute | solution.py:506
  22.7 2.7 %copy-start.5 = (f32[1,73728]{1,0:T(1,128)S(1)}, f32[1,73728]{1,0:T(1,128)}, u32[]{:S(2)}) copy-start(f32[1,73728]{1,0:T(1,128)} %param.8) | copy-start | bytes 884740
  22.7 2.7 %copy-start.6 = (f32[1,73728]{1,0:T(1,128)S(1)}, f32[1,73728]{1,0:T(1,128)}, u32[]{:S(2)}) copy-start(f32[1,73728]{1,0:T(1,128)} %param.9) | copy-start | bytes 884740
  28.2 8.8 %collective-permute-start.9 = (f32[4,48,384]{2,1,0:T(8,128)S(1)}, f32[4,48,384]{2,1,0:T(8,128)S(1)}, u32[]{:S(2)}, u32[]{:S(2)}) collective-permute-start(f32[4,48,384]{2,1,0:T(8,128)S(1)} %get-tuple-element.60), channel_id=1, source_target_pairs={{0,4},{4,0},{8,12},{12,8},{16,20},{20,16},{24,28},{28,24},{1,5},{5... | collective-permute-start | bytes 884744 | tf_op jit(solution)/shard_map/ppermute | solution.py:459
  35.0 9.1 %collective-permute-start.13 = (f32[576,128]{1,0:T(8,128)S(1)}, f32[576,128]{1,0:T(8,128)S(1)}, u32[]{:S(2)}, u32[]{:S(2)}) collective-permute-start(f32[576,128]{1,0:T(8,128)S(1)} %get-tuple-element.64), channel_id=1, source_target_pairs={{0,4},{4,0},{8,12},{12,8},{16,20},{20,16},{24,28},{28,24},{1,5},{5... | collective-permute-start | bytes 884744 | tf_op jit(solution)/shard_map/ppermute | solution.py:459
  37.1 7.9 %collective-permute-start.10 = (f32[48,384]{1,0:T(8,128)S(1)}, f32[48,384]{1,0:T(8,128)S(1)}, u32[]{:S(2)}, u32[]{:S(2)}) collective-permute-start(f32[48,384]{1,0:T(8,128)S(1)} %get-tuple-element.68), channel_id=1, source_target_pairs={{0,16},{4,20},{8,24},{12,28},{16,0},{20,4},{24,8},{28,12},{1,17},{... | collective-permute-start | bytes 221192 | tf_op jit(solution)/shard_map/ppermute | solution.py:456
  40.3 6.3 %collective-permute-start.11 = (f32[48,384]{1,0:T(8,128)S(1)}, f32[48,384]{1,0:T(8,128)S(1)}, u32[]{:S(2)}, u32[]{:S(2)}) collective-permute-start(f32[48,384]{1,0:T(8,128)S(1)} %get-tuple-element.69), channel_id=1, source_target_pairs={{0,24},{4,28},{8,16},{12,20},{16,8},{20,12},{24,0},{28,4},{1,25},{... | collective-permute-start | bytes 221192 | tf_op jit(solution)/shard_map/ppermute | solution.py:456
  41.6 5.1 %collective-permute-start.12 = (f32[48,384]{1,0:T(8,128)S(1)}, f32[48,384]{1,0:T(8,128)S(1)}, u32[]{:S(2)}, u32[]{:S(2)}) collective-permute-start(f32[48,384]{1,0:T(8,128)S(1)} %get-tuple-element.70), channel_id=1, source_target_pairs={{0,8},{4,12},{8,0},{12,4},{16,24},{20,28},{24,16},{28,20},{1,9},{5... | collective-permute-start | bytes 221192 | tf_op jit(solution)/shard_map/ppermute | solution.py:456

commit v21 on v20

--- a/solution.py
+++ b/solution.py
@@ -503,7 +503,7 @@
             cycle += [(place(t, i), place(t, i + 1)), (place(t, i + 1), place(t + 1, i + 1))]
             cycle += [(place(t + 1, i + 1), place(t + 1, i)), (place(t + 1, i), place(t, i))]
     cycle += [(place(t, i), place(t, i ^ 1)) for t in range(tensors - tensors % 2, tensors) for i in range(size)]
-    other_left = lax.ppermute(after(l_basis, *(theirs[:2] if near else mine)), ("shard", "tensor"), cycle)
+    other_left = lax.ppermute(after(l_basis, basis, *(theirs if near else mine)), ("shard", "tensor"), cycle)
     (x,) = call(begin_kernel, [square], [(2, full // 2, LANES)], 7, full, "begin")(got_corner, power, basis)
     new_one, new_two, other_rows, outer, x = call(
         functools.partial(update_kernel, hops), [flat, flat, strips, wide, square], [(3, full, LANES)], 5, full, "update"

time: 47.6 us -> 48 us (level)
  starting transfers between devices: 18.6 us -> 19.9 us
  waiting for transfers between devices: 9.28 us -> 8.3 us
    ppermute x7, waiting for transfers between devices: 3.26 us -> 2.23 us  [partner(): return lax.ppermute(x, 'shard', pairs)]
    ppermute x1, starting transfers between devices: 0.68 us -> 1.45 us  [local(): lax.ppermute(after(l_basis, basis, *(theirs if near else mine)), ('shard'...]
  transfers between devices with their start and end apart: 14 -> 14, of which waited for: 9 -> 7; matrix products, arithmetic and copies ran while one was open for 0% -> 0% of each run, Pallas kernels for 29% -> 29%
where the time goes in v21:
time: 48 us; the launch traced here: 47.9 us
  starting transfers between devices  19.9 us (41%)
  Pallas kernels  18.8 us (39%)
  waiting for transfers between devices  8.3 us (17%)
  between operations  0.79 us (2%)
    ppermute x6, starting transfers between devices, hop_by(): return lax.ppermute(x, 'shard', [(i, i ^ 2 * hop) for i in range(size)])  9.63 us
    ppermute x7, starting transfers between devices, partner(): return lax.ppermute(x, 'shard', pairs)  8.85 us
    ppermute x6, waiting for transfers between devices, hop_by(): return lax.ppermute(x, 'shard', [(i, i ^ 2 * hop) for i in range(size)])  6.07 us
    pallas_call x1, Pallas kernels, local(): call(functools.partial(end_kernel, hops, NS_ITERS - 2), [square, square,...  5.77 us
    pallas_call x1, Pallas kernels, local(): call(functools.partial(update_kernel, hops), [flat, flat, strips, wide, s...  2.84 us
    pallas_call x1, Pallas kernels, local(): call(begin_kernel, [square], [(2, full // 2, LANES)], 7, full, 'begin')  2.66 us
    ppermute x7, waiting for transfers between devices, partner(): return lax.ppermute(x, 'shard', pairs)  2.23 us
    pallas_call x1, Pallas kernels, local(): call(rest_kernel, [flat, flat, flat], [(3, full, LANES)], 1.5, full, 'rest')  2.06 us
  transfers between devices with their start and end apart: 14, of which 7 were waited for; matrix products, arithmetic and copies ran while one was open for 0% of the time, Pallas kernels for 29%

profile of v21, /device:TPU:0, one launch (start us, length us, event | category | flops | bytes accessed | tf_op | source)
XLA Modules:
  0.0 47.9 jit_solution(335255989351505473)
XLA Ops:
  0.6 0.0 copy-start
  0.6 0.0 copy-start.1
  0.7 0.0 copy-start.2
  0.7 0.0 copy-start.3
  0.7 1.3 %pack.1 = (f32[720,128]{1,0:T(8,128)S(1)}, f32[192,128]{1,0:T(8,128)S(1)}, f32[48,384]{1,0:T(8,128)S(1)}, f32[48,384]{1,0:T(8,128)S(1)}, f32[48,384]{1,0:T(8,128)S(1)}) custom-call(f32[576,128]{1,0:T(8,128)} %bitcast.12, f32[576,128]{1,0:T(8,128)} %bitcast.14, f32[576,128]{1,0:T(8,128)} %bitcast.18, f32[576,128]{1,0:T(8,128)} %bitcast.16, f32[4,48,384]{2,1,0:T(8,128)} %refs_0_.1), custom_call_target="tpu_custom_call" | custom-call | flops 33973864 | bytes 2359296 | tf_op jit(solution)/shard_map/pack/pallas_call | solution.py:466
  2.0 3.0 %collective-permute-start = (f32[720,128]{1,0:T(8,128)S(1)}, f32[720,128]{1,0:T(8,128)S(1)}, u32[]{:S(2)}, u32[]{:S(2)}) collective-permute-start(f32[720,128]{1,0:T(8,128)S(1)} %get-tuple-element.45), channel_id=1, source_target_pairs={{0,4},{4,0},{8,12},{12,8},{16,20},{20,16},{24,28},{28,24},{1,5},{5... | collective-permute-start | bytes 1105928 | tf_op jit(solution)/shard_map/ppermute | solution.py:459
  5.0 2.6 %collective-permute-start.1 = (f32[48,384]{1,0:T(8,128)S(1)}, f32[48,384]{1,0:T(8,128)S(1)}, u32[]{:S(2)}, u32[]{:S(2)}) collective-permute-start(f32[48,384]{1,0:T(8,128)S(1)} %get-tuple-element.49), channel_id=1, source_target_pairs={{0,16},{4,20},{8,24},{12,28},{16,0},{20,4},{24,8},{28,12},{1,17},{... | collective-permute-start | bytes 221192 | tf_op jit(solution)/shard_map/ppermute | solution.py:456
  7.6 1.3 %collective-permute-start.2 = (f32[48,384]{1,0:T(8,128)S(1)}, f32[48,384]{1,0:T(8,128)S(1)}, u32[]{:S(2)}, u32[]{:S(2)}) collective-permute-start(f32[48,384]{1,0:T(8,128)S(1)} %get-tuple-element.50), channel_id=1, source_target_pairs={{0,24},{4,28},{8,16},{12,20},{16,8},{20,12},{24,0},{28,4},{1,25},{... | collective-permute-start | bytes 221192 | tf_op jit(solution)/shard_map/ppermute | solution.py:456
  8.9 0.2 collective-permute-start.3
  9.2 3.2 %collective-permute-done.1.refs_1_ = f32[48,384]{1,0:T(8,128)S(1)} collective-permute-done((f32[48,384]{1,0:T(8,128)S(1)}, f32[48,384]{1,0:T(8,128)S(1)}, u32[]{:S(2)}, u32[]{:S(2)}) %collective-permute-start.1) | collective-permute-done | bytes 73760 | tf_op jit(solution)/shard_map/ppermute | solution.py:456
  12.4 0.5 collective-permute-start.4
  12.9 1.1 %collective-permute-done.2.refs_2_ = f32[48,384]{1,0:T(8,128)S(1)} collective-permute-done((f32[48,384]{1,0:T(8,128)S(1)}, f32[48,384]{1,0:T(8,128)S(1)}, u32[]{:S(2)}, u32[]{:S(2)}) %collective-permute-start.2) | collective-permute-done | bytes 73760 | tf_op jit(solution)/shard_map/ppermute | solution.py:456
  13.9 0.5 %collective-permute-start.5 = (f32[48,384]{1,0:T(8,128)S(1)}, f32[48,384]{1,0:T(8,128)S(1)}, u32[]{:S(2)}, u32[]{:S(2)}) collective-permute-start(f32[48,384]{1,0:T(8,128)S(1)} %collective-permute-done.2.refs_2_), channel_id=1, source_target_pairs={{0,4},{4,0},{8,12},{12,8},{16,20},{20,16},{24,28},{28,24},{1,5},{5... | collective-permute-start | bytes 221192 | tf_op jit(solution)/shard_map/ppermute | solution.py:459
  14.4 0.0 collective-permute-done.3.refs_3_
  14.4 1.5 %collective-permute-start.6 = (f32[48,384]{1,0:T(8,128)S(1)}, f32[48,384]{1,0:T(8,128)S(1)}, u32[]{:S(2)}, u32[]{:S(2)}) collective-permute-start(f32[48,384]{1,0:T(8,128)S(1)} %collective-permute-done.3.refs_3_), channel_id=1, source_target_pairs={{0,4},{4,0},{8,12},{12,8},{16,20},{20,16},{24,28},{28,24},{1,5},{5... | collective-permute-start | bytes 221192 | tf_op jit(solution)/shard_map/ppermute | solution.py:459
  15.9 1.0 %collective-permute-done.4.refs_4_ = f32[48,384]{1,0:T(8,128)S(1)} collective-permute-done((f32[48,384]{1,0:T(8,128)S(1)}, f32[48,384]{1,0:T(8,128)S(1)}, u32[]{:S(2)}, u32[]{:S(2)}) %collective-permute-start.4) | collective-permute-done | bytes 73760 | tf_op jit(solution)/shard_map/ppermute | solution.py:459
  17.0 1.1 %collective-permute-start.8 = (f32[192,128]{1,0:T(8,128)S(1)}, f32[192,128]{1,0:T(8,128)S(1)}, u32[]{:S(2)}, u32[]{:S(2)}) collective-permute-start(f32[192,128]{1,0:T(8,128)S(1)} %get-tuple-element.57), channel_id=1, source_target_pairs={{0,4},{4,0},{8,12},{12,8},{16,20},{20,16},{24,28},{28,24},{1,5},{5... | collective-permute-start | bytes 294920 | tf_op jit(solution)/shard_map/ppermute | solution.py:459
  18.1 0.0 collective-permute-done.got_ref
  18.1 0.0 copy-done
  18.1 0.0 copy-done.1
  18.1 0.0 copy-done.2
  18.1 0.0 copy-done.3
  18.1 0.7 %prepare.1 = (f32[384,384]{1,0:T(8,128)S(1)}, f32[384,384]{1,0:T(8,128)S(1)}, f32[384,256]{1,0:T(8,128)S(1)}, f32[256,384]{1,0:T(8,128)S(1)}, f32[576,128]{1,0:T(8,128)S(1)}, /*index=5*/f32[576,128]{1,0:T(8,128)S(1)}) custom-call(f32[576,128]{1,0:T(8,128)S(1)} %bitcast.13, f32[576,128]{1,0:T(8,128)S(1)} %bitcast.15, f32[576,128]{1,0:T(8,128)S(1)} %bitcast.19, ...), custom_call_target="tpu_custom_call" | custom-call | flops 33973864 | bytes 2359296 | tf_op jit(solution)/shard_map/prepare/pallas_call | solution.py:492
  18.9 0.0 collective-permute-done.5.refs_5_
  18.9 0.8 %collective-permute-done.6.refs_6_ = f32[48,384]{1,0:T(8,128)S(1)} collective-permute-done((f32[48,384]{1,0:T(8,128)S(1)}, f32[48,384]{1,0:T(8,128)S(1)}, u32[]{:S(2)}, u32[]{:S(2)}) %collective-permute-start.6) | collective-permute-done | bytes 73760 | tf_op jit(solution)/shard_map/ppermute | solution.py:459
  19.7 1.4 %collective-permute-start.7 = (f32[576,128]{1,0:T(8,128)S(1)}, f32[576,128]{1,0:T(8,128)S(1)}, u32[]{:S(2)}, u32[]{:S(2)}) collective-permute-start(f32[576,128]{1,0:T(8,128)S(1)} %bitcast.20), channel_id=1, source_target_pairs={{0,4},{4,5},{5,1},{1,0},{8,12},{12,13},{13,9},{9,8},{16,20},{20,21... | collective-permute-start | bytes 884744 | tf_op jit(solution)/shard_map/ppermute | solution.py:506
  21.1 0.0 copy-done.4
  21.1 1.8 %products.1 = (f32[384,384]{1,0:T(8,128)S(1)}, f32[384,384]{1,0:T(8,128)S(1)}, f32[384,384]{1,0:T(8,128)S(1)}, f32[256,384]{1,0:T(8,128)S(1)}) custom-call(f32[384,384]{1,0:T(8,128)S(1)} %get-tuple-element.46.basis_ref, f32[384,384]{1,0:T(8,128)S(1)} %get-tuple-element.47.known_ref, f32[256,384]{1,0:T(8,128)S(1)} %get-tuple-element.48.turned_ref, ...), custom_call_target="tpu_custom_call" | custom-call | flops 1019215872 | bytes 2359296 | tf_op jit(solution)/shard_map/products/pallas_call | solution.py:495
  23.0 0.0 collective-permute-done.8.corner_ref
  23.0 0.0 copy-start.5
  23.0 0.0 copy-start.6
  23.0 2.7 %begin.1.start_ref = f32[384,384]{1,0:T(8,128)S(1)} custom-call(f32[192,128]{1,0:T(8,128)S(1)} %collective-permute-done.8.corner_ref, f32[384,384]{1,0:T(8,128)S(1)} %get-tuple-element.58.power_ref, f32[384,384]{1,0:T(8,128)S(1)} %get-tuple-element.46.basis_ref), custom_call_target="tpu_custom_call" | custom-call | flops 2378170368 | bytes 2359296 | tf_op jit(solution)/shard_map/begin/pallas_call | solution.py:507
  25.7 0.0 collective-permute-done.7.other_left_ref
  25.7 2.8 %update.1 = (f32[576,128]{1,0:T(8,128)}, f32[576,128]{1,0:T(8,128)}, f32[4,48,384]{2,1,0:T(8,128)S(1)}, f32[384,256]{1,0:T(8,128)S(1)}, f32[384,384]{1,0:T(8,128)S(1)}) custom-call(f32[256,384]{1,0:T(8,128)S(1)} %get-tuple-element.52.inner_ref, f32[384,384]{1,0:T(8,128)S(1)} %get-tuple-element.46.basis_ref, f32[576,128]{1,0:T(8,128)S(1)} %get-tuple-element.53.left_ref, ...), custom_call_target="tpu_custom_call" | custom-call | flops 1698693120 | bytes 2359296 | tf_op jit(solution)/shard_map/update/pallas_call | solution.py:508
  28.6 2.1 %collective-permute-start.9 = (f32[4,48,384]{2,1,0:T(8,128)S(1)}, f32[4,48,384]{2,1,0:T(8,128)S(1)}, u32[]{:S(2)}, u32[]{:S(2)}) collective-permute-start(f32[4,48,384]{2,1,0:T(8,128)S(1)} %get-tuple-element.60), channel_id=1, source_target_pairs={{0,4},{4,0},{8,12},{12,8},{16,20},{20,16},{24,28},{28,24},{1,5},{5... | collective-permute-start | bytes 884744 | tf_op jit(solution)/shard_map/ppermute | solution.py:459
  30.7 5.8 %end.1 = (f32[384,384]{1,0:T(8,128)S(1)}, f32[384,384]{1,0:T(8,128)S(1)}, f32[576,128]{1,0:T(8,128)S(1)}, f32[4,48,384]{2,1,0:T(8,128)S(1)}) custom-call(f32[384,384]{1,0:T(8,128)S(1)} %get-tuple-element.61.start_ref, f32[384,256]{1,0:T(8,128)S(1)} %get-tuple-element.62.outer_ref, f32[384,256]{1,0:T(8,128)S(1)} %get-tuple-element.54.right_ref), custom_call_target="tpu_custom_call" | custom-call | flops 3057647616 | bytes 2359296 | tf_op jit(solution)/shard_map/end/pallas_call | solution.py:515
  36.5 0.1 collective-permute-start.13
  36.5 0.4 collective-permute-done.9.theirs_ref
  37.0 4.0 %collective-permute-start.10 = (f32[48,384]{1,0:T(8,128)S(1)}, f32[48,384]{1,0:T(8,128)S(1)}, u32[]{:S(2)}, u32[]{:S(2)}) collective-permute-start(f32[48,384]{1,0:T(8,128)S(1)} %get-tuple-element.68), channel_id=1, source_target_pairs={{0,16},{4,20},{8,24},{12,28},{16,0},{20,4},{24,8},{28,12},{1,17},{... | collective-permute-start | bytes 221192 | tf_op jit(solution)/shard_map/ppermute | solution.py:456
  41.0 1.0 %collective-permute-start.11 = (f32[48,384]{1,0:T(8,128)S(1)}, f32[48,384]{1,0:T(8,128)S(1)}, u32[]{:S(2)}, u32[]{:S(2)}) collective-permute-start(f32[48,384]{1,0:T(8,128)S(1)} %get-tuple-element.69), channel_id=1, source_target_pairs={{0,24},{4,28},{8,16},{12,20},{16,8},{20,12},{24,0},{28,4},{1,25},{... | collective-permute-start | bytes 221192 | tf_op jit(solution)/shard_map/ppermute | solution.py:456
  41.9 0.5 %collective-permute-start.12 = (f32[48,384]{1,0:T(8,128)S(1)}, f32[48,384]{1,0:T(8,128)S(1)}, u32[]{:S(2)}, u32[]{:S(2)}) collective-permute-start(f32[48,384]{1,0:T(8,128)S(1)} %get-tuple-element.70), channel_id=1, source_target_pairs={{0,8},{4,12},{8,0},{12,4},{16,24},{20,28},{24,16},{28,20},{1,9},{5... | collective-permute-start | bytes 221192 | tf_op jit(solution)/shard_map/ppermute | solution.py:456
  42.4 2.1 %rest.1 = (f32[576,128]{1,0:T(8,128)S(1)}, f32[576,128]{1,0:T(8,128)}, f32[576,128]{1,0:T(8,128)}) custom-call(f32[384,384]{1,0:T(8,128)S(1)} %get-tuple-element.73.x_ref, f32[384,384]{1,0:T(8,128)S(1)} %get-tuple-element.74.poly_ref, f32[384,384]{1,0:T(8,128)S(1)} %get-tuple-element.75.grad_ref, f32[384,384]{1,0:T(8,128)S(1)} %get-tuple-element.76.new_stat_ref, ...), custom_call_target="tpu_custom_call" | custom-call | flops 509607936 | bytes 2359296 | tf_op jit(solution)/shard_map/rest/pallas_call | solution.py:524
  44.5 0.0 collective-permute-done.13.back_ref
  44.5 0.8 %bases.1 = (f32[576,128]{1,0:T(8,128)}, f32[576,128]{1,0:T(8,128)}) custom-call(f32[576,128]{1,0:T(8,128)S(1)} %get-tuple-element.80.keep_ref, f32[576,128]{1,0:T(8,128)S(1)} %collective-permute-done.13.back_ref), custom_call_target="tpu_custom_call" | custom-call | flops 33973864 | bytes 2359296 | tf_op jit(solution)/shard_map/bases/pallas_call | solution.py:546
  45.3 0.2 collective-permute-done.10.refs_1_
  45.5 1.6 %collective-permute-done.11.refs_2_ = f32[48,384]{1,0:T(8,128)S(1)} collective-permute-done((f32[48,384]{1,0:T(8,128)S(1)}, f32[48,384]{1,0:T(8,128)S(1)}, u32[]{:S(2)}, u32[]{:S(2)}) %collective-permute-start.11) | collective-permute-done | bytes 73760 | tf_op jit(solution)/shard_map/ppermute | solution.py:456
  47.1 0.0 collective-permute-done.12.refs_3_
  47.1 0.7 %rows.1 = f32[4,48,384]{2,1,0:T(8,128)} custom-call(f32[48,384]{1,0:T(8,128)S(1)} %get-tuple-element.67.refs_0_, f32[48,384]{1,0:T(8,128)S(1)} %collective-permute-done.10.refs_1_, f32[48,384]{1,0:T(8,128)S(1)} %collective-permute-done.11.refs_2_, f32[48,384]{1,0:T(8,128)S(1)} %collective-permute-done.12.refs_3_), custom_call_target="tpu_custom_call" | custom-call | flops 33973864 | bytes 2359296 | tf_op jit(solution)/shard_map/rows/pallas_call | solution.py:532
  (4 shorter events, 0.0 us)
Async XLA Ops:
  0.6 17.4 %copy-start = (f32[1,73728]{1,0:T(1,128)S(1)}, f32[1,73728]{1,0:T(1,128)}, u32[]{:S(2)}) copy-start(f32[1,73728]{1,0:T(1,128)} %param.10) | copy-start | bytes 884740
  0.6 17.4 %copy-start.1 = (f32[1,73728]{1,0:T(1,128)S(1)}, f32[1,73728]{1,0:T(1,128)}, u32[]{:S(2)}) copy-start(f32[1,73728]{1,0:T(1,128)} %param.11) | copy-start | bytes 884740
  0.7 17.4 %copy-start.2 = (f32[1,73728]{1,0:T(1,128)S(1)}, f32[1,73728]{1,0:T(1,128)}, u32[]{:S(2)}) copy-start(f32[1,73728]{1,0:T(1,128)} %param.13) | copy-start | bytes 884740
  0.7 17.4 %copy-start.3 = (f32[1,73728]{1,0:T(1,128)S(1)}, f32[1,73728]{1,0:T(1,128)}, u32[]{:S(2)}) copy-start(f32[1,73728]{1,0:T(1,128)} %param.12) | copy-start | bytes 884740
  2.0 16.1 %collective-permute-start = (f32[720,128]{1,0:T(8,128)S(1)}, f32[720,128]{1,0:T(8,128)S(1)}, u32[]{:S(2)}, u32[]{:S(2)}) collective-permute-start(f32[720,128]{1,0:T(8,128)S(1)} %get-tuple-element.45), channel_id=1, source_target_pairs={{0,4},{4,0},{8,12},{12,8},{16,20},{20,16},{24,28},{28,24},{1,5},{5... | collective-permute-start | bytes 1105928 | tf_op jit(solution)/shard_map/ppermute | solution.py:459
  5.0 7.4 %collective-permute-start.1 = (f32[48,384]{1,0:T(8,128)S(1)}, f32[48,384]{1,0:T(8,128)S(1)}, u32[]{:S(2)}, u32[]{:S(2)}) collective-permute-start(f32[48,384]{1,0:T(8,128)S(1)} %get-tuple-element.49), channel_id=1, source_target_pairs={{0,16},{4,20},{8,24},{12,28},{16,0},{20,4},{24,8},{28,12},{1,17},{... | collective-permute-start | bytes 221192 | tf_op jit(solution)/shard_map/ppermute | solution.py:456
  7.6 6.3 %collective-permute-start.2 = (f32[48,384]{1,0:T(8,128)S(1)}, f32[48,384]{1,0:T(8,128)S(1)}, u32[]{:S(2)}, u32[]{:S(2)}) collective-permute-start(f32[48,384]{1,0:T(8,128)S(1)} %get-tuple-element.50), channel_id=1, source_target_pairs={{0,24},{4,28},{8,16},{12,20},{16,8},{20,12},{24,0},{28,4},{1,25},{... | collective-permute-start | bytes 221192 | tf_op jit(solution)/shard_map/ppermute | solution.py:456
  8.9 5.5 %collective-permute-start.3 = (f32[48,384]{1,0:T(8,128)S(1)}, f32[48,384]{1,0:T(8,128)S(1)}, u32[]{:S(2)}, u32[]{:S(2)}) collective-permute-start(f32[48,384]{1,0:T(8,128)S(1)} %get-tuple-element.51), channel_id=1, source_target_pairs={{0,8},{4,12},{8,0},{12,4},{16,24},{20,28},{24,16},{28,20},{1,9},{5... | collective-permute-start | bytes 221192 | tf_op jit(solution)/shard_map/ppermute | solution.py:456
  12.4 4.6 %collective-permute-start.4 = (f32[48,384]{1,0:T(8,128)S(1)}, f32[48,384]{1,0:T(8,128)S(1)}, u32[]{:S(2)}, u32[]{:S(2)}) collective-permute-start(f32[48,384]{1,0:T(8,128)S(1)} %collective-permute-done.1.refs_1_), channel_id=1, source_target_pairs={{0,4},{4,0},{8,12},{12,8},{16,20},{20,16},{24,28},{28,24},{1,5},{5... | collective-permute-start | bytes 221192 | tf_op jit(solution)/shard_map/ppermute | solution.py:459
  13.9 5.0 %collective-permute-start.5 = (f32[48,384]{1,0:T(8,128)S(1)}, f32[48,384]{1,0:T(8,128)S(1)}, u32[]{:S(2)}, u32[]{:S(2)}) collective-permute-start(f32[48,384]{1,0:T(8,128)S(1)} %collective-permute-done.2.refs_2_), channel_id=1, source_target_pairs={{0,4},{4,0},{8,12},{12,8},{16,20},{20,16},{24,28},{28,24},{1,5},{5... | collective-permute-start | bytes 221192 | tf_op jit(solution)/shard_map/ppermute | solution.py:459
  14.4 5.3 %collective-permute-start.6 = (f32[48,384]{1,0:T(8,128)S(1)}, f32[48,384]{1,0:T(8,128)S(1)}, u32[]{:S(2)}, u32[]{:S(2)}) collective-permute-start(f32[48,384]{1,0:T(8,128)S(1)} %collective-permute-done.3.refs_3_), channel_id=1, source_target_pairs={{0,4},{4,0},{8,12},{12,8},{16,20},{20,16},{24,28},{28,24},{1,5},{5... | collective-permute-start | bytes 221192 | tf_op jit(solution)/shard_map/ppermute | solution.py:459
  17.0 4.2 %copy-start.4 = (f32[4,48,384]{2,1,0:T(8,128)S(1)}, f32[4,48,384]{2,1,0:T(8,128)}, u32[]{:S(2)}) copy-start(f32[4,48,384]{2,1,0:T(8,128)} %refs_0_.1) | copy-start | bytes 884740
  17.0 6.0 %collective-permute-start.8 = (f32[192,128]{1,0:T(8,128)S(1)}, f32[192,128]{1,0:T(8,128)S(1)}, u32[]{:S(2)}, u32[]{:S(2)}) collective-permute-start(f32[192,128]{1,0:T(8,128)S(1)} %get-tuple-element.57), channel_id=1, source_target_pairs={{0,4},{4,0},{8,12},{12,8},{16,20},{20,16},{24,28},{28,24},{1,5},{5... | collective-permute-start | bytes 294920 | tf_op jit(solution)/shard_map/ppermute | solution.py:459
  19.7 6.0 %collective-permute-start.7 = (f32[576,128]{1,0:T(8,128)S(1)}, f32[576,128]{1,0:T(8,128)S(1)}, u32[]{:S(2)}, u32[]{:S(2)}) collective-permute-start(f32[576,128]{1,0:T(8,128)S(1)} %bitcast.20), channel_id=1, source_target_pairs={{0,4},{4,5},{5,1},{1,0},{8,12},{12,13},{13,9},{9,8},{16,20},{20,21... | collective-permute-start | bytes 884744 | tf_op jit(solution)/shard_map/ppermute | solution.py:506
  23.0 2.7 %copy-start.5 = (f32[1,73728]{1,0:T(1,128)S(1)}, f32[1,73728]{1,0:T(1,128)}, u32[]{:S(2)}) copy-start(f32[1,73728]{1,0:T(1,128)} %param.8) | copy-start | bytes 884740
  23.0 2.7 %copy-start.6 = (f32[1,73728]{1,0:T(1,128)S(1)}, f32[1,73728]{1,0:T(1,128)}, u32[]{:S(2)}) copy-start(f32[1,73728]{1,0:T(1,128)} %param.9) | copy-start | bytes 884740
  28.6 8.4 %collective-permute-start.9 = (f32[4,48,384]{2,1,0:T(8,128)S(1)}, f32[4,48,384]{2,1,0:T(8,128)S(1)}, u32[]{:S(2)}, u32[]{:S(2)}) collective-permute-start(f32[4,48,384]{2,1,0:T(8,128)S(1)} %get-tuple-element.60), channel_id=1, source_target_pairs={{0,4},{4,0},{8,12},{12,8},{16,20},{20,16},{24,28},{28,24},{1,5},{5... | collective-permute-start | bytes 884744 | tf_op jit(solution)/shard_map/ppermute | solution.py:459
  36.5 8.0 %collective-permute-start.13 = (f32[576,128]{1,0:T(8,128)S(1)}, f32[576,128]{1,0:T(8,128)S(1)}, u32[]{:S(2)}, u32[]{:S(2)}) collective-permute-start(f32[576,128]{1,0:T(8,128)S(1)} %get-tuple-element.64), channel_id=1, source_target_pairs={{0,4},{4,0},{8,12},{12,8},{16,20},{20,16},{24,28},{28,24},{1,5},{5... | collective-permute-start | bytes 884744 | tf_op jit(solution)/shard_map/ppermute | solution.py:459
  37.0 8.6 %collective-permute-start.10 = (f32[48,384]{1,0:T(8,128)S(1)}, f32[48,384]{1,0:T(8,128)S(1)}, u32[]{:S(2)}, u32[]{:S(2)}) collective-permute-start(f32[48,384]{1,0:T(8,128)S(1)} %get-tuple-element.68), channel_id=1, source_target_pairs={{0,16},{4,20},{8,24},{12,28},{16,0},{20,4},{24,8},{28,12},{1,17},{... | collective-permute-start | bytes 221192 | tf_op jit(solution)/shard_map/ppermute | solution.py:456
  41.0 6.2 %collective-permute-start.11 = (f32[48,384]{1,0:T(8,128)S(1)}, f32[48,384]{1,0:T(8,128)S(1)}, u32[]{:S(2)}, u32[]{:S(2)}) collective-permute-start(f32[48,384]{1,0:T(8,128)S(1)} %get-tuple-element.69), channel_id=1, source_target_pairs={{0,24},{4,28},{8,16},{12,20},{16,8},{20,12},{24,0},{28,4},{1,25},{... | collective-permute-start | bytes 221192 | tf_op jit(solution)/shard_map/ppermute | solution.py:456
  41.9 5.2 %collective-permute-start.12 = (f32[48,384]{1,0:T(8,128)S(1)}, f32[48,384]{1,0:T(8,128)S(1)}, u32[]{:S(2)}, u32[]{:S(2)}) collective-permute-start(f32[48,384]{1,0:T(8,128)S(1)} %get-tuple-element.70), channel_id=1, source_target_pairs={{0,8},{4,12},{8,0},{12,4},{16,24},{20,28},{24,16},{28,20},{1,9},{5... | collective-permute-start | bytes 221192 | tf_op jit(solution)/shard_map/ppermute | solution.py:456

commit v22 on v19

--- a/solution.py
+++ b/solution.py
@@ -323,13 +323,13 @@
     left, first = is_left(), is_first()
     x = start_ref[...]
     parts = split(x)
-    gram = dot_parts(parts, parts, ((1,), (1,)))
+    gram = symmetric_dot(parts, parts, ((1,), (1,)))
     own, got = thirds(left_ref), thirds(other_left_ref)
     basis_left = jnp.where(left, basis_ref[...], whole_of(scratch, pick(first, own, got), pick(first, got, own)))
     left_parts = split(basis_left)
     rotated = dot_parts(split(inner_ref[...]), left_parts).T
     gram_parts = split(gram)
-    square = dot_parts(gram_parts, gram_parts)
+    square = symmetric_dot(gram_parts, gram_parts)
     rotated = flat_of(scratch, rotated)
     ones = thirds(one_ref)
     twos = thirds(two_ref)

time: 47.1 us -> 47.1 us (level)
  no operation moved by 1% of the time
where the time goes in v22:
time: 47.1 us; the launch traced here: 46.9 us
  starting transfers between devices  19.2 us (41%)
  Pallas kernels  18.8 us (40%)
  waiting for transfers between devices  8.18 us (17%)
  between operations  0.77 us (2%)
    ppermute x6, starting transfers between devices, hop_by(): return lax.ppermute(x, 'shard', [(i, i ^ 2 * hop) for i in range(size)])  9.54 us
    ppermute x7, starting transfers between devices, partner(): return lax.ppermute(x, 'shard', pairs)  8.73 us
    ppermute x6, waiting for transfers between devices, hop_by(): return lax.ppermute(x, 'shard', [(i, i ^ 2 * hop) for i in range(size)])  6.02 us
    pallas_call x1, Pallas kernels, local(): call(functools.partial(end_kernel, hops, NS_ITERS - 2), [square, square,...  5.77 us
    pallas_call x1, Pallas kernels, local(): call(functools.partial(update_kernel, hops), [flat, flat, strips, wide, s...  2.81 us
    pallas_call x1, Pallas kernels, local(): call(begin_kernel, [square], [(2, full // 2, LANES)], 7, full, 'begin')  2.66 us
    ppermute x7, waiting for transfers between devices, partner(): return lax.ppermute(x, 'shard', pairs)  2.15 us
    pallas_call x1, Pallas kernels, local(): call(rest_kernel, [flat, flat, flat], [(3, full, LANES)], 1.5, full, 'rest')  2.06 us
  transfers between devices with their start and end apart: 14, of which 7 were waited for; matrix products, arithmetic and copies ran while one was open for 0% of the time, Pallas kernels for 30%

profile of v22, /device:TPU:0, one launch (start us, length us, event | category | flops | bytes accessed | tf_op | source)
XLA Modules:
  0.0 46.9 jit_solution(10391904123318914896)
XLA Ops:
  0.6 0.0 copy-start
  0.6 0.0 copy-start.1
  0.7 0.0 copy-start.2
  0.7 0.0 copy-start.3
  0.7 1.3 %pack.1 = (f32[720,128]{1,0:T(8,128)S(1)}, f32[192,128]{1,0:T(8,128)S(1)}, f32[48,384]{1,0:T(8,128)S(1)}, f32[48,384]{1,0:T(8,128)S(1)}, f32[48,384]{1,0:T(8,128)S(1)}) custom-call(f32[576,128]{1,0:T(8,128)} %bitcast.12, f32[576,128]{1,0:T(8,128)} %bitcast.14, f32[576,128]{1,0:T(8,128)} %bitcast.18, f32[576,128]{1,0:T(8,128)} %bitcast.16, f32[4,48,384]{2,1,0:T(8,128)} %refs_0_.1), custom_call_target="tpu_custom_call" | custom-call | flops 33973864 | bytes 2359296 | tf_op jit(solution)/shard_map/pack/pallas_call | solution.py:466
  2.0 3.0 %collective-permute-start = (f32[720,128]{1,0:T(8,128)S(1)}, f32[720,128]{1,0:T(8,128)S(1)}, u32[]{:S(2)}, u32[]{:S(2)}) collective-permute-start(f32[720,128]{1,0:T(8,128)S(1)} %get-tuple-element.45), channel_id=1, source_target_pairs={{0,4},{4,0},{8,12},{12,8},{16,20},{20,16},{24,28},{28,24},{1,5},{5... | collective-permute-start | bytes 1105928 | tf_op jit(solution)/shard_map/ppermute | solution.py:459
  5.0 2.6 %collective-permute-start.1 = (f32[48,384]{1,0:T(8,128)S(1)}, f32[48,384]{1,0:T(8,128)S(1)}, u32[]{:S(2)}, u32[]{:S(2)}) collective-permute-start(f32[48,384]{1,0:T(8,128)S(1)} %get-tuple-element.49), channel_id=1, source_target_pairs={{0,16},{4,20},{8,24},{12,28},{16,0},{20,4},{24,8},{28,12},{1,17},{... | collective-permute-start | bytes 221192 | tf_op jit(solution)/shard_map/ppermute | solution.py:456
  7.6 1.3 %collective-permute-start.2 = (f32[48,384]{1,0:T(8,128)S(1)}, f32[48,384]{1,0:T(8,128)S(1)}, u32[]{:S(2)}, u32[]{:S(2)}) collective-permute-start(f32[48,384]{1,0:T(8,128)S(1)} %get-tuple-element.50), channel_id=1, source_target_pairs={{0,24},{4,28},{8,16},{12,20},{16,8},{20,12},{24,0},{28,4},{1,25},{... | collective-permute-start | bytes 221192 | tf_op jit(solution)/shard_map/ppermute | solution.py:456
  8.9 0.2 collective-permute-start.3
  9.2 3.2 %collective-permute-done.1.refs_1_ = f32[48,384]{1,0:T(8,128)S(1)} collective-permute-done((f32[48,384]{1,0:T(8,128)S(1)}, f32[48,384]{1,0:T(8,128)S(1)}, u32[]{:S(2)}, u32[]{:S(2)}) %collective-permute-start.1) | collective-permute-done | bytes 73760 | tf_op jit(solution)/shard_map/ppermute | solution.py:456
  12.4 0.5 collective-permute-start.4
  12.9 1.1 %collective-permute-done.2.refs_2_ = f32[48,384]{1,0:T(8,128)S(1)} collective-permute-done((f32[48,384]{1,0:T(8,128)S(1)}, f32[48,384]{1,0:T(8,128)S(1)}, u32[]{:S(2)}, u32[]{:S(2)}) %collective-permute-start.2) | collective-permute-done | bytes 73760 | tf_op jit(solution)/shard_map/ppermute | solution.py:456
  13.9 0.5 %collective-permute-start.5 = (f32[48,384]{1,0:T(8,128)S(1)}, f32[48,384]{1,0:T(8,128)S(1)}, u32[]{:S(2)}, u32[]{:S(2)}) collective-permute-start(f32[48,384]{1,0:T(8,128)S(1)} %collective-permute-done.2.refs_2_), channel_id=1, source_target_pairs={{0,4},{4,0},{8,12},{12,8},{16,20},{20,16},{24,28},{28,24},{1,5},{5... | collective-permute-start | bytes 221192 | tf_op jit(solution)/shard_map/ppermute | solution.py:459
  14.4 0.0 collective-permute-done.3.refs_3_
  14.4 1.5 %collective-permute-start.6 = (f32[48,384]{1,0:T(8,128)S(1)}, f32[48,384]{1,0:T(8,128)S(1)}, u32[]{:S(2)}, u32[]{:S(2)}) collective-permute-start(f32[48,384]{1,0:T(8,128)S(1)} %collective-permute-done.3.refs_3_), channel_id=1, source_target_pairs={{0,4},{4,0},{8,12},{12,8},{16,20},{20,16},{24,28},{28,24},{1,5},{5... | collective-permute-start | bytes 221192 | tf_op jit(solution)/shard_map/ppermute | solution.py:459
  15.9 1.0 %collective-permute-done.4.refs_4_ = f32[48,384]{1,0:T(8,128)S(1)} collective-permute-done((f32[48,384]{1,0:T(8,128)S(1)}, f32[48,384]{1,0:T(8,128)S(1)}, u32[]{:S(2)}, u32[]{:S(2)}) %collective-permute-start.4) | collective-permute-done | bytes 73760 | tf_op jit(solution)/shard_map/ppermute | solution.py:459
  17.0 1.1 %collective-permute-start.8 = (f32[192,128]{1,0:T(8,128)S(1)}, f32[192,128]{1,0:T(8,128)S(1)}, u32[]{:S(2)}, u32[]{:S(2)}) collective-permute-start(f32[192,128]{1,0:T(8,128)S(1)} %get-tuple-element.57), channel_id=1, source_target_pairs={{0,4},{4,0},{8,12},{12,8},{16,20},{20,16},{24,28},{28,24},{1,5},{5... | collective-permute-start | bytes 294920 | tf_op jit(solution)/shard_map/ppermute | solution.py:459
  18.1 0.0 collective-permute-done.got_ref
  18.1 0.0 copy-done
  18.1 0.0 copy-done.1
  18.1 0.0 copy-done.2
  18.1 0.0 copy-done.3
  18.1 0.7 %prepare.1 = (f32[384,384]{1,0:T(8,128)S(1)}, f32[384,384]{1,0:T(8,128)S(1)}, f32[384,256]{1,0:T(8,128)S(1)}, f32[256,384]{1,0:T(8,128)S(1)}, f32[576,128]{1,0:T(8,128)S(1)}, /*index=5*/f32[576,128]{1,0:T(8,128)S(1)}) custom-call(f32[576,128]{1,0:T(8,128)S(1)} %bitcast.13, f32[576,128]{1,0:T(8,128)S(1)} %bitcast.15, f32[576,128]{1,0:T(8,128)S(1)} %bitcast.19, ...), custom_call_target="tpu_custom_call" | custom-call | flops 33973864 | bytes 2359296 | tf_op jit(solution)/shard_map/prepare/pallas_call | solution.py:492
  18.9 0.0 collective-permute-done.5.refs_5_
  18.9 0.9 %collective-permute-start.7 = (f32[576,128]{1,0:T(8,128)S(1)}, f32[576,128]{1,0:T(8,128)S(1)}, u32[]{:S(2)}, u32[]{:S(2)}) collective-permute-start(f32[576,128]{1,0:T(8,128)S(1)} %bitcast.20), channel_id=1, source_target_pairs={{0,4},{4,5},{5,1},{1,0},{8,12},{12,13},{13,9},{9,8},{16,20},{20,21... | collective-permute-start | bytes 884744 | tf_op jit(solution)/shard_map/ppermute | solution.py:506
  19.8 0.5 %collective-permute-done.6.refs_6_ = f32[48,384]{1,0:T(8,128)S(1)} collective-permute-done((f32[48,384]{1,0:T(8,128)S(1)}, f32[48,384]{1,0:T(8,128)S(1)}, u32[]{:S(2)}, u32[]{:S(2)}) %collective-permute-start.6) | collective-permute-done | bytes 73760 | tf_op jit(solution)/shard_map/ppermute | solution.py:459
  20.3 0.0 copy-done.4
  20.3 1.8 %products.1 = (f32[384,384]{1,0:T(8,128)S(1)}, f32[384,384]{1,0:T(8,128)S(1)}, f32[384,384]{1,0:T(8,128)S(1)}, f32[256,384]{1,0:T(8,128)S(1)}) custom-call(f32[384,384]{1,0:T(8,128)S(1)} %get-tuple-element.46.basis_ref, f32[384,384]{1,0:T(8,128)S(1)} %get-tuple-element.47.known_ref, f32[256,384]{1,0:T(8,128)S(1)} %get-tuple-element.48.turned_ref, ...), custom_call_target="tpu_custom_call" | custom-call | flops 1019215872 | bytes 2359296 | tf_op jit(solution)/shard_map/products/pallas_call | solution.py:495
  22.2 0.5 %collective-permute-done.8.corner_ref = f32[192,128]{1,0:T(8,128)S(1)} collective-permute-done((f32[192,128]{1,0:T(8,128)S(1)}, f32[192,128]{1,0:T(8,128)S(1)}, u32[]{:S(2)}, u32[]{:S(2)}) %collective-permute-start.8) | collective-permute-done | bytes 98336 | tf_op jit(solution)/shard_map/ppermute | solution.py:459
  22.7 2.7 %begin.1.start_ref = f32[384,384]{1,0:T(8,128)S(1)} custom-call(f32[192,128]{1,0:T(8,128)S(1)} %collective-permute-done.8.corner_ref, f32[384,384]{1,0:T(8,128)S(1)} %get-tuple-element.58.power_ref, f32[384,384]{1,0:T(8,128)S(1)} %get-tuple-element.46.basis_ref), custom_call_target="tpu_custom_call" | custom-call | flops 2378170368 | bytes 2359296 | tf_op jit(solution)/shard_map/begin/pallas_call | solution.py:507
  25.4 0.0 collective-permute-done.7.other_left_ref
  25.4 0.0 copy-done.5
  25.4 0.0 copy-done.6
  25.4 2.8 %update.1 = (f32[576,128]{1,0:T(8,128)}, f32[576,128]{1,0:T(8,128)}, f32[4,48,384]{2,1,0:T(8,128)S(1)}, f32[384,256]{1,0:T(8,128)S(1)}, f32[384,384]{1,0:T(8,128)S(1)}) custom-call(f32[256,384]{1,0:T(8,128)S(1)} %get-tuple-element.52.inner_ref, f32[384,384]{1,0:T(8,128)S(1)} %get-tuple-element.46.basis_ref, f32[576,128]{1,0:T(8,128)S(1)} %get-tuple-element.53.left_ref, ...), custom_call_target="tpu_custom_call" | custom-call | flops 1698693120 | bytes 2359296 | tf_op jit(solution)/shard_map/update/pallas_call | solution.py:508
  28.2 1.1 %collective-permute-start.9 = (f32[4,48,384]{2,1,0:T(8,128)S(1)}, f32[4,48,384]{2,1,0:T(8,128)S(1)}, u32[]{:S(2)}, u32[]{:S(2)}) collective-permute-start(f32[4,48,384]{2,1,0:T(8,128)S(1)} %get-tuple-element.60), channel_id=1, source_target_pairs={{0,4},{4,0},{8,12},{12,8},{16,20},{20,16},{24,28},{28,24},{1,5},{5... | collective-permute-start | bytes 884744 | tf_op jit(solution)/shard_map/ppermute | solution.py:459
  29.3 5.8 %end.1 = (f32[384,384]{1,0:T(8,128)S(1)}, f32[384,384]{1,0:T(8,128)S(1)}, f32[576,128]{1,0:T(8,128)S(1)}, f32[4,48,384]{2,1,0:T(8,128)S(1)}) custom-call(f32[384,384]{1,0:T(8,128)S(1)} %get-tuple-element.61.start_ref, f32[384,256]{1,0:T(8,128)S(1)} %get-tuple-element.62.outer_ref, f32[384,256]{1,0:T(8,128)S(1)} %get-tuple-element.54.right_ref), custom_call_target="tpu_custom_call" | custom-call | flops 3057647616 | bytes 2359296 | tf_op jit(solution)/shard_map/end/pallas_call | solution.py:515
  35.1 1.0 %collective-permute-start.13 = (f32[576,128]{1,0:T(8,128)S(1)}, f32[576,128]{1,0:T(8,128)S(1)}, u32[]{:S(2)}, u32[]{:S(2)}) collective-permute-start(f32[576,128]{1,0:T(8,128)S(1)} %get-tuple-element.64), channel_id=1, source_target_pairs={{0,4},{4,0},{8,12},{12,8},{16,20},{20,16},{24,28},{28,24},{1,5},{5... | collective-permute-start | bytes 884744 | tf_op jit(solution)/shard_map/ppermute | solution.py:459
  36.1 0.1 collective-permute-done.9.theirs_ref
  36.2 3.7 %collective-permute-start.10 = (f32[48,384]{1,0:T(8,128)S(1)}, f32[48,384]{1,0:T(8,128)S(1)}, u32[]{:S(2)}, u32[]{:S(2)}) collective-permute-start(f32[48,384]{1,0:T(8,128)S(1)} %get-tuple-element.68), channel_id=1, source_target_pairs={{0,16},{4,20},{8,24},{12,28},{16,0},{20,4},{24,8},{28,12},{1,17},{... | collective-permute-start | bytes 221192 | tf_op jit(solution)/shard_map/ppermute | solution.py:456
  39.9 1.2 %collective-permute-start.11 = (f32[48,384]{1,0:T(8,128)S(1)}, f32[48,384]{1,0:T(8,128)S(1)}, u32[]{:S(2)}, u32[]{:S(2)}) collective-permute-start(f32[48,384]{1,0:T(8,128)S(1)} %get-tuple-element.69), channel_id=1, source_target_pairs={{0,24},{4,28},{8,16},{12,20},{16,8},{20,12},{24,0},{28,4},{1,25},{... | collective-permute-start | bytes 221192 | tf_op jit(solution)/shard_map/ppermute | solution.py:456
  41.0 0.5 %collective-permute-start.12 = (f32[48,384]{1,0:T(8,128)S(1)}, f32[48,384]{1,0:T(8,128)S(1)}, u32[]{:S(2)}, u32[]{:S(2)}) collective-permute-start(f32[48,384]{1,0:T(8,128)S(1)} %get-tuple-element.70), channel_id=1, source_target_pairs={{0,8},{4,12},{8,0},{12,4},{16,24},{20,28},{24,16},{28,20},{1,9},{5... | collective-permute-start | bytes 221192 | tf_op jit(solution)/shard_map/ppermute | solution.py:456
  41.5 2.1 %rest.1 = (f32[576,128]{1,0:T(8,128)S(1)}, f32[576,128]{1,0:T(8,128)}, f32[576,128]{1,0:T(8,128)}) custom-call(f32[384,384]{1,0:T(8,128)S(1)} %get-tuple-element.73.x_ref, f32[384,384]{1,0:T(8,128)S(1)} %get-tuple-element.74.poly_ref, f32[384,384]{1,0:T(8,128)S(1)} %get-tuple-element.75.grad_ref, f32[384,384]{1,0:T(8,128)S(1)} %get-tuple-element.76.new_stat_ref, ...), custom_call_target="tpu_custom_call" | custom-call | flops 509607936 | bytes 2359296 | tf_op jit(solution)/shard_map/rest/pallas_call | solution.py:524
  43.6 0.0 collective-permute-done.13.back_ref
  43.6 0.8 %bases.1 = (f32[576,128]{1,0:T(8,128)}, f32[576,128]{1,0:T(8,128)}) custom-call(f32[576,128]{1,0:T(8,128)S(1)} %get-tuple-element.80.keep_ref, f32[576,128]{1,0:T(8,128)S(1)} %collective-permute-done.13.back_ref), custom_call_target="tpu_custom_call" | custom-call | flops 33973864 | bytes 2359296 | tf_op jit(solution)/shard_map/bases/pallas_call | solution.py:546
  44.4 0.0 collective-permute-done.10.refs_1_
  44.4 1.7 %collective-permute-done.11.refs_2_ = f32[48,384]{1,0:T(8,128)S(1)} collective-permute-done((f32[48,384]{1,0:T(8,128)S(1)}, f32[48,384]{1,0:T(8,128)S(1)}, u32[]{:S(2)}, u32[]{:S(2)}) %collective-permute-start.11) | collective-permute-done | bytes 73760 | tf_op jit(solution)/shard_map/ppermute | solution.py:456
  46.2 0.0 collective-permute-done.12.refs_3_
  46.2 0.7 %rows.1 = f32[4,48,384]{2,1,0:T(8,128)} custom-call(f32[48,384]{1,0:T(8,128)S(1)} %get-tuple-element.67.refs_0_, f32[48,384]{1,0:T(8,128)S(1)} %collective-permute-done.10.refs_1_, f32[48,384]{1,0:T(8,128)S(1)} %collective-permute-done.11.refs_2_, f32[48,384]{1,0:T(8,128)S(1)} %collective-permute-done.12.refs_3_), custom_call_target="tpu_custom_call" | custom-call | flops 33973864 | bytes 2359296 | tf_op jit(solution)/shard_map/rows/pallas_call | solution.py:532
  (4 shorter events, 0.0 us)
Async XLA Ops:
  0.6 17.4 %copy-start = (f32[1,73728]{1,0:T(1,128)S(1)}, f32[1,73728]{1,0:T(1,128)}, u32[]{:S(2)}) copy-start(f32[1,73728]{1,0:T(1,128)} %param.10) | copy-start | bytes 884740
  0.6 17.4 %copy-start.1 = (f32[1,73728]{1,0:T(1,128)S(1)}, f32[1,73728]{1,0:T(1,128)}, u32[]{:S(2)}) copy-start(f32[1,73728]{1,0:T(1,128)} %param.11) | copy-start | bytes 884740
  0.7 17.4 %copy-start.2 = (f32[1,73728]{1,0:T(1,128)S(1)}, f32[1,73728]{1,0:T(1,128)}, u32[]{:S(2)}) copy-start(f32[1,73728]{1,0:T(1,128)} %param.13) | copy-start | bytes 884740
  0.7 17.4 %copy-start.3 = (f32[1,73728]{1,0:T(1,128)S(1)}, f32[1,73728]{1,0:T(1,128)}, u32[]{:S(2)}) copy-start(f32[1,73728]{1,0:T(1,128)} %param.12) | copy-start | bytes 884740
  2.0 16.1 %collective-permute-start = (f32[720,128]{1,0:T(8,128)S(1)}, f32[720,128]{1,0:T(8,128)S(1)}, u32[]{:S(2)}, u32[]{:S(2)}) collective-permute-start(f32[720,128]{1,0:T(8,128)S(1)} %get-tuple-element.45), channel_id=1, source_target_pairs={{0,4},{4,0},{8,12},{12,8},{16,20},{20,16},{24,28},{28,24},{1,5},{5... | collective-permute-start | bytes 1105928 | tf_op jit(solution)/shard_map/ppermute | solution.py:459
  5.0 7.4 %collective-permute-start.1 = (f32[48,384]{1,0:T(8,128)S(1)}, f32[48,384]{1,0:T(8,128)S(1)}, u32[]{:S(2)}, u32[]{:S(2)}) collective-permute-start(f32[48,384]{1,0:T(8,128)S(1)} %get-tuple-element.49), channel_id=1, source_target_pairs={{0,16},{4,20},{8,24},{12,28},{16,0},{20,4},{24,8},{28,12},{1,17},{... | collective-permute-start | bytes 221192 | tf_op jit(solution)/shard_map/ppermute | solution.py:456
  7.6 6.3 %collective-permute-start.2 = (f32[48,384]{1,0:T(8,128)S(1)}, f32[48,384]{1,0:T(8,128)S(1)}, u32[]{:S(2)}, u32[]{:S(2)}) collective-permute-start(f32[48,384]{1,0:T(8,128)S(1)} %get-tuple-element.50), channel_id=1, source_target_pairs={{0,24},{4,28},{8,16},{12,20},{16,8},{20,12},{24,0},{28,4},{1,25},{... | collective-permute-start | bytes 221192 | tf_op jit(solution)/shard_map/ppermute | solution.py:456
  8.9 5.5 %collective-permute-start.3 = (f32[48,384]{1,0:T(8,128)S(1)}, f32[48,384]{1,0:T(8,128)S(1)}, u32[]{:S(2)}, u32[]{:S(2)}) collective-permute-start(f32[48,384]{1,0:T(8,128)S(1)} %get-tuple-element.51), channel_id=1, source_target_pairs={{0,8},{4,12},{8,0},{12,4},{16,24},{20,28},{24,16},{28,20},{1,9},{5... | collective-permute-start | bytes 221192 | tf_op jit(solution)/shard_map/ppermute | solution.py:456
  12.4 4.6 %collective-permute-start.4 = (f32[48,384]{1,0:T(8,128)S(1)}, f32[48,384]{1,0:T(8,128)S(1)}, u32[]{:S(2)}, u32[]{:S(2)}) collective-permute-start(f32[48,384]{1,0:T(8,128)S(1)} %collective-permute-done.1.refs_1_), channel_id=1, source_target_pairs={{0,4},{4,0},{8,12},{12,8},{16,20},{20,16},{24,28},{28,24},{1,5},{5... | collective-permute-start | bytes 221192 | tf_op jit(solution)/shard_map/ppermute | solution.py:459
  13.9 5.0 %collective-permute-start.5 = (f32[48,384]{1,0:T(8,128)S(1)}, f32[48,384]{1,0:T(8,128)S(1)}, u32[]{:S(2)}, u32[]{:S(2)}) collective-permute-start(f32[48,384]{1,0:T(8,128)S(1)} %collective-permute-done.2.refs_2_), channel_id=1, source_target_pairs={{0,4},{4,0},{8,12},{12,8},{16,20},{20,16},{24,28},{28,24},{1,5},{5... | collective-permute-start | bytes 221192 | tf_op jit(solution)/shard_map/ppermute | solution.py:459
  14.4 5.9 %collective-permute-start.6 = (f32[48,384]{1,0:T(8,128)S(1)}, f32[48,384]{1,0:T(8,128)S(1)}, u32[]{:S(2)}, u32[]{:S(2)}) collective-permute-start(f32[48,384]{1,0:T(8,128)S(1)} %collective-permute-done.3.refs_3_), channel_id=1, source_target_pairs={{0,4},{4,0},{8,12},{12,8},{16,20},{20,16},{24,28},{28,24},{1,5},{5... | collective-permute-start | bytes 221192 | tf_op jit(solution)/shard_map/ppermute | solution.py:459
  17.0 3.3 %copy-start.4 = (f32[4,48,384]{2,1,0:T(8,128)S(1)}, f32[4,48,384]{2,1,0:T(8,128)}, u32[]{:S(2)}) copy-start(f32[4,48,384]{2,1,0:T(8,128)} %refs_0_.1) | copy-start | bytes 884740
  17.0 5.7 %collective-permute-start.8 = (f32[192,128]{1,0:T(8,128)S(1)}, f32[192,128]{1,0:T(8,128)S(1)}, u32[]{:S(2)}, u32[]{:S(2)}) collective-permute-start(f32[192,128]{1,0:T(8,128)S(1)} %get-tuple-element.57), channel_id=1, source_target_pairs={{0,4},{4,0},{8,12},{12,8},{16,20},{20,16},{24,28},{28,24},{1,5},{5... | collective-permute-start | bytes 294920 | tf_op jit(solution)/shard_map/ppermute | solution.py:459
  18.9 6.5 %collective-permute-start.7 = (f32[576,128]{1,0:T(8,128)S(1)}, f32[576,128]{1,0:T(8,128)S(1)}, u32[]{:S(2)}, u32[]{:S(2)}) collective-permute-start(f32[576,128]{1,0:T(8,128)S(1)} %bitcast.20), channel_id=1, source_target_pairs={{0,4},{4,5},{5,1},{1,0},{8,12},{12,13},{13,9},{9,8},{16,20},{20,21... | collective-permute-start | bytes 884744 | tf_op jit(solution)/shard_map/ppermute | solution.py:506
  22.7 2.7 %copy-start.5 = (f32[1,73728]{1,0:T(1,128)S(1)}, f32[1,73728]{1,0:T(1,128)}, u32[]{:S(2)}) copy-start(f32[1,73728]{1,0:T(1,128)} %param.8) | copy-start | bytes 884740
  22.7 2.7 %copy-start.6 = (f32[1,73728]{1,0:T(1,128)S(1)}, f32[1,73728]{1,0:T(1,128)}, u32[]{:S(2)}) copy-start(f32[1,73728]{1,0:T(1,128)} %param.9) | copy-start | bytes 884740
  28.2 7.9 %collective-permute-start.9 = (f32[4,48,384]{2,1,0:T(8,128)S(1)}, f32[4,48,384]{2,1,0:T(8,128)S(1)}, u32[]{:S(2)}, u32[]{:S(2)}) collective-permute-start(f32[4,48,384]{2,1,0:T(8,128)S(1)} %get-tuple-element.60), channel_id=1, source_target_pairs={{0,4},{4,0},{8,12},{12,8},{16,20},{20,16},{24,28},{28,24},{1,5},{5... | collective-permute-start | bytes 884744 | tf_op jit(solution)/shard_map/ppermute | solution.py:459
  35.1 8.5 %collective-permute-start.13 = (f32[576,128]{1,0:T(8,128)S(1)}, f32[576,128]{1,0:T(8,128)S(1)}, u32[]{:S(2)}, u32[]{:S(2)}) collective-permute-start(f32[576,128]{1,0:T(8,128)S(1)} %get-tuple-element.64), channel_id=1, source_target_pairs={{0,4},{4,0},{8,12},{12,8},{16,20},{20,16},{24,28},{28,24},{1,5},{5... | collective-permute-start | bytes 884744 | tf_op jit(solution)/shard_map/ppermute | solution.py:459
  36.2 8.3 %collective-permute-start.10 = (f32[48,384]{1,0:T(8,128)S(1)}, f32[48,384]{1,0:T(8,128)S(1)}, u32[]{:S(2)}, u32[]{:S(2)}) collective-permute-start(f32[48,384]{1,0:T(8,128)S(1)} %get-tuple-element.68), channel_id=1, source_target_pairs={{0,16},{4,20},{8,24},{12,28},{16,0},{20,4},{24,8},{28,12},{1,17},{... | collective-permute-start | bytes 221192 | tf_op jit(solution)/shard_map/ppermute | solution.py:456
  39.9 6.3 %collective-permute-start.11 = (f32[48,384]{1,0:T(8,128)S(1)}, f32[48,384]{1,0:T(8,128)S(1)}, u32[]{:S(2)}, u32[]{:S(2)}) collective-permute-start(f32[48,384]{1,0:T(8,128)S(1)} %get-tuple-element.69), channel_id=1, source_target_pairs={{0,24},{4,28},{8,16},{12,20},{16,8},{20,12},{24,0},{28,4},{1,25},{... | collective-permute-start | bytes 221192 | tf_op jit(solution)/shard_map/ppermute | solution.py:456
  41.0 5.1 %collective-permute-start.12 = (f32[48,384]{1,0:T(8,128)S(1)}, f32[48,384]{1,0:T(8,128)S(1)}, u32[]{:S(2)}, u32[]{:S(2)}) collective-permute-start(f32[48,384]{1,0:T(8,128)S(1)} %get-tuple-element.70), channel_id=1, source_target_pairs={{0,8},{4,12},{8,0},{12,4},{16,24},{20,28},{24,16},{28,20},{1,9},{5... | collective-permute-start | bytes 221192 | tf_op jit(solution)/shard_map/ppermute | solution.py:456

commit v23 on v22

--- a/solution.py
+++ b/solution.py
@@ -349,7 +349,10 @@
     x = iterate(start_ref[...], steps - 1)
     x_ref[...] = x
     rows_for(hops, outer_ref, split(right_ref[...]), mine_ref, lax.axis_index("shard") % 2)
-    poly = polynomial(split(x))
+    parts = split(x)
+    gram = symmetric_dot(parts, parts, ((1,), (1,)))
+    gram_parts = split(gram)
+    poly = CUBIC_COEFF * gram + QUINTIC_COEFF * symmetric_dot(gram_parts, gram_parts)
     poly_ref[...] = poly
     half = take_half(x, jnp.logical_not(is_first()))
     put_thirds(send_ref, flat_of(scratch, LINEAR_COEFF * half + dot(poly, half)))

time: 47.1 us -> 47.1 us (level)
  no operation moved by 1% of the time
where the time goes in v23:
time: 47.1 us; the launch traced here: 47 us
  starting transfers between devices  19.2 us (41%)
  Pallas kernels  18.8 us (40%)
  waiting for transfers between devices  8.12 us (17%)
  between operations  0.77 us (2%)
    ppermute x6, starting transfers between devices, hop_by(): return lax.ppermute(x, 'shard', [(i, i ^ 2 * hop) for i in range(size)])  9.6 us
    ppermute x7, starting transfers between devices, partner(): return lax.ppermute(x, 'shard', pairs)  8.73 us
    ppermute x6, waiting for transfers between devices, hop_by(): return lax.ppermute(x, 'shard', [(i, i ^ 2 * hop) for i in range(size)])  6.02 us
    pallas_call x1, Pallas kernels, local(): call(functools.partial(end_kernel, hops, NS_ITERS - 2), [square, square,...  5.81 us
    pallas_call x1, Pallas kernels, local(): call(functools.partial(update_kernel, hops), [flat, flat, strips, wide, s...  2.81 us
    pallas_call x1, Pallas kernels, local(): call(begin_kernel, [square], [(2, full // 2, LANES)], 7, full, 'begin')  2.66 us
    ppermute x7, waiting for transfers between devices, partner(): return lax.ppermute(x, 'shard', pairs)  2.1 us
    pallas_call x1, Pallas kernels, local(): call(rest_kernel, [flat, flat, flat], [(3, full, LANES)], 1.5, full, 'rest')  2.06 us
  transfers between devices with their start and end apart: 14, of which 7 were waited for; matrix products, arithmetic and copies ran while one was open for 0% of the time, Pallas kernels for 30%

profile of v23, /device:TPU:0, one launch (start us, length us, event | category | flops | bytes accessed | tf_op | source)
XLA Modules:
  0.0 47.0 jit_solution(14955064720808929763)
XLA Ops:
  0.6 0.0 copy-start
  0.6 0.0 copy-start.1
  0.7 0.0 copy-start.2
  0.7 0.0 copy-start.3
  0.7 1.3 %pack.1 = (f32[720,128]{1,0:T(8,128)S(1)}, f32[192,128]{1,0:T(8,128)S(1)}, f32[48,384]{1,0:T(8,128)S(1)}, f32[48,384]{1,0:T(8,128)S(1)}, f32[48,384]{1,0:T(8,128)S(1)}) custom-call(f32[576,128]{1,0:T(8,128)} %bitcast.12, f32[576,128]{1,0:T(8,128)} %bitcast.14, f32[576,128]{1,0:T(8,128)} %bitcast.18, f32[576,128]{1,0:T(8,128)} %bitcast.16, f32[4,48,384]{2,1,0:T(8,128)} %refs_0_.1), custom_call_target="tpu_custom_call" | custom-call | flops 33973864 | bytes 2359296 | tf_op jit(solution)/shard_map/pack/pallas_call | solution.py:469
  2.0 3.0 %collective-permute-start = (f32[720,128]{1,0:T(8,128)S(1)}, f32[720,128]{1,0:T(8,128)S(1)}, u32[]{:S(2)}, u32[]{:S(2)}) collective-permute-start(f32[720,128]{1,0:T(8,128)S(1)} %get-tuple-element.45), channel_id=1, source_target_pairs={{0,4},{4,0},{8,12},{12,8},{16,20},{20,16},{24,28},{28,24},{1,5},{5... | collective-permute-start | bytes 1105928 | tf_op jit(solution)/shard_map/ppermute | solution.py:462
  5.0 2.6 %collective-permute-start.1 = (f32[48,384]{1,0:T(8,128)S(1)}, f32[48,384]{1,0:T(8,128)S(1)}, u32[]{:S(2)}, u32[]{:S(2)}) collective-permute-start(f32[48,384]{1,0:T(8,128)S(1)} %get-tuple-element.49), channel_id=1, source_target_pairs={{0,16},{4,20},{8,24},{12,28},{16,0},{20,4},{24,8},{28,12},{1,17},{... | collective-permute-start | bytes 221192 | tf_op jit(solution)/shard_map/ppermute | solution.py:459
  7.6 1.3 %collective-permute-start.2 = (f32[48,384]{1,0:T(8,128)S(1)}, f32[48,384]{1,0:T(8,128)S(1)}, u32[]{:S(2)}, u32[]{:S(2)}) collective-permute-start(f32[48,384]{1,0:T(8,128)S(1)} %get-tuple-element.50), channel_id=1, source_target_pairs={{0,24},{4,28},{8,16},{12,20},{16,8},{20,12},{24,0},{28,4},{1,25},{... | collective-permute-start | bytes 221192 | tf_op jit(solution)/shard_map/ppermute | solution.py:459
  8.9 0.2 collective-permute-start.3
  9.2 3.2 %collective-permute-done.1.refs_1_ = f32[48,384]{1,0:T(8,128)S(1)} collective-permute-done((f32[48,384]{1,0:T(8,128)S(1)}, f32[48,384]{1,0:T(8,128)S(1)}, u32[]{:S(2)}, u32[]{:S(2)}) %collective-permute-start.1) | collective-permute-done | bytes 73760 | tf_op jit(solution)/shard_map/ppermute | solution.py:459
  12.4 0.5 collective-permute-start.4
  12.9 1.1 %collective-permute-done.2.refs_2_ = f32[48,384]{1,0:T(8,128)S(1)} collective-permute-done((f32[48,384]{1,0:T(8,128)S(1)}, f32[48,384]{1,0:T(8,128)S(1)}, u32[]{:S(2)}, u32[]{:S(2)}) %collective-permute-start.2) | collective-permute-done | bytes 73760 | tf_op jit(solution)/shard_map/ppermute | solution.py:459
  13.9 0.5 %collective-permute-start.5 = (f32[48,384]{1,0:T(8,128)S(1)}, f32[48,384]{1,0:T(8,128)S(1)}, u32[]{:S(2)}, u32[]{:S(2)}) collective-permute-start(f32[48,384]{1,0:T(8,128)S(1)} %collective-permute-done.2.refs_2_), channel_id=1, source_target_pairs={{0,4},{4,0},{8,12},{12,8},{16,20},{20,16},{24,28},{28,24},{1,5},{5... | collective-permute-start | bytes 221192 | tf_op jit(solution)/shard_map/ppermute | solution.py:462
  14.4 0.0 collective-permute-done.3.refs_3_
  14.4 1.5 %collective-permute-start.6 = (f32[48,384]{1,0:T(8,128)S(1)}, f32[48,384]{1,0:T(8,128)S(1)}, u32[]{:S(2)}, u32[]{:S(2)}) collective-permute-start(f32[48,384]{1,0:T(8,128)S(1)} %collective-permute-done.3.refs_3_), channel_id=1, source_target_pairs={{0,4},{4,0},{8,12},{12,8},{16,20},{20,16},{24,28},{28,24},{1,5},{5... | collective-permute-start | bytes 221192 | tf_op jit(solution)/shard_map/ppermute | solution.py:462
  15.9 1.0 %collective-permute-done.4.refs_4_ = f32[48,384]{1,0:T(8,128)S(1)} collective-permute-done((f32[48,384]{1,0:T(8,128)S(1)}, f32[48,384]{1,0:T(8,128)S(1)}, u32[]{:S(2)}, u32[]{:S(2)}) %collective-permute-start.4) | collective-permute-done | bytes 73760 | tf_op jit(solution)/shard_map/ppermute | solution.py:462
  17.0 1.1 %collective-permute-start.8 = (f32[192,128]{1,0:T(8,128)S(1)}, f32[192,128]{1,0:T(8,128)S(1)}, u32[]{:S(2)}, u32[]{:S(2)}) collective-permute-start(f32[192,128]{1,0:T(8,128)S(1)} %get-tuple-element.57), channel_id=1, source_target_pairs={{0,4},{4,0},{8,12},{12,8},{16,20},{20,16},{24,28},{28,24},{1,5},{5... | collective-permute-start | bytes 294920 | tf_op jit(solution)/shard_map/ppermute | solution.py:462
  18.1 0.0 collective-permute-done.got_ref
  18.1 0.0 copy-done
  18.1 0.0 copy-done.1
  18.1 0.0 copy-done.2
  18.1 0.0 copy-done.3
  18.1 0.7 %prepare.1 = (f32[384,384]{1,0:T(8,128)S(1)}, f32[384,384]{1,0:T(8,128)S(1)}, f32[384,256]{1,0:T(8,128)S(1)}, f32[256,384]{1,0:T(8,128)S(1)}, f32[576,128]{1,0:T(8,128)S(1)}, /*index=5*/f32[576,128]{1,0:T(8,128)S(1)}) custom-call(f32[576,128]{1,0:T(8,128)S(1)} %bitcast.13, f32[576,128]{1,0:T(8,128)S(1)} %bitcast.15, f32[576,128]{1,0:T(8,128)S(1)} %bitcast.19, ...), custom_call_target="tpu_custom_call" | custom-call | flops 33973864 | bytes 2359296 | tf_op jit(solution)/shard_map/prepare/pallas_call | solution.py:495
  18.9 0.0 collective-permute-done.5.refs_5_
  18.9 0.9 %collective-permute-start.7 = (f32[576,128]{1,0:T(8,128)S(1)}, f32[576,128]{1,0:T(8,128)S(1)}, u32[]{:S(2)}, u32[]{:S(2)}) collective-permute-start(f32[576,128]{1,0:T(8,128)S(1)} %bitcast.20), channel_id=1, source_target_pairs={{0,4},{4,5},{5,1},{1,0},{8,12},{12,13},{13,9},{9,8},{16,20},{20,21... | collective-permute-start | bytes 884744 | tf_op jit(solution)/shard_map/ppermute | solution.py:509
  19.8 0.5 %collective-permute-done.6.refs_6_ = f32[48,384]{1,0:T(8,128)S(1)} collective-permute-done((f32[48,384]{1,0:T(8,128)S(1)}, f32[48,384]{1,0:T(8,128)S(1)}, u32[]{:S(2)}, u32[]{:S(2)}) %collective-permute-start.6) | collective-permute-done | bytes 73760 | tf_op jit(solution)/shard_map/ppermute | solution.py:462
  20.3 0.0 copy-done.4
  20.3 1.8 %products.1 = (f32[384,384]{1,0:T(8,128)S(1)}, f32[384,384]{1,0:T(8,128)S(1)}, f32[384,384]{1,0:T(8,128)S(1)}, f32[256,384]{1,0:T(8,128)S(1)}) custom-call(f32[384,384]{1,0:T(8,128)S(1)} %get-tuple-element.46.basis_ref, f32[384,384]{1,0:T(8,128)S(1)} %get-tuple-element.47.known_ref, f32[256,384]{1,0:T(8,128)S(1)} %get-tuple-element.48.turned_ref, ...), custom_call_target="tpu_custom_call" | custom-call | flops 1019215872 | bytes 2359296 | tf_op jit(solution)/shard_map/products/pallas_call | solution.py:498
  22.2 0.5 %collective-permute-done.8.corner_ref = f32[192,128]{1,0:T(8,128)S(1)} collective-permute-done((f32[192,128]{1,0:T(8,128)S(1)}, f32[192,128]{1,0:T(8,128)S(1)}, u32[]{:S(2)}, u32[]{:S(2)}) %collective-permute-start.8) | collective-permute-done | bytes 98336 | tf_op jit(solution)/shard_map/ppermute | solution.py:462
  22.7 2.7 %begin.1.start_ref = f32[384,384]{1,0:T(8,128)S(1)} custom-call(f32[192,128]{1,0:T(8,128)S(1)} %collective-permute-done.8.corner_ref, f32[384,384]{1,0:T(8,128)S(1)} %get-tuple-element.58.power_ref, f32[384,384]{1,0:T(8,128)S(1)} %get-tuple-element.46.basis_ref), custom_call_target="tpu_custom_call" | custom-call | flops 2378170368 | bytes 2359296 | tf_op jit(solution)/shard_map/begin/pallas_call | solution.py:510
  25.4 0.0 collective-permute-done.7.other_left_ref
  25.4 0.0 copy-done.5
  25.4 0.0 copy-done.6
  25.4 2.8 %update.1 = (f32[576,128]{1,0:T(8,128)}, f32[576,128]{1,0:T(8,128)}, f32[4,48,384]{2,1,0:T(8,128)S(1)}, f32[384,256]{1,0:T(8,128)S(1)}, f32[384,384]{1,0:T(8,128)S(1)}) custom-call(f32[256,384]{1,0:T(8,128)S(1)} %get-tuple-element.52.inner_ref, f32[384,384]{1,0:T(8,128)S(1)} %get-tuple-element.46.basis_ref, f32[576,128]{1,0:T(8,128)S(1)} %get-tuple-element.53.left_ref, ...), custom_call_target="tpu_custom_call" | custom-call | flops 1698693120 | bytes 2359296 | tf_op jit(solution)/shard_map/update/pallas_call | solution.py:511
  28.2 1.1 %collective-permute-start.9 = (f32[4,48,384]{2,1,0:T(8,128)S(1)}, f32[4,48,384]{2,1,0:T(8,128)S(1)}, u32[]{:S(2)}, u32[]{:S(2)}) collective-permute-start(f32[4,48,384]{2,1,0:T(8,128)S(1)} %get-tuple-element.60), channel_id=1, source_target_pairs={{0,4},{4,0},{8,12},{12,8},{16,20},{20,16},{24,28},{28,24},{1,5},{5... | collective-permute-start | bytes 884744 | tf_op jit(solution)/shard_map/ppermute | solution.py:462
  29.3 5.8 %end.1 = (f32[384,384]{1,0:T(8,128)S(1)}, f32[384,384]{1,0:T(8,128)S(1)}, f32[576,128]{1,0:T(8,128)S(1)}, f32[4,48,384]{2,1,0:T(8,128)S(1)}) custom-call(f32[384,384]{1,0:T(8,128)S(1)} %get-tuple-element.61.start_ref, f32[384,256]{1,0:T(8,128)S(1)} %get-tuple-element.62.outer_ref, f32[384,256]{1,0:T(8,128)S(1)} %get-tuple-element.54.right_ref), custom_call_target="tpu_custom_call" | custom-call | flops 3057647616 | bytes 2359296 | tf_op jit(solution)/shard_map/end/pallas_call | solution.py:518
  35.1 1.0 %collective-permute-start.13 = (f32[576,128]{1,0:T(8,128)S(1)}, f32[576,128]{1,0:T(8,128)S(1)}, u32[]{:S(2)}, u32[]{:S(2)}) collective-permute-start(f32[576,128]{1,0:T(8,128)S(1)} %get-tuple-element.64), channel_id=1, source_target_pairs={{0,4},{4,0},{8,12},{12,8},{16,20},{20,16},{24,28},{28,24},{1,5},{5... | collective-permute-start | bytes 884744 | tf_op jit(solution)/shard_map/ppermute | solution.py:462
  36.1 0.0 collective-permute-done.9.theirs_ref
  36.1 3.7 %collective-permute-start.10 = (f32[48,384]{1,0:T(8,128)S(1)}, f32[48,384]{1,0:T(8,128)S(1)}, u32[]{:S(2)}, u32[]{:S(2)}) collective-permute-start(f32[48,384]{1,0:T(8,128)S(1)} %get-tuple-element.68), channel_id=1, source_target_pairs={{0,16},{4,20},{8,24},{12,28},{16,0},{20,4},{24,8},{28,12},{1,17},{... | collective-permute-start | bytes 221192 | tf_op jit(solution)/shard_map/ppermute | solution.py:459
  39.8 1.2 %collective-permute-start.11 = (f32[48,384]{1,0:T(8,128)S(1)}, f32[48,384]{1,0:T(8,128)S(1)}, u32[]{:S(2)}, u32[]{:S(2)}) collective-permute-start(f32[48,384]{1,0:T(8,128)S(1)} %get-tuple-element.69), channel_id=1, source_target_pairs={{0,24},{4,28},{8,16},{12,20},{16,8},{20,12},{24,0},{28,4},{1,25},{... | collective-permute-start | bytes 221192 | tf_op jit(solution)/shard_map/ppermute | solution.py:459
  41.1 0.5 %collective-permute-start.12 = (f32[48,384]{1,0:T(8,128)S(1)}, f32[48,384]{1,0:T(8,128)S(1)}, u32[]{:S(2)}, u32[]{:S(2)}) collective-permute-start(f32[48,384]{1,0:T(8,128)S(1)} %get-tuple-element.70), channel_id=1, source_target_pairs={{0,8},{4,12},{8,0},{12,4},{16,24},{20,28},{24,16},{28,20},{1,9},{5... | collective-permute-start | bytes 221192 | tf_op jit(solution)/shard_map/ppermute | solution.py:459
  41.6 2.1 %rest.1 = (f32[576,128]{1,0:T(8,128)S(1)}, f32[576,128]{1,0:T(8,128)}, f32[576,128]{1,0:T(8,128)}) custom-call(f32[384,384]{1,0:T(8,128)S(1)} %get-tuple-element.73.x_ref, f32[384,384]{1,0:T(8,128)S(1)} %get-tuple-element.74.poly_ref, f32[384,384]{1,0:T(8,128)S(1)} %get-tuple-element.75.grad_ref, f32[384,384]{1,0:T(8,128)S(1)} %get-tuple-element.76.new_stat_ref, ...), custom_call_target="tpu_custom_call" | custom-call | flops 509607936 | bytes 2359296 | tf_op jit(solution)/shard_map/rest/pallas_call | solution.py:527
  43.6 0.0 collective-permute-done.13.back_ref
  43.6 0.8 %bases.1 = (f32[576,128]{1,0:T(8,128)}, f32[576,128]{1,0:T(8,128)}) custom-call(f32[576,128]{1,0:T(8,128)S(1)} %get-tuple-element.80.keep_ref, f32[576,128]{1,0:T(8,128)S(1)} %collective-permute-done.13.back_ref), custom_call_target="tpu_custom_call" | custom-call | flops 33973864 | bytes 2359296 | tf_op jit(solution)/shard_map/bases/pallas_call | solution.py:549
  44.5 0.0 collective-permute-done.10.refs_1_
  44.5 1.7 %collective-permute-done.11.refs_2_ = f32[48,384]{1,0:T(8,128)S(1)} collective-permute-done((f32[48,384]{1,0:T(8,128)S(1)}, f32[48,384]{1,0:T(8,128)S(1)}, u32[]{:S(2)}, u32[]{:S(2)}) %collective-permute-start.11) | collective-permute-done | bytes 73760 | tf_op jit(solution)/shard_map/ppermute | solution.py:459
  46.1 0.1 collective-permute-done.12.refs_3_
  46.2 0.7 %rows.1 = f32[4,48,384]{2,1,0:T(8,128)} custom-call(f32[48,384]{1,0:T(8,128)S(1)} %get-tuple-element.67.refs_0_, f32[48,384]{1,0:T(8,128)S(1)} %collective-permute-done.10.refs_1_, f32[48,384]{1,0:T(8,128)S(1)} %collective-permute-done.11.refs_2_, f32[48,384]{1,0:T(8,128)S(1)} %collective-permute-done.12.refs_3_), custom_call_target="tpu_custom_call" | custom-call | flops 33973864 | bytes 2359296 | tf_op jit(solution)/shard_map/rows/pallas_call | solution.py:535
  (4 shorter events, 0.0 us)
Async XLA Ops:
  0.6 17.4 %copy-start = (f32[1,73728]{1,0:T(1,128)S(1)}, f32[1,73728]{1,0:T(1,128)}, u32[]{:S(2)}) copy-start(f32[1,73728]{1,0:T(1,128)} %param.10) | copy-start | bytes 884740
  0.6 17.4 %copy-start.1 = (f32[1,73728]{1,0:T(1,128)S(1)}, f32[1,73728]{1,0:T(1,128)}, u32[]{:S(2)}) copy-start(f32[1,73728]{1,0:T(1,128)} %param.11) | copy-start | bytes 884740
  0.7 17.4 %copy-start.2 = (f32[1,73728]{1,0:T(1,128)S(1)}, f32[1,73728]{1,0:T(1,128)}, u32[]{:S(2)}) copy-start(f32[1,73728]{1,0:T(1,128)} %param.13) | copy-start | bytes 884740
  0.7 17.4 %copy-start.3 = (f32[1,73728]{1,0:T(1,128)S(1)}, f32[1,73728]{1,0:T(1,128)}, u32[]{:S(2)}) copy-start(f32[1,73728]{1,0:T(1,128)} %param.12) | copy-start | bytes 884740
  2.0 16.1 %collective-permute-start = (f32[720,128]{1,0:T(8,128)S(1)}, f32[720,128]{1,0:T(8,128)S(1)}, u32[]{:S(2)}, u32[]{:S(2)}) collective-permute-start(f32[720,128]{1,0:T(8,128)S(1)} %get-tuple-element.45), channel_id=1, source_target_pairs={{0,4},{4,0},{8,12},{12,8},{16,20},{20,16},{24,28},{28,24},{1,5},{5... | collective-permute-start | bytes 1105928 | tf_op jit(solution)/shard_map/ppermute | solution.py:462
  5.0 7.4 %collective-permute-start.1 = (f32[48,384]{1,0:T(8,128)S(1)}, f32[48,384]{1,0:T(8,128)S(1)}, u32[]{:S(2)}, u32[]{:S(2)}) collective-permute-start(f32[48,384]{1,0:T(8,128)S(1)} %get-tuple-element.49), channel_id=1, source_target_pairs={{0,16},{4,20},{8,24},{12,28},{16,0},{20,4},{24,8},{28,12},{1,17},{... | collective-permute-start | bytes 221192 | tf_op jit(solution)/shard_map/ppermute | solution.py:459
  7.6 6.3 %collective-permute-start.2 = (f32[48,384]{1,0:T(8,128)S(1)}, f32[48,384]{1,0:T(8,128)S(1)}, u32[]{:S(2)}, u32[]{:S(2)}) collective-permute-start(f32[48,384]{1,0:T(8,128)S(1)} %get-tuple-element.50), channel_id=1, source_target_pairs={{0,24},{4,28},{8,16},{12,20},{16,8},{20,12},{24,0},{28,4},{1,25},{... | collective-permute-start | bytes 221192 | tf_op jit(solution)/shard_map/ppermute | solution.py:459
  8.9 5.5 %collective-permute-start.3 = (f32[48,384]{1,0:T(8,128)S(1)}, f32[48,384]{1,0:T(8,128)S(1)}, u32[]{:S(2)}, u32[]{:S(2)}) collective-permute-start(f32[48,384]{1,0:T(8,128)S(1)} %get-tuple-element.51), channel_id=1, source_target_pairs={{0,8},{4,12},{8,0},{12,4},{16,24},{20,28},{24,16},{28,20},{1,9},{5... | collective-permute-start | bytes 221192 | tf_op jit(solution)/shard_map/ppermute | solution.py:459
  12.4 4.6 %collective-permute-start.4 = (f32[48,384]{1,0:T(8,128)S(1)}, f32[48,384]{1,0:T(8,128)S(1)}, u32[]{:S(2)}, u32[]{:S(2)}) collective-permute-start(f32[48,384]{1,0:T(8,128)S(1)} %collective-permute-done.1.refs_1_), channel_id=1, source_target_pairs={{0,4},{4,0},{8,12},{12,8},{16,20},{20,16},{24,28},{28,24},{1,5},{5... | collective-permute-start | bytes 221192 | tf_op jit(solution)/shard_map/ppermute | solution.py:462
  13.9 5.0 %collective-permute-start.5 = (f32[48,384]{1,0:T(8,128)S(1)}, f32[48,384]{1,0:T(8,128)S(1)}, u32[]{:S(2)}, u32[]{:S(2)}) collective-permute-start(f32[48,384]{1,0:T(8,128)S(1)} %collective-permute-done.2.refs_2_), channel_id=1, source_target_pairs={{0,4},{4,0},{8,12},{12,8},{16,20},{20,16},{24,28},{28,24},{1,5},{5... | collective-permute-start | bytes 221192 | tf_op jit(solution)/shard_map/ppermute | solution.py:462
  14.4 5.9 %collective-permute-start.6 = (f32[48,384]{1,0:T(8,128)S(1)}, f32[48,384]{1,0:T(8,128)S(1)}, u32[]{:S(2)}, u32[]{:S(2)}) collective-permute-start(f32[48,384]{1,0:T(8,128)S(1)} %collective-permute-done.3.refs_3_), channel_id=1, source_target_pairs={{0,4},{4,0},{8,12},{12,8},{16,20},{20,16},{24,28},{28,24},{1,5},{5... | collective-permute-start | bytes 221192 | tf_op jit(solution)/shard_map/ppermute | solution.py:462
  17.0 3.3 %copy-start.4 = (f32[4,48,384]{2,1,0:T(8,128)S(1)}, f32[4,48,384]{2,1,0:T(8,128)}, u32[]{:S(2)}) copy-start(f32[4,48,384]{2,1,0:T(8,128)} %refs_0_.1) | copy-start | bytes 884740
  17.0 5.7 %collective-permute-start.8 = (f32[192,128]{1,0:T(8,128)S(1)}, f32[192,128]{1,0:T(8,128)S(1)}, u32[]{:S(2)}, u32[]{:S(2)}) collective-permute-start(f32[192,128]{1,0:T(8,128)S(1)} %get-tuple-element.57), channel_id=1, source_target_pairs={{0,4},{4,0},{8,12},{12,8},{16,20},{20,16},{24,28},{28,24},{1,5},{5... | collective-permute-start | bytes 294920 | tf_op jit(solution)/shard_map/ppermute | solution.py:462
  18.9 6.5 %collective-permute-start.7 = (f32[576,128]{1,0:T(8,128)S(1)}, f32[576,128]{1,0:T(8,128)S(1)}, u32[]{:S(2)}, u32[]{:S(2)}) collective-permute-start(f32[576,128]{1,0:T(8,128)S(1)} %bitcast.20), channel_id=1, source_target_pairs={{0,4},{4,5},{5,1},{1,0},{8,12},{12,13},{13,9},{9,8},{16,20},{20,21... | collective-permute-start | bytes 884744 | tf_op jit(solution)/shard_map/ppermute | solution.py:509
  22.7 2.7 %copy-start.5 = (f32[1,73728]{1,0:T(1,128)S(1)}, f32[1,73728]{1,0:T(1,128)}, u32[]{:S(2)}) copy-start(f32[1,73728]{1,0:T(1,128)} %param.8) | copy-start | bytes 884740
  22.7 2.7 %copy-start.6 = (f32[1,73728]{1,0:T(1,128)S(1)}, f32[1,73728]{1,0:T(1,128)}, u32[]{:S(2)}) copy-start(f32[1,73728]{1,0:T(1,128)} %param.9) | copy-start | bytes 884740
  28.2 7.9 %collective-permute-start.9 = (f32[4,48,384]{2,1,0:T(8,128)S(1)}, f32[4,48,384]{2,1,0:T(8,128)S(1)}, u32[]{:S(2)}, u32[]{:S(2)}) collective-permute-start(f32[4,48,384]{2,1,0:T(8,128)S(1)} %get-tuple-element.60), channel_id=1, source_target_pairs={{0,4},{4,0},{8,12},{12,8},{16,20},{20,16},{24,28},{28,24},{1,5},{5... | collective-permute-start | bytes 884744 | tf_op jit(solution)/shard_map/ppermute | solution.py:462
  35.1 8.5 %collective-permute-start.13 = (f32[576,128]{1,0:T(8,128)S(1)}, f32[576,128]{1,0:T(8,128)S(1)}, u32[]{:S(2)}, u32[]{:S(2)}) collective-permute-start(f32[576,128]{1,0:T(8,128)S(1)} %get-tuple-element.64), channel_id=1, source_target_pairs={{0,4},{4,0},{8,12},{12,8},{16,20},{20,16},{24,28},{28,24},{1,5},{5... | collective-permute-start | bytes 884744 | tf_op jit(solution)/shard_map/ppermute | solution.py:462
  36.1 8.3 %collective-permute-start.10 = (f32[48,384]{1,0:T(8,128)S(1)}, f32[48,384]{1,0:T(8,128)S(1)}, u32[]{:S(2)}, u32[]{:S(2)}) collective-permute-start(f32[48,384]{1,0:T(8,128)S(1)} %get-tuple-element.68), channel_id=1, source_target_pairs={{0,16},{4,20},{8,24},{12,28},{16,0},{20,4},{24,8},{28,12},{1,17},{... | collective-permute-start | bytes 221192 | tf_op jit(solution)/shard_map/ppermute | solution.py:459
  39.8 6.3 %collective-permute-start.11 = (f32[48,384]{1,0:T(8,128)S(1)}, f32[48,384]{1,0:T(8,128)S(1)}, u32[]{:S(2)}, u32[]{:S(2)}) collective-permute-start(f32[48,384]{1,0:T(8,128)S(1)} %get-tuple-element.69), channel_id=1, source_target_pairs={{0,24},{4,28},{8,16},{12,20},{16,8},{20,12},{24,0},{28,4},{1,25},{... | collective-permute-start | bytes 221192 | tf_op jit(solution)/shard_map/ppermute | solution.py:459
  41.1 5.1 %collective-permute-start.12 = (f32[48,384]{1,0:T(8,128)S(1)}, f32[48,384]{1,0:T(8,128)S(1)}, u32[]{:S(2)}, u32[]{:S(2)}) collective-permute-start(f32[48,384]{1,0:T(8,128)S(1)} %get-tuple-element.70), channel_id=1, source_target_pairs={{0,8},{4,12},{8,0},{12,4},{16,24},{20,28},{24,16},{28,20},{1,9},{5... | collective-permute-start | bytes 221192 | tf_op jit(solution)/shard_map/ppermute | solution.py:459
